TPU v7x, 32 devices: a whole 2x2x4 slice. The times are simulated.
32 devices in a mesh: leaf: 8 (over z, y), draw: 4 (over x, core).
Axes of the slice: x: 2, y: 2, z: 4, core: 2. Of those that a mesh axis runs over, the one named last changes fastest.
Arguments:
- noise_draws: bfloat16 [3, 16, 256, 2048], P(None, 'leaf', None, 'draw'), may hold values from -6 to 6
- inverse_diagonal: bfloat16 [3, 16, 256, 256], P(None, 'leaf', 'draw'), as said below
- coupling_blocks: bfloat16 [2, 16, 8, 256, 256], P(None, 'leaf', 'draw'), may hold values from -0.09375 to 0.09375
- ancestor_pick: int32 [2, 8, 8], replicated, may hold values from 0 to 1
- coupling_lists: int32 [2, 16, 8], P(None, 'leaf'), may hold values from 0 to 15, as said below
- live_counts: int32 [2, 16], P(None, 'leaf'), may hold values from 1 to 8, as said below
Outputs:
- samples: bfloat16 [3, 16, 256, 2048], P(None, 'leaf', None, 'draw')
Inputs may be any that keep to these rules, and one draw needn't show every extreme that they name: `coupling_lists`: the 8 entries of one supernode are distinct. Level 1 entries are below 8, and the live entries of the 2 level-1 supernodes of one owner together name every owner. In level 2 the first 4 entries are 8 or more and the rest below 8; the first halves of one owner's level-2 supernodes together name every value from 8 to 15. `live_counts`: the level-1 counts of one owner's 2 supernodes sum to more than 8; level-2 counts are 4 or more; in each level some supernode has 8. `inverse_diagonal`: each block is lower triangular, with diagonal entries between 0.6 and 1.4.
All inputs are finite; a program needn't handle non-finite values.
Results may differ from a plain program's by a relative error of at most 0.0052.
Values may be sent and summed in bfloat16 or wider, within the bound.
No kernel may reach another device: no remote copies, remote signals or barrier semaphores. Data moves between devices by JAX's collectives and lax.ppermute only.
A program may use at most 64 MiB of HBM per device.

v0:
```python
import jax
import jax.numpy as jnp
from jax import lax
from jax.sharding import PartitionSpec as P


def inverse_fold(right_side, piece):
    return jnp.einsum("nrc,nrs->ncs", piece, right_side, preferred_element_type=jnp.float32)


def apply_inverse(inverse_part, right_side):
    solved = inverse_fold(right_side, lax.all_gather(inverse_part, "draw", axis=1, tiled=True))
    return solved.astype(jnp.bfloat16)


def coupling_fold(table, rows_used, counts_here):
    most = jnp.max(counts_here)

    def fold(carry, piece, start):
        width = piece.shape[1]
        stop = jnp.clip(most, 0, width)

        def turn(offset, total):
            wanted = lax.dynamic_index_in_dim(rows_used, offset, 1, keepdims=False)
            picked = jnp.take(table, wanted, axis=0)
            alive = (offset < counts_here).astype(jnp.bfloat16)
            picked = picked * alive[:, None, None]
            block = lax.dynamic_index_in_dim(piece, offset, 1, keepdims=False)
            return total + jnp.einsum(
                "nrc,nrs->ncs", block, picked, preferred_element_type=jnp.float32
            )

        return lax.fori_loop(0, stop, turn, carry)

    return fold


def gather_updates(block_part, table, rows_used, counts_here, shape):
    empty = jnp.zeros(shape, jnp.float32)
    fold = coupling_fold(table, rows_used, counts_here)
    return fold(empty, lax.all_gather(block_part, "draw", axis=1, tiled=True), jnp.int32(0))


def share_level(solved, picks_level, myself):
    chosen = lax.dynamic_index_in_dim(picks_level, myself, 1, keepdims=False)
    outgoing = jnp.take(solved, chosen, axis=0)
    return lax.all_to_all(outgoing, "leaf", split_axis=0, concat_axis=0, tiled=True)


def on_device(
    noise_draws, inverse_diagonal, coupling_blocks, ancestor_pick, coupling_lists, live_counts
):
    myself = lax.axis_index("leaf")
    inverse_all, blocks_all = (inverse_diagonal, coupling_blocks)
    solved = apply_inverse(inverse_all[0], noise_draws[0])
    levels_done = [solved]
    tables = []
    for level in range(1, noise_draws.shape[0]):
        tables.append(share_level(levels_done[-1], ancestor_pick[level - 1], myself))
        table = jnp.concatenate(tables, axis=0)
        rows_used = coupling_lists[level - 1]
        updates = gather_updates(
            blocks_all[level - 1], table, rows_used, live_counts[level - 1], solved.shape
        )
        right_side = (noise_draws[level].astype(jnp.float32) - updates).astype(jnp.bfloat16)
        levels_done.append(apply_inverse(inverse_all[level], right_side))
    return jnp.stack(levels_done, axis=0)


def solution(mesh):
    placed = (
        P(None, "leaf", None, "draw"),
        P(None, "leaf", "draw", None),
        P(None, "leaf", "draw", None, None),
        P(),
        P(None, "leaf", None),
        P(None, "leaf"),
    )
    return jax.shard_map(
        on_device,
        mesh=mesh,
        in_specs=placed,
        out_specs=P(None, "leaf", None, "draw"),
        check_vma=False,
    )
```

profile of v0, /device:TPU:9, one launch (start us, length us, event | category | flops | bytes accessed | tf_op | source)
XLA Modules:
  0.0 206.2 jit_solution(17815000820539296653)
XLA Ops:
  8.5 6.3 %all-gather = bf16[1,2,256,256]{3,1,0,2:T(2,128)(2,1)S(1)} all-gather(bf16[1,2,64,256]{3,1,0,2:T(2,128)(2,1)S(1)} %copy.34), channel_id=2, replica_groups=mesh['leaf'=8,'draw'=4] {'draw'}, dimensions={2}, use_global_device_ids=true | all-gather | bytes 327680 | tf_op jit(solution)/shard_map/all_gather | solution.py:12
  17.0 1.6 broadcast_select_fusion.1
  18.6 5.7 %all-to-all-start = ((bf16[8,256,512]{2,1,0:T(8,128)(2,1)}), bf16[8,256,512]{2,1,0:T(8,128)(2,1)S(1)}, u32[]{:S(2)}, u32[]{:S(2)}) async-start(bf16[8,256,512]{2,1,0:T(8,128)(2,1)} %broadcast_select_fusion.1), calls=%async_computation | async-start | bytes 4194304 | tf_op jit(solution)/shard_map/all_to_all | solution.py:47
  24.3 2.1 %fusion.32 = (bf16[1,2,2,256,256]{4,3,2,1,0:T(8,128)(2,1)S(1)}, bf16[1,2,2,256,256]{4,3,2,1,0:T(8,128)(2,1)}) fusion(bf16[2,2,2,256,256]{4,3,2,1,0:T(8,128)(2,1)} %param.14), kind=kLoop, calls=%fused_computation.67 | loop fusion | bytes 2097152 | tf_op jit(solution)/shard_map/slice | solution.py:63
  28.8 6.3 %all-gather.2 = bf16[1,2,256,256]{3,2,1,0:T(8,128)(2,1)S(1)} all-gather(bf16[1,2,64,256]{3,2,1,0:T(8,128)(2,1)S(1)} %get-tuple-element.150), channel_id=4, replica_groups=mesh['leaf'=8,'draw'=4] {'draw'}, dimensions={2}, use_global_device_ids=true | all-gather | bytes 327680 | tf_op jit(solution)/shard_map/all_gather | solution.py:12
  35.2 16.2 %all-gather.8.cloned.1.call-done = bf16[1,2,8,256,256]{4,3,1,0,2:T(8,128)(2,1)} async-done(((bf16[1,2,2,256,256]{4,3,1,0,2:T(8,128)(2,1)}), bf16[1,2,8,256,256]{4,3,1,0,2:T(8,128)(2,1)}) %all-gather.8.cloned.1.call-update) | async-done | bytes 2097168 | tf_op jit(solution)/shard_map/all_gather | solution.py:41
  51.3 19.5 %all-to-all-done = bf16[8,256,512]{2,1,0:T(8,128)(2,1)S(1)} async-done(((bf16[8,256,512]{2,1,0:T(8,128)(2,1)}), bf16[8,256,512]{2,1,0:T(8,128)(2,1)S(1)}, u32[]{:S(2)}, u32[]{:S(2)}) %all-to-all-start) | async-done | bytes 2097184 | tf_op jit(solution)/shard_map/all_to_all | solution.py:47
  72.3 22.3 %while.20 = (s32[]{:T(128)}, f32[2,256,512]{2,1,0:T(8,128)S(1)}, s32[]{:T(128)}, bf16[2,8,256,256]{3,2,0,1:T(8,128)(2,1)}, s32[2,8]{0,1:T(8,128)S(1)}, /*index=5...) while((s32[]{:T(128)}, f32[2,256,512]{2,1,0:T(8,128)S(1)}, s32[]{:T(128)}, ...), condition=%wide.region_2.4_spmd, body=%wide.region_1.3_spmd.sunk | while | flops 135005200 | bytes 3936455 | solution.py:33
  72.3 2.2 %gather_fusion = bf16[2,256,512]{2,1,0:T(8,128)(2,1)S(1)} fusion(bf16[8,256,512]{2,1,0:T(8,128)(2,1)} %get-tuple-element.280, s32[1024]{0:T(1024)S(1)} %pad_clamp_fusion.6), kind=kCustom, calls=%fused_computation.1.clone.1 | custom fusion | bytes 1048584 | tf_op jit(solution)/shard_map/while/body/jit(_take)/gather | solution.py:25
  76.0 2.2 %gather_fusion = bf16[2,256,512]{2,1,0:T(8,128)(2,1)S(1)} fusion(bf16[8,256,512]{2,1,0:T(8,128)(2,1)} %get-tuple-element.280, s32[1024]{0:T(1024)S(1)} %pad_clamp_fusion.6), kind=kCustom, calls=%fused_computation.1.clone.1 | custom fusion | bytes 1048584 | tf_op jit(solution)/shard_map/while/body/jit(_take)/gather | solution.py:25
  79.8 2.2 %gather_fusion = bf16[2,256,512]{2,1,0:T(8,128)(2,1)S(1)} fusion(bf16[8,256,512]{2,1,0:T(8,128)(2,1)} %get-tuple-element.280, s32[1024]{0:T(1024)S(1)} %pad_clamp_fusion.6), kind=kCustom, calls=%fused_computation.1.clone.1 | custom fusion | bytes 1048584 | tf_op jit(solution)/shard_map/while/body/jit(_take)/gather | solution.py:25
  83.5 2.2 %gather_fusion = bf16[2,256,512]{2,1,0:T(8,128)(2,1)S(1)} fusion(bf16[8,256,512]{2,1,0:T(8,128)(2,1)} %get-tuple-element.280, s32[1024]{0:T(1024)S(1)} %pad_clamp_fusion.6), kind=kCustom, calls=%fused_computation.1.clone.1 | custom fusion | bytes 1048584 | tf_op jit(solution)/shard_map/while/body/jit(_take)/gather | solution.py:25
  87.2 2.2 %gather_fusion = bf16[2,256,512]{2,1,0:T(8,128)(2,1)S(1)} fusion(bf16[8,256,512]{2,1,0:T(8,128)(2,1)} %get-tuple-element.280, s32[1024]{0:T(1024)S(1)} %pad_clamp_fusion.6), kind=kCustom, calls=%fused_computation.1.clone.1 | custom fusion | bytes 1048584 | tf_op jit(solution)/shard_map/while/body/jit(_take)/gather | solution.py:25
  90.9 2.2 %gather_fusion = bf16[2,256,512]{2,1,0:T(8,128)(2,1)S(1)} fusion(bf16[8,256,512]{2,1,0:T(8,128)(2,1)} %get-tuple-element.280, s32[1024]{0:T(1024)S(1)} %pad_clamp_fusion.6), kind=kCustom, calls=%fused_computation.1.clone.1 | custom fusion | bytes 1048584 | tf_op jit(solution)/shard_map/while/body/jit(_take)/gather | solution.py:25
  96.7 1.6 broadcast_select_fusion
  98.3 13.2 %all-to-all-start.1 = ((bf16[8,256,512]{2,1,0:T(8,128)(2,1)}), bf16[8,256,512]{2,1,0:T(8,128)(2,1)}, u32[]{:S(2)}, u32[]{:S(2)}) async-start(bf16[8,256,512]{2,1,0:T(8,128)(2,1)} %broadcast_select_fusion), calls=%async_computation.1 | async-start | bytes 4194304 | tf_op jit(solution)/shard_map/all_to_all | solution.py:47
  111.5 1.9 copy.36
  114.2 7.2 %all-gather.4 = bf16[1,2,256,256]{3,2,1,0:T(8,128)(2,1)S(1)} all-gather(bf16[1,2,64,256]{3,2,1,0:T(8,128)(2,1)S(1)} %get-tuple-element.148), channel_id=6, replica_groups=mesh['leaf'=8,'draw'=4] {'draw'}, dimensions={2}, use_global_device_ids=true | all-gather | bytes 327680 | tf_op jit(solution)/shard_map/all_gather | solution.py:12
  121.3 36.7 %all-to-all-done.1 = bf16[8,256,512]{2,1,0:T(8,128)(2,1)} async-done(((bf16[8,256,512]{2,1,0:T(8,128)(2,1)}), bf16[8,256,512]{2,1,0:T(8,128)(2,1)}, u32[]{:S(2)}, u32[]{:S(2)}) %all-to-all-start.1) | async-done | bytes 2097184 | tf_op jit(solution)/shard_map/all_to_all | solution.py:47
  158.0 3.9 %pad_maximum_fusion = bf16[16,256,512]{2,1,0:T(8,128)(2,1)} fusion(bf16[8,256,512]{2,1,0:T(8,128)(2,1)} %all-to-all-done.1, bf16[8,256,512]{2,1,0:T(8,128)(2,1)S(1)} %copy-done.1), kind=kLoop, calls=%fused_computation.32 | loop fusion | flops 2097152 | bytes 8388608 | tf_op jit(solution)/shard_map/concatenate | solution.py:60
  162.1 34.6 %while.21 = (s32[]{:T(128)}, f32[2,256,512]{2,1,0:T(8,128)S(1)}, s32[]{:T(128)}, bf16[2,8,256,256]{3,2,0,1:T(8,128)(2,1)}, s32[2,8]{0,1:T(8,128)S(1)}, /*index=5...) while((s32[]{:T(128)}, f32[2,256,512]{2,1,0:T(8,128)S(1)}, s32[]{:T(128)}, ...), condition=%wide.region_5.7_spmd, body=%wide.region_4.6_spmd.sunk | while | flops 135005200 | bytes 3936455 | solution.py:33
  162.1 2.8 %gather_fusion.1 = bf16[2,256,512]{2,1,0:T(8,128)(2,1)S(1)} fusion(bf16[16,256,512]{2,1,0:T(8,128)(2,1)} %get-tuple-element.310, s32[1024]{0:T(1024)S(1)} %pad_clamp_fusion.7), kind=kCustom, calls=%fused_computation.2.clone.1 | custom fusion | bytes 1048584 | tf_op jit(solution)/shard_map/while/body/jit(_take)/gather | solution.py:25
  166.4 2.8 %gather_fusion.1 = bf16[2,256,512]{2,1,0:T(8,128)(2,1)S(1)} fusion(bf16[16,256,512]{2,1,0:T(8,128)(2,1)} %get-tuple-element.310, s32[1024]{0:T(1024)S(1)} %pad_clamp_fusion.7), kind=kCustom, calls=%fused_computation.2.clone.1 | custom fusion | bytes 1048584 | tf_op jit(solution)/shard_map/while/body/jit(_take)/gather | solution.py:25
  169.2 1.5 convolution_add_fusion.5
  170.8 2.8 %gather_fusion.1 = bf16[2,256,512]{2,1,0:T(8,128)(2,1)S(1)} fusion(bf16[16,256,512]{2,1,0:T(8,128)(2,1)} %get-tuple-element.310, s32[1024]{0:T(1024)S(1)} %pad_clamp_fusion.7), kind=kCustom, calls=%fused_computation.2.clone.1 | custom fusion | bytes 1048584 | tf_op jit(solution)/shard_map/while/body/jit(_take)/gather | solution.py:25
  173.5 1.5 convolution_add_fusion.5
  175.1 2.8 %gather_fusion.1 = bf16[2,256,512]{2,1,0:T(8,128)(2,1)S(1)} fusion(bf16[16,256,512]{2,1,0:T(8,128)(2,1)} %get-tuple-element.310, s32[1024]{0:T(1024)S(1)} %pad_clamp_fusion.7), kind=kCustom, calls=%fused_computation.2.clone.1 | custom fusion | bytes 1048584 | tf_op jit(solution)/shard_map/while/body/jit(_take)/gather | solution.py:25
  177.9 1.5 convolution_add_fusion.5
  179.4 2.8 %gather_fusion.1 = bf16[2,256,512]{2,1,0:T(8,128)(2,1)S(1)} fusion(bf16[16,256,512]{2,1,0:T(8,128)(2,1)} %get-tuple-element.310, s32[1024]{0:T(1024)S(1)} %pad_clamp_fusion.7), kind=kCustom, calls=%fused_computation.2.clone.1 | custom fusion | bytes 1048584 | tf_op jit(solution)/shard_map/while/body/jit(_take)/gather | solution.py:25
  183.7 2.8 %gather_fusion.1 = bf16[2,256,512]{2,1,0:T(8,128)(2,1)S(1)} fusion(bf16[16,256,512]{2,1,0:T(8,128)(2,1)} %get-tuple-element.310, s32[1024]{0:T(1024)S(1)} %pad_clamp_fusion.7), kind=kCustom, calls=%fused_computation.2.clone.1 | custom fusion | bytes 1048584 | tf_op jit(solution)/shard_map/while/body/jit(_take)/gather | solution.py:25
  188.0 2.8 %gather_fusion.1 = bf16[2,256,512]{2,1,0:T(8,128)(2,1)S(1)} fusion(bf16[16,256,512]{2,1,0:T(8,128)(2,1)} %get-tuple-element.310, s32[1024]{0:T(1024)S(1)} %pad_clamp_fusion.7), kind=kCustom, calls=%fused_computation.2.clone.1 | custom fusion | bytes 1048584 | tf_op jit(solution)/shard_map/while/body/jit(_take)/gather | solution.py:25
  192.4 2.8 %gather_fusion.1 = bf16[2,256,512]{2,1,0:T(8,128)(2,1)S(1)} fusion(bf16[16,256,512]{2,1,0:T(8,128)(2,1)} %get-tuple-element.310, s32[1024]{0:T(1024)S(1)} %pad_clamp_fusion.7), kind=kCustom, calls=%fused_computation.2.clone.1 | custom fusion | bytes 1048584 | tf_op jit(solution)/shard_map/while/body/jit(_take)/gather | solution.py:25
  (91 shorter events, 28.9 us)
Async XLA Ops:
  18.6 52.3 %all-to-all-start = ((bf16[8,256,512]{2,1,0:T(8,128)(2,1)}), bf16[8,256,512]{2,1,0:T(8,128)(2,1)S(1)}, u32[]{:S(2)}, u32[]{:S(2)}) async-start(bf16[8,256,512]{2,1,0:T(8,128)(2,1)} %broadcast_select_fusion.1), calls=%async_computation | async-start | bytes 4194304 | tf_op jit(solution)/shard_map/all_to_all | solution.py:47
  24.3 3.0 %copy-start.3 = (s32[2,2]{1,0:T(2,128)S(1)}, s32[2,2]{1,0:T(2,128)}, u32[]{:S(2)}) copy-start(s32[2,2]{1,0:T(2,128)} %param.17) | copy-start | bytes 52
  24.3 4.2 %copy-start.2 = (s32[2,2,8]{2,1,0:T(2,128)S(1)}, s32[2,2,8]{2,1,0:T(2,128)}, u32[]{:S(2)}) copy-start(s32[2,2,8]{2,1,0:T(2,128)} %param.16) | copy-start | bytes 388
  24.3 27.0 %all-gather.8.cloned.1.call-start = ((), (), s32[]{:S(2)}) async-start(), calls=%async_computation.2 | async-start | bytes 2621440 | tf_op jit(solution)/shard_map/all_gather | solution.py:41
  70.8 1.3 copy-start
  98.3 59.7 %copy-start.1 = (bf16[8,256,512]{2,1,0:T(8,128)(2,1)S(1)}, bf16[8,256,512]{2,1,0:T(8,128)(2,1)}, u32[]{:S(2)}) copy-start(bf16[8,256,512]{2,1,0:T(8,128)(2,1)} %get-tuple-element.318) | copy-start | bytes 6291460
  98.3 59.7 %all-to-all-start.1 = ((bf16[8,256,512]{2,1,0:T(8,128)(2,1)}), bf16[8,256,512]{2,1,0:T(8,128)(2,1)}, u32[]{:S(2)}, u32[]{:S(2)}) async-start(bf16[8,256,512]{2,1,0:T(8,128)(2,1)} %broadcast_select_fusion), calls=%async_computation.1 | async-start | bytes 4194304 | tf_op jit(solution)/shard_map/all_to_all | solution.py:47
  111.5 50.5 %all-gather.10.cloned.1.call-start = ((), (), s32[]{:S(2)}) async-start(), calls=%async_computation.3 | async-start | bytes 2621440 | tf_op jit(solution)/shard_map/all_gather | solution.py:41
Sparse Core Ops, SparseCore 0:
  27.4 23.9 all-gather.7
  113.9 24.7 all-gather.9
where the time goes:
time: 209 us; the launch traced here: 206 us
  waiting for transfers between devices  72.4 us (35%)
  local copies, waits for them, and re-layouts  45.3 us (22%)
  matrix products  24.7 us (12%)
  blocking collectives  19.8 us (9%)
  starting transfers between devices  18.9 us (9%)
  between operations  14.8 us (7%)
  other arithmetic  9.48 us (5%)
    all_to_all x2, waiting for transfers between devices, share_level(): lax.all_to_all(outgoing, 'leaf', split_axis=0, concat_axis=0, tiled=True)  56.2 us
    gather x14, local copies, waits for them, and re-layouts, turn(): picked = jnp.take(table, wanted, axis=0)  35.2 us
    dot_general x14, matrix products, turn(): jnp.einsum('nrc,nrs->ncs', block, picked, preferred_element_type=jnp.floa...  20.6 us
    all_gather x3, blocking collectives, apply_inverse(): lax.all_gather(inverse_part, 'draw', axis=1, tiled=True)  19.8 us
    all_to_all x2, starting transfers between devices, share_level(): lax.all_to_all(outgoing, 'leaf', split_axis=0, concat_axis=0, tiled=True)  18.9 us
    all_gather x2, waiting for transfers between devices, gather_updates(): lax.all_gather(block_part, 'draw', axis=1, tiled=True)  16.2 us
  transfers between devices with their start and end apart: 4, of which 3 were waited for; matrix products, arithmetic and copies ran while one was open for 5% of the time, Pallas kernels for 0%

commit v1 on v0

v1 whole, which is shorter than its diff:
```python
import functools

import jax
import jax.numpy as jnp
from jax import lax
from jax.experimental import pallas as pl
from jax.experimental.pallas import tpu as pltpu
from jax.sharding import PartitionSpec as P

CHUNKS = 2
VMEM = pl.BlockSpec(memory_space=pltpu.VMEM)
SMEM = pl.BlockSpec(memory_space=pltpu.SMEM)


def hop(value, axis, size, step):
    return lax.ppermute(value, axis, [(at, at ^ step) for at in range(size)])


def gather_parts(value, axis, size):
    parts = {0: value}
    step = size // 2
    while step:
        for have in sorted(parts):
            parts[have ^ step] = hop(parts[have], axis, size, step)
        step //= 2
    return [parts[at] for at in range(size)]


def transposed_dot(left, right):
    return lax.dot_general(
        left, right, (((0,), (0,)), ((), ())), preferred_element_type=jnp.float32
    )


def pick_block(blocks, index):
    return lax.dynamic_index_in_dim(blocks, index, 0, keepdims=False)


def exchange(blocks, picks, myself, owners):
    half = owners // 2
    far = hop(blocks, "leaf", owners, half)
    table = {}
    for step in range(1, half):
        table[step] = hop(pick_block(blocks, picks[myself ^ step, myself]), "leaf", owners, step)
    for step in range(1, half):
        wanted = pick_block(far, picks[myself ^ step, myself ^ half])
        table[step ^ half] = hop(wanted, "leaf", owners, step)
    table[0] = pick_block(blocks, picks[myself, myself])
    table[half] = pick_block(far, picks[myself, myself ^ half])
    return [table[at] for at in range(owners)]


def fill_rows(target, parts, draw):
    rows = parts[0].shape[1]
    for step, part in enumerate(parts):
        start = pl.multiple_of((draw ^ step) * rows, rows)
        target[:, pl.ds(start, rows), :] = part[...]


def add_slots(total, table, parts, scalars, lists, counts, source):
    owners = table.shape[0]
    myself, draw = scalars[0], scalars[1]
    nodes, width = parts[0].shape[:2]
    for step, part in enumerate(parts):
        for offset in range(width):
            slot = (draw ^ step) * width + offset
            for node in range(nodes):
                entry = lists[node, slot] - source * owners
                live = (slot < counts[node]) & (entry >= 0) & (entry < owners)

                @pl.when(live)
                def _():
                    total[node] += transposed_dot(part[node, offset], table[entry ^ myself])


def solve(result, inverse, total, noise):
    for node in range(noise.shape[0]):
        right_side = (noise[node].astype(jnp.float32) - total[node]).astype(jnp.bfloat16)
        result[node] = transposed_dot(inverse[node], right_side).astype(jnp.bfloat16)


def first_kernel(owners, draws, scalars, lists, counts, *refs):
    refs = list(refs)
    take = lambda count: [refs.pop(0) for _ in range(count)]
    table_in, picked, inv_first, inv_here, blocks = (
        take(owners), take(draws), take(draws), take(draws), take(draws)
    )
    noise_first, noise, below, here, table, inv_table, inv_full, total = take(8)
    draw = scalars[1]
    fill_rows(inv_table, picked, draw)
    for step in range(owners):
        table[step] = transposed_dot(inv_table[step], table_in[step][...]).astype(jnp.bfloat16)
    fill_rows(inv_full, inv_first, draw)
    for node in range(noise.shape[0]):
        below[node] = transposed_dot(inv_full[node], noise_first[node]).astype(jnp.bfloat16)
    total[...] = jnp.zeros_like(total)
    add_slots(total, table, blocks, scalars, lists, counts, 0)
    fill_rows(inv_full, inv_here, draw)
    solve(here, inv_full, total, noise)


def partial_kernel(source, draws, scalars, lists, counts, *refs):
    blocks, (table, total) = refs[:draws], refs[draws:]
    total[...] = jnp.zeros_like(total)
    add_slots(total, table, blocks, scalars, lists, counts, source)


def last_kernel(source, owners, draws, scalars, lists, counts, *refs):
    refs = list(refs)
    take = lambda count: [refs.pop(0) for _ in range(count)]
    table_in, inv_here, blocks = take(owners), take(draws), take(draws)
    before, noise, here, table, inv_full, total = take(6)
    for step in range(owners):
        table[step] = table_in[step][...]
    total[...] = before[...]
    add_slots(total, table, blocks, scalars, lists, counts, source)
    fill_rows(inv_full, inv_here, scalars[1])
    solve(here, inv_full, total, noise)


def call(kernel, outs, scratch, small, arrays):
    return pl.pallas_call(
        kernel,
        out_shape=outs,
        in_specs=[SMEM] * len(small) + [VMEM] * len(arrays),
        out_specs=jax.tree.map(lambda _: VMEM, outs),
        scratch_shapes=scratch,
        compiler_params=pltpu.CompilerParams(vmem_limit_bytes=48 * 1024 * 1024),
    )(*small, *arrays)


def on_device(owners, draws, noise, inverse, coupling, picks, lists, counts):
    myself, draw = lax.axis_index("leaf"), lax.axis_index("draw")
    scalars = jnp.stack([myself, draw]).astype(jnp.int32)
    levels, nodes, rows, columns = noise.shape
    wide = columns // CHUNKS
    bf16, f32 = jnp.bfloat16, jnp.float32
    pieces = [
        [noise[level, :, :, at * wide:(at + 1) * wide] for at in range(CHUNKS)]
        for level in range(levels)
    ]
    tables = [exchange(piece, picks[0], myself, owners) for piece in pieces[0]]
    mine = jnp.take(inverse[0], picks[0][:, myself], axis=0)
    got = lax.all_to_all(mine, "leaf", split_axis=0, concat_axis=0, tiled=True)
    got = jnp.take(got, myself ^ jnp.arange(owners), axis=0)
    picked = gather_parts(got, "draw", draws)
    blocks = [gather_parts(coupling[0], "draw", draws)]
    inv = gather_parts(inverse, "draw", draws)
    blocks += [gather_parts(coupling[at], "draw", draws) for at in range(1, levels - 1)]
    inv_at = lambda level: [part[level] for part in inv]
    table_shape = pltpu.VMEM((owners, rows, wide), bf16)
    total_shape = pltpu.VMEM((nodes, rows, wide), f32)
    inv_shape = pltpu.VMEM((nodes, rows, rows), bf16)
    solved = [[], []]
    known = []
    for at in range(CHUNKS):
        part = jax.ShapeDtypeStruct((nodes, rows, wide), bf16)
        below, here, table = call(
            functools.partial(first_kernel, owners, draws),
            (part, part, jax.ShapeDtypeStruct((owners, rows, wide), bf16)),
            [pltpu.VMEM((owners, rows, rows), bf16), inv_shape, total_shape],
            (scalars, lists[0], counts[0]),
            (*tables[at], *picked, *inv_at(0), *inv_at(1), *blocks[0],
             pieces[0][at], pieces[1][at]),
        )
        solved[0].append(below)
        solved[1].append(here)
        known.append([table])
    for level in range(2, levels):
        fresh = [exchange(piece, picks[level - 1], myself, owners) for piece in solved[level - 1]]
        solved.append([])
        for at in range(CHUNKS):
            before = sum(
                call(
                    functools.partial(partial_kernel, source, draws),
                    jax.ShapeDtypeStruct((nodes, rows, wide), f32),
                    [],
                    (scalars, lists[level - 1], counts[level - 1]),
                    (*blocks[level - 1], known[at][source]),
                )
                for source in range(level - 1)
            )
            here = call(
                functools.partial(last_kernel, level - 1, owners, draws),
                jax.ShapeDtypeStruct((nodes, rows, wide), bf16),
                [table_shape, inv_shape, total_shape],
                (scalars, lists[level - 1], counts[level - 1]),
                (*fresh[at], *inv_at(level), *blocks[level - 1], before, pieces[level][at]),
            )
            solved[level].append(here)
            known[at].append(jnp.stack(fresh[at]))
    return jnp.stack([jnp.concatenate(parts, axis=2) for parts in solved])


def solution(mesh):
    placed = (
        P(None, "leaf", None, "draw"),
        P(None, "leaf", "draw", None),
        P(None, "leaf", "draw", None, None),
        P(),
        P(None, "leaf", None),
        P(None, "leaf"),
    )
    return jax.shard_map(
        functools.partial(on_device, mesh.shape["leaf"], mesh.shape["draw"]),
        mesh=mesh,
        in_specs=placed,
        out_specs=P(None, "leaf", None, "draw"),
        check_vma=False,
    )
```

time: 209 us -> 176 us (0.84)
  the two profiles are of different devices: /device:TPU:9 before, /device:TPU:0 now
where the time goes in v1:
time: 176 us; the launch traced here: 174 us
  starting transfers between devices  46.6 us (26%)
  local copies, waits for them, and re-layouts  46.4 us (26%)
  between operations  30.3 us (17%)
  waiting for transfers between devices  26.8 us (15%)
  Pallas kernels  19.9 us (11%)
  other arithmetic  3.63 us (2%)
    ppermute x40, starting transfers between devices, hop(): return lax.ppermute(value, axis, [(at, at ^ step) for at in range(size)])  42.8 us
    unnamed x128, local copies, waits for them, and re-layouts  29.4 us
    ppermute x40, waiting for transfers between devices, hop(): return lax.ppermute(value, axis, [(at, at ^ step) for at in range(size)])  26.8 us
    pallas_call x6, Pallas kernels, call(): pl.pallas_call(kernel, out_shape=outs, in_specs=[SMEM] * len(small) + [VM...  19.9 us
    squeeze x8, local copies, waits for them, and re-layouts, pick_block(): return lax.dynamic_index_in_dim(blocks, index, 0, keepdims=False)  5.46 us
    squeeze x4, local copies, waits for them, and re-layouts, on_device(): inv_at = lambda level: [part[level] for part in inv]  5.43 us
    all_to_all x1, starting transfers between devices, on_device(): got = lax.all_to_all(mine, 'leaf', split_axis=0, concat_axis=0, tiled=True)  3.81 us
  transfers between devices with their start and end apart: 41, of which 8 were waited for; matrix products, arithmetic and copies ran while one was open for 10% of the time, Pallas kernels for 10%

profile of v1, /device:TPU:0, one launch (start us, length us, event | category | flops | bytes accessed | tf_op | source)
XLA Modules:
  0.0 173.7 jit_solution(9517612567922167463)
XLA Ops:
  0.0 2.3 %slice_bitcast_fusion.3 = (bf16[2,256,256]{2,1,0:T(8,128)(2,1)}, bf16[2,256,256]{2,1,0:T(8,128)(2,1)S(1)}, bf16[2,256,256]{2,1,0:T(8,128)(2,1)S(1)}, bf16[2,256,...) fusion(bf16[3,2,256,512]{3,2,1,0:T(8,128)(2,1)} %param.6), kind=kLoop, calls=%fused_computation.9 | loop fusion | bytes 3670016 | tf_op jit(solution)/shard_map/squeeze | solution.py:139
  2.3 4.0 %collective-permute-start.3 = (bf16[2,256,256]{2,1,0:T(8,128)(2,1)S(1)}, bf16[2,256,256]{2,1,0:T(8,128)(2,1)S(1)}, u32[]{:S(2)}, u32[]{:S(2)}) collective-permute-start(bf16[2,256,256]{2,1,0:T(8,128)(2,1)S(1)} %get-tuple-element.18.refs_24_), channel_id=1, source_target_pairs={{0,16},{4,20},{8,24},{12,28},{16,0},{20,4},{24,8},{28,12},{1,17},{... | collective-permute-start | bytes 786440 | tf_op jit(solution)/shard_map/ppermute | solution.py:16
  15.6 1.5 collective-permute-start
  17.2 1.6 collective-permute-start.1
  19.1 1.5 collective-permute-start.11
  20.8 1.5 slice_bitcast_fusion.15
  23.8 3.8 %all-to-all-start = ((bf16[8,64,256]{2,1,0:T(8,128)(2,1)}), bf16[8,64,256]{2,1,0:T(8,128)(2,1)S(1)}, u32[]{:S(2)}, u32[]{:S(2)}) async-start(bf16[8,64,256]{2,1,0:T(8,128)(2,1)} %broadcast_select_fusion), calls=%async_computation | async-start | bytes 524288 | tf_op jit(solution)/shard_map/all_to_all | solution.py:144
  31.5 2.0 %collective-permute-start.16 = (bf16[256,256]{1,0:T(8,128)(2,1)}, bf16[256,256]{1,0:T(8,128)(2,1)S(1)}, u32[]{:S(2)}, u32[]{:S(2)}) collective-permute-start(bf16[256,256]{1,0:T(8,128)(2,1)} %get-tuple-element.57), channel_id=1, source_target_pairs={{0,4},{4,0},{8,12},{12,8},{16,20},{20,16},{24,28},{28,24},{1,5},{5... | collective-permute-start | bytes 393224 | tf_op jit(solution)/shard_map/ppermute | solution.py:16
  41.7 2.4 %collective-permute-start.19 = (bf16[2,256,256]{2,1,0:T(8,128)(2,1)S(1)}, bf16[2,256,256]{2,1,0:T(8,128)(2,1)}, u32[]{:S(2)}, u32[]{:S(2)}) collective-permute-start(bf16[2,256,256]{2,1,0:T(8,128)(2,1)S(1)} %get-tuple-element.19.refs_24_), channel_id=1, source_target_pairs={{0,16},{4,20},{8,24},{12,28},{16,0},{20,4},{24,8},{28,12},{1,17},{... | collective-permute-start | bytes 786440 | tf_op jit(solution)/shard_map/ppermute | solution.py:16
  49.8 6.9 %collective-permute-done.19 = bf16[2,256,256]{2,1,0:T(8,128)(2,1)} collective-permute-done((bf16[2,256,256]{2,1,0:T(8,128)(2,1)S(1)}, bf16[2,256,256]{2,1,0:T(8,128)(2,1)}, u32[]{:S(2)}, u32[]{:S(2)}) %collective-permute-start.19) | collective-permute-done | bytes 262176 | tf_op jit(solution)/shard_map/ppermute | solution.py:16
  59.4 1.5 slice_bitcast_fusion.7
  61.2 4.7 %collective-permute-done.8.refs_10_ = bf16[8,64,256]{2,1,0:T(8,128)(2,1)S(1)} collective-permute-done((bf16[8,64,256]{2,1,0:T(8,128)(2,1)S(1)}, bf16[8,64,256]{2,1,0:T(8,128)(2,1)S(1)}, u32[]{:S(2)}, u32[]{:S(2)}) %collective-permute-start.8) | collective-permute-done | bytes 262176 | tf_op jit(solution)/shard_map/ppermute | solution.py:16
  65.9 1.6 slice_bitcast_fusion.8
  67.5 1.9 %dynamic-slice_bitcast_fusion.16 = (bf16[256,256]{1,0:T(8,128)(2,1)}, bf16[256,256]{1,0:T(8,128)(2,1)}, bf16[256,256]{1,0:T(8,128)(2,1)S(1)}, bf16[256,256]{1,0:T(8,128)(2,1)}) fusion(bf16[2,256,256]{2,1,0:T(8,128)(2,1)} %collective-permute-done.19, s32[]{:T(128)S(6)} %select_n.191, s32[]{:T(128)S(6)} %select_n.190, s32[]{:T(128)S(6)} %select_n.189, ...), kind=kLoop, calls=%fused_computation.30 | loop fusion | bytes 1048592 | tf_op jit(solution)/shard_map/jit(dynamic_index_in_dim)/squeeze | solution.py:36
  69.9 5.2 %collective-permute-done.31.refs_2_.refs_14_ = bf16[2,2,256,256]{3,2,1,0:T(8,128)(2,1)S(1)} collective-permute-done((bf16[2,2,256,256]{3,2,1,0:T(8,128)(2,1)S(1)}, bf16[2,2,256,256]{3,2,1,0:T(8,128)(2,1)S(1)}, u32[]{:S(2)}, u32[]{:S(2)}) %collective-permute-start.31) | collective-permute-done | bytes 524320 | tf_op jit(solution)/shard_map/ppermute | solution.py:16
  85.7 5.1 %shard_map.64 = (bf16[2,256,256]{2,1,0:T(8,128)(2,1)S(1)}, bf16[2,256,256]{2,1,0:T(8,128)(2,1)S(1)}, bf16[8,256,256]{2,1,0:T(8,128)(2,1)}) custom-call(s32[2]{0:T(128)S(1)} %pad_add_fusion.scalars, s32[2,8]{1,0:T(2,128)S(1)} %get-tuple-element.89.lists, s32[2]{0:T(128)S(1)} %copy-done.59, bf16[256,256]{1,0:T(8,128)(2,1)S(1)} %copy-done.40, ...), custom_call_target="tpu_custom_call" | custom-call | tf_op jit(solution)/shard_map/pallas_call | solution.py:122
  92.2 2.4 %collective-permute-start.26 = (bf16[2,256,256]{2,1,0:T(8,128)(2,1)S(1)}, bf16[2,256,256]{2,1,0:T(8,128)(2,1)}, u32[]{:S(2)}, u32[]{:S(2)}) collective-permute-start(bf16[2,256,256]{2,1,0:T(8,128)(2,1)S(1)} %get-tuple-element.13), channel_id=1, source_target_pairs={{0,16},{4,20},{8,24},{12,28},{16,0},{20,4},{24,8},{28,12},{1,17},{... | collective-permute-start | bytes 786440 | tf_op jit(solution)/shard_map/ppermute | solution.py:16
  95.3 2.0 %collective-permute-start.21 = (bf16[256,256]{1,0:T(8,128)(2,1)}, bf16[256,256]{1,0:T(8,128)(2,1)}, u32[]{:S(2)}, u32[]{:S(2)}) collective-permute-start(bf16[256,256]{1,0:T(8,128)(2,1)} %get-tuple-element.52), channel_id=1, source_target_pairs={{0,8},{4,12},{8,0},{12,4},{16,24},{20,28},{24,16},{28,20},{1,9},{5... | collective-permute-start | bytes 393224 | tf_op jit(solution)/shard_map/ppermute | solution.py:16
  132.4 5.5 %shard_map.65 = (bf16[2,256,256]{2,1,0:T(8,128)(2,1)S(1)}, bf16[2,256,256]{2,1,0:T(8,128)(2,1)S(1)}, bf16[8,256,256]{2,1,0:T(8,128)(2,1)}) custom-call(s32[2]{0:T(128)S(1)} %pad_add_fusion.scalars, s32[2,8]{1,0:T(2,128)S(1)} %get-tuple-element.89.lists, s32[2]{0:T(128)S(1)} %copy-done.60, bf16[256,256]{1,0:T(8,128)(2,1)S(1)} %copy-done.39, ...), custom_call_target="tpu_custom_call" | custom-call | tf_op jit(solution)/shard_map/pallas_call | solution.py:122
  138.0 1.7 collective-permute-start.23
  142.9 1.6 collective-permute-start.33
  144.9 2.6 %collective-permute-done.24.refs_2_ = bf16[256,256]{1,0:T(8,128)(2,1)S(1)} collective-permute-done((bf16[256,256]{1,0:T(8,128)(2,1)S(1)}, bf16[256,256]{1,0:T(8,128)(2,1)S(1)}, u32[]{:S(2)}, u32[]{:S(2)}) %collective-permute-start.24) | collective-permute-done | bytes 131104 | tf_op jit(solution)/shard_map/ppermute | solution.py:16
  147.5 2.5 %collective-permute-start.28 = (bf16[256,256]{1,0:T(8,128)(2,1)S(1)}, bf16[256,256]{1,0:T(8,128)(2,1)S(1)}, u32[]{:S(2)}, u32[]{:S(2)}) collective-permute-start(bf16[256,256]{1,0:T(8,128)(2,1)S(1)} %get-tuple-element.28), channel_id=1, source_target_pairs={{0,8},{4,12},{8,0},{12,4},{16,24},{20,28},{24,16},{28,20},{1,9},{5... | collective-permute-start | bytes 393224 | tf_op jit(solution)/shard_map/ppermute | solution.py:16
  149.9 2.5 %collective-permute-done.36 = bf16[2,256,256]{2,1,0:T(8,128)(2,1)S(1)} collective-permute-done((bf16[2,256,256]{2,1,0:T(8,128)(2,1)S(1)}, bf16[2,256,256]{2,1,0:T(8,128)(2,1)S(1)}, u32[]{:S(2)}, u32[]{:S(2)}) %collective-permute-start.36) | collective-permute-done | bytes 262176 | tf_op jit(solution)/shard_map/ppermute | solution.py:16
  152.5 1.8 %collective-permute-start.34 = (bf16[256,256]{1,0:T(8,128)(2,1)S(1)}, bf16[256,256]{1,0:T(8,128)(2,1)S(1)}, u32[]{:S(2)}, u32[]{:S(2)}) collective-permute-start(bf16[256,256]{1,0:T(8,128)(2,1)S(1)} %get-tuple-element.48), channel_id=1, source_target_pairs={{0,8},{4,12},{8,0},{12,4},{16,24},{20,28},{24,16},{28,20},{1,9},{5... | collective-permute-start | bytes 393224 | tf_op jit(solution)/shard_map/ppermute | solution.py:16
  156.2 1.7 collective-permute-start.38
  157.8 2.1 %collective-permute-done.29.refs_7_ = bf16[256,256]{1,0:T(8,128)(2,1)S(1)} collective-permute-done((bf16[256,256]{1,0:T(8,128)(2,1)S(1)}, bf16[256,256]{1,0:T(8,128)(2,1)S(1)}, u32[]{:S(2)}, u32[]{:S(2)}) %collective-permute-start.29) | collective-permute-done | bytes 131104 | tf_op jit(solution)/shard_map/ppermute | solution.py:16
  160.0 1.7 shard_map.66.refs_16_
  161.7 1.8 %shard_map.68.refs_16_ = f32[2,256,256]{2,1,0:T(8,128)S(1)} custom-call(s32[2]{0:T(128)S(1)} %pad_add_fusion.scalars, s32[2,8]{1,0:T(2,128)S(1)} %get-tuple-element.90.lists, s32[2]{0:T(128)S(1)} %get-tuple-element.92.counts, bf16[2,2,256,256]{3,2,1,0:T(8,128)(2,1)S(1)} %get-tuple-element.25.refs_0_.refs_12_, ...), custom_call_target="tpu_custom_call" | custom-call | tf_op jit(solution)/shard_map/pallas_call | solution.py:122
  163.6 3.0 %shard_map.67 = bf16[2,256,256]{2,1,0:T(8,128)(2,1)S(1)} custom-call(s32[2]{0:T(128)S(1)} %pad_add_fusion.scalars, s32[2,8]{1,0:T(2,128)S(1)} %get-tuple-element.90.lists, s32[2]{0:T(128)S(1)} %get-tuple-element.92.counts, bf16[256,256]{1,0:T(8,128)(2,1)S(1)} %get-tuple-element.34.refs_0_, bf16[256,256]{1,0:T(8,128)(2,1)S(1)} %collective-permute-done.23.refs_1_, ...), custom_call_target="tpu_custom_call" | custom-call | tf_op jit(solution)/shard_map/pallas_call | solution.py:122
  167.0 2.3 %collective-permute-done.39.refs_7_ = bf16[256,256]{1,0:T(8,128)(2,1)S(1)} collective-permute-done((bf16[256,256]{1,0:T(8,128)(2,1)S(1)}, bf16[256,256]{1,0:T(8,128)(2,1)S(1)}, u32[]{:S(2)}, u32[]{:S(2)}) %collective-permute-start.39) | collective-permute-done | bytes 131104 | tf_op jit(solution)/shard_map/ppermute | solution.py:16
  169.4 2.9 %shard_map.69 = bf16[2,256,256]{2,1,0:T(8,128)(2,1)S(1)} custom-call(s32[2]{0:T(128)S(1)} %pad_add_fusion.scalars, s32[2,8]{1,0:T(2,128)S(1)} %get-tuple-element.90.lists, s32[2]{0:T(128)S(1)} %get-tuple-element.92.counts, bf16[256,256]{1,0:T(8,128)(2,1)S(1)} %get-tuple-element.50.refs_0_, bf16[256,256]{1,0:T(8,128)(2,1)S(1)} %collective-permute-done.33.refs_1_, ...), custom_call_target="tpu_custom_call" | custom-call | tf_op jit(solution)/shard_map/pallas_call | solution.py:122
  (218 shorter events, 57.9 us)
Async XLA Ops:
  2.3 39.4 %collective-permute-start.3 = (bf16[2,256,256]{2,1,0:T(8,128)(2,1)S(1)}, bf16[2,256,256]{2,1,0:T(8,128)(2,1)S(1)}, u32[]{:S(2)}, u32[]{:S(2)}) collective-permute-start(bf16[2,256,256]{2,1,0:T(8,128)(2,1)S(1)} %get-tuple-element.18.refs_24_), channel_id=1, source_target_pairs={{0,16},{4,20},{8,24},{12,28},{16,0},{20,4},{24,8},{28,12},{1,17},{... | collective-permute-start | bytes 786440 | tf_op jit(solution)/shard_map/ppermute | solution.py:16
  15.6 14.6 %collective-permute-start = (bf16[256,256]{1,0:T(8,128)(2,1)S(1)}, bf16[256,256]{1,0:T(8,128)(2,1)S(1)}, u32[]{:S(2)}, u32[]{:S(2)}) collective-permute-start(bf16[256,256]{1,0:T(8,128)(2,1)S(1)} %get-tuple-element.41), channel_id=1, source_target_pairs={{0,4},{4,0},{8,12},{12,8},{16,20},{20,16},{24,28},{28,24},{1,5},{5... | collective-permute-start | bytes 393224 | tf_op jit(solution)/shard_map/ppermute | solution.py:16
  17.2 13.7 %collective-permute-start.1 = (bf16[256,256]{1,0:T(8,128)(2,1)S(1)}, bf16[256,256]{1,0:T(8,128)(2,1)S(1)}, u32[]{:S(2)}, u32[]{:S(2)}) collective-permute-start(bf16[256,256]{1,0:T(8,128)(2,1)S(1)} %get-tuple-element.40), channel_id=1, source_target_pairs={{0,8},{4,12},{8,0},{12,4},{16,24},{20,28},{24,16},{28,20},{1,9},{5... | collective-permute-start | bytes 393224 | tf_op jit(solution)/shard_map/ppermute | solution.py:16
  18.7 12.7 %collective-permute-start.2 = (bf16[256,256]{1,0:T(8,128)(2,1)}, bf16[256,256]{1,0:T(8,128)(2,1)S(1)}, u32[]{:S(2)}, u32[]{:S(2)}) collective-permute-start(bf16[256,256]{1,0:T(8,128)(2,1)} %get-tuple-element.39), channel_id=1, source_target_pairs={{0,12},{4,8},{8,4},{12,0},{16,28},{20,24},{24,20},{28,16},{1,13},{... | collective-permute-start | bytes 393224 | tf_op jit(solution)/shard_map/ppermute | solution.py:16
  19.1 27.0 %collective-permute-start.11 = (bf16[3,2,64,256]{3,2,1,0:T(8,128)(2,1)}, bf16[3,2,64,256]{3,2,1,0:T(8,128)(2,1)}, u32[]{:S(2)}, u32[]{:S(2)}) collective-permute-start(bf16[3,2,64,256]{3,2,1,0:T(8,128)(2,1)} %param.7), channel_id=1, source_target_pairs={{0,2},{1,3},{2,0},{3,1},{4,6},{5,7},{6,4},{7,5},{8,10},{9,11},{10,... | collective-permute-start | bytes 589832 | tf_op jit(solution)/shard_map/ppermute | solution.py:16
  23.8 21.1 %all-to-all-start = ((bf16[8,64,256]{2,1,0:T(8,128)(2,1)}), bf16[8,64,256]{2,1,0:T(8,128)(2,1)S(1)}, u32[]{:S(2)}, u32[]{:S(2)}) async-start(bf16[8,64,256]{2,1,0:T(8,128)(2,1)} %broadcast_select_fusion), calls=%async_computation | async-start | bytes 524288 | tf_op jit(solution)/shard_map/all_to_all | solution.py:144
  30.8 16.7 %collective-permute-start.10 = (bf16[3,2,64,256]{3,2,1,0:T(8,128)(2,1)}, bf16[3,2,64,256]{3,2,1,0:T(8,128)(2,1)}, u32[]{:S(2)}, u32[]{:S(2)}) collective-permute-start(bf16[3,2,64,256]{3,2,1,0:T(8,128)(2,1)} %param.7), channel_id=1, source_target_pairs={{0,1},{1,0},{2,3},{3,2},{4,5},{5,4},{6,7},{7,6},{8,9},{9,8},{10,11... | collective-permute-start | bytes 589832 | tf_op jit(solution)/shard_map/ppermute | solution.py:16
  30.9 28.2 %collective-permute-start.14 = (bf16[2,2,256,256]{3,2,1,0:T(8,128)(2,1)S(1)}, bf16[2,2,256,256]{3,2,1,0:T(8,128)(2,1)S(1)}, u32[]{:S(2)}, u32[]{:S(2)}) collective-permute-start(bf16[2,2,256,256]{3,2,1,0:T(8,128)(2,1)S(1)} %get-tuple-element.26.refs_20_), channel_id=1, source_target_pairs={{0,2},{1,3},{2,0},{3,1},{4,6},{5,7},{6,4},{7,5},{8,10},{9,11},{10,... | collective-permute-start | bytes 1572872 | tf_op jit(solution)/shard_map/ppermute | solution.py:16
  31.5 14.0 %collective-permute-start.16 = (bf16[256,256]{1,0:T(8,128)(2,1)}, bf16[256,256]{1,0:T(8,128)(2,1)S(1)}, u32[]{:S(2)}, u32[]{:S(2)}) collective-permute-start(bf16[256,256]{1,0:T(8,128)(2,1)} %get-tuple-element.57), channel_id=1, source_target_pairs={{0,4},{4,0},{8,12},{12,8},{16,20},{20,16},{24,28},{28,24},{1,5},{5... | collective-permute-start | bytes 393224 | tf_op jit(solution)/shard_map/ppermute | solution.py:16
  41.7 14.9 %collective-permute-start.19 = (bf16[2,256,256]{2,1,0:T(8,128)(2,1)S(1)}, bf16[2,256,256]{2,1,0:T(8,128)(2,1)}, u32[]{:S(2)}, u32[]{:S(2)}) collective-permute-start(bf16[2,256,256]{2,1,0:T(8,128)(2,1)S(1)} %get-tuple-element.19.refs_24_), channel_id=1, source_target_pairs={{0,16},{4,20},{8,24},{12,28},{16,0},{20,4},{24,8},{28,12},{1,17},{... | collective-permute-start | bytes 786440 | tf_op jit(solution)/shard_map/ppermute | solution.py:16
  45.5 12.7 %collective-permute-start.4 = (bf16[256,256]{1,0:T(8,128)(2,1)S(1)}, bf16[256,256]{1,0:T(8,128)(2,1)S(1)}, u32[]{:S(2)}, u32[]{:S(2)}) collective-permute-start(bf16[256,256]{1,0:T(8,128)(2,1)S(1)} %get-tuple-element.37), channel_id=1, source_target_pairs={{0,4},{4,0},{8,12},{12,8},{16,20},{20,16},{24,28},{28,24},{1,5},{5... | collective-permute-start | bytes 393224 | tf_op jit(solution)/shard_map/ppermute | solution.py:16
  46.1 12.1 %collective-permute-start.5 = (bf16[256,256]{1,0:T(8,128)(2,1)S(1)}, bf16[256,256]{1,0:T(8,128)(2,1)S(1)}, u32[]{:S(2)}, u32[]{:S(2)}) collective-permute-start(bf16[256,256]{1,0:T(8,128)(2,1)S(1)} %get-tuple-element.36), channel_id=1, source_target_pairs={{0,8},{4,12},{8,0},{12,4},{16,24},{20,28},{24,16},{28,20},{1,9},{5... | collective-permute-start | bytes 393224 | tf_op jit(solution)/shard_map/ppermute | solution.py:16
  47.6 11.3 %collective-permute-start.6 = (bf16[256,256]{1,0:T(8,128)(2,1)S(1)}, bf16[256,256]{1,0:T(8,128)(2,1)S(1)}, u32[]{:S(2)}, u32[]{:S(2)}) collective-permute-start(bf16[256,256]{1,0:T(8,128)(2,1)S(1)} %get-tuple-element.35), channel_id=1, source_target_pairs={{0,12},{4,8},{8,4},{12,0},{16,28},{20,24},{24,20},{28,16},{1,13},{... | collective-permute-start | bytes 393224 | tf_op jit(solution)/shard_map/ppermute | solution.py:16
  58.2 11.2 %collective-permute-start.13 = (bf16[2,2,256,256]{3,2,1,0:T(8,128)(2,1)S(1)}, bf16[2,2,256,256]{3,2,1,0:T(8,128)(2,1)S(1)}, u32[]{:S(2)}, u32[]{:S(2)}) collective-permute-start(bf16[2,2,256,256]{3,2,1,0:T(8,128)(2,1)S(1)} %get-tuple-element.26.refs_20_), channel_id=1, source_target_pairs={{0,1},{1,0},{2,3},{3,2},{4,5},{5,4},{6,7},{7,6},{8,9},{9,8},{10,11... | collective-permute-start | bytes 1572872 | tf_op jit(solution)/shard_map/ppermute | solution.py:16
  58.3 16.8 %collective-permute-start.31 = (bf16[2,2,256,256]{3,2,1,0:T(8,128)(2,1)S(1)}, bf16[2,2,256,256]{3,2,1,0:T(8,128)(2,1)S(1)}, u32[]{:S(2)}, u32[]{:S(2)}) collective-permute-start(bf16[2,2,256,256]{3,2,1,0:T(8,128)(2,1)S(1)} %get-tuple-element.25.refs_0_.refs_12_), channel_id=1, source_target_pairs={{0,2},{1,3},{2,0},{3,1},{4,6},{5,7},{6,4},{7,5},{8,10},{9,11},{10,... | collective-permute-start | bytes 1572872 | tf_op jit(solution)/shard_map/ppermute | solution.py:16
  59.1 19.5 %collective-permute-start.15 = (bf16[2,2,256,256]{3,2,1,0:T(8,128)(2,1)S(1)}, bf16[2,2,256,256]{3,2,1,0:T(8,128)(2,1)S(1)}, u32[]{:S(2)}, u32[]{:S(2)}) collective-permute-start(bf16[2,2,256,256]{3,2,1,0:T(8,128)(2,1)S(1)} %collective-permute-done.14.refs_22_), channel_id=1, source_target_pairs={{0,1},{1,0},{2,3},{3,2},{4,5},{5,4},{6,7},{7,6},{8,9},{9,8},{10,11... | collective-permute-start | bytes 1572872 | tf_op jit(solution)/shard_map/ppermute | solution.py:16
  60.9 15.4 %collective-permute-start.7 = (bf16[8,64,256]{2,1,0:T(8,128)(2,1)S(1)}, bf16[8,64,256]{2,1,0:T(8,128)(2,1)S(1)}, u32[]{:S(2)}, u32[]{:S(2)}) collective-permute-start(bf16[8,64,256]{2,1,0:T(8,128)(2,1)S(1)} %broadcast_select_fusion.1.refs_8_), channel_id=1, source_target_pairs={{0,1},{1,0},{2,3},{3,2},{4,5},{5,4},{6,7},{7,6},{8,9},{9,8},{10,11... | collective-permute-start | bytes 786440 | tf_op jit(solution)/shard_map/ppermute | solution.py:16
  65.9 11.3 %collective-permute-start.9 = (bf16[8,64,256]{2,1,0:T(8,128)(2,1)S(1)}, bf16[8,64,256]{2,1,0:T(8,128)(2,1)S(1)}, u32[]{:S(2)}, u32[]{:S(2)}) collective-permute-start(bf16[8,64,256]{2,1,0:T(8,128)(2,1)S(1)} %collective-permute-done.8.refs_10_), channel_id=1, source_target_pairs={{0,1},{1,0},{2,3},{3,2},{4,5},{5,4},{6,7},{7,6},{8,9},{9,8},{10,11... | collective-permute-start | bytes 786440 | tf_op jit(solution)/shard_map/ppermute | solution.py:16
  69.4 72.9 %collective-permute-start.30 = (bf16[2,2,256,256]{3,2,1,0:T(8,128)(2,1)S(1)}, bf16[2,2,256,256]{3,2,1,0:T(8,128)(2,1)S(1)}, u32[]{:S(2)}, u32[]{:S(2)}) collective-permute-start(bf16[2,2,256,256]{3,2,1,0:T(8,128)(2,1)S(1)} %get-tuple-element.25.refs_0_.refs_12_), channel_id=1, source_target_pairs={{0,1},{1,0},{2,3},{3,2},{4,5},{5,4},{6,7},{7,6},{8,9},{9,8},{10,11... | collective-permute-start | bytes 1572872 | tf_op jit(solution)/shard_map/ppermute | solution.py:16
  75.1 16.5 %collective-permute-start.17 = (bf16[256,256]{1,0:T(8,128)(2,1)}, bf16[256,256]{1,0:T(8,128)(2,1)S(1)}, u32[]{:S(2)}, u32[]{:S(2)}) collective-permute-start(bf16[256,256]{1,0:T(8,128)(2,1)} %get-tuple-element.56), channel_id=1, source_target_pairs={{0,8},{4,12},{8,0},{12,4},{16,24},{20,28},{24,16},{28,20},{1,9},{5... | collective-permute-start | bytes 393224 | tf_op jit(solution)/shard_map/ppermute | solution.py:16
  76.4 18.2 %collective-permute-start.18 = (bf16[256,256]{1,0:T(8,128)(2,1)}, bf16[256,256]{1,0:T(8,128)(2,1)S(1)}, u32[]{:S(2)}, u32[]{:S(2)}) collective-permute-start(bf16[256,256]{1,0:T(8,128)(2,1)} %get-tuple-element.55), channel_id=1, source_target_pairs={{0,12},{4,8},{8,4},{12,0},{16,28},{20,24},{24,20},{28,16},{1,13},{... | collective-permute-start | bytes 393224 | tf_op jit(solution)/shard_map/ppermute | solution.py:16
  77.1 20.1 %collective-permute-start.20 = (bf16[256,256]{1,0:T(8,128)(2,1)S(1)}, bf16[256,256]{1,0:T(8,128)(2,1)S(1)}, u32[]{:S(2)}, u32[]{:S(2)}) collective-permute-start(bf16[256,256]{1,0:T(8,128)(2,1)S(1)} %get-tuple-element.53), channel_id=1, source_target_pairs={{0,4},{4,0},{8,12},{12,8},{16,20},{20,16},{24,28},{28,24},{1,5},{5... | collective-permute-start | bytes 393224 | tf_op jit(solution)/shard_map/ppermute | solution.py:16
  78.6 64.2 %collective-permute-start.32 = (bf16[2,2,256,256]{3,2,1,0:T(8,128)(2,1)S(1)}, bf16[2,2,256,256]{3,2,1,0:T(8,128)(2,1)S(1)}, u32[]{:S(2)}, u32[]{:S(2)}) collective-permute-start(bf16[2,2,256,256]{3,2,1,0:T(8,128)(2,1)S(1)} %collective-permute-done.31.refs_2_.refs_14_), channel_id=1, source_target_pairs={{0,1},{1,0},{2,3},{3,2},{4,5},{5,4},{6,7},{7,6},{8,9},{9,8},{10,11... | collective-permute-start | bytes 1572872 | tf_op jit(solution)/shard_map/ppermute | solution.py:16
  92.2 47.4 %collective-permute-start.26 = (bf16[2,256,256]{2,1,0:T(8,128)(2,1)S(1)}, bf16[2,256,256]{2,1,0:T(8,128)(2,1)}, u32[]{:S(2)}, u32[]{:S(2)}) collective-permute-start(bf16[2,256,256]{2,1,0:T(8,128)(2,1)S(1)} %get-tuple-element.13), channel_id=1, source_target_pairs={{0,16},{4,20},{8,24},{12,28},{16,0},{20,4},{24,8},{28,12},{1,17},{... | collective-permute-start | bytes 786440 | tf_op jit(solution)/shard_map/ppermute | solution.py:16
  95.3 17.4 %collective-permute-start.21 = (bf16[256,256]{1,0:T(8,128)(2,1)}, bf16[256,256]{1,0:T(8,128)(2,1)}, u32[]{:S(2)}, u32[]{:S(2)}) collective-permute-start(bf16[256,256]{1,0:T(8,128)(2,1)} %get-tuple-element.52), channel_id=1, source_target_pairs={{0,8},{4,12},{8,0},{12,4},{16,24},{20,28},{24,16},{28,20},{1,9},{5... | collective-permute-start | bytes 393224 | tf_op jit(solution)/shard_map/ppermute | solution.py:16
  97.9 14.8 %collective-permute-start.22 = (bf16[256,256]{1,0:T(8,128)(2,1)}, bf16[256,256]{1,0:T(8,128)(2,1)}, u32[]{:S(2)}, u32[]{:S(2)}) collective-permute-start(bf16[256,256]{1,0:T(8,128)(2,1)} %get-tuple-element.51), channel_id=1, source_target_pairs={{0,12},{4,8},{8,4},{12,0},{16,28},{20,24},{24,20},{28,16},{1,13},{... | collective-permute-start | bytes 393224 | tf_op jit(solution)/shard_map/ppermute | solution.py:16
  137.9 14.6 %collective-permute-start.36 = (bf16[2,256,256]{2,1,0:T(8,128)(2,1)S(1)}, bf16[2,256,256]{2,1,0:T(8,128)(2,1)S(1)}, u32[]{:S(2)}, u32[]{:S(2)}) collective-permute-start(bf16[2,256,256]{2,1,0:T(8,128)(2,1)S(1)} %get-tuple-element.14), channel_id=1, source_target_pairs={{0,16},{4,20},{8,24},{12,28},{16,0},{20,4},{24,8},{28,12},{1,17},{... | collective-permute-start | bytes 786440 | tf_op jit(solution)/shard_map/ppermute | solution.py:16
  142.9 11.5 %collective-permute-start.33 = (bf16[256,256]{1,0:T(8,128)(2,1)S(1)}, bf16[256,256]{1,0:T(8,128)(2,1)S(1)}, u32[]{:S(2)}, u32[]{:S(2)}) collective-permute-start(bf16[256,256]{1,0:T(8,128)(2,1)S(1)} %get-tuple-element.49), channel_id=1, source_target_pairs={{0,4},{4,0},{8,12},{12,8},{16,20},{20,16},{24,28},{28,24},{1,5},{5... | collective-permute-start | bytes 393224 | tf_op jit(solution)/shard_map/ppermute | solution.py:16
  144.5 11.1 %collective-permute-start.27 = (bf16[256,256]{1,0:T(8,128)(2,1)S(1)}, bf16[256,256]{1,0:T(8,128)(2,1)S(1)}, u32[]{:S(2)}, u32[]{:S(2)}) collective-permute-start(bf16[256,256]{1,0:T(8,128)(2,1)S(1)} %get-tuple-element.29), channel_id=1, source_target_pairs={{0,4},{4,0},{8,12},{12,8},{16,20},{20,16},{24,28},{28,24},{1,5},{5... | collective-permute-start | bytes 393224 | tf_op jit(solution)/shard_map/ppermute | solution.py:16
  152.5 14.1 %collective-permute-start.34 = (bf16[256,256]{1,0:T(8,128)(2,1)S(1)}, bf16[256,256]{1,0:T(8,128)(2,1)S(1)}, u32[]{:S(2)}, u32[]{:S(2)}) collective-permute-start(bf16[256,256]{1,0:T(8,128)(2,1)S(1)} %get-tuple-element.48), channel_id=1, source_target_pairs={{0,8},{4,12},{8,0},{12,4},{16,24},{20,28},{24,16},{28,20},{1,9},{5... | collective-permute-start | bytes 393224 | tf_op jit(solution)/shard_map/ppermute | solution.py:16
  154.3 12.3 %collective-permute-start.35 = (bf16[256,256]{1,0:T(8,128)(2,1)S(1)}, bf16[256,256]{1,0:T(8,128)(2,1)S(1)}, u32[]{:S(2)}, u32[]{:S(2)}) collective-permute-start(bf16[256,256]{1,0:T(8,128)(2,1)S(1)} %get-tuple-element.47), channel_id=1, source_target_pairs={{0,12},{4,8},{8,4},{12,0},{16,28},{20,24},{24,20},{28,16},{1,13},{... | collective-permute-start | bytes 393224 | tf_op jit(solution)/shard_map/ppermute | solution.py:16
  155.6 11.0 %collective-permute-start.37 = (bf16[256,256]{1,0:T(8,128)(2,1)S(1)}, bf16[256,256]{1,0:T(8,128)(2,1)S(1)}, u32[]{:S(2)}, u32[]{:S(2)}) collective-permute-start(bf16[256,256]{1,0:T(8,128)(2,1)S(1)} %get-tuple-element.45), channel_id=1, source_target_pairs={{0,4},{4,0},{8,12},{12,8},{16,20},{20,16},{24,28},{28,24},{1,5},{5... | collective-permute-start | bytes 393224 | tf_op jit(solution)/shard_map/ppermute | solution.py:16
  (73 other events, 589.8 us)

commit v2 on v0

v2 whole, which is shorter than its diff:
```python
import functools

import jax
import jax.numpy as jnp
from jax import lax
from jax.experimental import pallas as pl
from jax.experimental.pallas import tpu as pltpu
from jax.sharding import PartitionSpec as P

CHUNKS = 2
ANY = pl.BlockSpec(memory_space=pl.ANY)
SMEM = pl.BlockSpec(memory_space=pltpu.SMEM)
BF16, F32 = jnp.bfloat16, jnp.float32


def hop(value, axis, size, step):
    return lax.ppermute(value, axis, [(at, at ^ step) for at in range(size)])


def transposed_dot(left, right):
    return lax.dot_general(left, right, (((0,), (0,)), ((), ())), preferred_element_type=F32)


class Copies:
    def __init__(self, sems):
        self.sems, self.used = sems, 0

    def start(self, source, target):
        copy = pltpu.make_async_copy(source, target, self.sems.at[self.used])
        self.used += 1
        copy.start()
        return copy


def wait_all(copies):
    for copy in copies:
        copy.wait()


def load_rows(copies, target, parts):
    draws, _, rows, _ = parts.shape
    return [
        copies.start(parts.at[at], target.at[:, pl.ds(at * rows, rows), :])
        for at in range(draws)
    ]


def add_slots(total, table, blocks, lists, counts, source, myself):
    owners = table.shape[0]
    draws, nodes, width = blocks.shape[:3]
    for part in range(draws):
        for offset in range(width):
            slot = part * width + offset
            for node in range(nodes):
                entry = lists(node, slot) - source * owners
                live = (slot < counts(node)) & (entry >= 0) & (entry < owners)

                @pl.when(live)
                def _():
                    total[node] += transposed_dot(
                        blocks[part, node, offset], table[entry ^ myself]
                    )


def call(kernel, outs, scratch, small, arrays, aliases={}, sems=64, flops=0):
    return pl.pallas_call(
        kernel,
        out_shape=outs,
        in_specs=[SMEM] * len(small) + [ANY] * len(arrays),
        out_specs=jax.tree.map(lambda _: ANY, outs),
        scratch_shapes=[*scratch, pltpu.SemaphoreType.DMA((sems,))],
        input_output_aliases=aliases,
        compiler_params=pltpu.CompilerParams(vmem_limit_bytes=24 * 1024 * 1024),
    )(*small, *arrays)


def here_pick(picks, source, myself, step, origin):
    return picks[source, myself ^ step, myself ^ origin]


def own_first(owners, wide, picks, noise, inverse, *refs):
    out, own, *rest = refs
    sends, (right, inv, solved, sems) = rest[:-4], rest[-4:]
    myself = lax.axis_index("leaf")
    copies = Copies(sems)
    loads = [copies.start(noise.at[0], right)] + load_rows(copies, inv, inverse.at[:, 0])
    wait_all(loads)
    for node in range(inv.shape[0]):
        solved[node] = transposed_dot(inv[node], right[node]).astype(BF16)
    stores = [copies.start(solved, out.at[0]), copies.start(solved, own)]
    for step, send in enumerate(sends, 1):
        node = here_pick(picks, 0, myself, step, 0)
        stores.append(copies.start(solved.at[node, :, pl.ds(0, wide)], send))
    wait_all(stores)


def far_first(owners, wide, chunk, last, picks, far, inverse, own, *refs):
    half = owners // 2
    mine, *rest = refs
    sends, (right, inv, solved, sems) = rest[:-4], rest[-4:]
    myself = lax.axis_index("leaf")
    copies = Copies(sems)
    loads = [copies.start(far, right)] + load_rows(copies, inv, inverse)
    stores = []
    if not last:
        columns = pl.ds((chunk + 1) * wide, wide)
        for step, send in enumerate(sends, 1):
            node = here_pick(picks, 0, myself, step, 0)
            stores.append(copies.start(own.at[node, :, columns], send.at[1]))
    wait_all(loads)
    for node in range(inv.shape[0]):
        solved[node] = transposed_dot(inv[node], right[node]).astype(BF16)
    stores.append(copies.start(solved.at[here_pick(picks, 0, myself, 0, half)], mine))
    for step, send in enumerate(sends, 1):
        node = here_pick(picks, 0, myself, step, half)
        stores.append(copies.start(solved.at[node], send.at[0]))
    wait_all(stores)


def far_next(owners, source, last, picks, far, *refs):
    half = owners // 2
    own, refs = (None, refs) if last else (refs[0], refs[1:])
    sends, sems = refs[:-1], refs[-1]
    myself = lax.axis_index("leaf")
    copies = Copies(sems)
    stores = []
    for step, send in enumerate(sends, 1):
        node = here_pick(picks, source, myself, step, half)
        stores.append(copies.start(far.at[node], send.at[0]))
        if not last:
            node = here_pick(picks, source, myself, step, 0)
            stores.append(copies.start(own.at[node], send.at[1]))
    wait_all(stores)


def table_loads(copies, owners, wide, chunk, source, picks, myself, pieces, table):
    half = owners // 2
    own, far, near, distant = pieces
    columns = pl.ds(chunk * wide, wide)
    node = here_pick(picks, source, myself, 0, 0)
    whole = own.shape[-1] != wide
    loads = [copies.start(own.at[node, :, columns] if whole else own.at[node], table.at[0])]
    if len(far.shape) == 3:
        far = far.at[here_pick(picks, source, myself, 0, half)]
    loads.append(copies.start(far, table.at[half]))
    for step in range(1, half):
        ref = near[step - 1]
        loads.append(copies.start(ref if len(ref.shape) == 2 else ref.at[1], table.at[step]))
        loads.append(copies.start(distant[step - 1].at[0], table.at[half ^ step]))
    return loads


def split_pieces(owners, refs):
    side = owners // 2 - 1
    own, far = refs[:2]
    return (own, far, refs[2:2 + side], refs[2 + side:2 + 2 * side]), refs[2 + 2 * side:]


def partial_kernel(level, source, owners, wide, chunk, picks, lists, counts, blocks, *refs):
    pieces, refs = split_pieces(owners, refs)
    result, table, coupling, total, sems = refs
    myself = lax.axis_index("leaf")
    copies = Copies(sems)
    loads = [copies.start(blocks, coupling)]
    loads += table_loads(copies, owners, wide, chunk, source, picks, myself, pieces, table)
    total[...] = jnp.zeros_like(total)
    wait_all(loads)
    add_slots(
        total, table, coupling, lambda node, slot: lists[level - 1, node, slot],
        lambda node: counts[level - 1, node], source, myself,
    )
    copies.start(total, result).wait()


def level_kernel(
    level, owners, wide, chunk, befores, sending,
    picks, lists, counts, noise, inverse, blocks, out_before, *refs,
):
    befores_in, refs = refs[:befores], refs[befores:]
    pieces, refs = split_pieces(owners, refs)
    out, solved, *refs = refs
    side = owners // 2 - 1 if sending else 0
    sends, (table, coupling, total, inv, right, here, sems) = refs[:side], refs[side:]
    myself = lax.axis_index("leaf")
    copies = Copies(sems)
    source = level - 1
    columns = pl.ds(chunk * wide, wide)
    loads = [copies.start(before, total) for before in befores_in]
    if not befores:
        total[...] = jnp.zeros_like(total)
    loads.append(copies.start(blocks, coupling))
    loads += table_loads(copies, owners, wide, chunk, source, picks, myself, pieces, table)
    later = [copies.start(noise.at[level, :, :, columns], right)]
    later += load_rows(copies, inv, inverse.at[:, level])
    wait_all(loads)
    add_slots(
        total, table, coupling, lambda node, slot: lists[level - 1, node, slot],
        lambda node: counts[level - 1, node], source, myself,
    )
    wait_all(later)
    for node in range(inv.shape[0]):
        side_here = (right[node].astype(F32) - total[node]).astype(BF16)
        here[node] = transposed_dot(inv[node], side_here).astype(BF16)
    stores = [copies.start(here, out.at[level, :, :, columns]), copies.start(here, solved)]
    for step, send in enumerate(sends, 1):
        node = here_pick(picks, level, myself, step, 0)
        stores.append(copies.start(here.at[node], send))
    wait_all(stores)


def on_device(owners, draws, noise, inverse, coupling, picks, lists, counts):
    levels, nodes, rows, columns = noise.shape
    wide, half = columns // CHUNKS, owners // 2
    width = coupling.shape[2]
    shape = lambda *dims, kind=BF16: jax.ShapeDtypeStruct(dims, kind)
    block = shape(rows, wide)
    message = shape(2, rows, wide)
    part = shape(nodes, rows, wide)
    table = pltpu.VMEM((owners, rows, wide), BF16)
    blocks_here = pltpu.VMEM((draws, nodes, width, rows, rows), BF16)
    total = pltpu.VMEM((nodes, rows, wide), F32)
    inv = pltpu.VMEM((nodes, rows, rows), BF16)
    chunk_here = pltpu.VMEM((nodes, rows, wide), BF16)
    leaf = lambda value, step: hop(value, "leaf", owners, step)
    near = lambda values: [leaf(value, step) for step, value in enumerate(values, 1)]
    gather = lambda value: lax.all_gather(value, "draw", axis=0)

    chunks = range(CHUNKS)
    far_inverse = leaf(inverse[0], half)
    far = [leaf(noise[0, :, :, at * wide:(at + 1) * wide], half) for at in chunks]
    blocks = [gather(coupling[at]) for at in range(levels - 1)]
    inverse_all = gather(inverse)
    far_inverse_all = gather(far_inverse)

    out, own, *sends = call(
        functools.partial(own_first, owners, wide),
        [shape(levels, nodes, rows, columns), shape(nodes, rows, columns)] + [block] * (half - 1),
        [pltpu.VMEM((nodes, rows, columns), BF16), inv, pltpu.VMEM((nodes, rows, columns), BF16)],
        (picks,),
        (noise, inverse_all),
    )
    got = [near(sends)]
    mine = []
    for at in chunks:
        last = at == CHUNKS - 1
        kept, *sends = call(
            functools.partial(far_first, owners, wide, at, last),
            [block] + [shape(1, rows, wide) if last else message] * (half - 1),
            [chunk_here, inv, chunk_here],
            (picks,),
            (far[at], far_inverse_all, own),
        )
        mine.append(kept)
        got.append(near(sends))
    pieces = [[(own, mine[at], *got[at], *got[at + 1]) for at in chunks]]

    for level in range(1, levels):
        solved, sends = [], []
        for at in chunks:
            befores = [
                call(
                    functools.partial(partial_kernel, level, source, owners, wide, at),
                    shape(nodes, rows, wide, kind=F32),
                    [table, blocks_here, total],
                    (picks, lists, counts),
                    (blocks[level - 1], *pieces[source][at]),
                )
                for source in range(level - 1)
            ]
            befores = [functools.reduce(jnp.add, befores)] if befores else []
            sending = at == 0 and level < levels - 1
            out, here, *sent = call(
                functools.partial(level_kernel, level, owners, wide, at, len(befores), sending),
                [shape(*out.shape), part] + ([block] * (half - 1) if sending else []),
                [table, blocks_here, total, inv, chunk_here, chunk_here],
                (picks, lists, counts),
                (noise, inverse_all, blocks[level - 1], out, *befores, *pieces[level - 1][at]),
                aliases={6: 0},
            )
            solved.append(here)
            sends += sent
        if level == levels - 1:
            break
        far = [leaf(here, half) for here in solved]
        got = [near(sends)]
        for at in chunks:
            last = at == CHUNKS - 1
            sends = call(
                functools.partial(far_next, owners, level, last),
                [shape(1, rows, wide) if last else message] * (half - 1),
                [],
                (picks,),
                (far[at],) if last else (far[at], solved[at + 1]),
            )
            got.append(near(sends))
        pieces.append([(solved[at], far[at], *got[at], *got[at + 1]) for at in chunks])
    return out


def solution(mesh):
    placed = (
        P(None, "leaf", None, "draw"),
        P(None, "leaf", "draw", None),
        P(None, "leaf", "draw", None, None),
        P(),
        P(None, "leaf", None),
        P(None, "leaf"),
    )
    return jax.shard_map(
        functools.partial(on_device, mesh.shape["leaf"], mesh.shape["draw"]),
        mesh=mesh,
        in_specs=placed,
        out_specs=P(None, "leaf", None, "draw"),
        check_vma=False,
    )
```

time: 209 us -> 152 us (0.73)
  the two profiles are of different devices: /device:TPU:9 before, /device:TPU:0 now
where the time goes in v2:
time: 152 us; the launch traced here: 151 us
  Pallas kernels  44.7 us (29%)
  starting transfers between devices  33.8 us (22%)
  waiting for transfers between devices  21.2 us (14%)
  local copies, waits for them, and re-layouts  19 us (12%)
  blocking collectives  18.3 us (12%)
  between operations  13.8 us (9%)
    pallas_call x11, Pallas kernels, call(): pl.pallas_call(kernel, out_shape=outs, in_specs=[SMEM] * len(small) + [AN...  44.7 us
    ppermute x23, starting transfers between devices, hop(): return lax.ppermute(value, axis, [(at, at ^ step) for at in range(size)])  33.7 us
    ppermute x23, waiting for transfers between devices, hop(): return lax.ppermute(value, axis, [(at, at ^ step) for at in range(size)])  20.5 us
    all_gather x2, blocking collectives, on_device(): gather = lambda value: lax.all_gather(value, 'draw', axis=0)  18.3 us
    unnamed x80, local copies, waits for them, and re-layouts  16.5 us
  transfers between devices with their start and end apart: 25, of which 5 were waited for; matrix products, arithmetic and copies ran while one was open for 0% of the time, Pallas kernels for 26%

profile of v2, /device:TPU:0, one launch (start us, length us, event | category | flops | bytes accessed | tf_op | source)
XLA Modules:
  0.0 150.9 jit_solution(17431864267313740555)
XLA Ops:
  6.5 2.4 %fusion = (bf16[1,2,2,256,256]{4,3,2,1,0:T(8,128)(2,1)}, bf16[1,2,2,256,256]{4,3,2,1,0:T(8,128)(2,1)}) fusion(bf16[2,2,2,256,256]{4,3,2,1,0:T(8,128)(2,1)} %param.8), kind=kLoop, calls=%fused_computation.3 | loop fusion | bytes 2097152 | tf_op jit(solution)/shard_map/slice | solution.py:231
  9.8 4.1 %collective-permute-start = (bf16[2,256,256]{2,1,0:T(8,128)(2,1)S(1)}, bf16[2,256,256]{2,1,0:T(8,128)(2,1)S(1)}, u32[]{:S(2)}, u32[]{:S(2)}) collective-permute-start(bf16[2,256,256]{2,1,0:T(8,128)(2,1)S(1)} %get-tuple-element.62), channel_id=1, source_target_pairs={{0,16},{4,20},{8,24},{12,28},{16,0},{20,4},{24,8},{28,12},{1,17},{... | collective-permute-start | bytes 786440 | tf_op jit(solution)/shard_map/ppermute | solution.py:17
  14.0 2.9 %collective-permute-start.8 = (bf16[2,256,256]{2,1,0:T(8,128)(2,1)S(1)}, bf16[2,256,256]{2,1,0:T(8,128)(2,1)S(1)}, u32[]{:S(2)}, u32[]{:S(2)}) collective-permute-start(bf16[2,256,256]{2,1,0:T(8,128)(2,1)S(1)} %get-tuple-element.61), channel_id=1, source_target_pairs={{0,16},{4,20},{8,24},{12,28},{16,0},{20,4},{24,8},{28,12},{1,17},{... | collective-permute-start | bytes 786440 | tf_op jit(solution)/shard_map/ppermute | solution.py:17
  16.9 12.2 %all-gather = bf16[12,2,64,256]{3,2,1,0:T(8,128)(2,1)S(1)} all-gather(bf16[3,2,64,256]{3,2,1,0:T(8,128)(2,1)S(1)} %copy-done.39), channel_id=2, replica_groups=mesh['leaf'=8,'draw'=4] {'draw'}, dimensions={0}, use_global_device_ids=true | all-gather | bytes 983040 | tf_op jit(solution)/shard_map/all_gather | solution.py:226
  29.1 2.6 %shard_map.64 = (bf16[3,2,256,512]{3,2,1,0:T(8,128)(2,1)}, bf16[2,256,512]{2,1,0:T(8,128)(2,1)S(1)}, bf16[256,256]{1,0:T(8,128)(2,1)S(1)}, bf16[256,256]{1,0:T(8,128)(2,1)S(1)}, bf16[256,256]{1,0:T(8,128)(2,1)S(1)}) custom-call(s32[2,8,8]{2,1,0:T(8,128)S(1)} %copy-done.16, bf16[3,2,256,512]{3,2,1,0:T(8,128)(2,1)S(1)} %copy-done, ...), custom_call_target="tpu_custom_call" | custom-call | tf_op jit(solution)/shard_map/pallas_call | solution.py:66
  31.7 1.6 %collective-permute-start.2 = (bf16[256,256]{1,0:T(8,128)(2,1)S(1)}, bf16[256,256]{1,0:T(8,128)(2,1)S(1)}, u32[]{:S(2)}, u32[]{:S(2)}) collective-permute-start(bf16[256,256]{1,0:T(8,128)(2,1)S(1)} %get-tuple-element.36), channel_id=1, source_target_pairs={{0,4},{4,0},{8,12},{12,8},{16,20},{20,16},{24,28},{28,24},{1,5},{5... | collective-permute-start | bytes 393224 | tf_op jit(solution)/shard_map/ppermute | solution.py:17
  33.4 1.7 %collective-permute-done.1 = bf16[2,64,256]{2,1,0:T(8,128)(2,1)S(1)} collective-permute-done((bf16[2,64,256]{2,1,0:T(8,128)(2,1)S(1)}, bf16[2,64,256]{2,1,0:T(8,128)(2,1)S(1)}, u32[]{:S(2)}, u32[]{:S(2)}) %collective-permute-start.1) | collective-permute-done | bytes 65568 | tf_op jit(solution)/shard_map/ppermute | solution.py:17
  35.1 6.1 %all-gather.1 = bf16[8,64,256]{2,1,0:T(8,128)(2,1)S(1)} all-gather(bf16[2,64,256]{2,1,0:T(8,128)(2,1)S(1)} %collective-permute-done.1), channel_id=3, replica_groups=mesh['leaf'=8,'draw'=4] {'draw'}, dimensions={0}, use_global_device_ids=true | all-gather | bytes 327680 | tf_op jit(solution)/shard_map/all_gather | solution.py:226
  41.1 2.5 %shard_map.65 = (bf16[256,256]{1,0:T(8,128)(2,1)S(1)}, bf16[2,256,256]{2,1,0:T(8,128)(2,1)S(1)}, bf16[2,256,256]{2,1,0:T(8,128)(2,1)S(1)}, bf16[2,256,256]{2,1,0:T(8,128)(2,1)S(1)}) custom-call(s32[2,8,8]{2,1,0:T(8,128)S(1)} %copy-done.16, bf16[2,256,256]{2,1,0:T(8,128)(2,1)S(1)} %collective-permute-done.far, bf16[4,2,64,256]{3,2,1,0:T(8,128)(2,1)S(1)} %bitcast.13, ...), custom_call_target="tpu_custom_call" | custom-call | tf_op jit(solution)/shard_map/pallas_call | solution.py:66
  44.3 1.6 %collective-permute-start.5 = (bf16[2,256,256]{2,1,0:T(8,128)(2,1)S(1)}, bf16[2,256,256]{2,1,0:T(8,128)(2,1)S(1)}, u32[]{:S(2)}, u32[]{:S(2)}) collective-permute-start(bf16[2,256,256]{2,1,0:T(8,128)(2,1)S(1)} %get-tuple-element.39), channel_id=1, source_target_pairs={{0,4},{4,0},{8,12},{12,8},{16,20},{20,16},{24,28},{28,24},{1,5},{5... | collective-permute-start | bytes 786440 | tf_op jit(solution)/shard_map/ppermute | solution.py:17
  45.8 1.9 %collective-permute-start.7 = (bf16[2,256,256]{2,1,0:T(8,128)(2,1)S(1)}, bf16[2,256,256]{2,1,0:T(8,128)(2,1)S(1)}, u32[]{:S(2)}, u32[]{:S(2)}) collective-permute-start(bf16[2,256,256]{2,1,0:T(8,128)(2,1)S(1)} %get-tuple-element.41), channel_id=1, source_target_pairs={{0,12},{4,8},{8,4},{12,0},{16,28},{20,24},{24,20},{28,16},{1,13},{... | collective-permute-start | bytes 786440 | tf_op jit(solution)/shard_map/ppermute | solution.py:17
  47.9 2.9 %collective-permute-start.4 = (bf16[256,256]{1,0:T(8,128)(2,1)S(1)}, bf16[256,256]{1,0:T(8,128)(2,1)S(1)}, u32[]{:S(2)}, u32[]{:S(2)}) collective-permute-start(bf16[256,256]{1,0:T(8,128)(2,1)S(1)} %get-tuple-element.38), channel_id=1, source_target_pairs={{0,12},{4,8},{8,4},{12,0},{16,28},{20,24},{24,20},{28,16},{1,13},{... | collective-permute-start | bytes 393224 | tf_op jit(solution)/shard_map/ppermute | solution.py:17
  50.8 2.6 %shard_map.67 = (bf16[256,256]{1,0:T(8,128)(2,1)S(1)}, bf16[1,256,256]{2,1,0:T(8,128)(2,1)}, bf16[1,256,256]{2,1,0:T(8,128)(2,1)}, bf16[1,256,256]{2,1,0:T(8,128)(2,1)}) custom-call(s32[2,8,8]{2,1,0:T(8,128)S(1)} %copy-done.16, bf16[2,256,256]{2,1,0:T(8,128)(2,1)S(1)} %collective-permute-done.8.far, bf16[4,2,64,256]{3,2,1,0:T(8,128)(2,1)S(1)} %bitcast.14, ...), custom_call_target="tpu_custom_call" | custom-call | tf_op jit(solution)/shard_map/pallas_call | solution.py:66
  54.1 9.3 %collective-permute-done.3.refs_3_ = bf16[256,256]{1,0:T(8,128)(2,1)S(1)} collective-permute-done((bf16[256,256]{1,0:T(8,128)(2,1)S(1)}, bf16[256,256]{1,0:T(8,128)(2,1)S(1)}, u32[]{:S(2)}, u32[]{:S(2)}) %collective-permute-start.3) | collective-permute-done | bytes 131104 | tf_op jit(solution)/shard_map/ppermute | solution.py:17
  66.2 2.8 %collective-permute-start.11 = (bf16[1,256,256]{2,1,0:T(8,128)(2,1)}, bf16[1,256,256]{2,1,0:T(8,128)(2,1)}, u32[]{:S(2)}, u32[]{:S(2)}) collective-permute-start(bf16[1,256,256]{2,1,0:T(8,128)(2,1)} %get-tuple-element.46), channel_id=1, source_target_pairs={{0,12},{4,8},{8,4},{12,0},{16,28},{20,24},{24,20},{28,16},{1,13},{... | collective-permute-start | bytes 393224 | tf_op jit(solution)/shard_map/ppermute | solution.py:17
  69.7 1.6 %copy-done.3 = bf16[4,2,2,256,256]{4,3,2,1,0:T(8,128)(2,1)S(1)} copy-done((bf16[4,2,2,256,256]{4,3,2,1,0:T(8,128)(2,1)S(1)}, bf16[4,2,2,256,256]{4,3,2,1,0:T(8,128)(2,1)}, u32[]{:S(2)}) %copy-start.3) | copy-done | bytes 2097176
  75.0 6.0 %shard_map.66 = (bf16[3,2,256,512]{3,2,1,0:T(8,128)(2,1)}, bf16[2,256,256]{2,1,0:T(8,128)(2,1)S(1)}, bf16[256,256]{1,0:T(8,128)(2,1)S(1)}, bf16[256,256]{1,0:T(8,128)(2,1)S(1)}, bf16[256,256]{1,0:T(8,128)(2,1)S(1)}) custom-call(s32[2,8,8]{2,1,0:T(8,128)S(1)} %copy-done.16, s32[2,2,8]{2,1,0:T(2,128)S(1)} %copy-done.37, ...), custom_call_target="tpu_custom_call", output_to_operand_aliasing={{0}: (6, {})} | custom-call | tf_op jit(solution)/shard_map/pallas_call | solution.py:66
  81.0 1.8 %collective-permute-start.12 = (bf16[2,256,256]{2,1,0:T(8,128)(2,1)S(1)}, bf16[2,256,256]{2,1,0:T(8,128)(2,1)S(1)}, u32[]{:S(2)}, u32[]{:S(2)}) collective-permute-start(bf16[2,256,256]{2,1,0:T(8,128)(2,1)S(1)} %get-tuple-element.48.refs_1_), channel_id=1, source_target_pairs={{0,16},{4,20},{8,24},{12,28},{16,0},{20,4},{24,8},{28,12},{1,17},{... | collective-permute-start | bytes 786440 | tf_op jit(solution)/shard_map/ppermute | solution.py:17
  82.8 6.2 %shard_map.68 = (bf16[3,2,256,512]{3,2,1,0:T(8,128)(2,1)}, bf16[2,256,256]{2,1,0:T(8,128)(2,1)S(1)}) custom-call(s32[2,8,8]{2,1,0:T(8,128)S(1)} %copy-done.16, s32[2,2,8]{2,1,0:T(2,128)S(1)} %copy-done.37, s32[2,2]{1,0:T(2,128)S(1)} %copy-done.38, bf16[3,2,256,512]{3,2,1,0:T(8,128)(2,1)S(1)} %copy-done, ...), custom_call_target="tpu_custom_call", output_to_operand_aliasing={{0}: (6, {})} | custom-call | tf_op jit(solution)/shard_map/pallas_call | solution.py:66
  89.0 1.7 %collective-permute-start.19 = (bf16[2,256,256]{2,1,0:T(8,128)(2,1)S(1)}, bf16[2,256,256]{2,1,0:T(8,128)(2,1)S(1)}, u32[]{:S(2)}, u32[]{:S(2)}) collective-permute-start(bf16[2,256,256]{2,1,0:T(8,128)(2,1)S(1)} %get-tuple-element.52.refs_0_.refs_1_), channel_id=1, source_target_pairs={{0,16},{4,20},{8,24},{12,28},{16,0},{20,4},{24,8},{28,12},{1,17},{... | collective-permute-start | bytes 786440 | tf_op jit(solution)/shard_map/ppermute | solution.py:17
  91.7 8.4 %collective-permute-done.12.far.refs_2_ = bf16[2,256,256]{2,1,0:T(8,128)(2,1)S(1)} collective-permute-done((bf16[2,256,256]{2,1,0:T(8,128)(2,1)S(1)}, bf16[2,256,256]{2,1,0:T(8,128)(2,1)S(1)}, u32[]{:S(2)}, u32[]{:S(2)}) %collective-permute-start.12) | collective-permute-done | bytes 262176 | tf_op jit(solution)/shard_map/ppermute | solution.py:17
  100.1 2.4 %shard_map.70 = (bf16[2,256,256]{2,1,0:T(8,128)(2,1)S(1)}, bf16[2,256,256]{2,1,0:T(8,128)(2,1)}, bf16[2,256,256]{2,1,0:T(8,128)(2,1)}) custom-call(s32[2,8,8]{2,1,0:T(8,128)S(1)} %copy-done.16, bf16[2,256,256]{2,1,0:T(8,128)(2,1)S(1)} %collective-permute-done.12.far.refs_2_, bf16[2,256,256]{2,1,0:T(8,128)(2,1)S(1)} %get-tuple-element.52.refs_0_.refs_1_), custom_call_target="tpu_custom_call" | custom-call | tf_op jit(solution)/shard_map/pallas_call | solution.py:66
  102.5 1.9 %collective-permute-start.16 = (bf16[2,256,256]{2,1,0:T(8,128)(2,1)S(1)}, bf16[2,256,256]{2,1,0:T(8,128)(2,1)S(1)}, u32[]{:S(2)}, u32[]{:S(2)}) collective-permute-start(bf16[2,256,256]{2,1,0:T(8,128)(2,1)S(1)} %get-tuple-element.53), channel_id=1, source_target_pairs={{0,4},{4,0},{8,12},{12,8},{16,20},{20,16},{24,28},{28,24},{1,5},{5... | collective-permute-start | bytes 786440 | tf_op jit(solution)/shard_map/ppermute | solution.py:17
  104.4 1.6 %collective-permute-start.15 = (bf16[256,256]{1,0:T(8,128)(2,1)S(1)}, bf16[256,256]{1,0:T(8,128)(2,1)S(1)}, u32[]{:S(2)}, u32[]{:S(2)}) collective-permute-start(bf16[256,256]{1,0:T(8,128)(2,1)S(1)} %get-tuple-element.51), channel_id=1, source_target_pairs={{0,12},{4,8},{8,4},{12,0},{16,28},{20,24},{24,20},{28,16},{1,13},{... | collective-permute-start | bytes 393224 | tf_op jit(solution)/shard_map/ppermute | solution.py:17
  107.2 2.9 %collective-permute-start.18 = (bf16[2,256,256]{2,1,0:T(8,128)(2,1)}, bf16[2,256,256]{2,1,0:T(8,128)(2,1)}, u32[]{:S(2)}, u32[]{:S(2)}) collective-permute-start(bf16[2,256,256]{2,1,0:T(8,128)(2,1)} %get-tuple-element.55), channel_id=1, source_target_pairs={{0,12},{4,8},{8,4},{12,0},{16,28},{20,24},{24,20},{28,16},{1,13},{... | collective-permute-start | bytes 786440 | tf_op jit(solution)/shard_map/ppermute | solution.py:17
  110.1 2.0 %shard_map.73 = (bf16[1,256,256]{2,1,0:T(8,128)(2,1)}, bf16[1,256,256]{2,1,0:T(8,128)(2,1)}, bf16[1,256,256]{2,1,0:T(8,128)(2,1)}) custom-call(s32[2,8,8]{2,1,0:T(8,128)S(1)} %copy-done.16, bf16[2,256,256]{2,1,0:T(8,128)(2,1)S(1)} %collective-permute-done.19.far.refs_2_), custom_call_target="tpu_custom_call" | custom-call | tf_op jit(solution)/shard_map/pallas_call | solution.py:66
  115.2 2.8 %collective-permute-start.22 = (bf16[1,256,256]{2,1,0:T(8,128)(2,1)}, bf16[1,256,256]{2,1,0:T(8,128)(2,1)}, u32[]{:S(2)}, u32[]{:S(2)}) collective-permute-start(bf16[1,256,256]{2,1,0:T(8,128)(2,1)} %get-tuple-element.59), channel_id=1, source_target_pairs={{0,12},{4,8},{8,4},{12,0},{16,28},{20,24},{24,20},{28,16},{1,13},{... | collective-permute-start | bytes 393224 | tf_op jit(solution)/shard_map/ppermute | solution.py:17
  118.0 1.6 %copy-done.1 = bf16[4,2,2,256,256]{4,3,2,1,0:T(8,128)(2,1)S(1)} copy-done((bf16[4,2,2,256,256]{4,3,2,1,0:T(8,128)(2,1)S(1)}, bf16[4,2,2,256,256]{4,3,2,1,0:T(8,128)(2,1)}, u32[]{:S(2)}) %copy-start.1) | copy-done | bytes 2097176
  123.2 3.7 %shard_map.69.refs_0_ = f32[2,256,256]{2,1,0:T(8,128)S(1)} custom-call(s32[2,8,8]{2,1,0:T(8,128)S(1)} %copy-done.16, s32[2,2,8]{2,1,0:T(2,128)S(1)} %copy-done.37, s32[2,2]{1,0:T(2,128)S(1)} %copy-done.38, bf16[4,2,2,256,256]{4,3,2,1,0:T(8,128)(2,1)S(1)} %copy-done.1, bf16[2,256,512]{2,1,0:T(8,128)(2,1)S(1)} %get-tuple-element.34.own.refs_0_, ...), custom_call_target="tpu_custom_call" | custom-call | tf_op jit(solution)/shard_map/pallas_call | solution.py:66
  127.1 4.2 %shard_map.72.refs_0_ = f32[2,256,256]{2,1,0:T(8,128)S(1)} custom-call(s32[2,8,8]{2,1,0:T(8,128)S(1)} %copy-done.16, s32[2,2,8]{2,1,0:T(2,128)S(1)} %copy-done.37, s32[2,2]{1,0:T(2,128)S(1)} %copy-done.38, bf16[4,2,2,256,256]{4,3,2,1,0:T(8,128)(2,1)S(1)} %copy-done.1, bf16[2,256,512]{2,1,0:T(8,128)(2,1)S(1)} %get-tuple-element.34.own.refs_0_, ...), custom_call_target="tpu_custom_call" | custom-call | tf_op jit(solution)/shard_map/pallas_call | solution.py:66
  131.4 6.4 %shard_map.71 = (bf16[3,2,256,512]{3,2,1,0:T(8,128)(2,1)}, bf16[2,256,256]{2,1,0:T(8,128)(2,1)}) custom-call(s32[2,8,8]{2,1,0:T(8,128)S(1)} %copy-done.16, s32[2,2,8]{2,1,0:T(2,128)S(1)} %copy-done.37, s32[2,2]{1,0:T(2,128)S(1)} %copy-done.38, bf16[3,2,256,512]{3,2,1,0:T(8,128)(2,1)S(1)} %copy-done, ...), custom_call_target="tpu_custom_call", output_to_operand_aliasing={{0}: (6, {})} | custom-call | tf_op jit(solution)/shard_map/pallas_call | solution.py:66
  137.9 6.1 %shard_map.74 = (bf16[3,2,256,512]{3,2,1,0:T(8,128)(2,1)}, bf16[2,256,256]{2,1,0:T(8,128)(2,1)}) custom-call(s32[2,8,8]{2,1,0:T(8,128)S(1)} %copy-done.16, s32[2,2,8]{2,1,0:T(2,128)S(1)} %copy-done.37, s32[2,2]{1,0:T(2,128)S(1)} %copy-done.38, bf16[3,2,256,512]{3,2,1,0:T(8,128)(2,1)S(1)} %copy-done, ...), custom_call_target="tpu_custom_call", output_to_operand_aliasing={{0}: (6, {})} | custom-call | tf_op jit(solution)/shard_map/pallas_call | solution.py:66
  (116 shorter events, 18.4 us)
Async XLA Ops:
  6.5 63.2 %all-gather.7.cloned.1.call-start = ((), (), s32[]{:S(2)}) async-start(), calls=%async_computation.1 | async-start | bytes 2621440 | tf_op jit(solution)/shard_map/all_gather | solution.py:226
  9.0 20.1 %copy-start.16 = (s32[2,8,8]{2,1,0:T(8,128)S(1)}, s32[2,8,8]{2,1,0:T(8,128)}, u32[]{:S(2)}) copy-start(s32[2,8,8]{2,1,0:T(8,128)} %picks.21) | copy-start | bytes 1540
  9.0 109.0 %all-gather.5.cloned.1.call-start = ((), (), s32[]{:S(2)}) async-start(), calls=%async_computation | async-start | bytes 2621440 | tf_op jit(solution)/shard_map/all_gather | solution.py:226
  9.8 31.4 %collective-permute-start = (bf16[2,256,256]{2,1,0:T(8,128)(2,1)S(1)}, bf16[2,256,256]{2,1,0:T(8,128)(2,1)S(1)}, u32[]{:S(2)}, u32[]{:S(2)}) collective-permute-start(bf16[2,256,256]{2,1,0:T(8,128)(2,1)S(1)} %get-tuple-element.62), channel_id=1, source_target_pairs={{0,16},{4,20},{8,24},{12,28},{16,0},{20,4},{24,8},{28,12},{1,17},{... | collective-permute-start | bytes 786440 | tf_op jit(solution)/shard_map/ppermute | solution.py:17
  13.9 21.2 %collective-permute-start.1 = (bf16[2,64,256]{2,1,0:T(8,128)(2,1)S(1)}, bf16[2,64,256]{2,1,0:T(8,128)(2,1)S(1)}, u32[]{:S(2)}, u32[]{:S(2)}) collective-permute-start(bf16[2,64,256]{2,1,0:T(8,128)(2,1)S(1)} %slice_bitcast_fusion.2), channel_id=1, source_target_pairs={{0,16},{4,20},{8,24},{12,28},{16,0},{20,4},{24,8},{28,12},{1,17},{... | collective-permute-start | bytes 196616 | tf_op jit(solution)/shard_map/ppermute | solution.py:17
  14.0 33.9 %collective-permute-start.8 = (bf16[2,256,256]{2,1,0:T(8,128)(2,1)S(1)}, bf16[2,256,256]{2,1,0:T(8,128)(2,1)S(1)}, u32[]{:S(2)}, u32[]{:S(2)}) collective-permute-start(bf16[2,256,256]{2,1,0:T(8,128)(2,1)S(1)} %get-tuple-element.61), channel_id=1, source_target_pairs={{0,16},{4,20},{8,24},{12,28},{16,0},{20,4},{24,8},{28,12},{1,17},{... | collective-permute-start | bytes 786440 | tf_op jit(solution)/shard_map/ppermute | solution.py:17
  31.7 38.0 %copy-start.37 = (s32[2,2,8]{2,1,0:T(2,128)S(1)}, s32[2,2,8]{2,1,0:T(2,128)}, u32[]{:S(2)}) copy-start(s32[2,2,8]{2,1,0:T(2,128)} %lists.11) | copy-start | bytes 388
  31.7 38.0 %copy-start.38 = (s32[2,2]{1,0:T(2,128)S(1)}, s32[2,2]{1,0:T(2,128)}, u32[]{:S(2)}) copy-start(s32[2,2]{1,0:T(2,128)} %counts.11) | copy-start | bytes 52
  31.7 16.0 %collective-permute-start.2 = (bf16[256,256]{1,0:T(8,128)(2,1)S(1)}, bf16[256,256]{1,0:T(8,128)(2,1)S(1)}, u32[]{:S(2)}, u32[]{:S(2)}) collective-permute-start(bf16[256,256]{1,0:T(8,128)(2,1)S(1)} %get-tuple-element.36), channel_id=1, source_target_pairs={{0,4},{4,0},{8,12},{12,8},{16,20},{20,16},{24,28},{28,24},{1,5},{5... | collective-permute-start | bytes 393224 | tf_op jit(solution)/shard_map/ppermute | solution.py:17
  44.3 21.9 %collective-permute-start.5 = (bf16[2,256,256]{2,1,0:T(8,128)(2,1)S(1)}, bf16[2,256,256]{2,1,0:T(8,128)(2,1)S(1)}, u32[]{:S(2)}, u32[]{:S(2)}) collective-permute-start(bf16[2,256,256]{2,1,0:T(8,128)(2,1)S(1)} %get-tuple-element.39), channel_id=1, source_target_pairs={{0,4},{4,0},{8,12},{12,8},{16,20},{20,16},{24,28},{28,24},{1,5},{5... | collective-permute-start | bytes 786440 | tf_op jit(solution)/shard_map/ppermute | solution.py:17
  45.8 23.2 %collective-permute-start.6 = (bf16[2,256,256]{2,1,0:T(8,128)(2,1)S(1)}, bf16[2,256,256]{2,1,0:T(8,128)(2,1)S(1)}, u32[]{:S(2)}, u32[]{:S(2)}) collective-permute-start(bf16[2,256,256]{2,1,0:T(8,128)(2,1)S(1)} %get-tuple-element.40), channel_id=1, source_target_pairs={{0,8},{4,12},{8,0},{12,4},{16,24},{20,28},{24,16},{28,20},{1,9},{5... | collective-permute-start | bytes 786440 | tf_op jit(solution)/shard_map/ppermute | solution.py:17
  45.8 23.2 %collective-permute-start.7 = (bf16[2,256,256]{2,1,0:T(8,128)(2,1)S(1)}, bf16[2,256,256]{2,1,0:T(8,128)(2,1)S(1)}, u32[]{:S(2)}, u32[]{:S(2)}) collective-permute-start(bf16[2,256,256]{2,1,0:T(8,128)(2,1)S(1)} %get-tuple-element.41), channel_id=1, source_target_pairs={{0,12},{4,8},{8,4},{12,0},{16,28},{20,24},{24,20},{28,16},{1,13},{... | collective-permute-start | bytes 786440 | tf_op jit(solution)/shard_map/ppermute | solution.py:17
  47.8 15.7 %collective-permute-start.3 = (bf16[256,256]{1,0:T(8,128)(2,1)S(1)}, bf16[256,256]{1,0:T(8,128)(2,1)S(1)}, u32[]{:S(2)}, u32[]{:S(2)}) collective-permute-start(bf16[256,256]{1,0:T(8,128)(2,1)S(1)} %get-tuple-element.37), channel_id=1, source_target_pairs={{0,8},{4,12},{8,0},{12,4},{16,24},{20,28},{24,16},{28,20},{1,9},{5... | collective-permute-start | bytes 393224 | tf_op jit(solution)/shard_map/ppermute | solution.py:17
  47.9 17.4 %collective-permute-start.4 = (bf16[256,256]{1,0:T(8,128)(2,1)S(1)}, bf16[256,256]{1,0:T(8,128)(2,1)S(1)}, u32[]{:S(2)}, u32[]{:S(2)}) collective-permute-start(bf16[256,256]{1,0:T(8,128)(2,1)S(1)} %get-tuple-element.38), channel_id=1, source_target_pairs={{0,12},{4,8},{8,4},{12,0},{16,28},{20,24},{24,20},{28,16},{1,13},{... | collective-permute-start | bytes 393224 | tf_op jit(solution)/shard_map/ppermute | solution.py:17
  64.1 18.7 %collective-permute-start.9 = (bf16[1,256,256]{2,1,0:T(8,128)(2,1)}, bf16[1,256,256]{2,1,0:T(8,128)(2,1)}, u32[]{:S(2)}, u32[]{:S(2)}) collective-permute-start(bf16[1,256,256]{2,1,0:T(8,128)(2,1)} %get-tuple-element.44), channel_id=1, source_target_pairs={{0,4},{4,0},{8,12},{12,8},{16,20},{20,16},{24,28},{28,24},{1,5},{5... | collective-permute-start | bytes 393224 | tf_op jit(solution)/shard_map/ppermute | solution.py:17
  65.9 16.8 %collective-permute-start.10 = (bf16[1,256,256]{2,1,0:T(8,128)(2,1)}, bf16[1,256,256]{2,1,0:T(8,128)(2,1)}, u32[]{:S(2)}, u32[]{:S(2)}) collective-permute-start(bf16[1,256,256]{2,1,0:T(8,128)(2,1)} %get-tuple-element.45), channel_id=1, source_target_pairs={{0,8},{4,12},{8,0},{12,4},{16,24},{20,28},{24,16},{28,20},{1,9},{5... | collective-permute-start | bytes 393224 | tf_op jit(solution)/shard_map/ppermute | solution.py:17
  66.2 16.6 %collective-permute-start.11 = (bf16[1,256,256]{2,1,0:T(8,128)(2,1)}, bf16[1,256,256]{2,1,0:T(8,128)(2,1)}, u32[]{:S(2)}, u32[]{:S(2)}) collective-permute-start(bf16[1,256,256]{2,1,0:T(8,128)(2,1)} %get-tuple-element.46), channel_id=1, source_target_pairs={{0,12},{4,8},{8,4},{12,0},{16,28},{20,24},{24,20},{28,16},{1,13},{... | collective-permute-start | bytes 393224 | tf_op jit(solution)/shard_map/ppermute | solution.py:17
  81.0 8.0 %copy-start.29 = (bf16[2,256,256]{2,1,0:T(8,128)(2,1)}, bf16[2,256,256]{2,1,0:T(8,128)(2,1)S(1)}, u32[]{:S(2)}) copy-start(bf16[2,256,256]{2,1,0:T(8,128)(2,1)S(1)} %get-tuple-element.48.refs_1_) | copy-start | bytes 786436
  81.0 19.1 %collective-permute-start.12 = (bf16[2,256,256]{2,1,0:T(8,128)(2,1)S(1)}, bf16[2,256,256]{2,1,0:T(8,128)(2,1)S(1)}, u32[]{:S(2)}, u32[]{:S(2)}) collective-permute-start(bf16[2,256,256]{2,1,0:T(8,128)(2,1)S(1)} %get-tuple-element.48.refs_1_), channel_id=1, source_target_pairs={{0,16},{4,20},{8,24},{12,28},{16,0},{20,4},{24,8},{28,12},{1,17},{... | collective-permute-start | bytes 786440 | tf_op jit(solution)/shard_map/ppermute | solution.py:17
  88.9 25.5 %copy-start.10 = (bf16[2,256,256]{2,1,0:T(8,128)(2,1)}, bf16[2,256,256]{2,1,0:T(8,128)(2,1)S(1)}, u32[]{:S(2)}) copy-start(bf16[2,256,256]{2,1,0:T(8,128)(2,1)S(1)} %get-tuple-element.52.refs_0_.refs_1_) | copy-start | bytes 786436
  89.0 18.2 %collective-permute-start.19 = (bf16[2,256,256]{2,1,0:T(8,128)(2,1)S(1)}, bf16[2,256,256]{2,1,0:T(8,128)(2,1)S(1)}, u32[]{:S(2)}, u32[]{:S(2)}) collective-permute-start(bf16[2,256,256]{2,1,0:T(8,128)(2,1)S(1)} %get-tuple-element.52.refs_0_.refs_1_), channel_id=1, source_target_pairs={{0,16},{4,20},{8,24},{12,28},{16,0},{20,4},{24,8},{28,12},{1,17},{... | collective-permute-start | bytes 786440 | tf_op jit(solution)/shard_map/ppermute | solution.py:17
  90.7 15.4 %collective-permute-start.13 = (bf16[256,256]{1,0:T(8,128)(2,1)S(1)}, bf16[256,256]{1,0:T(8,128)(2,1)S(1)}, u32[]{:S(2)}, u32[]{:S(2)}) collective-permute-start(bf16[256,256]{1,0:T(8,128)(2,1)S(1)} %get-tuple-element.49), channel_id=1, source_target_pairs={{0,4},{4,0},{8,12},{12,8},{16,20},{20,16},{24,28},{28,24},{1,5},{5... | collective-permute-start | bytes 393224 | tf_op jit(solution)/shard_map/ppermute | solution.py:17
  100.1 15.1 %copy-start.14 = (bf16[2,256,256]{2,1,0:T(8,128)(2,1)}, bf16[2,256,256]{2,1,0:T(8,128)(2,1)S(1)}, u32[]{:S(2)}) copy-start(bf16[2,256,256]{2,1,0:T(8,128)(2,1)S(1)} %collective-permute-done.12.far.refs_2_) | copy-start | bytes 786436
  102.5 11.9 %collective-permute-start.16 = (bf16[2,256,256]{2,1,0:T(8,128)(2,1)S(1)}, bf16[2,256,256]{2,1,0:T(8,128)(2,1)S(1)}, u32[]{:S(2)}, u32[]{:S(2)}) collective-permute-start(bf16[2,256,256]{2,1,0:T(8,128)(2,1)S(1)} %get-tuple-element.53), channel_id=1, source_target_pairs={{0,4},{4,0},{8,12},{12,8},{16,20},{20,16},{24,28},{28,24},{1,5},{5... | collective-permute-start | bytes 786440 | tf_op jit(solution)/shard_map/ppermute | solution.py:17
  104.4 7.6 %collective-permute-start.14 = (bf16[256,256]{1,0:T(8,128)(2,1)S(1)}, bf16[256,256]{1,0:T(8,128)(2,1)S(1)}, u32[]{:S(2)}, u32[]{:S(2)}) collective-permute-start(bf16[256,256]{1,0:T(8,128)(2,1)S(1)} %get-tuple-element.50), channel_id=1, source_target_pairs={{0,8},{4,12},{8,0},{12,4},{16,24},{20,28},{24,16},{28,20},{1,9},{5... | collective-permute-start | bytes 393224 | tf_op jit(solution)/shard_map/ppermute | solution.py:17
  104.4 8.8 %collective-permute-start.15 = (bf16[256,256]{1,0:T(8,128)(2,1)S(1)}, bf16[256,256]{1,0:T(8,128)(2,1)S(1)}, u32[]{:S(2)}, u32[]{:S(2)}) collective-permute-start(bf16[256,256]{1,0:T(8,128)(2,1)S(1)} %get-tuple-element.51), channel_id=1, source_target_pairs={{0,12},{4,8},{8,4},{12,0},{16,28},{20,24},{24,20},{28,16},{1,13},{... | collective-permute-start | bytes 393224 | tf_op jit(solution)/shard_map/ppermute | solution.py:17
  106.7 24.6 %collective-permute-start.17 = (bf16[2,256,256]{2,1,0:T(8,128)(2,1)}, bf16[2,256,256]{2,1,0:T(8,128)(2,1)}, u32[]{:S(2)}, u32[]{:S(2)}) collective-permute-start(bf16[2,256,256]{2,1,0:T(8,128)(2,1)} %get-tuple-element.54), channel_id=1, source_target_pairs={{0,8},{4,12},{8,0},{12,4},{16,24},{20,28},{24,16},{28,20},{1,9},{5... | collective-permute-start | bytes 786440 | tf_op jit(solution)/shard_map/ppermute | solution.py:17
  107.2 8.0 %copy-start.12 = (bf16[2,256,256]{2,1,0:T(8,128)(2,1)}, bf16[2,256,256]{2,1,0:T(8,128)(2,1)S(1)}, u32[]{:S(2)}) copy-start(bf16[2,256,256]{2,1,0:T(8,128)(2,1)S(1)} %collective-permute-done.19.far.refs_2_) | copy-start | bytes 786436
  107.2 24.2 %collective-permute-start.18 = (bf16[2,256,256]{2,1,0:T(8,128)(2,1)}, bf16[2,256,256]{2,1,0:T(8,128)(2,1)}, u32[]{:S(2)}, u32[]{:S(2)}) collective-permute-start(bf16[2,256,256]{2,1,0:T(8,128)(2,1)} %get-tuple-element.55), channel_id=1, source_target_pairs={{0,12},{4,8},{8,4},{12,0},{16,28},{20,24},{24,20},{28,16},{1,13},{... | collective-permute-start | bytes 786440 | tf_op jit(solution)/shard_map/ppermute | solution.py:17
  112.7 25.1 %collective-permute-start.20 = (bf16[1,256,256]{2,1,0:T(8,128)(2,1)}, bf16[1,256,256]{2,1,0:T(8,128)(2,1)}, u32[]{:S(2)}, u32[]{:S(2)}) collective-permute-start(bf16[1,256,256]{2,1,0:T(8,128)(2,1)} %get-tuple-element.57), channel_id=1, source_target_pairs={{0,4},{4,0},{8,12},{12,8},{16,20},{20,16},{24,28},{28,24},{1,5},{5... | collective-permute-start | bytes 393224 | tf_op jit(solution)/shard_map/ppermute | solution.py:17
  113.9 24.0 %collective-permute-start.21 = (bf16[1,256,256]{2,1,0:T(8,128)(2,1)}, bf16[1,256,256]{2,1,0:T(8,128)(2,1)}, u32[]{:S(2)}, u32[]{:S(2)}) collective-permute-start(bf16[1,256,256]{2,1,0:T(8,128)(2,1)} %get-tuple-element.58), channel_id=1, source_target_pairs={{0,8},{4,12},{8,0},{12,4},{16,24},{20,28},{24,16},{28,20},{1,9},{5... | collective-permute-start | bytes 393224 | tf_op jit(solution)/shard_map/ppermute | solution.py:17
  115.2 22.7 %collective-permute-start.22 = (bf16[1,256,256]{2,1,0:T(8,128)(2,1)}, bf16[1,256,256]{2,1,0:T(8,128)(2,1)}, u32[]{:S(2)}, u32[]{:S(2)}) collective-permute-start(bf16[1,256,256]{2,1,0:T(8,128)(2,1)} %get-tuple-element.59), channel_id=1, source_target_pairs={{0,12},{4,8},{8,4},{12,0},{16,28},{20,24},{24,20},{28,16},{1,13},{... | collective-permute-start | bytes 393224 | tf_op jit(solution)/shard_map/ppermute | solution.py:17
  (33 other events, 87.1 us)
Sparse Core Ops, SparseCore 0:
  9.1 28.2 all-gather.6
  38.9 20.9 all-gather.4

commit v3 on v2

--- a/solution.py
+++ b/solution.py
@@ -8,13 +8,23 @@
 from jax.sharding import PartitionSpec as P
 
 CHUNKS = 2
-ANY = pl.BlockSpec(memory_space=pl.ANY)
+HBM = pl.BlockSpec(memory_space=pltpu.HBM)
 SMEM = pl.BlockSpec(memory_space=pltpu.SMEM)
 BF16, F32 = jnp.bfloat16, jnp.float32
 
 
 def hop(value, axis, size, step):
     return lax.ppermute(value, axis, [(at, at ^ step) for at in range(size)])
+
+
+def gather_parts(value, axis, size):
+    parts = {0: value}
+    step = size // 2
+    while step:
+        for have in sorted(parts):
+            parts[have ^ step] = hop(parts[have], axis, size, step)
+        step //= 2
+    return [parts[at] for at in range(size)]
 
 
 def transposed_dot(left, right):
@@ -38,11 +48,18 @@
 
 
 def load_rows(copies, target, parts):
-    draws, _, rows, _ = parts.shape
-    return [
-        copies.start(parts.at[at], target.at[:, pl.ds(at * rows, rows), :])
-        for at in range(draws)
-    ]
+    draw = lax.axis_index("draw")
+    rows = parts[0].shape[1]
+    loads = []
+    for step, part in enumerate(parts):
+        start = pl.multiple_of((draw ^ step) * rows, rows)
+        loads.append(copies.start(part, target.at[:, pl.ds(start, rows), :]))
+    return loads
+
+
+def load_blocks(copies, target, parts):
+    draw = lax.axis_index("draw")
+    return [copies.start(part, target.at[draw ^ step]) for step, part in enumerate(parts)]
 
 
 def add_slots(total, table, blocks, lists, counts, source, myself):
@@ -66,8 +83,8 @@
     return pl.pallas_call(
         kernel,
         out_shape=outs,
-        in_specs=[SMEM] * len(small) + [ANY] * len(arrays),
-        out_specs=jax.tree.map(lambda _: ANY, outs),
+        in_specs=[SMEM] * len(small) + [HBM] * len(arrays),
+        out_specs=jax.tree.map(lambda _: HBM, outs),
         scratch_shapes=[*scratch, pltpu.SemaphoreType.DMA((sems,))],
         input_output_aliases=aliases,
         compiler_params=pltpu.CompilerParams(vmem_limit_bytes=24 * 1024 * 1024),
@@ -78,24 +95,33 @@
     return picks[source, myself ^ step, myself ^ origin]
 
 
-def own_first(owners, wide, picks, noise, inverse, *refs):
+def own_first(owners, draws, wide, picks, noise, *refs):
+    inverse, refs = refs[:draws], refs[draws:]
     out, own, *rest = refs
+    chunks = noise.shape[-1] // wide
+    nexts, rest = rest[:chunks - 1], rest[chunks - 1:]
     sends, (right, inv, solved, sems) = rest[:-4], rest[-4:]
     myself = lax.axis_index("leaf")
     copies = Copies(sems)
-    loads = [copies.start(noise.at[0], right)] + load_rows(copies, inv, inverse.at[:, 0])
+    stores = [
+        copies.start(noise.at[0, :, :, pl.ds(at * wide, wide)], target)
+        for at, target in enumerate(nexts, 1)
+    ]
+    loads = [copies.start(noise.at[0], right)]
+    loads += load_rows(copies, inv, [part.at[0] for part in inverse])
     wait_all(loads)
     for node in range(inv.shape[0]):
         solved[node] = transposed_dot(inv[node], right[node]).astype(BF16)
-    stores = [copies.start(solved, out.at[0]), copies.start(solved, own)]
+    stores += [copies.start(solved, out.at[0]), copies.start(solved, own)]
     for step, send in enumerate(sends, 1):
         node = here_pick(picks, 0, myself, step, 0)
         stores.append(copies.start(solved.at[node, :, pl.ds(0, wide)], send))
     wait_all(stores)
 
 
-def far_first(owners, wide, chunk, last, picks, far, inverse, own, *refs):
+def far_first(owners, draws, wide, chunk, last, picks, far, own, *refs):
     half = owners // 2
+    inverse, refs = refs[:draws], refs[draws:]
     mine, *rest = refs
     sends, (right, inv, solved, sems) = rest[:-4], rest[-4:]
     myself = lax.axis_index("leaf")
@@ -156,12 +182,13 @@
     return (own, far, refs[2:2 + side], refs[2 + side:2 + 2 * side]), refs[2 + 2 * side:]
 
 
-def partial_kernel(level, source, owners, wide, chunk, picks, lists, counts, blocks, *refs):
+def partial_kernel(level, source, owners, draws, wide, chunk, picks, lists, counts, *refs):
+    blocks, refs = refs[:draws], refs[draws:]
     pieces, refs = split_pieces(owners, refs)
     result, table, coupling, total, sems = refs
     myself = lax.axis_index("leaf")
     copies = Copies(sems)
-    loads = [copies.start(blocks, coupling)]
+    loads = load_blocks(copies, coupling, blocks)
     loads += table_loads(copies, owners, wide, chunk, source, picks, myself, pieces, table)
     total[...] = jnp.zeros_like(total)
     wait_all(loads)
@@ -173,9 +200,11 @@
 
 
 def level_kernel(
-    level, owners, wide, chunk, befores, sending,
-    picks, lists, counts, noise, inverse, blocks, out_before, *refs,
+    level, owners, draws, wide, chunk, befores, sending,
+    picks, lists, counts, noise, out_before, *refs,
 ):
+    inverse, refs = refs[:draws], refs[draws:]
+    blocks, refs = refs[:draws], refs[draws:]
     befores_in, refs = refs[:befores], refs[befores:]
     pieces, refs = split_pieces(owners, refs)
     out, solved, *refs = refs
@@ -188,10 +217,10 @@
     loads = [copies.start(before, total) for before in befores_in]
     if not befores:
         total[...] = jnp.zeros_like(total)
-    loads.append(copies.start(blocks, coupling))
+    loads += load_blocks(copies, coupling, blocks)
     loads += table_loads(copies, owners, wide, chunk, source, picks, myself, pieces, table)
     later = [copies.start(noise.at[level, :, :, columns], right)]
-    later += load_rows(copies, inv, inverse.at[:, level])
+    later += load_rows(copies, inv, [part.at[level] for part in inverse])
     wait_all(loads)
     add_slots(
         total, table, coupling, lambda node, slot: lists[level - 1, node, slot],
@@ -223,32 +252,34 @@
     chunk_here = pltpu.VMEM((nodes, rows, wide), BF16)
     leaf = lambda value, step: hop(value, "leaf", owners, step)
     near = lambda values: [leaf(value, step) for step, value in enumerate(values, 1)]
-    gather = lambda value: lax.all_gather(value, "draw", axis=0)
+    gather = lambda value: gather_parts(value, "draw", draws)
 
     chunks = range(CHUNKS)
     far_inverse = leaf(inverse[0], half)
-    far = [leaf(noise[0, :, :, at * wide:(at + 1) * wide], half) for at in chunks]
-    blocks = [gather(coupling[at]) for at in range(levels - 1)]
+    far = [leaf(noise[0, :, :, :wide], half)]
     inverse_all = gather(inverse)
     far_inverse_all = gather(far_inverse)
+    blocks = [gather(coupling[at]) for at in range(levels - 1)]
 
     out, own, *sends = call(
-        functools.partial(own_first, owners, wide),
-        [shape(levels, nodes, rows, columns), shape(nodes, rows, columns)] + [block] * (half - 1),
+        functools.partial(own_first, owners, draws, wide),
+        [shape(levels, nodes, rows, columns), shape(nodes, rows, columns)]
+        + [part] * (CHUNKS - 1) + [block] * (half - 1),
         [pltpu.VMEM((nodes, rows, columns), BF16), inv, pltpu.VMEM((nodes, rows, columns), BF16)],
         (picks,),
-        (noise, inverse_all),
-    )
-    got = [near(sends)]
+        (noise, *inverse_all),
+    )
+    far += [leaf(piece, half) for piece in sends[:CHUNKS - 1]]
+    got = [near(sends[CHUNKS - 1:])]
     mine = []
     for at in chunks:
         last = at == CHUNKS - 1
         kept, *sends = call(
-            functools.partial(far_first, owners, wide, at, last),
+            functools.partial(far_first, owners, draws, wide, at, last),
             [block] + [shape(1, rows, wide) if last else message] * (half - 1),
             [chunk_here, inv, chunk_here],
             (picks,),
-            (far[at], far_inverse_all, own),
+            (far[at], own, *far_inverse_all),
         )
         mine.append(kept)
         got.append(near(sends))
@@ -259,23 +290,23 @@
         for at in chunks:
             befores = [
                 call(
-                    functools.partial(partial_kernel, level, source, owners, wide, at),
+                    functools.partial(partial_kernel, level, source, owners, draws, wide, at),
                     shape(nodes, rows, wide, kind=F32),
                     [table, blocks_here, total],
                     (picks, lists, counts),
-                    (blocks[level - 1], *pieces[source][at]),
+                    (*blocks[level - 1], *pieces[source][at]),
                 )
                 for source in range(level - 1)
             ]
             befores = [functools.reduce(jnp.add, befores)] if befores else []
             sending = at == 0 and level < levels - 1
             out, here, *sent = call(
-                functools.partial(level_kernel, level, owners, wide, at, len(befores), sending),
+                functools.partial(level_kernel, level, owners, draws, wide, at, len(befores), sending),
                 [shape(*out.shape), part] + ([block] * (half - 1) if sending else []),
                 [table, blocks_here, total, inv, chunk_here, chunk_here],
                 (picks, lists, counts),
-                (noise, inverse_all, blocks[level - 1], out, *befores, *pieces[level - 1][at]),
-                aliases={6: 0},
+                (noise, out, *inverse_all, *blocks[level - 1], *befores, *pieces[level - 1][at]),
+                aliases={4: 0},
             )
             solved.append(here)
             sends += sent

time: 152 us -> 138 us (0.908)
  waiting for transfers between devices: 21.2 us -> 54.7 us
  blocking collectives: 18.3 us -> 0 us
  local copies, waits for them, and re-layouts: 19 us -> 2.28 us
  between operations: 13.8 us -> 0.38 us
  starting transfers between devices: 33.8 us -> 36.5 us
    ppermute x23 -> x35, waiting for transfers between devices: 20.5 us -> 54.7 us  [hop(): return lax.ppermute(value, axis, [(at, at ^ step) for at in range(size)])]
    all_gather x2 -> x0, blocking collectives: 18.3 us -> none  [on_device(): gather = lambda value: lax.all_gather(value, 'draw', axis=0)]
    unnamed x80 -> x10, local copies, waits for them, and re-layouts: 16.5 us -> 0.02 us
    ppermute x23 -> x35, starting transfers between devices: 33.7 us -> 36.5 us  [hop(): return lax.ppermute(value, axis, [(at, at ^ step) for at in range(size)])]
    slice x1 -> x0, local copies, waits for them, and re-layouts: 2.41 us -> none  [on_device(): blocks = [gather(coupling[at]) for at in range(levels - 1)]]
  transfers between devices with their start and end apart: 25 -> 35, of which waited for: 5 -> 12; matrix products, arithmetic and copies ran while one was open for 0% -> 1% of each run, Pallas kernels for 26% -> 28%
where the time goes in v3:
time: 138 us
  waiting for transfers between devices  54.7 us (40%)
  Pallas kernels  44.3 us (32%)
  starting transfers between devices  36.5 us (26%)
  local copies, waits for them, and re-layouts  2.28 us (2%)
    ppermute x35, waiting for transfers between devices, hop(): return lax.ppermute(value, axis, [(at, at ^ step) for at in range(size)])  54.7 us
    pallas_call x11, Pallas kernels, call(): pl.pallas_call(kernel, out_shape=outs, in_specs=[SMEM] * len(small) + [HB...  44.3 us
    ppermute x35, starting transfers between devices, hop(): return lax.ppermute(value, axis, [(at, at ^ step) for at in range(size)])  36.5 us
  transfers between devices with their start and end apart: 35, of which 12 were waited for; matrix products, arithmetic and copies ran while one was open for 1% of the time, Pallas kernels for 28%

profile of v3, /device:TPU:0, one launch (start us, length us, event | category | flops | bytes accessed | tf_op | source)
XLA Modules:
  0.0 138.1 jit_solution(5905564183503908374)
XLA Ops:
  1.0 4.0 %collective-permute-start.7 = (bf16[2,64,256]{2,1,0:T(8,128)(2,1)S(1)}, bf16[2,64,256]{2,1,0:T(8,128)(2,1)S(1)}, u32[]{:S(2)}, u32[]{:S(2)}) collective-permute-start(bf16[2,64,256]{2,1,0:T(8,128)(2,1)S(1)} %slice_bitcast_fusion.3), channel_id=1, source_target_pairs={{0,16},{4,20},{8,24},{12,28},{16,0},{20,4},{24,8},{28,12},{1,17},{... | collective-permute-start | bytes 196616 | tf_op jit(solution)/shard_map/ppermute | solution.py:17
  5.0 3.6 %collective-permute-done.7.refs_0_ = bf16[2,64,256]{2,1,0:T(8,128)(2,1)S(1)} collective-permute-done((bf16[2,64,256]{2,1,0:T(8,128)(2,1)S(1)}, bf16[2,64,256]{2,1,0:T(8,128)(2,1)S(1)}, u32[]{:S(2)}, u32[]{:S(2)}) %collective-permute-start.7) | collective-permute-done | bytes 65568 | tf_op jit(solution)/shard_map/ppermute | solution.py:17
  9.9 1.8 %collective-permute-start.4 = (bf16[2,2,256,256]{3,2,1,0:T(8,128)(2,1)S(1)}, bf16[2,2,256,256]{3,2,1,0:T(8,128)(2,1)S(1)}, u32[]{:S(2)}, u32[]{:S(2)}) collective-permute-start(bf16[2,2,256,256]{3,2,1,0:T(8,128)(2,1)S(1)} %get-tuple-element.64.refs_4_), channel_id=1, source_target_pairs={{0,2},{1,3},{2,0},{3,1},{4,6},{5,7},{6,4},{7,5},{8,10},{9,11},{10,... | collective-permute-start | bytes 1572872 | tf_op jit(solution)/shard_map/ppermute | solution.py:17
  12.6 1.7 %collective-permute-start.9 = (bf16[2,64,256]{2,1,0:T(8,128)(2,1)S(1)}, bf16[2,64,256]{2,1,0:T(8,128)(2,1)S(1)}, u32[]{:S(2)}, u32[]{:S(2)}) collective-permute-start(bf16[2,64,256]{2,1,0:T(8,128)(2,1)S(1)} %collective-permute-done.7.refs_0_), channel_id=1, source_target_pairs={{0,2},{1,3},{2,0},{3,1},{4,6},{5,7},{6,4},{7,5},{8,10},{9,11},{10,... | collective-permute-start | bytes 196616 | tf_op jit(solution)/shard_map/ppermute | solution.py:17
  14.3 14.7 %collective-permute-done.1.refs_2_ = bf16[3,2,64,256]{3,2,1,0:T(8,128)(2,1)S(1)} collective-permute-done((bf16[3,2,64,256]{3,2,1,0:T(8,128)(2,1)S(1)}, bf16[3,2,64,256]{3,2,1,0:T(8,128)(2,1)S(1)}, u32[]{:S(2)}, u32[]{:S(2)}) %collective-permute-start.1) | collective-permute-done | bytes 196640 | tf_op jit(solution)/shard_map/ppermute | solution.py:17
  30.0 1.7 %collective-permute-start.22 = (bf16[2,2,256,256]{3,2,1,0:T(8,128)(2,1)S(1)}, bf16[2,2,256,256]{3,2,1,0:T(8,128)(2,1)S(1)}, u32[]{:S(2)}, u32[]{:S(2)}) collective-permute-start(bf16[2,2,256,256]{3,2,1,0:T(8,128)(2,1)S(1)} %get-tuple-element.63.refs_0_.refs_4_), channel_id=1, source_target_pairs={{0,2},{1,3},{2,0},{3,1},{4,6},{5,7},{6,4},{7,5},{8,10},{9,11},{10,... | collective-permute-start | bytes 1572872 | tf_op jit(solution)/shard_map/ppermute | solution.py:17
  33.0 2.6 %shard_map.64 = (bf16[3,2,256,512]{3,2,1,0:T(8,128)(2,1)}, bf16[2,256,512]{2,1,0:T(8,128)(2,1)S(1)}, bf16[2,256,256]{2,1,0:T(8,128)(2,1)S(1)}, bf16[256,256]{1,0...) custom-call(s32[2,8,8]{2,1,0:T(8,128)S(1)} %copy-done.2, ...), custom_call_target="tpu_custom_call" | custom-call | tf_op jit(solution)/shard_map/pallas_call | solution.py:83
  37.2 8.6 %collective-permute-done.6.far = bf16[2,256,256]{2,1,0:T(8,128)(2,1)S(1)} collective-permute-done((bf16[2,256,256]{2,1,0:T(8,128)(2,1)S(1)}, bf16[2,256,256]{2,1,0:T(8,128)(2,1)S(1)}, u32[]{:S(2)}, u32[]{:S(2)}) %collective-permute-start.6) | collective-permute-done | bytes 262176 | tf_op jit(solution)/shard_map/ppermute | solution.py:17
  45.9 3.0 %collective-permute-start.13 = (bf16[256,256]{1,0:T(8,128)(2,1)S(1)}, bf16[256,256]{1,0:T(8,128)(2,1)S(1)}, u32[]{:S(2)}, u32[]{:S(2)}) collective-permute-start(bf16[256,256]{1,0:T(8,128)(2,1)S(1)} %get-tuple-element.39), channel_id=1, source_target_pairs={{0,12},{4,8},{8,4},{12,0},{16,28},{20,24},{24,20},{28,16},{1,13},{... | collective-permute-start | bytes 393224 | tf_op jit(solution)/shard_map/ppermute | solution.py:17
  48.9 2.5 %shard_map.65 = (bf16[256,256]{1,0:T(8,128)(2,1)S(1)}, bf16[2,256,256]{2,1,0:T(8,128)(2,1)S(1)}, bf16[2,256,256]{2,1,0:T(8,128)(2,1)S(1)}, bf16[2,256,256]{2,1,0:T(8,128)(2,1)S(1)}) custom-call(s32[2,8,8]{2,1,0:T(8,128)S(1)} %copy-done.2, bf16[2,256,256]{2,1,0:T(8,128)(2,1)S(1)} %collective-permute-done.6.far, ...), custom_call_target="tpu_custom_call" | custom-call | tf_op jit(solution)/shard_map/pallas_call | solution.py:83
  52.8 1.7 %collective-permute-done.13.refs_12_.refs_8_ = bf16[256,256]{1,0:T(8,128)(2,1)S(1)} collective-permute-done((bf16[256,256]{1,0:T(8,128)(2,1)S(1)}, bf16[256,256]{1,0:T(8,128)(2,1)S(1)}, u32[]{:S(2)}, u32[]{:S(2)}) %collective-permute-start.13) | collective-permute-done | bytes 131104 | tf_op jit(solution)/shard_map/ppermute | solution.py:17
  55.0 1.6 %collective-permute-start.16 = (bf16[2,256,256]{2,1,0:T(8,128)(2,1)S(1)}, bf16[2,256,256]{2,1,0:T(8,128)(2,1)S(1)}, u32[]{:S(2)}, u32[]{:S(2)}) collective-permute-start(bf16[2,256,256]{2,1,0:T(8,128)(2,1)S(1)} %get-tuple-element.42), channel_id=1, source_target_pairs={{0,12},{4,8},{8,4},{12,0},{16,28},{20,24},{24,20},{28,16},{1,13},{... | collective-permute-start | bytes 786440 | tf_op jit(solution)/shard_map/ppermute | solution.py:17
  56.6 3.5 %collective-permute-done.14.refs_13_.refs_10_.refs_9_.refs_6_ = bf16[2,256,256]{2,1,0:T(8,128)(2,1)S(1)} collective-permute-done((bf16[2,256,256]{2,1,0:T(8,128)(2,1)S(1)}, bf16[2,256,256]{2,1,0:T(8,128)(2,1)S(1)}, u32[]{:S(2)}, u32[]{:S(2)}) %collective-permute-start.14) | collective-permute-done | bytes 262176 | tf_op jit(solution)/shard_map/ppermute | solution.py:17
  60.0 6.4 %collective-permute-done.17.far = bf16[2,256,256]{2,1,0:T(8,128)(2,1)S(1)} collective-permute-done((bf16[2,256,256]{2,1,0:T(8,128)(2,1)S(1)}, bf16[2,256,256]{2,1,0:T(8,128)(2,1)S(1)}, u32[]{:S(2)}, u32[]{:S(2)}) %collective-permute-start.17) | collective-permute-done | bytes 262176 | tf_op jit(solution)/shard_map/ppermute | solution.py:17
  66.5 2.4 %shard_map.67 = (bf16[256,256]{1,0:T(8,128)(2,1)S(1)}, bf16[1,256,256]{2,1,0:T(8,128)(2,1)S(1)}, bf16[1,256,256]{2,1,0:T(8,128)(2,1)S(1)}, bf16[1,256,256]{2,1,0:T(8,128)(2,1)S(1)}) custom-call(s32[2,8,8]{2,1,0:T(8,128)S(1)} %copy-done.2, bf16[2,256,256]{2,1,0:T(8,128)(2,1)S(1)} %collective-permute-done.17.far, ...), custom_call_target="tpu_custom_call" | custom-call | tf_op jit(solution)/shard_map/pallas_call | solution.py:83
  70.2 3.0 %collective-permute-done.16.refs_15_.refs_12_.refs_11_.refs_8_ = bf16[2,256,256]{2,1,0:T(8,128)(2,1)S(1)} collective-permute-done((bf16[2,256,256]{2,1,0:T(8,128)(2,1)S(1)}, bf16[2,256,256]{2,1,0:T(8,128)(2,1)S(1)}, u32[]{:S(2)}, u32[]{:S(2)}) %collective-permute-start.16) | collective-permute-done | bytes 262176 | tf_op jit(solution)/shard_map/ppermute | solution.py:17
  73.2 1.8 %collective-permute-start.20 = (bf16[1,256,256]{2,1,0:T(8,128)(2,1)S(1)}, bf16[1,256,256]{2,1,0:T(8,128)(2,1)S(1)}, u32[]{:S(2)}, u32[]{:S(2)}) collective-permute-start(bf16[1,256,256]{2,1,0:T(8,128)(2,1)S(1)} %get-tuple-element.48), channel_id=1, source_target_pairs={{0,12},{4,8},{8,4},{12,0},{16,28},{20,24},{24,20},{28,16},{1,13},{... | collective-permute-start | bytes 393224 | tf_op jit(solution)/shard_map/ppermute | solution.py:17
  75.1 6.2 %shard_map.66 = (bf16[3,2,256,512]{3,2,1,0:T(8,128)(2,1)}, bf16[2,256,256]{2,1,0:T(8,128)(2,1)S(1)}, bf16[256,256]{1,0:T(8,128)(2,1)S(1)}, bf16[256,256]{1,0:T(8,128)(2,1)S(1)}, bf16[256,256]{1,0:T(8,128)(2,1)S(1)}) custom-call(s32[2,8,8]{2,1,0:T(8,128)S(1)} %copy-done.2, s32[2,2,8]{2,1,0:T(2,128)S(1)} %copy-done.3, ...), custom_call_target="tpu_custom_call", output_to_operand_aliasing={{0}: (4, {})} | custom-call | tf_op jit(solution)/shard_map/pallas_call | solution.py:83
  81.3 2.3 %collective-permute-start.24 = (bf16[2,256,256]{2,1,0:T(8,128)(2,1)S(1)}, bf16[2,256,256]{2,1,0:T(8,128)(2,1)S(1)}, u32[]{:S(2)}, u32[]{:S(2)}) collective-permute-start(bf16[2,256,256]{2,1,0:T(8,128)(2,1)S(1)} %get-tuple-element.50.refs_9_), channel_id=1, source_target_pairs={{0,16},{4,20},{8,24},{12,28},{16,0},{20,4},{24,8},{28,12},{1,17},{... | collective-permute-start | bytes 786440 | tf_op jit(solution)/shard_map/ppermute | solution.py:17
  83.7 6.2 %shard_map.68 = (bf16[3,2,256,512]{3,2,1,0:T(8,128)(2,1)}, bf16[2,256,256]{2,1,0:T(8,128)(2,1)S(1)}) custom-call(s32[2,8,8]{2,1,0:T(8,128)S(1)} %copy-done.2, s32[2,2,8]{2,1,0:T(2,128)S(1)} %copy-done.3, s32[2,2]{1,0:T(2,128)S(1)} %copy-done.4, bf16[3,2,256,512]{3,2,1,0:T(8,128)(2,1)S(1)} %copy-done, ...), custom_call_target="tpu_custom_call", output_to_operand_aliasing={{0}: (4, {})} | custom-call | tf_op jit(solution)/shard_map/pallas_call | solution.py:83
  90.6 2.3 %collective-permute-start.25 = (bf16[256,256]{1,0:T(8,128)(2,1)S(1)}, bf16[256,256]{1,0:T(8,128)(2,1)S(1)}, u32[]{:S(2)}, u32[]{:S(2)}) collective-permute-start(bf16[256,256]{1,0:T(8,128)(2,1)S(1)} %get-tuple-element.51), channel_id=1, source_target_pairs={{0,4},{4,0},{8,12},{12,8},{16,20},{20,16},{24,28},{28,24},{1,5},{5... | collective-permute-start | bytes 393224 | tf_op jit(solution)/shard_map/ppermute | solution.py:17
  92.9 8.6 %collective-permute-done.24.far.refs_10_ = bf16[2,256,256]{2,1,0:T(8,128)(2,1)S(1)} collective-permute-done((bf16[2,256,256]{2,1,0:T(8,128)(2,1)S(1)}, bf16[2,256,256]{2,1,0:T(8,128)(2,1)S(1)}, u32[]{:S(2)}, u32[]{:S(2)}) %collective-permute-start.24) | collective-permute-done | bytes 262176 | tf_op jit(solution)/shard_map/ppermute | solution.py:17
  101.5 2.3 %shard_map.70 = (bf16[2,256,256]{2,1,0:T(8,128)(2,1)S(1)}, bf16[2,256,256]{2,1,0:T(8,128)(2,1)S(1)}, bf16[2,256,256]{2,1,0:T(8,128)(2,1)S(1)}) custom-call(s32[2,8,8]{2,1,0:T(8,128)S(1)} %copy-done.2, bf16[2,256,256]{2,1,0:T(8,128)(2,1)S(1)} %collective-permute-done.24.far.refs_10_, bf16[2,256,256]{2,1,0:T(8,128)(2,1)S(1)} %get-tuple-element.54.refs_0_.refs_9_), custom_call_target="tpu_custom_call" | custom-call | tf_op jit(solution)/shard_map/pallas_call | solution.py:83
  104.1 3.3 %collective-permute-start.27 = (bf16[256,256]{1,0:T(8,128)(2,1)S(1)}, bf16[256,256]{1,0:T(8,128)(2,1)S(1)}, u32[]{:S(2)}, u32[]{:S(2)}) collective-permute-start(bf16[256,256]{1,0:T(8,128)(2,1)S(1)} %get-tuple-element.53), channel_id=1, source_target_pairs={{0,12},{4,8},{8,4},{12,0},{16,28},{20,24},{24,20},{28,16},{1,13},{... | collective-permute-start | bytes 393224 | tf_op jit(solution)/shard_map/ppermute | solution.py:17
  109.0 1.8 %shard_map.73 = (bf16[1,256,256]{2,1,0:T(8,128)(2,1)S(1)}, bf16[1,256,256]{2,1,0:T(8,128)(2,1)S(1)}, bf16[1,256,256]{2,1,0:T(8,128)(2,1)S(1)}) custom-call(s32[2,8,8]{2,1,0:T(8,128)S(1)} %copy-done.2, bf16[2,256,256]{2,1,0:T(8,128)(2,1)S(1)} %collective-permute-done.31.far.refs_10_), custom_call_target="tpu_custom_call" | custom-call | tf_op jit(solution)/shard_map/pallas_call | solution.py:83
  110.8 1.9 %collective-permute-start.32 = (bf16[1,256,256]{2,1,0:T(8,128)(2,1)S(1)}, bf16[1,256,256]{2,1,0:T(8,128)(2,1)S(1)}, u32[]{:S(2)}, u32[]{:S(2)}) collective-permute-start(bf16[1,256,256]{2,1,0:T(8,128)(2,1)S(1)} %get-tuple-element.59), channel_id=1, source_target_pairs={{0,4},{4,0},{8,12},{12,8},{16,20},{20,16},{24,28},{28,24},{1,5},{5... | collective-permute-start | bytes 393224 | tf_op jit(solution)/shard_map/ppermute | solution.py:17
  112.7 1.9 %collective-permute-done.27.refs_13_ = bf16[256,256]{1,0:T(8,128)(2,1)S(1)} collective-permute-done((bf16[256,256]{1,0:T(8,128)(2,1)S(1)}, bf16[256,256]{1,0:T(8,128)(2,1)S(1)}, u32[]{:S(2)}, u32[]{:S(2)}) %collective-permute-start.27) | collective-permute-done | bytes 131104 | tf_op jit(solution)/shard_map/ppermute | solution.py:17
  114.6 1.7 %collective-permute-start.34 = (bf16[1,256,256]{2,1,0:T(8,128)(2,1)S(1)}, bf16[1,256,256]{2,1,0:T(8,128)(2,1)S(1)}, u32[]{:S(2)}, u32[]{:S(2)}) collective-permute-start(bf16[1,256,256]{2,1,0:T(8,128)(2,1)S(1)} %get-tuple-element.61), channel_id=1, source_target_pairs={{0,12},{4,8},{8,4},{12,0},{16,28},{20,24},{24,20},{28,16},{1,13},{... | collective-permute-start | bytes 393224 | tf_op jit(solution)/shard_map/ppermute | solution.py:17
  116.2 4.0 %shard_map.69.refs_8_ = f32[2,256,256]{2,1,0:T(8,128)S(1)} custom-call(s32[2,8,8]{2,1,0:T(8,128)S(1)} %copy-done.2, s32[2,2,8]{2,1,0:T(2,128)S(1)} %copy-done.3, s32[2,2]{1,0:T(2,128)S(1)} %copy-done.4, bf16[2,2,256,256]{3,2,1,0:T(8,128)(2,1)S(1)} %get-tuple-element.63.refs_0_.refs_4_, bf16[2,2,256,256]{3,2,1,0:T(8,128)(2,1)S(1)} %collective-permute-done.21.refs_1_.refs_5_, ...), custom_call_target="tpu_custom_call" | custom-call | tf_op jit(solution)/shard_map/pallas_call | solution.py:83
  120.2 4.2 %shard_map.72.refs_8_ = f32[2,256,256]{2,1,0:T(8,128)S(1)} custom-call(s32[2,8,8]{2,1,0:T(8,128)S(1)} %copy-done.2, s32[2,2,8]{2,1,0:T(2,128)S(1)} %copy-done.3, s32[2,2]{1,0:T(2,128)S(1)} %copy-done.4, bf16[2,2,256,256]{3,2,1,0:T(8,128)(2,1)S(1)} %get-tuple-element.63.refs_0_.refs_4_, bf16[2,2,256,256]{3,2,1,0:T(8,128)(2,1)S(1)} %collective-permute-done.21.refs_1_.refs_5_, ...), custom_call_target="tpu_custom_call" | custom-call | tf_op jit(solution)/shard_map/pallas_call | solution.py:83
  125.8 6.1 %shard_map.71 = (bf16[3,2,256,512]{3,2,1,0:T(8,128)(2,1)}, bf16[2,256,256]{2,1,0:T(8,128)(2,1)}) custom-call(s32[2,8,8]{2,1,0:T(8,128)S(1)} %copy-done.2, s32[2,2,8]{2,1,0:T(2,128)S(1)} %copy-done.3, s32[2,2]{1,0:T(2,128)S(1)} %copy-done.4, bf16[3,2,256,512]{3,2,1,0:T(8,128)(2,1)S(1)} %copy-done, ...), custom_call_target="tpu_custom_call", output_to_operand_aliasing={{0}: (4, {})} | custom-call | tf_op jit(solution)/shard_map/pallas_call | solution.py:83
  131.9 6.1 %shard_map.74 = (bf16[3,2,256,512]{3,2,1,0:T(8,128)(2,1)}, bf16[2,256,256]{2,1,0:T(8,128)(2,1)}) custom-call(s32[2,8,8]{2,1,0:T(8,128)S(1)} %copy-done.2, s32[2,2,8]{2,1,0:T(2,128)S(1)} %copy-done.3, s32[2,2]{1,0:T(2,128)S(1)} %copy-done.4, bf16[3,2,256,512]{3,2,1,0:T(8,128)(2,1)S(1)} %copy-done, ...), custom_call_target="tpu_custom_call", output_to_operand_aliasing={{0}: (4, {})} | custom-call | tf_op jit(solution)/shard_map/pallas_call | solution.py:83
  (62 shorter events, 14.5 us)
Async XLA Ops:
  1.0 7.7 %collective-permute-start.7 = (bf16[2,64,256]{2,1,0:T(8,128)(2,1)S(1)}, bf16[2,64,256]{2,1,0:T(8,128)(2,1)S(1)}, u32[]{:S(2)}, u32[]{:S(2)}) collective-permute-start(bf16[2,64,256]{2,1,0:T(8,128)(2,1)S(1)} %slice_bitcast_fusion.3), channel_id=1, source_target_pairs={{0,16},{4,20},{8,24},{12,28},{16,0},{20,4},{24,8},{28,12},{1,17},{... | collective-permute-start | bytes 196616 | tf_op jit(solution)/shard_map/ppermute | solution.py:17
  9.9 35.9 %collective-permute-start.4 = (bf16[2,2,256,256]{3,2,1,0:T(8,128)(2,1)S(1)}, bf16[2,2,256,256]{3,2,1,0:T(8,128)(2,1)S(1)}, u32[]{:S(2)}, u32[]{:S(2)}) collective-permute-start(bf16[2,2,256,256]{3,2,1,0:T(8,128)(2,1)S(1)} %get-tuple-element.64.refs_4_), channel_id=1, source_target_pairs={{0,2},{1,3},{2,0},{3,1},{4,6},{5,7},{6,4},{7,5},{8,10},{9,11},{10,... | collective-permute-start | bytes 1572872 | tf_op jit(solution)/shard_map/ppermute | solution.py:17
  11.7 34.1 %collective-permute-start.3 = (bf16[2,2,256,256]{3,2,1,0:T(8,128)(2,1)S(1)}, bf16[2,2,256,256]{3,2,1,0:T(8,128)(2,1)S(1)}, u32[]{:S(2)}, u32[]{:S(2)}) collective-permute-start(bf16[2,2,256,256]{3,2,1,0:T(8,128)(2,1)S(1)} %get-tuple-element.64.refs_4_), channel_id=1, source_target_pairs={{0,1},{1,0},{2,3},{3,2},{4,5},{5,4},{6,7},{7,6},{8,9},{9,8},{10,11... | collective-permute-start | bytes 1572872 | tf_op jit(solution)/shard_map/ppermute | solution.py:17
  11.9 19.7 %collective-permute-start = (bf16[3,2,64,256]{3,2,1,0:T(8,128)(2,1)S(1)}, bf16[3,2,64,256]{3,2,1,0:T(8,128)(2,1)S(1)}, u32[]{:S(2)}, u32[]{:S(2)}) collective-permute-start(bf16[3,2,64,256]{3,2,1,0:T(8,128)(2,1)S(1)} %copy-done.1), channel_id=1, source_target_pairs={{0,1},{1,0},{2,3},{3,2},{4,5},{5,4},{6,7},{7,6},{8,9},{9,8},{10,11... | collective-permute-start | bytes 589832 | tf_op jit(solution)/shard_map/ppermute | solution.py:17
  12.2 16.7 %collective-permute-start.1 = (bf16[3,2,64,256]{3,2,1,0:T(8,128)(2,1)S(1)}, bf16[3,2,64,256]{3,2,1,0:T(8,128)(2,1)S(1)}, u32[]{:S(2)}, u32[]{:S(2)}) collective-permute-start(bf16[3,2,64,256]{3,2,1,0:T(8,128)(2,1)S(1)} %copy-done.1), channel_id=1, source_target_pairs={{0,2},{1,3},{2,0},{3,1},{4,6},{5,7},{6,4},{7,5},{8,10},{9,11},{10,... | collective-permute-start | bytes 589832 | tf_op jit(solution)/shard_map/ppermute | solution.py:17
  12.6 17.4 %collective-permute-start.9 = (bf16[2,64,256]{2,1,0:T(8,128)(2,1)S(1)}, bf16[2,64,256]{2,1,0:T(8,128)(2,1)S(1)}, u32[]{:S(2)}, u32[]{:S(2)}) collective-permute-start(bf16[2,64,256]{2,1,0:T(8,128)(2,1)S(1)} %collective-permute-done.7.refs_0_), channel_id=1, source_target_pairs={{0,2},{1,3},{2,0},{3,1},{4,6},{5,7},{6,4},{7,5},{8,10},{9,11},{10,... | collective-permute-start | bytes 196616 | tf_op jit(solution)/shard_map/ppermute | solution.py:17
  30.0 25.0 %collective-permute-start.22 = (bf16[2,2,256,256]{3,2,1,0:T(8,128)(2,1)S(1)}, bf16[2,2,256,256]{3,2,1,0:T(8,128)(2,1)S(1)}, u32[]{:S(2)}, u32[]{:S(2)}) collective-permute-start(bf16[2,2,256,256]{3,2,1,0:T(8,128)(2,1)S(1)} %get-tuple-element.63.refs_0_.refs_4_), channel_id=1, source_target_pairs={{0,2},{1,3},{2,0},{3,1},{4,6},{5,7},{6,4},{7,5},{8,10},{9,11},{10,... | collective-permute-start | bytes 1572872 | tf_op jit(solution)/shard_map/ppermute | solution.py:17
  31.7 14.2 %collective-permute-start.6 = (bf16[2,256,256]{2,1,0:T(8,128)(2,1)S(1)}, bf16[2,256,256]{2,1,0:T(8,128)(2,1)S(1)}, u32[]{:S(2)}, u32[]{:S(2)}) collective-permute-start(bf16[2,256,256]{2,1,0:T(8,128)(2,1)S(1)} %slice_bitcast_fusion.2), channel_id=1, source_target_pairs={{0,16},{4,20},{8,24},{12,28},{16,0},{20,4},{24,8},{28,12},{1,17},{... | collective-permute-start | bytes 786440 | tf_op jit(solution)/shard_map/ppermute | solution.py:17
  35.6 15.7 %collective-permute-start.11 = (bf16[256,256]{1,0:T(8,128)(2,1)S(1)}, bf16[256,256]{1,0:T(8,128)(2,1)S(1)}, u32[]{:S(2)}, u32[]{:S(2)}) collective-permute-start(bf16[256,256]{1,0:T(8,128)(2,1)S(1)} %get-tuple-element.37), channel_id=1, source_target_pairs={{0,4},{4,0},{8,12},{12,8},{16,20},{20,16},{24,28},{28,24},{1,5},{5... | collective-permute-start | bytes 393224 | tf_op jit(solution)/shard_map/ppermute | solution.py:17
  45.8 6.1 %collective-permute-start.12 = (bf16[256,256]{1,0:T(8,128)(2,1)S(1)}, bf16[256,256]{1,0:T(8,128)(2,1)S(1)}, u32[]{:S(2)}, u32[]{:S(2)}) collective-permute-start(bf16[256,256]{1,0:T(8,128)(2,1)S(1)} %get-tuple-element.38), channel_id=1, source_target_pairs={{0,8},{4,12},{8,0},{12,4},{16,24},{20,28},{24,16},{28,20},{1,9},{5... | collective-permute-start | bytes 393224 | tf_op jit(solution)/shard_map/ppermute | solution.py:17
  45.8 27.4 %collective-permute-start.5 = (bf16[2,2,256,256]{3,2,1,0:T(8,128)(2,1)S(1)}, bf16[2,2,256,256]{3,2,1,0:T(8,128)(2,1)S(1)}, u32[]{:S(2)}, u32[]{:S(2)}) collective-permute-start(bf16[2,2,256,256]{3,2,1,0:T(8,128)(2,1)S(1)} %collective-permute-done.4.refs_6_), channel_id=1, source_target_pairs={{0,1},{1,0},{2,3},{3,2},{4,5},{5,4},{6,7},{7,6},{8,9},{9,8},{10,11... | collective-permute-start | bytes 1572872 | tf_op jit(solution)/shard_map/ppermute | solution.py:17
  45.9 8.6 %collective-permute-start.13 = (bf16[256,256]{1,0:T(8,128)(2,1)S(1)}, bf16[256,256]{1,0:T(8,128)(2,1)S(1)}, u32[]{:S(2)}, u32[]{:S(2)}) collective-permute-start(bf16[256,256]{1,0:T(8,128)(2,1)S(1)} %get-tuple-element.39), channel_id=1, source_target_pairs={{0,12},{4,8},{8,4},{12,0},{16,28},{20,24},{24,20},{28,16},{1,13},{... | collective-permute-start | bytes 393224 | tf_op jit(solution)/shard_map/ppermute | solution.py:17
  51.4 8.7 %collective-permute-start.14 = (bf16[2,256,256]{2,1,0:T(8,128)(2,1)S(1)}, bf16[2,256,256]{2,1,0:T(8,128)(2,1)S(1)}, u32[]{:S(2)}, u32[]{:S(2)}) collective-permute-start(bf16[2,256,256]{2,1,0:T(8,128)(2,1)S(1)} %get-tuple-element.40), channel_id=1, source_target_pairs={{0,4},{4,0},{8,12},{12,8},{16,20},{20,16},{24,28},{28,24},{1,5},{5... | collective-permute-start | bytes 786440 | tf_op jit(solution)/shard_map/ppermute | solution.py:17
  52.0 14.5 %collective-permute-start.17 = (bf16[2,256,256]{2,1,0:T(8,128)(2,1)S(1)}, bf16[2,256,256]{2,1,0:T(8,128)(2,1)S(1)}, u32[]{:S(2)}, u32[]{:S(2)}) collective-permute-start(bf16[2,256,256]{2,1,0:T(8,128)(2,1)S(1)} %get-tuple-element.44), channel_id=1, source_target_pairs={{0,16},{4,20},{8,24},{12,28},{16,0},{20,4},{24,8},{28,12},{1,17},{... | collective-permute-start | bytes 786440 | tf_op jit(solution)/shard_map/ppermute | solution.py:17
  54.4 14.8 %collective-permute-start.15 = (bf16[2,256,256]{2,1,0:T(8,128)(2,1)S(1)}, bf16[2,256,256]{2,1,0:T(8,128)(2,1)S(1)}, u32[]{:S(2)}, u32[]{:S(2)}) collective-permute-start(bf16[2,256,256]{2,1,0:T(8,128)(2,1)S(1)} %get-tuple-element.41), channel_id=1, source_target_pairs={{0,8},{4,12},{8,0},{12,4},{16,24},{20,28},{24,16},{28,20},{1,9},{5... | collective-permute-start | bytes 786440 | tf_op jit(solution)/shard_map/ppermute | solution.py:17
  55.0 18.3 %collective-permute-start.16 = (bf16[2,256,256]{2,1,0:T(8,128)(2,1)S(1)}, bf16[2,256,256]{2,1,0:T(8,128)(2,1)S(1)}, u32[]{:S(2)}, u32[]{:S(2)}) collective-permute-start(bf16[2,256,256]{2,1,0:T(8,128)(2,1)S(1)} %get-tuple-element.42), channel_id=1, source_target_pairs={{0,12},{4,8},{8,4},{12,0},{16,28},{20,24},{24,20},{28,16},{1,13},{... | collective-permute-start | bytes 786440 | tf_op jit(solution)/shard_map/ppermute | solution.py:17
  60.0 44.0 %collective-permute-start.21 = (bf16[2,2,256,256]{3,2,1,0:T(8,128)(2,1)S(1)}, bf16[2,2,256,256]{3,2,1,0:T(8,128)(2,1)S(1)}, u32[]{:S(2)}, u32[]{:S(2)}) collective-permute-start(bf16[2,2,256,256]{3,2,1,0:T(8,128)(2,1)S(1)} %get-tuple-element.63.refs_0_.refs_4_), channel_id=1, source_target_pairs={{0,1},{1,0},{2,3},{3,2},{4,5},{5,4},{6,7},{7,6},{8,9},{9,8},{10,11... | collective-permute-start | bytes 1572872 | tf_op jit(solution)/shard_map/ppermute | solution.py:17
  66.5 37.6 %collective-permute-start.23 = (bf16[2,2,256,256]{3,2,1,0:T(8,128)(2,1)S(1)}, bf16[2,2,256,256]{3,2,1,0:T(8,128)(2,1)S(1)}, u32[]{:S(2)}, u32[]{:S(2)}) collective-permute-start(bf16[2,2,256,256]{3,2,1,0:T(8,128)(2,1)S(1)} %collective-permute-done.22.refs_2_.refs_6_), channel_id=1, source_target_pairs={{0,1},{1,0},{2,3},{3,2},{4,5},{5,4},{6,7},{7,6},{8,9},{9,8},{10,11... | collective-permute-start | bytes 1572872 | tf_op jit(solution)/shard_map/ppermute | solution.py:17
  69.2 12.1 %collective-permute-start.18 = (bf16[1,256,256]{2,1,0:T(8,128)(2,1)S(1)}, bf16[1,256,256]{2,1,0:T(8,128)(2,1)S(1)}, u32[]{:S(2)}, u32[]{:S(2)}) collective-permute-start(bf16[1,256,256]{2,1,0:T(8,128)(2,1)S(1)} %get-tuple-element.46), channel_id=1, source_target_pairs={{0,4},{4,0},{8,12},{12,8},{16,20},{20,16},{24,28},{28,24},{1,5},{5... | collective-permute-start | bytes 393224 | tf_op jit(solution)/shard_map/ppermute | solution.py:17
  73.2 10.4 %collective-permute-start.19 = (bf16[1,256,256]{2,1,0:T(8,128)(2,1)S(1)}, bf16[1,256,256]{2,1,0:T(8,128)(2,1)S(1)}, u32[]{:S(2)}, u32[]{:S(2)}) collective-permute-start(bf16[1,256,256]{2,1,0:T(8,128)(2,1)S(1)} %get-tuple-element.47), channel_id=1, source_target_pairs={{0,8},{4,12},{8,0},{12,4},{16,24},{20,28},{24,16},{28,20},{1,9},{5... | collective-permute-start | bytes 393224 | tf_op jit(solution)/shard_map/ppermute | solution.py:17
  73.2 10.4 %collective-permute-start.20 = (bf16[1,256,256]{2,1,0:T(8,128)(2,1)S(1)}, bf16[1,256,256]{2,1,0:T(8,128)(2,1)S(1)}, u32[]{:S(2)}, u32[]{:S(2)}) collective-permute-start(bf16[1,256,256]{2,1,0:T(8,128)(2,1)S(1)} %get-tuple-element.48), channel_id=1, source_target_pairs={{0,12},{4,8},{8,4},{12,0},{16,28},{20,24},{24,20},{28,16},{1,13},{... | collective-permute-start | bytes 393224 | tf_op jit(solution)/shard_map/ppermute | solution.py:17
  81.3 20.2 %collective-permute-start.24 = (bf16[2,256,256]{2,1,0:T(8,128)(2,1)S(1)}, bf16[2,256,256]{2,1,0:T(8,128)(2,1)S(1)}, u32[]{:S(2)}, u32[]{:S(2)}) collective-permute-start(bf16[2,256,256]{2,1,0:T(8,128)(2,1)S(1)} %get-tuple-element.50.refs_9_), channel_id=1, source_target_pairs={{0,16},{4,20},{8,24},{12,28},{16,0},{20,4},{24,8},{28,12},{1,17},{... | collective-permute-start | bytes 786440 | tf_op jit(solution)/shard_map/ppermute | solution.py:17
  89.9 17.6 %collective-permute-start.31 = (bf16[2,256,256]{2,1,0:T(8,128)(2,1)S(1)}, bf16[2,256,256]{2,1,0:T(8,128)(2,1)S(1)}, u32[]{:S(2)}, u32[]{:S(2)}) collective-permute-start(bf16[2,256,256]{2,1,0:T(8,128)(2,1)S(1)} %get-tuple-element.54.refs_0_.refs_9_), channel_id=1, source_target_pairs={{0,16},{4,20},{8,24},{12,28},{16,0},{20,4},{24,8},{28,12},{1,17},{... | collective-permute-start | bytes 786440 | tf_op jit(solution)/shard_map/ppermute | solution.py:17
  90.6 16.8 %collective-permute-start.25 = (bf16[256,256]{1,0:T(8,128)(2,1)S(1)}, bf16[256,256]{1,0:T(8,128)(2,1)S(1)}, u32[]{:S(2)}, u32[]{:S(2)}) collective-permute-start(bf16[256,256]{1,0:T(8,128)(2,1)S(1)} %get-tuple-element.51), channel_id=1, source_target_pairs={{0,4},{4,0},{8,12},{12,8},{16,20},{20,16},{24,28},{28,24},{1,5},{5... | collective-permute-start | bytes 393224 | tf_op jit(solution)/shard_map/ppermute | solution.py:17
  103.8 10.8 %collective-permute-start.28 = (bf16[2,256,256]{2,1,0:T(8,128)(2,1)S(1)}, bf16[2,256,256]{2,1,0:T(8,128)(2,1)S(1)}, u32[]{:S(2)}, u32[]{:S(2)}) collective-permute-start(bf16[2,256,256]{2,1,0:T(8,128)(2,1)S(1)} %get-tuple-element.55), channel_id=1, source_target_pairs={{0,4},{4,0},{8,12},{12,8},{16,20},{20,16},{24,28},{28,24},{1,5},{5... | collective-permute-start | bytes 786440 | tf_op jit(solution)/shard_map/ppermute | solution.py:17
  104.1 6.8 %collective-permute-start.26 = (bf16[256,256]{1,0:T(8,128)(2,1)S(1)}, bf16[256,256]{1,0:T(8,128)(2,1)S(1)}, u32[]{:S(2)}, u32[]{:S(2)}) collective-permute-start(bf16[256,256]{1,0:T(8,128)(2,1)S(1)} %get-tuple-element.52), channel_id=1, source_target_pairs={{0,8},{4,12},{8,0},{12,4},{16,24},{20,28},{24,16},{28,20},{1,9},{5... | collective-permute-start | bytes 393224 | tf_op jit(solution)/shard_map/ppermute | solution.py:17
  104.1 10.5 %collective-permute-start.27 = (bf16[256,256]{1,0:T(8,128)(2,1)S(1)}, bf16[256,256]{1,0:T(8,128)(2,1)S(1)}, u32[]{:S(2)}, u32[]{:S(2)}) collective-permute-start(bf16[256,256]{1,0:T(8,128)(2,1)S(1)} %get-tuple-element.53), channel_id=1, source_target_pairs={{0,12},{4,8},{8,4},{12,0},{16,28},{20,24},{24,20},{28,16},{1,13},{... | collective-permute-start | bytes 393224 | tf_op jit(solution)/shard_map/ppermute | solution.py:17
  107.4 17.0 %collective-permute-start.29 = (bf16[2,256,256]{2,1,0:T(8,128)(2,1)S(1)}, bf16[2,256,256]{2,1,0:T(8,128)(2,1)S(1)}, u32[]{:S(2)}, u32[]{:S(2)}) collective-permute-start(bf16[2,256,256]{2,1,0:T(8,128)(2,1)S(1)} %get-tuple-element.56), channel_id=1, source_target_pairs={{0,8},{4,12},{8,0},{12,4},{16,24},{20,28},{24,16},{28,20},{1,9},{5... | collective-permute-start | bytes 786440 | tf_op jit(solution)/shard_map/ppermute | solution.py:17
  107.4 18.4 %collective-permute-start.30 = (bf16[2,256,256]{2,1,0:T(8,128)(2,1)S(1)}, bf16[2,256,256]{2,1,0:T(8,128)(2,1)S(1)}, u32[]{:S(2)}, u32[]{:S(2)}) collective-permute-start(bf16[2,256,256]{2,1,0:T(8,128)(2,1)S(1)} %get-tuple-element.57), channel_id=1, source_target_pairs={{0,12},{4,8},{8,4},{12,0},{16,28},{20,24},{24,20},{28,16},{1,13},{... | collective-permute-start | bytes 786440 | tf_op jit(solution)/shard_map/ppermute | solution.py:17
  110.8 21.0 %collective-permute-start.32 = (bf16[1,256,256]{2,1,0:T(8,128)(2,1)S(1)}, bf16[1,256,256]{2,1,0:T(8,128)(2,1)S(1)}, u32[]{:S(2)}, u32[]{:S(2)}) collective-permute-start(bf16[1,256,256]{2,1,0:T(8,128)(2,1)S(1)} %get-tuple-element.59), channel_id=1, source_target_pairs={{0,4},{4,0},{8,12},{12,8},{16,20},{20,16},{24,28},{28,24},{1,5},{5... | collective-permute-start | bytes 393224 | tf_op jit(solution)/shard_map/ppermute | solution.py:17
  114.6 17.3 %collective-permute-start.33 = (bf16[1,256,256]{2,1,0:T(8,128)(2,1)S(1)}, bf16[1,256,256]{2,1,0:T(8,128)(2,1)S(1)}, u32[]{:S(2)}, u32[]{:S(2)}) collective-permute-start(bf16[1,256,256]{2,1,0:T(8,128)(2,1)S(1)} %get-tuple-element.60), channel_id=1, source_target_pairs={{0,8},{4,12},{8,0},{12,4},{16,24},{20,28},{24,16},{28,20},{1,9},{5... | collective-permute-start | bytes 393224 | tf_op jit(solution)/shard_map/ppermute | solution.py:17
  114.6 17.3 %collective-permute-start.34 = (bf16[1,256,256]{2,1,0:T(8,128)(2,1)S(1)}, bf16[1,256,256]{2,1,0:T(8,128)(2,1)S(1)}, u32[]{:S(2)}, u32[]{:S(2)}) collective-permute-start(bf16[1,256,256]{2,1,0:T(8,128)(2,1)S(1)} %get-tuple-element.61), channel_id=1, source_target_pairs={{0,12},{4,8},{8,4},{12,0},{16,28},{20,24},{24,20},{28,16},{1,13},{... | collective-permute-start | bytes 393224 | tf_op jit(solution)/shard_map/ppermute | solution.py:17
  (8 other events, 148.7 us)

commit v4 on v3

--- a/solution.py
+++ b/solution.py
@@ -62,24 +62,19 @@
     return [copies.start(part, target.at[draw ^ step]) for step, part in enumerate(parts)]
 
 
-def add_slots(total, table, blocks, lists, counts, source, myself):
-    owners = table.shape[0]
-    draws, nodes, width = blocks.shape[:3]
-    for part in range(draws):
-        for offset in range(width):
-            slot = part * width + offset
-            for node in range(nodes):
-                entry = lists(node, slot) - source * owners
-                live = (slot < counts(node)) & (entry >= 0) & (entry < owners)
-
-                @pl.when(live)
-                def _():
-                    total[node] += transposed_dot(
-                        blocks[part, node, offset], table[entry ^ myself]
-                    )
-
-
-def call(kernel, outs, scratch, small, arrays, aliases={}, sems=64, flops=0):
+def coupled(node, table, blocks, entries, count, owners, myself):
+    draws, _, width = blocks.shape[:3]
+    empty = table.shape[0] - 1
+    total = None
+    for slot in range(draws * width):
+        entry = jnp.where(slot < count, entries(slot) ^ myself, empty)
+        term = transposed_dot(blocks[slot // width, node, slot % width], table[entry])
+        total = term if total is None else total + term
+    return total
+
+
+def call(kernel, outs, scratch, small, arrays, aliases={}):
+    sems = len(arrays) + 2 * len(outs)
     return pl.pallas_call(
         kernel,
         out_shape=outs,
@@ -95,20 +90,21 @@
     return picks[source, myself ^ step, myself ^ origin]
 
 
-def own_first(owners, draws, wide, picks, noise, *refs):
+def own_first(owners, draws, wide, picks, noise, coupling, *refs):
     inverse, refs = refs[:draws], refs[draws:]
-    out, own, *rest = refs
+    out, own, blocks, *rest = refs
     chunks = noise.shape[-1] // wide
     nexts, rest = rest[:chunks - 1], rest[chunks - 1:]
     sends, (right, inv, solved, sems) = rest[:-4], rest[-4:]
     myself = lax.axis_index("leaf")
     copies = Copies(sems)
+    loads = [copies.start(noise.at[0], right)]
+    loads += load_rows(copies, inv, [part.at[0] for part in inverse])
     stores = [
         copies.start(noise.at[0, :, :, pl.ds(at * wide, wide)], target)
         for at, target in enumerate(nexts, 1)
     ]
-    loads = [copies.start(noise.at[0], right)]
-    loads += load_rows(copies, inv, [part.at[0] for part in inverse])
+    stores.append(copies.start(coupling.at[0], blocks))
     wait_all(loads)
     for node in range(inv.shape[0]):
         solved[node] = transposed_dot(inv[node], right[node]).astype(BF16)
@@ -119,15 +115,16 @@
     wait_all(stores)
 
 
-def far_first(owners, draws, wide, chunk, last, picks, far, own, *refs):
+def far_first(owners, draws, wide, chunk, last, picks, far, own, coupling, *refs):
     half = owners // 2
     inverse, refs = refs[:draws], refs[draws:]
     mine, *rest = refs
+    later, rest = (rest[:coupling.shape[0] - 1], rest[coupling.shape[0] - 1:]) if chunk == 0 else ([], rest)
     sends, (right, inv, solved, sems) = rest[:-4], rest[-4:]
     myself = lax.axis_index("leaf")
     copies = Copies(sems)
     loads = [copies.start(far, right)] + load_rows(copies, inv, inverse)
-    stores = []
+    stores = [copies.start(coupling.at[at], target) for at, target in enumerate(later, 1)]
     if not last:
         columns = pl.ds((chunk + 1) * wide, wide)
         for step, send in enumerate(sends, 1):
@@ -165,14 +162,15 @@
     columns = pl.ds(chunk * wide, wide)
     node = here_pick(picks, source, myself, 0, 0)
     whole = own.shape[-1] != wide
-    loads = [copies.start(own.at[node, :, columns] if whole else own.at[node], table.at[0])]
+    first = source * owners
+    loads = [copies.start(own.at[node, :, columns] if whole else own.at[node], table.at[first])]
     if len(far.shape) == 3:
         far = far.at[here_pick(picks, source, myself, 0, half)]
-    loads.append(copies.start(far, table.at[half]))
+    loads.append(copies.start(far, table.at[first + half]))
     for step in range(1, half):
         ref = near[step - 1]
-        loads.append(copies.start(ref if len(ref.shape) == 2 else ref.at[1], table.at[step]))
-        loads.append(copies.start(distant[step - 1].at[0], table.at[half ^ step]))
+        loads.append(copies.start(ref if len(ref.shape) == 2 else ref.at[1], table.at[first + step]))
+        loads.append(copies.start(distant[step - 1].at[0], table.at[first + (half ^ step)]))
     return loads
 
 
@@ -182,55 +180,42 @@
     return (own, far, refs[2:2 + side], refs[2 + side:2 + 2 * side]), refs[2 + 2 * side:]
 
 
-def partial_kernel(level, source, owners, draws, wide, chunk, picks, lists, counts, *refs):
-    blocks, refs = refs[:draws], refs[draws:]
-    pieces, refs = split_pieces(owners, refs)
-    result, table, coupling, total, sems = refs
-    myself = lax.axis_index("leaf")
-    copies = Copies(sems)
-    loads = load_blocks(copies, coupling, blocks)
-    loads += table_loads(copies, owners, wide, chunk, source, picks, myself, pieces, table)
-    total[...] = jnp.zeros_like(total)
-    wait_all(loads)
-    add_slots(
-        total, table, coupling, lambda node, slot: lists[level - 1, node, slot],
-        lambda node: counts[level - 1, node], source, myself,
-    )
-    copies.start(total, result).wait()
-
-
 def level_kernel(
-    level, owners, draws, wide, chunk, befores, sending,
-    picks, lists, counts, noise, out_before, *refs,
+    level, owners, draws, wide, chunk, sending, picks, lists, counts, noise, out_before, *refs
 ):
     inverse, refs = refs[:draws], refs[draws:]
     blocks, refs = refs[:draws], refs[draws:]
-    befores_in, refs = refs[:befores], refs[befores:]
-    pieces, refs = split_pieces(owners, refs)
+    pieces = []
+    for _ in range(level):
+        piece, refs = split_pieces(owners, refs)
+        pieces.append(piece)
     out, solved, *refs = refs
     side = owners // 2 - 1 if sending else 0
-    sends, (table, coupling, total, inv, right, here, sems) = refs[:side], refs[side:]
+    sends, (table, coupling, inv, right, here, sems) = refs[:side], refs[side:]
     myself = lax.axis_index("leaf")
     copies = Copies(sems)
-    source = level - 1
     columns = pl.ds(chunk * wide, wide)
-    loads = [copies.start(before, total) for before in befores_in]
-    if not befores:
-        total[...] = jnp.zeros_like(total)
-    loads += load_blocks(copies, coupling, blocks)
-    loads += table_loads(copies, owners, wide, chunk, source, picks, myself, pieces, table)
+    loads = load_blocks(copies, coupling, blocks)
+    for source, piece in enumerate(pieces):
+        loads += table_loads(copies, owners, wide, chunk, source, picks, myself, piece, table)
     later = [copies.start(noise.at[level, :, :, columns], right)]
     later += load_rows(copies, inv, [part.at[level] for part in inverse])
+    table[level * owners] = jnp.zeros_like(table[level * owners])
     wait_all(loads)
-    add_slots(
-        total, table, coupling, lambda node, slot: lists[level - 1, node, slot],
-        lambda node: counts[level - 1, node], source, myself,
-    )
+    nodes = inv.shape[0]
+    totals = [
+        coupled(
+            node, table, coupling, lambda slot: lists[level - 1, node, slot],
+            counts[level - 1, node], owners, myself,
+        )
+        for node in range(nodes)
+    ]
     wait_all(later)
-    for node in range(inv.shape[0]):
-        side_here = (right[node].astype(F32) - total[node]).astype(BF16)
+    stores = []
+    for node in range(nodes):
+        side_here = (right[node].astype(F32) - totals[node]).astype(BF16)
         here[node] = transposed_dot(inv[node], side_here).astype(BF16)
-    stores = [copies.start(here, out.at[level, :, :, columns]), copies.start(here, solved)]
+    stores += [copies.start(here, solved), copies.start(here, out.at[level, :, :, columns])]
     for step, send in enumerate(sends, 1):
         node = here_pick(picks, level, myself, step, 0)
         stores.append(copies.start(here.at[node], send))
@@ -245,9 +230,8 @@
     block = shape(rows, wide)
     message = shape(2, rows, wide)
     part = shape(nodes, rows, wide)
-    table = pltpu.VMEM((owners, rows, wide), BF16)
+    table = lambda level: pltpu.VMEM((level * owners + 1, rows, wide), BF16)
     blocks_here = pltpu.VMEM((draws, nodes, width, rows, rows), BF16)
-    total = pltpu.VMEM((nodes, rows, wide), F32)
     inv = pltpu.VMEM((nodes, rows, rows), BF16)
     chunk_here = pltpu.VMEM((nodes, rows, wide), BF16)
     leaf = lambda value, step: hop(value, "leaf", owners, step)
@@ -259,16 +243,16 @@
     far = [leaf(noise[0, :, :, :wide], half)]
     inverse_all = gather(inverse)
     far_inverse_all = gather(far_inverse)
-    blocks = [gather(coupling[at]) for at in range(levels - 1)]
-
-    out, own, *sends = call(
+
+    out, own, first, *sends = call(
         functools.partial(own_first, owners, draws, wide),
-        [shape(levels, nodes, rows, columns), shape(nodes, rows, columns)]
+        [shape(levels, nodes, rows, columns), shape(nodes, rows, columns), shape(*coupling.shape[1:])]
         + [part] * (CHUNKS - 1) + [block] * (half - 1),
         [pltpu.VMEM((nodes, rows, columns), BF16), inv, pltpu.VMEM((nodes, rows, columns), BF16)],
         (picks,),
-        (noise, *inverse_all),
+        (noise, coupling, *inverse_all),
     )
+    blocks = [gather(first)]
     far += [leaf(piece, half) for piece in sends[:CHUNKS - 1]]
     got = [near(sends[CHUNKS - 1:])]
     mine = []
@@ -276,36 +260,32 @@
         last = at == CHUNKS - 1
         kept, *sends = call(
             functools.partial(far_first, owners, draws, wide, at, last),
-            [block] + [shape(1, rows, wide) if last else message] * (half - 1),
+            [block] + ([shape(*coupling.shape[1:])] * (levels - 2) if at == 0 else [])
+            + [shape(1, rows, wide) if last else message] * (half - 1),
             [chunk_here, inv, chunk_here],
             (picks,),
-            (far[at], own, *far_inverse_all),
+            (far[at], own, coupling, *far_inverse_all),
         )
         mine.append(kept)
+        if at == 0:
+            blocks += [gather(value) for value in sends[:levels - 2]]
+            sends = sends[levels - 2:]
         got.append(near(sends))
     pieces = [[(own, mine[at], *got[at], *got[at + 1]) for at in chunks]]
 
     for level in range(1, levels):
         solved, sends = [], []
         for at in chunks:
-            befores = [
-                call(
-                    functools.partial(partial_kernel, level, source, owners, draws, wide, at),
-                    shape(nodes, rows, wide, kind=F32),
-                    [table, blocks_here, total],
-                    (picks, lists, counts),
-                    (*blocks[level - 1], *pieces[source][at]),
-                )
-                for source in range(level - 1)
-            ]
-            befores = [functools.reduce(jnp.add, befores)] if befores else []
             sending = at == 0 and level < levels - 1
             out, here, *sent = call(
-                functools.partial(level_kernel, level, owners, draws, wide, at, len(befores), sending),
+                functools.partial(level_kernel, level, owners, draws, wide, at, sending),
                 [shape(*out.shape), part] + ([block] * (half - 1) if sending else []),
-                [table, blocks_here, total, inv, chunk_here, chunk_here],
+                [table(level), blocks_here, inv, chunk_here, chunk_here],
                 (picks, lists, counts),
-                (noise, out, *inverse_all, *blocks[level - 1], *befores, *pieces[level - 1][at]),
+                (
+                    noise, out, *inverse_all, *blocks[level - 1],
+                    *(ref for source in range(level) for ref in pieces[source][at]),
+                ),
                 aliases={4: 0},
             )
             solved.append(here)

time: 138 us -> 130 us (0.942)
  Pallas kernels: 44.3 us -> 29.9 us
  waiting for transfers between devices: 54.7 us -> 58.4 us
  local copies, waits for them, and re-layouts: 2.28 us -> 5.26 us
    pallas_call x11 -> x9, Pallas kernels: 44.3 us -> 29.9 us  [call(): pl.pallas_call(kernel, out_shape=outs, in_specs=[SMEM] * len(small) + [HB...]
    unnamed x10 -> x18, local copies, waits for them, and re-layouts: 0.02 us -> 4.28 us
    ppermute x35, waiting for transfers between devices: 54.7 us -> 58.4 us  [hop(): return lax.ppermute(value, axis, [(at, at ^ step) for at in range(size)])]
  transfers between devices with their start and end apart: 35 -> 35, of which waited for: 12 -> 15; matrix products, arithmetic and copies ran while one was open for 1% -> 1% of each run, Pallas kernels for 28% -> 18%
where the time goes in v4:
time: 130 us
  waiting for transfers between devices  58.4 us (45%)
  starting transfers between devices  36.2 us (28%)
  Pallas kernels  29.9 us (23%)
  local copies, waits for them, and re-layouts  5.26 us (4%)
    ppermute x35, waiting for transfers between devices, hop(): return lax.ppermute(value, axis, [(at, at ^ step) for at in range(size)])  58.4 us
    ppermute x35, starting transfers between devices, hop(): return lax.ppermute(value, axis, [(at, at ^ step) for at in range(size)])  36.2 us
    pallas_call x9, Pallas kernels, call(): pl.pallas_call(kernel, out_shape=outs, in_specs=[SMEM] * len(small) + [HB...  29.9 us
    unnamed x18, local copies, waits for them, and re-layouts  4.28 us
  transfers between devices with their start and end apart: 35, of which 15 were waited for; matrix products, arithmetic and copies ran while one was open for 1% of the time, Pallas kernels for 18%

profile of v4, /device:TPU:0, one launch (start us, length us, event | category | flops | bytes accessed | tf_op | source)
XLA Modules:
  0.0 130.0 jit_solution(14278594705847267899)
XLA Ops:
  0.0 2.9 %collective-permute-start.1 = (bf16[3,2,64,256]{3,2,1,0:T(8,128)(2,1)}, bf16[3,2,64,256]{3,2,1,0:T(8,128)(2,1)S(1)}, u32[]{:S(2)}, u32[]{:S(2)}) collective-permute-start(bf16[3,2,64,256]{3,2,1,0:T(8,128)(2,1)} %refs_0_.9), channel_id=1, source_target_pairs={{0,2},{1,3},{2,0},{3,1},{4,6},{5,7},{6,4},{7,5},{8,10},{9,11},{10,... | collective-permute-start | bytes 589832 | tf_op jit(solution)/shard_map/ppermute | solution.py:17
  2.9 5.1 %collective-permute-done.1.refs_2_ = bf16[3,2,64,256]{3,2,1,0:T(8,128)(2,1)S(1)} collective-permute-done((bf16[3,2,64,256]{3,2,1,0:T(8,128)(2,1)}, bf16[3,2,64,256]{3,2,1,0:T(8,128)(2,1)S(1)}, u32[]{:S(2)}, u32[]{:S(2)}) %collective-permute-start.1) | collective-permute-done | bytes 196640 | tf_op jit(solution)/shard_map/ppermute | solution.py:17
  9.0 2.9 %collective-permute-start.6 = (bf16[2,256,256]{2,1,0:T(8,128)(2,1)S(1)}, bf16[2,256,256]{2,1,0:T(8,128)(2,1)S(1)}, u32[]{:S(2)}, u32[]{:S(2)}) collective-permute-start(bf16[2,256,256]{2,1,0:T(8,128)(2,1)S(1)} %slice_bitcast_fusion), channel_id=1, source_target_pairs={{0,16},{4,20},{8,24},{12,28},{16,0},{20,4},{24,8},{28,12},{1,17},{... | collective-permute-start | bytes 786440 | tf_op jit(solution)/shard_map/ppermute | solution.py:17
  16.2 2.2 %shard_map.64 = (bf16[3,2,256,512]{3,2,1,0:T(8,128)(2,1)}, bf16[2,256,512]{2,1,0:T(8,128)(2,1)S(1)}, bf16[2,2,256,256]{3,2,1,0:T(8,128)(2,1)S(1)}, bf16[2,256,25...) custom-call(s32[2,8,8]{2,1,0:T(8,128)S(1)} %copy-done.6, ...), custom_call_target="tpu_custom_call" | custom-call | tf_op jit(solution)/shard_map/pallas_call | solution.py:78
  18.4 1.6 %collective-permute-start.4 = (bf16[2,2,256,256]{3,2,1,0:T(8,128)(2,1)S(1)}, bf16[2,2,256,256]{3,2,1,0:T(8,128)(2,1)S(1)}, u32[]{:S(2)}, u32[]{:S(2)}) collective-permute-start(bf16[2,2,256,256]{3,2,1,0:T(8,128)(2,1)S(1)} %get-tuple-element.37.refs_4_), channel_id=1, source_target_pairs={{0,2},{1,3},{2,0},{3,1},{4,6},{5,7},{6,4},{7,5},{8,10},{9,11},{10,... | collective-permute-start | bytes 1572872 | tf_op jit(solution)/shard_map/ppermute | solution.py:17
  20.4 6.9 %collective-permute-done.7.refs_0_ = bf16[2,64,256]{2,1,0:T(8,128)(2,1)S(1)} collective-permute-done((bf16[2,64,256]{2,1,0:T(8,128)(2,1)S(1)}, bf16[2,64,256]{2,1,0:T(8,128)(2,1)S(1)}, u32[]{:S(2)}, u32[]{:S(2)}) %collective-permute-start.7) | collective-permute-done | bytes 65568 | tf_op jit(solution)/shard_map/ppermute | solution.py:17
  27.3 1.5 %collective-permute-start.9 = (bf16[2,64,256]{2,1,0:T(8,128)(2,1)S(1)}, bf16[2,64,256]{2,1,0:T(8,128)(2,1)S(1)}, u32[]{:S(2)}, u32[]{:S(2)}) collective-permute-start(bf16[2,64,256]{2,1,0:T(8,128)(2,1)S(1)} %collective-permute-done.7.refs_0_), channel_id=1, source_target_pairs={{0,2},{1,3},{2,0},{3,1},{4,6},{5,7},{6,4},{7,5},{8,10},{9,11},{10,... | collective-permute-start | bytes 196616 | tf_op jit(solution)/shard_map/ppermute | solution.py:17
  30.4 3.6 %collective-permute-done.9.refs_2_ = bf16[2,64,256]{2,1,0:T(8,128)(2,1)S(1)} collective-permute-done((bf16[2,64,256]{2,1,0:T(8,128)(2,1)S(1)}, bf16[2,64,256]{2,1,0:T(8,128)(2,1)S(1)}, u32[]{:S(2)}, u32[]{:S(2)}) %collective-permute-start.9) | collective-permute-done | bytes 65568 | tf_op jit(solution)/shard_map/ppermute | solution.py:17
  34.0 1.6 %collective-permute-start.12 = (bf16[256,256]{1,0:T(8,128)(2,1)S(1)}, bf16[256,256]{1,0:T(8,128)(2,1)S(1)}, u32[]{:S(2)}, u32[]{:S(2)}) collective-permute-start(bf16[256,256]{1,0:T(8,128)(2,1)S(1)} %get-tuple-element.41), channel_id=1, source_target_pairs={{0,8},{4,12},{8,0},{12,4},{16,24},{20,28},{24,16},{28,20},{1,9},{5... | collective-permute-start | bytes 393224 | tf_op jit(solution)/shard_map/ppermute | solution.py:17
  36.8 2.1 %shard_map.65 = (bf16[256,256]{1,0:T(8,128)(2,1)S(1)}, bf16[2,2,256,256]{3,2,1,0:T(8,128)(2,1)S(1)}, bf16[2,256,256]{2,1,0:T(8,128)(2,1)S(1)}, bf16[2,256,256]{2,1,0:T(8,128)(2,1)S(1)}, bf16[2,256,256]{2,1,0:T(8,128)(2,1)S(1)}) custom-call(s32[2,8,8]{2,1,0:T(8,128)S(1)} %copy-done.6, bf16[2,256,256]{2,1,0:T(8,128)(2,1)S(1)} %collective-permute-done.6.far, ...), custom_call_target="tpu_custom_call" | custom-call | tf_op jit(solution)/shard_map/pallas_call | solution.py:78
  39.0 1.6 %collective-permute-start.14 = (bf16[2,256,256]{2,1,0:T(8,128)(2,1)S(1)}, bf16[2,256,256]{2,1,0:T(8,128)(2,1)S(1)}, u32[]{:S(2)}, u32[]{:S(2)}) collective-permute-start(bf16[2,256,256]{2,1,0:T(8,128)(2,1)S(1)} %get-tuple-element.43), channel_id=1, source_target_pairs={{0,4},{4,0},{8,12},{12,8},{16,20},{20,16},{24,28},{28,24},{1,5},{5... | collective-permute-start | bytes 786440 | tf_op jit(solution)/shard_map/ppermute | solution.py:17
  42.4 1.6 %collective-permute-start.15 = (bf16[2,256,256]{2,1,0:T(8,128)(2,1)S(1)}, bf16[2,256,256]{2,1,0:T(8,128)(2,1)S(1)}, u32[]{:S(2)}, u32[]{:S(2)}) collective-permute-start(bf16[2,256,256]{2,1,0:T(8,128)(2,1)S(1)} %get-tuple-element.44), channel_id=1, source_target_pairs={{0,8},{4,12},{8,0},{12,4},{16,24},{20,28},{24,16},{28,20},{1,9},{5... | collective-permute-start | bytes 786440 | tf_op jit(solution)/shard_map/ppermute | solution.py:17
  44.0 3.8 %collective-permute-done.13.refs_12_ = bf16[256,256]{1,0:T(8,128)(2,1)S(1)} collective-permute-done((bf16[256,256]{1,0:T(8,128)(2,1)S(1)}, bf16[256,256]{1,0:T(8,128)(2,1)S(1)}, u32[]{:S(2)}, u32[]{:S(2)}) %collective-permute-start.13) | collective-permute-done | bytes 131104 | tf_op jit(solution)/shard_map/ppermute | solution.py:17
  48.3 1.9 %collective-permute-done.14.refs_13_.refs_10_ = bf16[2,256,256]{2,1,0:T(8,128)(2,1)S(1)} collective-permute-done((bf16[2,256,256]{2,1,0:T(8,128)(2,1)S(1)}, bf16[2,256,256]{2,1,0:T(8,128)(2,1)S(1)}, u32[]{:S(2)}, u32[]{:S(2)}) %collective-permute-start.14) | collective-permute-done | bytes 262176 | tf_op jit(solution)/shard_map/ppermute | solution.py:17
  52.8 11.4 %collective-permute-done.17.far = bf16[2,256,256]{2,1,0:T(8,128)(2,1)S(1)} collective-permute-done((bf16[2,256,256]{2,1,0:T(8,128)(2,1)S(1)}, bf16[2,256,256]{2,1,0:T(8,128)(2,1)S(1)}, u32[]{:S(2)}, u32[]{:S(2)}) %collective-permute-start.17) | collective-permute-done | bytes 262176 | tf_op jit(solution)/shard_map/ppermute | solution.py:17
  64.8 2.0 %shard_map.67 = (bf16[256,256]{1,0:T(8,128)(2,1)S(1)}, bf16[1,256,256]{2,1,0:T(8,128)(2,1)S(1)}, bf16[1,256,256]{2,1,0:T(8,128)(2,1)S(1)}, bf16[1,256,256]{2,1,0:T(8,128)(2,1)S(1)}) custom-call(s32[2,8,8]{2,1,0:T(8,128)S(1)} %copy-done.6, bf16[2,256,256]{2,1,0:T(8,128)(2,1)S(1)} %collective-permute-done.17.far, ...), custom_call_target="tpu_custom_call" | custom-call | tf_op jit(solution)/shard_map/pallas_call | solution.py:78
  66.7 1.6 %collective-permute-start.18 = (bf16[1,256,256]{2,1,0:T(8,128)(2,1)S(1)}, bf16[1,256,256]{2,1,0:T(8,128)(2,1)S(1)}, u32[]{:S(2)}, u32[]{:S(2)}) collective-permute-start(bf16[1,256,256]{2,1,0:T(8,128)(2,1)S(1)} %get-tuple-element.49), channel_id=1, source_target_pairs={{0,4},{4,0},{8,12},{12,8},{16,20},{20,16},{24,28},{28,24},{1,5},{5... | collective-permute-start | bytes 393224 | tf_op jit(solution)/shard_map/ppermute | solution.py:17
  68.3 2.0 %collective-permute-start.20 = (bf16[1,256,256]{2,1,0:T(8,128)(2,1)S(1)}, bf16[1,256,256]{2,1,0:T(8,128)(2,1)S(1)}, u32[]{:S(2)}, u32[]{:S(2)}) collective-permute-start(bf16[1,256,256]{2,1,0:T(8,128)(2,1)S(1)} %get-tuple-element.51), channel_id=1, source_target_pairs={{0,12},{4,8},{8,4},{12,0},{16,28},{20,24},{24,20},{28,16},{1,13},{... | collective-permute-start | bytes 393224 | tf_op jit(solution)/shard_map/ppermute | solution.py:17
  70.3 4.4 %shard_map.66 = (bf16[3,2,256,512]{3,2,1,0:T(8,128)(2,1)}, bf16[2,256,256]{2,1,0:T(8,128)(2,1)S(1)}, bf16[256,256]{1,0:T(8,128)(2,1)S(1)}, bf16[256,256]{1,0:T(8,128)(2,1)S(1)}, bf16[256,256]{1,0:T(8,128)(2,1)S(1)}) custom-call(s32[2,8,8]{2,1,0:T(8,128)S(1)} %copy-done.6, s32[2,2,8]{2,1,0:T(2,128)S(1)} %copy-done.7, ...), custom_call_target="tpu_custom_call", output_to_operand_aliasing={{0}: (4, {})} | custom-call | tf_op jit(solution)/shard_map/pallas_call | solution.py:78
  76.2 4.3 %shard_map.68 = (bf16[3,2,256,512]{3,2,1,0:T(8,128)(2,1)}, bf16[2,256,256]{2,1,0:T(8,128)(2,1)S(1)}) custom-call(s32[2,8,8]{2,1,0:T(8,128)S(1)} %copy-done.6, s32[2,2,8]{2,1,0:T(2,128)S(1)} %copy-done.7, s32[2,2]{1,0:T(2,128)S(1)} %copy-done.8, bf16[3,2,256,512]{3,2,1,0:T(8,128)(2,1)S(1)} %copy-done.1, ...), custom_call_target="tpu_custom_call", output_to_operand_aliasing={{0}: (4, {})} | custom-call | tf_op jit(solution)/shard_map/pallas_call | solution.py:78
  80.5 1.5 %collective-permute-start.31 = (bf16[2,256,256]{2,1,0:T(8,128)(2,1)S(1)}, bf16[2,256,256]{2,1,0:T(8,128)(2,1)S(1)}, u32[]{:S(2)}, u32[]{:S(2)}) collective-permute-start(bf16[2,256,256]{2,1,0:T(8,128)(2,1)S(1)} %get-tuple-element.58.refs_0_.refs_16_), channel_id=1, source_target_pairs={{0,16},{4,20},{8,24},{12,28},{16,0},{20,4},{24,8},{28,12},{1,17},{... | collective-permute-start | bytes 786440 | tf_op jit(solution)/shard_map/ppermute | solution.py:17
  83.5 10.6 %collective-permute-done.24.far.refs_17_ = bf16[2,256,256]{2,1,0:T(8,128)(2,1)S(1)} collective-permute-done((bf16[2,256,256]{2,1,0:T(8,128)(2,1)S(1)}, bf16[2,256,256]{2,1,0:T(8,128)(2,1)S(1)}, u32[]{:S(2)}, u32[]{:S(2)}) %collective-permute-start.24) | collective-permute-done | bytes 262176 | tf_op jit(solution)/shard_map/ppermute | solution.py:17
  94.2 1.8 %shard_map.69 = (bf16[2,256,256]{2,1,0:T(8,128)(2,1)S(1)}, bf16[2,256,256]{2,1,0:T(8,128)(2,1)S(1)}, bf16[2,256,256]{2,1,0:T(8,128)(2,1)S(1)}) custom-call(s32[2,8,8]{2,1,0:T(8,128)S(1)} %copy-done.6, bf16[2,256,256]{2,1,0:T(8,128)(2,1)S(1)} %collective-permute-done.24.far.refs_17_, bf16[2,256,256]{2,1,0:T(8,128)(2,1)S(1)} %get-tuple-element.58.refs_0_.refs_16_), custom_call_target="tpu_custom_call" | custom-call | tf_op jit(solution)/shard_map/pallas_call | solution.py:78
  96.0 1.6 %collective-permute-start.28 = (bf16[2,256,256]{2,1,0:T(8,128)(2,1)S(1)}, bf16[2,256,256]{2,1,0:T(8,128)(2,1)S(1)}, u32[]{:S(2)}, u32[]{:S(2)}) collective-permute-start(bf16[2,256,256]{2,1,0:T(8,128)(2,1)S(1)} %get-tuple-element.59), channel_id=1, source_target_pairs={{0,4},{4,0},{8,12},{12,8},{16,20},{20,16},{24,28},{28,24},{1,5},{5... | collective-permute-start | bytes 786440 | tf_op jit(solution)/shard_map/ppermute | solution.py:17
  97.5 2.0 %collective-permute-start.27 = (bf16[256,256]{1,0:T(8,128)(2,1)S(1)}, bf16[256,256]{1,0:T(8,128)(2,1)S(1)}, u32[]{:S(2)}, u32[]{:S(2)}) collective-permute-start(bf16[256,256]{1,0:T(8,128)(2,1)S(1)} %get-tuple-element.57), channel_id=1, source_target_pairs={{0,12},{4,8},{8,4},{12,0},{16,28},{20,24},{24,20},{28,16},{1,13},{... | collective-permute-start | bytes 393224 | tf_op jit(solution)/shard_map/ppermute | solution.py:17
  99.7 2.8 %collective-permute-start.30 = (bf16[2,256,256]{2,1,0:T(8,128)(2,1)S(1)}, bf16[2,256,256]{2,1,0:T(8,128)(2,1)S(1)}, u32[]{:S(2)}, u32[]{:S(2)}) collective-permute-start(bf16[2,256,256]{2,1,0:T(8,128)(2,1)S(1)} %get-tuple-element.61), channel_id=1, source_target_pairs={{0,12},{4,8},{8,4},{12,0},{16,28},{20,24},{24,20},{28,16},{1,13},{... | collective-permute-start | bytes 786440 | tf_op jit(solution)/shard_map/ppermute | solution.py:17
  104.5 2.3 %collective-permute-done.27.refs_20_ = bf16[256,256]{1,0:T(8,128)(2,1)S(1)} collective-permute-done((bf16[256,256]{1,0:T(8,128)(2,1)S(1)}, bf16[256,256]{1,0:T(8,128)(2,1)S(1)}, u32[]{:S(2)}, u32[]{:S(2)}) %collective-permute-start.27) | collective-permute-done | bytes 131104 | tf_op jit(solution)/shard_map/ppermute | solution.py:17
  107.5 2.1 %collective-permute-start.34 = (bf16[1,256,256]{2,1,0:T(8,128)(2,1)S(1)}, bf16[1,256,256]{2,1,0:T(8,128)(2,1)S(1)}, u32[]{:S(2)}, u32[]{:S(2)}) collective-permute-start(bf16[1,256,256]{2,1,0:T(8,128)(2,1)S(1)} %get-tuple-element.65), channel_id=1, source_target_pairs={{0,12},{4,8},{8,4},{12,0},{16,28},{20,24},{24,20},{28,16},{1,13},{... | collective-permute-start | bytes 393224 | tf_op jit(solution)/shard_map/ppermute | solution.py:17
  109.7 2.7 %collective-permute-done.29.refs_22_.refs_19_ = bf16[2,256,256]{2,1,0:T(8,128)(2,1)S(1)} collective-permute-done((bf16[2,256,256]{2,1,0:T(8,128)(2,1)S(1)}, bf16[2,256,256]{2,1,0:T(8,128)(2,1)S(1)}, u32[]{:S(2)}, u32[]{:S(2)}) %collective-permute-start.29) | collective-permute-done | bytes 262176 | tf_op jit(solution)/shard_map/ppermute | solution.py:17
  112.4 5.6 %collective-permute-done.30.refs_23_.refs_20_ = bf16[2,256,256]{2,1,0:T(8,128)(2,1)S(1)} collective-permute-done((bf16[2,256,256]{2,1,0:T(8,128)(2,1)S(1)}, bf16[2,256,256]{2,1,0:T(8,128)(2,1)S(1)}, u32[]{:S(2)}, u32[]{:S(2)}) %collective-permute-start.30) | collective-permute-done | bytes 262176 | tf_op jit(solution)/shard_map/ppermute | solution.py:17
  118.0 6.0 %shard_map.70 = (bf16[3,2,256,512]{3,2,1,0:T(8,128)(2,1)}, bf16[2,256,256]{2,1,0:T(8,128)(2,1)}) custom-call(s32[2,8,8]{2,1,0:T(8,128)S(1)} %copy-done.6, s32[2,2,8]{2,1,0:T(2,128)S(1)} %copy-done.7, s32[2,2]{1,0:T(2,128)S(1)} %copy-done.8, bf16[3,2,256,512]{3,2,1,0:T(8,128)(2,1)S(1)} %copy-done.1, ...), custom_call_target="tpu_custom_call", output_to_operand_aliasing={{0}: (4, {})} | custom-call | tf_op jit(solution)/shard_map/pallas_call | solution.py:78
  124.0 6.0 %shard_map.72 = (bf16[3,2,256,512]{3,2,1,0:T(8,128)(2,1)}, bf16[2,256,256]{2,1,0:T(8,128)(2,1)}) custom-call(s32[2,8,8]{2,1,0:T(8,128)S(1)} %copy-done.6, s32[2,2,8]{2,1,0:T(2,128)S(1)} %copy-done.7, s32[2,2]{1,0:T(2,128)S(1)} %copy-done.8, bf16[3,2,256,512]{3,2,1,0:T(8,128)(2,1)S(1)} %copy-done.1, ...), custom_call_target="tpu_custom_call", output_to_operand_aliasing={{0}: (4, {})} | custom-call | tf_op jit(solution)/shard_map/pallas_call | solution.py:78
  (67 shorter events, 19.9 us)
Async XLA Ops:
  0.0 8.0 %collective-permute-start.1 = (bf16[3,2,64,256]{3,2,1,0:T(8,128)(2,1)}, bf16[3,2,64,256]{3,2,1,0:T(8,128)(2,1)S(1)}, u32[]{:S(2)}, u32[]{:S(2)}) collective-permute-start(bf16[3,2,64,256]{3,2,1,0:T(8,128)(2,1)} %refs_0_.9), channel_id=1, source_target_pairs={{0,2},{1,3},{2,0},{3,1},{4,6},{5,7},{6,4},{7,5},{8,10},{9,11},{10,... | collective-permute-start | bytes 589832 | tf_op jit(solution)/shard_map/ppermute | solution.py:17
  2.9 9.0 %collective-permute-start = (bf16[3,2,64,256]{3,2,1,0:T(8,128)(2,1)}, bf16[3,2,64,256]{3,2,1,0:T(8,128)(2,1)S(1)}, u32[]{:S(2)}, u32[]{:S(2)}) collective-permute-start(bf16[3,2,64,256]{3,2,1,0:T(8,128)(2,1)} %refs_0_.9), channel_id=1, source_target_pairs={{0,1},{1,0},{2,3},{3,2},{4,5},{5,4},{6,7},{7,6},{8,9},{9,8},{10,11... | collective-permute-start | bytes 589832 | tf_op jit(solution)/shard_map/ppermute | solution.py:17
  9.0 27.8 %collective-permute-start.6 = (bf16[2,256,256]{2,1,0:T(8,128)(2,1)S(1)}, bf16[2,256,256]{2,1,0:T(8,128)(2,1)S(1)}, u32[]{:S(2)}, u32[]{:S(2)}) collective-permute-start(bf16[2,256,256]{2,1,0:T(8,128)(2,1)S(1)} %slice_bitcast_fusion), channel_id=1, source_target_pairs={{0,16},{4,20},{8,24},{12,28},{16,0},{20,4},{24,8},{28,12},{1,17},{... | collective-permute-start | bytes 786440 | tf_op jit(solution)/shard_map/ppermute | solution.py:17
  18.4 29.4 %collective-permute-start.4 = (bf16[2,2,256,256]{3,2,1,0:T(8,128)(2,1)S(1)}, bf16[2,2,256,256]{3,2,1,0:T(8,128)(2,1)S(1)}, u32[]{:S(2)}, u32[]{:S(2)}) collective-permute-start(bf16[2,2,256,256]{3,2,1,0:T(8,128)(2,1)S(1)} %get-tuple-element.37.refs_4_), channel_id=1, source_target_pairs={{0,2},{1,3},{2,0},{3,1},{4,6},{5,7},{6,4},{7,5},{8,10},{9,11},{10,... | collective-permute-start | bytes 1572872 | tf_op jit(solution)/shard_map/ppermute | solution.py:17
  20.0 7.3 %collective-permute-start.7 = (bf16[2,64,256]{2,1,0:T(8,128)(2,1)S(1)}, bf16[2,64,256]{2,1,0:T(8,128)(2,1)S(1)}, u32[]{:S(2)}, u32[]{:S(2)}) collective-permute-start(bf16[2,64,256]{2,1,0:T(8,128)(2,1)S(1)} %slice_bitcast_fusion.1), channel_id=1, source_target_pairs={{0,16},{4,20},{8,24},{12,28},{16,0},{20,4},{24,8},{28,12},{1,17},{... | collective-permute-start | bytes 196616 | tf_op jit(solution)/shard_map/ppermute | solution.py:17
  27.3 6.6 %collective-permute-start.9 = (bf16[2,64,256]{2,1,0:T(8,128)(2,1)S(1)}, bf16[2,64,256]{2,1,0:T(8,128)(2,1)S(1)}, u32[]{:S(2)}, u32[]{:S(2)}) collective-permute-start(bf16[2,64,256]{2,1,0:T(8,128)(2,1)S(1)} %collective-permute-done.7.refs_0_), channel_id=1, source_target_pairs={{0,2},{1,3},{2,0},{3,1},{4,6},{5,7},{6,4},{7,5},{8,10},{9,11},{10,... | collective-permute-start | bytes 196616 | tf_op jit(solution)/shard_map/ppermute | solution.py:17
  28.9 6.7 %collective-permute-start.8 = (bf16[2,64,256]{2,1,0:T(8,128)(2,1)S(1)}, bf16[2,64,256]{2,1,0:T(8,128)(2,1)S(1)}, u32[]{:S(2)}, u32[]{:S(2)}) collective-permute-start(bf16[2,64,256]{2,1,0:T(8,128)(2,1)S(1)} %collective-permute-done.7.refs_0_), channel_id=1, source_target_pairs={{0,1},{1,0},{2,3},{3,2},{4,5},{5,4},{6,7},{7,6},{8,9},{9,8},{10,11... | collective-permute-start | bytes 196616 | tf_op jit(solution)/shard_map/ppermute | solution.py:17
  28.9 12.1 %collective-permute-start.11 = (bf16[256,256]{1,0:T(8,128)(2,1)S(1)}, bf16[256,256]{1,0:T(8,128)(2,1)S(1)}, u32[]{:S(2)}, u32[]{:S(2)}) collective-permute-start(bf16[256,256]{1,0:T(8,128)(2,1)S(1)} %get-tuple-element.40), channel_id=1, source_target_pairs={{0,4},{4,0},{8,12},{12,8},{16,20},{20,16},{24,28},{28,24},{1,5},{5... | collective-permute-start | bytes 393224 | tf_op jit(solution)/shard_map/ppermute | solution.py:17
  34.0 8.5 %collective-permute-start.12 = (bf16[256,256]{1,0:T(8,128)(2,1)S(1)}, bf16[256,256]{1,0:T(8,128)(2,1)S(1)}, u32[]{:S(2)}, u32[]{:S(2)}) collective-permute-start(bf16[256,256]{1,0:T(8,128)(2,1)S(1)} %get-tuple-element.41), channel_id=1, source_target_pairs={{0,8},{4,12},{8,0},{12,4},{16,24},{20,28},{24,16},{28,20},{1,9},{5... | collective-permute-start | bytes 393224 | tf_op jit(solution)/shard_map/ppermute | solution.py:17
  39.0 11.2 %collective-permute-start.14 = (bf16[2,256,256]{2,1,0:T(8,128)(2,1)S(1)}, bf16[2,256,256]{2,1,0:T(8,128)(2,1)S(1)}, u32[]{:S(2)}, u32[]{:S(2)}) collective-permute-start(bf16[2,256,256]{2,1,0:T(8,128)(2,1)S(1)} %get-tuple-element.43), channel_id=1, source_target_pairs={{0,4},{4,0},{8,12},{12,8},{16,20},{20,16},{24,28},{28,24},{1,5},{5... | collective-permute-start | bytes 786440 | tf_op jit(solution)/shard_map/ppermute | solution.py:17
  40.5 7.3 %collective-permute-start.13 = (bf16[256,256]{1,0:T(8,128)(2,1)S(1)}, bf16[256,256]{1,0:T(8,128)(2,1)S(1)}, u32[]{:S(2)}, u32[]{:S(2)}) collective-permute-start(bf16[256,256]{1,0:T(8,128)(2,1)S(1)} %get-tuple-element.42), channel_id=1, source_target_pairs={{0,12},{4,8},{8,4},{12,0},{16,28},{20,24},{24,20},{28,16},{1,13},{... | collective-permute-start | bytes 393224 | tf_op jit(solution)/shard_map/ppermute | solution.py:17
  40.9 23.3 %collective-permute-start.22 = (bf16[2,2,256,256]{3,2,1,0:T(8,128)(2,1)S(1)}, bf16[2,2,256,256]{3,2,1,0:T(8,128)(2,1)S(1)}, u32[]{:S(2)}, u32[]{:S(2)}) collective-permute-start(bf16[2,2,256,256]{3,2,1,0:T(8,128)(2,1)S(1)} %get-tuple-element.53.refs_4_), channel_id=1, source_target_pairs={{0,2},{1,3},{2,0},{3,1},{4,6},{5,7},{6,4},{7,5},{8,10},{9,11},{10,... | collective-permute-start | bytes 1572872 | tf_op jit(solution)/shard_map/ppermute | solution.py:17
  42.4 9.0 %collective-permute-start.15 = (bf16[2,256,256]{2,1,0:T(8,128)(2,1)S(1)}, bf16[2,256,256]{2,1,0:T(8,128)(2,1)S(1)}, u32[]{:S(2)}, u32[]{:S(2)}) collective-permute-start(bf16[2,256,256]{2,1,0:T(8,128)(2,1)S(1)} %get-tuple-element.44), channel_id=1, source_target_pairs={{0,8},{4,12},{8,0},{12,4},{16,24},{20,28},{24,16},{28,20},{1,9},{5... | collective-permute-start | bytes 786440 | tf_op jit(solution)/shard_map/ppermute | solution.py:17
  47.8 20.5 %collective-permute-start.3 = (bf16[2,2,256,256]{3,2,1,0:T(8,128)(2,1)S(1)}, bf16[2,2,256,256]{3,2,1,0:T(8,128)(2,1)S(1)}, u32[]{:S(2)}, u32[]{:S(2)}) collective-permute-start(bf16[2,2,256,256]{3,2,1,0:T(8,128)(2,1)S(1)} %get-tuple-element.37.refs_4_), channel_id=1, source_target_pairs={{0,1},{1,0},{2,3},{3,2},{4,5},{5,4},{6,7},{7,6},{8,9},{9,8},{10,11... | collective-permute-start | bytes 1572872 | tf_op jit(solution)/shard_map/ppermute | solution.py:17
  47.8 20.5 %collective-permute-start.5 = (bf16[2,2,256,256]{3,2,1,0:T(8,128)(2,1)S(1)}, bf16[2,2,256,256]{3,2,1,0:T(8,128)(2,1)S(1)}, u32[]{:S(2)}, u32[]{:S(2)}) collective-permute-start(bf16[2,2,256,256]{3,2,1,0:T(8,128)(2,1)S(1)} %collective-permute-done.4.refs_6_), channel_id=1, source_target_pairs={{0,1},{1,0},{2,3},{3,2},{4,5},{5,4},{6,7},{7,6},{8,9},{9,8},{10,11... | collective-permute-start | bytes 1572872 | tf_op jit(solution)/shard_map/ppermute | solution.py:17
  50.2 14.0 %collective-permute-start.17 = (bf16[2,256,256]{2,1,0:T(8,128)(2,1)S(1)}, bf16[2,256,256]{2,1,0:T(8,128)(2,1)S(1)}, u32[]{:S(2)}, u32[]{:S(2)}) collective-permute-start(bf16[2,256,256]{2,1,0:T(8,128)(2,1)S(1)} %get-tuple-element.47), channel_id=1, source_target_pairs={{0,16},{4,20},{8,24},{12,28},{16,0},{20,4},{24,8},{28,12},{1,17},{... | collective-permute-start | bytes 786440 | tf_op jit(solution)/shard_map/ppermute | solution.py:17
  51.4 15.3 %collective-permute-start.16 = (bf16[2,256,256]{2,1,0:T(8,128)(2,1)S(1)}, bf16[2,256,256]{2,1,0:T(8,128)(2,1)S(1)}, u32[]{:S(2)}, u32[]{:S(2)}) collective-permute-start(bf16[2,256,256]{2,1,0:T(8,128)(2,1)S(1)} %get-tuple-element.45), channel_id=1, source_target_pairs={{0,12},{4,8},{8,4},{12,0},{16,28},{20,24},{24,20},{28,16},{1,13},{... | collective-permute-start | bytes 786440 | tf_op jit(solution)/shard_map/ppermute | solution.py:17
  64.2 33.3 %collective-permute-start.21 = (bf16[2,2,256,256]{3,2,1,0:T(8,128)(2,1)S(1)}, bf16[2,2,256,256]{3,2,1,0:T(8,128)(2,1)S(1)}, u32[]{:S(2)}, u32[]{:S(2)}) collective-permute-start(bf16[2,2,256,256]{3,2,1,0:T(8,128)(2,1)S(1)} %get-tuple-element.53.refs_4_), channel_id=1, source_target_pairs={{0,1},{1,0},{2,3},{3,2},{4,5},{5,4},{6,7},{7,6},{8,9},{9,8},{10,11... | collective-permute-start | bytes 1572872 | tf_op jit(solution)/shard_map/ppermute | solution.py:17
  64.2 33.3 %collective-permute-start.23 = (bf16[2,2,256,256]{3,2,1,0:T(8,128)(2,1)S(1)}, bf16[2,2,256,256]{3,2,1,0:T(8,128)(2,1)S(1)}, u32[]{:S(2)}, u32[]{:S(2)}) collective-permute-start(bf16[2,2,256,256]{3,2,1,0:T(8,128)(2,1)S(1)} %collective-permute-done.22.refs_6_), channel_id=1, source_target_pairs={{0,1},{1,0},{2,3},{3,2},{4,5},{5,4},{6,7},{7,6},{8,9},{9,8},{10,11... | collective-permute-start | bytes 1572872 | tf_op jit(solution)/shard_map/ppermute | solution.py:17
  66.7 7.9 %collective-permute-start.18 = (bf16[1,256,256]{2,1,0:T(8,128)(2,1)S(1)}, bf16[1,256,256]{2,1,0:T(8,128)(2,1)S(1)}, u32[]{:S(2)}, u32[]{:S(2)}) collective-permute-start(bf16[1,256,256]{2,1,0:T(8,128)(2,1)S(1)} %get-tuple-element.49), channel_id=1, source_target_pairs={{0,4},{4,0},{8,12},{12,8},{16,20},{20,16},{24,28},{28,24},{1,5},{5... | collective-permute-start | bytes 393224 | tf_op jit(solution)/shard_map/ppermute | solution.py:17
  68.3 6.4 %collective-permute-start.19 = (bf16[1,256,256]{2,1,0:T(8,128)(2,1)S(1)}, bf16[1,256,256]{2,1,0:T(8,128)(2,1)S(1)}, u32[]{:S(2)}, u32[]{:S(2)}) collective-permute-start(bf16[1,256,256]{2,1,0:T(8,128)(2,1)S(1)} %get-tuple-element.50), channel_id=1, source_target_pairs={{0,8},{4,12},{8,0},{12,4},{16,24},{20,28},{24,16},{28,20},{1,9},{5... | collective-permute-start | bytes 393224 | tf_op jit(solution)/shard_map/ppermute | solution.py:17
  68.3 7.9 %collective-permute-start.20 = (bf16[1,256,256]{2,1,0:T(8,128)(2,1)S(1)}, bf16[1,256,256]{2,1,0:T(8,128)(2,1)S(1)}, u32[]{:S(2)}, u32[]{:S(2)}) collective-permute-start(bf16[1,256,256]{2,1,0:T(8,128)(2,1)S(1)} %get-tuple-element.51), channel_id=1, source_target_pairs={{0,12},{4,8},{8,4},{12,0},{16,28},{20,24},{24,20},{28,16},{1,13},{... | collective-permute-start | bytes 393224 | tf_op jit(solution)/shard_map/ppermute | solution.py:17
  74.7 19.5 %collective-permute-start.24 = (bf16[2,256,256]{2,1,0:T(8,128)(2,1)S(1)}, bf16[2,256,256]{2,1,0:T(8,128)(2,1)S(1)}, u32[]{:S(2)}, u32[]{:S(2)}) collective-permute-start(bf16[2,256,256]{2,1,0:T(8,128)(2,1)S(1)} %get-tuple-element.54.refs_16_), channel_id=1, source_target_pairs={{0,16},{4,20},{8,24},{12,28},{16,0},{20,4},{24,8},{28,12},{1,17},{... | collective-permute-start | bytes 786440 | tf_op jit(solution)/shard_map/ppermute | solution.py:17
  80.5 19.2 %collective-permute-start.31 = (bf16[2,256,256]{2,1,0:T(8,128)(2,1)S(1)}, bf16[2,256,256]{2,1,0:T(8,128)(2,1)S(1)}, u32[]{:S(2)}, u32[]{:S(2)}) collective-permute-start(bf16[2,256,256]{2,1,0:T(8,128)(2,1)S(1)} %get-tuple-element.58.refs_0_.refs_16_), channel_id=1, source_target_pairs={{0,16},{4,20},{8,24},{12,28},{16,0},{20,4},{24,8},{28,12},{1,17},{... | collective-permute-start | bytes 786440 | tf_op jit(solution)/shard_map/ppermute | solution.py:17
  82.0 17.5 %collective-permute-start.25 = (bf16[256,256]{1,0:T(8,128)(2,1)S(1)}, bf16[256,256]{1,0:T(8,128)(2,1)S(1)}, u32[]{:S(2)}, u32[]{:S(2)}) collective-permute-start(bf16[256,256]{1,0:T(8,128)(2,1)S(1)} %get-tuple-element.55), channel_id=1, source_target_pairs={{0,4},{4,0},{8,12},{12,8},{16,20},{20,16},{24,28},{28,24},{1,5},{5... | collective-permute-start | bytes 393224 | tf_op jit(solution)/shard_map/ppermute | solution.py:17
  96.0 11.6 %collective-permute-start.28 = (bf16[2,256,256]{2,1,0:T(8,128)(2,1)S(1)}, bf16[2,256,256]{2,1,0:T(8,128)(2,1)S(1)}, u32[]{:S(2)}, u32[]{:S(2)}) collective-permute-start(bf16[2,256,256]{2,1,0:T(8,128)(2,1)S(1)} %get-tuple-element.59), channel_id=1, source_target_pairs={{0,4},{4,0},{8,12},{12,8},{16,20},{20,16},{24,28},{28,24},{1,5},{5... | collective-permute-start | bytes 786440 | tf_op jit(solution)/shard_map/ppermute | solution.py:17
  97.5 9.2 %collective-permute-start.27 = (bf16[256,256]{1,0:T(8,128)(2,1)S(1)}, bf16[256,256]{1,0:T(8,128)(2,1)S(1)}, u32[]{:S(2)}, u32[]{:S(2)}) collective-permute-start(bf16[256,256]{1,0:T(8,128)(2,1)S(1)} %get-tuple-element.57), channel_id=1, source_target_pairs={{0,12},{4,8},{8,4},{12,0},{16,28},{20,24},{24,20},{28,16},{1,13},{... | collective-permute-start | bytes 393224 | tf_op jit(solution)/shard_map/ppermute | solution.py:17
  99.5 12.8 %collective-permute-start.29 = (bf16[2,256,256]{2,1,0:T(8,128)(2,1)S(1)}, bf16[2,256,256]{2,1,0:T(8,128)(2,1)S(1)}, u32[]{:S(2)}, u32[]{:S(2)}) collective-permute-start(bf16[2,256,256]{2,1,0:T(8,128)(2,1)S(1)} %get-tuple-element.60), channel_id=1, source_target_pairs={{0,8},{4,12},{8,0},{12,4},{16,24},{20,28},{24,16},{28,20},{1,9},{5... | collective-permute-start | bytes 786440 | tf_op jit(solution)/shard_map/ppermute | solution.py:17
  99.7 18.3 %collective-permute-start.30 = (bf16[2,256,256]{2,1,0:T(8,128)(2,1)S(1)}, bf16[2,256,256]{2,1,0:T(8,128)(2,1)S(1)}, u32[]{:S(2)}, u32[]{:S(2)}) collective-permute-start(bf16[2,256,256]{2,1,0:T(8,128)(2,1)S(1)} %get-tuple-element.61), channel_id=1, source_target_pairs={{0,12},{4,8},{8,4},{12,0},{16,28},{20,24},{24,20},{28,16},{1,13},{... | collective-permute-start | bytes 786440 | tf_op jit(solution)/shard_map/ppermute | solution.py:17
  104.0 20.0 %collective-permute-start.32 = (bf16[1,256,256]{2,1,0:T(8,128)(2,1)S(1)}, bf16[1,256,256]{2,1,0:T(8,128)(2,1)S(1)}, u32[]{:S(2)}, u32[]{:S(2)}) collective-permute-start(bf16[1,256,256]{2,1,0:T(8,128)(2,1)S(1)} %get-tuple-element.63), channel_id=1, source_target_pairs={{0,4},{4,0},{8,12},{12,8},{16,20},{20,16},{24,28},{28,24},{1,5},{5... | collective-permute-start | bytes 393224 | tf_op jit(solution)/shard_map/ppermute | solution.py:17
  106.8 17.2 %collective-permute-start.33 = (bf16[1,256,256]{2,1,0:T(8,128)(2,1)S(1)}, bf16[1,256,256]{2,1,0:T(8,128)(2,1)S(1)}, u32[]{:S(2)}, u32[]{:S(2)}) collective-permute-start(bf16[1,256,256]{2,1,0:T(8,128)(2,1)S(1)} %get-tuple-element.64), channel_id=1, source_target_pairs={{0,8},{4,12},{8,0},{12,4},{16,24},{20,28},{24,16},{28,20},{1,9},{5... | collective-permute-start | bytes 393224 | tf_op jit(solution)/shard_map/ppermute | solution.py:17
  107.5 16.4 %collective-permute-start.34 = (bf16[1,256,256]{2,1,0:T(8,128)(2,1)S(1)}, bf16[1,256,256]{2,1,0:T(8,128)(2,1)S(1)}, u32[]{:S(2)}, u32[]{:S(2)}) collective-permute-start(bf16[1,256,256]{2,1,0:T(8,128)(2,1)S(1)} %get-tuple-element.65), channel_id=1, source_target_pairs={{0,12},{4,8},{8,4},{12,0},{16,28},{20,24},{24,20},{28,16},{1,13},{... | collective-permute-start | bytes 393224 | tf_op jit(solution)/shard_map/ppermute | solution.py:17
  (12 other events, 162.0 us)

commit v5 on v0

v5 whole, which is shorter than its diff:
```python
import functools

import jax
import jax.numpy as jnp
from jax import lax
from jax.experimental import pallas as pl
from jax.experimental.pallas import tpu as pltpu
from jax.sharding import PartitionSpec as P

CHUNKS = 2
VMEM = pl.BlockSpec(memory_space=pltpu.VMEM)
SMEM = pl.BlockSpec(memory_space=pltpu.SMEM)
ANY = pl.BlockSpec(memory_space=pl.ANY)
BF16, F32 = jnp.bfloat16, jnp.float32


def hop(value, axis, size, step):
    return lax.ppermute(value, axis, [(at, at ^ step) for at in range(size)])


def gather_parts(value, axis, size):
    parts = {0: value}
    step = size // 2
    while step:
        for have in sorted(parts):
            parts[have ^ step] = hop(parts[have], axis, size, step)
        step //= 2
    return [parts[at] for at in range(size)]


def transposed_dot(left, right):
    return lax.dot_general(left, right, (((0,), (0,)), ((), ())), preferred_element_type=F32)


def take(refs, count):
    return list(refs[:count]), list(refs[count:])


def call(kernel, outs, scratch, small, arrays, out_spec=VMEM, flops=0):
    size = sum(value.size * value.dtype.itemsize for value in (*arrays, *outs))
    return pl.pallas_call(
        kernel,
        out_shape=outs,
        in_specs=[SMEM] * len(small) + [VMEM] * len(arrays),
        out_specs=[out_spec] * len(outs),
        scratch_shapes=scratch,
        cost_estimate=pl.CostEstimate(flops=flops, bytes_accessed=size, transcendentals=0),
        compiler_params=pltpu.CompilerParams(vmem_limit_bytes=16 * 1024 * 1024),
    )(*small, *arrays)


def first_kernel(sides, picks, noise, inverse, *refs):
    *refs, inv = refs
    solved, sends = refs[:-sides], refs[-sides:]
    myself = lax.axis_index("leaf")
    draws, nodes, rows = inverse.shape[:3]
    wide = solved[0].shape[-1]
    for part in range(draws):
        inv[:, part * rows:(part + 1) * rows, :] = inverse[part]
    for at, target in enumerate(solved):
        for node in range(nodes):
            right = noise[node, :, at * wide:(at + 1) * wide]
            target[node] = transposed_dot(inv[node], right).astype(BF16)
    for step, send in enumerate(sends, 1):
        send[0] = solved[0][picks[0, myself ^ step, myself]]


def relay_kernel(half, source, last, picks, far, *refs):
    own, sends = (None, refs) if last else (refs[0], refs[1:])
    myself = lax.axis_index("leaf")
    for step, send in enumerate(sends, 1):
        send[0] = far[picks[source, myself ^ step, myself ^ half]]
        if not last:
            send[1] = own[picks[source, myself ^ step, myself]]


def level_kernel(
    level, owners, draws, chunk, waits, sides, earlier, width, picks, lists, counts, noise, *refs
):
    half = owners // 2
    _, refs = take(refs, waits)
    packs, refs = take(refs, draws)
    pieces = []
    for _ in range(level):
        piece, refs = take(refs, owners)
        pieces.append(piece)
    done, refs = take(refs, earlier)
    target, refs = refs[0], refs[1:]
    sends, (table, inv, *refs) = take(refs, sides)
    myself, draw = lax.axis_index("leaf"), lax.axis_index("draw")
    nodes, wide = noise.shape[1], table.shape[-1]
    depth = inv.shape[1]
    rows = depth // draws
    copies = []
    solved = target
    if earlier:
        solved, sems = refs
        per_level = (earlier + 1) // (level + 1)
        for at, ref in enumerate(done):
            here = target.at[at // per_level, :, :, pl.ds(at % per_level * wide, wide)]
            copies.append(pltpu.make_async_copy(ref, here, sems.at[at]))
            copies[-1].start()
    for source, (own, far, *others) in enumerate(pieces):
        first = source * owners
        table[first] = own[picks[source, myself, myself]]
        table[first + half] = far[picks[source, myself, myself ^ half]]
        for step in range(1, half):
            near, distant = others[step - 1], others[half + step - 2]
            table[first + step] = near[near.shape[0] - 1]
            table[first + (half ^ step)] = distant[0]
    empty = level * owners
    table[empty] = jnp.zeros_like(table[empty])
    for step, pack in enumerate(packs):
        start = pl.multiple_of((draw ^ step) * rows, rows)
        for node in range(nodes):
            at = nodes * width * depth + node * rows
            inv[node, pl.ds(start, rows), :] = pack[at:at + rows, :]
    for node in range(nodes):
        total = None
        for step, pack in enumerate(packs):
            for offset in range(width):
                slot = (draw ^ step) * width + offset
                live = slot < counts[level - 1, node]
                entry = jnp.where(live, lists[level - 1, node, slot] ^ myself, empty)
                at = (node * width + offset) * depth
                term = transposed_dot(pack[at:at + depth, :], table[entry])
                total = term if total is None else total + term
        side = noise[level, node, :, chunk * wide:(chunk + 1) * wide].astype(F32) - total
        solved[node] = transposed_dot(inv[node], side.astype(BF16)).astype(BF16)
    for step, send in enumerate(sends, 1):
        send[0] = solved[picks[level, myself ^ step, myself]]
    if earlier:
        here = target.at[level, :, :, pl.ds(chunk * wide, wide)]
        copies.append(pltpu.make_async_copy(solved, here, sems.at[earlier]))
        copies[-1].start()
    for copy in copies:
        copy.wait()


def on_device(owners, draws, noise, inverse, coupling, picks, lists, counts):
    levels, nodes, rows, columns = noise.shape
    wide, half, chunks = columns // CHUNKS, owners // 2, range(CHUNKS)
    width, last_level = coupling.shape[2], levels - 1
    shape = lambda *dims: jax.ShapeDtypeStruct(dims, BF16)
    part = shape(nodes, rows, wide)
    leaf = lambda value, step: hop(value, "leaf", owners, step)
    near = lambda values: [leaf(value, step) for step, value in enumerate(values, 1)]
    inv_here = pltpu.VMEM((nodes, rows, rows), BF16)
    dot_flops = 2 * rows * rows * wide

    inverse_first = lax.all_gather(inverse[0], "draw", axis=0)
    packs = [
        gather_parts(
            jnp.concatenate([coupling[level - 1].reshape(-1, rows), inverse[level].reshape(-1, rows)]),
            "draw", draws,
        )
        for level in range(1, levels)
    ]
    solved = call(
        functools.partial(first_kernel, half - 1),
        [part] * CHUNKS + [shape(1, rows, wide)] * (half - 1),
        [inv_here],
        (picks,),
        (noise[0], inverse_first),
        flops=nodes * CHUNKS * dot_flops,
    )
    solved, sends = solved[:CHUNKS], solved[CHUNKS:]
    done, pieces = [solved], []
    for level in range(1, levels):
        far = [leaf(value, half) for value in solved]
        got = [near(sends)]
        for at in chunks:
            last = at == CHUNKS - 1
            sends = call(
                functools.partial(relay_kernel, half, level - 1, last),
                [shape(1 if last else 2, rows, wide)] * (half - 1),
                [],
                (picks,),
                (far[at],) if last else (far[at], solved[at + 1]),
            )
            got.append(near(sends))
        pieces.append([(solved[at], far[at], *got[at], *got[at + 1]) for at in chunks])
        token = sends[:1]
        solved, sends = [], []
        for at in chunks:
            sides = half - 1 if at == 0 and level < last_level else 0
            final = level == last_level and at == CHUNKS - 1
            earlier = [value for values in done for value in values] + solved if final else []
            waits = token if at == 0 else []
            scratch = [pltpu.VMEM((level * owners + 1, rows, wide), BF16), inv_here]
            if final:
                scratch += [
                    pltpu.VMEM((nodes, rows, wide), BF16),
                    pltpu.SemaphoreType.DMA((len(earlier) + 1,)),
                ]
            here, *sent = call(
                functools.partial(
                    level_kernel, level, owners, draws, at, len(waits), sides, len(earlier), width
                ),
                [shape(levels, nodes, rows, columns) if final else part]
                + [shape(1, rows, wide)] * sides,
                scratch,
                (picks, lists, counts),
                (
                    noise, *waits, *packs[level - 1],
                    *(ref for source in range(level) for ref in pieces[source][at]),
                    *earlier,
                ),
                out_spec=ANY if final else VMEM,
                flops=nodes * (draws * width + 1) * dot_flops,
            )
            solved.append(here)
            sends += sent
        done.append(solved)
    return here


def solution(mesh):
    placed = (
        P(None, "leaf", None, "draw"),
        P(None, "leaf", "draw", None),
        P(None, "leaf", "draw", None, None),
        P(),
        P(None, "leaf", None),
        P(None, "leaf"),
    )
    return jax.shard_map(
        functools.partial(on_device, mesh.shape["leaf"], mesh.shape["draw"]),
        mesh=mesh,
        in_specs=placed,
        out_specs=P(None, "leaf", None, "draw"),
        check_vma=False,
    )
```

time: 209 us -> 123 us (0.59)
  the two profiles are of different devices: /device:TPU:9 before, /device:TPU:0 now
where the time goes in v5:
time: 123 us; the launch traced here: 122 us
  waiting for transfers between devices  52.1 us (42%)
  starting transfers between devices  37.4 us (30%)
  blocking collectives  15.5 us (13%)
  Pallas kernels  14.4 us (12%)
  local copies, waits for them, and re-layouts  2.36 us (2%)
    ppermute x28, waiting for transfers between devices, hop(): return lax.ppermute(value, axis, [(at, at ^ step) for at in range(size)])  52.1 us
    ppermute x28, starting transfers between devices, hop(): return lax.ppermute(value, axis, [(at, at ^ step) for at in range(size)])  37.4 us
    all_gather x1, blocking collectives, on_device(): inverse_first = lax.all_gather(inverse[0], 'draw', axis=0)  15.5 us
    pallas_call x9, Pallas kernels, call(): pl.pallas_call(kernel, out_shape=outs, in_specs=[SMEM] * len(small) + [VM...  14.4 us
  transfers between devices with their start and end apart: 28, of which 11 were waited for; matrix products, arithmetic and copies ran while one was open for 0% of the time, Pallas kernels for 9%

profile of v5, /device:TPU:0, one launch (start us, length us, event | category | flops | bytes accessed | tf_op | source)
XLA Modules:
  0.0 122.0 jit_solution(3205912076479646105)
XLA Ops:
  0.0 0.9 fusion.1
  0.9 1.4 %fusion = (bf16[1,2,2,256,256]{4,3,2,1,0:T(8,128)(2,1)S(1)}, bf16[1,2,2,256,256]{4,3,2,1,0:T(8,128)(2,1)S(1)}) fusion(bf16[2,2,2,256,256]{4,3,2,1,0:T(8,128)(2,1)} %param.8), kind=kLoop, calls=%fused_computation.3 | loop fusion | bytes 2097152 | tf_op jit(solution)/shard_map/slice | solution.py:154
  2.4 3.0 %collective-permute-start.12 = (bf16[1152,256]{1,0:T(8,128)(2,1)S(1)}, bf16[1152,256]{1,0:T(8,128)(2,1)S(1)}, u32[]{:S(2)}, u32[]{:S(2)}) collective-permute-start(bf16[1152,256]{1,0:T(8,128)(2,1)S(1)} %pad_maximum_fusion.1.refs_0_.refs_1_), channel_id=1, source_target_pairs={{0,2},{1,3},{2,0},{3,1},{4,6},{5,7},{6,4},{7,5},{8,10},{9,11},{10,... | collective-permute-start | bytes 1769480 | tf_op jit(solution)/shard_map/ppermute | solution.py:18
  5.4 15.5 %all_gather.3.inverse = bf16[4,2,64,256]{3,2,1,0:T(8,128)(2,1)S(1)} all-gather(bf16[1,2,64,256]{3,2,1,0:T(8,128)(2,1)S(1)} %get-tuple-element.51), channel_id=1, replica_groups=mesh['leaf'=8,'draw'=4] {'draw'}, dimensions={0}, use_global_device_ids=true | all-gather | bytes 327680 | tf_op jit(solution)/shard_map/all_gather | solution.py:151
  21.0 1.0 shard_map.64
  22.0 2.9 %collective-permute-start.4 = (bf16[2,256,256]{2,1,0:T(8,128)(2,1)S(1)}, bf16[2,256,256]{2,1,0:T(8,128)(2,1)S(1)}, u32[]{:S(2)}, u32[]{:S(2)}) collective-permute-start(bf16[2,256,256]{2,1,0:T(8,128)(2,1)S(1)} %get-tuple-element.27.refs_5_.refs_20_), channel_id=1, source_target_pairs={{0,16},{4,20},{8,24},{12,28},{16,0},{20,4},{24,8},{28,12},{1,17},{... | collective-permute-start | bytes 786440 | tf_op jit(solution)/shard_map/ppermute | solution.py:18
  24.9 1.5 %collective-permute-start.15 = (bf16[1,256,256]{2,1,0:T(8,128)(2,1)S(1)}, bf16[1,256,256]{2,1,0:T(8,128)(2,1)S(1)}, u32[]{:S(2)}, u32[]{:S(2)}) collective-permute-start(bf16[1,256,256]{2,1,0:T(8,128)(2,1)S(1)} %get-tuple-element.34), channel_id=1, source_target_pairs={{0,4},{4,0},{8,12},{12,8},{16,20},{20,16},{24,28},{28,24},{1,5},{5... | collective-permute-start | bytes 393224 | tf_op jit(solution)/shard_map/ppermute | solution.py:18
  26.5 1.6 %collective-permute-start.1 = (bf16[1152,256]{1,0:T(8,128)(2,1)S(1)}, bf16[1152,256]{1,0:T(8,128)(2,1)S(1)}, u32[]{:S(2)}, u32[]{:S(2)}) collective-permute-start(bf16[1152,256]{1,0:T(8,128)(2,1)S(1)} %pad_maximum_fusion.refs_1_.refs_0_), channel_id=1, source_target_pairs={{0,2},{1,3},{2,0},{3,1},{4,6},{5,7},{6,4},{7,5},{8,10},{9,11},{10,... | collective-permute-start | bytes 1769480 | tf_op jit(solution)/shard_map/ppermute | solution.py:18
  28.0 1.6 %collective-permute-start.16 = (bf16[1,256,256]{2,1,0:T(8,128)(2,1)S(1)}, bf16[1,256,256]{2,1,0:T(8,128)(2,1)S(1)}, u32[]{:S(2)}, u32[]{:S(2)}) collective-permute-start(bf16[1,256,256]{2,1,0:T(8,128)(2,1)S(1)} %get-tuple-element.35), channel_id=1, source_target_pairs={{0,8},{4,12},{8,0},{12,4},{16,24},{20,28},{24,16},{28,20},{1,9},{5... | collective-permute-start | bytes 393224 | tf_op jit(solution)/shard_map/ppermute | solution.py:18
  30.4 2.5 %collective-permute-start.17 = (bf16[1,256,256]{2,1,0:T(8,128)(2,1)S(1)}, bf16[1,256,256]{2,1,0:T(8,128)(2,1)S(1)}, u32[]{:S(2)}, u32[]{:S(2)}) collective-permute-start(bf16[1,256,256]{2,1,0:T(8,128)(2,1)S(1)} %get-tuple-element.36), channel_id=1, source_target_pairs={{0,12},{4,8},{8,4},{12,0},{16,28},{20,24},{24,20},{28,16},{1,13},{... | collective-permute-start | bytes 393224 | tf_op jit(solution)/shard_map/ppermute | solution.py:18
  32.9 4.5 %collective-permute-done.4.far.refs_6_ = bf16[2,256,256]{2,1,0:T(8,128)(2,1)S(1)} collective-permute-done((bf16[2,256,256]{2,1,0:T(8,128)(2,1)S(1)}, bf16[2,256,256]{2,1,0:T(8,128)(2,1)S(1)}, u32[]{:S(2)}, u32[]{:S(2)}) %collective-permute-start.4) | collective-permute-done | bytes 262176 | tf_op jit(solution)/shard_map/ppermute | solution.py:18
  38.2 1.6 %collective-permute-start.5 = (bf16[2,256,256]{2,1,0:T(8,128)(2,1)S(1)}, bf16[2,256,256]{2,1,0:T(8,128)(2,1)S(1)}, u32[]{:S(2)}, u32[]{:S(2)}) collective-permute-start(bf16[2,256,256]{2,1,0:T(8,128)(2,1)S(1)} %get-tuple-element.28), channel_id=1, source_target_pairs={{0,4},{4,0},{8,12},{12,8},{16,20},{20,16},{24,28},{28,24},{1,5},{5... | collective-permute-start | bytes 786440 | tf_op jit(solution)/shard_map/ppermute | solution.py:18
  40.9 11.0 %collective-permute-done.3.far.refs_5_ = bf16[2,256,256]{2,1,0:T(8,128)(2,1)S(1)} collective-permute-done((bf16[2,256,256]{2,1,0:T(8,128)(2,1)S(1)}, bf16[2,256,256]{2,1,0:T(8,128)(2,1)S(1)}, u32[]{:S(2)}, u32[]{:S(2)}) %collective-permute-start.3) | collective-permute-done | bytes 262176 | tf_op jit(solution)/shard_map/ppermute | solution.py:18
  51.9 2.8 %collective-permute-start.7 = (bf16[2,256,256]{2,1,0:T(8,128)(2,1)S(1)}, bf16[2,256,256]{2,1,0:T(8,128)(2,1)S(1)}, u32[]{:S(2)}, u32[]{:S(2)}) collective-permute-start(bf16[2,256,256]{2,1,0:T(8,128)(2,1)S(1)} %get-tuple-element.30), channel_id=1, source_target_pairs={{0,12},{4,8},{8,4},{12,0},{16,28},{20,24},{24,20},{28,16},{1,13},{... | collective-permute-start | bytes 786440 | tf_op jit(solution)/shard_map/ppermute | solution.py:18
  54.7 6.4 %collective-permute-done.6.refs_7_.refs_11_ = bf16[2,256,256]{2,1,0:T(8,128)(2,1)S(1)} collective-permute-done((bf16[2,256,256]{2,1,0:T(8,128)(2,1)S(1)}, bf16[2,256,256]{2,1,0:T(8,128)(2,1)S(1)}, u32[]{:S(2)}, u32[]{:S(2)}) %collective-permute-start.6) | collective-permute-done | bytes 262176 | tf_op jit(solution)/shard_map/ppermute | solution.py:18
  62.4 2.7 %collective-permute-done.7.refs_8_.refs_12_ = bf16[2,256,256]{2,1,0:T(8,128)(2,1)S(1)} collective-permute-done((bf16[2,256,256]{2,1,0:T(8,128)(2,1)S(1)}, bf16[2,256,256]{2,1,0:T(8,128)(2,1)S(1)}, u32[]{:S(2)}, u32[]{:S(2)}) %collective-permute-start.7) | collective-permute-done | bytes 262176 | tf_op jit(solution)/shard_map/ppermute | solution.py:18
  65.1 0.9 collective-permute-start.8
  66.8 1.7 %collective-permute-start.9 = (bf16[1,256,256]{2,1,0:T(8,128)(2,1)S(1)}, bf16[1,256,256]{2,1,0:T(8,128)(2,1)S(1)}, u32[]{:S(2)}, u32[]{:S(2)}) collective-permute-start(bf16[1,256,256]{2,1,0:T(8,128)(2,1)S(1)} %get-tuple-element.32), channel_id=1, source_target_pairs={{0,8},{4,12},{8,0},{12,4},{16,24},{20,28},{24,16},{28,20},{1,9},{5... | collective-permute-start | bytes 393224 | tf_op jit(solution)/shard_map/ppermute | solution.py:18
  68.6 2.4 %shard_map.68 = (bf16[2,256,256]{2,1,0:T(8,128)(2,1)S(1)}, bf16[1,256,256]{2,1,0:T(8,128)(2,1)S(1)}, bf16[1,256,256]{2,1,0:T(8,128)(2,1)S(1)}, bf16[1,256,256]{2,1,0:T(8,128)(2,1)S(1)}) custom-call(s32[2,8,8]{2,1,0:T(8,128)S(1)} %copy-done.1, s32[2,2,8]{2,1,0:T(2,128)S(1)} %copy-done.2, s32[2,2]{1,0:T(2,128)S(1)} %copy-done.3, ...), custom_call_target="tpu_custom_call" | custom-call | flops 603979776 | bytes 6422528 | tf_op jit(solution)/shard_map/pallas_call | solution.py:41
  71.0 2.9 %collective-permute-start.18 = (bf16[2,256,256]{2,1,0:T(8,128)(2,1)S(1)}, bf16[2,256,256]{2,1,0:T(8,128)(2,1)S(1)}, u32[]{:S(2)}, u32[]{:S(2)}) collective-permute-start(bf16[2,256,256]{2,1,0:T(8,128)(2,1)S(1)} %get-tuple-element.37.refs_13_.refs_22_), channel_id=1, source_target_pairs={{0,16},{4,20},{8,24},{12,28},{16,0},{20,4},{24,8},{28,12},{1,17},{... | collective-permute-start | bytes 786440 | tf_op jit(solution)/shard_map/ppermute | solution.py:18
  73.9 0.9 collective-permute-done.9.refs_10_
  74.8 2.4 %shard_map.67.refs_0_.refs_12_.refs_23_ = bf16[2,256,256]{2,1,0:T(8,128)(2,1)S(1)} custom-call(s32[2,8,8]{2,1,0:T(8,128)S(1)} %copy-done.1, s32[2,2,8]{2,1,0:T(2,128)S(1)} %copy-done.2, s32[2,2]{1,0:T(2,128)S(1)} %copy-done.3, bf16[3,2,256,512]{3,2,1,0:T(8,128)(2,1)S(1)} %copy-done, bf16[1152,256]{1,0:T(8,128)(2,1)S(1)} %pad_maximum_fusion.1.refs_0_.refs_1_, ...), custom_call_target="tpu_custom_call" | custom-call | flops 603979776 | bytes 5898240 | tf_op jit(solution)/shard_map/pallas_call | solution.py:41
  77.2 2.5 %collective-permute-start.14 = (bf16[2,256,256]{2,1,0:T(8,128)(2,1)S(1)}, bf16[2,256,256]{2,1,0:T(8,128)(2,1)S(1)}, u32[]{:S(2)}, u32[]{:S(2)}) collective-permute-start(bf16[2,256,256]{2,1,0:T(8,128)(2,1)S(1)} %shard_map.67.refs_0_.refs_12_.refs_23_), channel_id=1, source_target_pairs={{0,16},{4,20},{8,24},{12,28},{16,0},{20,4},{24,8},{28,12},{1,17},{... | collective-permute-start | bytes 786440 | tf_op jit(solution)/shard_map/ppermute | solution.py:18
  80.4 10.9 %collective-permute-done.18.far.refs_14_ = bf16[2,256,256]{2,1,0:T(8,128)(2,1)S(1)} collective-permute-done((bf16[2,256,256]{2,1,0:T(8,128)(2,1)S(1)}, bf16[2,256,256]{2,1,0:T(8,128)(2,1)S(1)}, u32[]{:S(2)}, u32[]{:S(2)}) %collective-permute-start.18) | collective-permute-done | bytes 262176 | tf_op jit(solution)/shard_map/ppermute | solution.py:18
  92.9 2.7 %collective-permute-start.21 = (bf16[2,256,256]{2,1,0:T(8,128)(2,1)S(1)}, bf16[2,256,256]{2,1,0:T(8,128)(2,1)S(1)}, u32[]{:S(2)}, u32[]{:S(2)}) collective-permute-start(bf16[2,256,256]{2,1,0:T(8,128)(2,1)S(1)} %get-tuple-element.40), channel_id=1, source_target_pairs={{0,12},{4,8},{8,4},{12,0},{16,28},{20,24},{24,20},{28,16},{1,13},{... | collective-permute-start | bytes 786440 | tf_op jit(solution)/shard_map/ppermute | solution.py:18
  95.6 2.2 %collective-permute-start.27 = (bf16[1,256,256]{2,1,0:T(8,128)(2,1)S(1)}, bf16[1,256,256]{2,1,0:T(8,128)(2,1)S(1)}, u32[]{:S(2)}, u32[]{:S(2)}) collective-permute-start(bf16[1,256,256]{2,1,0:T(8,128)(2,1)S(1)} %get-tuple-element.46), channel_id=1, source_target_pairs={{0,12},{4,8},{8,4},{12,0},{16,28},{20,24},{24,20},{28,16},{1,13},{... | collective-permute-start | bytes 393224 | tf_op jit(solution)/shard_map/ppermute | solution.py:18
  98.6 11.4 %collective-permute-done.26.refs_16_ = bf16[1,256,256]{2,1,0:T(8,128)(2,1)S(1)} collective-permute-done((bf16[1,256,256]{2,1,0:T(8,128)(2,1)S(1)}, bf16[1,256,256]{2,1,0:T(8,128)(2,1)S(1)}, u32[]{:S(2)}, u32[]{:S(2)}) %collective-permute-start.26) | collective-permute-done | bytes 131104 | tf_op jit(solution)/shard_map/ppermute | solution.py:18
  110.7 0.9 collective-permute-done.27.refs_17_
  111.6 2.8 %collective-permute-start.24 = (bf16[1,256,256]{2,1,0:T(8,128)(2,1)S(1)}, bf16[1,256,256]{2,1,0:T(8,128)(2,1)S(1)}, u32[]{:S(2)}, u32[]{:S(2)}) collective-permute-start(bf16[1,256,256]{2,1,0:T(8,128)(2,1)S(1)} %get-tuple-element.43), channel_id=1, source_target_pairs={{0,12},{4,8},{8,4},{12,0},{16,28},{20,24},{24,20},{28,16},{1,13},{... | collective-permute-start | bytes 393224 | tf_op jit(solution)/shard_map/ppermute | solution.py:18
  114.4 2.5 %shard_map.71.refs_24_ = bf16[2,256,256]{2,1,0:T(8,128)(2,1)S(1)} custom-call(s32[2,8,8]{2,1,0:T(8,128)S(1)} %copy-done.1, s32[2,2,8]{2,1,0:T(2,128)S(1)} %copy-done.2, s32[2,2]{1,0:T(2,128)S(1)} %copy-done.3, bf16[3,2,256,512]{3,2,1,0:T(8,128)(2,1)S(1)} %copy-done, bf16[1,256,256]{2,1,0:T(8,128)(2,1)S(1)} %get-tuple-element.41.refs_0_, ...), custom_call_target="tpu_custom_call" | custom-call | flops 603979776 | bytes 7733248 | tf_op jit(solution)/shard_map/pallas_call | solution.py:41
  116.9 1.8 %collective-permute-done.24.refs_19_ = bf16[1,256,256]{2,1,0:T(8,128)(2,1)S(1)} collective-permute-done((bf16[1,256,256]{2,1,0:T(8,128)(2,1)S(1)}, bf16[1,256,256]{2,1,0:T(8,128)(2,1)S(1)}, u32[]{:S(2)}, u32[]{:S(2)}) %collective-permute-start.24) | collective-permute-done | bytes 131104 | tf_op jit(solution)/shard_map/ppermute | solution.py:18
  118.8 3.2 %shard_map.72 = bf16[3,2,256,512]{3,2,1,0:T(8,128)(2,1)} custom-call(s32[2,8,8]{2,1,0:T(8,128)S(1)} %copy-done.1, s32[2,2,8]{2,1,0:T(2,128)S(1)} %copy-done.2, s32[2,2]{1,0:T(2,128)S(1)} %copy-done.3, bf16[3,2,256,512]{3,2,1,0:T(8,128)(2,1)S(1)} %copy-done, bf16[1152,256]{1,0:T(8,128)(2,1)S(1)} %pad_maximum_fusion.refs_1_.refs_0_, ...), custom_call_target="tpu_custom_call" | custom-call | flops 603979776 | bytes 10223616 | tf_op jit(solution)/shard_map/pallas_call | solution.py:41
  (47 shorter events, 8.6 us)
Async XLA Ops:
  0.9 4.5 %copy-start = (bf16[3,2,256,512]{3,2,1,0:T(8,128)(2,1)S(1)}, bf16[3,2,256,512]{3,2,1,0:T(8,128)(2,1)}, u32[]{:S(2)}) copy-start(bf16[3,2,256,512]{3,2,1,0:T(8,128)(2,1)} %noise.7) | copy-start | bytes 4718596
  2.3 18.6 %copy-start.1 = (s32[2,8,8]{2,1,0:T(8,128)S(1)}, s32[2,8,8]{2,1,0:T(8,128)}, u32[]{:S(2)}) copy-start(s32[2,8,8]{2,1,0:T(8,128)} %picks.17) | copy-start | bytes 1540
  2.4 38.0 %collective-permute-start.12 = (bf16[1152,256]{1,0:T(8,128)(2,1)S(1)}, bf16[1152,256]{1,0:T(8,128)(2,1)S(1)}, u32[]{:S(2)}, u32[]{:S(2)}) collective-permute-start(bf16[1152,256]{1,0:T(8,128)(2,1)S(1)} %pad_maximum_fusion.1.refs_0_.refs_1_), channel_id=1, source_target_pairs={{0,2},{1,3},{2,0},{3,1},{4,6},{5,7},{6,4},{7,5},{8,10},{9,11},{10,... | collective-permute-start | bytes 1769480 | tf_op jit(solution)/shard_map/ppermute | solution.py:18
  22.0 46.6 %copy-start.2 = (s32[2,2,8]{2,1,0:T(2,128)S(1)}, s32[2,2,8]{2,1,0:T(2,128)}, u32[]{:S(2)}) copy-start(s32[2,2,8]{2,1,0:T(2,128)} %lists.7) | copy-start | bytes 388
  22.0 46.6 %copy-start.3 = (s32[2,2]{1,0:T(2,128)S(1)}, s32[2,2]{1,0:T(2,128)}, u32[]{:S(2)}) copy-start(s32[2,2]{1,0:T(2,128)} %counts.7) | copy-start | bytes 52
  22.0 15.4 %collective-permute-start.4 = (bf16[2,256,256]{2,1,0:T(8,128)(2,1)S(1)}, bf16[2,256,256]{2,1,0:T(8,128)(2,1)S(1)}, u32[]{:S(2)}, u32[]{:S(2)}) collective-permute-start(bf16[2,256,256]{2,1,0:T(8,128)(2,1)S(1)} %get-tuple-element.27.refs_5_.refs_20_), channel_id=1, source_target_pairs={{0,16},{4,20},{8,24},{12,28},{16,0},{20,4},{24,8},{28,12},{1,17},{... | collective-permute-start | bytes 786440 | tf_op jit(solution)/shard_map/ppermute | solution.py:18
  24.9 5.5 %collective-permute-start.15 = (bf16[1,256,256]{2,1,0:T(8,128)(2,1)S(1)}, bf16[1,256,256]{2,1,0:T(8,128)(2,1)S(1)}, u32[]{:S(2)}, u32[]{:S(2)}) collective-permute-start(bf16[1,256,256]{2,1,0:T(8,128)(2,1)S(1)} %get-tuple-element.34), channel_id=1, source_target_pairs={{0,4},{4,0},{8,12},{12,8},{16,20},{20,16},{24,28},{28,24},{1,5},{5... | collective-permute-start | bytes 393224 | tf_op jit(solution)/shard_map/ppermute | solution.py:18
  26.5 34.7 %collective-permute-start.1 = (bf16[1152,256]{1,0:T(8,128)(2,1)S(1)}, bf16[1152,256]{1,0:T(8,128)(2,1)S(1)}, u32[]{:S(2)}, u32[]{:S(2)}) collective-permute-start(bf16[1152,256]{1,0:T(8,128)(2,1)S(1)} %pad_maximum_fusion.refs_1_.refs_0_), channel_id=1, source_target_pairs={{0,2},{1,3},{2,0},{3,1},{4,6},{5,7},{6,4},{7,5},{8,10},{9,11},{10,... | collective-permute-start | bytes 1769480 | tf_op jit(solution)/shard_map/ppermute | solution.py:18
  28.0 10.2 %collective-permute-start.16 = (bf16[1,256,256]{2,1,0:T(8,128)(2,1)S(1)}, bf16[1,256,256]{2,1,0:T(8,128)(2,1)S(1)}, u32[]{:S(2)}, u32[]{:S(2)}) collective-permute-start(bf16[1,256,256]{2,1,0:T(8,128)(2,1)S(1)} %get-tuple-element.35), channel_id=1, source_target_pairs={{0,8},{4,12},{8,0},{12,4},{16,24},{20,28},{24,16},{28,20},{1,9},{5... | collective-permute-start | bytes 393224 | tf_op jit(solution)/shard_map/ppermute | solution.py:18
  30.4 10.0 %collective-permute-start.17 = (bf16[1,256,256]{2,1,0:T(8,128)(2,1)S(1)}, bf16[1,256,256]{2,1,0:T(8,128)(2,1)S(1)}, u32[]{:S(2)}, u32[]{:S(2)}) collective-permute-start(bf16[1,256,256]{2,1,0:T(8,128)(2,1)S(1)} %get-tuple-element.36), channel_id=1, source_target_pairs={{0,12},{4,8},{8,4},{12,0},{16,28},{20,24},{24,20},{28,16},{1,13},{... | collective-permute-start | bytes 393224 | tf_op jit(solution)/shard_map/ppermute | solution.py:18
  37.4 14.4 %collective-permute-start.3 = (bf16[2,256,256]{2,1,0:T(8,128)(2,1)S(1)}, bf16[2,256,256]{2,1,0:T(8,128)(2,1)S(1)}, u32[]{:S(2)}, u32[]{:S(2)}) collective-permute-start(bf16[2,256,256]{2,1,0:T(8,128)(2,1)S(1)} %get-tuple-element.26.refs_0_.refs_4_.refs_21_), channel_id=1, source_target_pairs={{0,16},{4,20},{8,24},{12,28},{16,0},{20,4},{24,8},{28,12},{1,17},{... | collective-permute-start | bytes 786440 | tf_op jit(solution)/shard_map/ppermute | solution.py:18
  38.2 13.7 %collective-permute-start.5 = (bf16[2,256,256]{2,1,0:T(8,128)(2,1)S(1)}, bf16[2,256,256]{2,1,0:T(8,128)(2,1)S(1)}, u32[]{:S(2)}, u32[]{:S(2)}) collective-permute-start(bf16[2,256,256]{2,1,0:T(8,128)(2,1)S(1)} %get-tuple-element.28), channel_id=1, source_target_pairs={{0,4},{4,0},{8,12},{12,8},{16,20},{20,16},{24,28},{28,24},{1,5},{5... | collective-permute-start | bytes 786440 | tf_op jit(solution)/shard_map/ppermute | solution.py:18
  40.4 25.6 %collective-permute-start.11 = (bf16[1152,256]{1,0:T(8,128)(2,1)S(1)}, bf16[1152,256]{1,0:T(8,128)(2,1)S(1)}, u32[]{:S(2)}, u32[]{:S(2)}) collective-permute-start(bf16[1152,256]{1,0:T(8,128)(2,1)S(1)} %pad_maximum_fusion.1.refs_0_.refs_1_), channel_id=1, source_target_pairs={{0,1},{1,0},{2,3},{3,2},{4,5},{5,4},{6,7},{7,6},{8,9},{9,8},{10,11... | collective-permute-start | bytes 1769480 | tf_op jit(solution)/shard_map/ppermute | solution.py:18
  40.4 26.4 %collective-permute-start.13 = (bf16[1152,256]{1,0:T(8,128)(2,1)S(1)}, bf16[1152,256]{1,0:T(8,128)(2,1)S(1)}, u32[]{:S(2)}, u32[]{:S(2)}) collective-permute-start(bf16[1152,256]{1,0:T(8,128)(2,1)S(1)} %collective-permute-done.12.refs_2_.refs_3_), channel_id=1, source_target_pairs={{0,1},{1,0},{2,3},{3,2},{4,5},{5,4},{6,7},{7,6},{8,9},{9,8},{10,11... | collective-permute-start | bytes 1769480 | tf_op jit(solution)/shard_map/ppermute | solution.py:18
  51.9 9.2 %collective-permute-start.6 = (bf16[2,256,256]{2,1,0:T(8,128)(2,1)S(1)}, bf16[2,256,256]{2,1,0:T(8,128)(2,1)S(1)}, u32[]{:S(2)}, u32[]{:S(2)}) collective-permute-start(bf16[2,256,256]{2,1,0:T(8,128)(2,1)S(1)} %get-tuple-element.29), channel_id=1, source_target_pairs={{0,8},{4,12},{8,0},{12,4},{16,24},{20,28},{24,16},{28,20},{1,9},{5... | collective-permute-start | bytes 786440 | tf_op jit(solution)/shard_map/ppermute | solution.py:18
  51.9 13.2 %collective-permute-start.7 = (bf16[2,256,256]{2,1,0:T(8,128)(2,1)S(1)}, bf16[2,256,256]{2,1,0:T(8,128)(2,1)S(1)}, u32[]{:S(2)}, u32[]{:S(2)}) collective-permute-start(bf16[2,256,256]{2,1,0:T(8,128)(2,1)S(1)} %get-tuple-element.30), channel_id=1, source_target_pairs={{0,12},{4,8},{8,4},{12,0},{16,28},{20,24},{24,20},{28,16},{1,13},{... | collective-permute-start | bytes 786440 | tf_op jit(solution)/shard_map/ppermute | solution.py:18
  61.1 31.7 %collective-permute-start = (bf16[1152,256]{1,0:T(8,128)(2,1)S(1)}, bf16[1152,256]{1,0:T(8,128)(2,1)S(1)}, u32[]{:S(2)}, u32[]{:S(2)}) collective-permute-start(bf16[1152,256]{1,0:T(8,128)(2,1)S(1)} %pad_maximum_fusion.refs_1_.refs_0_), channel_id=1, source_target_pairs={{0,1},{1,0},{2,3},{3,2},{4,5},{5,4},{6,7},{7,6},{8,9},{9,8},{10,11... | collective-permute-start | bytes 1769480 | tf_op jit(solution)/shard_map/ppermute | solution.py:18
  61.1 31.7 %collective-permute-start.2 = (bf16[1152,256]{1,0:T(8,128)(2,1)S(1)}, bf16[1152,256]{1,0:T(8,128)(2,1)S(1)}, u32[]{:S(2)}, u32[]{:S(2)}) collective-permute-start(bf16[1152,256]{1,0:T(8,128)(2,1)S(1)} %collective-permute-done.1.refs_3_.refs_2_), channel_id=1, source_target_pairs={{0,1},{1,0},{2,3},{3,2},{4,5},{5,4},{6,7},{7,6},{8,9},{9,8},{10,11... | collective-permute-start | bytes 1769480 | tf_op jit(solution)/shard_map/ppermute | solution.py:18
  65.1 5.9 %collective-permute-start.8 = (bf16[1,256,256]{2,1,0:T(8,128)(2,1)S(1)}, bf16[1,256,256]{2,1,0:T(8,128)(2,1)S(1)}, u32[]{:S(2)}, u32[]{:S(2)}) collective-permute-start(bf16[1,256,256]{2,1,0:T(8,128)(2,1)S(1)} %get-tuple-element.31.refs_0_), channel_id=1, source_target_pairs={{0,4},{4,0},{8,12},{12,8},{16,20},{20,16},{24,28},{28,24},{1,5},{5... | collective-permute-start | bytes 393224 | tf_op jit(solution)/shard_map/ppermute | solution.py:18
  66.0 7.9 %collective-permute-start.10 = (bf16[1,256,256]{2,1,0:T(8,128)(2,1)S(1)}, bf16[1,256,256]{2,1,0:T(8,128)(2,1)S(1)}, u32[]{:S(2)}, u32[]{:S(2)}) collective-permute-start(bf16[1,256,256]{2,1,0:T(8,128)(2,1)S(1)} %get-tuple-element.33), channel_id=1, source_target_pairs={{0,12},{4,8},{8,4},{12,0},{16,28},{20,24},{24,20},{28,16},{1,13},{... | collective-permute-start | bytes 393224 | tf_op jit(solution)/shard_map/ppermute | solution.py:18
  66.8 8.0 %collective-permute-start.9 = (bf16[1,256,256]{2,1,0:T(8,128)(2,1)S(1)}, bf16[1,256,256]{2,1,0:T(8,128)(2,1)S(1)}, u32[]{:S(2)}, u32[]{:S(2)}) collective-permute-start(bf16[1,256,256]{2,1,0:T(8,128)(2,1)S(1)} %get-tuple-element.32), channel_id=1, source_target_pairs={{0,8},{4,12},{8,0},{12,4},{16,24},{20,28},{24,16},{28,20},{1,9},{5... | collective-permute-start | bytes 393224 | tf_op jit(solution)/shard_map/ppermute | solution.py:18
  71.0 20.2 %collective-permute-start.18 = (bf16[2,256,256]{2,1,0:T(8,128)(2,1)S(1)}, bf16[2,256,256]{2,1,0:T(8,128)(2,1)S(1)}, u32[]{:S(2)}, u32[]{:S(2)}) collective-permute-start(bf16[2,256,256]{2,1,0:T(8,128)(2,1)S(1)} %get-tuple-element.37.refs_13_.refs_22_), channel_id=1, source_target_pairs={{0,16},{4,20},{8,24},{12,28},{16,0},{20,4},{24,8},{28,12},{1,17},{... | collective-permute-start | bytes 786440 | tf_op jit(solution)/shard_map/ppermute | solution.py:18
  77.2 18.4 %collective-permute-start.14 = (bf16[2,256,256]{2,1,0:T(8,128)(2,1)S(1)}, bf16[2,256,256]{2,1,0:T(8,128)(2,1)S(1)}, u32[]{:S(2)}, u32[]{:S(2)}) collective-permute-start(bf16[2,256,256]{2,1,0:T(8,128)(2,1)S(1)} %shard_map.67.refs_0_.refs_12_.refs_23_), channel_id=1, source_target_pairs={{0,16},{4,20},{8,24},{12,28},{16,0},{20,4},{24,8},{28,12},{1,17},{... | collective-permute-start | bytes 786440 | tf_op jit(solution)/shard_map/ppermute | solution.py:18
  79.7 15.9 %collective-permute-start.25 = (bf16[1,256,256]{2,1,0:T(8,128)(2,1)S(1)}, bf16[1,256,256]{2,1,0:T(8,128)(2,1)S(1)}, u32[]{:S(2)}, u32[]{:S(2)}) collective-permute-start(bf16[1,256,256]{2,1,0:T(8,128)(2,1)S(1)} %get-tuple-element.44), channel_id=1, source_target_pairs={{0,4},{4,0},{8,12},{12,8},{16,20},{20,16},{24,28},{28,24},{1,5},{5... | collective-permute-start | bytes 393224 | tf_op jit(solution)/shard_map/ppermute | solution.py:18
  92.0 19.6 %collective-permute-start.19 = (bf16[2,256,256]{2,1,0:T(8,128)(2,1)S(1)}, bf16[2,256,256]{2,1,0:T(8,128)(2,1)S(1)}, u32[]{:S(2)}, u32[]{:S(2)}) collective-permute-start(bf16[2,256,256]{2,1,0:T(8,128)(2,1)S(1)} %get-tuple-element.38), channel_id=1, source_target_pairs={{0,4},{4,0},{8,12},{12,8},{16,20},{20,16},{24,28},{28,24},{1,5},{5... | collective-permute-start | bytes 786440 | tf_op jit(solution)/shard_map/ppermute | solution.py:18
  92.9 21.6 %collective-permute-start.20 = (bf16[2,256,256]{2,1,0:T(8,128)(2,1)S(1)}, bf16[2,256,256]{2,1,0:T(8,128)(2,1)S(1)}, u32[]{:S(2)}, u32[]{:S(2)}) collective-permute-start(bf16[2,256,256]{2,1,0:T(8,128)(2,1)S(1)} %get-tuple-element.39), channel_id=1, source_target_pairs={{0,8},{4,12},{8,0},{12,4},{16,24},{20,28},{24,16},{28,20},{1,9},{5... | collective-permute-start | bytes 786440 | tf_op jit(solution)/shard_map/ppermute | solution.py:18
  92.9 21.6 %collective-permute-start.21 = (bf16[2,256,256]{2,1,0:T(8,128)(2,1)S(1)}, bf16[2,256,256]{2,1,0:T(8,128)(2,1)S(1)}, u32[]{:S(2)}, u32[]{:S(2)}) collective-permute-start(bf16[2,256,256]{2,1,0:T(8,128)(2,1)S(1)} %get-tuple-element.40), channel_id=1, source_target_pairs={{0,12},{4,8},{8,4},{12,0},{16,28},{20,24},{24,20},{28,16},{1,13},{... | collective-permute-start | bytes 786440 | tf_op jit(solution)/shard_map/ppermute | solution.py:18
  95.6 14.4 %collective-permute-start.26 = (bf16[1,256,256]{2,1,0:T(8,128)(2,1)S(1)}, bf16[1,256,256]{2,1,0:T(8,128)(2,1)S(1)}, u32[]{:S(2)}, u32[]{:S(2)}) collective-permute-start(bf16[1,256,256]{2,1,0:T(8,128)(2,1)S(1)} %get-tuple-element.45), channel_id=1, source_target_pairs={{0,8},{4,12},{8,0},{12,4},{16,24},{20,28},{24,16},{28,20},{1,9},{5... | collective-permute-start | bytes 393224 | tf_op jit(solution)/shard_map/ppermute | solution.py:18
  95.6 16.0 %collective-permute-start.27 = (bf16[1,256,256]{2,1,0:T(8,128)(2,1)S(1)}, bf16[1,256,256]{2,1,0:T(8,128)(2,1)S(1)}, u32[]{:S(2)}, u32[]{:S(2)}) collective-permute-start(bf16[1,256,256]{2,1,0:T(8,128)(2,1)S(1)} %get-tuple-element.46), channel_id=1, source_target_pairs={{0,12},{4,8},{8,4},{12,0},{16,28},{20,24},{24,20},{28,16},{1,13},{... | collective-permute-start | bytes 393224 | tf_op jit(solution)/shard_map/ppermute | solution.py:18
  110.0 6.9 %collective-permute-start.22 = (bf16[1,256,256]{2,1,0:T(8,128)(2,1)S(1)}, bf16[1,256,256]{2,1,0:T(8,128)(2,1)S(1)}, u32[]{:S(2)}, u32[]{:S(2)}) collective-permute-start(bf16[1,256,256]{2,1,0:T(8,128)(2,1)S(1)} %get-tuple-element.41.refs_0_), channel_id=1, source_target_pairs={{0,4},{4,0},{8,12},{12,8},{16,20},{20,16},{24,28},{28,24},{1,5},{5... | collective-permute-start | bytes 393224 | tf_op jit(solution)/shard_map/ppermute | solution.py:18
  111.6 5.3 %collective-permute-start.23 = (bf16[1,256,256]{2,1,0:T(8,128)(2,1)S(1)}, bf16[1,256,256]{2,1,0:T(8,128)(2,1)S(1)}, u32[]{:S(2)}, u32[]{:S(2)}) collective-permute-start(bf16[1,256,256]{2,1,0:T(8,128)(2,1)S(1)} %get-tuple-element.42), channel_id=1, source_target_pairs={{0,8},{4,12},{8,0},{12,4},{16,24},{20,28},{24,16},{28,20},{1,9},{5... | collective-permute-start | bytes 393224 | tf_op jit(solution)/shard_map/ppermute | solution.py:18
  111.6 7.2 %collective-permute-start.24 = (bf16[1,256,256]{2,1,0:T(8,128)(2,1)S(1)}, bf16[1,256,256]{2,1,0:T(8,128)(2,1)S(1)}, u32[]{:S(2)}, u32[]{:S(2)}) collective-permute-start(bf16[1,256,256]{2,1,0:T(8,128)(2,1)S(1)} %get-tuple-element.43), channel_id=1, source_target_pairs={{0,12},{4,8},{8,4},{12,0},{16,28},{20,24},{24,20},{28,16},{1,13},{... | collective-permute-start | bytes 393224 | tf_op jit(solution)/shard_map/ppermute | solution.py:18

commit v6 on v5

--- a/solution.py
+++ b/solution.py
@@ -49,43 +49,62 @@
     )(*small, *arrays)
 
 
-def first_kernel(sides, picks, noise, inverse, *refs):
-    *refs, inv = refs
-    solved, sends = refs[:-sides], refs[-sides:]
+def write_pack(target, level, inverse, coupling):
+    nodes, width, depth = coupling.shape[1:4]
+    rows = inverse.shape[2]
+    for node in range(nodes):
+        for offset in range(width):
+            at = (node * width + offset) * depth
+            target[at:at + depth, :] = coupling[level - 1, node, offset]
+        at = nodes * width * depth + node * rows
+        target[at:at + rows, :] = inverse[level, node]
+
+
+def first_kernel(chunks, picks, noise, inverse, coupling, gathered, *refs):
+    pack, *refs, inv = refs
+    solved, sends = take(refs, chunks)
     myself = lax.axis_index("leaf")
-    draws, nodes, rows = inverse.shape[:3]
+    draws, nodes, rows = gathered.shape[:3]
     wide = solved[0].shape[-1]
     for part in range(draws):
-        inv[:, part * rows:(part + 1) * rows, :] = inverse[part]
+        inv[:, part * rows:(part + 1) * rows, :] = gathered[part]
     for at, target in enumerate(solved):
         for node in range(nodes):
-            right = noise[node, :, at * wide:(at + 1) * wide]
+            right = noise[0, node, :, at * wide:(at + 1) * wide]
             target[node] = transposed_dot(inv[node], right).astype(BF16)
     for step, send in enumerate(sends, 1):
-        send[0] = solved[0][picks[0, myself ^ step, myself]]
-
-
-def relay_kernel(half, source, last, picks, far, *refs):
-    own, sends = (None, refs) if last else (refs[0], refs[1:])
+        node = picks[0, myself ^ step, myself]
+        for at, target in enumerate(solved):
+            send[at] = target[node]
+    write_pack(pack, 1, inverse, coupling)
+
+
+def relay_kernel(owners, source, follow, pack_level, waits, picks, far, *refs):
+    half = owners // 2
+    if pack_level:
+        inverse, coupling, *refs = refs
+    own, refs = take(refs, follow)
+    _, refs = take(refs, waits)
+    sends, refs = take(refs, half - 1)
     myself = lax.axis_index("leaf")
     for step, send in enumerate(sends, 1):
         send[0] = far[picks[source, myself ^ step, myself ^ half]]
-        if not last:
-            send[1] = own[picks[source, myself ^ step, myself]]
+        if own:
+            send[1] = own[0][picks[source, myself ^ step, myself]]
+    if pack_level:
+        write_pack(refs[0], pack_level, inverse, coupling)
 
 
 def level_kernel(
-    level, owners, draws, chunk, waits, sides, earlier, width, picks, lists, counts, noise, *refs
+    level, owners, draws, width, chunk, places, sides, earlier, waits,
+    picks, lists, counts, noise, *refs,
 ):
     half = owners // 2
+    packs, refs = take(refs, draws)
+    known, refs = take(refs, level * owners)
+    done, refs = take(refs, earlier)
     _, refs = take(refs, waits)
-    packs, refs = take(refs, draws)
-    pieces = []
-    for _ in range(level):
-        piece, refs = take(refs, owners)
-        pieces.append(piece)
-    done, refs = take(refs, earlier)
-    target, refs = refs[0], refs[1:]
+    target, *refs = refs
     sends, (table, inv, *refs) = take(refs, sides)
     myself, draw = lax.axis_index("leaf"), lax.axis_index("draw")
     nodes, wide = noise.shape[1], table.shape[-1]
@@ -100,14 +119,11 @@
             here = target.at[at // per_level, :, :, pl.ds(at % per_level * wide, wide)]
             copies.append(pltpu.make_async_copy(ref, here, sems.at[at]))
             copies[-1].start()
-    for source, (own, far, *others) in enumerate(pieces):
-        first = source * owners
-        table[first] = own[picks[source, myself, myself]]
-        table[first + half] = far[picks[source, myself, myself ^ half]]
-        for step in range(1, half):
-            near, distant = others[step - 1], others[half + step - 2]
-            table[first + step] = near[near.shape[0] - 1]
-            table[first + (half ^ step)] = distant[0]
+    for at, (ref, place) in enumerate(zip(known, places, strict=True)):
+        step = at % owners
+        if step % half == 0:
+            place = picks[at // owners, myself, myself ^ step]
+        table[at] = ref[place]
     empty = level * owners
     table[empty] = jnp.zeros_like(table[empty])
     for step, pack in enumerate(packs):
@@ -143,50 +159,60 @@
     width, last_level = coupling.shape[2], levels - 1
     shape = lambda *dims: jax.ShapeDtypeStruct(dims, BF16)
     part = shape(nodes, rows, wide)
+    pack_shape = shape(nodes * (width * rows + inverse.shape[2]), rows)
     leaf = lambda value, step: hop(value, "leaf", owners, step)
     near = lambda values: [leaf(value, step) for step, value in enumerate(values, 1)]
+    gather = lambda value: gather_parts(value, "draw", draws)
     inv_here = pltpu.VMEM((nodes, rows, rows), BF16)
     dot_flops = 2 * rows * rows * wide
 
-    inverse_first = lax.all_gather(inverse[0], "draw", axis=0)
-    packs = [
-        gather_parts(
-            jnp.concatenate([coupling[level - 1].reshape(-1, rows), inverse[level].reshape(-1, rows)]),
-            "draw", draws,
-        )
-        for level in range(1, levels)
-    ]
-    solved = call(
-        functools.partial(first_kernel, half - 1),
-        [part] * CHUNKS + [shape(1, rows, wide)] * (half - 1),
+    pack, *refs = call(
+        functools.partial(first_kernel, CHUNKS),
+        [pack_shape] + [part] * CHUNKS + [shape(CHUNKS, rows, wide)] * (half - 1),
         [inv_here],
         (picks,),
-        (noise[0], inverse_first),
+        (noise, inverse, coupling, lax.all_gather(inverse[0], "draw", axis=0)),
         flops=nodes * CHUNKS * dot_flops,
     )
-    solved, sends = solved[:CHUNKS], solved[CHUNKS:]
+    solved, sends = take(refs, CHUNKS)
+    packs = [gather(pack)]
     done, pieces = [solved], []
     for level in range(1, levels):
+        source = level - 1
         far = [leaf(value, half) for value in solved]
-        got = [near(sends)]
+        got = near(sends)
+        close = [[(ref, at) for ref in got] for at in chunks] if source == 0 else [[(ref, 0) for ref in got]]
+        distant, waits = [], packs[source] if source == 0 else got
         for at in chunks:
-            last = at == CHUNKS - 1
-            sends = call(
-                functools.partial(relay_kernel, half, level - 1, last),
-                [shape(1 if last else 2, rows, wide)] * (half - 1),
+            follow = source > 0 and at < CHUNKS - 1
+            pack_level = source + 2 if at == 0 and source + 2 < levels else 0
+            sends = list(call(
+                functools.partial(relay_kernel, owners, source, int(follow), pack_level, len(waits)),
+                [shape(1 + follow, rows, wide)] * (half - 1) + [pack_shape] * bool(pack_level),
                 [],
                 (picks,),
-                (far[at],) if last else (far[at], solved[at + 1]),
-            )
-            got.append(near(sends))
-        pieces.append([(solved[at], far[at], *got[at], *got[at + 1]) for at in chunks])
-        token = sends[:1]
+                (
+                    far[at], *((inverse, coupling) if pack_level else ()),
+                    *([solved[at + 1]] if follow else []), *waits,
+                ),
+            ))
+            if pack_level:
+                packs.append(gather(sends.pop()))
+            got = near(sends)
+            distant.append([(ref, 0) for ref in got])
+            if follow:
+                close.append([(ref, 1) for ref in got])
+            waits = []
+        pieces.append([
+            [(solved[at], 0), *close[at], (far[at], 0), *distant[at]] for at in chunks
+        ])
+        waits = sends[:1]
         solved, sends = [], []
         for at in chunks:
             sides = half - 1 if at == 0 and level < last_level else 0
             final = level == last_level and at == CHUNKS - 1
             earlier = [value for values in done for value in values] + solved if final else []
-            waits = token if at == 0 else []
+            known = [entry for below in range(level) for entry in pieces[below][at]]
             scratch = [pltpu.VMEM((level * owners + 1, rows, wide), BF16), inv_here]
             if final:
                 scratch += [
@@ -195,22 +221,20 @@
                 ]
             here, *sent = call(
                 functools.partial(
-                    level_kernel, level, owners, draws, at, len(waits), sides, len(earlier), width
+                    level_kernel, level, owners, draws, width, at,
+                    [place for _, place in known], sides, len(earlier), len(waits),
                 ),
                 [shape(levels, nodes, rows, columns) if final else part]
                 + [shape(1, rows, wide)] * sides,
                 scratch,
                 (picks, lists, counts),
-                (
-                    noise, *waits, *packs[level - 1],
-                    *(ref for source in range(level) for ref in pieces[source][at]),
-                    *earlier,
-                ),
+                (noise, *packs[level - 1], *(ref for ref, _ in known), *earlier, *waits),
                 out_spec=ANY if final else VMEM,
                 flops=nodes * (draws * width + 1) * dot_flops,
             )
             solved.append(here)
             sends += sent
+            waits = packs[level] if at == 0 and level < last_level else []
         done.append(solved)
     return here
 

time: 123 us -> 122 us (level)
  waiting for transfers between devices: 52.1 us -> 63.9 us
  blocking collectives: 15.5 us -> 7.18 us
  starting transfers between devices: 37.4 us -> 31.3 us
  local copies, waits for them, and re-layouts: 2.36 us -> 5.12 us
    ppermute x28, waiting for transfers between devices: 52.1 us -> 63.9 us  [hop(): return lax.ppermute(value, axis, [(at, at ^ step) for at in range(size)])]
    all_gather x1, blocking collectives: 15.5 us -> 7.18 us  [on_device(): lax.all_gather(inverse[0], 'draw', axis=0)]
    ppermute x28, starting transfers between devices: 37.4 us -> 31.3 us  [hop(): return lax.ppermute(value, axis, [(at, at ^ step) for at in range(size)])]
    unnamed x8 -> x18, local copies, waits for them, and re-layouts: 0.03 us -> 4.27 us
    slice x2 -> x1, local copies, waits for them, and re-layouts: 2.3 us -> 0.84 us  [on_device(): inverse[0]]
  transfers between devices with their start and end apart: 28 -> 28, of which waited for: 11 -> 15; matrix products, arithmetic and copies ran while one was open for 0% -> 0% of each run, Pallas kernels for 9% -> 8%
where the time goes in v6:
time: 122 us
  waiting for transfers between devices  63.9 us (52%)
  starting transfers between devices  31.3 us (26%)
  Pallas kernels  14.4 us (12%)
  blocking collectives  7.18 us (6%)
  local copies, waits for them, and re-layouts  5.12 us (4%)
    ppermute x28, waiting for transfers between devices, hop(): return lax.ppermute(value, axis, [(at, at ^ step) for at in range(size)])  63.9 us
    ppermute x28, starting transfers between devices, hop(): return lax.ppermute(value, axis, [(at, at ^ step) for at in range(size)])  31.3 us
    pallas_call x9, Pallas kernels, call(): pl.pallas_call(kernel, out_shape=outs, in_specs=[SMEM] * len(small) + [VM...  14.4 us
    all_gather x1, blocking collectives, on_device(): lax.all_gather(inverse[0], 'draw', axis=0)  7.18 us
    unnamed x18, local copies, waits for them, and re-layouts  4.27 us
  transfers between devices with their start and end apart: 28, of which 15 were waited for; matrix products, arithmetic and copies ran while one was open for 0% of the time, Pallas kernels for 8%

profile of v6, /device:TPU:0, one launch (start us, length us, event | category | flops | bytes accessed | tf_op | source)
XLA Modules:
  0.0 122.1 jit_solution(12575286232409228017)
XLA Ops:
  0.8 7.2 %all_gather.3.gathered = bf16[4,2,64,256]{3,2,1,0:T(8,128)(2,1)S(1)} all-gather(bf16[1,2,64,256]{3,2,1,0:T(8,128)(2,1)S(1)} %slice.3), channel_id=1, replica_groups=mesh['leaf'=8,'draw'=4] {'draw'}, dimensions={0}, use_global_device_ids=true | all-gather | bytes 327680 | tf_op jit(solution)/shard_map/all_gather | solution.py:174
  8.0 1.4 %copy-done = bf16[3,2,256,512]{3,2,1,0:T(8,128)(2,1)S(1)} copy-done((bf16[3,2,256,512]{3,2,1,0:T(8,128)(2,1)S(1)}, bf16[3,2,256,512]{3,2,1,0:T(8,128)(2,1)}, u32[]{:S(2)}) %copy-start) | copy-done | bytes 1572888
  9.4 1.2 %copy-done.2 = bf16[2,2,2,256,256]{4,3,2,1,0:T(8,128)(2,1)S(1)} copy-done((bf16[2,2,2,256,256]{4,3,2,1,0:T(8,128)(2,1)S(1)}, bf16[2,2,2,256,256]{4,3,2,1,0:T(8,128)(2,1)}, u32[]{:S(2)}) %copy-start.2) | copy-done | bytes 1048600
  12.3 1.1 shard_map.64
  13.3 1.6 %collective-permute-start.2 = (bf16[1152,256]{1,0:T(8,128)(2,1)S(1)}, bf16[1152,256]{1,0:T(8,128)(2,1)S(1)}, u32[]{:S(2)}, u32[]{:S(2)}) collective-permute-start(bf16[1152,256]{1,0:T(8,128)(2,1)S(1)} %get-tuple-element.29.refs_2_.refs_0_), channel_id=1, source_target_pairs={{0,2},{1,3},{2,0},{3,1},{4,6},{5,7},{6,4},{7,5},{8,10},{9,11},{10,... | collective-permute-start | bytes 1769480 | tf_op jit(solution)/shard_map/ppermute | solution.py:18
  15.0 14.0 %collective-permute-done.2.refs_4_.refs_2_ = bf16[1152,256]{1,0:T(8,128)(2,1)S(1)} collective-permute-done((bf16[1152,256]{1,0:T(8,128)(2,1)S(1)}, bf16[1152,256]{1,0:T(8,128)(2,1)S(1)}, u32[]{:S(2)}, u32[]{:S(2)}) %collective-permute-start.2) | collective-permute-done | bytes 589856 | tf_op jit(solution)/shard_map/ppermute | solution.py:18
  29.0 2.7 %collective-permute-start = (bf16[2,256,256]{2,1,0:T(8,128)(2,1)S(1)}, bf16[2,256,256]{2,1,0:T(8,128)(2,1)S(1)}, u32[]{:S(2)}, u32[]{:S(2)}) collective-permute-start(bf16[2,256,256]{2,1,0:T(8,128)(2,1)S(1)} %get-tuple-element.28.refs_4_.refs_20_), channel_id=1, source_target_pairs={{0,16},{4,20},{8,24},{12,28},{16,0},{20,4},{24,8},{28,12},{1,17},{... | collective-permute-start | bytes 786440 | tf_op jit(solution)/shard_map/ppermute | solution.py:18
  31.7 12.5 %collective-permute-done.far.refs_8_ = bf16[2,256,256]{2,1,0:T(8,128)(2,1)S(1)} collective-permute-done((bf16[2,256,256]{2,1,0:T(8,128)(2,1)S(1)}, bf16[2,256,256]{2,1,0:T(8,128)(2,1)S(1)}, u32[]{:S(2)}, u32[]{:S(2)}) %collective-permute-start) | collective-permute-done | bytes 262176 | tf_op jit(solution)/shard_map/ppermute | solution.py:18
  45.0 1.6 %collective-permute-start.5 = (bf16[1152,256]{1,0:T(8,128)(2,1)S(1)}, bf16[1152,256]{1,0:T(8,128)(2,1)S(1)}, u32[]{:S(2)}, u32[]{:S(2)}) collective-permute-start(bf16[1152,256]{1,0:T(8,128)(2,1)S(1)} %get-tuple-element.30.refs_12_.refs_0_), channel_id=1, source_target_pairs={{0,2},{1,3},{2,0},{3,1},{4,6},{5,7},{6,4},{7,5},{8,10},{9,11},{10,... | collective-permute-start | bytes 1769480 | tf_op jit(solution)/shard_map/ppermute | solution.py:18
  46.6 1.5 %collective-permute-start.7 = (bf16[2,256,256]{2,1,0:T(8,128)(2,1)S(1)}, bf16[2,256,256]{2,1,0:T(8,128)(2,1)S(1)}, u32[]{:S(2)}, u32[]{:S(2)}) collective-permute-start(bf16[2,256,256]{2,1,0:T(8,128)(2,1)S(1)} %get-tuple-element.32), channel_id=1, source_target_pairs={{0,4},{4,0},{8,12},{12,8},{16,20},{20,16},{24,28},{28,24},{1,5},{5... | collective-permute-start | bytes 786440 | tf_op jit(solution)/shard_map/ppermute | solution.py:18
  48.8 1.3 %collective-permute-start.9 = (bf16[2,256,256]{2,1,0:T(8,128)(2,1)S(1)}, bf16[2,256,256]{2,1,0:T(8,128)(2,1)S(1)}, u32[]{:S(2)}, u32[]{:S(2)}) collective-permute-start(bf16[2,256,256]{2,1,0:T(8,128)(2,1)S(1)} %get-tuple-element.34), channel_id=1, source_target_pairs={{0,12},{4,8},{8,4},{12,0},{16,28},{20,24},{24,20},{28,16},{1,13},{... | collective-permute-start | bytes 786440 | tf_op jit(solution)/shard_map/ppermute | solution.py:18
  50.1 4.8 %collective-permute-done.7.refs_5_ = bf16[2,256,256]{2,1,0:T(8,128)(2,1)S(1)} collective-permute-done((bf16[2,256,256]{2,1,0:T(8,128)(2,1)S(1)}, bf16[2,256,256]{2,1,0:T(8,128)(2,1)S(1)}, u32[]{:S(2)}, u32[]{:S(2)}) %collective-permute-start.7) | collective-permute-done | bytes 262176 | tf_op jit(solution)/shard_map/ppermute | solution.py:18
  54.9 5.0 %collective-permute-done.5.refs_14_.refs_2_ = bf16[1152,256]{1,0:T(8,128)(2,1)S(1)} collective-permute-done((bf16[1152,256]{1,0:T(8,128)(2,1)S(1)}, bf16[1152,256]{1,0:T(8,128)(2,1)S(1)}, u32[]{:S(2)}, u32[]{:S(2)}) %collective-permute-start.5) | collective-permute-done | bytes 589856 | tf_op jit(solution)/shard_map/ppermute | solution.py:18
  59.9 3.0 %collective-permute-done.8.refs_6_ = bf16[2,256,256]{2,1,0:T(8,128)(2,1)S(1)} collective-permute-done((bf16[2,256,256]{2,1,0:T(8,128)(2,1)S(1)}, bf16[2,256,256]{2,1,0:T(8,128)(2,1)S(1)}, u32[]{:S(2)}, u32[]{:S(2)}) %collective-permute-start.8) | collective-permute-done | bytes 262176 | tf_op jit(solution)/shard_map/ppermute | solution.py:18
  63.0 3.7 %collective-permute-done.9.refs_7_ = bf16[2,256,256]{2,1,0:T(8,128)(2,1)S(1)} collective-permute-done((bf16[2,256,256]{2,1,0:T(8,128)(2,1)S(1)}, bf16[2,256,256]{2,1,0:T(8,128)(2,1)S(1)}, u32[]{:S(2)}, u32[]{:S(2)}) %collective-permute-start.9) | collective-permute-done | bytes 262176 | tf_op jit(solution)/shard_map/ppermute | solution.py:18
  66.7 3.2 %collective-permute-start.16 = (bf16[1,256,256]{2,1,0:T(8,128)(2,1)S(1)}, bf16[1,256,256]{2,1,0:T(8,128)(2,1)S(1)}, u32[]{:S(2)}, u32[]{:S(2)}) collective-permute-start(bf16[1,256,256]{2,1,0:T(8,128)(2,1)S(1)} %get-tuple-element.40), channel_id=1, source_target_pairs={{0,12},{4,8},{8,4},{12,0},{16,28},{20,24},{24,20},{28,16},{1,13},{... | collective-permute-start | bytes 393224 | tf_op jit(solution)/shard_map/ppermute | solution.py:18
  70.6 2.2 %collective-permute-start.11 = (bf16[1,256,256]{2,1,0:T(8,128)(2,1)S(1)}, bf16[1,256,256]{2,1,0:T(8,128)(2,1)S(1)}, u32[]{:S(2)}, u32[]{:S(2)}) collective-permute-start(bf16[1,256,256]{2,1,0:T(8,128)(2,1)S(1)} %get-tuple-element.35.refs_12_), channel_id=1, source_target_pairs={{0,4},{4,0},{8,12},{12,8},{16,20},{20,16},{24,28},{28,24},{1,5},{5... | collective-permute-start | bytes 393224 | tf_op jit(solution)/shard_map/ppermute | solution.py:18
  72.8 1.3 %collective-permute-done.16.refs_11_ = bf16[1,256,256]{2,1,0:T(8,128)(2,1)S(1)} collective-permute-done((bf16[1,256,256]{2,1,0:T(8,128)(2,1)S(1)}, bf16[1,256,256]{2,1,0:T(8,128)(2,1)S(1)}, u32[]{:S(2)}, u32[]{:S(2)}) %collective-permute-start.16) | collective-permute-done | bytes 131104 | tf_op jit(solution)/shard_map/ppermute | solution.py:18
  74.1 1.7 %collective-permute-start.13 = (bf16[1,256,256]{2,1,0:T(8,128)(2,1)S(1)}, bf16[1,256,256]{2,1,0:T(8,128)(2,1)S(1)}, u32[]{:S(2)}, u32[]{:S(2)}) collective-permute-start(bf16[1,256,256]{2,1,0:T(8,128)(2,1)S(1)} %get-tuple-element.37), channel_id=1, source_target_pairs={{0,12},{4,8},{8,4},{12,0},{16,28},{20,24},{24,20},{28,16},{1,13},{... | collective-permute-start | bytes 393224 | tf_op jit(solution)/shard_map/ppermute | solution.py:18
  75.8 2.4 %shard_map.68 = (bf16[2,256,256]{2,1,0:T(8,128)(2,1)S(1)}, bf16[1,256,256]{2,1,0:T(8,128)(2,1)S(1)}, bf16[1,256,256]{2,1,0:T(8,128)(2,1)S(1)}, bf16[1,256,256]{2,1,0:T(8,128)(2,1)S(1)}) custom-call(s32[2,8,8]{2,1,0:T(8,128)S(1)} %copy-done.6, s32[2,2,8]{2,1,0:T(2,128)S(1)} %copy-done.7, s32[2,2]{1,0:T(2,128)S(1)} %copy-done.8, ...), custom_call_target="tpu_custom_call" | custom-call | flops 603979776 | bytes 6422528 | tf_op jit(solution)/shard_map/pallas_call | solution.py:41
  78.3 3.7 %collective-permute-start.17 = (bf16[2,256,256]{2,1,0:T(8,128)(2,1)S(1)}, bf16[2,256,256]{2,1,0:T(8,128)(2,1)S(1)}, u32[]{:S(2)}, u32[]{:S(2)}) collective-permute-start(bf16[2,256,256]{2,1,0:T(8,128)(2,1)S(1)} %get-tuple-element.41.refs_12_.refs_22_), channel_id=1, source_target_pairs={{0,16},{4,20},{8,24},{12,28},{16,0},{20,4},{24,8},{28,12},{1,17},{... | collective-permute-start | bytes 786440 | tf_op jit(solution)/shard_map/ppermute | solution.py:18
  82.0 1.2 %collective-permute-start.18 = (bf16[1,256,256]{2,1,0:T(8,128)(2,1)S(1)}, bf16[1,256,256]{2,1,0:T(8,128)(2,1)S(1)}, u32[]{:S(2)}, u32[]{:S(2)}) collective-permute-start(bf16[1,256,256]{2,1,0:T(8,128)(2,1)S(1)} %get-tuple-element.42), channel_id=1, source_target_pairs={{0,4},{4,0},{8,12},{12,8},{16,20},{20,16},{24,28},{28,24},{1,5},{5... | collective-permute-start | bytes 393224 | tf_op jit(solution)/shard_map/ppermute | solution.py:18
  83.3 2.2 %collective-permute-start.20 = (bf16[1,256,256]{2,1,0:T(8,128)(2,1)S(1)}, bf16[1,256,256]{2,1,0:T(8,128)(2,1)S(1)}, u32[]{:S(2)}, u32[]{:S(2)}) collective-permute-start(bf16[1,256,256]{2,1,0:T(8,128)(2,1)S(1)} %get-tuple-element.44), channel_id=1, source_target_pairs={{0,12},{4,8},{8,4},{12,0},{16,28},{20,24},{24,20},{28,16},{1,13},{... | collective-permute-start | bytes 393224 | tf_op jit(solution)/shard_map/ppermute | solution.py:18
  85.5 2.4 %shard_map.67.refs_0_.refs_12_.refs_23_ = bf16[2,256,256]{2,1,0:T(8,128)(2,1)S(1)} custom-call(s32[2,8,8]{2,1,0:T(8,128)S(1)} %copy-done.6, s32[2,2,8]{2,1,0:T(2,128)S(1)} %copy-done.7, s32[2,2]{1,0:T(2,128)S(1)} %copy-done.8, bf16[3,2,256,512]{3,2,1,0:T(8,128)(2,1)S(1)} %copy-done.1, bf16[1152,256]{1,0:T(8,128)(2,1)S(1)} %get-tuple-element.29.refs_2_.refs_0_, ...), custom_call_target="tpu_custom_call" | custom-call | flops 603979776 | bytes 8257536 | tf_op jit(solution)/shard_map/pallas_call | solution.py:41
  87.9 3.4 %collective-permute-start.24 = (bf16[2,256,256]{2,1,0:T(8,128)(2,1)S(1)}, bf16[2,256,256]{2,1,0:T(8,128)(2,1)S(1)}, u32[]{:S(2)}, u32[]{:S(2)}) collective-permute-start(bf16[2,256,256]{2,1,0:T(8,128)(2,1)S(1)} %shard_map.67.refs_0_.refs_12_.refs_23_), channel_id=1, source_target_pairs={{0,16},{4,20},{8,24},{12,28},{16,0},{20,4},{24,8},{28,12},{1,17},{... | collective-permute-start | bytes 786440 | tf_op jit(solution)/shard_map/ppermute | solution.py:18
  91.6 2.3 %collective-permute-done.20.refs_3_.refs_15_ = bf16[1,256,256]{2,1,0:T(8,128)(2,1)S(1)} collective-permute-done((bf16[1,256,256]{2,1,0:T(8,128)(2,1)S(1)}, bf16[1,256,256]{2,1,0:T(8,128)(2,1)S(1)}, u32[]{:S(2)}, u32[]{:S(2)}) %collective-permute-start.20) | collective-permute-done | bytes 131104 | tf_op jit(solution)/shard_map/ppermute | solution.py:18
  94.0 5.1 %collective-permute-done.17.far.refs_16_ = bf16[2,256,256]{2,1,0:T(8,128)(2,1)S(1)} collective-permute-done((bf16[2,256,256]{2,1,0:T(8,128)(2,1)S(1)}, bf16[2,256,256]{2,1,0:T(8,128)(2,1)S(1)}, u32[]{:S(2)}, u32[]{:S(2)}) %collective-permute-start.17) | collective-permute-done | bytes 262176 | tf_op jit(solution)/shard_map/ppermute | solution.py:18
  100.3 3.0 %collective-permute-start.23 = (bf16[2,256,256]{2,1,0:T(8,128)(2,1)S(1)}, bf16[2,256,256]{2,1,0:T(8,128)(2,1)S(1)}, u32[]{:S(2)}, u32[]{:S(2)}) collective-permute-start(bf16[2,256,256]{2,1,0:T(8,128)(2,1)S(1)} %get-tuple-element.47), channel_id=1, source_target_pairs={{0,12},{4,8},{8,4},{12,0},{16,28},{20,24},{24,20},{28,16},{1,13},{... | collective-permute-start | bytes 786440 | tf_op jit(solution)/shard_map/ppermute | solution.py:18
  105.1 4.2 %collective-permute-done.21.refs_17_.refs_13_ = bf16[2,256,256]{2,1,0:T(8,128)(2,1)S(1)} collective-permute-done((bf16[2,256,256]{2,1,0:T(8,128)(2,1)S(1)}, bf16[2,256,256]{2,1,0:T(8,128)(2,1)S(1)}, u32[]{:S(2)}, u32[]{:S(2)}) %collective-permute-start.21) | collective-permute-done | bytes 262176 | tf_op jit(solution)/shard_map/ppermute | solution.py:18
  109.6 6.5 %collective-permute-done.23.refs_19_.refs_15_ = bf16[2,256,256]{2,1,0:T(8,128)(2,1)S(1)} collective-permute-done((bf16[2,256,256]{2,1,0:T(8,128)(2,1)S(1)}, bf16[2,256,256]{2,1,0:T(8,128)(2,1)S(1)}, u32[]{:S(2)}, u32[]{:S(2)}) %collective-permute-start.23) | collective-permute-done | bytes 262176 | tf_op jit(solution)/shard_map/ppermute | solution.py:18
  116.1 2.5 %shard_map.71.refs_24_ = bf16[2,256,256]{2,1,0:T(8,128)(2,1)S(1)} custom-call(s32[2,8,8]{2,1,0:T(8,128)S(1)} %copy-done.6, s32[2,2,8]{2,1,0:T(2,128)S(1)} %copy-done.7, s32[2,2]{1,0:T(2,128)S(1)} %copy-done.8, bf16[3,2,256,512]{3,2,1,0:T(8,128)(2,1)S(1)} %copy-done.1, bf16[1152,256]{1,0:T(8,128)(2,1)S(1)} %get-tuple-element.30.refs_12_.refs_0_, ...), custom_call_target="tpu_custom_call" | custom-call | flops 603979776 | bytes 7733248 | tf_op jit(solution)/shard_map/pallas_call | solution.py:41
  118.9 3.2 %shard_map.72 = bf16[3,2,256,512]{3,2,1,0:T(8,128)(2,1)} custom-call(s32[2,8,8]{2,1,0:T(8,128)S(1)} %copy-done.6, s32[2,2,8]{2,1,0:T(2,128)S(1)} %copy-done.7, s32[2,2]{1,0:T(2,128)S(1)} %copy-done.8, bf16[3,2,256,512]{3,2,1,0:T(8,128)(2,1)S(1)} %copy-done.1, bf16[1152,256]{1,0:T(8,128)(2,1)S(1)} %get-tuple-element.30.refs_12_.refs_0_, ...), custom_call_target="tpu_custom_call" | custom-call | flops 603979776 | bytes 10223616 | tf_op jit(solution)/shard_map/pallas_call | solution.py:41
  (53 shorter events, 8.6 us)
Async XLA Ops:
  12.3 32.0 %copy-start.5 = (bf16[3,2,64,256]{3,2,1,0:T(8,128)(2,1)S(1)}, bf16[3,2,64,256]{3,2,1,0:T(8,128)(2,1)}, u32[]{:S(2)}) copy-start(bf16[3,2,64,256]{3,2,1,0:T(8,128)(2,1)} %refs_0_.1) | copy-start | bytes 589828
  13.3 15.6 %collective-permute-start.2 = (bf16[1152,256]{1,0:T(8,128)(2,1)S(1)}, bf16[1152,256]{1,0:T(8,128)(2,1)S(1)}, u32[]{:S(2)}, u32[]{:S(2)}) collective-permute-start(bf16[1152,256]{1,0:T(8,128)(2,1)S(1)} %get-tuple-element.29.refs_2_.refs_0_), channel_id=1, source_target_pairs={{0,2},{1,3},{2,0},{3,1},{4,6},{5,7},{6,4},{7,5},{8,10},{9,11},{10,... | collective-permute-start | bytes 1769480 | tf_op jit(solution)/shard_map/ppermute | solution.py:18
  14.9 29.3 %collective-permute-start.1 = (bf16[1152,256]{1,0:T(8,128)(2,1)S(1)}, bf16[1152,256]{1,0:T(8,128)(2,1)S(1)}, u32[]{:S(2)}, u32[]{:S(2)}) collective-permute-start(bf16[1152,256]{1,0:T(8,128)(2,1)S(1)} %get-tuple-element.29.refs_2_.refs_0_), channel_id=1, source_target_pairs={{0,1},{1,0},{2,3},{3,2},{4,5},{5,4},{6,7},{7,6},{8,9},{9,8},{10,11... | collective-permute-start | bytes 1769480 | tf_op jit(solution)/shard_map/ppermute | solution.py:18
  29.0 15.3 %collective-permute-start.3 = (bf16[1152,256]{1,0:T(8,128)(2,1)S(1)}, bf16[1152,256]{1,0:T(8,128)(2,1)S(1)}, u32[]{:S(2)}, u32[]{:S(2)}) collective-permute-start(bf16[1152,256]{1,0:T(8,128)(2,1)S(1)} %collective-permute-done.2.refs_4_.refs_2_), channel_id=1, source_target_pairs={{0,1},{1,0},{2,3},{3,2},{4,5},{5,4},{6,7},{7,6},{8,9},{9,8},{10,11... | collective-permute-start | bytes 1769480 | tf_op jit(solution)/shard_map/ppermute | solution.py:18
  29.0 46.8 %copy-start.1 = (bf16[3,2,256,512]{3,2,1,0:T(8,128)(2,1)S(1)}, bf16[3,2,256,512]{3,2,1,0:T(8,128)(2,1)}, u32[]{:S(2)}) copy-start(bf16[3,2,256,512]{3,2,1,0:T(8,128)(2,1)} %noise.9) | copy-start | bytes 4718596
  29.0 46.8 %copy-start.7 = (s32[2,2,8]{2,1,0:T(2,128)S(1)}, s32[2,2,8]{2,1,0:T(2,128)}, u32[]{:S(2)}) copy-start(s32[2,2,8]{2,1,0:T(2,128)} %lists.7) | copy-start | bytes 388
  29.0 46.8 %copy-start.8 = (s32[2,2]{1,0:T(2,128)S(1)}, s32[2,2]{1,0:T(2,128)}, u32[]{:S(2)}) copy-start(s32[2,2]{1,0:T(2,128)} %counts.7) | copy-start | bytes 52
  29.0 15.2 %collective-permute-start = (bf16[2,256,256]{2,1,0:T(8,128)(2,1)S(1)}, bf16[2,256,256]{2,1,0:T(8,128)(2,1)S(1)}, u32[]{:S(2)}, u32[]{:S(2)}) collective-permute-start(bf16[2,256,256]{2,1,0:T(8,128)(2,1)S(1)} %get-tuple-element.28.refs_4_.refs_20_), channel_id=1, source_target_pairs={{0,16},{4,20},{8,24},{12,28},{16,0},{20,4},{24,8},{28,12},{1,17},{... | collective-permute-start | bytes 786440 | tf_op jit(solution)/shard_map/ppermute | solution.py:18
  45.0 14.9 %collective-permute-start.5 = (bf16[1152,256]{1,0:T(8,128)(2,1)S(1)}, bf16[1152,256]{1,0:T(8,128)(2,1)S(1)}, u32[]{:S(2)}, u32[]{:S(2)}) collective-permute-start(bf16[1152,256]{1,0:T(8,128)(2,1)S(1)} %get-tuple-element.30.refs_12_.refs_0_), channel_id=1, source_target_pairs={{0,2},{1,3},{2,0},{3,1},{4,6},{5,7},{6,4},{7,5},{8,10},{9,11},{10,... | collective-permute-start | bytes 1769480 | tf_op jit(solution)/shard_map/ppermute | solution.py:18
  46.6 8.3 %collective-permute-start.7 = (bf16[2,256,256]{2,1,0:T(8,128)(2,1)S(1)}, bf16[2,256,256]{2,1,0:T(8,128)(2,1)S(1)}, u32[]{:S(2)}, u32[]{:S(2)}) collective-permute-start(bf16[2,256,256]{2,1,0:T(8,128)(2,1)S(1)} %get-tuple-element.32), channel_id=1, source_target_pairs={{0,4},{4,0},{8,12},{12,8},{16,20},{20,16},{24,28},{28,24},{1,5},{5... | collective-permute-start | bytes 786440 | tf_op jit(solution)/shard_map/ppermute | solution.py:18
  48.1 14.9 %collective-permute-start.8 = (bf16[2,256,256]{2,1,0:T(8,128)(2,1)S(1)}, bf16[2,256,256]{2,1,0:T(8,128)(2,1)S(1)}, u32[]{:S(2)}, u32[]{:S(2)}) collective-permute-start(bf16[2,256,256]{2,1,0:T(8,128)(2,1)S(1)} %get-tuple-element.33), channel_id=1, source_target_pairs={{0,8},{4,12},{8,0},{12,4},{16,24},{20,28},{24,16},{28,20},{1,9},{5... | collective-permute-start | bytes 786440 | tf_op jit(solution)/shard_map/ppermute | solution.py:18
  48.8 34.5 %collective-permute-start.4 = (bf16[1152,256]{1,0:T(8,128)(2,1)S(1)}, bf16[1152,256]{1,0:T(8,128)(2,1)S(1)}, u32[]{:S(2)}, u32[]{:S(2)}) collective-permute-start(bf16[1152,256]{1,0:T(8,128)(2,1)S(1)} %get-tuple-element.30.refs_12_.refs_0_), channel_id=1, source_target_pairs={{0,1},{1,0},{2,3},{3,2},{4,5},{5,4},{6,7},{7,6},{8,9},{9,8},{10,11... | collective-permute-start | bytes 1769480 | tf_op jit(solution)/shard_map/ppermute | solution.py:18
  48.8 17.9 %collective-permute-start.9 = (bf16[2,256,256]{2,1,0:T(8,128)(2,1)S(1)}, bf16[2,256,256]{2,1,0:T(8,128)(2,1)S(1)}, u32[]{:S(2)}, u32[]{:S(2)}) collective-permute-start(bf16[2,256,256]{2,1,0:T(8,128)(2,1)S(1)} %get-tuple-element.34), channel_id=1, source_target_pairs={{0,12},{4,8},{8,4},{12,0},{16,28},{20,24},{24,20},{28,16},{1,13},{... | collective-permute-start | bytes 786440 | tf_op jit(solution)/shard_map/ppermute | solution.py:18
  54.9 11.7 %collective-permute-start.10 = (bf16[2,256,256]{2,1,0:T(8,128)(2,1)S(1)}, bf16[2,256,256]{2,1,0:T(8,128)(2,1)S(1)}, u32[]{:S(2)}, u32[]{:S(2)}) collective-permute-start(bf16[2,256,256]{2,1,0:T(8,128)(2,1)S(1)} %get-tuple-element.31.refs_4_.refs_21_), channel_id=1, source_target_pairs={{0,16},{4,20},{8,24},{12,28},{16,0},{20,4},{24,8},{28,12},{1,17},{... | collective-permute-start | bytes 786440 | tf_op jit(solution)/shard_map/ppermute | solution.py:18
  59.9 25.6 %collective-permute-start.6 = (bf16[1152,256]{1,0:T(8,128)(2,1)S(1)}, bf16[1152,256]{1,0:T(8,128)(2,1)S(1)}, u32[]{:S(2)}, u32[]{:S(2)}) collective-permute-start(bf16[1152,256]{1,0:T(8,128)(2,1)S(1)} %collective-permute-done.5.refs_14_.refs_2_), channel_id=1, source_target_pairs={{0,1},{1,0},{2,3},{3,2},{4,5},{5,4},{6,7},{7,6},{8,9},{9,8},{10,11... | collective-permute-start | bytes 1769480 | tf_op jit(solution)/shard_map/ppermute | solution.py:18
  63.0 7.6 %collective-permute-start.14 = (bf16[1,256,256]{2,1,0:T(8,128)(2,1)S(1)}, bf16[1,256,256]{2,1,0:T(8,128)(2,1)S(1)}, u32[]{:S(2)}, u32[]{:S(2)}) collective-permute-start(bf16[1,256,256]{2,1,0:T(8,128)(2,1)S(1)} %get-tuple-element.38), channel_id=1, source_target_pairs={{0,4},{4,0},{8,12},{12,8},{16,20},{20,16},{24,28},{28,24},{1,5},{5... | collective-permute-start | bytes 393224 | tf_op jit(solution)/shard_map/ppermute | solution.py:18
  66.7 6.2 %collective-permute-start.15 = (bf16[1,256,256]{2,1,0:T(8,128)(2,1)S(1)}, bf16[1,256,256]{2,1,0:T(8,128)(2,1)S(1)}, u32[]{:S(2)}, u32[]{:S(2)}) collective-permute-start(bf16[1,256,256]{2,1,0:T(8,128)(2,1)S(1)} %get-tuple-element.39), channel_id=1, source_target_pairs={{0,8},{4,12},{8,0},{12,4},{16,24},{20,28},{24,16},{28,20},{1,9},{5... | collective-permute-start | bytes 393224 | tf_op jit(solution)/shard_map/ppermute | solution.py:18
  66.7 7.4 %collective-permute-start.16 = (bf16[1,256,256]{2,1,0:T(8,128)(2,1)S(1)}, bf16[1,256,256]{2,1,0:T(8,128)(2,1)S(1)}, u32[]{:S(2)}, u32[]{:S(2)}) collective-permute-start(bf16[1,256,256]{2,1,0:T(8,128)(2,1)S(1)} %get-tuple-element.40), channel_id=1, source_target_pairs={{0,12},{4,8},{8,4},{12,0},{16,28},{20,24},{24,20},{28,16},{1,13},{... | collective-permute-start | bytes 393224 | tf_op jit(solution)/shard_map/ppermute | solution.py:18
  70.6 7.6 %collective-permute-start.11 = (bf16[1,256,256]{2,1,0:T(8,128)(2,1)S(1)}, bf16[1,256,256]{2,1,0:T(8,128)(2,1)S(1)}, u32[]{:S(2)}, u32[]{:S(2)}) collective-permute-start(bf16[1,256,256]{2,1,0:T(8,128)(2,1)S(1)} %get-tuple-element.35.refs_12_), channel_id=1, source_target_pairs={{0,4},{4,0},{8,12},{12,8},{16,20},{20,16},{24,28},{28,24},{1,5},{5... | collective-permute-start | bytes 393224 | tf_op jit(solution)/shard_map/ppermute | solution.py:18
  72.8 9.2 %collective-permute-start.12 = (bf16[1,256,256]{2,1,0:T(8,128)(2,1)S(1)}, bf16[1,256,256]{2,1,0:T(8,128)(2,1)S(1)}, u32[]{:S(2)}, u32[]{:S(2)}) collective-permute-start(bf16[1,256,256]{2,1,0:T(8,128)(2,1)S(1)} %get-tuple-element.36), channel_id=1, source_target_pairs={{0,8},{4,12},{8,0},{12,4},{16,24},{20,28},{24,16},{28,20},{1,9},{5... | collective-permute-start | bytes 393224 | tf_op jit(solution)/shard_map/ppermute | solution.py:18
  74.1 9.1 %collective-permute-start.13 = (bf16[1,256,256]{2,1,0:T(8,128)(2,1)S(1)}, bf16[1,256,256]{2,1,0:T(8,128)(2,1)S(1)}, u32[]{:S(2)}, u32[]{:S(2)}) collective-permute-start(bf16[1,256,256]{2,1,0:T(8,128)(2,1)S(1)} %get-tuple-element.37), channel_id=1, source_target_pairs={{0,12},{4,8},{8,4},{12,0},{16,28},{20,24},{24,20},{28,16},{1,13},{... | collective-permute-start | bytes 393224 | tf_op jit(solution)/shard_map/ppermute | solution.py:18
  78.3 20.8 %collective-permute-start.17 = (bf16[2,256,256]{2,1,0:T(8,128)(2,1)S(1)}, bf16[2,256,256]{2,1,0:T(8,128)(2,1)S(1)}, u32[]{:S(2)}, u32[]{:S(2)}) collective-permute-start(bf16[2,256,256]{2,1,0:T(8,128)(2,1)S(1)} %get-tuple-element.41.refs_12_.refs_22_), channel_id=1, source_target_pairs={{0,16},{4,20},{8,24},{12,28},{16,0},{20,4},{24,8},{28,12},{1,17},{... | collective-permute-start | bytes 786440 | tf_op jit(solution)/shard_map/ppermute | solution.py:18
  82.0 9.2 %collective-permute-start.18 = (bf16[1,256,256]{2,1,0:T(8,128)(2,1)S(1)}, bf16[1,256,256]{2,1,0:T(8,128)(2,1)S(1)}, u32[]{:S(2)}, u32[]{:S(2)}) collective-permute-start(bf16[1,256,256]{2,1,0:T(8,128)(2,1)S(1)} %get-tuple-element.42), channel_id=1, source_target_pairs={{0,4},{4,0},{8,12},{12,8},{16,20},{20,16},{24,28},{28,24},{1,5},{5... | collective-permute-start | bytes 393224 | tf_op jit(solution)/shard_map/ppermute | solution.py:18
  83.2 8.4 %collective-permute-start.19 = (bf16[1,256,256]{2,1,0:T(8,128)(2,1)S(1)}, bf16[1,256,256]{2,1,0:T(8,128)(2,1)S(1)}, u32[]{:S(2)}, u32[]{:S(2)}) collective-permute-start(bf16[1,256,256]{2,1,0:T(8,128)(2,1)S(1)} %get-tuple-element.43), channel_id=1, source_target_pairs={{0,8},{4,12},{8,0},{12,4},{16,24},{20,28},{24,16},{28,20},{1,9},{5... | collective-permute-start | bytes 393224 | tf_op jit(solution)/shard_map/ppermute | solution.py:18
  83.3 10.7 %collective-permute-start.20 = (bf16[1,256,256]{2,1,0:T(8,128)(2,1)S(1)}, bf16[1,256,256]{2,1,0:T(8,128)(2,1)S(1)}, u32[]{:S(2)}, u32[]{:S(2)}) collective-permute-start(bf16[1,256,256]{2,1,0:T(8,128)(2,1)S(1)} %get-tuple-element.44), channel_id=1, source_target_pairs={{0,12},{4,8},{8,4},{12,0},{16,28},{20,24},{24,20},{28,16},{1,13},{... | collective-permute-start | bytes 393224 | tf_op jit(solution)/shard_map/ppermute | solution.py:18
  87.9 15.9 %collective-permute-start.24 = (bf16[2,256,256]{2,1,0:T(8,128)(2,1)S(1)}, bf16[2,256,256]{2,1,0:T(8,128)(2,1)S(1)}, u32[]{:S(2)}, u32[]{:S(2)}) collective-permute-start(bf16[2,256,256]{2,1,0:T(8,128)(2,1)S(1)} %shard_map.67.refs_0_.refs_12_.refs_23_), channel_id=1, source_target_pairs={{0,16},{4,20},{8,24},{12,28},{16,0},{20,4},{24,8},{28,12},{1,17},{... | collective-permute-start | bytes 786440 | tf_op jit(solution)/shard_map/ppermute | solution.py:18
  99.8 9.5 %collective-permute-start.21 = (bf16[2,256,256]{2,1,0:T(8,128)(2,1)S(1)}, bf16[2,256,256]{2,1,0:T(8,128)(2,1)S(1)}, u32[]{:S(2)}, u32[]{:S(2)}) collective-permute-start(bf16[2,256,256]{2,1,0:T(8,128)(2,1)S(1)} %get-tuple-element.45), channel_id=1, source_target_pairs={{0,4},{4,0},{8,12},{12,8},{16,20},{20,16},{24,28},{28,24},{1,5},{5... | collective-permute-start | bytes 786440 | tf_op jit(solution)/shard_map/ppermute | solution.py:18
  100.3 9.2 %collective-permute-start.22 = (bf16[2,256,256]{2,1,0:T(8,128)(2,1)S(1)}, bf16[2,256,256]{2,1,0:T(8,128)(2,1)S(1)}, u32[]{:S(2)}, u32[]{:S(2)}) collective-permute-start(bf16[2,256,256]{2,1,0:T(8,128)(2,1)S(1)} %get-tuple-element.46), channel_id=1, source_target_pairs={{0,8},{4,12},{8,0},{12,4},{16,24},{20,28},{24,16},{28,20},{1,9},{5... | collective-permute-start | bytes 786440 | tf_op jit(solution)/shard_map/ppermute | solution.py:18
  100.3 15.7 %collective-permute-start.23 = (bf16[2,256,256]{2,1,0:T(8,128)(2,1)S(1)}, bf16[2,256,256]{2,1,0:T(8,128)(2,1)S(1)}, u32[]{:S(2)}, u32[]{:S(2)}) collective-permute-start(bf16[2,256,256]{2,1,0:T(8,128)(2,1)S(1)} %get-tuple-element.47), channel_id=1, source_target_pairs={{0,12},{4,8},{8,4},{12,0},{16,28},{20,24},{24,20},{28,16},{1,13},{... | collective-permute-start | bytes 786440 | tf_op jit(solution)/shard_map/ppermute | solution.py:18
  104.5 14.1 %collective-permute-start.25 = (bf16[1,256,256]{2,1,0:T(8,128)(2,1)S(1)}, bf16[1,256,256]{2,1,0:T(8,128)(2,1)S(1)}, u32[]{:S(2)}, u32[]{:S(2)}) collective-permute-start(bf16[1,256,256]{2,1,0:T(8,128)(2,1)S(1)} %get-tuple-element.48.refs_20_), channel_id=1, source_target_pairs={{0,4},{4,0},{8,12},{12,8},{16,20},{20,16},{24,28},{28,24},{1,5},{5... | collective-permute-start | bytes 393224 | tf_op jit(solution)/shard_map/ppermute | solution.py:18
  105.1 13.5 %collective-permute-start.26 = (bf16[1,256,256]{2,1,0:T(8,128)(2,1)S(1)}, bf16[1,256,256]{2,1,0:T(8,128)(2,1)S(1)}, u32[]{:S(2)}, u32[]{:S(2)}) collective-permute-start(bf16[1,256,256]{2,1,0:T(8,128)(2,1)S(1)} %get-tuple-element.49), channel_id=1, source_target_pairs={{0,8},{4,12},{8,0},{12,4},{16,24},{20,28},{24,16},{28,20},{1,9},{5... | collective-permute-start | bytes 393224 | tf_op jit(solution)/shard_map/ppermute | solution.py:18
  109.3 9.6 %collective-permute-start.27 = (bf16[1,256,256]{2,1,0:T(8,128)(2,1)S(1)}, bf16[1,256,256]{2,1,0:T(8,128)(2,1)S(1)}, u32[]{:S(2)}, u32[]{:S(2)}) collective-permute-start(bf16[1,256,256]{2,1,0:T(8,128)(2,1)S(1)} %get-tuple-element.50), channel_id=1, source_target_pairs={{0,12},{4,8},{8,4},{12,0},{16,28},{20,24},{24,20},{28,16},{1,13},{... | collective-permute-start | bytes 393224 | tf_op jit(solution)/shard_map/ppermute | solution.py:18
  (5 other events, 36.2 us)

commit v7 on v6

--- a/solution.py
+++ b/solution.py
@@ -60,14 +60,15 @@
         target[at:at + rows, :] = inverse[level, node]
 
 
-def first_kernel(chunks, picks, noise, inverse, coupling, gathered, *refs):
-    pack, *refs, inv = refs
+def first_kernel(chunks, draws, picks, noise, *refs):
+    *refs, inv = refs
+    parts, refs = take(refs, draws)
     solved, sends = take(refs, chunks)
-    myself = lax.axis_index("leaf")
-    draws, nodes, rows = gathered.shape[:3]
+    myself, draw = lax.axis_index("leaf"), lax.axis_index("draw")
+    nodes, rows = parts[0].shape[:2]
     wide = solved[0].shape[-1]
-    for part in range(draws):
-        inv[:, part * rows:(part + 1) * rows, :] = gathered[part]
+    for step, part in enumerate(parts):
+        inv[:, pl.ds(pl.multiple_of((draw ^ step) * rows, rows), rows), :] = part[...]
     for at, target in enumerate(solved):
         for node in range(nodes):
             right = noise[0, node, :, at * wide:(at + 1) * wide]
@@ -76,7 +77,6 @@
         node = picks[0, myself ^ step, myself]
         for at, target in enumerate(solved):
             send[at] = target[node]
-    write_pack(pack, 1, inverse, coupling)
 
 
 def relay_kernel(owners, source, follow, pack_level, waits, picks, far, *refs):
@@ -166,23 +166,23 @@
     inv_here = pltpu.VMEM((nodes, rows, rows), BF16)
     dot_flops = 2 * rows * rows * wide
 
-    pack, *refs = call(
-        functools.partial(first_kernel, CHUNKS),
-        [pack_shape] + [part] * CHUNKS + [shape(CHUNKS, rows, wide)] * (half - 1),
+    refs = call(
+        functools.partial(first_kernel, CHUNKS, draws),
+        [part] * CHUNKS + [shape(CHUNKS, rows, wide)] * (half - 1),
         [inv_here],
         (picks,),
-        (noise, inverse, coupling, lax.all_gather(inverse[0], "draw", axis=0)),
+        (noise, *gather(inverse[0])),
         flops=nodes * CHUNKS * dot_flops,
     )
     solved, sends = take(refs, CHUNKS)
-    packs = [gather(pack)]
+    packs = [gather(jnp.concatenate([coupling[0].reshape(-1, rows), inverse[1].reshape(-1, rows)]))]
     done, pieces = [solved], []
     for level in range(1, levels):
         source = level - 1
         far = [leaf(value, half) for value in solved]
         got = near(sends)
         close = [[(ref, at) for ref in got] for at in chunks] if source == 0 else [[(ref, 0) for ref in got]]
-        distant, waits = [], packs[source] if source == 0 else got
+        distant, waits = [], packs[source] + got if source == 0 else got
         for at in chunks:
             follow = source > 0 and at < CHUNKS - 1
             pack_level = source + 2 if at == 0 and source + 2 < levels else 0

time: 122 us -> 118 us (0.967)
  blocking collectives: 7.18 us -> 0 us
  starting transfers between devices: 31.3 us -> 37.6 us
  local copies, waits for them, and re-layouts: 5.12 us -> 1.11 us
    all_gather x1 -> x0, blocking collectives: 7.18 us -> none  [on_device(): lax.all_gather(inverse[0], 'draw', axis=0)]
    ppermute x28 -> x31, starting transfers between devices: 31.3 us -> 37.6 us  [hop(): return lax.ppermute(value, axis, [(at, at ^ step) for at in range(size)])]
    unnamed x18 -> x12, local copies, waits for them, and re-layouts: 4.27 us -> 0.03 us
    ppermute x28 -> x31, waiting for transfers between devices: 63.9 us -> 64.9 us  [hop(): return lax.ppermute(value, axis, [(at, at ^ step) for at in range(size)])]
  transfers between devices with their start and end apart: 28 -> 31, of which waited for: 15 -> 15; matrix products, arithmetic and copies ran while one was open for 0% -> 0% of each run, Pallas kernels for 8% -> 9%
where the time goes in v7:
time: 118 us
  waiting for transfers between devices  64.9 us (55%)
  starting transfers between devices  37.6 us (32%)
  Pallas kernels  14.4 us (12%)
    ppermute x31, waiting for transfers between devices, hop(): return lax.ppermute(value, axis, [(at, at ^ step) for at in range(size)])  64.9 us
    ppermute x31, starting transfers between devices, hop(): return lax.ppermute(value, axis, [(at, at ^ step) for at in range(size)])  37.6 us
    pallas_call x9, Pallas kernels, call(): pl.pallas_call(kernel, out_shape=outs, in_specs=[SMEM] * len(small) + [VM...  14.4 us
  transfers between devices with their start and end apart: 31, of which 15 were waited for; matrix products, arithmetic and copies ran while one was open for 0% of the time, Pallas kernels for 9%

profile of v7, /device:TPU:0, one launch (start us, length us, event | category | flops | bytes accessed | tf_op | source)
XLA Modules:
  0.0 118.2 jit_solution(5612788228747341228)
XLA Ops:
  0.0 0.9 fusion
  1.2 3.0 %collective-permute-start.5 = (bf16[1152,256]{1,0:T(8,128)(2,1)S(1)}, bf16[1152,256]{1,0:T(8,128)(2,1)S(1)}, u32[]{:S(2)}, u32[]{:S(2)}) collective-permute-start(bf16[1152,256]{1,0:T(8,128)(2,1)S(1)} %pad_maximum_fusion.refs_2_.refs_0_), channel_id=1, source_target_pairs={{0,2},{1,3},{2,0},{3,1},{4,6},{5,7},{6,4},{7,5},{8,10},{9,11},{10,... | collective-permute-start | bytes 1769480 | tf_op jit(solution)/shard_map/ppermute | solution.py:18
  4.3 14.7 %collective-permute-done.1.refs_2_ = bf16[2,64,256]{2,1,0:T(8,128)(2,1)S(1)} collective-permute-done((bf16[2,64,256]{2,1,0:T(8,128)(2,1)S(1)}, bf16[2,64,256]{2,1,0:T(8,128)(2,1)S(1)}, u32[]{:S(2)}, u32[]{:S(2)}) %collective-permute-start.1) | collective-permute-done | bytes 65568 | tf_op jit(solution)/shard_map/ppermute | solution.py:18
  20.2 1.1 shard_map.64
  21.2 2.9 %collective-permute-start.3 = (bf16[2,256,256]{2,1,0:T(8,128)(2,1)S(1)}, bf16[2,256,256]{2,1,0:T(8,128)(2,1)S(1)}, u32[]{:S(2)}, u32[]{:S(2)}) collective-permute-start(bf16[2,256,256]{2,1,0:T(8,128)(2,1)S(1)} %get-tuple-element.27.refs_4_.refs_20_), channel_id=1, source_target_pairs={{0,16},{4,20},{8,24},{12,28},{16,0},{20,4},{24,8},{28,12},{1,17},{... | collective-permute-start | bytes 786440 | tf_op jit(solution)/shard_map/ppermute | solution.py:18
  24.1 1.5 %collective-permute-start.7 = (bf16[2,256,256]{2,1,0:T(8,128)(2,1)S(1)}, bf16[2,256,256]{2,1,0:T(8,128)(2,1)S(1)}, u32[]{:S(2)}, u32[]{:S(2)}) collective-permute-start(bf16[2,256,256]{2,1,0:T(8,128)(2,1)S(1)} %get-tuple-element.28), channel_id=1, source_target_pairs={{0,4},{4,0},{8,12},{12,8},{16,20},{20,16},{24,28},{28,24},{1,5},{5... | collective-permute-start | bytes 786440 | tf_op jit(solution)/shard_map/ppermute | solution.py:18
  25.7 1.6 %collective-permute-start.8 = (bf16[2,256,256]{2,1,0:T(8,128)(2,1)S(1)}, bf16[2,256,256]{2,1,0:T(8,128)(2,1)S(1)}, u32[]{:S(2)}, u32[]{:S(2)}) collective-permute-start(bf16[2,256,256]{2,1,0:T(8,128)(2,1)S(1)} %get-tuple-element.29), channel_id=1, source_target_pairs={{0,8},{4,12},{8,0},{12,4},{16,24},{20,28},{24,16},{28,20},{1,9},{5... | collective-permute-start | bytes 786440 | tf_op jit(solution)/shard_map/ppermute | solution.py:18
  27.2 9.3 %collective-permute-done.3.far.refs_8_ = bf16[2,256,256]{2,1,0:T(8,128)(2,1)S(1)} collective-permute-done((bf16[2,256,256]{2,1,0:T(8,128)(2,1)S(1)}, bf16[2,256,256]{2,1,0:T(8,128)(2,1)S(1)}, u32[]{:S(2)}, u32[]{:S(2)}) %collective-permute-start.3) | collective-permute-done | bytes 262176 | tf_op jit(solution)/shard_map/ppermute | solution.py:18
  36.5 1.6 %collective-permute-start.9 = (bf16[2,256,256]{2,1,0:T(8,128)(2,1)S(1)}, bf16[2,256,256]{2,1,0:T(8,128)(2,1)S(1)}, u32[]{:S(2)}, u32[]{:S(2)}) collective-permute-start(bf16[2,256,256]{2,1,0:T(8,128)(2,1)S(1)} %get-tuple-element.30), channel_id=1, source_target_pairs={{0,12},{4,8},{8,4},{12,0},{16,28},{20,24},{24,20},{28,16},{1,13},{... | collective-permute-start | bytes 786440 | tf_op jit(solution)/shard_map/ppermute | solution.py:18
  38.1 7.0 %collective-permute-done.9.refs_8_.refs_7_ = bf16[2,256,256]{2,1,0:T(8,128)(2,1)S(1)} collective-permute-done((bf16[2,256,256]{2,1,0:T(8,128)(2,1)S(1)}, bf16[2,256,256]{2,1,0:T(8,128)(2,1)S(1)}, u32[]{:S(2)}, u32[]{:S(2)}) %collective-permute-start.9) | collective-permute-done | bytes 262176 | tf_op jit(solution)/shard_map/ppermute | solution.py:18
  45.9 1.4 %collective-permute-start.11 = (bf16[1152,256]{1,0:T(8,128)(2,1)S(1)}, bf16[1152,256]{1,0:T(8,128)(2,1)S(1)}, u32[]{:S(2)}, u32[]{:S(2)}) collective-permute-start(bf16[1152,256]{1,0:T(8,128)(2,1)S(1)} %get-tuple-element.31.refs_12_.refs_0_), channel_id=1, source_target_pairs={{0,2},{1,3},{2,0},{3,1},{4,6},{5,7},{6,4},{7,5},{8,10},{9,11},{10,... | collective-permute-start | bytes 1769480 | tf_op jit(solution)/shard_map/ppermute | solution.py:18
  47.3 3.0 %collective-permute-start.13 = (bf16[2,256,256]{2,1,0:T(8,128)(2,1)S(1)}, bf16[2,256,256]{2,1,0:T(8,128)(2,1)S(1)}, u32[]{:S(2)}, u32[]{:S(2)}) collective-permute-start(bf16[2,256,256]{2,1,0:T(8,128)(2,1)S(1)} %get-tuple-element.32.refs_4_.refs_21_), channel_id=1, source_target_pairs={{0,16},{4,20},{8,24},{12,28},{16,0},{20,4},{24,8},{28,12},{1,17},{... | collective-permute-start | bytes 786440 | tf_op jit(solution)/shard_map/ppermute | solution.py:18
  50.3 9.5 %collective-permute-done.11.refs_14_.refs_2_ = bf16[1152,256]{1,0:T(8,128)(2,1)S(1)} collective-permute-done((bf16[1152,256]{1,0:T(8,128)(2,1)S(1)}, bf16[1152,256]{1,0:T(8,128)(2,1)S(1)}, u32[]{:S(2)}, u32[]{:S(2)}) %collective-permute-start.11) | collective-permute-done | bytes 589856 | tf_op jit(solution)/shard_map/ppermute | solution.py:18
  59.7 1.1 collective-permute-start.17
  60.9 2.2 %collective-permute-start.18 = (bf16[1,256,256]{2,1,0:T(8,128)(2,1)S(1)}, bf16[1,256,256]{2,1,0:T(8,128)(2,1)S(1)}, u32[]{:S(2)}, u32[]{:S(2)}) collective-permute-start(bf16[1,256,256]{2,1,0:T(8,128)(2,1)S(1)} %get-tuple-element.37), channel_id=1, source_target_pairs={{0,8},{4,12},{8,0},{12,4},{16,24},{20,28},{24,16},{28,20},{1,9},{5... | collective-permute-start | bytes 393224 | tf_op jit(solution)/shard_map/ppermute | solution.py:18
  64.3 1.3 %collective-permute-done.17.refs_9_ = bf16[1,256,256]{2,1,0:T(8,128)(2,1)S(1)} collective-permute-done((bf16[1,256,256]{2,1,0:T(8,128)(2,1)S(1)}, bf16[1,256,256]{2,1,0:T(8,128)(2,1)S(1)}, u32[]{:S(2)}, u32[]{:S(2)}) %collective-permute-start.17) | collective-permute-done | bytes 131104 | tf_op jit(solution)/shard_map/ppermute | solution.py:18
  65.7 1.1 collective-permute-start.14
  67.3 2.1 %collective-permute-start.15 = (bf16[1,256,256]{2,1,0:T(8,128)(2,1)S(1)}, bf16[1,256,256]{2,1,0:T(8,128)(2,1)S(1)}, u32[]{:S(2)}, u32[]{:S(2)}) collective-permute-start(bf16[1,256,256]{2,1,0:T(8,128)(2,1)S(1)} %get-tuple-element.34), channel_id=1, source_target_pairs={{0,8},{4,12},{8,0},{12,4},{16,24},{20,28},{24,16},{28,20},{1,9},{5... | collective-permute-start | bytes 393224 | tf_op jit(solution)/shard_map/ppermute | solution.py:18
  70.1 2.7 %collective-permute-start.16 = (bf16[1,256,256]{2,1,0:T(8,128)(2,1)S(1)}, bf16[1,256,256]{2,1,0:T(8,128)(2,1)S(1)}, u32[]{:S(2)}, u32[]{:S(2)}) collective-permute-start(bf16[1,256,256]{2,1,0:T(8,128)(2,1)S(1)} %get-tuple-element.35), channel_id=1, source_target_pairs={{0,12},{4,8},{8,4},{12,0},{16,28},{20,24},{24,20},{28,16},{1,13},{... | collective-permute-start | bytes 393224 | tf_op jit(solution)/shard_map/ppermute | solution.py:18
  72.8 2.4 %shard_map.68 = (bf16[2,256,256]{2,1,0:T(8,128)(2,1)S(1)}, bf16[1,256,256]{2,1,0:T(8,128)(2,1)S(1)}, bf16[1,256,256]{2,1,0:T(8,128)(2,1)S(1)}, bf16[1,256,256]{2,1,0:T(8,128)(2,1)S(1)}) custom-call(s32[2,8,8]{2,1,0:T(8,128)S(1)} %copy-done.2, s32[2,2,8]{2,1,0:T(2,128)S(1)} %copy-done.4, s32[2,2]{1,0:T(2,128)S(1)} %copy-done.5, ...), custom_call_target="tpu_custom_call" | custom-call | flops 603979776 | bytes 6422528 | tf_op jit(solution)/shard_map/pallas_call | solution.py:41
  75.2 3.5 %collective-permute-start.20 = (bf16[2,256,256]{2,1,0:T(8,128)(2,1)S(1)}, bf16[2,256,256]{2,1,0:T(8,128)(2,1)S(1)}, u32[]{:S(2)}, u32[]{:S(2)}) collective-permute-start(bf16[2,256,256]{2,1,0:T(8,128)(2,1)S(1)} %get-tuple-element.39.refs_12_.refs_22_), channel_id=1, source_target_pairs={{0,16},{4,20},{8,24},{12,28},{16,0},{20,4},{24,8},{28,12},{1,17},{... | collective-permute-start | bytes 786440 | tf_op jit(solution)/shard_map/ppermute | solution.py:18
  79.9 2.3 %collective-permute-start.23 = (bf16[1,256,256]{2,1,0:T(8,128)(2,1)S(1)}, bf16[1,256,256]{2,1,0:T(8,128)(2,1)S(1)}, u32[]{:S(2)}, u32[]{:S(2)}) collective-permute-start(bf16[1,256,256]{2,1,0:T(8,128)(2,1)S(1)} %get-tuple-element.42), channel_id=1, source_target_pairs={{0,12},{4,8},{8,4},{12,0},{16,28},{20,24},{24,20},{28,16},{1,13},{... | collective-permute-start | bytes 393224 | tf_op jit(solution)/shard_map/ppermute | solution.py:18
  82.2 2.4 %shard_map.67.refs_0_.refs_12_.refs_23_ = bf16[2,256,256]{2,1,0:T(8,128)(2,1)S(1)} custom-call(s32[2,8,8]{2,1,0:T(8,128)S(1)} %copy-done.2, s32[2,2,8]{2,1,0:T(2,128)S(1)} %copy-done.4, s32[2,2]{1,0:T(2,128)S(1)} %copy-done.5, bf16[3,2,256,512]{3,2,1,0:T(8,128)(2,1)S(1)} %copy-done, bf16[1152,256]{1,0:T(8,128)(2,1)S(1)} %pad_maximum_fusion.refs_2_.refs_0_, ...), custom_call_target="tpu_custom_call" | custom-call | flops 603979776 | bytes 8257536 | tf_op jit(solution)/shard_map/pallas_call | solution.py:41
  85.3 2.9 %collective-permute-done.22.refs_2_.refs_14_ = bf16[1,256,256]{2,1,0:T(8,128)(2,1)S(1)} collective-permute-done((bf16[1,256,256]{2,1,0:T(8,128)(2,1)S(1)}, bf16[1,256,256]{2,1,0:T(8,128)(2,1)S(1)}, u32[]{:S(2)}, u32[]{:S(2)}) %collective-permute-start.22) | collective-permute-done | bytes 131104 | tf_op jit(solution)/shard_map/ppermute | solution.py:18
  88.3 3.9 %collective-permute-done.23.refs_3_.refs_15_ = bf16[1,256,256]{2,1,0:T(8,128)(2,1)S(1)} collective-permute-done((bf16[1,256,256]{2,1,0:T(8,128)(2,1)S(1)}, bf16[1,256,256]{2,1,0:T(8,128)(2,1)S(1)}, u32[]{:S(2)}, u32[]{:S(2)}) %collective-permute-start.23) | collective-permute-done | bytes 131104 | tf_op jit(solution)/shard_map/ppermute | solution.py:18
  92.2 3.6 %collective-permute-done.20.far.refs_16_ = bf16[2,256,256]{2,1,0:T(8,128)(2,1)S(1)} collective-permute-done((bf16[2,256,256]{2,1,0:T(8,128)(2,1)S(1)}, bf16[2,256,256]{2,1,0:T(8,128)(2,1)S(1)}, u32[]{:S(2)}, u32[]{:S(2)}) %collective-permute-start.20) | collective-permute-done | bytes 262176 | tf_op jit(solution)/shard_map/ppermute | solution.py:18
  96.6 1.1 collective-permute-start.24
  97.7 2.4 %collective-permute-start.26 = (bf16[2,256,256]{2,1,0:T(8,128)(2,1)S(1)}, bf16[2,256,256]{2,1,0:T(8,128)(2,1)S(1)}, u32[]{:S(2)}, u32[]{:S(2)}) collective-permute-start(bf16[2,256,256]{2,1,0:T(8,128)(2,1)S(1)} %get-tuple-element.45), channel_id=1, source_target_pairs={{0,12},{4,8},{8,4},{12,0},{16,28},{20,24},{24,20},{28,16},{1,13},{... | collective-permute-start | bytes 786440 | tf_op jit(solution)/shard_map/ppermute | solution.py:18
  102.6 4.3 %collective-permute-done.24.refs_17_.refs_13_ = bf16[2,256,256]{2,1,0:T(8,128)(2,1)S(1)} collective-permute-done((bf16[2,256,256]{2,1,0:T(8,128)(2,1)S(1)}, bf16[2,256,256]{2,1,0:T(8,128)(2,1)S(1)}, u32[]{:S(2)}, u32[]{:S(2)}) %collective-permute-start.24) | collective-permute-done | bytes 262176 | tf_op jit(solution)/shard_map/ppermute | solution.py:18
  106.9 5.3 %collective-permute-done.26.refs_19_.refs_15_ = bf16[2,256,256]{2,1,0:T(8,128)(2,1)S(1)} collective-permute-done((bf16[2,256,256]{2,1,0:T(8,128)(2,1)S(1)}, bf16[2,256,256]{2,1,0:T(8,128)(2,1)S(1)}, u32[]{:S(2)}, u32[]{:S(2)}) %collective-permute-start.26) | collective-permute-done | bytes 262176 | tf_op jit(solution)/shard_map/ppermute | solution.py:18
  112.2 2.5 %shard_map.71.refs_24_ = bf16[2,256,256]{2,1,0:T(8,128)(2,1)S(1)} custom-call(s32[2,8,8]{2,1,0:T(8,128)S(1)} %copy-done.2, s32[2,2,8]{2,1,0:T(2,128)S(1)} %copy-done.4, s32[2,2]{1,0:T(2,128)S(1)} %copy-done.5, bf16[3,2,256,512]{3,2,1,0:T(8,128)(2,1)S(1)} %copy-done, bf16[1152,256]{1,0:T(8,128)(2,1)S(1)} %get-tuple-element.31.refs_12_.refs_0_, ...), custom_call_target="tpu_custom_call" | custom-call | flops 603979776 | bytes 7733248 | tf_op jit(solution)/shard_map/pallas_call | solution.py:41
  115.0 3.2 %shard_map.72 = bf16[3,2,256,512]{3,2,1,0:T(8,128)(2,1)} custom-call(s32[2,8,8]{2,1,0:T(8,128)S(1)} %copy-done.2, s32[2,2,8]{2,1,0:T(2,128)S(1)} %copy-done.4, s32[2,2]{1,0:T(2,128)S(1)} %copy-done.5, bf16[3,2,256,512]{3,2,1,0:T(8,128)(2,1)S(1)} %copy-done, bf16[1152,256]{1,0:T(8,128)(2,1)S(1)} %get-tuple-element.31.refs_12_.refs_0_, ...), custom_call_target="tpu_custom_call" | custom-call | flops 603979776 | bytes 10223616 | tf_op jit(solution)/shard_map/pallas_call | solution.py:41
  (55 shorter events, 10.4 us)
Async XLA Ops:
  1.1 44.0 %copy-start.1 = (bf16[2,2,2,256,256]{4,3,2,1,0:T(8,128)(2,1)S(1)}, bf16[2,2,2,256,256]{4,3,2,1,0:T(8,128)(2,1)}, u32[]{:S(2)}) copy-start(bf16[2,2,2,256,256]{4,3,2,1,0:T(8,128)(2,1)} %refs_1_.1) | copy-start | bytes 3145732
  1.2 18.3 %collective-permute-start.5 = (bf16[1152,256]{1,0:T(8,128)(2,1)S(1)}, bf16[1152,256]{1,0:T(8,128)(2,1)S(1)}, u32[]{:S(2)}, u32[]{:S(2)}) collective-permute-start(bf16[1152,256]{1,0:T(8,128)(2,1)S(1)} %pad_maximum_fusion.refs_2_.refs_0_), channel_id=1, source_target_pairs={{0,2},{1,3},{2,0},{3,1},{4,6},{5,7},{6,4},{7,5},{8,10},{9,11},{10,... | collective-permute-start | bytes 1769480 | tf_op jit(solution)/shard_map/ppermute | solution.py:18
  4.2 14.7 %collective-permute-start.1 = (bf16[2,64,256]{2,1,0:T(8,128)(2,1)S(1)}, bf16[2,64,256]{2,1,0:T(8,128)(2,1)S(1)}, u32[]{:S(2)}, u32[]{:S(2)}) collective-permute-start(bf16[2,64,256]{2,1,0:T(8,128)(2,1)S(1)} %get-tuple-element.50.refs_0_), channel_id=1, source_target_pairs={{0,2},{1,3},{2,0},{3,1},{4,6},{5,7},{6,4},{7,5},{8,10},{9,11},{10,... | collective-permute-start | bytes 196616 | tf_op jit(solution)/shard_map/ppermute | solution.py:18
  4.3 15.2 %collective-permute-start = (bf16[2,64,256]{2,1,0:T(8,128)(2,1)S(1)}, bf16[2,64,256]{2,1,0:T(8,128)(2,1)S(1)}, u32[]{:S(2)}, u32[]{:S(2)}) collective-permute-start(bf16[2,64,256]{2,1,0:T(8,128)(2,1)S(1)} %get-tuple-element.50.refs_0_), channel_id=1, source_target_pairs={{0,1},{1,0},{2,3},{3,2},{4,5},{5,4},{6,7},{7,6},{8,9},{9,8},{10,11... | collective-permute-start | bytes 196616 | tf_op jit(solution)/shard_map/ppermute | solution.py:18
  18.9 1.3 %collective-permute-start.2 = (bf16[2,64,256]{2,1,0:T(8,128)(2,1)S(1)}, bf16[2,64,256]{2,1,0:T(8,128)(2,1)S(1)}, u32[]{:S(2)}, u32[]{:S(2)}) collective-permute-start(bf16[2,64,256]{2,1,0:T(8,128)(2,1)S(1)} %collective-permute-done.1.refs_2_), channel_id=1, source_target_pairs={{0,1},{1,0},{2,3},{3,2},{4,5},{5,4},{6,7},{7,6},{8,9},{9,8},{10,11... | collective-permute-start | bytes 196616 | tf_op jit(solution)/shard_map/ppermute | solution.py:18
  18.9 26.2 %collective-permute-start.4 = (bf16[1152,256]{1,0:T(8,128)(2,1)S(1)}, bf16[1152,256]{1,0:T(8,128)(2,1)S(1)}, u32[]{:S(2)}, u32[]{:S(2)}) collective-permute-start(bf16[1152,256]{1,0:T(8,128)(2,1)S(1)} %pad_maximum_fusion.refs_2_.refs_0_), channel_id=1, source_target_pairs={{0,1},{1,0},{2,3},{3,2},{4,5},{5,4},{6,7},{7,6},{8,9},{9,8},{10,11... | collective-permute-start | bytes 1769480 | tf_op jit(solution)/shard_map/ppermute | solution.py:18
  19.4 25.7 %collective-permute-start.6 = (bf16[1152,256]{1,0:T(8,128)(2,1)S(1)}, bf16[1152,256]{1,0:T(8,128)(2,1)S(1)}, u32[]{:S(2)}, u32[]{:S(2)}) collective-permute-start(bf16[1152,256]{1,0:T(8,128)(2,1)S(1)} %collective-permute-done.5.refs_4_.refs_2_), channel_id=1, source_target_pairs={{0,1},{1,0},{2,3},{3,2},{4,5},{5,4},{6,7},{7,6},{8,9},{9,8},{10,11... | collective-permute-start | bytes 1769480 | tf_op jit(solution)/shard_map/ppermute | solution.py:18
  21.2 15.3 %collective-permute-start.3 = (bf16[2,256,256]{2,1,0:T(8,128)(2,1)S(1)}, bf16[2,256,256]{2,1,0:T(8,128)(2,1)S(1)}, u32[]{:S(2)}, u32[]{:S(2)}) collective-permute-start(bf16[2,256,256]{2,1,0:T(8,128)(2,1)S(1)} %get-tuple-element.27.refs_4_.refs_20_), channel_id=1, source_target_pairs={{0,16},{4,20},{8,24},{12,28},{16,0},{20,4},{24,8},{28,12},{1,17},{... | collective-permute-start | bytes 786440 | tf_op jit(solution)/shard_map/ppermute | solution.py:18
  24.1 13.9 %collective-permute-start.7 = (bf16[2,256,256]{2,1,0:T(8,128)(2,1)S(1)}, bf16[2,256,256]{2,1,0:T(8,128)(2,1)S(1)}, u32[]{:S(2)}, u32[]{:S(2)}) collective-permute-start(bf16[2,256,256]{2,1,0:T(8,128)(2,1)S(1)} %get-tuple-element.28), channel_id=1, source_target_pairs={{0,4},{4,0},{8,12},{12,8},{16,20},{20,16},{24,28},{28,24},{1,5},{5... | collective-permute-start | bytes 786440 | tf_op jit(solution)/shard_map/ppermute | solution.py:18
  25.7 12.4 %collective-permute-start.8 = (bf16[2,256,256]{2,1,0:T(8,128)(2,1)S(1)}, bf16[2,256,256]{2,1,0:T(8,128)(2,1)S(1)}, u32[]{:S(2)}, u32[]{:S(2)}) collective-permute-start(bf16[2,256,256]{2,1,0:T(8,128)(2,1)S(1)} %get-tuple-element.29), channel_id=1, source_target_pairs={{0,8},{4,12},{8,0},{12,4},{16,24},{20,28},{24,16},{28,20},{1,9},{5... | collective-permute-start | bytes 786440 | tf_op jit(solution)/shard_map/ppermute | solution.py:18
  36.5 8.6 %collective-permute-start.9 = (bf16[2,256,256]{2,1,0:T(8,128)(2,1)S(1)}, bf16[2,256,256]{2,1,0:T(8,128)(2,1)S(1)}, u32[]{:S(2)}, u32[]{:S(2)}) collective-permute-start(bf16[2,256,256]{2,1,0:T(8,128)(2,1)S(1)} %get-tuple-element.30), channel_id=1, source_target_pairs={{0,12},{4,8},{8,4},{12,0},{16,28},{20,24},{24,20},{28,16},{1,13},{... | collective-permute-start | bytes 786440 | tf_op jit(solution)/shard_map/ppermute | solution.py:18
  45.9 13.9 %collective-permute-start.11 = (bf16[1152,256]{1,0:T(8,128)(2,1)S(1)}, bf16[1152,256]{1,0:T(8,128)(2,1)S(1)}, u32[]{:S(2)}, u32[]{:S(2)}) collective-permute-start(bf16[1152,256]{1,0:T(8,128)(2,1)S(1)} %get-tuple-element.31.refs_12_.refs_0_), channel_id=1, source_target_pairs={{0,2},{1,3},{2,0},{3,1},{4,6},{5,7},{6,4},{7,5},{8,10},{9,11},{10,... | collective-permute-start | bytes 1769480 | tf_op jit(solution)/shard_map/ppermute | solution.py:18
  47.3 32.6 %collective-permute-start.10 = (bf16[1152,256]{1,0:T(8,128)(2,1)S(1)}, bf16[1152,256]{1,0:T(8,128)(2,1)S(1)}, u32[]{:S(2)}, u32[]{:S(2)}) collective-permute-start(bf16[1152,256]{1,0:T(8,128)(2,1)S(1)} %get-tuple-element.31.refs_12_.refs_0_), channel_id=1, source_target_pairs={{0,1},{1,0},{2,3},{3,2},{4,5},{5,4},{6,7},{7,6},{8,9},{9,8},{10,11... | collective-permute-start | bytes 1769480 | tf_op jit(solution)/shard_map/ppermute | solution.py:18
  47.3 15.8 %collective-permute-start.13 = (bf16[2,256,256]{2,1,0:T(8,128)(2,1)S(1)}, bf16[2,256,256]{2,1,0:T(8,128)(2,1)S(1)}, u32[]{:S(2)}, u32[]{:S(2)}) collective-permute-start(bf16[2,256,256]{2,1,0:T(8,128)(2,1)S(1)} %get-tuple-element.32.refs_4_.refs_21_), channel_id=1, source_target_pairs={{0,16},{4,20},{8,24},{12,28},{16,0},{20,4},{24,8},{28,12},{1,17},{... | collective-permute-start | bytes 786440 | tf_op jit(solution)/shard_map/ppermute | solution.py:18
  59.7 22.4 %collective-permute-start.12 = (bf16[1152,256]{1,0:T(8,128)(2,1)S(1)}, bf16[1152,256]{1,0:T(8,128)(2,1)S(1)}, u32[]{:S(2)}, u32[]{:S(2)}) collective-permute-start(bf16[1152,256]{1,0:T(8,128)(2,1)S(1)} %collective-permute-done.11.refs_14_.refs_2_), channel_id=1, source_target_pairs={{0,1},{1,0},{2,3},{3,2},{4,5},{5,4},{6,7},{7,6},{8,9},{9,8},{10,11... | collective-permute-start | bytes 1769480 | tf_op jit(solution)/shard_map/ppermute | solution.py:18
  59.7 5.9 %collective-permute-start.17 = (bf16[1,256,256]{2,1,0:T(8,128)(2,1)S(1)}, bf16[1,256,256]{2,1,0:T(8,128)(2,1)S(1)}, u32[]{:S(2)}, u32[]{:S(2)}) collective-permute-start(bf16[1,256,256]{2,1,0:T(8,128)(2,1)S(1)} %get-tuple-element.36), channel_id=1, source_target_pairs={{0,4},{4,0},{8,12},{12,8},{16,20},{20,16},{24,28},{28,24},{1,5},{5... | collective-permute-start | bytes 393224 | tf_op jit(solution)/shard_map/ppermute | solution.py:18
  60.9 6.4 %collective-permute-start.18 = (bf16[1,256,256]{2,1,0:T(8,128)(2,1)S(1)}, bf16[1,256,256]{2,1,0:T(8,128)(2,1)S(1)}, u32[]{:S(2)}, u32[]{:S(2)}) collective-permute-start(bf16[1,256,256]{2,1,0:T(8,128)(2,1)S(1)} %get-tuple-element.37), channel_id=1, source_target_pairs={{0,8},{4,12},{8,0},{12,4},{16,24},{20,28},{24,16},{28,20},{1,9},{5... | collective-permute-start | bytes 393224 | tf_op jit(solution)/shard_map/ppermute | solution.py:18
  63.0 7.1 %collective-permute-start.19 = (bf16[1,256,256]{2,1,0:T(8,128)(2,1)S(1)}, bf16[1,256,256]{2,1,0:T(8,128)(2,1)S(1)}, u32[]{:S(2)}, u32[]{:S(2)}) collective-permute-start(bf16[1,256,256]{2,1,0:T(8,128)(2,1)S(1)} %get-tuple-element.38), channel_id=1, source_target_pairs={{0,12},{4,8},{8,4},{12,0},{16,28},{20,24},{24,20},{28,16},{1,13},{... | collective-permute-start | bytes 393224 | tf_op jit(solution)/shard_map/ppermute | solution.py:18
  65.7 9.6 %collective-permute-start.14 = (bf16[1,256,256]{2,1,0:T(8,128)(2,1)S(1)}, bf16[1,256,256]{2,1,0:T(8,128)(2,1)S(1)}, u32[]{:S(2)}, u32[]{:S(2)}) collective-permute-start(bf16[1,256,256]{2,1,0:T(8,128)(2,1)S(1)} %get-tuple-element.33.refs_12_), channel_id=1, source_target_pairs={{0,4},{4,0},{8,12},{12,8},{16,20},{20,16},{24,28},{28,24},{1,5},{5... | collective-permute-start | bytes 393224 | tf_op jit(solution)/shard_map/ppermute | solution.py:18
  67.3 11.4 %collective-permute-start.15 = (bf16[1,256,256]{2,1,0:T(8,128)(2,1)S(1)}, bf16[1,256,256]{2,1,0:T(8,128)(2,1)S(1)}, u32[]{:S(2)}, u32[]{:S(2)}) collective-permute-start(bf16[1,256,256]{2,1,0:T(8,128)(2,1)S(1)} %get-tuple-element.34), channel_id=1, source_target_pairs={{0,8},{4,12},{8,0},{12,4},{16,24},{20,28},{24,16},{28,20},{1,9},{5... | collective-permute-start | bytes 393224 | tf_op jit(solution)/shard_map/ppermute | solution.py:18
  70.1 9.0 %collective-permute-start.16 = (bf16[1,256,256]{2,1,0:T(8,128)(2,1)S(1)}, bf16[1,256,256]{2,1,0:T(8,128)(2,1)S(1)}, u32[]{:S(2)}, u32[]{:S(2)}) collective-permute-start(bf16[1,256,256]{2,1,0:T(8,128)(2,1)S(1)} %get-tuple-element.35), channel_id=1, source_target_pairs={{0,12},{4,8},{8,4},{12,0},{16,28},{20,24},{24,20},{28,16},{1,13},{... | collective-permute-start | bytes 393224 | tf_op jit(solution)/shard_map/ppermute | solution.py:18
  75.2 20.6 %collective-permute-start.20 = (bf16[2,256,256]{2,1,0:T(8,128)(2,1)S(1)}, bf16[2,256,256]{2,1,0:T(8,128)(2,1)S(1)}, u32[]{:S(2)}, u32[]{:S(2)}) collective-permute-start(bf16[2,256,256]{2,1,0:T(8,128)(2,1)S(1)} %get-tuple-element.39.refs_12_.refs_22_), channel_id=1, source_target_pairs={{0,16},{4,20},{8,24},{12,28},{16,0},{20,4},{24,8},{28,12},{1,17},{... | collective-permute-start | bytes 786440 | tf_op jit(solution)/shard_map/ppermute | solution.py:18
  78.7 6.7 %collective-permute-start.21 = (bf16[1,256,256]{2,1,0:T(8,128)(2,1)S(1)}, bf16[1,256,256]{2,1,0:T(8,128)(2,1)S(1)}, u32[]{:S(2)}, u32[]{:S(2)}) collective-permute-start(bf16[1,256,256]{2,1,0:T(8,128)(2,1)S(1)} %get-tuple-element.40), channel_id=1, source_target_pairs={{0,4},{4,0},{8,12},{12,8},{16,20},{20,16},{24,28},{28,24},{1,5},{5... | collective-permute-start | bytes 393224 | tf_op jit(solution)/shard_map/ppermute | solution.py:18
  79.2 9.1 %collective-permute-start.22 = (bf16[1,256,256]{2,1,0:T(8,128)(2,1)S(1)}, bf16[1,256,256]{2,1,0:T(8,128)(2,1)S(1)}, u32[]{:S(2)}, u32[]{:S(2)}) collective-permute-start(bf16[1,256,256]{2,1,0:T(8,128)(2,1)S(1)} %get-tuple-element.41), channel_id=1, source_target_pairs={{0,8},{4,12},{8,0},{12,4},{16,24},{20,28},{24,16},{28,20},{1,9},{5... | collective-permute-start | bytes 393224 | tf_op jit(solution)/shard_map/ppermute | solution.py:18
  79.9 12.3 %collective-permute-start.23 = (bf16[1,256,256]{2,1,0:T(8,128)(2,1)S(1)}, bf16[1,256,256]{2,1,0:T(8,128)(2,1)S(1)}, u32[]{:S(2)}, u32[]{:S(2)}) collective-permute-start(bf16[1,256,256]{2,1,0:T(8,128)(2,1)S(1)} %get-tuple-element.42), channel_id=1, source_target_pairs={{0,12},{4,8},{8,4},{12,0},{16,28},{20,24},{24,20},{28,16},{1,13},{... | collective-permute-start | bytes 393224 | tf_op jit(solution)/shard_map/ppermute | solution.py:18
  84.6 16.3 %collective-permute-start.27 = (bf16[2,256,256]{2,1,0:T(8,128)(2,1)S(1)}, bf16[2,256,256]{2,1,0:T(8,128)(2,1)S(1)}, u32[]{:S(2)}, u32[]{:S(2)}) collective-permute-start(bf16[2,256,256]{2,1,0:T(8,128)(2,1)S(1)} %shard_map.67.refs_0_.refs_12_.refs_23_), channel_id=1, source_target_pairs={{0,16},{4,20},{8,24},{12,28},{16,0},{20,4},{24,8},{28,12},{1,17},{... | collective-permute-start | bytes 786440 | tf_op jit(solution)/shard_map/ppermute | solution.py:18
  96.6 10.3 %collective-permute-start.24 = (bf16[2,256,256]{2,1,0:T(8,128)(2,1)S(1)}, bf16[2,256,256]{2,1,0:T(8,128)(2,1)S(1)}, u32[]{:S(2)}, u32[]{:S(2)}) collective-permute-start(bf16[2,256,256]{2,1,0:T(8,128)(2,1)S(1)} %get-tuple-element.43), channel_id=1, source_target_pairs={{0,4},{4,0},{8,12},{12,8},{16,20},{20,16},{24,28},{28,24},{1,5},{5... | collective-permute-start | bytes 786440 | tf_op jit(solution)/shard_map/ppermute | solution.py:18
  97.7 9.2 %collective-permute-start.25 = (bf16[2,256,256]{2,1,0:T(8,128)(2,1)S(1)}, bf16[2,256,256]{2,1,0:T(8,128)(2,1)S(1)}, u32[]{:S(2)}, u32[]{:S(2)}) collective-permute-start(bf16[2,256,256]{2,1,0:T(8,128)(2,1)S(1)} %get-tuple-element.44), channel_id=1, source_target_pairs={{0,8},{4,12},{8,0},{12,4},{16,24},{20,28},{24,16},{28,20},{1,9},{5... | collective-permute-start | bytes 786440 | tf_op jit(solution)/shard_map/ppermute | solution.py:18
  97.7 14.5 %collective-permute-start.26 = (bf16[2,256,256]{2,1,0:T(8,128)(2,1)S(1)}, bf16[2,256,256]{2,1,0:T(8,128)(2,1)S(1)}, u32[]{:S(2)}, u32[]{:S(2)}) collective-permute-start(bf16[2,256,256]{2,1,0:T(8,128)(2,1)S(1)} %get-tuple-element.45), channel_id=1, source_target_pairs={{0,12},{4,8},{8,4},{12,0},{16,28},{20,24},{24,20},{28,16},{1,13},{... | collective-permute-start | bytes 786440 | tf_op jit(solution)/shard_map/ppermute | solution.py:18
  101.6 13.1 %collective-permute-start.28 = (bf16[1,256,256]{2,1,0:T(8,128)(2,1)S(1)}, bf16[1,256,256]{2,1,0:T(8,128)(2,1)S(1)}, u32[]{:S(2)}, u32[]{:S(2)}) collective-permute-start(bf16[1,256,256]{2,1,0:T(8,128)(2,1)S(1)} %get-tuple-element.46.refs_20_), channel_id=1, source_target_pairs={{0,4},{4,0},{8,12},{12,8},{16,20},{20,16},{24,28},{28,24},{1,5},{5... | collective-permute-start | bytes 393224 | tf_op jit(solution)/shard_map/ppermute | solution.py:18
  102.1 12.6 %collective-permute-start.29 = (bf16[1,256,256]{2,1,0:T(8,128)(2,1)S(1)}, bf16[1,256,256]{2,1,0:T(8,128)(2,1)S(1)}, u32[]{:S(2)}, u32[]{:S(2)}) collective-permute-start(bf16[1,256,256]{2,1,0:T(8,128)(2,1)S(1)} %get-tuple-element.47), channel_id=1, source_target_pairs={{0,8},{4,12},{8,0},{12,4},{16,24},{20,28},{24,16},{28,20},{1,9},{5... | collective-permute-start | bytes 393224 | tf_op jit(solution)/shard_map/ppermute | solution.py:18
  106.9 8.1 %collective-permute-start.30 = (bf16[1,256,256]{2,1,0:T(8,128)(2,1)S(1)}, bf16[1,256,256]{2,1,0:T(8,128)(2,1)S(1)}, u32[]{:S(2)}, u32[]{:S(2)}) collective-permute-start(bf16[1,256,256]{2,1,0:T(8,128)(2,1)S(1)} %get-tuple-element.48), channel_id=1, source_target_pairs={{0,12},{4,8},{8,4},{12,0},{16,28},{20,24},{24,20},{28,16},{1,13},{... | collective-permute-start | bytes 393224 | tf_op jit(solution)/shard_map/ppermute | solution.py:18
  (6 other events, 156.1 us)

commit v8 on v7

--- a/solution.py
+++ b/solution.py
@@ -60,8 +60,8 @@
         target[at:at + rows, :] = inverse[level, node]
 
 
-def first_kernel(chunks, draws, picks, noise, *refs):
-    *refs, inv = refs
+def first_kernel(chunks, draws, picks, noise, inverse, coupling, *refs):
+    *refs, pack, inv = refs
     parts, refs = take(refs, draws)
     solved, sends = take(refs, chunks)
     myself, draw = lax.axis_index("leaf"), lax.axis_index("draw")
@@ -77,26 +77,22 @@
         node = picks[0, myself ^ step, myself]
         for at, target in enumerate(solved):
             send[at] = target[node]
-
-
-def relay_kernel(owners, source, follow, pack_level, waits, picks, far, *refs):
+    write_pack(pack, 1, inverse, coupling)
+
+
+def relay_kernel(owners, source, follow, waits, picks, far, *refs):
     half = owners // 2
-    if pack_level:
-        inverse, coupling, *refs = refs
     own, refs = take(refs, follow)
-    _, refs = take(refs, waits)
-    sends, refs = take(refs, half - 1)
+    sends = refs[waits:]
     myself = lax.axis_index("leaf")
     for step, send in enumerate(sends, 1):
         send[0] = far[picks[source, myself ^ step, myself ^ half]]
         if own:
             send[1] = own[0][picks[source, myself ^ step, myself]]
-    if pack_level:
-        write_pack(refs[0], pack_level, inverse, coupling)
 
 
 def level_kernel(
-    level, owners, draws, width, chunk, places, sides, earlier, waits,
+    level, owners, draws, width, chunk, places, sides, earlier, waits, packing,
     picks, lists, counts, noise, *refs,
 ):
     half = owners // 2
@@ -104,8 +100,14 @@
     known, refs = take(refs, level * owners)
     done, refs = take(refs, earlier)
     _, refs = take(refs, waits)
+    if packing:
+        inverse, coupling, *refs = refs
     target, *refs = refs
-    sends, (table, inv, *refs) = take(refs, sides)
+    sends, refs = take(refs, sides)
+    if packing:
+        write_pack(refs[0], level + 1, inverse, coupling)
+        refs = refs[1:]
+    table, inv, *refs = refs
     myself, draw = lax.axis_index("leaf"), lax.axis_index("draw")
     nodes, wide = noise.shape[1], table.shape[-1]
     depth = inv.shape[1]
@@ -166,50 +168,45 @@
     inv_here = pltpu.VMEM((nodes, rows, rows), BF16)
     dot_flops = 2 * rows * rows * wide
 
-    refs = call(
+    *refs, pack = call(
         functools.partial(first_kernel, CHUNKS, draws),
-        [part] * CHUNKS + [shape(CHUNKS, rows, wide)] * (half - 1),
+        [part] * CHUNKS + [shape(CHUNKS, rows, wide)] * (half - 1) + [pack_shape],
         [inv_here],
         (picks,),
-        (noise, *gather(inverse[0])),
+        (noise, inverse, coupling, *gather(inverse[0])),
         flops=nodes * CHUNKS * dot_flops,
     )
     solved, sends = take(refs, CHUNKS)
-    packs = [gather(jnp.concatenate([coupling[0].reshape(-1, rows), inverse[1].reshape(-1, rows)]))]
+    packs = [gather(pack)]
     done, pieces = [solved], []
     for level in range(1, levels):
         source = level - 1
         far = [leaf(value, half) for value in solved]
         got = near(sends)
         close = [[(ref, at) for ref in got] for at in chunks] if source == 0 else [[(ref, 0) for ref in got]]
-        distant, waits = [], packs[source] + got if source == 0 else got
+        distant, waits = [], got
         for at in chunks:
             follow = source > 0 and at < CHUNKS - 1
-            pack_level = source + 2 if at == 0 and source + 2 < levels else 0
-            sends = list(call(
-                functools.partial(relay_kernel, owners, source, int(follow), pack_level, len(waits)),
-                [shape(1 + follow, rows, wide)] * (half - 1) + [pack_shape] * bool(pack_level),
+            sends = call(
+                functools.partial(relay_kernel, owners, source, int(follow), len(waits)),
+                [shape(1 + follow, rows, wide)] * (half - 1),
                 [],
                 (picks,),
-                (
-                    far[at], *((inverse, coupling) if pack_level else ()),
-                    *([solved[at + 1]] if follow else []), *waits,
-                ),
-            ))
-            if pack_level:
-                packs.append(gather(sends.pop()))
+                (far[at], *([solved[at + 1]] if follow else []), *waits),
+            )
             got = near(sends)
             distant.append([(ref, 0) for ref in got])
             if follow:
                 close.append([(ref, 1) for ref in got])
-            waits = []
+            waits = packs[source]
         pieces.append([
             [(solved[at], 0), *close[at], (far[at], 0), *distant[at]] for at in chunks
         ])
         waits = sends[:1]
         solved, sends = [], []
         for at in chunks:
-            sides = half - 1 if at == 0 and level < last_level else 0
+            packing = at == 0 and level < last_level
+            sides = half - 1 if packing else 0
             final = level == last_level and at == CHUNKS - 1
             earlier = [value for values in done for value in values] + solved if final else []
             known = [entry for below in range(level) for entry in pieces[below][at]]
@@ -222,19 +219,22 @@
             here, *sent = call(
                 functools.partial(
                     level_kernel, level, owners, draws, width, at,
-                    [place for _, place in known], sides, len(earlier), len(waits),
+                    [place for _, place in known], sides, len(earlier), len(waits), packing,
                 ),
                 [shape(levels, nodes, rows, columns) if final else part]
-                + [shape(1, rows, wide)] * sides,
+                + [shape(1, rows, wide)] * sides + [pack_shape] * packing,
                 scratch,
                 (picks, lists, counts),
-                (noise, *packs[level - 1], *(ref for ref, _ in known), *earlier, *waits),
+                (noise, *packs[level - 1], *(ref for ref, _ in known), *earlier, *waits)
+                + ((inverse, coupling) if packing else ()),
                 out_spec=ANY if final else VMEM,
                 flops=nodes * (draws * width + 1) * dot_flops,
             )
             solved.append(here)
+            if packing:
+                packs.append(gather(sent.pop()))
             sends += sent
-            waits = packs[level] if at == 0 and level < last_level else []
+            waits = []
         done.append(solved)
     return here
 

time: 118 us -> 128 us (1.085)
  waiting for transfers between devices: 64.9 us -> 79.4 us
  starting transfers between devices: 37.6 us -> 28.6 us
  local copies, waits for them, and re-layouts: 1.11 us -> 5.12 us
    ppermute x31, waiting for transfers between devices: 64.9 us -> 79.4 us  [hop(): return lax.ppermute(value, axis, [(at, at ^ step) for at in range(size)])]
    ppermute x31, starting transfers between devices: 37.6 us -> 28.6 us  [hop(): return lax.ppermute(value, axis, [(at, at ^ step) for at in range(size)])]
    unnamed x12 -> x16, local copies, waits for them, and re-layouts: 0.03 us -> 4.28 us
  transfers between devices with their start and end apart: 31 -> 31, of which waited for: 15 -> 16; matrix products, arithmetic and copies ran while one was open for 0% -> 0% of each run, Pallas kernels for 9% -> 6%
where the time goes in v8:
time: 128 us
  waiting for transfers between devices  79.4 us (62%)
  starting transfers between devices  28.6 us (22%)
  Pallas kernels  14.5 us (11%)
  local copies, waits for them, and re-layouts  5.12 us (4%)
    ppermute x31, waiting for transfers between devices, hop(): return lax.ppermute(value, axis, [(at, at ^ step) for at in range(size)])  79.4 us
    ppermute x31, starting transfers between devices, hop(): return lax.ppermute(value, axis, [(at, at ^ step) for at in range(size)])  28.6 us
    pallas_call x9, Pallas kernels, call(): pl.pallas_call(kernel, out_shape=outs, in_specs=[SMEM] * len(small) + [VM...  14.5 us
    unnamed x16, local copies, waits for them, and re-layouts  4.28 us
  transfers between devices with their start and end apart: 31, of which 16 were waited for; matrix products, arithmetic and copies ran while one was open for 0% of the time, Pallas kernels for 6%

profile of v8, /device:TPU:0, one launch (start us, length us, event | category | flops | bytes accessed | tf_op | source)
XLA Modules:
  0.0 127.8 jit_solution(11668049015724545308)
XLA Ops:
  0.8 2.9 %collective-permute-start.1 = (bf16[2,64,256]{2,1,0:T(8,128)(2,1)S(1)}, bf16[2,64,256]{2,1,0:T(8,128)(2,1)S(1)}, u32[]{:S(2)}, u32[]{:S(2)}) collective-permute-start(bf16[2,64,256]{2,1,0:T(8,128)(2,1)S(1)} %slice_bitcast_fusion.refs_0_), channel_id=1, source_target_pairs={{0,2},{1,3},{2,0},{3,1},{4,6},{5,7},{6,4},{7,5},{8,10},{9,11},{10,... | collective-permute-start | bytes 196616 | tf_op jit(solution)/shard_map/ppermute | solution.py:18
  3.8 2.2 %collective-permute-done.1.refs_2_ = bf16[2,64,256]{2,1,0:T(8,128)(2,1)S(1)} collective-permute-done((bf16[2,64,256]{2,1,0:T(8,128)(2,1)S(1)}, bf16[2,64,256]{2,1,0:T(8,128)(2,1)S(1)}, u32[]{:S(2)}, u32[]{:S(2)}) %collective-permute-start.1) | collective-permute-done | bytes 65568 | tf_op jit(solution)/shard_map/ppermute | solution.py:18
  6.0 1.2 collective-permute-done.2.refs_3_
  7.3 1.4 %copy-done = bf16[3,2,256,512]{3,2,1,0:T(8,128)(2,1)S(1)} copy-done((bf16[3,2,256,512]{3,2,1,0:T(8,128)(2,1)S(1)}, bf16[3,2,256,512]{3,2,1,0:T(8,128)(2,1)}, u32[]{:S(2)}) %copy-start) | copy-done | bytes 1572888
  12.6 2.1 %collective-permute-start.4 = (bf16[1152,256]{1,0:T(8,128)(2,1)S(1)}, bf16[1152,256]{1,0:T(8,128)(2,1)S(1)}, u32[]{:S(2)}, u32[]{:S(2)}) collective-permute-start(bf16[1152,256]{1,0:T(8,128)(2,1)S(1)} %get-tuple-element.28.refs_0_), channel_id=1, source_target_pairs={{0,2},{1,3},{2,0},{3,1},{4,6},{5,7},{6,4},{7,5},{8,10},{9,11},{10,... | collective-permute-start | bytes 1769480 | tf_op jit(solution)/shard_map/ppermute | solution.py:18
  14.7 1.5 %collective-permute-start.6 = (bf16[2,256,256]{2,1,0:T(8,128)(2,1)S(1)}, bf16[2,256,256]{2,1,0:T(8,128)(2,1)S(1)}, u32[]{:S(2)}, u32[]{:S(2)}) collective-permute-start(bf16[2,256,256]{2,1,0:T(8,128)(2,1)S(1)} %get-tuple-element.30), channel_id=1, source_target_pairs={{0,4},{4,0},{8,12},{12,8},{16,20},{20,16},{24,28},{28,24},{1,5},{5... | collective-permute-start | bytes 786440 | tf_op jit(solution)/shard_map/ppermute | solution.py:18
  16.2 1.6 %collective-permute-start.7 = (bf16[2,256,256]{2,1,0:T(8,128)(2,1)S(1)}, bf16[2,256,256]{2,1,0:T(8,128)(2,1)S(1)}, u32[]{:S(2)}, u32[]{:S(2)}) collective-permute-start(bf16[2,256,256]{2,1,0:T(8,128)(2,1)S(1)} %get-tuple-element.31), channel_id=1, source_target_pairs={{0,8},{4,12},{8,0},{12,4},{16,24},{20,28},{24,16},{28,20},{1,9},{5... | collective-permute-start | bytes 786440 | tf_op jit(solution)/shard_map/ppermute | solution.py:18
  17.8 10.6 %collective-permute-done.4.refs_2_ = bf16[1152,256]{1,0:T(8,128)(2,1)S(1)} collective-permute-done((bf16[1152,256]{1,0:T(8,128)(2,1)S(1)}, bf16[1152,256]{1,0:T(8,128)(2,1)S(1)}, u32[]{:S(2)}, u32[]{:S(2)}) %collective-permute-start.4) | collective-permute-done | bytes 589856 | tf_op jit(solution)/shard_map/ppermute | solution.py:18
  28.4 2.8 %collective-permute-start.8 = (bf16[2,256,256]{2,1,0:T(8,128)(2,1)S(1)}, bf16[2,256,256]{2,1,0:T(8,128)(2,1)S(1)}, u32[]{:S(2)}, u32[]{:S(2)}) collective-permute-start(bf16[2,256,256]{2,1,0:T(8,128)(2,1)S(1)} %get-tuple-element.32), channel_id=1, source_target_pairs={{0,12},{4,8},{8,4},{12,0},{16,28},{20,24},{24,20},{28,16},{1,13},{... | collective-permute-start | bytes 786440 | tf_op jit(solution)/shard_map/ppermute | solution.py:18
  31.2 2.6 %collective-permute-start.9 = (bf16[2,256,256]{2,1,0:T(8,128)(2,1)S(1)}, bf16[2,256,256]{2,1,0:T(8,128)(2,1)S(1)}, u32[]{:S(2)}, u32[]{:S(2)}) collective-permute-start(bf16[2,256,256]{2,1,0:T(8,128)(2,1)S(1)} %get-tuple-element.29.refs_4_.refs_20_), channel_id=1, source_target_pairs={{0,16},{4,20},{8,24},{12,28},{16,0},{20,4},{24,8},{28,12},{1,17},{... | collective-permute-start | bytes 786440 | tf_op jit(solution)/shard_map/ppermute | solution.py:18
  34.1 9.5 %collective-permute-done.8.refs_2_.refs_7_ = bf16[2,256,256]{2,1,0:T(8,128)(2,1)S(1)} collective-permute-done((bf16[2,256,256]{2,1,0:T(8,128)(2,1)S(1)}, bf16[2,256,256]{2,1,0:T(8,128)(2,1)S(1)}, u32[]{:S(2)}, u32[]{:S(2)}) %collective-permute-start.8) | collective-permute-done | bytes 262176 | tf_op jit(solution)/shard_map/ppermute | solution.py:18
  43.6 8.8 %collective-permute-done.9.far.refs_8_ = bf16[2,256,256]{2,1,0:T(8,128)(2,1)S(1)} collective-permute-done((bf16[2,256,256]{2,1,0:T(8,128)(2,1)S(1)}, bf16[2,256,256]{2,1,0:T(8,128)(2,1)S(1)}, u32[]{:S(2)}, u32[]{:S(2)}) %collective-permute-start.9) | collective-permute-done | bytes 262176 | tf_op jit(solution)/shard_map/ppermute | solution.py:18
  53.8 3.7 %collective-permute-done.13.far.refs_8_ = bf16[2,256,256]{2,1,0:T(8,128)(2,1)S(1)} collective-permute-done((bf16[2,256,256]{2,1,0:T(8,128)(2,1)S(1)}, bf16[2,256,256]{2,1,0:T(8,128)(2,1)S(1)}, u32[]{:S(2)}, u32[]{:S(2)}) %collective-permute-start.13) | collective-permute-done | bytes 262176 | tf_op jit(solution)/shard_map/ppermute | solution.py:18
  58.3 2.0 %collective-permute-done.11.refs_10_ = bf16[1,256,256]{2,1,0:T(8,128)(2,1)S(1)} collective-permute-done((bf16[1,256,256]{2,1,0:T(8,128)(2,1)S(1)}, bf16[1,256,256]{2,1,0:T(8,128)(2,1)S(1)}, u32[]{:S(2)}, u32[]{:S(2)}) %collective-permute-start.11) | collective-permute-done | bytes 131104 | tf_op jit(solution)/shard_map/ppermute | solution.py:18
  60.3 3.1 %collective-permute-done.12.refs_11_ = bf16[1,256,256]{2,1,0:T(8,128)(2,1)S(1)} collective-permute-done((bf16[1,256,256]{2,1,0:T(8,128)(2,1)S(1)}, bf16[1,256,256]{2,1,0:T(8,128)(2,1)S(1)}, u32[]{:S(2)}, u32[]{:S(2)}) %collective-permute-start.12) | collective-permute-done | bytes 131104 | tf_op jit(solution)/shard_map/ppermute | solution.py:18
  63.4 2.5 %shard_map.67 = (bf16[2,256,256]{2,1,0:T(8,128)(2,1)S(1)}, bf16[1,256,256]{2,1,0:T(8,128)(2,1)S(1)}, bf16[1,256,256]{2,1,0:T(8,128)(2,1)S(1)}, bf16[1,256,256]{2,1,0:T(8,128)(2,1)S(1)}, bf16[1152,256]{1,0:T(8,128)(2,1)S(1)}) custom-call(s32[2,8,8]{2,1,0:T(8,128)S(1)} %copy-done.5, s32[2,2,8]{2,1,0:T(2,128)S(1)} %copy-done.6, s32[2,2]{1,0:T(2,128)S(1)} %copy-done.7, ...), custom_call_target="tpu_custom_call" | custom-call | flops 603979776 | bytes 8257536 | tf_op jit(solution)/shard_map/pallas_call | solution.py:41
  65.9 1.6 %collective-permute-start.15 = (bf16[1152,256]{1,0:T(8,128)(2,1)S(1)}, bf16[1152,256]{1,0:T(8,128)(2,1)S(1)}, u32[]{:S(2)}, u32[]{:S(2)}) collective-permute-start(bf16[1152,256]{1,0:T(8,128)(2,1)S(1)} %get-tuple-element.38.refs_0_), channel_id=1, source_target_pairs={{0,2},{1,3},{2,0},{3,1},{4,6},{5,7},{6,4},{7,5},{8,10},{9,11},{10,... | collective-permute-start | bytes 1769480 | tf_op jit(solution)/shard_map/ppermute | solution.py:18
  67.4 2.6 %collective-permute-start.19 = (bf16[1,256,256]{2,1,0:T(8,128)(2,1)S(1)}, bf16[1,256,256]{2,1,0:T(8,128)(2,1)S(1)}, u32[]{:S(2)}, u32[]{:S(2)}) collective-permute-start(bf16[1,256,256]{2,1,0:T(8,128)(2,1)S(1)} %get-tuple-element.40), channel_id=1, source_target_pairs={{0,12},{4,8},{8,4},{12,0},{16,28},{20,24},{24,20},{28,16},{1,13},{... | collective-permute-start | bytes 393224 | tf_op jit(solution)/shard_map/ppermute | solution.py:18
  70.9 8.4 %collective-permute-done.15.refs_2_ = bf16[1152,256]{1,0:T(8,128)(2,1)S(1)} collective-permute-done((bf16[1152,256]{1,0:T(8,128)(2,1)S(1)}, bf16[1152,256]{1,0:T(8,128)(2,1)S(1)}, u32[]{:S(2)}, u32[]{:S(2)}) %collective-permute-start.15) | collective-permute-done | bytes 589856 | tf_op jit(solution)/shard_map/ppermute | solution.py:18
  79.4 2.2 %collective-permute-start.21 = (bf16[1,256,256]{2,1,0:T(8,128)(2,1)S(1)}, bf16[1,256,256]{2,1,0:T(8,128)(2,1)S(1)}, u32[]{:S(2)}, u32[]{:S(2)}) collective-permute-start(bf16[1,256,256]{2,1,0:T(8,128)(2,1)S(1)} %get-tuple-element.42), channel_id=1, source_target_pairs={{0,4},{4,0},{8,12},{12,8},{16,20},{20,16},{24,28},{28,24},{1,5},{5... | collective-permute-start | bytes 393224 | tf_op jit(solution)/shard_map/ppermute | solution.py:18
  81.5 3.0 %collective-permute-start.20 = (bf16[2,256,256]{2,1,0:T(8,128)(2,1)S(1)}, bf16[2,256,256]{2,1,0:T(8,128)(2,1)S(1)}, u32[]{:S(2)}, u32[]{:S(2)}) collective-permute-start(bf16[2,256,256]{2,1,0:T(8,128)(2,1)S(1)} %get-tuple-element.41.refs_12_.refs_22_), channel_id=1, source_target_pairs={{0,16},{4,20},{8,24},{12,28},{16,0},{20,4},{24,8},{28,12},{1,17},{... | collective-permute-start | bytes 786440 | tf_op jit(solution)/shard_map/ppermute | solution.py:18
  84.6 2.4 %shard_map.68.refs_0_.refs_12_.refs_23_ = bf16[2,256,256]{2,1,0:T(8,128)(2,1)S(1)} custom-call(s32[2,8,8]{2,1,0:T(8,128)S(1)} %copy-done.5, s32[2,2,8]{2,1,0:T(2,128)S(1)} %copy-done.6, s32[2,2]{1,0:T(2,128)S(1)} %copy-done.7, bf16[3,2,256,512]{3,2,1,0:T(8,128)(2,1)S(1)} %copy-done.1, bf16[1152,256]{1,0:T(8,128)(2,1)S(1)} %get-tuple-element.28.refs_0_, ...), custom_call_target="tpu_custom_call" | custom-call | flops 603979776 | bytes 5898240 | tf_op jit(solution)/shard_map/pallas_call | solution.py:41
  87.1 2.7 %collective-permute-done.22.refs_2_.refs_14_ = bf16[1,256,256]{2,1,0:T(8,128)(2,1)S(1)} collective-permute-done((bf16[1,256,256]{2,1,0:T(8,128)(2,1)S(1)}, bf16[1,256,256]{2,1,0:T(8,128)(2,1)S(1)}, u32[]{:S(2)}, u32[]{:S(2)}) %collective-permute-start.22) | collective-permute-done | bytes 131104 | tf_op jit(solution)/shard_map/ppermute | solution.py:18
  89.9 9.1 %collective-permute-done.23.refs_3_.refs_15_ = bf16[1,256,256]{2,1,0:T(8,128)(2,1)S(1)} collective-permute-done((bf16[1,256,256]{2,1,0:T(8,128)(2,1)S(1)}, bf16[1,256,256]{2,1,0:T(8,128)(2,1)S(1)}, u32[]{:S(2)}, u32[]{:S(2)}) %collective-permute-start.23) | collective-permute-done | bytes 131104 | tf_op jit(solution)/shard_map/ppermute | solution.py:18
  99.0 3.9 %collective-permute-done.20.far.refs_16_ = bf16[2,256,256]{2,1,0:T(8,128)(2,1)S(1)} collective-permute-done((bf16[2,256,256]{2,1,0:T(8,128)(2,1)S(1)}, bf16[2,256,256]{2,1,0:T(8,128)(2,1)S(1)}, u32[]{:S(2)}, u32[]{:S(2)}) %collective-permute-start.20) | collective-permute-done | bytes 262176 | tf_op jit(solution)/shard_map/ppermute | solution.py:18
  103.9 4.1 %collective-permute-done.27.far.refs_16_ = bf16[2,256,256]{2,1,0:T(8,128)(2,1)S(1)} collective-permute-done((bf16[2,256,256]{2,1,0:T(8,128)(2,1)S(1)}, bf16[2,256,256]{2,1,0:T(8,128)(2,1)S(1)}, u32[]{:S(2)}, u32[]{:S(2)}) %collective-permute-start.27) | collective-permute-done | bytes 262176 | tf_op jit(solution)/shard_map/ppermute | solution.py:18
  108.7 1.9 %collective-permute-start.29 = (bf16[1,256,256]{2,1,0:T(8,128)(2,1)S(1)}, bf16[1,256,256]{2,1,0:T(8,128)(2,1)S(1)}, u32[]{:S(2)}, u32[]{:S(2)}) collective-permute-start(bf16[1,256,256]{2,1,0:T(8,128)(2,1)S(1)} %get-tuple-element.49), channel_id=1, source_target_pairs={{0,8},{4,12},{8,0},{12,4},{16,24},{20,28},{24,16},{28,20},{1,9},{5... | collective-permute-start | bytes 393224 | tf_op jit(solution)/shard_map/ppermute | solution.py:18
  112.3 1.3 %collective-permute-done.25.refs_18_.refs_14_ = bf16[2,256,256]{2,1,0:T(8,128)(2,1)S(1)} collective-permute-done((bf16[2,256,256]{2,1,0:T(8,128)(2,1)S(1)}, bf16[2,256,256]{2,1,0:T(8,128)(2,1)S(1)}, u32[]{:S(2)}, u32[]{:S(2)}) %collective-permute-start.25) | collective-permute-done | bytes 262176 | tf_op jit(solution)/shard_map/ppermute | solution.py:18
  113.6 6.5 %collective-permute-done.26.refs_19_.refs_15_ = bf16[2,256,256]{2,1,0:T(8,128)(2,1)S(1)} collective-permute-done((bf16[2,256,256]{2,1,0:T(8,128)(2,1)S(1)}, bf16[2,256,256]{2,1,0:T(8,128)(2,1)S(1)}, u32[]{:S(2)}, u32[]{:S(2)}) %collective-permute-start.26) | collective-permute-done | bytes 262176 | tf_op jit(solution)/shard_map/ppermute | solution.py:18
  120.1 2.5 %shard_map.71.refs_24_ = bf16[2,256,256]{2,1,0:T(8,128)(2,1)S(1)} custom-call(s32[2,8,8]{2,1,0:T(8,128)S(1)} %copy-done.5, s32[2,2,8]{2,1,0:T(2,128)S(1)} %copy-done.6, s32[2,2]{1,0:T(2,128)S(1)} %copy-done.7, bf16[3,2,256,512]{3,2,1,0:T(8,128)(2,1)S(1)} %copy-done.1, bf16[1152,256]{1,0:T(8,128)(2,1)S(1)} %get-tuple-element.38.refs_0_, ...), custom_call_target="tpu_custom_call" | custom-call | flops 603979776 | bytes 7733248 | tf_op jit(solution)/shard_map/pallas_call | solution.py:41
  122.6 1.9 %collective-permute-done.30.refs_19_ = bf16[1,256,256]{2,1,0:T(8,128)(2,1)S(1)} collective-permute-done((bf16[1,256,256]{2,1,0:T(8,128)(2,1)S(1)}, bf16[1,256,256]{2,1,0:T(8,128)(2,1)S(1)}, u32[]{:S(2)}, u32[]{:S(2)}) %collective-permute-start.30) | collective-permute-done | bytes 131104 | tf_op jit(solution)/shard_map/ppermute | solution.py:18
  124.6 3.2 %shard_map.72 = bf16[3,2,256,512]{3,2,1,0:T(8,128)(2,1)} custom-call(s32[2,8,8]{2,1,0:T(8,128)S(1)} %copy-done.5, s32[2,2,8]{2,1,0:T(2,128)S(1)} %copy-done.6, s32[2,2]{1,0:T(2,128)S(1)} %copy-done.7, bf16[3,2,256,512]{3,2,1,0:T(8,128)(2,1)S(1)} %copy-done.1, bf16[1152,256]{1,0:T(8,128)(2,1)S(1)} %get-tuple-element.38.refs_0_, ...), custom_call_target="tpu_custom_call" | custom-call | flops 603979776 | bytes 10223616 | tf_op jit(solution)/shard_map/pallas_call | solution.py:41
  (56 shorter events, 11.7 us)
Async XLA Ops:
  0.8 5.2 %collective-permute-start.1 = (bf16[2,64,256]{2,1,0:T(8,128)(2,1)S(1)}, bf16[2,64,256]{2,1,0:T(8,128)(2,1)S(1)}, u32[]{:S(2)}, u32[]{:S(2)}) collective-permute-start(bf16[2,64,256]{2,1,0:T(8,128)(2,1)S(1)} %slice_bitcast_fusion.refs_0_), channel_id=1, source_target_pairs={{0,2},{1,3},{2,0},{3,1},{4,6},{5,7},{6,4},{7,5},{8,10},{9,11},{10,... | collective-permute-start | bytes 196616 | tf_op jit(solution)/shard_map/ppermute | solution.py:18
  3.8 2.2 %collective-permute-start = (bf16[2,64,256]{2,1,0:T(8,128)(2,1)S(1)}, bf16[2,64,256]{2,1,0:T(8,128)(2,1)S(1)}, u32[]{:S(2)}, u32[]{:S(2)}) collective-permute-start(bf16[2,64,256]{2,1,0:T(8,128)(2,1)S(1)} %slice_bitcast_fusion.refs_0_), channel_id=1, source_target_pairs={{0,1},{1,0},{2,3},{3,2},{4,5},{5,4},{6,7},{7,6},{8,9},{9,8},{10,11... | collective-permute-start | bytes 196616 | tf_op jit(solution)/shard_map/ppermute | solution.py:18
  6.0 1.3 collective-permute-start.2
  12.6 15.7 %collective-permute-start.4 = (bf16[1152,256]{1,0:T(8,128)(2,1)S(1)}, bf16[1152,256]{1,0:T(8,128)(2,1)S(1)}, u32[]{:S(2)}, u32[]{:S(2)}) collective-permute-start(bf16[1152,256]{1,0:T(8,128)(2,1)S(1)} %get-tuple-element.28.refs_0_), channel_id=1, source_target_pairs={{0,2},{1,3},{2,0},{3,1},{4,6},{5,7},{6,4},{7,5},{8,10},{9,11},{10,... | collective-permute-start | bytes 1769480 | tf_op jit(solution)/shard_map/ppermute | solution.py:18
  14.7 16.4 %collective-permute-start.6 = (bf16[2,256,256]{2,1,0:T(8,128)(2,1)S(1)}, bf16[2,256,256]{2,1,0:T(8,128)(2,1)S(1)}, u32[]{:S(2)}, u32[]{:S(2)}) collective-permute-start(bf16[2,256,256]{2,1,0:T(8,128)(2,1)S(1)} %get-tuple-element.30), channel_id=1, source_target_pairs={{0,4},{4,0},{8,12},{12,8},{16,20},{20,16},{24,28},{28,24},{1,5},{5... | collective-permute-start | bytes 786440 | tf_op jit(solution)/shard_map/ppermute | solution.py:18
  16.2 17.5 %collective-permute-start.7 = (bf16[2,256,256]{2,1,0:T(8,128)(2,1)S(1)}, bf16[2,256,256]{2,1,0:T(8,128)(2,1)S(1)}, u32[]{:S(2)}, u32[]{:S(2)}) collective-permute-start(bf16[2,256,256]{2,1,0:T(8,128)(2,1)S(1)} %get-tuple-element.31), channel_id=1, source_target_pairs={{0,8},{4,12},{8,0},{12,4},{16,24},{20,28},{24,16},{28,20},{1,9},{5... | collective-permute-start | bytes 786440 | tf_op jit(solution)/shard_map/ppermute | solution.py:18
  17.8 39.7 %collective-permute-start.3 = (bf16[1152,256]{1,0:T(8,128)(2,1)S(1)}, bf16[1152,256]{1,0:T(8,128)(2,1)S(1)}, u32[]{:S(2)}, u32[]{:S(2)}) collective-permute-start(bf16[1152,256]{1,0:T(8,128)(2,1)S(1)} %get-tuple-element.28.refs_0_), channel_id=1, source_target_pairs={{0,1},{1,0},{2,3},{3,2},{4,5},{5,4},{6,7},{7,6},{8,9},{9,8},{10,11... | collective-permute-start | bytes 1769480 | tf_op jit(solution)/shard_map/ppermute | solution.py:18
  28.4 29.1 %collective-permute-start.5 = (bf16[1152,256]{1,0:T(8,128)(2,1)S(1)}, bf16[1152,256]{1,0:T(8,128)(2,1)S(1)}, u32[]{:S(2)}, u32[]{:S(2)}) collective-permute-start(bf16[1152,256]{1,0:T(8,128)(2,1)S(1)} %collective-permute-done.4.refs_2_), channel_id=1, source_target_pairs={{0,1},{1,0},{2,3},{3,2},{4,5},{5,4},{6,7},{7,6},{8,9},{9,8},{10,11... | collective-permute-start | bytes 1769480 | tf_op jit(solution)/shard_map/ppermute | solution.py:18
  28.4 15.3 %collective-permute-start.8 = (bf16[2,256,256]{2,1,0:T(8,128)(2,1)S(1)}, bf16[2,256,256]{2,1,0:T(8,128)(2,1)S(1)}, u32[]{:S(2)}, u32[]{:S(2)}) collective-permute-start(bf16[2,256,256]{2,1,0:T(8,128)(2,1)S(1)} %get-tuple-element.32), channel_id=1, source_target_pairs={{0,12},{4,8},{8,4},{12,0},{16,28},{20,24},{24,20},{28,16},{1,13},{... | collective-permute-start | bytes 786440 | tf_op jit(solution)/shard_map/ppermute | solution.py:18
  31.2 21.3 %collective-permute-start.9 = (bf16[2,256,256]{2,1,0:T(8,128)(2,1)S(1)}, bf16[2,256,256]{2,1,0:T(8,128)(2,1)S(1)}, u32[]{:S(2)}, u32[]{:S(2)}) collective-permute-start(bf16[2,256,256]{2,1,0:T(8,128)(2,1)S(1)} %get-tuple-element.29.refs_4_.refs_20_), channel_id=1, source_target_pairs={{0,16},{4,20},{8,24},{12,28},{16,0},{20,4},{24,8},{28,12},{1,17},{... | collective-permute-start | bytes 786440 | tf_op jit(solution)/shard_map/ppermute | solution.py:18
  33.8 23.7 %collective-permute-start.13 = (bf16[2,256,256]{2,1,0:T(8,128)(2,1)S(1)}, bf16[2,256,256]{2,1,0:T(8,128)(2,1)S(1)}, u32[]{:S(2)}, u32[]{:S(2)}) collective-permute-start(bf16[2,256,256]{2,1,0:T(8,128)(2,1)S(1)} %get-tuple-element.36.refs_4_.refs_21_), channel_id=1, source_target_pairs={{0,16},{4,20},{8,24},{12,28},{16,0},{20,4},{24,8},{28,12},{1,17},{... | collective-permute-start | bytes 786440 | tf_op jit(solution)/shard_map/ppermute | solution.py:18
  53.2 10.2 %copy-start.1 = (bf16[3,2,256,512]{3,2,1,0:T(8,128)(2,1)S(1)}, bf16[3,2,256,512]{3,2,1,0:T(8,128)(2,1)}, u32[]{:S(2)}) copy-start(bf16[3,2,256,512]{3,2,1,0:T(8,128)(2,1)} %noise.9) | copy-start | bytes 4718596
  53.2 5.0 %collective-permute-start.10 = (bf16[1,256,256]{2,1,0:T(8,128)(2,1)S(1)}, bf16[1,256,256]{2,1,0:T(8,128)(2,1)S(1)}, u32[]{:S(2)}, u32[]{:S(2)}) collective-permute-start(bf16[1,256,256]{2,1,0:T(8,128)(2,1)S(1)} %get-tuple-element.33), channel_id=1, source_target_pairs={{0,4},{4,0},{8,12},{12,8},{16,20},{20,16},{24,28},{28,24},{1,5},{5... | collective-permute-start | bytes 393224 | tf_op jit(solution)/shard_map/ppermute | solution.py:18
  53.8 6.5 %collective-permute-start.11 = (bf16[1,256,256]{2,1,0:T(8,128)(2,1)S(1)}, bf16[1,256,256]{2,1,0:T(8,128)(2,1)S(1)}, u32[]{:S(2)}, u32[]{:S(2)}) collective-permute-start(bf16[1,256,256]{2,1,0:T(8,128)(2,1)S(1)} %get-tuple-element.34), channel_id=1, source_target_pairs={{0,8},{4,12},{8,0},{12,4},{16,24},{20,28},{24,16},{28,20},{1,9},{5... | collective-permute-start | bytes 393224 | tf_op jit(solution)/shard_map/ppermute | solution.py:18
  57.5 5.9 %collective-permute-start.12 = (bf16[1,256,256]{2,1,0:T(8,128)(2,1)S(1)}, bf16[1,256,256]{2,1,0:T(8,128)(2,1)S(1)}, u32[]{:S(2)}, u32[]{:S(2)}) collective-permute-start(bf16[1,256,256]{2,1,0:T(8,128)(2,1)S(1)} %get-tuple-element.35), channel_id=1, source_target_pairs={{0,12},{4,8},{8,4},{12,0},{16,28},{20,24},{24,20},{28,16},{1,13},{... | collective-permute-start | bytes 393224 | tf_op jit(solution)/shard_map/ppermute | solution.py:18
  65.9 13.5 %collective-permute-start.15 = (bf16[1152,256]{1,0:T(8,128)(2,1)S(1)}, bf16[1152,256]{1,0:T(8,128)(2,1)S(1)}, u32[]{:S(2)}, u32[]{:S(2)}) collective-permute-start(bf16[1152,256]{1,0:T(8,128)(2,1)S(1)} %get-tuple-element.38.refs_0_), channel_id=1, source_target_pairs={{0,2},{1,3},{2,0},{3,1},{4,6},{5,7},{6,4},{7,5},{8,10},{9,11},{10,... | collective-permute-start | bytes 1769480 | tf_op jit(solution)/shard_map/ppermute | solution.py:18
  67.4 11.9 %collective-permute-start.18 = (bf16[1,256,256]{2,1,0:T(8,128)(2,1)S(1)}, bf16[1,256,256]{2,1,0:T(8,128)(2,1)S(1)}, u32[]{:S(2)}, u32[]{:S(2)}) collective-permute-start(bf16[1,256,256]{2,1,0:T(8,128)(2,1)S(1)} %get-tuple-element.39), channel_id=1, source_target_pairs={{0,8},{4,12},{8,0},{12,4},{16,24},{20,28},{24,16},{28,20},{1,9},{5... | collective-permute-start | bytes 393224 | tf_op jit(solution)/shard_map/ppermute | solution.py:18
  67.4 14.1 %collective-permute-start.19 = (bf16[1,256,256]{2,1,0:T(8,128)(2,1)S(1)}, bf16[1,256,256]{2,1,0:T(8,128)(2,1)S(1)}, u32[]{:S(2)}, u32[]{:S(2)}) collective-permute-start(bf16[1,256,256]{2,1,0:T(8,128)(2,1)S(1)} %get-tuple-element.40), channel_id=1, source_target_pairs={{0,12},{4,8},{8,4},{12,0},{16,28},{20,24},{24,20},{28,16},{1,13},{... | collective-permute-start | bytes 393224 | tf_op jit(solution)/shard_map/ppermute | solution.py:18
  70.0 11.5 %collective-permute-start.17 = (bf16[1,256,256]{2,1,0:T(8,128)(2,1)S(1)}, bf16[1,256,256]{2,1,0:T(8,128)(2,1)S(1)}, u32[]{:S(2)}, u32[]{:S(2)}) collective-permute-start(bf16[1,256,256]{2,1,0:T(8,128)(2,1)S(1)} %get-tuple-element.37.refs_12_), channel_id=1, source_target_pairs={{0,4},{4,0},{8,12},{12,8},{16,20},{20,16},{24,28},{28,24},{1,5},{5... | collective-permute-start | bytes 393224 | tf_op jit(solution)/shard_map/ppermute | solution.py:18
  70.9 37.1 %collective-permute-start.14 = (bf16[1152,256]{1,0:T(8,128)(2,1)S(1)}, bf16[1152,256]{1,0:T(8,128)(2,1)S(1)}, u32[]{:S(2)}, u32[]{:S(2)}) collective-permute-start(bf16[1152,256]{1,0:T(8,128)(2,1)S(1)} %get-tuple-element.38.refs_0_), channel_id=1, source_target_pairs={{0,1},{1,0},{2,3},{3,2},{4,5},{5,4},{6,7},{7,6},{8,9},{9,8},{10,11... | collective-permute-start | bytes 1769480 | tf_op jit(solution)/shard_map/ppermute | solution.py:18
  79.4 28.6 %collective-permute-start.16 = (bf16[1152,256]{1,0:T(8,128)(2,1)S(1)}, bf16[1152,256]{1,0:T(8,128)(2,1)S(1)}, u32[]{:S(2)}, u32[]{:S(2)}) collective-permute-start(bf16[1152,256]{1,0:T(8,128)(2,1)S(1)} %collective-permute-done.15.refs_2_), channel_id=1, source_target_pairs={{0,1},{1,0},{2,3},{3,2},{4,5},{5,4},{6,7},{7,6},{8,9},{9,8},{10,11... | collective-permute-start | bytes 1769480 | tf_op jit(solution)/shard_map/ppermute | solution.py:18
  79.4 7.6 %collective-permute-start.21 = (bf16[1,256,256]{2,1,0:T(8,128)(2,1)S(1)}, bf16[1,256,256]{2,1,0:T(8,128)(2,1)S(1)}, u32[]{:S(2)}, u32[]{:S(2)}) collective-permute-start(bf16[1,256,256]{2,1,0:T(8,128)(2,1)S(1)} %get-tuple-element.42), channel_id=1, source_target_pairs={{0,4},{4,0},{8,12},{12,8},{16,20},{20,16},{24,28},{28,24},{1,5},{5... | collective-permute-start | bytes 393224 | tf_op jit(solution)/shard_map/ppermute | solution.py:18
  81.5 8.2 %collective-permute-start.22 = (bf16[1,256,256]{2,1,0:T(8,128)(2,1)S(1)}, bf16[1,256,256]{2,1,0:T(8,128)(2,1)S(1)}, u32[]{:S(2)}, u32[]{:S(2)}) collective-permute-start(bf16[1,256,256]{2,1,0:T(8,128)(2,1)S(1)} %get-tuple-element.43), channel_id=1, source_target_pairs={{0,8},{4,12},{8,0},{12,4},{16,24},{20,28},{24,16},{28,20},{1,9},{5... | collective-permute-start | bytes 393224 | tf_op jit(solution)/shard_map/ppermute | solution.py:18
  81.5 21.4 %collective-permute-start.20 = (bf16[2,256,256]{2,1,0:T(8,128)(2,1)S(1)}, bf16[2,256,256]{2,1,0:T(8,128)(2,1)S(1)}, u32[]{:S(2)}, u32[]{:S(2)}) collective-permute-start(bf16[2,256,256]{2,1,0:T(8,128)(2,1)S(1)} %get-tuple-element.41.refs_12_.refs_22_), channel_id=1, source_target_pairs={{0,16},{4,20},{8,24},{12,28},{16,0},{20,4},{24,8},{28,12},{1,17},{... | collective-permute-start | bytes 786440 | tf_op jit(solution)/shard_map/ppermute | solution.py:18
  87.0 21.0 %collective-permute-start.27 = (bf16[2,256,256]{2,1,0:T(8,128)(2,1)S(1)}, bf16[2,256,256]{2,1,0:T(8,128)(2,1)S(1)}, u32[]{:S(2)}, u32[]{:S(2)}) collective-permute-start(bf16[2,256,256]{2,1,0:T(8,128)(2,1)S(1)} %shard_map.68.refs_0_.refs_12_.refs_23_), channel_id=1, source_target_pairs={{0,16},{4,20},{8,24},{12,28},{16,0},{20,4},{24,8},{28,12},{1,17},{... | collective-permute-start | bytes 786440 | tf_op jit(solution)/shard_map/ppermute | solution.py:18
  89.7 9.3 %collective-permute-start.23 = (bf16[1,256,256]{2,1,0:T(8,128)(2,1)S(1)}, bf16[1,256,256]{2,1,0:T(8,128)(2,1)S(1)}, u32[]{:S(2)}, u32[]{:S(2)}) collective-permute-start(bf16[1,256,256]{2,1,0:T(8,128)(2,1)S(1)} %get-tuple-element.44), channel_id=1, source_target_pairs={{0,12},{4,8},{8,4},{12,0},{16,28},{20,24},{24,20},{28,16},{1,13},{... | collective-permute-start | bytes 393224 | tf_op jit(solution)/shard_map/ppermute | solution.py:18
  103.7 8.1 %collective-permute-start.24 = (bf16[2,256,256]{2,1,0:T(8,128)(2,1)S(1)}, bf16[2,256,256]{2,1,0:T(8,128)(2,1)S(1)}, u32[]{:S(2)}, u32[]{:S(2)}) collective-permute-start(bf16[2,256,256]{2,1,0:T(8,128)(2,1)S(1)} %get-tuple-element.45), channel_id=1, source_target_pairs={{0,4},{4,0},{8,12},{12,8},{16,20},{20,16},{24,28},{28,24},{1,5},{5... | collective-permute-start | bytes 786440 | tf_op jit(solution)/shard_map/ppermute | solution.py:18
  103.8 9.8 %collective-permute-start.25 = (bf16[2,256,256]{2,1,0:T(8,128)(2,1)S(1)}, bf16[2,256,256]{2,1,0:T(8,128)(2,1)S(1)}, u32[]{:S(2)}, u32[]{:S(2)}) collective-permute-start(bf16[2,256,256]{2,1,0:T(8,128)(2,1)S(1)} %get-tuple-element.46), channel_id=1, source_target_pairs={{0,8},{4,12},{8,0},{12,4},{16,24},{20,28},{24,16},{28,20},{1,9},{5... | collective-permute-start | bytes 786440 | tf_op jit(solution)/shard_map/ppermute | solution.py:18
  108.0 12.2 %collective-permute-start.26 = (bf16[2,256,256]{2,1,0:T(8,128)(2,1)S(1)}, bf16[2,256,256]{2,1,0:T(8,128)(2,1)S(1)}, u32[]{:S(2)}, u32[]{:S(2)}) collective-permute-start(bf16[2,256,256]{2,1,0:T(8,128)(2,1)S(1)} %get-tuple-element.47), channel_id=1, source_target_pairs={{0,12},{4,8},{8,4},{12,0},{16,28},{20,24},{24,20},{28,16},{1,13},{... | collective-permute-start | bytes 786440 | tf_op jit(solution)/shard_map/ppermute | solution.py:18
  108.7 13.9 %collective-permute-start.29 = (bf16[1,256,256]{2,1,0:T(8,128)(2,1)S(1)}, bf16[1,256,256]{2,1,0:T(8,128)(2,1)S(1)}, u32[]{:S(2)}, u32[]{:S(2)}) collective-permute-start(bf16[1,256,256]{2,1,0:T(8,128)(2,1)S(1)} %get-tuple-element.49), channel_id=1, source_target_pairs={{0,8},{4,12},{8,0},{12,4},{16,24},{20,28},{24,16},{28,20},{1,9},{5... | collective-permute-start | bytes 393224 | tf_op jit(solution)/shard_map/ppermute | solution.py:18
  110.6 14.0 %collective-permute-start.30 = (bf16[1,256,256]{2,1,0:T(8,128)(2,1)S(1)}, bf16[1,256,256]{2,1,0:T(8,128)(2,1)S(1)}, u32[]{:S(2)}, u32[]{:S(2)}) collective-permute-start(bf16[1,256,256]{2,1,0:T(8,128)(2,1)S(1)} %get-tuple-element.50), channel_id=1, source_target_pairs={{0,12},{4,8},{8,4},{12,0},{16,28},{20,24},{24,20},{28,16},{1,13},{... | collective-permute-start | bytes 393224 | tf_op jit(solution)/shard_map/ppermute | solution.py:18
  111.8 12.8 %collective-permute-start.28 = (bf16[1,256,256]{2,1,0:T(8,128)(2,1)S(1)}, bf16[1,256,256]{2,1,0:T(8,128)(2,1)S(1)}, u32[]{:S(2)}, u32[]{:S(2)}) collective-permute-start(bf16[1,256,256]{2,1,0:T(8,128)(2,1)S(1)} %get-tuple-element.48.refs_20_), channel_id=1, source_target_pairs={{0,4},{4,0},{8,12},{12,8},{16,20},{20,16},{24,28},{28,24},{1,5},{5... | collective-permute-start | bytes 393224 | tf_op jit(solution)/shard_map/ppermute | solution.py:18
  (7 other events, 34.7 us)

commit v9 on v8

--- a/solution.py
+++ b/solution.py
@@ -7,7 +7,7 @@
 from jax.experimental.pallas import tpu as pltpu
 from jax.sharding import PartitionSpec as P
 
-CHUNKS = 2
+CHUNKS = 1
 VMEM = pl.BlockSpec(memory_space=pltpu.VMEM)
 SMEM = pl.BlockSpec(memory_space=pltpu.SMEM)
 ANY = pl.BlockSpec(memory_space=pl.ANY)
@@ -18,14 +18,15 @@
     return lax.ppermute(value, axis, [(at, at ^ step) for at in range(size)])
 
 
-def gather_parts(value, axis, size):
-    parts = {0: value}
-    step = size // 2
+def gather_rows(value, axis, size):
+    steps, step = [0], size // 2
     while step:
-        for have in sorted(parts):
-            parts[have ^ step] = hop(parts[have], axis, size, step)
+        other, others = hop(value, axis, size, step), [have ^ step for have in steps]
+        if step == 1:
+            return [value, other], [steps, others]
+        value, steps = jnp.concatenate([value, other]), steps + others
         step //= 2
-    return [parts[at] for at in range(size)]
+    return [value], [steps]
 
 
 def transposed_dot(left, right):
@@ -36,7 +37,7 @@
     return list(refs[:count]), list(refs[count:])
 
 
-def call(kernel, outs, scratch, small, arrays, out_spec=VMEM, flops=0):
+def call(kernel, outs, scratch, small, arrays, out_spec=VMEM, flops=0, aliases={}):
     size = sum(value.size * value.dtype.itemsize for value in (*arrays, *outs))
     return pl.pallas_call(
         kernel,
@@ -44,40 +45,44 @@
         in_specs=[SMEM] * len(small) + [VMEM] * len(arrays),
         out_specs=[out_spec] * len(outs),
         scratch_shapes=scratch,
+        input_output_aliases=aliases,
         cost_estimate=pl.CostEstimate(flops=flops, bytes_accessed=size, transcendentals=0),
         compiler_params=pltpu.CompilerParams(vmem_limit_bytes=16 * 1024 * 1024),
     )(*small, *arrays)
 
 
-def write_pack(target, level, inverse, coupling):
-    nodes, width, depth = coupling.shape[1:4]
-    rows = inverse.shape[2]
-    for node in range(nodes):
-        for offset in range(width):
-            at = (node * width + offset) * depth
-            target[at:at + depth, :] = coupling[level - 1, node, offset]
-        at = nodes * width * depth + node * rows
-        target[at:at + rows, :] = inverse[level, node]
-
-
-def first_kernel(chunks, draws, picks, noise, inverse, coupling, *refs):
-    *refs, pack, inv = refs
-    parts, refs = take(refs, draws)
-    solved, sends = take(refs, chunks)
+def row_blocks(refs, steps, block):
+    return [
+        (ref, at * block, step)
+        for ref, held in zip(refs, steps, strict=True) for at, step in enumerate(held)
+    ]
+
+
+def fill_inverse(target, found, offset, rows, draw):
+    for ref, at, step in found:
+        start = pl.multiple_of((draw ^ step) * rows, rows)
+        for node in range(target.shape[0]):
+            first = at + offset + node * rows
+            target[node, pl.ds(start, rows), :] = ref[first:first + rows, :]
+
+
+def first_kernel(chunks, steps, picks, noise, *refs):
+    *refs, _, inv = refs
+    parts, refs = take(refs, len(steps))
+    solved, sends = take(refs[1:], chunks)
     myself, draw = lax.axis_index("leaf"), lax.axis_index("draw")
-    nodes, rows = parts[0].shape[:2]
-    wide = solved[0].shape[-1]
-    for step, part in enumerate(parts):
-        inv[:, pl.ds(pl.multiple_of((draw ^ step) * rows, rows), rows), :] = part[...]
+    nodes, wide = noise.shape[0], solved[0].shape[-1]
+    draws = sum(map(len, steps))
+    rows = inv.shape[1] // draws
+    fill_inverse(inv, row_blocks(parts, steps, nodes * rows), 0, rows, draw)
     for at, target in enumerate(solved):
         for node in range(nodes):
-            right = noise[0, node, :, at * wide:(at + 1) * wide]
+            right = noise[node, :, at * wide:(at + 1) * wide]
             target[node] = transposed_dot(inv[node], right).astype(BF16)
     for step, send in enumerate(sends, 1):
         node = picks[0, myself ^ step, myself]
         for at, target in enumerate(solved):
             send[at] = target[node]
-    write_pack(pack, 1, inverse, coupling)
 
 
 def relay_kernel(owners, source, follow, waits, picks, far, *refs):
@@ -92,26 +97,26 @@
 
 
 def level_kernel(
-    level, owners, draws, width, chunk, places, sides, earlier, waits, packing,
+    level, owners, steps, width, chunk, places, sides, earlier, waits, packing,
     picks, lists, counts, noise, *refs,
 ):
     half = owners // 2
-    packs, refs = take(refs, draws)
+    packs, refs = take(refs, len(steps))
     known, refs = take(refs, level * owners)
     done, refs = take(refs, earlier)
     _, refs = take(refs, waits)
     if packing:
-        inverse, coupling, *refs = refs
+        refs = refs[1:]
     target, *refs = refs
     sends, refs = take(refs, sides)
     if packing:
-        write_pack(refs[0], level + 1, inverse, coupling)
         refs = refs[1:]
     table, inv, *refs = refs
     myself, draw = lax.axis_index("leaf"), lax.axis_index("draw")
     nodes, wide = noise.shape[1], table.shape[-1]
     depth = inv.shape[1]
-    rows = depth // draws
+    rows = depth // sum(map(len, steps))
+    found = row_blocks(packs, steps, nodes * (width * depth + rows))
     copies = []
     solved = target
     if earlier:
@@ -128,19 +133,15 @@
         table[at] = ref[place]
     empty = level * owners
     table[empty] = jnp.zeros_like(table[empty])
-    for step, pack in enumerate(packs):
-        start = pl.multiple_of((draw ^ step) * rows, rows)
-        for node in range(nodes):
-            at = nodes * width * depth + node * rows
-            inv[node, pl.ds(start, rows), :] = pack[at:at + rows, :]
+    fill_inverse(inv, found, nodes * width * depth, rows, draw)
     for node in range(nodes):
         total = None
-        for step, pack in enumerate(packs):
+        for pack, start, step in found:
             for offset in range(width):
                 slot = (draw ^ step) * width + offset
                 live = slot < counts[level - 1, node]
                 entry = jnp.where(live, lists[level - 1, node, slot] ^ myself, empty)
-                at = (node * width + offset) * depth
+                at = start + (node * width + offset) * depth
                 term = transposed_dot(pack[at:at + depth, :], table[entry])
                 total = term if total is None else total + term
         side = noise[level, node, :, chunk * wide:(chunk + 1) * wide].astype(F32) - total
@@ -161,30 +162,37 @@
     width, last_level = coupling.shape[2], levels - 1
     shape = lambda *dims: jax.ShapeDtypeStruct(dims, BF16)
     part = shape(nodes, rows, wide)
-    pack_shape = shape(nodes * (width * rows + inverse.shape[2]), rows)
+    flat = lambda value: value.reshape(-1, rows)
+    raw = [
+        jnp.concatenate([flat(coupling[level - 1]), flat(inverse[level])])
+        for level in range(1, levels)
+    ]
+    pack_shape = shape(*raw[0].shape)
     leaf = lambda value, step: hop(value, "leaf", owners, step)
     near = lambda values: [leaf(value, step) for step, value in enumerate(values, 1)]
-    gather = lambda value: gather_parts(value, "draw", draws)
+    gather = lambda value: gather_rows(value, "draw", draws)
     inv_here = pltpu.VMEM((nodes, rows, rows), BF16)
     dot_flops = 2 * rows * rows * wide
 
+    parts, steps = gather(flat(inverse[0]))
     *refs, pack = call(
-        functools.partial(first_kernel, CHUNKS, draws),
+        functools.partial(first_kernel, CHUNKS, steps),
         [part] * CHUNKS + [shape(CHUNKS, rows, wide)] * (half - 1) + [pack_shape],
         [inv_here],
         (picks,),
-        (noise, inverse, coupling, *gather(inverse[0])),
+        (noise[0], *parts, raw[0]),
         flops=nodes * CHUNKS * dot_flops,
+        aliases={2 + len(parts): CHUNKS + half - 1},
     )
     solved, sends = take(refs, CHUNKS)
-    packs = [gather(pack)]
+    packs = [gather(pack)[0]]
     done, pieces = [solved], []
     for level in range(1, levels):
         source = level - 1
         far = [leaf(value, half) for value in solved]
         got = near(sends)
         close = [[(ref, at) for ref in got] for at in chunks] if source == 0 else [[(ref, 0) for ref in got]]
-        distant, waits = [], got
+        distant, waits = [], got + packs[source][:1]
         for at in chunks:
             follow = source > 0 and at < CHUNKS - 1
             sends = call(
@@ -198,7 +206,7 @@
             distant.append([(ref, 0) for ref in got])
             if follow:
                 close.append([(ref, 1) for ref in got])
-            waits = packs[source]
+            waits = []
         pieces.append([
             [(solved[at], 0), *close[at], (far[at], 0), *distant[at]] for at in chunks
         ])
@@ -218,7 +226,7 @@
                 ]
             here, *sent = call(
                 functools.partial(
-                    level_kernel, level, owners, draws, width, at,
+                    level_kernel, level, owners, steps, width, at,
                     [place for _, place in known], sides, len(earlier), len(waits), packing,
                 ),
                 [shape(levels, nodes, rows, columns) if final else part]
@@ -226,13 +234,16 @@
                 scratch,
                 (picks, lists, counts),
                 (noise, *packs[level - 1], *(ref for ref, _ in known), *earlier, *waits)
-                + ((inverse, coupling) if packing else ()),
+                + ((raw[level],) if packing else ()),
                 out_spec=ANY if final else VMEM,
+                aliases={
+                    4 + len(packs[level - 1]) + len(known) + len(earlier) + len(waits): 1 + sides
+                } if packing else {},
                 flops=nodes * (draws * width + 1) * dot_flops,
             )
             solved.append(here)
             if packing:
-                packs.append(gather(sent.pop()))
+                packs.append(gather(sent.pop())[0])
             sends += sent
             waits = []
         done.append(solved)

time: 128 us -> 131 us (1.023)
  waiting for transfers between devices: 79.4 us -> 92.4 us
  Pallas kernels: 14.5 us -> 8.61 us
  local copies, waits for them, and re-layouts: 5.12 us -> 2.52 us
  starting transfers between devices: 28.6 us -> 26.9 us
    ppermute x31 -> x20, waiting for transfers between devices: 79.4 us -> 92.4 us  [hop(): return lax.ppermute(value, axis, [(at, at ^ step) for at in range(size)])]
    pallas_call x9 -> x5, Pallas kernels: 14.5 us -> 8.61 us  [call(): pl.pallas_call(kernel, out_shape=outs, in_specs=[SMEM] * len(small) + [VM...]
    unnamed x16 -> x10, local copies, waits for them, and re-layouts: 4.28 us -> 0.1 us
    slice x0 -> x2, local copies, waits for them, and re-layouts: none -> 2.3 us  [the longest x1 1.27 us: on_device(): coupling[level - 1]]
    ppermute x31 -> x20, starting transfers between devices: 28.6 us -> 26.9 us  [hop(): return lax.ppermute(value, axis, [(at, at ^ step) for at in range(size)])]
  transfers between devices with their start and end apart: 31 -> 20, of which waited for: 16 -> 16; matrix products, arithmetic and copies ran while one was open for 0% -> 1% of each run, Pallas kernels for 6% -> 1%
where the time goes in v9:
time: 131 us
  waiting for transfers between devices  92.4 us (71%)
  starting transfers between devices  26.9 us (21%)
  Pallas kernels  8.61 us (7%)
  local copies, waits for them, and re-layouts  2.52 us (2%)
    ppermute x20, waiting for transfers between devices, hop(): return lax.ppermute(value, axis, [(at, at ^ step) for at in range(size)])  92.4 us
    ppermute x20, starting transfers between devices, hop(): return lax.ppermute(value, axis, [(at, at ^ step) for at in range(size)])  26.9 us
    pallas_call x5, Pallas kernels, call(): pl.pallas_call(kernel, out_shape=outs, in_specs=[SMEM] * len(small) + [VM...  8.61 us
  transfers between devices with their start and end apart: 20, of which 16 were waited for; matrix products, arithmetic and copies ran while one was open for 1% of the time, Pallas kernels for 1%

profile of v9, /device:TPU:0, one launch (start us, length us, event | category | flops | bytes accessed | tf_op | source)
XLA Modules:
  0.0 130.6 jit_solution(131136354678493560)
XLA Ops:
  0.0 1.0 fusion.1
  1.0 3.0 %collective-permute-start = (bf16[128,256]{1,0:T(8,128)(2,1)S(1)}, bf16[128,256]{1,0:T(8,128)(2,1)S(1)}, u32[]{:S(2)}, u32[]{:S(2)}) collective-permute-start(bf16[128,256]{1,0:T(8,128)(2,1)S(1)} %bitcast.11), channel_id=1, source_target_pairs={{0,2},{1,3},{2,0},{3,1},{4,6},{5,7},{6,4},{7,5},{8,10},{9,11},{10,... | collective-permute-start | bytes 196616 | tf_op jit(solution)/shard_map/ppermute | solution.py:18
  4.0 1.3 fusion
  6.4 1.3 collective-permute-done.1.refs_1_
  7.7 1.1 shard_map.64
  8.8 2.1 %collective-permute-start.2 = (bf16[1152,256]{1,0:T(8,128)(2,1)S(1)}, bf16[1152,256]{1,0:T(8,128)(2,1)S(1)}, u32[]{:S(2)}, u32[]{:S(2)}) collective-permute-start(bf16[1152,256]{1,0:T(8,128)(2,1)S(1)} %get-tuple-element.21), channel_id=1, source_target_pairs={{0,2},{1,3},{2,0},{3,1},{4,6},{5,7},{6,4},{7,5},{8,10},{9,11},{10,... | collective-permute-start | bytes 1769480 | tf_op jit(solution)/shard_map/ppermute | solution.py:18
  10.9 13.6 %collective-permute-done.2 = bf16[1152,256]{1,0:T(8,128)(2,1)S(1)} collective-permute-done((bf16[1152,256]{1,0:T(8,128)(2,1)S(1)}, bf16[1152,256]{1,0:T(8,128)(2,1)S(1)}, u32[]{:S(2)}, u32[]{:S(2)}) %collective-permute-start.2) | collective-permute-done | bytes 589856 | tf_op jit(solution)/shard_map/ppermute | solution.py:18
  24.6 2.9 %collective-permute-start.7 = (bf16[2,256,512]{2,1,0:T(8,128)(2,1)S(1)}, bf16[2,256,512]{2,1,0:T(8,128)(2,1)S(1)}, u32[]{:S(2)}, u32[]{:S(2)}) collective-permute-start(bf16[2,256,512]{2,1,0:T(8,128)(2,1)S(1)} %get-tuple-element.22.refs_2_.refs_18_), channel_id=1, source_target_pairs={{0,16},{4,20},{8,24},{12,28},{16,0},{20,4},{24,8},{28,12},{1,17},{... | collective-permute-start | bytes 1572872 | tf_op jit(solution)/shard_map/ppermute | solution.py:18
  27.5 1.5 %collective-permute-start.4 = (bf16[1,256,512]{2,1,0:T(8,128)(2,1)S(1)}, bf16[1,256,512]{2,1,0:T(8,128)(2,1)S(1)}, u32[]{:S(2)}, u32[]{:S(2)}) collective-permute-start(bf16[1,256,512]{2,1,0:T(8,128)(2,1)S(1)} %get-tuple-element.23), channel_id=1, source_target_pairs={{0,4},{4,0},{8,12},{12,8},{16,20},{20,16},{24,28},{28,24},{1,5},{5... | collective-permute-start | bytes 786440 | tf_op jit(solution)/shard_map/ppermute | solution.py:18
  29.1 1.6 %collective-permute-start.5 = (bf16[1,256,512]{2,1,0:T(8,128)(2,1)S(1)}, bf16[1,256,512]{2,1,0:T(8,128)(2,1)S(1)}, u32[]{:S(2)}, u32[]{:S(2)}) collective-permute-start(bf16[1,256,512]{2,1,0:T(8,128)(2,1)S(1)} %get-tuple-element.24), channel_id=1, source_target_pairs={{0,8},{4,12},{8,0},{12,4},{16,24},{20,28},{24,16},{28,20},{1,9},{5... | collective-permute-start | bytes 786440 | tf_op jit(solution)/shard_map/ppermute | solution.py:18
  31.0 4.9 %collective-permute-done.4.refs_0_.refs_3_ = bf16[1,256,512]{2,1,0:T(8,128)(2,1)S(1)} collective-permute-done((bf16[1,256,512]{2,1,0:T(8,128)(2,1)S(1)}, bf16[1,256,512]{2,1,0:T(8,128)(2,1)S(1)}, u32[]{:S(2)}, u32[]{:S(2)}) %collective-permute-start.4) | collective-permute-done | bytes 262176 | tf_op jit(solution)/shard_map/ppermute | solution.py:18
  35.9 9.5 %collective-permute-done.5.refs_1_.refs_4_ = bf16[1,256,512]{2,1,0:T(8,128)(2,1)S(1)} collective-permute-done((bf16[1,256,512]{2,1,0:T(8,128)(2,1)S(1)}, bf16[1,256,512]{2,1,0:T(8,128)(2,1)S(1)}, u32[]{:S(2)}, u32[]{:S(2)}) %collective-permute-start.5) | collective-permute-done | bytes 262176 | tf_op jit(solution)/shard_map/ppermute | solution.py:18
  45.5 7.4 %collective-permute-done.6.refs_2_.refs_5_ = bf16[1,256,512]{2,1,0:T(8,128)(2,1)S(1)} collective-permute-done((bf16[1,256,512]{2,1,0:T(8,128)(2,1)S(1)}, bf16[1,256,512]{2,1,0:T(8,128)(2,1)S(1)}, u32[]{:S(2)}, u32[]{:S(2)}) %collective-permute-start.6) | collective-permute-done | bytes 262176 | tf_op jit(solution)/shard_map/ppermute | solution.py:18
  53.6 1.3 collective-permute-start.9
  54.9 1.7 %collective-permute-start.10 = (bf16[1,256,512]{2,1,0:T(8,128)(2,1)S(1)}, bf16[1,256,512]{2,1,0:T(8,128)(2,1)S(1)}, u32[]{:S(2)}, u32[]{:S(2)}) collective-permute-start(bf16[1,256,512]{2,1,0:T(8,128)(2,1)S(1)} %get-tuple-element.28), channel_id=1, source_target_pairs={{0,12},{4,8},{8,4},{12,0},{16,28},{20,24},{24,20},{28,16},{1,13},{... | collective-permute-start | bytes 786440 | tf_op jit(solution)/shard_map/ppermute | solution.py:18
  57.2 5.7 %collective-permute-done.9.refs_8_ = bf16[1,256,512]{2,1,0:T(8,128)(2,1)S(1)} collective-permute-done((bf16[1,256,512]{2,1,0:T(8,128)(2,1)S(1)}, bf16[1,256,512]{2,1,0:T(8,128)(2,1)S(1)}, u32[]{:S(2)}, u32[]{:S(2)}) %collective-permute-start.9) | collective-permute-done | bytes 262176 | tf_op jit(solution)/shard_map/ppermute | solution.py:18
  62.9 4.6 %collective-permute-done.10.refs_9_ = bf16[1,256,512]{2,1,0:T(8,128)(2,1)S(1)} collective-permute-done((bf16[1,256,512]{2,1,0:T(8,128)(2,1)S(1)}, bf16[1,256,512]{2,1,0:T(8,128)(2,1)S(1)}, u32[]{:S(2)}, u32[]{:S(2)}) %collective-permute-start.10) | collective-permute-done | bytes 262176 | tf_op jit(solution)/shard_map/ppermute | solution.py:18
  67.5 1.4 %collective-permute-done.8.refs_7_ = bf16[1,256,512]{2,1,0:T(8,128)(2,1)S(1)} collective-permute-done((bf16[1,256,512]{2,1,0:T(8,128)(2,1)S(1)}, bf16[1,256,512]{2,1,0:T(8,128)(2,1)S(1)}, u32[]{:S(2)}, u32[]{:S(2)}) %collective-permute-start.8) | collective-permute-done | bytes 262176 | tf_op jit(solution)/shard_map/ppermute | solution.py:18
  68.9 2.6 %shard_map.66 = (bf16[2,256,512]{2,1,0:T(8,128)(2,1)S(1)}, bf16[1,256,512]{2,1,0:T(8,128)(2,1)S(1)}, bf16[1,256,512]{2,1,0:T(8,128)(2,1)S(1)}, bf16[1,256,512]{2,1,0:T(8,128)(2,1)S(1)}, bf16[1152,256]{1,0:T(8,128)(2,1)S(1)}) custom-call(s32[2,8,8]{2,1,0:T(8,128)S(1)} %copy-done.1, s32[2,2,8]{2,1,0:T(2,128)S(1)} %copy-done.2, ...), custom_call_target="tpu_custom_call", output_to_operand_aliasing={{4}: (15, {})} | custom-call | flops 1207959552 | bytes 9306112 | tf_op jit(solution)/shard_map/pallas_call | solution.py:42
  71.5 1.6 %collective-permute-start.11 = (bf16[1152,256]{1,0:T(8,128)(2,1)S(1)}, bf16[1152,256]{1,0:T(8,128)(2,1)S(1)}, u32[]{:S(2)}, u32[]{:S(2)}) collective-permute-start(bf16[1152,256]{1,0:T(8,128)(2,1)S(1)} %get-tuple-element.29), channel_id=1, source_target_pairs={{0,2},{1,3},{2,0},{3,1},{4,6},{5,7},{6,4},{7,5},{8,10},{9,11},{10,... | collective-permute-start | bytes 1769480 | tf_op jit(solution)/shard_map/ppermute | solution.py:18
  73.2 10.3 %collective-permute-done.11 = bf16[1152,256]{1,0:T(8,128)(2,1)S(1)} collective-permute-done((bf16[1152,256]{1,0:T(8,128)(2,1)S(1)}, bf16[1152,256]{1,0:T(8,128)(2,1)S(1)}, u32[]{:S(2)}, u32[]{:S(2)}) %collective-permute-start.11) | collective-permute-done | bytes 589856 | tf_op jit(solution)/shard_map/ppermute | solution.py:18
  83.6 3.0 %collective-permute-start.16 = (bf16[2,256,512]{2,1,0:T(8,128)(2,1)S(1)}, bf16[2,256,512]{2,1,0:T(8,128)(2,1)S(1)}, u32[]{:S(2)}, u32[]{:S(2)}) collective-permute-start(bf16[2,256,512]{2,1,0:T(8,128)(2,1)S(1)} %get-tuple-element.30.refs_10_.refs_19_), channel_id=1, source_target_pairs={{0,16},{4,20},{8,24},{12,28},{16,0},{20,4},{24,8},{28,12},{1,17},{... | collective-permute-start | bytes 1572872 | tf_op jit(solution)/shard_map/ppermute | solution.py:18
  87.0 1.9 %collective-permute-start.14 = (bf16[1,256,512]{2,1,0:T(8,128)(2,1)S(1)}, bf16[1,256,512]{2,1,0:T(8,128)(2,1)S(1)}, u32[]{:S(2)}, u32[]{:S(2)}) collective-permute-start(bf16[1,256,512]{2,1,0:T(8,128)(2,1)S(1)} %get-tuple-element.32), channel_id=1, source_target_pairs={{0,8},{4,12},{8,0},{12,4},{16,24},{20,28},{24,16},{28,20},{1,9},{5... | collective-permute-start | bytes 786440 | tf_op jit(solution)/shard_map/ppermute | solution.py:18
  89.0 1.1 collective-permute-start.15
  90.1 4.9 %collective-permute-done.13.refs_0_.refs_11_ = bf16[1,256,512]{2,1,0:T(8,128)(2,1)S(1)} collective-permute-done((bf16[1,256,512]{2,1,0:T(8,128)(2,1)S(1)}, bf16[1,256,512]{2,1,0:T(8,128)(2,1)S(1)}, u32[]{:S(2)}, u32[]{:S(2)}) %collective-permute-start.13) | collective-permute-done | bytes 262176 | tf_op jit(solution)/shard_map/ppermute | solution.py:18
  95.0 9.5 %collective-permute-done.14.refs_1_.refs_12_ = bf16[1,256,512]{2,1,0:T(8,128)(2,1)S(1)} collective-permute-done((bf16[1,256,512]{2,1,0:T(8,128)(2,1)S(1)}, bf16[1,256,512]{2,1,0:T(8,128)(2,1)S(1)}, u32[]{:S(2)}, u32[]{:S(2)}) %collective-permute-start.14) | collective-permute-done | bytes 262176 | tf_op jit(solution)/shard_map/ppermute | solution.py:18
  104.5 6.7 %collective-permute-done.15.refs_2_.refs_13_ = bf16[1,256,512]{2,1,0:T(8,128)(2,1)S(1)} collective-permute-done((bf16[1,256,512]{2,1,0:T(8,128)(2,1)S(1)}, bf16[1,256,512]{2,1,0:T(8,128)(2,1)S(1)}, u32[]{:S(2)}, u32[]{:S(2)}) %collective-permute-start.15) | collective-permute-done | bytes 262176 | tf_op jit(solution)/shard_map/ppermute | solution.py:18
  112.8 2.1 %collective-permute-start.19 = (bf16[1,256,512]{2,1,0:T(8,128)(2,1)S(1)}, bf16[1,256,512]{2,1,0:T(8,128)(2,1)S(1)}, u32[]{:S(2)}, u32[]{:S(2)}) collective-permute-start(bf16[1,256,512]{2,1,0:T(8,128)(2,1)S(1)} %get-tuple-element.36), channel_id=1, source_target_pairs={{0,12},{4,8},{8,4},{12,0},{16,28},{20,24},{24,20},{28,16},{1,13},{... | collective-permute-start | bytes 786440 | tf_op jit(solution)/shard_map/ppermute | solution.py:18
  115.5 5.8 %collective-permute-done.18.refs_16_ = bf16[1,256,512]{2,1,0:T(8,128)(2,1)S(1)} collective-permute-done((bf16[1,256,512]{2,1,0:T(8,128)(2,1)S(1)}, bf16[1,256,512]{2,1,0:T(8,128)(2,1)S(1)}, u32[]{:S(2)}, u32[]{:S(2)}) %collective-permute-start.18) | collective-permute-done | bytes 262176 | tf_op jit(solution)/shard_map/ppermute | solution.py:18
  121.2 4.5 %collective-permute-done.19.refs_17_ = bf16[1,256,512]{2,1,0:T(8,128)(2,1)S(1)} collective-permute-done((bf16[1,256,512]{2,1,0:T(8,128)(2,1)S(1)}, bf16[1,256,512]{2,1,0:T(8,128)(2,1)S(1)}, u32[]{:S(2)}, u32[]{:S(2)}) %collective-permute-start.19) | collective-permute-done | bytes 262176 | tf_op jit(solution)/shard_map/ppermute | solution.py:18
  125.7 1.4 %collective-permute-done.17.refs_15_ = bf16[1,256,512]{2,1,0:T(8,128)(2,1)S(1)} collective-permute-done((bf16[1,256,512]{2,1,0:T(8,128)(2,1)S(1)}, bf16[1,256,512]{2,1,0:T(8,128)(2,1)S(1)}, u32[]{:S(2)}, u32[]{:S(2)}) %collective-permute-start.17) | collective-permute-done | bytes 262176 | tf_op jit(solution)/shard_map/ppermute | solution.py:18
  127.1 3.5 %shard_map.68 = bf16[3,2,256,512]{3,2,1,0:T(8,128)(2,1)} custom-call(s32[2,8,8]{2,1,0:T(8,128)S(1)} %copy-done.1, s32[2,2,8]{2,1,0:T(2,128)S(1)} %copy-done.2, s32[2,2]{1,0:T(2,128)S(1)} %copy-done.3, bf16[3,2,256,512]{3,2,1,0:T(8,128)(2,1)S(1)} %copy-done, bf16[2304,256]{1,0:T(8,128)(2,1)S(1)} %constant_dynamic-update-slice_fusion.2.refs_3_.refs_0_, ...), custom_call_target="tpu_custom_call" | custom-call | flops 1207959552 | bytes 12058624 | tf_op jit(solution)/shard_map/pallas_call | solution.py:42
  (31 shorter events, 5.8 us)
Async XLA Ops:
  0.0 5.3 %copy-start = (bf16[3,2,256,512]{3,2,1,0:T(8,128)(2,1)S(1)}, bf16[3,2,256,512]{3,2,1,0:T(8,128)(2,1)}, u32[]{:S(2)}) copy-start(bf16[3,2,256,512]{3,2,1,0:T(8,128)(2,1)} %noise.3) | copy-start | bytes 4718596
  1.0 5.2 %collective-permute-start = (bf16[128,256]{1,0:T(8,128)(2,1)S(1)}, bf16[128,256]{1,0:T(8,128)(2,1)S(1)}, u32[]{:S(2)}, u32[]{:S(2)}) collective-permute-start(bf16[128,256]{1,0:T(8,128)(2,1)S(1)} %bitcast.11), channel_id=1, source_target_pairs={{0,2},{1,3},{2,0},{3,1},{4,6},{5,7},{6,4},{7,5},{8,10},{9,11},{10,... | collective-permute-start | bytes 196616 | tf_op jit(solution)/shard_map/ppermute | solution.py:18
  5.3 2.4 %copy-start.1 = (s32[2,8,8]{2,1,0:T(8,128)S(1)}, s32[2,8,8]{2,1,0:T(8,128)}, u32[]{:S(2)}) copy-start(s32[2,8,8]{2,1,0:T(8,128)} %picks.9) | copy-start | bytes 1540
  6.3 1.4 %collective-permute-start.1 = (bf16[256,256]{1,0:T(8,128)(2,1)S(1)}, bf16[256,256]{1,0:T(8,128)(2,1)S(1)}, u32[]{:S(2)}, u32[]{:S(2)}) collective-permute-start(bf16[256,256]{1,0:T(8,128)(2,1)S(1)} %pad_maximum_fusion.2.refs_0_), channel_id=1, source_target_pairs={{0,1},{1,0},{2,3},{3,2},{4,5},{5,4},{6,7},{7,6},{8,9},{9,8},{10,11... | collective-permute-start | bytes 393224 | tf_op jit(solution)/shard_map/ppermute | solution.py:18
  8.8 15.7 %collective-permute-start.2 = (bf16[1152,256]{1,0:T(8,128)(2,1)S(1)}, bf16[1152,256]{1,0:T(8,128)(2,1)S(1)}, u32[]{:S(2)}, u32[]{:S(2)}) collective-permute-start(bf16[1152,256]{1,0:T(8,128)(2,1)S(1)} %get-tuple-element.21), channel_id=1, source_target_pairs={{0,2},{1,3},{2,0},{3,1},{4,6},{5,7},{6,4},{7,5},{8,10},{9,11},{10,... | collective-permute-start | bytes 1769480 | tf_op jit(solution)/shard_map/ppermute | solution.py:18
  24.6 44.3 %collective-permute-start.3 = (bf16[2304,256]{1,0:T(8,128)(2,1)S(1)}, bf16[2304,256]{1,0:T(8,128)(2,1)S(1)}, u32[]{:S(2)}, u32[]{:S(2)}) collective-permute-start(bf16[2304,256]{1,0:T(8,128)(2,1)S(1)} %constant_dynamic-update-slice_fusion.refs_3_.refs_0_), channel_id=1, source_target_pairs={{0,1},{1,0},{2,3},{3,2},{4,5},{5,4},{6,7},{7,6},{8,9},{9,8},{10,11... | collective-permute-start | bytes 3538952 | tf_op jit(solution)/shard_map/ppermute | solution.py:18
  24.6 28.2 %collective-permute-start.7 = (bf16[2,256,512]{2,1,0:T(8,128)(2,1)S(1)}, bf16[2,256,512]{2,1,0:T(8,128)(2,1)S(1)}, u32[]{:S(2)}, u32[]{:S(2)}) collective-permute-start(bf16[2,256,512]{2,1,0:T(8,128)(2,1)S(1)} %get-tuple-element.22.refs_2_.refs_18_), channel_id=1, source_target_pairs={{0,16},{4,20},{8,24},{12,28},{16,0},{20,4},{24,8},{28,12},{1,17},{... | collective-permute-start | bytes 1572872 | tf_op jit(solution)/shard_map/ppermute | solution.py:18
  27.5 8.4 %collective-permute-start.4 = (bf16[1,256,512]{2,1,0:T(8,128)(2,1)S(1)}, bf16[1,256,512]{2,1,0:T(8,128)(2,1)S(1)}, u32[]{:S(2)}, u32[]{:S(2)}) collective-permute-start(bf16[1,256,512]{2,1,0:T(8,128)(2,1)S(1)} %get-tuple-element.23), channel_id=1, source_target_pairs={{0,4},{4,0},{8,12},{12,8},{16,20},{20,16},{24,28},{28,24},{1,5},{5... | collective-permute-start | bytes 786440 | tf_op jit(solution)/shard_map/ppermute | solution.py:18
  29.1 16.4 %collective-permute-start.5 = (bf16[1,256,512]{2,1,0:T(8,128)(2,1)S(1)}, bf16[1,256,512]{2,1,0:T(8,128)(2,1)S(1)}, u32[]{:S(2)}, u32[]{:S(2)}) collective-permute-start(bf16[1,256,512]{2,1,0:T(8,128)(2,1)S(1)} %get-tuple-element.24), channel_id=1, source_target_pairs={{0,8},{4,12},{8,0},{12,4},{16,24},{20,28},{24,16},{28,20},{1,9},{5... | collective-permute-start | bytes 786440 | tf_op jit(solution)/shard_map/ppermute | solution.py:18
  30.6 22.2 %collective-permute-start.6 = (bf16[1,256,512]{2,1,0:T(8,128)(2,1)S(1)}, bf16[1,256,512]{2,1,0:T(8,128)(2,1)S(1)}, u32[]{:S(2)}, u32[]{:S(2)}) collective-permute-start(bf16[1,256,512]{2,1,0:T(8,128)(2,1)S(1)} %get-tuple-element.25), channel_id=1, source_target_pairs={{0,12},{4,8},{8,4},{12,0},{16,28},{20,24},{24,20},{28,16},{1,13},{... | collective-permute-start | bytes 786440 | tf_op jit(solution)/shard_map/ppermute | solution.py:18
  53.6 15.3 %copy-start.2 = (s32[2,2,8]{2,1,0:T(2,128)S(1)}, s32[2,2,8]{2,1,0:T(2,128)}, u32[]{:S(2)}) copy-start(s32[2,2,8]{2,1,0:T(2,128)} %lists.3) | copy-start | bytes 388
  53.6 15.3 %copy-start.3 = (s32[2,2]{1,0:T(2,128)S(1)}, s32[2,2]{1,0:T(2,128)}, u32[]{:S(2)}) copy-start(s32[2,2]{1,0:T(2,128)} %counts.3) | copy-start | bytes 52
  53.6 9.3 %collective-permute-start.9 = (bf16[1,256,512]{2,1,0:T(8,128)(2,1)S(1)}, bf16[1,256,512]{2,1,0:T(8,128)(2,1)S(1)}, u32[]{:S(2)}, u32[]{:S(2)}) collective-permute-start(bf16[1,256,512]{2,1,0:T(8,128)(2,1)S(1)} %get-tuple-element.27), channel_id=1, source_target_pairs={{0,8},{4,12},{8,0},{12,4},{16,24},{20,28},{24,16},{28,20},{1,9},{5... | collective-permute-start | bytes 786440 | tf_op jit(solution)/shard_map/ppermute | solution.py:18
  54.9 12.6 %collective-permute-start.10 = (bf16[1,256,512]{2,1,0:T(8,128)(2,1)S(1)}, bf16[1,256,512]{2,1,0:T(8,128)(2,1)S(1)}, u32[]{:S(2)}, u32[]{:S(2)}) collective-permute-start(bf16[1,256,512]{2,1,0:T(8,128)(2,1)S(1)} %get-tuple-element.28), channel_id=1, source_target_pairs={{0,12},{4,8},{8,4},{12,0},{16,28},{20,24},{24,20},{28,16},{1,13},{... | collective-permute-start | bytes 786440 | tf_op jit(solution)/shard_map/ppermute | solution.py:18
  56.6 12.3 %collective-permute-start.8 = (bf16[1,256,512]{2,1,0:T(8,128)(2,1)S(1)}, bf16[1,256,512]{2,1,0:T(8,128)(2,1)S(1)}, u32[]{:S(2)}, u32[]{:S(2)}) collective-permute-start(bf16[1,256,512]{2,1,0:T(8,128)(2,1)S(1)} %get-tuple-element.26.refs_10_), channel_id=1, source_target_pairs={{0,4},{4,0},{8,12},{12,8},{16,20},{20,16},{24,28},{28,24},{1,5},{5... | collective-permute-start | bytes 786440 | tf_op jit(solution)/shard_map/ppermute | solution.py:18
  71.5 12.0 %collective-permute-start.11 = (bf16[1152,256]{1,0:T(8,128)(2,1)S(1)}, bf16[1152,256]{1,0:T(8,128)(2,1)S(1)}, u32[]{:S(2)}, u32[]{:S(2)}) collective-permute-start(bf16[1152,256]{1,0:T(8,128)(2,1)S(1)} %get-tuple-element.29), channel_id=1, source_target_pairs={{0,2},{1,3},{2,0},{3,1},{4,6},{5,7},{6,4},{7,5},{8,10},{9,11},{10,... | collective-permute-start | bytes 1769480 | tf_op jit(solution)/shard_map/ppermute | solution.py:18
  83.5 43.6 %collective-permute-start.12 = (bf16[2304,256]{1,0:T(8,128)(2,1)S(1)}, bf16[2304,256]{1,0:T(8,128)(2,1)S(1)}, u32[]{:S(2)}, u32[]{:S(2)}) collective-permute-start(bf16[2304,256]{1,0:T(8,128)(2,1)S(1)} %constant_dynamic-update-slice_fusion.2.refs_3_.refs_0_), channel_id=1, source_target_pairs={{0,1},{1,0},{2,3},{3,2},{4,5},{5,4},{6,7},{7,6},{8,9},{9,8},{10,11... | collective-permute-start | bytes 3538952 | tf_op jit(solution)/shard_map/ppermute | solution.py:18
  83.6 27.6 %collective-permute-start.16 = (bf16[2,256,512]{2,1,0:T(8,128)(2,1)S(1)}, bf16[2,256,512]{2,1,0:T(8,128)(2,1)S(1)}, u32[]{:S(2)}, u32[]{:S(2)}) collective-permute-start(bf16[2,256,512]{2,1,0:T(8,128)(2,1)S(1)} %get-tuple-element.30.refs_10_.refs_19_), channel_id=1, source_target_pairs={{0,16},{4,20},{8,24},{12,28},{16,0},{20,4},{24,8},{28,12},{1,17},{... | collective-permute-start | bytes 1572872 | tf_op jit(solution)/shard_map/ppermute | solution.py:18
  86.6 8.4 %collective-permute-start.13 = (bf16[1,256,512]{2,1,0:T(8,128)(2,1)S(1)}, bf16[1,256,512]{2,1,0:T(8,128)(2,1)S(1)}, u32[]{:S(2)}, u32[]{:S(2)}) collective-permute-start(bf16[1,256,512]{2,1,0:T(8,128)(2,1)S(1)} %get-tuple-element.31), channel_id=1, source_target_pairs={{0,4},{4,0},{8,12},{12,8},{16,20},{20,16},{24,28},{28,24},{1,5},{5... | collective-permute-start | bytes 786440 | tf_op jit(solution)/shard_map/ppermute | solution.py:18
  87.0 17.4 %collective-permute-start.14 = (bf16[1,256,512]{2,1,0:T(8,128)(2,1)S(1)}, bf16[1,256,512]{2,1,0:T(8,128)(2,1)S(1)}, u32[]{:S(2)}, u32[]{:S(2)}) collective-permute-start(bf16[1,256,512]{2,1,0:T(8,128)(2,1)S(1)} %get-tuple-element.32), channel_id=1, source_target_pairs={{0,8},{4,12},{8,0},{12,4},{16,24},{20,28},{24,16},{28,20},{1,9},{5... | collective-permute-start | bytes 786440 | tf_op jit(solution)/shard_map/ppermute | solution.py:18
  89.0 22.2 %collective-permute-start.15 = (bf16[1,256,512]{2,1,0:T(8,128)(2,1)S(1)}, bf16[1,256,512]{2,1,0:T(8,128)(2,1)S(1)}, u32[]{:S(2)}, u32[]{:S(2)}) collective-permute-start(bf16[1,256,512]{2,1,0:T(8,128)(2,1)S(1)} %get-tuple-element.33), channel_id=1, source_target_pairs={{0,12},{4,8},{8,4},{12,0},{16,28},{20,24},{24,20},{28,16},{1,13},{... | collective-permute-start | bytes 786440 | tf_op jit(solution)/shard_map/ppermute | solution.py:18
  111.9 9.3 %collective-permute-start.18 = (bf16[1,256,512]{2,1,0:T(8,128)(2,1)S(1)}, bf16[1,256,512]{2,1,0:T(8,128)(2,1)S(1)}, u32[]{:S(2)}, u32[]{:S(2)}) collective-permute-start(bf16[1,256,512]{2,1,0:T(8,128)(2,1)S(1)} %get-tuple-element.35), channel_id=1, source_target_pairs={{0,8},{4,12},{8,0},{12,4},{16,24},{20,28},{24,16},{28,20},{1,9},{5... | collective-permute-start | bytes 786440 | tf_op jit(solution)/shard_map/ppermute | solution.py:18
  112.8 12.9 %collective-permute-start.19 = (bf16[1,256,512]{2,1,0:T(8,128)(2,1)S(1)}, bf16[1,256,512]{2,1,0:T(8,128)(2,1)S(1)}, u32[]{:S(2)}, u32[]{:S(2)}) collective-permute-start(bf16[1,256,512]{2,1,0:T(8,128)(2,1)S(1)} %get-tuple-element.36), channel_id=1, source_target_pairs={{0,12},{4,8},{8,4},{12,0},{16,28},{20,24},{24,20},{28,16},{1,13},{... | collective-permute-start | bytes 786440 | tf_op jit(solution)/shard_map/ppermute | solution.py:18
  114.9 12.2 %collective-permute-start.17 = (bf16[1,256,512]{2,1,0:T(8,128)(2,1)S(1)}, bf16[1,256,512]{2,1,0:T(8,128)(2,1)S(1)}, u32[]{:S(2)}, u32[]{:S(2)}) collective-permute-start(bf16[1,256,512]{2,1,0:T(8,128)(2,1)S(1)} %get-tuple-element.34.refs_20_), channel_id=1, source_target_pairs={{0,4},{4,0},{8,12},{12,8},{16,20},{20,16},{24,28},{28,24},{1,5},{5... | collective-permute-start | bytes 786440 | tf_op jit(solution)/shard_map/ppermute | solution.py:18

commit v10 on v9

--- a/solution.py
+++ b/solution.py
@@ -18,15 +18,18 @@
     return lax.ppermute(value, axis, [(at, at ^ step) for at in range(size)])
 
 
-def gather_rows(value, axis, size):
-    steps, step = [0], size // 2
-    while step:
-        other, others = hop(value, axis, size, step), [have ^ step for have in steps]
-        if step == 1:
-            return [value, other], [steps, others]
-        value, steps = jnp.concatenate([value, other]), steps + others
+def far_rows(value, axis, size):
+    steps, step, other = [0], size // 2, None
+    while step > 1:
+        value = value if other is None else jnp.concatenate([value, other])
+        other = hop(value, axis, size, step)
+        steps = steps + [have ^ step for have in steps]
         step //= 2
-    return [value], [steps]
+    return [value] if other is None else [value, other], steps
+
+
+def near_rows(value, steps, axis, size):
+    return [value, hop(value, axis, size, 1)], [steps, [have ^ 1 for have in steps]]
 
 
 def transposed_dot(left, right):
@@ -85,15 +88,21 @@
             send[at] = target[node]
 
 
-def relay_kernel(owners, source, follow, waits, picks, far, *refs):
+def relay_kernel(owners, source, follow, waits, joined, picks, far, *refs):
     half = owners // 2
     own, refs = take(refs, follow)
-    sends = refs[waits:]
+    _, refs = take(refs, waits)
+    parts, refs = take(refs, joined)
+    sends, joint = take(refs, half - 1)
     myself = lax.axis_index("leaf")
     for step, send in enumerate(sends, 1):
         send[0] = far[picks[source, myself ^ step, myself ^ half]]
         if own:
             send[1] = own[0][picks[source, myself ^ step, myself]]
+    at = 0
+    for part in parts:
+        joint[0][at:at + part.shape[0], :] = part[...]
+        at += part.shape[0]
 
 
 def level_kernel(
@@ -170,11 +179,11 @@
     pack_shape = shape(*raw[0].shape)
     leaf = lambda value, step: hop(value, "leaf", owners, step)
     near = lambda values: [leaf(value, step) for step, value in enumerate(values, 1)]
-    gather = lambda value: gather_rows(value, "draw", draws)
     inv_here = pltpu.VMEM((nodes, rows, rows), BF16)
     dot_flops = 2 * rows * rows * wide
 
-    parts, steps = gather(flat(inverse[0]))
+    parts, steps = far_rows(flat(inverse[0]), "draw", draws)
+    parts, steps = near_rows(jnp.concatenate(parts), steps, "draw", draws)
     *refs, pack = call(
         functools.partial(first_kernel, CHUNKS, steps),
         [part] * CHUNKS + [shape(CHUNKS, rows, wide)] * (half - 1) + [pack_shape],
@@ -185,23 +194,29 @@
         aliases={2 + len(parts): CHUNKS + half - 1},
     )
     solved, sends = take(refs, CHUNKS)
-    packs = [gather(pack)[0]]
+    packs = []
     done, pieces = [solved], []
     for level in range(1, levels):
         source = level - 1
         far = [leaf(value, half) for value in solved]
         got = near(sends)
         close = [[(ref, at) for ref in got] for at in chunks] if source == 0 else [[(ref, 0) for ref in got]]
-        distant, waits = [], got + packs[source][:1]
+        distant, waits = [], got
+        joined, far_steps = far_rows(pack, "draw", draws)
+        joint = sum(value.shape[0] for value in joined)
         for at in chunks:
             follow = source > 0 and at < CHUNKS - 1
             sends = call(
-                functools.partial(relay_kernel, owners, source, int(follow), len(waits)),
-                [shape(1 + follow, rows, wide)] * (half - 1),
+                functools.partial(relay_kernel, owners, source, int(follow), len(waits), len(joined)),
+                [shape(1 + follow, rows, wide)] * (half - 1) + [shape(joint, rows)] * bool(joined),
                 [],
                 (picks,),
-                (far[at], *([solved[at + 1]] if follow else []), *waits),
+                (far[at], *([solved[at + 1]] if follow else []), *waits, *joined),
             )
+            if joined:
+                *sends, joint = sends
+                packs.append(near_rows(joint, far_steps, "draw", draws)[0])
+                joined = []
             got = near(sends)
             distant.append([(ref, 0) for ref in got])
             if follow:
@@ -243,7 +258,7 @@
             )
             solved.append(here)
             if packing:
-                packs.append(gather(sent.pop())[0])
+                pack = sent.pop()
             sends += sent
             waits = []
         done.append(solved)

time: 131 us -> 106 us (0.81)
  waiting for transfers between devices: 92.4 us -> 70.3 us
  starting transfers between devices: 26.9 us -> 23.8 us
    ppermute x20, waiting for transfers between devices: 92.4 us -> 70.3 us  [hop(): return lax.ppermute(value, axis, [(at, at ^ step) for at in range(size)])]
    ppermute x20, starting transfers between devices: 26.9 us -> 23.8 us  [hop(): return lax.ppermute(value, axis, [(at, at ^ step) for at in range(size)])]
  transfers between devices with their start and end apart: 20 -> 20, of which waited for: 16 -> 14; matrix products, arithmetic and copies ran while one was open for 1% -> 1% of each run, Pallas kernels for 1% -> 0%
where the time goes in v10:
time: 106 us; the launch traced here: 105 us
  waiting for transfers between devices  70.3 us (66%)
  starting transfers between devices  23.8 us (22%)
  Pallas kernels  8.74 us (8%)
  local copies, waits for them, and re-layouts  2.36 us (2%)
    ppermute x20, waiting for transfers between devices, hop(): return lax.ppermute(value, axis, [(at, at ^ step) for at in range(size)])  70.3 us
    ppermute x20, starting transfers between devices, hop(): return lax.ppermute(value, axis, [(at, at ^ step) for at in range(size)])  23.8 us
    pallas_call x5, Pallas kernels, call(): pl.pallas_call(kernel, out_shape=outs, in_specs=[SMEM] * len(small) + [VM...  8.74 us
  transfers between devices with their start and end apart: 20, of which 14 were waited for; matrix products, arithmetic and copies ran while one was open for 1% of the time, Pallas kernels for 0%

profile of v10, /device:TPU:0, one launch (start us, length us, event | category | flops | bytes accessed | tf_op | source)
XLA Modules:
  0.0 105.4 jit_solution(9106671825170656828)
XLA Ops:
  0.0 1.0 fusion.1
  1.0 3.0 %collective-permute-start = (bf16[128,256]{1,0:T(8,128)(2,1)S(1)}, bf16[128,256]{1,0:T(8,128)(2,1)S(1)}, u32[]{:S(2)}, u32[]{:S(2)}) collective-permute-start(bf16[128,256]{1,0:T(8,128)(2,1)S(1)} %bitcast.11), channel_id=1, source_target_pairs={{0,2},{1,3},{2,0},{3,1},{4,6},{5,7},{6,4},{7,5},{8,10},{9,11},{10,... | collective-permute-start | bytes 196616 | tf_op jit(solution)/shard_map/ppermute | solution.py:18
  4.0 1.3 %fusion = (bf16[1,2,2,256,256]{4,3,2,1,0:T(8,128)(2,1)S(1)}, bf16[1,2,2,256,256]{4,3,2,1,0:T(8,128)(2,1)S(1)}) fusion(bf16[2,2,2,256,256]{4,3,2,1,0:T(8,128)(2,1)} %param.8), kind=kLoop, calls=%fused_computation.4 | loop fusion | bytes 2097152 | tf_op jit(solution)/shard_map/slice | solution.py:176
  5.4 0.9 collective-permute-done
  6.4 1.3 %collective-permute-done.1.refs_1_ = bf16[256,256]{1,0:T(8,128)(2,1)S(1)} collective-permute-done((bf16[256,256]{1,0:T(8,128)(2,1)S(1)}, bf16[256,256]{1,0:T(8,128)(2,1)S(1)}, u32[]{:S(2)}, u32[]{:S(2)}) %collective-permute-start.1) | collective-permute-done | bytes 131104 | tf_op jit(solution)/shard_map/ppermute | solution.py:18
  7.7 1.1 %shard_map.64 = (bf16[2,256,512]{2,1,0:T(8,128)(2,1)S(1)}, bf16[1,256,512]{2,1,0:T(8,128)(2,1)S(1)}, bf16[1,256,512]{2,1,0:T(8,128)(2,1)S(1)}, bf16[1,256,512]{2,1,0:T(8,128)(2,1)S(1)}, bf16[1152,256]{1,0:T(8,128)(2,1)S(1)}) custom-call(s32[2,8,8]{2,1,0:T(8,128)S(1)} %copy-done.1, ...), custom_call_target="tpu_custom_call", output_to_operand_aliasing={{4}: (4, {})} | custom-call | flops 134217728 | bytes 3276800 | tf_op jit(solution)/shard_map/pallas_call | solution.py:45
  8.8 2.1 %collective-permute-start.6 = (bf16[1152,256]{1,0:T(8,128)(2,1)S(1)}, bf16[1152,256]{1,0:T(8,128)(2,1)S(1)}, u32[]{:S(2)}, u32[]{:S(2)}) collective-permute-start(bf16[1152,256]{1,0:T(8,128)(2,1)S(1)} %get-tuple-element.27.refs_3_), channel_id=1, source_target_pairs={{0,2},{1,3},{2,0},{3,1},{4,6},{5,7},{6,4},{7,5},{8,10},{9,11},{10,... | collective-permute-start | bytes 1769480 | tf_op jit(solution)/shard_map/ppermute | solution.py:18
  10.9 2.6 %collective-permute-start.2 = (bf16[2,256,512]{2,1,0:T(8,128)(2,1)S(1)}, bf16[2,256,512]{2,1,0:T(8,128)(2,1)S(1)}, u32[]{:S(2)}, u32[]{:S(2)}) collective-permute-start(bf16[2,256,512]{2,1,0:T(8,128)(2,1)S(1)} %get-tuple-element.23.refs_2_.refs_18_), channel_id=1, source_target_pairs={{0,16},{4,20},{8,24},{12,28},{16,0},{20,4},{24,8},{28,12},{1,17},{... | collective-permute-start | bytes 1572872 | tf_op jit(solution)/shard_map/ppermute | solution.py:18
  13.5 1.5 %collective-permute-start.3 = (bf16[1,256,512]{2,1,0:T(8,128)(2,1)S(1)}, bf16[1,256,512]{2,1,0:T(8,128)(2,1)S(1)}, u32[]{:S(2)}, u32[]{:S(2)}) collective-permute-start(bf16[1,256,512]{2,1,0:T(8,128)(2,1)S(1)} %get-tuple-element.24), channel_id=1, source_target_pairs={{0,4},{4,0},{8,12},{12,8},{16,20},{20,16},{24,28},{28,24},{1,5},{5... | collective-permute-start | bytes 786440 | tf_op jit(solution)/shard_map/ppermute | solution.py:18
  15.0 1.6 %collective-permute-start.4 = (bf16[1,256,512]{2,1,0:T(8,128)(2,1)S(1)}, bf16[1,256,512]{2,1,0:T(8,128)(2,1)S(1)}, u32[]{:S(2)}, u32[]{:S(2)}) collective-permute-start(bf16[1,256,512]{2,1,0:T(8,128)(2,1)S(1)} %get-tuple-element.25), channel_id=1, source_target_pairs={{0,8},{4,12},{8,0},{12,4},{16,24},{20,28},{24,16},{28,20},{1,9},{5... | collective-permute-start | bytes 786440 | tf_op jit(solution)/shard_map/ppermute | solution.py:18
  17.0 4.8 %collective-permute-done.3.refs_0_.refs_3_ = bf16[1,256,512]{2,1,0:T(8,128)(2,1)S(1)} collective-permute-done((bf16[1,256,512]{2,1,0:T(8,128)(2,1)S(1)}, bf16[1,256,512]{2,1,0:T(8,128)(2,1)S(1)}, u32[]{:S(2)}, u32[]{:S(2)}) %collective-permute-start.3) | collective-permute-done | bytes 262176 | tf_op jit(solution)/shard_map/ppermute | solution.py:18
  21.8 9.6 %collective-permute-done.4.refs_1_.refs_4_ = bf16[1,256,512]{2,1,0:T(8,128)(2,1)S(1)} collective-permute-done((bf16[1,256,512]{2,1,0:T(8,128)(2,1)S(1)}, bf16[1,256,512]{2,1,0:T(8,128)(2,1)S(1)}, u32[]{:S(2)}, u32[]{:S(2)}) %collective-permute-start.4) | collective-permute-done | bytes 262176 | tf_op jit(solution)/shard_map/ppermute | solution.py:18
  31.5 6.7 %collective-permute-done.5.refs_2_.refs_5_ = bf16[1,256,512]{2,1,0:T(8,128)(2,1)S(1)} collective-permute-done((bf16[1,256,512]{2,1,0:T(8,128)(2,1)S(1)}, bf16[1,256,512]{2,1,0:T(8,128)(2,1)S(1)}, u32[]{:S(2)}, u32[]{:S(2)}) %collective-permute-start.5) | collective-permute-done | bytes 262176 | tf_op jit(solution)/shard_map/ppermute | solution.py:18
  38.2 0.8 shard_map.65
  39.1 1.3 %collective-permute-start.9 = (bf16[1,256,512]{2,1,0:T(8,128)(2,1)S(1)}, bf16[1,256,512]{2,1,0:T(8,128)(2,1)S(1)}, u32[]{:S(2)}, u32[]{:S(2)}) collective-permute-start(bf16[1,256,512]{2,1,0:T(8,128)(2,1)S(1)} %get-tuple-element.30), channel_id=1, source_target_pairs={{0,8},{4,12},{8,0},{12,4},{16,24},{20,28},{24,16},{28,20},{1,9},{5... | collective-permute-start | bytes 786440 | tf_op jit(solution)/shard_map/ppermute | solution.py:18
  40.4 1.8 %collective-permute-start.10 = (bf16[1,256,512]{2,1,0:T(8,128)(2,1)S(1)}, bf16[1,256,512]{2,1,0:T(8,128)(2,1)S(1)}, u32[]{:S(2)}, u32[]{:S(2)}) collective-permute-start(bf16[1,256,512]{2,1,0:T(8,128)(2,1)S(1)} %get-tuple-element.31), channel_id=1, source_target_pairs={{0,12},{4,8},{8,4},{12,0},{16,28},{20,24},{24,20},{28,16},{1,13},{... | collective-permute-start | bytes 786440 | tf_op jit(solution)/shard_map/ppermute | solution.py:18
  42.7 5.6 %collective-permute-done.9.refs_8_ = bf16[1,256,512]{2,1,0:T(8,128)(2,1)S(1)} collective-permute-done((bf16[1,256,512]{2,1,0:T(8,128)(2,1)S(1)}, bf16[1,256,512]{2,1,0:T(8,128)(2,1)S(1)}, u32[]{:S(2)}, u32[]{:S(2)}) %collective-permute-start.9) | collective-permute-done | bytes 262176 | tf_op jit(solution)/shard_map/ppermute | solution.py:18
  48.3 6.2 %collective-permute-done.10.refs_9_ = bf16[1,256,512]{2,1,0:T(8,128)(2,1)S(1)} collective-permute-done((bf16[1,256,512]{2,1,0:T(8,128)(2,1)S(1)}, bf16[1,256,512]{2,1,0:T(8,128)(2,1)S(1)}, u32[]{:S(2)}, u32[]{:S(2)}) %collective-permute-start.10) | collective-permute-done | bytes 262176 | tf_op jit(solution)/shard_map/ppermute | solution.py:18
  54.5 1.4 %collective-permute-done.8.refs_7_ = bf16[1,256,512]{2,1,0:T(8,128)(2,1)S(1)} collective-permute-done((bf16[1,256,512]{2,1,0:T(8,128)(2,1)S(1)}, bf16[1,256,512]{2,1,0:T(8,128)(2,1)S(1)}, u32[]{:S(2)}, u32[]{:S(2)}) %collective-permute-start.8) | collective-permute-done | bytes 262176 | tf_op jit(solution)/shard_map/ppermute | solution.py:18
  55.9 2.6 %shard_map.66 = (bf16[2,256,512]{2,1,0:T(8,128)(2,1)S(1)}, bf16[1,256,512]{2,1,0:T(8,128)(2,1)S(1)}, bf16[1,256,512]{2,1,0:T(8,128)(2,1)S(1)}, bf16[1,256,512]{2,1,0:T(8,128)(2,1)S(1)}, bf16[1152,256]{1,0:T(8,128)(2,1)S(1)}) custom-call(s32[2,8,8]{2,1,0:T(8,128)S(1)} %copy-done.1, s32[2,2,8]{2,1,0:T(2,128)S(1)} %copy-done.2, ...), custom_call_target="tpu_custom_call", output_to_operand_aliasing={{4}: (15, {})} | custom-call | flops 1207959552 | bytes 9306112 | tf_op jit(solution)/shard_map/pallas_call | solution.py:45
  59.0 1.3 %collective-permute-start.11 = (bf16[2,256,512]{2,1,0:T(8,128)(2,1)S(1)}, bf16[2,256,512]{2,1,0:T(8,128)(2,1)S(1)}, u32[]{:S(2)}, u32[]{:S(2)}) collective-permute-start(bf16[2,256,512]{2,1,0:T(8,128)(2,1)S(1)} %get-tuple-element.32.refs_10_.refs_19_), channel_id=1, source_target_pairs={{0,16},{4,20},{8,24},{12,28},{16,0},{20,4},{24,8},{28,12},{1,17},{... | collective-permute-start | bytes 1572872 | tf_op jit(solution)/shard_map/ppermute | solution.py:18
  60.9 1.5 %collective-permute-start.13 = (bf16[1,256,512]{2,1,0:T(8,128)(2,1)S(1)}, bf16[1,256,512]{2,1,0:T(8,128)(2,1)S(1)}, u32[]{:S(2)}, u32[]{:S(2)}) collective-permute-start(bf16[1,256,512]{2,1,0:T(8,128)(2,1)S(1)} %get-tuple-element.34), channel_id=1, source_target_pairs={{0,8},{4,12},{8,0},{12,4},{16,24},{20,28},{24,16},{28,20},{1,9},{5... | collective-permute-start | bytes 786440 | tf_op jit(solution)/shard_map/ppermute | solution.py:18
  62.4 1.4 %collective-permute-start.14 = (bf16[1,256,512]{2,1,0:T(8,128)(2,1)S(1)}, bf16[1,256,512]{2,1,0:T(8,128)(2,1)S(1)}, u32[]{:S(2)}, u32[]{:S(2)}) collective-permute-start(bf16[1,256,512]{2,1,0:T(8,128)(2,1)S(1)} %get-tuple-element.35), channel_id=1, source_target_pairs={{0,12},{4,8},{8,4},{12,0},{16,28},{20,24},{24,20},{28,16},{1,13},{... | collective-permute-start | bytes 786440 | tf_op jit(solution)/shard_map/ppermute | solution.py:18
  63.8 4.9 %collective-permute-done.12.refs_0_.refs_11_ = bf16[1,256,512]{2,1,0:T(8,128)(2,1)S(1)} collective-permute-done((bf16[1,256,512]{2,1,0:T(8,128)(2,1)S(1)}, bf16[1,256,512]{2,1,0:T(8,128)(2,1)S(1)}, u32[]{:S(2)}, u32[]{:S(2)}) %collective-permute-start.12) | collective-permute-done | bytes 262176 | tf_op jit(solution)/shard_map/ppermute | solution.py:18
  68.7 9.7 %collective-permute-done.13.refs_1_.refs_12_ = bf16[1,256,512]{2,1,0:T(8,128)(2,1)S(1)} collective-permute-done((bf16[1,256,512]{2,1,0:T(8,128)(2,1)S(1)}, bf16[1,256,512]{2,1,0:T(8,128)(2,1)S(1)}, u32[]{:S(2)}, u32[]{:S(2)}) %collective-permute-start.13) | collective-permute-done | bytes 262176 | tf_op jit(solution)/shard_map/ppermute | solution.py:18
  78.3 6.2 %collective-permute-done.14.refs_2_.refs_13_ = bf16[1,256,512]{2,1,0:T(8,128)(2,1)S(1)} collective-permute-done((bf16[1,256,512]{2,1,0:T(8,128)(2,1)S(1)}, bf16[1,256,512]{2,1,0:T(8,128)(2,1)S(1)}, u32[]{:S(2)}, u32[]{:S(2)}) %collective-permute-start.14) | collective-permute-done | bytes 262176 | tf_op jit(solution)/shard_map/ppermute | solution.py:18
  84.5 0.8 shard_map.67
  85.4 2.7 %collective-permute-start.19 = (bf16[1,256,512]{2,1,0:T(8,128)(2,1)S(1)}, bf16[1,256,512]{2,1,0:T(8,128)(2,1)S(1)}, u32[]{:S(2)}, u32[]{:S(2)}) collective-permute-start(bf16[1,256,512]{2,1,0:T(8,128)(2,1)S(1)} %get-tuple-element.40), channel_id=1, source_target_pairs={{0,12},{4,8},{8,4},{12,0},{16,28},{20,24},{24,20},{28,16},{1,13},{... | collective-permute-start | bytes 786440 | tf_op jit(solution)/shard_map/ppermute | solution.py:18
  88.9 5.6 %collective-permute-done.18.refs_16_ = bf16[1,256,512]{2,1,0:T(8,128)(2,1)S(1)} collective-permute-done((bf16[1,256,512]{2,1,0:T(8,128)(2,1)S(1)}, bf16[1,256,512]{2,1,0:T(8,128)(2,1)S(1)}, u32[]{:S(2)}, u32[]{:S(2)}) %collective-permute-start.18) | collective-permute-done | bytes 262176 | tf_op jit(solution)/shard_map/ppermute | solution.py:18
  94.5 6.0 %collective-permute-done.19.refs_17_ = bf16[1,256,512]{2,1,0:T(8,128)(2,1)S(1)} collective-permute-done((bf16[1,256,512]{2,1,0:T(8,128)(2,1)S(1)}, bf16[1,256,512]{2,1,0:T(8,128)(2,1)S(1)}, u32[]{:S(2)}, u32[]{:S(2)}) %collective-permute-start.19) | collective-permute-done | bytes 262176 | tf_op jit(solution)/shard_map/ppermute | solution.py:18
  100.5 1.4 %collective-permute-done.17.refs_15_ = bf16[1,256,512]{2,1,0:T(8,128)(2,1)S(1)} collective-permute-done((bf16[1,256,512]{2,1,0:T(8,128)(2,1)S(1)}, bf16[1,256,512]{2,1,0:T(8,128)(2,1)S(1)}, u32[]{:S(2)}, u32[]{:S(2)}) %collective-permute-start.17) | collective-permute-done | bytes 262176 | tf_op jit(solution)/shard_map/ppermute | solution.py:18
  101.9 3.5 %shard_map.68 = bf16[3,2,256,512]{3,2,1,0:T(8,128)(2,1)} custom-call(s32[2,8,8]{2,1,0:T(8,128)S(1)} %copy-done.1, s32[2,2,8]{2,1,0:T(2,128)S(1)} %copy-done.2, s32[2,2]{1,0:T(2,128)S(1)} %copy-done.3, bf16[3,2,256,512]{3,2,1,0:T(8,128)(2,1)S(1)} %copy-done, bf16[2304,256]{1,0:T(8,128)(2,1)S(1)} %get-tuple-element.37.refs_0_, ...), custom_call_target="tpu_custom_call" | custom-call | flops 1207959552 | bytes 12058624 | tf_op jit(solution)/shard_map/pallas_call | solution.py:45
  (27 shorter events, 3.2 us)
Async XLA Ops:
  0.0 5.3 %copy-start = (bf16[3,2,256,512]{3,2,1,0:T(8,128)(2,1)S(1)}, bf16[3,2,256,512]{3,2,1,0:T(8,128)(2,1)}, u32[]{:S(2)}) copy-start(bf16[3,2,256,512]{3,2,1,0:T(8,128)(2,1)} %noise.3) | copy-start | bytes 4718596
  1.0 5.2 %collective-permute-start = (bf16[128,256]{1,0:T(8,128)(2,1)S(1)}, bf16[128,256]{1,0:T(8,128)(2,1)S(1)}, u32[]{:S(2)}, u32[]{:S(2)}) collective-permute-start(bf16[128,256]{1,0:T(8,128)(2,1)S(1)} %bitcast.11), channel_id=1, source_target_pairs={{0,2},{1,3},{2,0},{3,1},{4,6},{5,7},{6,4},{7,5},{8,10},{9,11},{10,... | collective-permute-start | bytes 196616 | tf_op jit(solution)/shard_map/ppermute | solution.py:18
  5.3 2.4 %copy-start.1 = (s32[2,8,8]{2,1,0:T(8,128)S(1)}, s32[2,8,8]{2,1,0:T(8,128)}, u32[]{:S(2)}) copy-start(s32[2,8,8]{2,1,0:T(8,128)} %picks.9) | copy-start | bytes 1540
  6.3 1.4 %collective-permute-start.1 = (bf16[256,256]{1,0:T(8,128)(2,1)S(1)}, bf16[256,256]{1,0:T(8,128)(2,1)S(1)}, u32[]{:S(2)}, u32[]{:S(2)}) collective-permute-start(bf16[256,256]{1,0:T(8,128)(2,1)S(1)} %pad_maximum_fusion.2.refs_0_), channel_id=1, source_target_pairs={{0,1},{1,0},{2,3},{3,2},{4,5},{5,4},{6,7},{7,6},{8,9},{9,8},{10,11... | collective-permute-start | bytes 393224 | tf_op jit(solution)/shard_map/ppermute | solution.py:18
  8.8 29.4 %collective-permute-start.6 = (bf16[1152,256]{1,0:T(8,128)(2,1)S(1)}, bf16[1152,256]{1,0:T(8,128)(2,1)S(1)}, u32[]{:S(2)}, u32[]{:S(2)}) collective-permute-start(bf16[1152,256]{1,0:T(8,128)(2,1)S(1)} %get-tuple-element.27.refs_3_), channel_id=1, source_target_pairs={{0,2},{1,3},{2,0},{3,1},{4,6},{5,7},{6,4},{7,5},{8,10},{9,11},{10,... | collective-permute-start | bytes 1769480 | tf_op jit(solution)/shard_map/ppermute | solution.py:18
  10.9 27.3 %collective-permute-start.2 = (bf16[2,256,512]{2,1,0:T(8,128)(2,1)S(1)}, bf16[2,256,512]{2,1,0:T(8,128)(2,1)S(1)}, u32[]{:S(2)}, u32[]{:S(2)}) collective-permute-start(bf16[2,256,512]{2,1,0:T(8,128)(2,1)S(1)} %get-tuple-element.23.refs_2_.refs_18_), channel_id=1, source_target_pairs={{0,16},{4,20},{8,24},{12,28},{16,0},{20,4},{24,8},{28,12},{1,17},{... | collective-permute-start | bytes 1572872 | tf_op jit(solution)/shard_map/ppermute | solution.py:18
  13.5 8.3 %collective-permute-start.3 = (bf16[1,256,512]{2,1,0:T(8,128)(2,1)S(1)}, bf16[1,256,512]{2,1,0:T(8,128)(2,1)S(1)}, u32[]{:S(2)}, u32[]{:S(2)}) collective-permute-start(bf16[1,256,512]{2,1,0:T(8,128)(2,1)S(1)} %get-tuple-element.24), channel_id=1, source_target_pairs={{0,4},{4,0},{8,12},{12,8},{16,20},{20,16},{24,28},{28,24},{1,5},{5... | collective-permute-start | bytes 786440 | tf_op jit(solution)/shard_map/ppermute | solution.py:18
  15.0 16.5 %collective-permute-start.4 = (bf16[1,256,512]{2,1,0:T(8,128)(2,1)S(1)}, bf16[1,256,512]{2,1,0:T(8,128)(2,1)S(1)}, u32[]{:S(2)}, u32[]{:S(2)}) collective-permute-start(bf16[1,256,512]{2,1,0:T(8,128)(2,1)S(1)} %get-tuple-element.25), channel_id=1, source_target_pairs={{0,8},{4,12},{8,0},{12,4},{16,24},{20,28},{24,16},{28,20},{1,9},{5... | collective-permute-start | bytes 786440 | tf_op jit(solution)/shard_map/ppermute | solution.py:18
  16.6 21.6 %collective-permute-start.5 = (bf16[1,256,512]{2,1,0:T(8,128)(2,1)S(1)}, bf16[1,256,512]{2,1,0:T(8,128)(2,1)S(1)}, u32[]{:S(2)}, u32[]{:S(2)}) collective-permute-start(bf16[1,256,512]{2,1,0:T(8,128)(2,1)S(1)} %get-tuple-element.26), channel_id=1, source_target_pairs={{0,12},{4,8},{8,4},{12,0},{16,28},{20,24},{24,20},{28,16},{1,13},{... | collective-permute-start | bytes 786440 | tf_op jit(solution)/shard_map/ppermute | solution.py:18
  39.0 16.9 %copy-start.2 = (s32[2,2,8]{2,1,0:T(2,128)S(1)}, s32[2,2,8]{2,1,0:T(2,128)}, u32[]{:S(2)}) copy-start(s32[2,2,8]{2,1,0:T(2,128)} %lists.3) | copy-start | bytes 388
  39.0 16.9 %copy-start.3 = (s32[2,2]{1,0:T(2,128)S(1)}, s32[2,2]{1,0:T(2,128)}, u32[]{:S(2)}) copy-start(s32[2,2]{1,0:T(2,128)} %counts.3) | copy-start | bytes 52
  39.0 16.8 %collective-permute-start.7 = (bf16[2304,256]{1,0:T(8,128)(2,1)S(1)}, bf16[2304,256]{1,0:T(8,128)(2,1)S(1)}, u32[]{:S(2)}, u32[]{:S(2)}) collective-permute-start(bf16[2304,256]{1,0:T(8,128)(2,1)S(1)} %get-tuple-element.28.refs_0_), channel_id=1, source_target_pairs={{0,1},{1,0},{2,3},{3,2},{4,5},{5,4},{6,7},{7,6},{8,9},{9,8},{10,11... | collective-permute-start | bytes 3538952 | tf_op jit(solution)/shard_map/ppermute | solution.py:18
  39.1 9.2 %collective-permute-start.9 = (bf16[1,256,512]{2,1,0:T(8,128)(2,1)S(1)}, bf16[1,256,512]{2,1,0:T(8,128)(2,1)S(1)}, u32[]{:S(2)}, u32[]{:S(2)}) collective-permute-start(bf16[1,256,512]{2,1,0:T(8,128)(2,1)S(1)} %get-tuple-element.30), channel_id=1, source_target_pairs={{0,8},{4,12},{8,0},{12,4},{16,24},{20,28},{24,16},{28,20},{1,9},{5... | collective-permute-start | bytes 786440 | tf_op jit(solution)/shard_map/ppermute | solution.py:18
  40.4 14.1 %collective-permute-start.10 = (bf16[1,256,512]{2,1,0:T(8,128)(2,1)S(1)}, bf16[1,256,512]{2,1,0:T(8,128)(2,1)S(1)}, u32[]{:S(2)}, u32[]{:S(2)}) collective-permute-start(bf16[1,256,512]{2,1,0:T(8,128)(2,1)S(1)} %get-tuple-element.31), channel_id=1, source_target_pairs={{0,12},{4,8},{8,4},{12,0},{16,28},{20,24},{24,20},{28,16},{1,13},{... | collective-permute-start | bytes 786440 | tf_op jit(solution)/shard_map/ppermute | solution.py:18
  42.2 13.7 %collective-permute-start.8 = (bf16[1,256,512]{2,1,0:T(8,128)(2,1)S(1)}, bf16[1,256,512]{2,1,0:T(8,128)(2,1)S(1)}, u32[]{:S(2)}, u32[]{:S(2)}) collective-permute-start(bf16[1,256,512]{2,1,0:T(8,128)(2,1)S(1)} %get-tuple-element.29.refs_10_), channel_id=1, source_target_pairs={{0,4},{4,0},{8,12},{12,8},{16,20},{20,16},{24,28},{28,24},{1,5},{5... | collective-permute-start | bytes 786440 | tf_op jit(solution)/shard_map/ppermute | solution.py:18
  58.5 26.0 %collective-permute-start.15 = (bf16[1152,256]{1,0:T(8,128)(2,1)S(1)}, bf16[1152,256]{1,0:T(8,128)(2,1)S(1)}, u32[]{:S(2)}, u32[]{:S(2)}) collective-permute-start(bf16[1152,256]{1,0:T(8,128)(2,1)S(1)} %get-tuple-element.36.refs_3_), channel_id=1, source_target_pairs={{0,2},{1,3},{2,0},{3,1},{4,6},{5,7},{6,4},{7,5},{8,10},{9,11},{10,... | collective-permute-start | bytes 1769480 | tf_op jit(solution)/shard_map/ppermute | solution.py:18
  59.0 25.5 %collective-permute-start.11 = (bf16[2,256,512]{2,1,0:T(8,128)(2,1)S(1)}, bf16[2,256,512]{2,1,0:T(8,128)(2,1)S(1)}, u32[]{:S(2)}, u32[]{:S(2)}) collective-permute-start(bf16[2,256,512]{2,1,0:T(8,128)(2,1)S(1)} %get-tuple-element.32.refs_10_.refs_19_), channel_id=1, source_target_pairs={{0,16},{4,20},{8,24},{12,28},{16,0},{20,4},{24,8},{28,12},{1,17},{... | collective-permute-start | bytes 1572872 | tf_op jit(solution)/shard_map/ppermute | solution.py:18
  60.3 8.3 %collective-permute-start.12 = (bf16[1,256,512]{2,1,0:T(8,128)(2,1)S(1)}, bf16[1,256,512]{2,1,0:T(8,128)(2,1)S(1)}, u32[]{:S(2)}, u32[]{:S(2)}) collective-permute-start(bf16[1,256,512]{2,1,0:T(8,128)(2,1)S(1)} %get-tuple-element.33), channel_id=1, source_target_pairs={{0,4},{4,0},{8,12},{12,8},{16,20},{20,16},{24,28},{28,24},{1,5},{5... | collective-permute-start | bytes 786440 | tf_op jit(solution)/shard_map/ppermute | solution.py:18
  60.9 17.4 %collective-permute-start.13 = (bf16[1,256,512]{2,1,0:T(8,128)(2,1)S(1)}, bf16[1,256,512]{2,1,0:T(8,128)(2,1)S(1)}, u32[]{:S(2)}, u32[]{:S(2)}) collective-permute-start(bf16[1,256,512]{2,1,0:T(8,128)(2,1)S(1)} %get-tuple-element.34), channel_id=1, source_target_pairs={{0,8},{4,12},{8,0},{12,4},{16,24},{20,28},{24,16},{28,20},{1,9},{5... | collective-permute-start | bytes 786440 | tf_op jit(solution)/shard_map/ppermute | solution.py:18
  62.4 22.1 %collective-permute-start.14 = (bf16[1,256,512]{2,1,0:T(8,128)(2,1)S(1)}, bf16[1,256,512]{2,1,0:T(8,128)(2,1)S(1)}, u32[]{:S(2)}, u32[]{:S(2)}) collective-permute-start(bf16[1,256,512]{2,1,0:T(8,128)(2,1)S(1)} %get-tuple-element.35), channel_id=1, source_target_pairs={{0,12},{4,8},{8,4},{12,0},{16,28},{20,24},{24,20},{28,16},{1,13},{... | collective-permute-start | bytes 786440 | tf_op jit(solution)/shard_map/ppermute | solution.py:18
  85.3 16.6 %collective-permute-start.16 = (bf16[2304,256]{1,0:T(8,128)(2,1)S(1)}, bf16[2304,256]{1,0:T(8,128)(2,1)S(1)}, u32[]{:S(2)}, u32[]{:S(2)}) collective-permute-start(bf16[2304,256]{1,0:T(8,128)(2,1)S(1)} %get-tuple-element.37.refs_0_), channel_id=1, source_target_pairs={{0,1},{1,0},{2,3},{3,2},{4,5},{5,4},{6,7},{7,6},{8,9},{9,8},{10,11... | collective-permute-start | bytes 3538952 | tf_op jit(solution)/shard_map/ppermute | solution.py:18
  85.4 9.2 %collective-permute-start.18 = (bf16[1,256,512]{2,1,0:T(8,128)(2,1)S(1)}, bf16[1,256,512]{2,1,0:T(8,128)(2,1)S(1)}, u32[]{:S(2)}, u32[]{:S(2)}) collective-permute-start(bf16[1,256,512]{2,1,0:T(8,128)(2,1)S(1)} %get-tuple-element.39), channel_id=1, source_target_pairs={{0,8},{4,12},{8,0},{12,4},{16,24},{20,28},{24,16},{28,20},{1,9},{5... | collective-permute-start | bytes 786440 | tf_op jit(solution)/shard_map/ppermute | solution.py:18
  85.4 15.1 %collective-permute-start.19 = (bf16[1,256,512]{2,1,0:T(8,128)(2,1)S(1)}, bf16[1,256,512]{2,1,0:T(8,128)(2,1)S(1)}, u32[]{:S(2)}, u32[]{:S(2)}) collective-permute-start(bf16[1,256,512]{2,1,0:T(8,128)(2,1)S(1)} %get-tuple-element.40), channel_id=1, source_target_pairs={{0,12},{4,8},{8,4},{12,0},{16,28},{20,24},{24,20},{28,16},{1,13},{... | collective-permute-start | bytes 786440 | tf_op jit(solution)/shard_map/ppermute | solution.py:18
  88.2 13.7 %collective-permute-start.17 = (bf16[1,256,512]{2,1,0:T(8,128)(2,1)S(1)}, bf16[1,256,512]{2,1,0:T(8,128)(2,1)S(1)}, u32[]{:S(2)}, u32[]{:S(2)}) collective-permute-start(bf16[1,256,512]{2,1,0:T(8,128)(2,1)S(1)} %get-tuple-element.38.refs_20_), channel_id=1, source_target_pairs={{0,4},{4,0},{8,12},{12,8},{16,20},{20,16},{24,28},{28,24},{1,5},{5... | collective-permute-start | bytes 786440 | tf_op jit(solution)/shard_map/ppermute | solution.py:18

commit v11 on v10

--- a/solution.py
+++ b/solution.py
@@ -7,7 +7,7 @@
 from jax.experimental.pallas import tpu as pltpu
 from jax.sharding import PartitionSpec as P
 
-CHUNKS = 1
+CHUNKS = 2
 VMEM = pl.BlockSpec(memory_space=pltpu.VMEM)
 SMEM = pl.BlockSpec(memory_space=pltpu.SMEM)
 ANY = pl.BlockSpec(memory_space=pl.ANY)
@@ -69,11 +69,10 @@
             target[node, pl.ds(start, rows), :] = ref[first:first + rows, :]
 
 
-def first_kernel(chunks, steps, picks, noise, *refs):
+def first_kernel(steps, picks, noise, *refs):
     *refs, _, inv = refs
     parts, refs = take(refs, len(steps))
-    solved, sends = take(refs[1:], chunks)
-    myself, draw = lax.axis_index("leaf"), lax.axis_index("draw")
+    solved, draw = refs[1:], lax.axis_index("draw")
     nodes, wide = noise.shape[0], solved[0].shape[-1]
     draws = sum(map(len, steps))
     rows = inv.shape[1] // draws
@@ -82,23 +81,16 @@
         for node in range(nodes):
             right = noise[node, :, at * wide:(at + 1) * wide]
             target[node] = transposed_dot(inv[node], right).astype(BF16)
-    for step, send in enumerate(sends, 1):
-        node = picks[0, myself ^ step, myself]
-        for at, target in enumerate(solved):
-            send[at] = target[node]
-
-
-def relay_kernel(owners, source, follow, waits, joined, picks, far, *refs):
+
+
+def relay_kernel(owners, source, joined, picks, own, far, *refs):
     half = owners // 2
-    own, refs = take(refs, follow)
-    _, refs = take(refs, waits)
     parts, refs = take(refs, joined)
     sends, joint = take(refs, half - 1)
     myself = lax.axis_index("leaf")
     for step, send in enumerate(sends, 1):
-        send[0] = far[picks[source, myself ^ step, myself ^ half]]
-        if own:
-            send[1] = own[0][picks[source, myself ^ step, myself]]
+        send[0] = own[picks[source, myself ^ step, myself]]
+        send[1] = far[picks[source, myself ^ step, myself ^ half]]
     at = 0
     for part in parts:
         joint[0][at:at + part.shape[0], :] = part[...]
@@ -106,18 +98,16 @@
 
 
 def level_kernel(
-    level, owners, steps, width, chunk, places, sides, earlier, waits, packing,
+    level, owners, steps, width, chunk, places, earlier, packing,
     picks, lists, counts, noise, *refs,
 ):
     half = owners // 2
     packs, refs = take(refs, len(steps))
     known, refs = take(refs, level * owners)
     done, refs = take(refs, earlier)
-    _, refs = take(refs, waits)
     if packing:
         refs = refs[1:]
     target, *refs = refs
-    sends, refs = take(refs, sides)
     if packing:
         refs = refs[1:]
     table, inv, *refs = refs
@@ -155,8 +145,6 @@
                 total = term if total is None else total + term
         side = noise[level, node, :, chunk * wide:(chunk + 1) * wide].astype(F32) - total
         solved[node] = transposed_dot(inv[node], side.astype(BF16)).astype(BF16)
-    for step, send in enumerate(sends, 1):
-        send[0] = solved[picks[level, myself ^ step, myself]]
     if earlier:
         here = target.at[level, :, :, pl.ds(chunk * wide, wide)]
         copies.append(pltpu.make_async_copy(solved, here, sems.at[earlier]))
@@ -178,58 +166,48 @@
     ]
     pack_shape = shape(*raw[0].shape)
     leaf = lambda value, step: hop(value, "leaf", owners, step)
-    near = lambda values: [leaf(value, step) for step, value in enumerate(values, 1)]
     inv_here = pltpu.VMEM((nodes, rows, rows), BF16)
     dot_flops = 2 * rows * rows * wide
 
     parts, steps = far_rows(flat(inverse[0]), "draw", draws)
     parts, steps = near_rows(jnp.concatenate(parts), steps, "draw", draws)
-    *refs, pack = call(
-        functools.partial(first_kernel, CHUNKS, steps),
-        [part] * CHUNKS + [shape(CHUNKS, rows, wide)] * (half - 1) + [pack_shape],
+    *solved, pack = call(
+        functools.partial(first_kernel, steps),
+        [part] * CHUNKS + [pack_shape],
         [inv_here],
         (picks,),
         (noise[0], *parts, raw[0]),
         flops=nodes * CHUNKS * dot_flops,
-        aliases={2 + len(parts): CHUNKS + half - 1},
+        aliases={2 + len(parts): CHUNKS},
     )
-    solved, sends = take(refs, CHUNKS)
-    packs = []
-    done, pieces = [solved], []
+    packs, done, pieces = [], [], []
     for level in range(1, levels):
         source = level - 1
+        done.append(solved)
         far = [leaf(value, half) for value in solved]
-        got = near(sends)
-        close = [[(ref, at) for ref in got] for at in chunks] if source == 0 else [[(ref, 0) for ref in got]]
-        distant, waits = [], got
         joined, far_steps = far_rows(pack, "draw", draws)
-        joint = sum(value.shape[0] for value in joined)
+        joint = shape(sum(value.shape[0] for value in joined), rows)
+        pieces.append([])
         for at in chunks:
-            follow = source > 0 and at < CHUNKS - 1
+            joining = joined if at == 0 else []
             sends = call(
-                functools.partial(relay_kernel, owners, source, int(follow), len(waits), len(joined)),
-                [shape(1 + follow, rows, wide)] * (half - 1) + [shape(joint, rows)] * bool(joined),
+                functools.partial(relay_kernel, owners, source, len(joining)),
+                [shape(2, rows, wide)] * (half - 1) + [joint] * bool(joining),
                 [],
                 (picks,),
-                (far[at], *([solved[at + 1]] if follow else []), *waits, *joined),
+                (solved[at], far[at], *joining),
             )
-            if joined:
-                *sends, joint = sends
-                packs.append(near_rows(joint, far_steps, "draw", draws)[0])
-                joined = []
-            got = near(sends)
-            distant.append([(ref, 0) for ref in got])
-            if follow:
-                close.append([(ref, 1) for ref in got])
-            waits = []
-        pieces.append([
-            [(solved[at], 0), *close[at], (far[at], 0), *distant[at]] for at in chunks
-        ])
-        waits = sends[:1]
-        solved, sends = [], []
+            if joining:
+                *sends, pack = sends
+                packs.append(near_rows(pack, far_steps, "draw", draws)[0])
+            got = [leaf(value, step) for step, value in enumerate(sends, 1)]
+            pieces[source].append([
+                (solved[at], 0), *((ref, 0) for ref in got),
+                (far[at], 0), *((ref, 1) for ref in got),
+            ])
+        solved = []
         for at in chunks:
             packing = at == 0 and level < last_level
-            sides = half - 1 if packing else 0
             final = level == last_level and at == CHUNKS - 1
             earlier = [value for values in done for value in values] + solved if final else []
             known = [entry for below in range(level) for entry in pieces[below][at]]
@@ -239,29 +217,23 @@
                     pltpu.VMEM((nodes, rows, wide), BF16),
                     pltpu.SemaphoreType.DMA((len(earlier) + 1,)),
                 ]
-            here, *sent = call(
+            here, *passed = call(
                 functools.partial(
                     level_kernel, level, owners, steps, width, at,
-                    [place for _, place in known], sides, len(earlier), len(waits), packing,
+                    [place for _, place in known], len(earlier), packing,
                 ),
-                [shape(levels, nodes, rows, columns) if final else part]
-                + [shape(1, rows, wide)] * sides + [pack_shape] * packing,
+                [shape(levels, nodes, rows, columns) if final else part] + [pack_shape] * packing,
                 scratch,
                 (picks, lists, counts),
-                (noise, *packs[level - 1], *(ref for ref, _ in known), *earlier, *waits)
+                (noise, *packs[level - 1], *(ref for ref, _ in known), *earlier)
                 + ((raw[level],) if packing else ()),
                 out_spec=ANY if final else VMEM,
-                aliases={
-                    4 + len(packs[level - 1]) + len(known) + len(earlier) + len(waits): 1 + sides
-                } if packing else {},
                 flops=nodes * (draws * width + 1) * dot_flops,
+                aliases={4 + len(packs[level - 1]) + len(known) + len(earlier): 1} if packing else {},
             )
             solved.append(here)
             if packing:
-                pack = sent.pop()
-            sends += sent
-            waits = []
-        done.append(solved)
+                pack, = passed
     return here
 
 

time: 106 us -> 129 us (1.22)
  waiting for transfers between devices: 70.3 us -> 81.3 us
  starting transfers between devices: 23.8 us -> 30.1 us
  Pallas kernels: 8.74 us -> 14.5 us
    ppermute x20 -> x22, waiting for transfers between devices: 70.3 us -> 81.3 us  [hop(): return lax.ppermute(value, axis, [(at, at ^ step) for at in range(size)])]
    ppermute x20 -> x22, starting transfers between devices: 23.8 us -> 30.1 us  [hop(): return lax.ppermute(value, axis, [(at, at ^ step) for at in range(size)])]
    pallas_call x5 -> x9, Pallas kernels: 8.74 us -> 14.5 us  [call(): pl.pallas_call(kernel, out_shape=outs, in_specs=[SMEM] * len(small) + [VM...]
  transfers between devices with their start and end apart: 20 -> 22, of which waited for: 14 -> 17; matrix products, arithmetic and copies ran while one was open for 1% -> 1% of each run, Pallas kernels for 0% -> 5%
where the time goes in v11:
time: 129 us
  waiting for transfers between devices  81.3 us (63%)
  starting transfers between devices  30.1 us (23%)
  Pallas kernels  14.5 us (11%)
  local copies, waits for them, and re-layouts  2.36 us (2%)
    ppermute x22, waiting for transfers between devices, hop(): return lax.ppermute(value, axis, [(at, at ^ step) for at in range(size)])  81.3 us
    ppermute x22, starting transfers between devices, hop(): return lax.ppermute(value, axis, [(at, at ^ step) for at in range(size)])  30.1 us
    pallas_call x9, Pallas kernels, call(): pl.pallas_call(kernel, out_shape=outs, in_specs=[SMEM] * len(small) + [VM...  14.5 us
  transfers between devices with their start and end apart: 22, of which 17 were waited for; matrix products, arithmetic and copies ran while one was open for 1% of the time, Pallas kernels for 5%

profile of v11, /device:TPU:0, one launch (start us, length us, event | category | flops | bytes accessed | tf_op | source)
XLA Modules:
  0.0 128.5 jit_solution(4981490045789947030)
XLA Ops:
  1.0 3.0 %collective-permute-start = (bf16[128,256]{1,0:T(8,128)(2,1)S(1)}, bf16[128,256]{1,0:T(8,128)(2,1)S(1)}, u32[]{:S(2)}, u32[]{:S(2)}) collective-permute-start(bf16[128,256]{1,0:T(8,128)(2,1)S(1)} %bitcast.11), channel_id=1, source_target_pairs={{0,2},{1,3},{2,0},{3,1},{4,6},{5,7},{6,4},{7,5},{8,10},{9,11},{10,... | collective-permute-start | bytes 196616 | tf_op jit(solution)/shard_map/ppermute | solution.py:18
  4.0 1.3 fusion
  6.4 1.3 %collective-permute-done.1.refs_1_ = bf16[256,256]{1,0:T(8,128)(2,1)S(1)} collective-permute-done((bf16[256,256]{1,0:T(8,128)(2,1)S(1)}, bf16[256,256]{1,0:T(8,128)(2,1)S(1)}, u32[]{:S(2)}, u32[]{:S(2)}) %collective-permute-start.1) | collective-permute-done | bytes 131104 | tf_op jit(solution)/shard_map/ppermute | solution.py:18
  8.8 2.1 %collective-permute-start.3 = (bf16[1152,256]{1,0:T(8,128)(2,1)S(1)}, bf16[1152,256]{1,0:T(8,128)(2,1)S(1)}, u32[]{:S(2)}, u32[]{:S(2)}) collective-permute-start(bf16[1152,256]{1,0:T(8,128)(2,1)S(1)} %get-tuple-element.25.refs_0_), channel_id=1, source_target_pairs={{0,2},{1,3},{2,0},{3,1},{4,6},{5,7},{6,4},{7,5},{8,10},{9,11},{10,... | collective-permute-start | bytes 1769480 | tf_op jit(solution)/shard_map/ppermute | solution.py:18
  10.9 2.6 %collective-permute-start.2 = (bf16[2,256,256]{2,1,0:T(8,128)(2,1)S(1)}, bf16[2,256,256]{2,1,0:T(8,128)(2,1)S(1)}, u32[]{:S(2)}, u32[]{:S(2)}) collective-permute-start(bf16[2,256,256]{2,1,0:T(8,128)(2,1)S(1)} %get-tuple-element.24.own.refs_2_.refs_18_), channel_id=1, source_target_pairs={{0,16},{4,20},{8,24},{12,28},{16,0},{20,4},{24,8},{28,12},{1,17},{... | collective-permute-start | bytes 786440 | tf_op jit(solution)/shard_map/ppermute | solution.py:18
  13.4 12.0 %collective-permute-done.2.far.refs_6_ = bf16[2,256,256]{2,1,0:T(8,128)(2,1)S(1)} collective-permute-done((bf16[2,256,256]{2,1,0:T(8,128)(2,1)S(1)}, bf16[2,256,256]{2,1,0:T(8,128)(2,1)S(1)}, u32[]{:S(2)}, u32[]{:S(2)}) %collective-permute-start.2) | collective-permute-done | bytes 262176 | tf_op jit(solution)/shard_map/ppermute | solution.py:18
  26.3 1.6 %collective-permute-start.5 = (bf16[2,256,256]{2,1,0:T(8,128)(2,1)S(1)}, bf16[2,256,256]{2,1,0:T(8,128)(2,1)S(1)}, u32[]{:S(2)}, u32[]{:S(2)}) collective-permute-start(bf16[2,256,256]{2,1,0:T(8,128)(2,1)S(1)} %get-tuple-element.27), channel_id=1, source_target_pairs={{0,4},{4,0},{8,12},{12,8},{16,20},{20,16},{24,28},{28,24},{1,5},{5... | collective-permute-start | bytes 786440 | tf_op jit(solution)/shard_map/ppermute | solution.py:18
  29.9 5.1 %collective-permute-done.5.refs_3_.refs_7_ = bf16[2,256,256]{2,1,0:T(8,128)(2,1)S(1)} collective-permute-done((bf16[2,256,256]{2,1,0:T(8,128)(2,1)S(1)}, bf16[2,256,256]{2,1,0:T(8,128)(2,1)S(1)}, u32[]{:S(2)}, u32[]{:S(2)}) %collective-permute-start.5) | collective-permute-done | bytes 262176 | tf_op jit(solution)/shard_map/ppermute | solution.py:18
  35.1 2.0 %collective-permute-done.6.refs_4_.refs_8_ = bf16[2,256,256]{2,1,0:T(8,128)(2,1)S(1)} collective-permute-done((bf16[2,256,256]{2,1,0:T(8,128)(2,1)S(1)}, bf16[2,256,256]{2,1,0:T(8,128)(2,1)S(1)}, u32[]{:S(2)}, u32[]{:S(2)}) %collective-permute-start.6) | collective-permute-done | bytes 262176 | tf_op jit(solution)/shard_map/ppermute | solution.py:18
  37.1 4.8 %collective-permute-done.7.refs_5_.refs_9_ = bf16[2,256,256]{2,1,0:T(8,128)(2,1)S(1)} collective-permute-done((bf16[2,256,256]{2,1,0:T(8,128)(2,1)S(1)}, bf16[2,256,256]{2,1,0:T(8,128)(2,1)S(1)}, u32[]{:S(2)}, u32[]{:S(2)}) %collective-permute-start.7) | collective-permute-done | bytes 262176 | tf_op jit(solution)/shard_map/ppermute | solution.py:18
  41.9 2.4 %shard_map.66 = (bf16[2,256,256]{2,1,0:T(8,128)(2,1)S(1)}, bf16[1152,256]{1,0:T(8,128)(2,1)S(1)}) custom-call(s32[2,8,8]{2,1,0:T(8,128)S(1)} %copy-done.1, s32[2,2,8]{2,1,0:T(2,128)S(1)} %copy-done.2, s32[2,2]{1,0:T(2,128)S(1)} %copy-done.3, bf16[3,2,256,512]{3,2,1,0:T(8,128)(2,1)S(1)} %copy-done, ...), custom_call_target="tpu_custom_call", output_to_operand_aliasing={{1}: (14, {})} | custom-call | flops 603979776 | bytes 7471104 | tf_op jit(solution)/shard_map/pallas_call | solution.py:45
  45.1 2.6 %collective-permute-start.8 = (bf16[2,256,256]{2,1,0:T(8,128)(2,1)S(1)}, bf16[2,256,256]{2,1,0:T(8,128)(2,1)S(1)}, u32[]{:S(2)}, u32[]{:S(2)}) collective-permute-start(bf16[2,256,256]{2,1,0:T(8,128)(2,1)S(1)} %get-tuple-element.30.own.refs_10_.refs_20_), channel_id=1, source_target_pairs={{0,16},{4,20},{8,24},{12,28},{16,0},{20,4},{24,8},{28,12},{1,17},{... | collective-permute-start | bytes 786440 | tf_op jit(solution)/shard_map/ppermute | solution.py:18
  47.7 11.2 %collective-permute-done.8.far.refs_14_ = bf16[2,256,256]{2,1,0:T(8,128)(2,1)S(1)} collective-permute-done((bf16[2,256,256]{2,1,0:T(8,128)(2,1)S(1)}, bf16[2,256,256]{2,1,0:T(8,128)(2,1)S(1)}, u32[]{:S(2)}, u32[]{:S(2)}) %collective-permute-start.8) | collective-permute-done | bytes 262176 | tf_op jit(solution)/shard_map/ppermute | solution.py:18
  59.8 2.7 %collective-permute-start.11 = (bf16[2,256,256]{2,1,0:T(8,128)(2,1)S(1)}, bf16[2,256,256]{2,1,0:T(8,128)(2,1)S(1)}, u32[]{:S(2)}, u32[]{:S(2)}) collective-permute-start(bf16[2,256,256]{2,1,0:T(8,128)(2,1)S(1)} %get-tuple-element.33.own.refs_2_.refs_19_), channel_id=1, source_target_pairs={{0,16},{4,20},{8,24},{12,28},{16,0},{20,4},{24,8},{28,12},{1,17},{... | collective-permute-start | bytes 786440 | tf_op jit(solution)/shard_map/ppermute | solution.py:18
  62.5 12.5 %collective-permute-done.11.far.refs_6_ = bf16[2,256,256]{2,1,0:T(8,128)(2,1)S(1)} collective-permute-done((bf16[2,256,256]{2,1,0:T(8,128)(2,1)S(1)}, bf16[2,256,256]{2,1,0:T(8,128)(2,1)S(1)}, u32[]{:S(2)}, u32[]{:S(2)}) %collective-permute-start.11) | collective-permute-done | bytes 262176 | tf_op jit(solution)/shard_map/ppermute | solution.py:18
  75.8 1.6 %collective-permute-start.12 = (bf16[2,256,256]{2,1,0:T(8,128)(2,1)S(1)}, bf16[2,256,256]{2,1,0:T(8,128)(2,1)S(1)}, u32[]{:S(2)}, u32[]{:S(2)}) collective-permute-start(bf16[2,256,256]{2,1,0:T(8,128)(2,1)S(1)} %get-tuple-element.34), channel_id=1, source_target_pairs={{0,4},{4,0},{8,12},{12,8},{16,20},{20,16},{24,28},{28,24},{1,5},{5... | collective-permute-start | bytes 786440 | tf_op jit(solution)/shard_map/ppermute | solution.py:18
  78.0 1.3 %collective-permute-start.14 = (bf16[2,256,256]{2,1,0:T(8,128)(2,1)S(1)}, bf16[2,256,256]{2,1,0:T(8,128)(2,1)S(1)}, u32[]{:S(2)}, u32[]{:S(2)}) collective-permute-start(bf16[2,256,256]{2,1,0:T(8,128)(2,1)S(1)} %get-tuple-element.36), channel_id=1, source_target_pairs={{0,12},{4,8},{8,4},{12,0},{16,28},{20,24},{24,20},{28,16},{1,13},{... | collective-permute-start | bytes 786440 | tf_op jit(solution)/shard_map/ppermute | solution.py:18
  79.3 4.8 %collective-permute-done.12.refs_3_.refs_7_ = bf16[2,256,256]{2,1,0:T(8,128)(2,1)S(1)} collective-permute-done((bf16[2,256,256]{2,1,0:T(8,128)(2,1)S(1)}, bf16[2,256,256]{2,1,0:T(8,128)(2,1)S(1)}, u32[]{:S(2)}, u32[]{:S(2)}) %collective-permute-start.12) | collective-permute-done | bytes 262176 | tf_op jit(solution)/shard_map/ppermute | solution.py:18
  84.2 2.4 %collective-permute-done.13.refs_4_.refs_8_ = bf16[2,256,256]{2,1,0:T(8,128)(2,1)S(1)} collective-permute-done((bf16[2,256,256]{2,1,0:T(8,128)(2,1)S(1)}, bf16[2,256,256]{2,1,0:T(8,128)(2,1)S(1)}, u32[]{:S(2)}, u32[]{:S(2)}) %collective-permute-start.13) | collective-permute-done | bytes 262176 | tf_op jit(solution)/shard_map/ppermute | solution.py:18
  86.6 3.9 %collective-permute-done.14.refs_5_.refs_9_ = bf16[2,256,256]{2,1,0:T(8,128)(2,1)S(1)} collective-permute-done((bf16[2,256,256]{2,1,0:T(8,128)(2,1)S(1)}, bf16[2,256,256]{2,1,0:T(8,128)(2,1)S(1)}, u32[]{:S(2)}, u32[]{:S(2)}) %collective-permute-start.14) | collective-permute-done | bytes 262176 | tf_op jit(solution)/shard_map/ppermute | solution.py:18
  90.5 2.4 %shard_map.69.own.refs_10_.refs_21_ = bf16[2,256,256]{2,1,0:T(8,128)(2,1)S(1)} custom-call(s32[2,8,8]{2,1,0:T(8,128)S(1)} %copy-done.1, s32[2,2,8]{2,1,0:T(2,128)S(1)} %copy-done.2, s32[2,2]{1,0:T(2,128)S(1)} %copy-done.3, bf16[3,2,256,512]{3,2,1,0:T(8,128)(2,1)S(1)} %copy-done, bf16[2304,256]{1,0:T(8,128)(2,1)S(1)} %get-tuple-element.26.refs_0_, ...), custom_call_target="tpu_custom_call" | custom-call | flops 603979776 | bytes 6291456 | tf_op jit(solution)/shard_map/pallas_call | solution.py:45
  92.9 2.7 %collective-permute-start.15 = (bf16[2,256,256]{2,1,0:T(8,128)(2,1)S(1)}, bf16[2,256,256]{2,1,0:T(8,128)(2,1)S(1)}, u32[]{:S(2)}, u32[]{:S(2)}) collective-permute-start(bf16[2,256,256]{2,1,0:T(8,128)(2,1)S(1)} %shard_map.69.own.refs_10_.refs_21_), channel_id=1, source_target_pairs={{0,16},{4,20},{8,24},{12,28},{16,0},{20,4},{24,8},{28,12},{1,17},{... | collective-permute-start | bytes 786440 | tf_op jit(solution)/shard_map/ppermute | solution.py:18
  95.6 1.5 %collective-permute-start.19 = (bf16[2,256,256]{2,1,0:T(8,128)(2,1)S(1)}, bf16[2,256,256]{2,1,0:T(8,128)(2,1)S(1)}, u32[]{:S(2)}, u32[]{:S(2)}) collective-permute-start(bf16[2,256,256]{2,1,0:T(8,128)(2,1)S(1)} %get-tuple-element.40), channel_id=1, source_target_pairs={{0,4},{4,0},{8,12},{12,8},{16,20},{20,16},{24,28},{28,24},{1,5},{5... | collective-permute-start | bytes 786440 | tf_op jit(solution)/shard_map/ppermute | solution.py:18
  97.1 1.7 %collective-permute-start.20 = (bf16[2,256,256]{2,1,0:T(8,128)(2,1)S(1)}, bf16[2,256,256]{2,1,0:T(8,128)(2,1)S(1)}, u32[]{:S(2)}, u32[]{:S(2)}) collective-permute-start(bf16[2,256,256]{2,1,0:T(8,128)(2,1)S(1)} %get-tuple-element.41), channel_id=1, source_target_pairs={{0,8},{4,12},{8,0},{12,4},{16,24},{20,28},{24,16},{28,20},{1,9},{5... | collective-permute-start | bytes 786440 | tf_op jit(solution)/shard_map/ppermute | solution.py:18
  99.1 7.8 %collective-permute-done.15.far.refs_14_ = bf16[2,256,256]{2,1,0:T(8,128)(2,1)S(1)} collective-permute-done((bf16[2,256,256]{2,1,0:T(8,128)(2,1)S(1)}, bf16[2,256,256]{2,1,0:T(8,128)(2,1)S(1)}, u32[]{:S(2)}, u32[]{:S(2)}) %collective-permute-start.15) | collective-permute-done | bytes 262176 | tf_op jit(solution)/shard_map/ppermute | solution.py:18
  107.6 1.6 %collective-permute-start.16 = (bf16[2,256,256]{2,1,0:T(8,128)(2,1)S(1)}, bf16[2,256,256]{2,1,0:T(8,128)(2,1)S(1)}, u32[]{:S(2)}, u32[]{:S(2)}) collective-permute-start(bf16[2,256,256]{2,1,0:T(8,128)(2,1)S(1)} %get-tuple-element.37), channel_id=1, source_target_pairs={{0,4},{4,0},{8,12},{12,8},{16,20},{20,16},{24,28},{28,24},{1,5},{5... | collective-permute-start | bytes 786440 | tf_op jit(solution)/shard_map/ppermute | solution.py:18
  111.4 5.2 %collective-permute-done.21.refs_13_.refs_17_ = bf16[2,256,256]{2,1,0:T(8,128)(2,1)S(1)} collective-permute-done((bf16[2,256,256]{2,1,0:T(8,128)(2,1)S(1)}, bf16[2,256,256]{2,1,0:T(8,128)(2,1)S(1)}, u32[]{:S(2)}, u32[]{:S(2)}) %collective-permute-start.21) | collective-permute-done | bytes 262176 | tf_op jit(solution)/shard_map/ppermute | solution.py:18
  116.6 2.5 %shard_map.71.refs_22_ = bf16[2,256,256]{2,1,0:T(8,128)(2,1)S(1)} custom-call(s32[2,8,8]{2,1,0:T(8,128)S(1)} %copy-done.1, s32[2,2,8]{2,1,0:T(2,128)S(1)} %copy-done.2, s32[2,2]{1,0:T(2,128)S(1)} %copy-done.3, bf16[3,2,256,512]{3,2,1,0:T(8,128)(2,1)S(1)} %copy-done, bf16[2304,256]{1,0:T(8,128)(2,1)S(1)} %get-tuple-element.32.refs_0_, ...), custom_call_target="tpu_custom_call" | custom-call | flops 603979776 | bytes 8388608 | tf_op jit(solution)/shard_map/pallas_call | solution.py:45
  119.0 1.5 %collective-permute-done.16.refs_11_.refs_15_ = bf16[2,256,256]{2,1,0:T(8,128)(2,1)S(1)} collective-permute-done((bf16[2,256,256]{2,1,0:T(8,128)(2,1)S(1)}, bf16[2,256,256]{2,1,0:T(8,128)(2,1)S(1)}, u32[]{:S(2)}, u32[]{:S(2)}) %collective-permute-start.16) | collective-permute-done | bytes 262176 | tf_op jit(solution)/shard_map/ppermute | solution.py:18
  120.6 1.5 %collective-permute-done.17.refs_12_.refs_16_ = bf16[2,256,256]{2,1,0:T(8,128)(2,1)S(1)} collective-permute-done((bf16[2,256,256]{2,1,0:T(8,128)(2,1)S(1)}, bf16[2,256,256]{2,1,0:T(8,128)(2,1)S(1)}, u32[]{:S(2)}, u32[]{:S(2)}) %collective-permute-start.17) | collective-permute-done | bytes 262176 | tf_op jit(solution)/shard_map/ppermute | solution.py:18
  122.1 3.2 %collective-permute-done.18.refs_13_.refs_17_ = bf16[2,256,256]{2,1,0:T(8,128)(2,1)S(1)} collective-permute-done((bf16[2,256,256]{2,1,0:T(8,128)(2,1)S(1)}, bf16[2,256,256]{2,1,0:T(8,128)(2,1)S(1)}, u32[]{:S(2)}, u32[]{:S(2)}) %collective-permute-start.18) | collective-permute-done | bytes 262176 | tf_op jit(solution)/shard_map/ppermute | solution.py:18
  125.3 3.2 %shard_map.72 = bf16[3,2,256,512]{3,2,1,0:T(8,128)(2,1)} custom-call(s32[2,8,8]{2,1,0:T(8,128)S(1)} %copy-done.1, s32[2,2,8]{2,1,0:T(2,128)S(1)} %copy-done.2, s32[2,2]{1,0:T(2,128)S(1)} %copy-done.3, bf16[3,2,256,512]{3,2,1,0:T(8,128)(2,1)S(1)} %copy-done, bf16[2304,256]{1,0:T(8,128)(2,1)S(1)} %get-tuple-element.32.refs_0_, ...), custom_call_target="tpu_custom_call" | custom-call | flops 603979776 | bytes 11010048 | tf_op jit(solution)/shard_map/pallas_call | solution.py:45
  (35 shorter events, 12.3 us)
Async XLA Ops:
  0.0 5.3 %copy-start = (bf16[3,2,256,512]{3,2,1,0:T(8,128)(2,1)S(1)}, bf16[3,2,256,512]{3,2,1,0:T(8,128)(2,1)}, u32[]{:S(2)}) copy-start(bf16[3,2,256,512]{3,2,1,0:T(8,128)(2,1)} %noise.7) | copy-start | bytes 4718596
  1.0 5.2 %collective-permute-start = (bf16[128,256]{1,0:T(8,128)(2,1)S(1)}, bf16[128,256]{1,0:T(8,128)(2,1)S(1)}, u32[]{:S(2)}, u32[]{:S(2)}) collective-permute-start(bf16[128,256]{1,0:T(8,128)(2,1)S(1)} %bitcast.11), channel_id=1, source_target_pairs={{0,2},{1,3},{2,0},{3,1},{4,6},{5,7},{6,4},{7,5},{8,10},{9,11},{10,... | collective-permute-start | bytes 196616 | tf_op jit(solution)/shard_map/ppermute | solution.py:18
  5.3 2.4 %copy-start.1 = (s32[2,8,8]{2,1,0:T(8,128)S(1)}, s32[2,8,8]{2,1,0:T(8,128)}, u32[]{:S(2)}) copy-start(s32[2,8,8]{2,1,0:T(8,128)} %picks.17) | copy-start | bytes 1540
  6.3 1.4 %collective-permute-start.1 = (bf16[256,256]{1,0:T(8,128)(2,1)S(1)}, bf16[256,256]{1,0:T(8,128)(2,1)S(1)}, u32[]{:S(2)}, u32[]{:S(2)}) collective-permute-start(bf16[256,256]{1,0:T(8,128)(2,1)S(1)} %pad_maximum_fusion.2.refs_0_), channel_id=1, source_target_pairs={{0,1},{1,0},{2,3},{3,2},{4,5},{5,4},{6,7},{7,6},{8,9},{9,8},{10,11... | collective-permute-start | bytes 393224 | tf_op jit(solution)/shard_map/ppermute | solution.py:18
  8.8 16.7 %collective-permute-start.3 = (bf16[1152,256]{1,0:T(8,128)(2,1)S(1)}, bf16[1152,256]{1,0:T(8,128)(2,1)S(1)}, u32[]{:S(2)}, u32[]{:S(2)}) collective-permute-start(bf16[1152,256]{1,0:T(8,128)(2,1)S(1)} %get-tuple-element.25.refs_0_), channel_id=1, source_target_pairs={{0,2},{1,3},{2,0},{3,1},{4,6},{5,7},{6,4},{7,5},{8,10},{9,11},{10,... | collective-permute-start | bytes 1769480 | tf_op jit(solution)/shard_map/ppermute | solution.py:18
  10.9 31.0 %copy-start.2 = (s32[2,2,8]{2,1,0:T(2,128)S(1)}, s32[2,2,8]{2,1,0:T(2,128)}, u32[]{:S(2)}) copy-start(s32[2,2,8]{2,1,0:T(2,128)} %lists.7) | copy-start | bytes 388
  10.9 31.0 %copy-start.3 = (s32[2,2]{1,0:T(2,128)S(1)}, s32[2,2]{1,0:T(2,128)}, u32[]{:S(2)}) copy-start(s32[2,2]{1,0:T(2,128)} %counts.7) | copy-start | bytes 52
  10.9 14.6 %collective-permute-start.2 = (bf16[2,256,256]{2,1,0:T(8,128)(2,1)S(1)}, bf16[2,256,256]{2,1,0:T(8,128)(2,1)S(1)}, u32[]{:S(2)}, u32[]{:S(2)}) collective-permute-start(bf16[2,256,256]{2,1,0:T(8,128)(2,1)S(1)} %get-tuple-element.24.own.refs_2_.refs_18_), channel_id=1, source_target_pairs={{0,16},{4,20},{8,24},{12,28},{16,0},{20,4},{24,8},{28,12},{1,17},{... | collective-permute-start | bytes 786440 | tf_op jit(solution)/shard_map/ppermute | solution.py:18
  26.3 15.6 %collective-permute-start.4 = (bf16[2304,256]{1,0:T(8,128)(2,1)S(1)}, bf16[2304,256]{1,0:T(8,128)(2,1)S(1)}, u32[]{:S(2)}, u32[]{:S(2)}) collective-permute-start(bf16[2304,256]{1,0:T(8,128)(2,1)S(1)} %get-tuple-element.26.refs_0_), channel_id=1, source_target_pairs={{0,1},{1,0},{2,3},{3,2},{4,5},{5,4},{6,7},{7,6},{8,9},{9,8},{10,11... | collective-permute-start | bytes 3538952 | tf_op jit(solution)/shard_map/ppermute | solution.py:18
  26.3 8.7 %collective-permute-start.5 = (bf16[2,256,256]{2,1,0:T(8,128)(2,1)S(1)}, bf16[2,256,256]{2,1,0:T(8,128)(2,1)S(1)}, u32[]{:S(2)}, u32[]{:S(2)}) collective-permute-start(bf16[2,256,256]{2,1,0:T(8,128)(2,1)S(1)} %get-tuple-element.27), channel_id=1, source_target_pairs={{0,4},{4,0},{8,12},{12,8},{16,20},{20,16},{24,28},{28,24},{1,5},{5... | collective-permute-start | bytes 786440 | tf_op jit(solution)/shard_map/ppermute | solution.py:18
  27.9 9.2 %collective-permute-start.6 = (bf16[2,256,256]{2,1,0:T(8,128)(2,1)S(1)}, bf16[2,256,256]{2,1,0:T(8,128)(2,1)S(1)}, u32[]{:S(2)}, u32[]{:S(2)}) collective-permute-start(bf16[2,256,256]{2,1,0:T(8,128)(2,1)S(1)} %get-tuple-element.28), channel_id=1, source_target_pairs={{0,8},{4,12},{8,0},{12,4},{16,24},{20,28},{24,16},{28,20},{1,9},{5... | collective-permute-start | bytes 786440 | tf_op jit(solution)/shard_map/ppermute | solution.py:18
  28.8 13.1 %collective-permute-start.7 = (bf16[2,256,256]{2,1,0:T(8,128)(2,1)S(1)}, bf16[2,256,256]{2,1,0:T(8,128)(2,1)S(1)}, u32[]{:S(2)}, u32[]{:S(2)}) collective-permute-start(bf16[2,256,256]{2,1,0:T(8,128)(2,1)S(1)} %get-tuple-element.29), channel_id=1, source_target_pairs={{0,12},{4,8},{8,4},{12,0},{16,28},{20,24},{24,20},{28,16},{1,13},{... | collective-permute-start | bytes 786440 | tf_op jit(solution)/shard_map/ppermute | solution.py:18
  44.3 14.6 %collective-permute-start.9 = (bf16[1152,256]{1,0:T(8,128)(2,1)S(1)}, bf16[1152,256]{1,0:T(8,128)(2,1)S(1)}, u32[]{:S(2)}, u32[]{:S(2)}) collective-permute-start(bf16[1152,256]{1,0:T(8,128)(2,1)S(1)} %get-tuple-element.31.refs_0_), channel_id=1, source_target_pairs={{0,2},{1,3},{2,0},{3,1},{4,6},{5,7},{6,4},{7,5},{8,10},{9,11},{10,... | collective-permute-start | bytes 1769480 | tf_op jit(solution)/shard_map/ppermute | solution.py:18
  45.1 13.8 %collective-permute-start.8 = (bf16[2,256,256]{2,1,0:T(8,128)(2,1)S(1)}, bf16[2,256,256]{2,1,0:T(8,128)(2,1)S(1)}, u32[]{:S(2)}, u32[]{:S(2)}) collective-permute-start(bf16[2,256,256]{2,1,0:T(8,128)(2,1)S(1)} %get-tuple-element.30.own.refs_10_.refs_20_), channel_id=1, source_target_pairs={{0,16},{4,20},{8,24},{12,28},{16,0},{20,4},{24,8},{28,12},{1,17},{... | collective-permute-start | bytes 786440 | tf_op jit(solution)/shard_map/ppermute | solution.py:18
  59.7 56.9 %collective-permute-start.10 = (bf16[2304,256]{1,0:T(8,128)(2,1)S(1)}, bf16[2304,256]{1,0:T(8,128)(2,1)S(1)}, u32[]{:S(2)}, u32[]{:S(2)}) collective-permute-start(bf16[2304,256]{1,0:T(8,128)(2,1)S(1)} %get-tuple-element.32.refs_0_), channel_id=1, source_target_pairs={{0,1},{1,0},{2,3},{3,2},{4,5},{5,4},{6,7},{7,6},{8,9},{9,8},{10,11... | collective-permute-start | bytes 3538952 | tf_op jit(solution)/shard_map/ppermute | solution.py:18
  59.8 15.2 %collective-permute-start.11 = (bf16[2,256,256]{2,1,0:T(8,128)(2,1)S(1)}, bf16[2,256,256]{2,1,0:T(8,128)(2,1)S(1)}, u32[]{:S(2)}, u32[]{:S(2)}) collective-permute-start(bf16[2,256,256]{2,1,0:T(8,128)(2,1)S(1)} %get-tuple-element.33.own.refs_2_.refs_19_), channel_id=1, source_target_pairs={{0,16},{4,20},{8,24},{12,28},{16,0},{20,4},{24,8},{28,12},{1,17},{... | collective-permute-start | bytes 786440 | tf_op jit(solution)/shard_map/ppermute | solution.py:18
  75.8 8.4 %collective-permute-start.12 = (bf16[2,256,256]{2,1,0:T(8,128)(2,1)S(1)}, bf16[2,256,256]{2,1,0:T(8,128)(2,1)S(1)}, u32[]{:S(2)}, u32[]{:S(2)}) collective-permute-start(bf16[2,256,256]{2,1,0:T(8,128)(2,1)S(1)} %get-tuple-element.34), channel_id=1, source_target_pairs={{0,4},{4,0},{8,12},{12,8},{16,20},{20,16},{24,28},{28,24},{1,5},{5... | collective-permute-start | bytes 786440 | tf_op jit(solution)/shard_map/ppermute | solution.py:18
  77.4 9.2 %collective-permute-start.13 = (bf16[2,256,256]{2,1,0:T(8,128)(2,1)S(1)}, bf16[2,256,256]{2,1,0:T(8,128)(2,1)S(1)}, u32[]{:S(2)}, u32[]{:S(2)}) collective-permute-start(bf16[2,256,256]{2,1,0:T(8,128)(2,1)S(1)} %get-tuple-element.35), channel_id=1, source_target_pairs={{0,8},{4,12},{8,0},{12,4},{16,24},{20,28},{24,16},{28,20},{1,9},{5... | collective-permute-start | bytes 786440 | tf_op jit(solution)/shard_map/ppermute | solution.py:18
  78.0 12.5 %collective-permute-start.14 = (bf16[2,256,256]{2,1,0:T(8,128)(2,1)S(1)}, bf16[2,256,256]{2,1,0:T(8,128)(2,1)S(1)}, u32[]{:S(2)}, u32[]{:S(2)}) collective-permute-start(bf16[2,256,256]{2,1,0:T(8,128)(2,1)S(1)} %get-tuple-element.36), channel_id=1, source_target_pairs={{0,12},{4,8},{8,4},{12,0},{16,28},{20,24},{24,20},{28,16},{1,13},{... | collective-permute-start | bytes 786440 | tf_op jit(solution)/shard_map/ppermute | solution.py:18
  92.9 14.0 %collective-permute-start.15 = (bf16[2,256,256]{2,1,0:T(8,128)(2,1)S(1)}, bf16[2,256,256]{2,1,0:T(8,128)(2,1)S(1)}, u32[]{:S(2)}, u32[]{:S(2)}) collective-permute-start(bf16[2,256,256]{2,1,0:T(8,128)(2,1)S(1)} %shard_map.69.own.refs_10_.refs_21_), channel_id=1, source_target_pairs={{0,16},{4,20},{8,24},{12,28},{16,0},{20,4},{24,8},{28,12},{1,17},{... | collective-permute-start | bytes 786440 | tf_op jit(solution)/shard_map/ppermute | solution.py:18
  95.6 13.6 %collective-permute-start.19 = (bf16[2,256,256]{2,1,0:T(8,128)(2,1)S(1)}, bf16[2,256,256]{2,1,0:T(8,128)(2,1)S(1)}, u32[]{:S(2)}, u32[]{:S(2)}) collective-permute-start(bf16[2,256,256]{2,1,0:T(8,128)(2,1)S(1)} %get-tuple-element.40), channel_id=1, source_target_pairs={{0,4},{4,0},{8,12},{12,8},{16,20},{20,16},{24,28},{28,24},{1,5},{5... | collective-permute-start | bytes 786440 | tf_op jit(solution)/shard_map/ppermute | solution.py:18
  97.1 13.7 %collective-permute-start.20 = (bf16[2,256,256]{2,1,0:T(8,128)(2,1)S(1)}, bf16[2,256,256]{2,1,0:T(8,128)(2,1)S(1)}, u32[]{:S(2)}, u32[]{:S(2)}) collective-permute-start(bf16[2,256,256]{2,1,0:T(8,128)(2,1)S(1)} %get-tuple-element.41), channel_id=1, source_target_pairs={{0,8},{4,12},{8,0},{12,4},{16,24},{20,28},{24,16},{28,20},{1,9},{5... | collective-permute-start | bytes 786440 | tf_op jit(solution)/shard_map/ppermute | solution.py:18
  98.8 17.7 %collective-permute-start.21 = (bf16[2,256,256]{2,1,0:T(8,128)(2,1)S(1)}, bf16[2,256,256]{2,1,0:T(8,128)(2,1)S(1)}, u32[]{:S(2)}, u32[]{:S(2)}) collective-permute-start(bf16[2,256,256]{2,1,0:T(8,128)(2,1)S(1)} %get-tuple-element.42), channel_id=1, source_target_pairs={{0,12},{4,8},{8,4},{12,0},{16,28},{20,24},{24,20},{28,16},{1,13},{... | collective-permute-start | bytes 786440 | tf_op jit(solution)/shard_map/ppermute | solution.py:18
  107.6 12.9 %collective-permute-start.16 = (bf16[2,256,256]{2,1,0:T(8,128)(2,1)S(1)}, bf16[2,256,256]{2,1,0:T(8,128)(2,1)S(1)}, u32[]{:S(2)}, u32[]{:S(2)}) collective-permute-start(bf16[2,256,256]{2,1,0:T(8,128)(2,1)S(1)} %get-tuple-element.37), channel_id=1, source_target_pairs={{0,4},{4,0},{8,12},{12,8},{16,20},{20,16},{24,28},{28,24},{1,5},{5... | collective-permute-start | bytes 786440 | tf_op jit(solution)/shard_map/ppermute | solution.py:18
  109.2 12.9 %collective-permute-start.17 = (bf16[2,256,256]{2,1,0:T(8,128)(2,1)S(1)}, bf16[2,256,256]{2,1,0:T(8,128)(2,1)S(1)}, u32[]{:S(2)}, u32[]{:S(2)}) collective-permute-start(bf16[2,256,256]{2,1,0:T(8,128)(2,1)S(1)} %get-tuple-element.38), channel_id=1, source_target_pairs={{0,8},{4,12},{8,0},{12,4},{16,24},{20,28},{24,16},{28,20},{1,9},{5... | collective-permute-start | bytes 786440 | tf_op jit(solution)/shard_map/ppermute | solution.py:18
  110.8 14.5 %collective-permute-start.18 = (bf16[2,256,256]{2,1,0:T(8,128)(2,1)S(1)}, bf16[2,256,256]{2,1,0:T(8,128)(2,1)S(1)}, u32[]{:S(2)}, u32[]{:S(2)}) collective-permute-start(bf16[2,256,256]{2,1,0:T(8,128)(2,1)S(1)} %get-tuple-element.39), channel_id=1, source_target_pairs={{0,12},{4,8},{8,4},{12,0},{16,28},{20,24},{24,20},{28,16},{1,13},{... | collective-permute-start | bytes 786440 | tf_op jit(solution)/shard_map/ppermute | solution.py:18

commit v12 on v10

--- a/solution.py
+++ b/solution.py
@@ -77,7 +77,7 @@
     nodes, wide = noise.shape[0], solved[0].shape[-1]
     draws = sum(map(len, steps))
     rows = inv.shape[1] // draws
-    fill_inverse(inv, row_blocks(parts, steps, nodes * rows), 0, rows, draw)
+    fill_inverse(inv, row_blocks(parts, steps, 2 * nodes * rows), 0, rows, draw)
     for at, target in enumerate(solved):
         for node in range(nodes):
             right = noise[node, :, at * wide:(at + 1) * wide]
@@ -88,21 +88,28 @@
             send[at] = target[node]
 
 
-def relay_kernel(owners, source, follow, waits, joined, picks, far, *refs):
+def relay_kernel(owners, source, waits, joined, steps, picks, far, *refs):
     half = owners // 2
-    own, refs = take(refs, follow)
     _, refs = take(refs, waits)
     parts, refs = take(refs, joined)
-    sends, joint = take(refs, half - 1)
-    myself = lax.axis_index("leaf")
+    inverse, refs = take(refs, len(steps))
+    sends, (joint, *refs) = take(refs, half - 1)
+    myself, draw = lax.axis_index("leaf"), lax.axis_index("draw")
+    at = 0
+    for part in parts:
+        joint[at:at + part.shape[0], :] = part[...]
+        at += part.shape[0]
+    if inverse:
+        solved, inv = refs
+        nodes = far.shape[0]
+        rows = inv.shape[1] // sum(map(len, steps))
+        found = row_blocks(inverse, steps, 2 * nodes * rows)
+        fill_inverse(inv, found, nodes * rows, rows, draw)
+        for node in range(nodes):
+            solved[node] = transposed_dot(inv[node], far[node]).astype(BF16)
+        far = solved
     for step, send in enumerate(sends, 1):
         send[0] = far[picks[source, myself ^ step, myself ^ half]]
-        if own:
-            send[1] = own[0][picks[source, myself ^ step, myself]]
-    at = 0
-    for part in parts:
-        joint[0][at:at + part.shape[0], :] = part[...]
-        at += part.shape[0]
 
 
 def level_kernel(
@@ -182,7 +189,9 @@
     inv_here = pltpu.VMEM((nodes, rows, rows), BF16)
     dot_flops = 2 * rows * rows * wide
 
-    parts, steps = far_rows(flat(inverse[0]), "draw", draws)
+    far = leaf(noise[0], half)
+    both = jnp.concatenate([flat(inverse[0]), leaf(flat(inverse[0]), half)])
+    parts, steps = far_rows(both, "draw", draws)
     parts, steps = near_rows(jnp.concatenate(parts), steps, "draw", draws)
     *refs, pack = call(
         functools.partial(first_kernel, CHUNKS, steps),
@@ -198,34 +207,30 @@
     done, pieces = [solved], []
     for level in range(1, levels):
         source = level - 1
-        far = [leaf(value, half) for value in solved]
+        if source:
+            far = leaf(solved[0], half)
         got = near(sends)
-        close = [[(ref, at) for ref in got] for at in chunks] if source == 0 else [[(ref, 0) for ref in got]]
-        distant, waits = [], got
         joined, far_steps = far_rows(pack, "draw", draws)
-        joint = sum(value.shape[0] for value in joined)
-        for at in chunks:
-            follow = source > 0 and at < CHUNKS - 1
-            sends = call(
-                functools.partial(relay_kernel, owners, source, int(follow), len(waits), len(joined)),
-                [shape(1 + follow, rows, wide)] * (half - 1) + [shape(joint, rows)] * bool(joined),
-                [],
-                (picks,),
-                (far[at], *([solved[at + 1]] if follow else []), *waits, *joined),
-            )
-            if joined:
-                *sends, joint = sends
-                packs.append(near_rows(joint, far_steps, "draw", draws)[0])
-                joined = []
-            got = near(sends)
-            distant.append([(ref, 0) for ref in got])
-            if follow:
-                close.append([(ref, 1) for ref in got])
-            waits = []
-        pieces.append([
-            [(solved[at], 0), *close[at], (far[at], 0), *distant[at]] for at in chunks
-        ])
-        waits = sends[:1]
+        outs = call(
+            functools.partial(
+                relay_kernel, owners, source, len(got), len(joined), [] if source else steps
+            ),
+            [shape(1, rows, wide)] * (half - 1)
+            + [shape(sum(value.shape[0] for value in joined), rows)]
+            + ([] if source else [part]),
+            [] if source else [inv_here],
+            (picks,),
+            (far, *got, *joined, *([] if source else parts)),
+            flops=0 if source else nodes * dot_flops,
+        )
+        sends, joint = outs[:half - 1], outs[half - 1]
+        far = far if source else outs[half]
+        packs.append(near_rows(joint, far_steps, "draw", draws)[0])
+        pieces.append([[
+            (solved[0], 0), *((ref, 0) for ref in got),
+            (far, 0), *((ref, 0) for ref in near(sends)),
+        ]])
+        waits = []
         solved, sends = [], []
         for at in chunks:
             packing = at == 0 and level < last_level

time: 106 us -> 112 us (1.057)
  waiting for transfers between devices: 70.3 us -> 74.4 us
  starting transfers between devices: 23.8 us -> 25.4 us
    ppermute x20 -> x21, waiting for transfers between devices: 70.3 us -> 74.4 us  [hop(): return lax.ppermute(value, axis, [(at, at ^ step) for at in range(size)])]
    ppermute x20 -> x21, starting transfers between devices: 23.8 us -> 25.4 us  [hop(): return lax.ppermute(value, axis, [(at, at ^ step) for at in range(size)])]
  transfers between devices with their start and end apart: 20 -> 21, of which waited for: 14 -> 14; matrix products, arithmetic and copies ran while one was open for 1% -> 1% of each run, Pallas kernels for 0% -> 0%
where the time goes in v12:
time: 112 us; the launch traced here: 111 us
  waiting for transfers between devices  74.4 us (66%)
  starting transfers between devices  25.4 us (23%)
  Pallas kernels  9.05 us (8%)
  local copies, waits for them, and re-layouts  2.25 us (2%)
    ppermute x21, waiting for transfers between devices, hop(): return lax.ppermute(value, axis, [(at, at ^ step) for at in range(size)])  74.4 us
    ppermute x21, starting transfers between devices, hop(): return lax.ppermute(value, axis, [(at, at ^ step) for at in range(size)])  25.4 us
    pallas_call x5, Pallas kernels, call(): pl.pallas_call(kernel, out_shape=outs, in_specs=[SMEM] * len(small) + [VM...  9.05 us
  transfers between devices with their start and end apart: 21, of which 14 were waited for; matrix products, arithmetic and copies ran while one was open for 1% of the time, Pallas kernels for 0%

profile of v12, /device:TPU:0, one launch (start us, length us, event | category | flops | bytes accessed | tf_op | source)
XLA Modules:
  0.0 111.4 jit_solution(7443441383355290231)
XLA Ops:
  0.9 4.1 %collective-permute-start.1 = (bf16[128,256]{1,0:T(8,128)(2,1)S(1)}, bf16[128,256]{1,0:T(8,128)(2,1)S(1)}, u32[]{:S(2)}, u32[]{:S(2)}) collective-permute-start(bf16[128,256]{1,0:T(8,128)(2,1)S(1)} %bitcast.9), channel_id=1, source_target_pairs={{0,16},{4,20},{8,24},{12,28},{16,0},{20,4},{24,8},{28,12},{1,17},{... | collective-permute-start | bytes 196616 | tf_op jit(solution)/shard_map/ppermute | solution.py:18
  5.0 3.6 %collective-permute-done.1 = bf16[128,256]{1,0:T(8,128)(2,1)S(1)} collective-permute-done((bf16[128,256]{1,0:T(8,128)(2,1)S(1)}, bf16[128,256]{1,0:T(8,128)(2,1)S(1)}, u32[]{:S(2)}, u32[]{:S(2)}) %collective-permute-start.1) | collective-permute-done | bytes 65568 | tf_op jit(solution)/shard_map/ppermute | solution.py:18
  8.7 1.8 %collective-permute-start.2 = (bf16[256,256]{1,0:T(8,128)(2,1)S(1)}, bf16[256,256]{1,0:T(8,128)(2,1)S(1)}, u32[]{:S(2)}, u32[]{:S(2)}) collective-permute-start(bf16[256,256]{1,0:T(8,128)(2,1)S(1)} %pad_maximum_fusion.3), channel_id=1, source_target_pairs={{0,2},{1,3},{2,0},{3,1},{4,6},{5,7},{6,4},{7,5},{8,10},{9,11},{10,... | collective-permute-start | bytes 393224 | tf_op jit(solution)/shard_map/ppermute | solution.py:18
  10.5 1.3 %fusion = (bf16[1,2,2,256,256]{4,3,2,1,0:T(8,128)(2,1)S(1)}, bf16[1,2,2,256,256]{4,3,2,1,0:T(8,128)(2,1)S(1)}) fusion(bf16[2,2,2,256,256]{4,3,2,1,0:T(8,128)(2,1)} %param.8), kind=kLoop, calls=%fused_computation.5 | loop fusion | bytes 2097152 | tf_op jit(solution)/shard_map/slice | solution.py:183
  11.7 2.0 %collective-permute-done.2 = bf16[256,256]{1,0:T(8,128)(2,1)S(1)} collective-permute-done((bf16[256,256]{1,0:T(8,128)(2,1)S(1)}, bf16[256,256]{1,0:T(8,128)(2,1)S(1)}, u32[]{:S(2)}, u32[]{:S(2)}) %collective-permute-start.2) | collective-permute-done | bytes 131104 | tf_op jit(solution)/shard_map/ppermute | solution.py:18
  13.9 1.4 %collective-permute-done.3.refs_1_.refs_6_ = bf16[512,256]{1,0:T(8,128)(2,1)S(1)} collective-permute-done((bf16[512,256]{1,0:T(8,128)(2,1)S(1)}, bf16[512,256]{1,0:T(8,128)(2,1)S(1)}, u32[]{:S(2)}, u32[]{:S(2)}) %collective-permute-start.3) | collective-permute-done | bytes 262176 | tf_op jit(solution)/shard_map/ppermute | solution.py:18
  15.4 1.1 shard_map.64
  16.4 1.8 %collective-permute-start.7 = (bf16[1152,256]{1,0:T(8,128)(2,1)S(1)}, bf16[1152,256]{1,0:T(8,128)(2,1)S(1)}, u32[]{:S(2)}, u32[]{:S(2)}) collective-permute-start(bf16[1152,256]{1,0:T(8,128)(2,1)S(1)} %get-tuple-element.27.refs_3_), channel_id=1, source_target_pairs={{0,2},{1,3},{2,0},{3,1},{4,6},{5,7},{6,4},{7,5},{8,10},{9,11},{10,... | collective-permute-start | bytes 1769480 | tf_op jit(solution)/shard_map/ppermute | solution.py:18
  18.2 1.3 %collective-permute-start = (bf16[2,256,512]{2,1,0:T(8,128)(2,1)S(1)}, bf16[2,256,512]{2,1,0:T(8,128)(2,1)S(1)}, u32[]{:S(2)}, u32[]{:S(2)}) collective-permute-start(bf16[2,256,512]{2,1,0:T(8,128)(2,1)S(1)} %slice_bitcast_fusion.noise), channel_id=1, source_target_pairs={{0,16},{4,20},{8,24},{12,28},{16,0},{20,4},{24,8},{28,12},{1,17},{... | collective-permute-start | bytes 1572872 | tf_op jit(solution)/shard_map/ppermute | solution.py:18
  19.5 1.5 %collective-permute-start.4 = (bf16[1,256,512]{2,1,0:T(8,128)(2,1)S(1)}, bf16[1,256,512]{2,1,0:T(8,128)(2,1)S(1)}, u32[]{:S(2)}, u32[]{:S(2)}) collective-permute-start(bf16[1,256,512]{2,1,0:T(8,128)(2,1)S(1)} %get-tuple-element.24), channel_id=1, source_target_pairs={{0,4},{4,0},{8,12},{12,8},{16,20},{20,16},{24,28},{28,24},{1,5},{5... | collective-permute-start | bytes 786440 | tf_op jit(solution)/shard_map/ppermute | solution.py:18
  21.0 2.5 %collective-permute-start.5 = (bf16[1,256,512]{2,1,0:T(8,128)(2,1)S(1)}, bf16[1,256,512]{2,1,0:T(8,128)(2,1)S(1)}, u32[]{:S(2)}, u32[]{:S(2)}) collective-permute-start(bf16[1,256,512]{2,1,0:T(8,128)(2,1)S(1)} %get-tuple-element.25), channel_id=1, source_target_pairs={{0,8},{4,12},{8,0},{12,4},{16,24},{20,28},{24,16},{28,20},{1,9},{5... | collective-permute-start | bytes 786440 | tf_op jit(solution)/shard_map/ppermute | solution.py:18
  23.6 20.6 %collective-permute-done.far = bf16[2,256,512]{2,1,0:T(8,128)(2,1)S(1)} collective-permute-done((bf16[2,256,512]{2,1,0:T(8,128)(2,1)S(1)}, bf16[2,256,512]{2,1,0:T(8,128)(2,1)S(1)}, u32[]{:S(2)}, u32[]{:S(2)}) %collective-permute-start) | collective-permute-done | bytes 524320 | tf_op jit(solution)/shard_map/ppermute | solution.py:18
  44.1 1.3 %collective-permute-done.6.refs_2_.refs_5_ = bf16[1,256,512]{2,1,0:T(8,128)(2,1)S(1)} collective-permute-done((bf16[1,256,512]{2,1,0:T(8,128)(2,1)S(1)}, bf16[1,256,512]{2,1,0:T(8,128)(2,1)S(1)}, u32[]{:S(2)}, u32[]{:S(2)}) %collective-permute-start.6) | collective-permute-done | bytes 262176 | tf_op jit(solution)/shard_map/ppermute | solution.py:18
  45.4 1.1 %shard_map.65 = (bf16[1,256,512]{2,1,0:T(8,128)(2,1)S(1)}, bf16[1,256,512]{2,1,0:T(8,128)(2,1)S(1)}, bf16[1,256,512]{2,1,0:T(8,128)(2,1)S(1)}, bf16[2304,256]{1,0:T(8,128)(2,1)S(1)}, bf16[2,256,512]{2,1,0:T(8,128)(2,1)S(1)}) custom-call(s32[2,8,8]{2,1,0:T(8,128)S(1)} %copy-done.1, bf16[2,256,512]{2,1,0:T(8,128)(2,1)S(1)} %collective-permute-done.far, ...), custom_call_target="tpu_custom_call" | custom-call | flops 134217728 | bytes 5505024 | tf_op jit(solution)/shard_map/pallas_call | solution.py:45
  46.6 1.6 %collective-permute-start.9 = (bf16[1,256,512]{2,1,0:T(8,128)(2,1)S(1)}, bf16[1,256,512]{2,1,0:T(8,128)(2,1)S(1)}, u32[]{:S(2)}, u32[]{:S(2)}) collective-permute-start(bf16[1,256,512]{2,1,0:T(8,128)(2,1)S(1)} %get-tuple-element.31), channel_id=1, source_target_pairs={{0,4},{4,0},{8,12},{12,8},{16,20},{20,16},{24,28},{28,24},{1,5},{5... | collective-permute-start | bytes 786440 | tf_op jit(solution)/shard_map/ppermute | solution.py:18
  48.2 2.0 %collective-permute-start.11 = (bf16[1,256,512]{2,1,0:T(8,128)(2,1)S(1)}, bf16[1,256,512]{2,1,0:T(8,128)(2,1)S(1)}, u32[]{:S(2)}, u32[]{:S(2)}) collective-permute-start(bf16[1,256,512]{2,1,0:T(8,128)(2,1)S(1)} %get-tuple-element.33), channel_id=1, source_target_pairs={{0,12},{4,8},{8,4},{12,0},{16,28},{20,24},{24,20},{28,16},{1,13},{... | collective-permute-start | bytes 786440 | tf_op jit(solution)/shard_map/ppermute | solution.py:18
  50.2 5.1 %collective-permute-done.9.refs_7_ = bf16[1,256,512]{2,1,0:T(8,128)(2,1)S(1)} collective-permute-done((bf16[1,256,512]{2,1,0:T(8,128)(2,1)S(1)}, bf16[1,256,512]{2,1,0:T(8,128)(2,1)S(1)}, u32[]{:S(2)}, u32[]{:S(2)}) %collective-permute-start.9) | collective-permute-done | bytes 262176 | tf_op jit(solution)/shard_map/ppermute | solution.py:18
  55.3 2.0 %collective-permute-done.10.refs_8_ = bf16[1,256,512]{2,1,0:T(8,128)(2,1)S(1)} collective-permute-done((bf16[1,256,512]{2,1,0:T(8,128)(2,1)S(1)}, bf16[1,256,512]{2,1,0:T(8,128)(2,1)S(1)}, u32[]{:S(2)}, u32[]{:S(2)}) %collective-permute-start.10) | collective-permute-done | bytes 262176 | tf_op jit(solution)/shard_map/ppermute | solution.py:18
  57.4 4.8 %collective-permute-done.11.refs_9_ = bf16[1,256,512]{2,1,0:T(8,128)(2,1)S(1)} collective-permute-done((bf16[1,256,512]{2,1,0:T(8,128)(2,1)S(1)}, bf16[1,256,512]{2,1,0:T(8,128)(2,1)S(1)}, u32[]{:S(2)}, u32[]{:S(2)}) %collective-permute-start.11) | collective-permute-done | bytes 262176 | tf_op jit(solution)/shard_map/ppermute | solution.py:18
  62.2 2.6 %shard_map.66 = (bf16[2,256,512]{2,1,0:T(8,128)(2,1)S(1)}, bf16[1,256,512]{2,1,0:T(8,128)(2,1)S(1)}, bf16[1,256,512]{2,1,0:T(8,128)(2,1)S(1)}, bf16[1,256,512]{2,1,0:T(8,128)(2,1)S(1)}, bf16[1152,256]{1,0:T(8,128)(2,1)S(1)}) custom-call(s32[2,8,8]{2,1,0:T(8,128)S(1)} %copy-done.1, s32[2,2,8]{2,1,0:T(2,128)S(1)} %copy-done.2, ...), custom_call_target="tpu_custom_call", output_to_operand_aliasing={{4}: (14, {})} | custom-call | flops 1207959552 | bytes 9043968 | tf_op jit(solution)/shard_map/pallas_call | solution.py:45
  65.4 1.0 collective-permute-start.12
  66.4 1.5 %collective-permute-start.13 = (bf16[1,256,512]{2,1,0:T(8,128)(2,1)S(1)}, bf16[1,256,512]{2,1,0:T(8,128)(2,1)S(1)}, u32[]{:S(2)}, u32[]{:S(2)}) collective-permute-start(bf16[1,256,512]{2,1,0:T(8,128)(2,1)S(1)} %get-tuple-element.35), channel_id=1, source_target_pairs={{0,4},{4,0},{8,12},{12,8},{16,20},{20,16},{24,28},{28,24},{1,5},{5... | collective-permute-start | bytes 786440 | tf_op jit(solution)/shard_map/ppermute | solution.py:18
  67.9 1.7 %collective-permute-start.14 = (bf16[1,256,512]{2,1,0:T(8,128)(2,1)S(1)}, bf16[1,256,512]{2,1,0:T(8,128)(2,1)S(1)}, u32[]{:S(2)}, u32[]{:S(2)}) collective-permute-start(bf16[1,256,512]{2,1,0:T(8,128)(2,1)S(1)} %get-tuple-element.36), channel_id=1, source_target_pairs={{0,8},{4,12},{8,0},{12,4},{16,24},{20,28},{24,16},{28,20},{1,9},{5... | collective-permute-start | bytes 786440 | tf_op jit(solution)/shard_map/ppermute | solution.py:18
  69.9 4.8 %collective-permute-done.13.refs_0_.refs_11_ = bf16[1,256,512]{2,1,0:T(8,128)(2,1)S(1)} collective-permute-done((bf16[1,256,512]{2,1,0:T(8,128)(2,1)S(1)}, bf16[1,256,512]{2,1,0:T(8,128)(2,1)S(1)}, u32[]{:S(2)}, u32[]{:S(2)}) %collective-permute-start.13) | collective-permute-done | bytes 262176 | tf_op jit(solution)/shard_map/ppermute | solution.py:18
  74.7 9.7 %collective-permute-done.14.refs_1_.refs_12_ = bf16[1,256,512]{2,1,0:T(8,128)(2,1)S(1)} collective-permute-done((bf16[1,256,512]{2,1,0:T(8,128)(2,1)S(1)}, bf16[1,256,512]{2,1,0:T(8,128)(2,1)S(1)}, u32[]{:S(2)}, u32[]{:S(2)}) %collective-permute-start.14) | collective-permute-done | bytes 262176 | tf_op jit(solution)/shard_map/ppermute | solution.py:18
  84.4 7.1 %collective-permute-done.15.refs_2_.refs_13_ = bf16[1,256,512]{2,1,0:T(8,128)(2,1)S(1)} collective-permute-done((bf16[1,256,512]{2,1,0:T(8,128)(2,1)S(1)}, bf16[1,256,512]{2,1,0:T(8,128)(2,1)S(1)}, u32[]{:S(2)}, u32[]{:S(2)}) %collective-permute-start.15) | collective-permute-done | bytes 262176 | tf_op jit(solution)/shard_map/ppermute | solution.py:18
  92.4 1.7 %collective-permute-start.18 = (bf16[1,256,512]{2,1,0:T(8,128)(2,1)S(1)}, bf16[1,256,512]{2,1,0:T(8,128)(2,1)S(1)}, u32[]{:S(2)}, u32[]{:S(2)}) collective-permute-start(bf16[1,256,512]{2,1,0:T(8,128)(2,1)S(1)} %get-tuple-element.40), channel_id=1, source_target_pairs={{0,4},{4,0},{8,12},{12,8},{16,20},{20,16},{24,28},{28,24},{1,5},{5... | collective-permute-start | bytes 786440 | tf_op jit(solution)/shard_map/ppermute | solution.py:18
  94.1 1.9 %collective-permute-start.20 = (bf16[1,256,512]{2,1,0:T(8,128)(2,1)S(1)}, bf16[1,256,512]{2,1,0:T(8,128)(2,1)S(1)}, u32[]{:S(2)}, u32[]{:S(2)}) collective-permute-start(bf16[1,256,512]{2,1,0:T(8,128)(2,1)S(1)} %get-tuple-element.42), channel_id=1, source_target_pairs={{0,12},{4,8},{8,4},{12,0},{16,28},{20,24},{24,20},{28,16},{1,13},{... | collective-permute-start | bytes 786440 | tf_op jit(solution)/shard_map/ppermute | solution.py:18
  95.9 5.2 %collective-permute-done.18.refs_15_ = bf16[1,256,512]{2,1,0:T(8,128)(2,1)S(1)} collective-permute-done((bf16[1,256,512]{2,1,0:T(8,128)(2,1)S(1)}, bf16[1,256,512]{2,1,0:T(8,128)(2,1)S(1)}, u32[]{:S(2)}, u32[]{:S(2)}) %collective-permute-start.18) | collective-permute-done | bytes 262176 | tf_op jit(solution)/shard_map/ppermute | solution.py:18
  101.1 2.1 %collective-permute-done.19.refs_16_ = bf16[1,256,512]{2,1,0:T(8,128)(2,1)S(1)} collective-permute-done((bf16[1,256,512]{2,1,0:T(8,128)(2,1)S(1)}, bf16[1,256,512]{2,1,0:T(8,128)(2,1)S(1)}, u32[]{:S(2)}, u32[]{:S(2)}) %collective-permute-start.19) | collective-permute-done | bytes 262176 | tf_op jit(solution)/shard_map/ppermute | solution.py:18
  103.2 4.7 %collective-permute-done.20.refs_17_ = bf16[1,256,512]{2,1,0:T(8,128)(2,1)S(1)} collective-permute-done((bf16[1,256,512]{2,1,0:T(8,128)(2,1)S(1)}, bf16[1,256,512]{2,1,0:T(8,128)(2,1)S(1)}, u32[]{:S(2)}, u32[]{:S(2)}) %collective-permute-start.20) | collective-permute-done | bytes 262176 | tf_op jit(solution)/shard_map/ppermute | solution.py:18
  107.9 3.5 %shard_map.68 = bf16[3,2,256,512]{3,2,1,0:T(8,128)(2,1)} custom-call(s32[2,8,8]{2,1,0:T(8,128)S(1)} %copy-done.1, s32[2,2,8]{2,1,0:T(2,128)S(1)} %copy-done.2, s32[2,2]{1,0:T(2,128)S(1)} %copy-done.3, bf16[3,2,256,512]{3,2,1,0:T(8,128)(2,1)S(1)} %copy-done, bf16[2304,256]{1,0:T(8,128)(2,1)S(1)} %get-tuple-element.39.refs_0_, ...), custom_call_target="tpu_custom_call" | custom-call | flops 1207959552 | bytes 11796480 | tf_op jit(solution)/shard_map/pallas_call | solution.py:45
  (30 shorter events, 3.0 us)
Async XLA Ops:
  0.9 7.8 %collective-permute-start.1 = (bf16[128,256]{1,0:T(8,128)(2,1)S(1)}, bf16[128,256]{1,0:T(8,128)(2,1)S(1)}, u32[]{:S(2)}, u32[]{:S(2)}) collective-permute-start(bf16[128,256]{1,0:T(8,128)(2,1)S(1)} %bitcast.9), channel_id=1, source_target_pairs={{0,16},{4,20},{8,24},{12,28},{16,0},{20,4},{24,8},{28,12},{1,17},{... | collective-permute-start | bytes 196616 | tf_op jit(solution)/shard_map/ppermute | solution.py:18
  8.7 5.2 %copy-start = (bf16[3,2,256,512]{3,2,1,0:T(8,128)(2,1)S(1)}, bf16[3,2,256,512]{3,2,1,0:T(8,128)(2,1)}, u32[]{:S(2)}) copy-start(bf16[3,2,256,512]{3,2,1,0:T(8,128)(2,1)} %noise.3) | copy-start | bytes 4718596
  8.7 5.0 %collective-permute-start.2 = (bf16[256,256]{1,0:T(8,128)(2,1)S(1)}, bf16[256,256]{1,0:T(8,128)(2,1)S(1)}, u32[]{:S(2)}, u32[]{:S(2)}) collective-permute-start(bf16[256,256]{1,0:T(8,128)(2,1)S(1)} %pad_maximum_fusion.3), channel_id=1, source_target_pairs={{0,2},{1,3},{2,0},{3,1},{4,6},{5,7},{6,4},{7,5},{8,10},{9,11},{10,... | collective-permute-start | bytes 393224 | tf_op jit(solution)/shard_map/ppermute | solution.py:18
  13.8 1.6 %copy-start.1 = (s32[2,8,8]{2,1,0:T(8,128)S(1)}, s32[2,8,8]{2,1,0:T(8,128)}, u32[]{:S(2)}) copy-start(s32[2,8,8]{2,1,0:T(8,128)} %picks.9) | copy-start | bytes 1540
  13.8 1.6 %collective-permute-start.3 = (bf16[512,256]{1,0:T(8,128)(2,1)S(1)}, bf16[512,256]{1,0:T(8,128)(2,1)S(1)}, u32[]{:S(2)}, u32[]{:S(2)}) collective-permute-start(bf16[512,256]{1,0:T(8,128)(2,1)S(1)} %pad_maximum_fusion.2.refs_0_.refs_5_), channel_id=1, source_target_pairs={{0,1},{1,0},{2,3},{3,2},{4,5},{5,4},{6,7},{7,6},{8,9},{9,8},{10,11... | collective-permute-start | bytes 786440 | tf_op jit(solution)/shard_map/ppermute | solution.py:18
  16.4 29.0 %collective-permute-start.7 = (bf16[1152,256]{1,0:T(8,128)(2,1)S(1)}, bf16[1152,256]{1,0:T(8,128)(2,1)S(1)}, u32[]{:S(2)}, u32[]{:S(2)}) collective-permute-start(bf16[1152,256]{1,0:T(8,128)(2,1)S(1)} %get-tuple-element.27.refs_3_), channel_id=1, source_target_pairs={{0,2},{1,3},{2,0},{3,1},{4,6},{5,7},{6,4},{7,5},{8,10},{9,11},{10,... | collective-permute-start | bytes 1769480 | tf_op jit(solution)/shard_map/ppermute | solution.py:18
  18.2 25.9 %collective-permute-start = (bf16[2,256,512]{2,1,0:T(8,128)(2,1)S(1)}, bf16[2,256,512]{2,1,0:T(8,128)(2,1)S(1)}, u32[]{:S(2)}, u32[]{:S(2)}) collective-permute-start(bf16[2,256,512]{2,1,0:T(8,128)(2,1)S(1)} %slice_bitcast_fusion.noise), channel_id=1, source_target_pairs={{0,16},{4,20},{8,24},{12,28},{16,0},{20,4},{24,8},{28,12},{1,17},{... | collective-permute-start | bytes 1572872 | tf_op jit(solution)/shard_map/ppermute | solution.py:18
  19.5 24.6 %collective-permute-start.4 = (bf16[1,256,512]{2,1,0:T(8,128)(2,1)S(1)}, bf16[1,256,512]{2,1,0:T(8,128)(2,1)S(1)}, u32[]{:S(2)}, u32[]{:S(2)}) collective-permute-start(bf16[1,256,512]{2,1,0:T(8,128)(2,1)S(1)} %get-tuple-element.24), channel_id=1, source_target_pairs={{0,4},{4,0},{8,12},{12,8},{16,20},{20,16},{24,28},{28,24},{1,5},{5... | collective-permute-start | bytes 786440 | tf_op jit(solution)/shard_map/ppermute | solution.py:18
  21.0 23.1 %collective-permute-start.5 = (bf16[1,256,512]{2,1,0:T(8,128)(2,1)S(1)}, bf16[1,256,512]{2,1,0:T(8,128)(2,1)S(1)}, u32[]{:S(2)}, u32[]{:S(2)}) collective-permute-start(bf16[1,256,512]{2,1,0:T(8,128)(2,1)S(1)} %get-tuple-element.25), channel_id=1, source_target_pairs={{0,8},{4,12},{8,0},{12,4},{16,24},{20,28},{24,16},{28,20},{1,9},{5... | collective-permute-start | bytes 786440 | tf_op jit(solution)/shard_map/ppermute | solution.py:18
  23.6 21.8 %collective-permute-start.6 = (bf16[1,256,512]{2,1,0:T(8,128)(2,1)S(1)}, bf16[1,256,512]{2,1,0:T(8,128)(2,1)S(1)}, u32[]{:S(2)}, u32[]{:S(2)}) collective-permute-start(bf16[1,256,512]{2,1,0:T(8,128)(2,1)S(1)} %get-tuple-element.26), channel_id=1, source_target_pairs={{0,12},{4,8},{8,4},{12,0},{16,28},{20,24},{24,20},{28,16},{1,13},{... | collective-permute-start | bytes 786440 | tf_op jit(solution)/shard_map/ppermute | solution.py:18
  46.5 15.6 %copy-start.2 = (s32[2,2,8]{2,1,0:T(2,128)S(1)}, s32[2,2,8]{2,1,0:T(2,128)}, u32[]{:S(2)}) copy-start(s32[2,2,8]{2,1,0:T(2,128)} %lists.3) | copy-start | bytes 388
  46.5 15.6 %copy-start.3 = (s32[2,2]{1,0:T(2,128)S(1)}, s32[2,2]{1,0:T(2,128)}, u32[]{:S(2)}) copy-start(s32[2,2]{1,0:T(2,128)} %counts.3) | copy-start | bytes 52
  46.5 15.6 %collective-permute-start.8 = (bf16[2304,256]{1,0:T(8,128)(2,1)S(1)}, bf16[2304,256]{1,0:T(8,128)(2,1)S(1)}, u32[]{:S(2)}, u32[]{:S(2)}) collective-permute-start(bf16[2304,256]{1,0:T(8,128)(2,1)S(1)} %get-tuple-element.28.refs_0_), channel_id=1, source_target_pairs={{0,1},{1,0},{2,3},{3,2},{4,5},{5,4},{6,7},{7,6},{8,9},{9,8},{10,11... | collective-permute-start | bytes 3538952 | tf_op jit(solution)/shard_map/ppermute | solution.py:18
  46.6 8.7 %collective-permute-start.9 = (bf16[1,256,512]{2,1,0:T(8,128)(2,1)S(1)}, bf16[1,256,512]{2,1,0:T(8,128)(2,1)S(1)}, u32[]{:S(2)}, u32[]{:S(2)}) collective-permute-start(bf16[1,256,512]{2,1,0:T(8,128)(2,1)S(1)} %get-tuple-element.31), channel_id=1, source_target_pairs={{0,4},{4,0},{8,12},{12,8},{16,20},{20,16},{24,28},{28,24},{1,5},{5... | collective-permute-start | bytes 786440 | tf_op jit(solution)/shard_map/ppermute | solution.py:18
  48.2 9.2 %collective-permute-start.10 = (bf16[1,256,512]{2,1,0:T(8,128)(2,1)S(1)}, bf16[1,256,512]{2,1,0:T(8,128)(2,1)S(1)}, u32[]{:S(2)}, u32[]{:S(2)}) collective-permute-start(bf16[1,256,512]{2,1,0:T(8,128)(2,1)S(1)} %get-tuple-element.32), channel_id=1, source_target_pairs={{0,8},{4,12},{8,0},{12,4},{16,24},{20,28},{24,16},{28,20},{1,9},{5... | collective-permute-start | bytes 786440 | tf_op jit(solution)/shard_map/ppermute | solution.py:18
  48.2 13.9 %collective-permute-start.11 = (bf16[1,256,512]{2,1,0:T(8,128)(2,1)S(1)}, bf16[1,256,512]{2,1,0:T(8,128)(2,1)S(1)}, u32[]{:S(2)}, u32[]{:S(2)}) collective-permute-start(bf16[1,256,512]{2,1,0:T(8,128)(2,1)S(1)} %get-tuple-element.33), channel_id=1, source_target_pairs={{0,12},{4,8},{8,4},{12,0},{16,28},{20,24},{24,20},{28,16},{1,13},{... | collective-permute-start | bytes 786440 | tf_op jit(solution)/shard_map/ppermute | solution.py:18
  64.8 26.7 %collective-permute-start.16 = (bf16[1152,256]{1,0:T(8,128)(2,1)S(1)}, bf16[1152,256]{1,0:T(8,128)(2,1)S(1)}, u32[]{:S(2)}, u32[]{:S(2)}) collective-permute-start(bf16[1152,256]{1,0:T(8,128)(2,1)S(1)} %get-tuple-element.38.refs_3_), channel_id=1, source_target_pairs={{0,2},{1,3},{2,0},{3,1},{4,6},{5,7},{6,4},{7,5},{8,10},{9,11},{10,... | collective-permute-start | bytes 1769480 | tf_op jit(solution)/shard_map/ppermute | solution.py:18
  65.4 26.1 %collective-permute-start.12 = (bf16[2,256,512]{2,1,0:T(8,128)(2,1)S(1)}, bf16[2,256,512]{2,1,0:T(8,128)(2,1)S(1)}, u32[]{:S(2)}, u32[]{:S(2)}) collective-permute-start(bf16[2,256,512]{2,1,0:T(8,128)(2,1)S(1)} %get-tuple-element.34.refs_10_.refs_19_), channel_id=1, source_target_pairs={{0,16},{4,20},{8,24},{12,28},{16,0},{20,4},{24,8},{28,12},{1,17},{... | collective-permute-start | bytes 1572872 | tf_op jit(solution)/shard_map/ppermute | solution.py:18
  66.4 8.3 %collective-permute-start.13 = (bf16[1,256,512]{2,1,0:T(8,128)(2,1)S(1)}, bf16[1,256,512]{2,1,0:T(8,128)(2,1)S(1)}, u32[]{:S(2)}, u32[]{:S(2)}) collective-permute-start(bf16[1,256,512]{2,1,0:T(8,128)(2,1)S(1)} %get-tuple-element.35), channel_id=1, source_target_pairs={{0,4},{4,0},{8,12},{12,8},{16,20},{20,16},{24,28},{28,24},{1,5},{5... | collective-permute-start | bytes 786440 | tf_op jit(solution)/shard_map/ppermute | solution.py:18
  67.9 16.5 %collective-permute-start.14 = (bf16[1,256,512]{2,1,0:T(8,128)(2,1)S(1)}, bf16[1,256,512]{2,1,0:T(8,128)(2,1)S(1)}, u32[]{:S(2)}, u32[]{:S(2)}) collective-permute-start(bf16[1,256,512]{2,1,0:T(8,128)(2,1)S(1)} %get-tuple-element.36), channel_id=1, source_target_pairs={{0,8},{4,12},{8,0},{12,4},{16,24},{20,28},{24,16},{28,20},{1,9},{5... | collective-permute-start | bytes 786440 | tf_op jit(solution)/shard_map/ppermute | solution.py:18
  69.6 21.9 %collective-permute-start.15 = (bf16[1,256,512]{2,1,0:T(8,128)(2,1)S(1)}, bf16[1,256,512]{2,1,0:T(8,128)(2,1)S(1)}, u32[]{:S(2)}, u32[]{:S(2)}) collective-permute-start(bf16[1,256,512]{2,1,0:T(8,128)(2,1)S(1)} %get-tuple-element.37), channel_id=1, source_target_pairs={{0,12},{4,8},{8,4},{12,0},{16,28},{20,24},{24,20},{28,16},{1,13},{... | collective-permute-start | bytes 786440 | tf_op jit(solution)/shard_map/ppermute | solution.py:18
  92.3 15.6 %collective-permute-start.17 = (bf16[2304,256]{1,0:T(8,128)(2,1)S(1)}, bf16[2304,256]{1,0:T(8,128)(2,1)S(1)}, u32[]{:S(2)}, u32[]{:S(2)}) collective-permute-start(bf16[2304,256]{1,0:T(8,128)(2,1)S(1)} %get-tuple-element.39.refs_0_), channel_id=1, source_target_pairs={{0,1},{1,0},{2,3},{3,2},{4,5},{5,4},{6,7},{7,6},{8,9},{9,8},{10,11... | collective-permute-start | bytes 3538952 | tf_op jit(solution)/shard_map/ppermute | solution.py:18
  92.4 8.7 %collective-permute-start.18 = (bf16[1,256,512]{2,1,0:T(8,128)(2,1)S(1)}, bf16[1,256,512]{2,1,0:T(8,128)(2,1)S(1)}, u32[]{:S(2)}, u32[]{:S(2)}) collective-permute-start(bf16[1,256,512]{2,1,0:T(8,128)(2,1)S(1)} %get-tuple-element.40), channel_id=1, source_target_pairs={{0,4},{4,0},{8,12},{12,8},{16,20},{20,16},{24,28},{28,24},{1,5},{5... | collective-permute-start | bytes 786440 | tf_op jit(solution)/shard_map/ppermute | solution.py:18
  94.1 9.2 %collective-permute-start.19 = (bf16[1,256,512]{2,1,0:T(8,128)(2,1)S(1)}, bf16[1,256,512]{2,1,0:T(8,128)(2,1)S(1)}, u32[]{:S(2)}, u32[]{:S(2)}) collective-permute-start(bf16[1,256,512]{2,1,0:T(8,128)(2,1)S(1)} %get-tuple-element.41), channel_id=1, source_target_pairs={{0,8},{4,12},{8,0},{12,4},{16,24},{20,28},{24,16},{28,20},{1,9},{5... | collective-permute-start | bytes 786440 | tf_op jit(solution)/shard_map/ppermute | solution.py:18
  94.1 13.8 %collective-permute-start.20 = (bf16[1,256,512]{2,1,0:T(8,128)(2,1)S(1)}, bf16[1,256,512]{2,1,0:T(8,128)(2,1)S(1)}, u32[]{:S(2)}, u32[]{:S(2)}) collective-permute-start(bf16[1,256,512]{2,1,0:T(8,128)(2,1)S(1)} %get-tuple-element.42), channel_id=1, source_target_pairs={{0,12},{4,8},{8,4},{12,0},{16,28},{20,24},{24,20},{28,16},{1,13},{... | collective-permute-start | bytes 786440 | tf_op jit(solution)/shard_map/ppermute | solution.py:18

commit v13 on v11

v13 whole, which is shorter than its diff:
```python
import functools

import jax
import jax.numpy as jnp
from jax import lax
from jax.experimental import pallas as pl
from jax.experimental.pallas import tpu as pltpu
from jax.sharding import PartitionSpec as P

CHUNKS = 2
VMEM = pl.BlockSpec(memory_space=pltpu.VMEM)
SMEM = pl.BlockSpec(memory_space=pltpu.SMEM)
ANY = pl.BlockSpec(memory_space=pl.ANY)
BF16, F32 = jnp.bfloat16, jnp.float32


def hop(value, axis, size, step):
    return lax.ppermute(value, axis, [(at, at ^ step) for at in range(size)])


def far_rows(value, axis, size):
    values, held, step = [value], [[0]], size // 2
    while step > 1:
        if len(values) > 1:
            values, held = [jnp.concatenate(values)], [held[0] + held[1]]
        values.append(hop(values[0], axis, size, step))
        held.append([have ^ step for have in held[0]])
        step //= 2
    return values, held


def near_rows(values, held, axis, size):
    others = [hop(value, axis, size, 1) for value in values]
    return values + others, held + [[have ^ 1 for have in steps] for steps in held]


def transposed_dot(left, right):
    return lax.dot_general(left, right, (((0,), (0,)), ((), ())), preferred_element_type=F32)


def take(refs, count):
    return list(refs[:count]), list(refs[count:])


def shape(*dims):
    return jax.ShapeDtypeStruct(dims, BF16)


def call(kernel, outs, scratch, small, arrays, out_spec=VMEM, flops=0, aliases={}):
    size = sum(value.size * value.dtype.itemsize for value in (*arrays, *outs))
    return list(pl.pallas_call(
        kernel,
        out_shape=outs,
        in_specs=[SMEM] * len(small) + [VMEM] * len(arrays),
        out_specs=[out_spec] * len(outs),
        scratch_shapes=scratch,
        input_output_aliases=aliases,
        cost_estimate=pl.CostEstimate(flops=flops, bytes_accessed=size, transcendentals=0),
        compiler_params=pltpu.CompilerParams(vmem_limit_bytes=16 * 1024 * 1024),
    )(*small, *arrays))


def row_blocks(refs, held, block):
    return [
        (ref, at * block, step)
        for ref, steps in zip(refs, held, strict=True) for at, step in enumerate(steps)
    ]


def fill_inverse(target, found, offset, draw):
    rows = target.shape[1] // len(found)
    for ref, at, step in found:
        start = pl.multiple_of((draw ^ step) * rows, rows)
        for node in range(target.shape[0]):
            first = at + offset + node * rows
            target[node, pl.ds(start, rows), :] = ref[first:first + rows, :]


def first_kernel(held, picks, noise, *refs):
    parts, (_, solved, *sends, _, inv) = take(refs, len(held))
    myself, draw = lax.axis_index("leaf"), lax.axis_index("draw")
    nodes = noise.shape[0]
    draws = sum(map(len, held))
    rows = inv.shape[1] // draws
    fill_inverse(inv, row_blocks(parts, held, nodes * rows), 0, draw)
    for node in range(nodes):
        solved[node] = transposed_dot(inv[node], noise[node]).astype(BF16)
    for step, send in enumerate(sends, 1):
        send[0] = solved[picks[0, myself ^ step, myself]]


def relay_kernel(half, source, follow, waits, through, picks, far, *refs):
    own, refs = take(refs, follow)
    sends = refs[waits + through:][:half - 1]
    myself = lax.axis_index("leaf")
    for step, send in enumerate(sends, 1):
        send[0] = far[picks[source, myself ^ step, myself ^ half]]
        if follow:
            send[1] = own[0][picks[source, myself ^ step, myself]]


def level_kernel(
    level, owners, held, width, chunk, places, stored, sides, picks, lists, counts, noise, *refs
):
    half = owners // 2
    packs, refs = take(refs, len(held))
    known, refs = take(refs, level * owners)
    done, refs = take(refs, len(stored))
    target, *refs = refs
    sends, (table, inv, *refs) = take(refs, sides)
    myself, draw = lax.axis_index("leaf"), lax.axis_index("draw")
    levels, nodes = noise.shape[:2]
    wide = table.shape[-1]
    columns = slice(chunk * wide, (chunk + 1) * wide)
    depth = inv.shape[1]
    rows = depth // sum(map(len, held))
    span = nodes * (width * depth + rows)
    found = row_blocks(packs, held, (levels - 1) * span)
    offset = (level - 1) * span
    copies = []
    solved = target
    if done:
        solved, sems = refs
        for at, (ref, (into, first)) in enumerate(zip(done, stored, strict=True)):
            here = target.at[into, :, :, pl.ds(first, ref.shape[-1])]
            copies.append(pltpu.make_async_copy(ref, here, sems.at[at]))
            copies[-1].start()
    for at, (ref, place) in enumerate(zip(known, places, strict=True)):
        step = at % owners
        if step % half == 0:
            place = picks[at // owners, myself, myself ^ step]
        table[at] = ref[place] if ref.shape[-1] == wide else ref[place, :, columns]
    empty = level * owners
    table[empty] = jnp.zeros_like(table[empty])
    fill_inverse(inv, found, offset + nodes * width * depth, draw)
    for node in range(nodes):
        total = None
        for pack, start, step in found:
            for slot in range(width):
                entry = (draw ^ step) * width + slot
                live = entry < counts[level - 1, node]
                entry = jnp.where(live, lists[level - 1, node, entry] ^ myself, empty)
                at = start + offset + (node * width + slot) * depth
                term = transposed_dot(pack[at:at + depth, :], table[entry])
                total = term if total is None else total + term
        right_side = (noise[level, node, :, columns].astype(F32) - total).astype(BF16)
        solved[node] = transposed_dot(inv[node], right_side).astype(BF16)
    for step, send in enumerate(sends, 1):
        send[0] = solved[picks[level, myself ^ step, myself]]
    if done:
        here = target.at[level, :, :, pl.ds(chunk * wide, wide)]
        copies.append(pltpu.make_async_copy(solved, here, sems.at[len(done)]))
        copies[-1].start()
    for copy in copies:
        copy.wait()


def on_device(owners, draws, noise, inverse, coupling, picks, lists, counts):
    levels, nodes, rows, columns = noise.shape
    wide, half, chunks = columns // CHUNKS, owners // 2, range(CHUNKS)
    width = coupling.shape[2]
    part = shape(nodes, rows, wide)
    flat = lambda value: value.reshape(-1, rows)
    leaf = lambda value, step: hop(value, "leaf", owners, step)
    near = lambda values: [leaf(value, step) for step, value in enumerate(values, 1)]
    inv_here = pltpu.VMEM((nodes, rows, rows), BF16)
    dot_flops = 2 * rows * rows * wide

    raw = jnp.concatenate([
        flat(value) for level in range(1, levels) for value in (coupling[level - 1], inverse[level])
    ])
    values, steps = far_rows(flat(inverse[0]), "draw", draws)
    values, steps = near_rows(values, steps, "draw", draws)
    solved, *sends, raw = call(
        functools.partial(first_kernel, steps),
        [shape(nodes, rows, columns)] + [shape(1, rows, columns)] * (half - 1) + [shape(*raw.shape)],
        [inv_here],
        (picks,),
        (noise[0], *values, raw),
        flops=nodes * CHUNKS * dot_flops,
        aliases={2 + len(values): half},
    )
    far, got = leaf(solved, half), near(sends)
    values, steps = far_rows(raw, "draw", draws)
    sends = call(
        functools.partial(relay_kernel, half, 0, 0, len(got), len(values)),
        [shape(1, rows, columns)] * (half - 1) + [shape(*value.shape) for value in values],
        [],
        (picks,),
        (far, *got, *values),
        aliases={2 + len(got) + at: half - 1 + at for at in range(len(values))},
    )
    sends, values = take(sends, half - 1)
    packs, steps = near_rows(values, steps, "draw", draws)
    entries = [(solved, 0), *((ref, 0) for ref in got), (far, 0), *((ref, 0) for ref in near(sends))]
    pieces, done = [[entries] * CHUNKS], [(solved, (0, 0))]

    for level in range(1, levels):
        last_level = level == levels - 1
        solved, sends = [], []
        for at in chunks:
            sides = half - 1 if at == 0 and not last_level else 0
            final = last_level and at == CHUNKS - 1
            known = [entry for below in range(level) for entry in pieces[below][at]]
            stored = done if final else []
            scratch = [pltpu.VMEM((level * owners + 1, rows, wide), BF16), inv_here]
            if final:
                scratch += [
                    pltpu.VMEM((nodes, rows, wide), BF16),
                    pltpu.SemaphoreType.DMA((len(stored) + 1,)),
                ]
            here, *sent = call(
                functools.partial(
                    level_kernel, level, owners, steps, width, at,
                    [place for _, place in known], [place for _, place in stored], sides,
                ),
                [shape(*noise.shape) if final else part] + [shape(1, rows, wide)] * sides,
                scratch,
                (picks, lists, counts),
                (noise, *packs, *(ref for ref, _ in known), *(ref for ref, _ in stored)),
                out_spec=ANY if final else VMEM,
                flops=nodes * (draws * width + 1) * dot_flops,
            )
            solved.append(here)
            done.append((here, (level, at * wide)))
            sends += sent
        if last_level:
            return here
        far = [leaf(value, half) for value in solved]
        got = near(sends)
        close, distant, waits = [[(ref, 0) for ref in got]], [], got
        for at in chunks:
            follow = solved[at + 1:at + 2]
            sends = call(
                functools.partial(relay_kernel, half, level, len(follow), len(waits), 0),
                [shape(1 + len(follow), rows, wide)] * (half - 1),
                [],
                (picks,),
                (far[at], *follow, *waits),
            )
            got, waits = near(sends), []
            distant.append([(ref, 0) for ref in got])
            close.append([(ref, 1) for ref in got])
        pieces.append([
            [(solved[at], 0), *close[at], (far[at], 0), *distant[at]] for at in chunks
        ])


def solution(mesh):
    placed = (
        P(None, "leaf", None, "draw"),
        P(None, "leaf", "draw", None),
        P(None, "leaf", "draw", None, None),
        P(),
        P(None, "leaf", None),
        P(None, "leaf"),
    )
    return jax.shard_map(
        functools.partial(on_device, mesh.shape["leaf"], mesh.shape["draw"]),
        mesh=mesh,
        in_specs=placed,
        out_specs=P(None, "leaf", None, "draw"),
        check_vma=False,
    )
```

time: 129 us -> 102 us (0.79)
  waiting for transfers between devices: 81.3 us -> 57.1 us
  starting transfers between devices: 30.1 us -> 28.6 us
    ppermute x22 -> x24, waiting for transfers between devices: 81.3 us -> 57.1 us  [hop(): return lax.ppermute(value, axis, [(at, at ^ step) for at in range(size)])]
    ppermute x22 -> x24, starting transfers between devices: 30.1 us -> 28.6 us  [hop(): return lax.ppermute(value, axis, [(at, at ^ step) for at in range(size)])]
    pallas_call x9 -> x8, Pallas kernels: 14.5 us -> 13.7 us  [call(): pl.pallas_call(kernel, out_shape=outs, in_specs=[SMEM] * len(small) + [VM...]
  transfers between devices with their start and end apart: 22 -> 24, of which waited for: 17 -> 16; matrix products, arithmetic and copies ran while one was open for 1% -> 1% of each run, Pallas kernels for 5% -> 6%
where the time goes in v13:
time: 102 us
  waiting for transfers between devices  57.1 us (56%)
  starting transfers between devices  28.6 us (28%)
  Pallas kernels  13.7 us (13%)
  local copies, waits for them, and re-layouts  2.24 us (2%)
    ppermute x24, waiting for transfers between devices, hop(): return lax.ppermute(value, axis, [(at, at ^ step) for at in range(size)])  57.1 us
    ppermute x24, starting transfers between devices, hop(): return lax.ppermute(value, axis, [(at, at ^ step) for at in range(size)])  28.6 us
    pallas_call x8, Pallas kernels, call(): pl.pallas_call(kernel, out_shape=outs, in_specs=[SMEM] * len(small) + [VM...  13.7 us
  transfers between devices with their start and end apart: 24, of which 16 were waited for; matrix products, arithmetic and copies ran while one was open for 1% of the time, Pallas kernels for 6%

profile of v13, /device:TPU:0, one launch (start us, length us, event | category | flops | bytes accessed | tf_op | source)
XLA Modules:
  0.0 102.0 jit_solution(391323225257923948)
XLA Ops:
  1.4 2.6 %collective-permute-start = (bf16[128,256]{1,0:T(8,128)(2,1)S(1)}, bf16[128,256]{1,0:T(8,128)(2,1)S(1)}, u32[]{:S(2)}, u32[]{:S(2)}) collective-permute-start(bf16[128,256]{1,0:T(8,128)(2,1)S(1)} %bitcast.8), channel_id=1, source_target_pairs={{0,2},{1,3},{2,0},{3,1},{4,6},{5,7},{6,4},{7,5},{8,10},{9,11},{10,... | collective-permute-start | bytes 196616 | tf_op jit(solution)/shard_map/ppermute | solution.py:18
  4.0 1.3 %fusion = (bf16[1,2,2,256,256]{4,3,2,1,0:T(8,128)(2,1)S(1)}, bf16[1,2,2,256,256]{4,3,2,1,0:T(8,128)(2,1)S(1)}) fusion(bf16[2,2,2,256,256]{4,3,2,1,0:T(8,128)(2,1)} %param.8), kind=kLoop, calls=%fused_computation.2 | loop fusion | bytes 2097152 | tf_op jit(solution)/shard_map/slice | solution.py:170
  5.4 1.3 %collective-permute-done.refs_1_ = bf16[128,256]{1,0:T(8,128)(2,1)S(1)} collective-permute-done((bf16[128,256]{1,0:T(8,128)(2,1)S(1)}, bf16[128,256]{1,0:T(8,128)(2,1)S(1)}, u32[]{:S(2)}, u32[]{:S(2)}) %collective-permute-start) | collective-permute-done | bytes 65568 | tf_op jit(solution)/shard_map/ppermute | solution.py:18
  6.7 1.2 %collective-permute-done.2.refs_3_ = bf16[128,256]{1,0:T(8,128)(2,1)S(1)} collective-permute-done((bf16[128,256]{1,0:T(8,128)(2,1)S(1)}, bf16[128,256]{1,0:T(8,128)(2,1)S(1)}, u32[]{:S(2)}, u32[]{:S(2)}) %collective-permute-start.2) | collective-permute-done | bytes 65568 | tf_op jit(solution)/shard_map/ppermute | solution.py:18
  9.0 1.8 %collective-permute-start.7 = (bf16[2304,256]{1,0:T(8,128)(2,1)S(1)}, bf16[2304,256]{1,0:T(8,128)(2,1)S(1)}, u32[]{:S(2)}, u32[]{:S(2)}) collective-permute-start(bf16[2304,256]{1,0:T(8,128)(2,1)S(1)} %get-tuple-element.29.refs_3_), channel_id=1, source_target_pairs={{0,2},{1,3},{2,0},{3,1},{4,6},{5,7},{6,4},{7,5},{8,10},{9,11},{10,... | collective-permute-start | bytes 3538952 | tf_op jit(solution)/shard_map/ppermute | solution.py:18
  10.8 2.6 %collective-permute-start.3 = (bf16[2,256,512]{2,1,0:T(8,128)(2,1)S(1)}, bf16[2,256,512]{2,1,0:T(8,128)(2,1)S(1)}, u32[]{:S(2)}, u32[]{:S(2)}) collective-permute-start(bf16[2,256,512]{2,1,0:T(8,128)(2,1)S(1)} %get-tuple-element.25.refs_4_.refs_20_), channel_id=1, source_target_pairs={{0,16},{4,20},{8,24},{12,28},{16,0},{20,4},{24,8},{28,12},{1,17},{... | collective-permute-start | bytes 1572872 | tf_op jit(solution)/shard_map/ppermute | solution.py:18
  13.4 1.5 %collective-permute-start.4 = (bf16[1,256,512]{2,1,0:T(8,128)(2,1)S(1)}, bf16[1,256,512]{2,1,0:T(8,128)(2,1)S(1)}, u32[]{:S(2)}, u32[]{:S(2)}) collective-permute-start(bf16[1,256,512]{2,1,0:T(8,128)(2,1)S(1)} %get-tuple-element.26), channel_id=1, source_target_pairs={{0,4},{4,0},{8,12},{12,8},{16,20},{20,16},{24,28},{28,24},{1,5},{5... | collective-permute-start | bytes 786440 | tf_op jit(solution)/shard_map/ppermute | solution.py:18
  15.0 1.6 %collective-permute-start.5 = (bf16[1,256,512]{2,1,0:T(8,128)(2,1)S(1)}, bf16[1,256,512]{2,1,0:T(8,128)(2,1)S(1)}, u32[]{:S(2)}, u32[]{:S(2)}) collective-permute-start(bf16[1,256,512]{2,1,0:T(8,128)(2,1)S(1)} %get-tuple-element.27), channel_id=1, source_target_pairs={{0,8},{4,12},{8,0},{12,4},{16,24},{20,28},{24,16},{28,20},{1,9},{5... | collective-permute-start | bytes 786440 | tf_op jit(solution)/shard_map/ppermute | solution.py:18
  16.9 4.8 %collective-permute-done.4.refs_0_.refs_5_ = bf16[1,256,512]{2,1,0:T(8,128)(2,1)S(1)} collective-permute-done((bf16[1,256,512]{2,1,0:T(8,128)(2,1)S(1)}, bf16[1,256,512]{2,1,0:T(8,128)(2,1)S(1)}, u32[]{:S(2)}, u32[]{:S(2)}) %collective-permute-start.4) | collective-permute-done | bytes 262176 | tf_op jit(solution)/shard_map/ppermute | solution.py:18
  21.8 9.6 %collective-permute-done.5.refs_1_.refs_6_ = bf16[1,256,512]{2,1,0:T(8,128)(2,1)S(1)} collective-permute-done((bf16[1,256,512]{2,1,0:T(8,128)(2,1)S(1)}, bf16[1,256,512]{2,1,0:T(8,128)(2,1)S(1)}, u32[]{:S(2)}, u32[]{:S(2)}) %collective-permute-start.5) | collective-permute-done | bytes 262176 | tf_op jit(solution)/shard_map/ppermute | solution.py:18
  31.4 6.7 %collective-permute-done.6.refs_2_.refs_7_ = bf16[1,256,512]{2,1,0:T(8,128)(2,1)S(1)} collective-permute-done((bf16[1,256,512]{2,1,0:T(8,128)(2,1)S(1)}, bf16[1,256,512]{2,1,0:T(8,128)(2,1)S(1)}, u32[]{:S(2)}, u32[]{:S(2)}) %collective-permute-start.6) | collective-permute-done | bytes 262176 | tf_op jit(solution)/shard_map/ppermute | solution.py:18
  39.5 1.5 %collective-permute-start.10 = (bf16[1,256,512]{2,1,0:T(8,128)(2,1)S(1)}, bf16[1,256,512]{2,1,0:T(8,128)(2,1)S(1)}, u32[]{:S(2)}, u32[]{:S(2)}) collective-permute-start(bf16[1,256,512]{2,1,0:T(8,128)(2,1)S(1)} %get-tuple-element.32), channel_id=1, source_target_pairs={{0,4},{4,0},{8,12},{12,8},{16,20},{20,16},{24,28},{28,24},{1,5},{5... | collective-permute-start | bytes 786440 | tf_op jit(solution)/shard_map/ppermute | solution.py:18
  43.0 4.8 %collective-permute-done.10.refs_9_ = bf16[1,256,512]{2,1,0:T(8,128)(2,1)S(1)} collective-permute-done((bf16[1,256,512]{2,1,0:T(8,128)(2,1)S(1)}, bf16[1,256,512]{2,1,0:T(8,128)(2,1)S(1)}, u32[]{:S(2)}, u32[]{:S(2)}) %collective-permute-start.10) | collective-permute-done | bytes 262176 | tf_op jit(solution)/shard_map/ppermute | solution.py:18
  47.8 2.4 %collective-permute-done.11.refs_10_ = bf16[1,256,512]{2,1,0:T(8,128)(2,1)S(1)} collective-permute-done((bf16[1,256,512]{2,1,0:T(8,128)(2,1)S(1)}, bf16[1,256,512]{2,1,0:T(8,128)(2,1)S(1)}, u32[]{:S(2)}, u32[]{:S(2)}) %collective-permute-start.11) | collective-permute-done | bytes 262176 | tf_op jit(solution)/shard_map/ppermute | solution.py:18
  50.2 4.4 %collective-permute-done.12.refs_11_ = bf16[1,256,512]{2,1,0:T(8,128)(2,1)S(1)} collective-permute-done((bf16[1,256,512]{2,1,0:T(8,128)(2,1)S(1)}, bf16[1,256,512]{2,1,0:T(8,128)(2,1)S(1)}, u32[]{:S(2)}, u32[]{:S(2)}) %collective-permute-start.12) | collective-permute-done | bytes 262176 | tf_op jit(solution)/shard_map/ppermute | solution.py:18
  54.6 2.4 %shard_map.67 = (bf16[2,256,256]{2,1,0:T(8,128)(2,1)S(1)}, bf16[1,256,256]{2,1,0:T(8,128)(2,1)S(1)}, bf16[1,256,256]{2,1,0:T(8,128)(2,1)S(1)}, bf16[1,256,256]{2,1,0:T(8,128)(2,1)S(1)}) custom-call(s32[2,8,8]{2,1,0:T(8,128)S(1)} %copy-done.1, s32[2,2,8]{2,1,0:T(2,128)S(1)} %copy-done.2, s32[2,2]{1,0:T(2,128)S(1)} %copy-done.3, ...), custom_call_target="tpu_custom_call" | custom-call | flops 603979776 | bytes 9568256 | tf_op jit(solution)/shard_map/pallas_call | solution.py:51
  57.0 1.9 %collective-permute-start.13 = (bf16[2,256,256]{2,1,0:T(8,128)(2,1)S(1)}, bf16[2,256,256]{2,1,0:T(8,128)(2,1)S(1)}, u32[]{:S(2)}, u32[]{:S(2)}) collective-permute-start(bf16[2,256,256]{2,1,0:T(8,128)(2,1)S(1)} %get-tuple-element.35.refs_12_.refs_21_), channel_id=1, source_target_pairs={{0,16},{4,20},{8,24},{12,28},{16,0},{20,4},{24,8},{28,12},{1,17},{... | collective-permute-start | bytes 786440 | tf_op jit(solution)/shard_map/ppermute | solution.py:18
  58.9 1.5 %collective-permute-start.14 = (bf16[1,256,256]{2,1,0:T(8,128)(2,1)S(1)}, bf16[1,256,256]{2,1,0:T(8,128)(2,1)S(1)}, u32[]{:S(2)}, u32[]{:S(2)}) collective-permute-start(bf16[1,256,256]{2,1,0:T(8,128)(2,1)S(1)} %get-tuple-element.36), channel_id=1, source_target_pairs={{0,4},{4,0},{8,12},{12,8},{16,20},{20,16},{24,28},{28,24},{1,5},{5... | collective-permute-start | bytes 393224 | tf_op jit(solution)/shard_map/ppermute | solution.py:18
  60.4 1.6 %collective-permute-start.15 = (bf16[1,256,256]{2,1,0:T(8,128)(2,1)S(1)}, bf16[1,256,256]{2,1,0:T(8,128)(2,1)S(1)}, u32[]{:S(2)}, u32[]{:S(2)}) collective-permute-start(bf16[1,256,256]{2,1,0:T(8,128)(2,1)S(1)} %get-tuple-element.37), channel_id=1, source_target_pairs={{0,8},{4,12},{8,0},{12,4},{16,24},{20,28},{24,16},{28,20},{1,9},{5... | collective-permute-start | bytes 393224 | tf_op jit(solution)/shard_map/ppermute | solution.py:18
  62.4 2.4 %shard_map.66.refs_0_.refs_12_.refs_22_ = bf16[2,256,256]{2,1,0:T(8,128)(2,1)S(1)} custom-call(s32[2,8,8]{2,1,0:T(8,128)S(1)} %copy-done.1, s32[2,2,8]{2,1,0:T(2,128)S(1)} %copy-done.2, s32[2,2]{1,0:T(2,128)S(1)} %copy-done.3, bf16[3,2,256,512]{3,2,1,0:T(8,128)(2,1)S(1)} %copy-done, bf16[2304,256]{1,0:T(8,128)(2,1)S(1)} %get-tuple-element.30.refs_0_, ...), custom_call_target="tpu_custom_call" | custom-call | flops 603979776 | bytes 9175040 | tf_op jit(solution)/shard_map/pallas_call | solution.py:51
  64.8 1.2 %collective-permute-start.20 = (bf16[2,256,256]{2,1,0:T(8,128)(2,1)S(1)}, bf16[2,256,256]{2,1,0:T(8,128)(2,1)S(1)}, u32[]{:S(2)}, u32[]{:S(2)}) collective-permute-start(bf16[2,256,256]{2,1,0:T(8,128)(2,1)S(1)} %shard_map.66.refs_0_.refs_12_.refs_22_), channel_id=1, source_target_pairs={{0,16},{4,20},{8,24},{12,28},{16,0},{20,4},{24,8},{28,12},{1,17},{... | collective-permute-start | bytes 786440 | tf_op jit(solution)/shard_map/ppermute | solution.py:18
  66.0 2.5 %collective-permute-done.15.refs_2_.refs_14_ = bf16[1,256,256]{2,1,0:T(8,128)(2,1)S(1)} collective-permute-done((bf16[1,256,256]{2,1,0:T(8,128)(2,1)S(1)}, bf16[1,256,256]{2,1,0:T(8,128)(2,1)S(1)}, u32[]{:S(2)}, u32[]{:S(2)}) %collective-permute-start.15) | collective-permute-done | bytes 131104 | tf_op jit(solution)/shard_map/ppermute | solution.py:18
  68.5 4.1 %collective-permute-done.16.refs_3_.refs_15_ = bf16[1,256,256]{2,1,0:T(8,128)(2,1)S(1)} collective-permute-done((bf16[1,256,256]{2,1,0:T(8,128)(2,1)S(1)}, bf16[1,256,256]{2,1,0:T(8,128)(2,1)S(1)}, u32[]{:S(2)}, u32[]{:S(2)}) %collective-permute-start.16) | collective-permute-done | bytes 131104 | tf_op jit(solution)/shard_map/ppermute | solution.py:18
  72.6 4.8 %collective-permute-done.13.far.refs_16_ = bf16[2,256,256]{2,1,0:T(8,128)(2,1)S(1)} collective-permute-done((bf16[2,256,256]{2,1,0:T(8,128)(2,1)S(1)}, bf16[2,256,256]{2,1,0:T(8,128)(2,1)S(1)}, u32[]{:S(2)}, u32[]{:S(2)}) %collective-permute-start.13) | collective-permute-done | bytes 262176 | tf_op jit(solution)/shard_map/ppermute | solution.py:18
  78.2 3.4 %collective-permute-start.19 = (bf16[2,256,256]{2,1,0:T(8,128)(2,1)S(1)}, bf16[2,256,256]{2,1,0:T(8,128)(2,1)S(1)}, u32[]{:S(2)}, u32[]{:S(2)}) collective-permute-start(bf16[2,256,256]{2,1,0:T(8,128)(2,1)S(1)} %get-tuple-element.41), channel_id=1, source_target_pairs={{0,12},{4,8},{8,4},{12,0},{16,28},{20,24},{24,20},{28,16},{1,13},{... | collective-permute-start | bytes 786440 | tf_op jit(solution)/shard_map/ppermute | solution.py:18
  82.9 1.6 %collective-permute-start.21 = (bf16[1,256,256]{2,1,0:T(8,128)(2,1)S(1)}, bf16[1,256,256]{2,1,0:T(8,128)(2,1)S(1)}, u32[]{:S(2)}, u32[]{:S(2)}) collective-permute-start(bf16[1,256,256]{2,1,0:T(8,128)(2,1)S(1)} %get-tuple-element.42), channel_id=1, source_target_pairs={{0,4},{4,0},{8,12},{12,8},{16,20},{20,16},{24,28},{28,24},{1,5},{5... | collective-permute-start | bytes 393224 | tf_op jit(solution)/shard_map/ppermute | solution.py:18
  84.5 1.9 %collective-permute-start.23 = (bf16[1,256,256]{2,1,0:T(8,128)(2,1)S(1)}, bf16[1,256,256]{2,1,0:T(8,128)(2,1)S(1)}, u32[]{:S(2)}, u32[]{:S(2)}) collective-permute-start(bf16[1,256,256]{2,1,0:T(8,128)(2,1)S(1)} %get-tuple-element.44), channel_id=1, source_target_pairs={{0,12},{4,8},{8,4},{12,0},{16,28},{20,24},{24,20},{28,16},{1,13},{... | collective-permute-start | bytes 393224 | tf_op jit(solution)/shard_map/ppermute | solution.py:18
  86.4 1.4 %collective-permute-done.18.refs_18_.refs_14_ = bf16[2,256,256]{2,1,0:T(8,128)(2,1)S(1)} collective-permute-done((bf16[2,256,256]{2,1,0:T(8,128)(2,1)S(1)}, bf16[2,256,256]{2,1,0:T(8,128)(2,1)S(1)}, u32[]{:S(2)}, u32[]{:S(2)}) %collective-permute-start.18) | collective-permute-done | bytes 262176 | tf_op jit(solution)/shard_map/ppermute | solution.py:18
  87.8 6.7 %collective-permute-done.19.refs_19_.refs_15_ = bf16[2,256,256]{2,1,0:T(8,128)(2,1)S(1)} collective-permute-done((bf16[2,256,256]{2,1,0:T(8,128)(2,1)S(1)}, bf16[2,256,256]{2,1,0:T(8,128)(2,1)S(1)}, u32[]{:S(2)}, u32[]{:S(2)}) %collective-permute-start.19) | collective-permute-done | bytes 262176 | tf_op jit(solution)/shard_map/ppermute | solution.py:18
  94.5 2.5 %shard_map.70.refs_23_ = bf16[2,256,256]{2,1,0:T(8,128)(2,1)S(1)} custom-call(s32[2,8,8]{2,1,0:T(8,128)S(1)} %copy-done.1, s32[2,2,8]{2,1,0:T(2,128)S(1)} %copy-done.2, s32[2,2]{1,0:T(2,128)S(1)} %copy-done.3, bf16[3,2,256,512]{3,2,1,0:T(8,128)(2,1)S(1)} %copy-done, bf16[2304,256]{1,0:T(8,128)(2,1)S(1)} %get-tuple-element.30.refs_0_, ...), custom_call_target="tpu_custom_call" | custom-call | flops 603979776 | bytes 10878976 | tf_op jit(solution)/shard_map/pallas_call | solution.py:51
  97.0 1.8 %collective-permute-done.23.refs_19_ = bf16[1,256,256]{2,1,0:T(8,128)(2,1)S(1)} collective-permute-done((bf16[1,256,256]{2,1,0:T(8,128)(2,1)S(1)}, bf16[1,256,256]{2,1,0:T(8,128)(2,1)S(1)}, u32[]{:S(2)}, u32[]{:S(2)}) %collective-permute-start.23) | collective-permute-done | bytes 131104 | tf_op jit(solution)/shard_map/ppermute | solution.py:18
  98.7 3.2 %shard_map.71 = bf16[3,2,256,512]{3,2,1,0:T(8,128)(2,1)} custom-call(s32[2,8,8]{2,1,0:T(8,128)S(1)} %copy-done.1, s32[2,2,8]{2,1,0:T(2,128)S(1)} %copy-done.2, s32[2,2]{1,0:T(2,128)S(1)} %copy-done.3, bf16[3,2,256,512]{3,2,1,0:T(8,128)(2,1)S(1)} %copy-done, bf16[2304,256]{1,0:T(8,128)(2,1)S(1)} %get-tuple-element.30.refs_0_, ...), custom_call_target="tpu_custom_call" | custom-call | flops 603979776 | bytes 13500416 | tf_op jit(solution)/shard_map/pallas_call | solution.py:51
  (36 shorter events, 8.9 us)
Async XLA Ops:
  0.9 5.8 %collective-permute-start.1 = (bf16[128,256]{1,0:T(8,128)(2,1)S(1)}, bf16[128,256]{1,0:T(8,128)(2,1)S(1)}, u32[]{:S(2)}, u32[]{:S(2)}) collective-permute-start(bf16[128,256]{1,0:T(8,128)(2,1)S(1)} %bitcast.7), channel_id=1, source_target_pairs={{0,1},{1,0},{2,3},{3,2},{4,5},{5,4},{6,7},{7,6},{8,9},{9,8},{10,11... | collective-permute-start | bytes 196616 | tf_op jit(solution)/shard_map/ppermute | solution.py:18
  1.4 5.3 %collective-permute-start = (bf16[128,256]{1,0:T(8,128)(2,1)S(1)}, bf16[128,256]{1,0:T(8,128)(2,1)S(1)}, u32[]{:S(2)}, u32[]{:S(2)}) collective-permute-start(bf16[128,256]{1,0:T(8,128)(2,1)S(1)} %bitcast.8), channel_id=1, source_target_pairs={{0,2},{1,3},{2,0},{3,1},{4,6},{5,7},{6,4},{7,5},{8,10},{9,11},{10,... | collective-permute-start | bytes 196616 | tf_op jit(solution)/shard_map/ppermute | solution.py:18
  5.3 1.4 %copy-start = (bf16[3,2,256,512]{3,2,1,0:T(8,128)(2,1)S(1)}, bf16[3,2,256,512]{3,2,1,0:T(8,128)(2,1)}, u32[]{:S(2)}) copy-start(bf16[3,2,256,512]{3,2,1,0:T(8,128)(2,1)} %noise.7) | copy-start | bytes 4718596
  5.3 2.7 %copy-start.1 = (s32[2,8,8]{2,1,0:T(8,128)S(1)}, s32[2,8,8]{2,1,0:T(8,128)}, u32[]{:S(2)}) copy-start(s32[2,8,8]{2,1,0:T(8,128)} %picks.15) | copy-start | bytes 1540
  6.7 1.3 %collective-permute-start.2 = (bf16[128,256]{1,0:T(8,128)(2,1)S(1)}, bf16[128,256]{1,0:T(8,128)(2,1)S(1)}, u32[]{:S(2)}, u32[]{:S(2)}) collective-permute-start(bf16[128,256]{1,0:T(8,128)(2,1)S(1)} %collective-permute-done.refs_1_), channel_id=1, source_target_pairs={{0,1},{1,0},{2,3},{3,2},{4,5},{5,4},{6,7},{7,6},{8,9},{9,8},{10,11... | collective-permute-start | bytes 196616 | tf_op jit(solution)/shard_map/ppermute | solution.py:18
  9.0 29.1 %collective-permute-start.7 = (bf16[2304,256]{1,0:T(8,128)(2,1)S(1)}, bf16[2304,256]{1,0:T(8,128)(2,1)S(1)}, u32[]{:S(2)}, u32[]{:S(2)}) collective-permute-start(bf16[2304,256]{1,0:T(8,128)(2,1)S(1)} %get-tuple-element.29.refs_3_), channel_id=1, source_target_pairs={{0,2},{1,3},{2,0},{3,1},{4,6},{5,7},{6,4},{7,5},{8,10},{9,11},{10,... | collective-permute-start | bytes 3538952 | tf_op jit(solution)/shard_map/ppermute | solution.py:18
  10.8 27.3 %collective-permute-start.3 = (bf16[2,256,512]{2,1,0:T(8,128)(2,1)S(1)}, bf16[2,256,512]{2,1,0:T(8,128)(2,1)S(1)}, u32[]{:S(2)}, u32[]{:S(2)}) collective-permute-start(bf16[2,256,512]{2,1,0:T(8,128)(2,1)S(1)} %get-tuple-element.25.refs_4_.refs_20_), channel_id=1, source_target_pairs={{0,16},{4,20},{8,24},{12,28},{16,0},{20,4},{24,8},{28,12},{1,17},{... | collective-permute-start | bytes 1572872 | tf_op jit(solution)/shard_map/ppermute | solution.py:18
  13.4 8.3 %collective-permute-start.4 = (bf16[1,256,512]{2,1,0:T(8,128)(2,1)S(1)}, bf16[1,256,512]{2,1,0:T(8,128)(2,1)S(1)}, u32[]{:S(2)}, u32[]{:S(2)}) collective-permute-start(bf16[1,256,512]{2,1,0:T(8,128)(2,1)S(1)} %get-tuple-element.26), channel_id=1, source_target_pairs={{0,4},{4,0},{8,12},{12,8},{16,20},{20,16},{24,28},{28,24},{1,5},{5... | collective-permute-start | bytes 786440 | tf_op jit(solution)/shard_map/ppermute | solution.py:18
  15.0 16.5 %collective-permute-start.5 = (bf16[1,256,512]{2,1,0:T(8,128)(2,1)S(1)}, bf16[1,256,512]{2,1,0:T(8,128)(2,1)S(1)}, u32[]{:S(2)}, u32[]{:S(2)}) collective-permute-start(bf16[1,256,512]{2,1,0:T(8,128)(2,1)S(1)} %get-tuple-element.27), channel_id=1, source_target_pairs={{0,8},{4,12},{8,0},{12,4},{16,24},{20,28},{24,16},{28,20},{1,9},{5... | collective-permute-start | bytes 786440 | tf_op jit(solution)/shard_map/ppermute | solution.py:18
  16.5 38.1 %copy-start.2 = (s32[2,2,8]{2,1,0:T(2,128)S(1)}, s32[2,2,8]{2,1,0:T(2,128)}, u32[]{:S(2)}) copy-start(s32[2,2,8]{2,1,0:T(2,128)} %lists.7) | copy-start | bytes 388
  16.5 38.1 %copy-start.3 = (s32[2,2]{1,0:T(2,128)S(1)}, s32[2,2]{1,0:T(2,128)}, u32[]{:S(2)}) copy-start(s32[2,2]{1,0:T(2,128)} %counts.7) | copy-start | bytes 52
  16.5 21.6 %collective-permute-start.6 = (bf16[1,256,512]{2,1,0:T(8,128)(2,1)S(1)}, bf16[1,256,512]{2,1,0:T(8,128)(2,1)S(1)}, u32[]{:S(2)}, u32[]{:S(2)}) collective-permute-start(bf16[1,256,512]{2,1,0:T(8,128)(2,1)S(1)} %get-tuple-element.28), channel_id=1, source_target_pairs={{0,12},{4,8},{8,4},{12,0},{16,28},{20,24},{24,20},{28,16},{1,13},{... | collective-permute-start | bytes 786440 | tf_op jit(solution)/shard_map/ppermute | solution.py:18
  38.9 15.7 %collective-permute-start.8 = (bf16[2304,256]{1,0:T(8,128)(2,1)S(1)}, bf16[2304,256]{1,0:T(8,128)(2,1)S(1)}, u32[]{:S(2)}, u32[]{:S(2)}) collective-permute-start(bf16[2304,256]{1,0:T(8,128)(2,1)S(1)} %get-tuple-element.30.refs_0_), channel_id=1, source_target_pairs={{0,1},{1,0},{2,3},{3,2},{4,5},{5,4},{6,7},{7,6},{8,9},{9,8},{10,11... | collective-permute-start | bytes 3538952 | tf_op jit(solution)/shard_map/ppermute | solution.py:18
  39.0 15.6 %collective-permute-start.9 = (bf16[2304,256]{1,0:T(8,128)(2,1)S(1)}, bf16[2304,256]{1,0:T(8,128)(2,1)S(1)}, u32[]{:S(2)}, u32[]{:S(2)}) collective-permute-start(bf16[2304,256]{1,0:T(8,128)(2,1)S(1)} %get-tuple-element.31.refs_1_), channel_id=1, source_target_pairs={{0,1},{1,0},{2,3},{3,2},{4,5},{5,4},{6,7},{7,6},{8,9},{9,8},{10,11... | collective-permute-start | bytes 3538952 | tf_op jit(solution)/shard_map/ppermute | solution.py:18
  39.5 8.3 %collective-permute-start.10 = (bf16[1,256,512]{2,1,0:T(8,128)(2,1)S(1)}, bf16[1,256,512]{2,1,0:T(8,128)(2,1)S(1)}, u32[]{:S(2)}, u32[]{:S(2)}) collective-permute-start(bf16[1,256,512]{2,1,0:T(8,128)(2,1)S(1)} %get-tuple-element.32), channel_id=1, source_target_pairs={{0,4},{4,0},{8,12},{12,8},{16,20},{20,16},{24,28},{28,24},{1,5},{5... | collective-permute-start | bytes 786440 | tf_op jit(solution)/shard_map/ppermute | solution.py:18
  41.0 9.2 %collective-permute-start.11 = (bf16[1,256,512]{2,1,0:T(8,128)(2,1)S(1)}, bf16[1,256,512]{2,1,0:T(8,128)(2,1)S(1)}, u32[]{:S(2)}, u32[]{:S(2)}) collective-permute-start(bf16[1,256,512]{2,1,0:T(8,128)(2,1)S(1)} %get-tuple-element.33), channel_id=1, source_target_pairs={{0,8},{4,12},{8,0},{12,4},{16,24},{20,28},{24,16},{28,20},{1,9},{5... | collective-permute-start | bytes 786440 | tf_op jit(solution)/shard_map/ppermute | solution.py:18
  41.8 12.8 %collective-permute-start.12 = (bf16[1,256,512]{2,1,0:T(8,128)(2,1)S(1)}, bf16[1,256,512]{2,1,0:T(8,128)(2,1)S(1)}, u32[]{:S(2)}, u32[]{:S(2)}) collective-permute-start(bf16[1,256,512]{2,1,0:T(8,128)(2,1)S(1)} %get-tuple-element.34), channel_id=1, source_target_pairs={{0,12},{4,8},{8,4},{12,0},{16,28},{20,24},{24,20},{28,16},{1,13},{... | collective-permute-start | bytes 786440 | tf_op jit(solution)/shard_map/ppermute | solution.py:18
  57.0 20.3 %collective-permute-start.13 = (bf16[2,256,256]{2,1,0:T(8,128)(2,1)S(1)}, bf16[2,256,256]{2,1,0:T(8,128)(2,1)S(1)}, u32[]{:S(2)}, u32[]{:S(2)}) collective-permute-start(bf16[2,256,256]{2,1,0:T(8,128)(2,1)S(1)} %get-tuple-element.35.refs_12_.refs_21_), channel_id=1, source_target_pairs={{0,16},{4,20},{8,24},{12,28},{16,0},{20,4},{24,8},{28,12},{1,17},{... | collective-permute-start | bytes 786440 | tf_op jit(solution)/shard_map/ppermute | solution.py:18
  58.9 7.1 %collective-permute-start.14 = (bf16[1,256,256]{2,1,0:T(8,128)(2,1)S(1)}, bf16[1,256,256]{2,1,0:T(8,128)(2,1)S(1)}, u32[]{:S(2)}, u32[]{:S(2)}) collective-permute-start(bf16[1,256,256]{2,1,0:T(8,128)(2,1)S(1)} %get-tuple-element.36), channel_id=1, source_target_pairs={{0,4},{4,0},{8,12},{12,8},{16,20},{20,16},{24,28},{28,24},{1,5},{5... | collective-permute-start | bytes 393224 | tf_op jit(solution)/shard_map/ppermute | solution.py:18
  60.4 8.1 %collective-permute-start.15 = (bf16[1,256,256]{2,1,0:T(8,128)(2,1)S(1)}, bf16[1,256,256]{2,1,0:T(8,128)(2,1)S(1)}, u32[]{:S(2)}, u32[]{:S(2)}) collective-permute-start(bf16[1,256,256]{2,1,0:T(8,128)(2,1)S(1)} %get-tuple-element.37), channel_id=1, source_target_pairs={{0,8},{4,12},{8,0},{12,4},{16,24},{20,28},{24,16},{28,20},{1,9},{5... | collective-permute-start | bytes 393224 | tf_op jit(solution)/shard_map/ppermute | solution.py:18
  62.0 10.6 %collective-permute-start.16 = (bf16[1,256,256]{2,1,0:T(8,128)(2,1)S(1)}, bf16[1,256,256]{2,1,0:T(8,128)(2,1)S(1)}, u32[]{:S(2)}, u32[]{:S(2)}) collective-permute-start(bf16[1,256,256]{2,1,0:T(8,128)(2,1)S(1)} %get-tuple-element.38), channel_id=1, source_target_pairs={{0,12},{4,8},{8,4},{12,0},{16,28},{20,24},{24,20},{28,16},{1,13},{... | collective-permute-start | bytes 393224 | tf_op jit(solution)/shard_map/ppermute | solution.py:18
  64.8 17.3 %collective-permute-start.20 = (bf16[2,256,256]{2,1,0:T(8,128)(2,1)S(1)}, bf16[2,256,256]{2,1,0:T(8,128)(2,1)S(1)}, u32[]{:S(2)}, u32[]{:S(2)}) collective-permute-start(bf16[2,256,256]{2,1,0:T(8,128)(2,1)S(1)} %shard_map.66.refs_0_.refs_12_.refs_22_), channel_id=1, source_target_pairs={{0,16},{4,20},{8,24},{12,28},{16,0},{20,4},{24,8},{28,12},{1,17},{... | collective-permute-start | bytes 786440 | tf_op jit(solution)/shard_map/ppermute | solution.py:18
  78.1 6.4 %collective-permute-start.17 = (bf16[2,256,256]{2,1,0:T(8,128)(2,1)S(1)}, bf16[2,256,256]{2,1,0:T(8,128)(2,1)S(1)}, u32[]{:S(2)}, u32[]{:S(2)}) collective-permute-start(bf16[2,256,256]{2,1,0:T(8,128)(2,1)S(1)} %get-tuple-element.39), channel_id=1, source_target_pairs={{0,4},{4,0},{8,12},{12,8},{16,20},{20,16},{24,28},{28,24},{1,5},{5... | collective-permute-start | bytes 786440 | tf_op jit(solution)/shard_map/ppermute | solution.py:18
  78.1 9.7 %collective-permute-start.18 = (bf16[2,256,256]{2,1,0:T(8,128)(2,1)S(1)}, bf16[2,256,256]{2,1,0:T(8,128)(2,1)S(1)}, u32[]{:S(2)}, u32[]{:S(2)}) collective-permute-start(bf16[2,256,256]{2,1,0:T(8,128)(2,1)S(1)} %get-tuple-element.40), channel_id=1, source_target_pairs={{0,8},{4,12},{8,0},{12,4},{16,24},{20,28},{24,16},{28,20},{1,9},{5... | collective-permute-start | bytes 786440 | tf_op jit(solution)/shard_map/ppermute | solution.py:18
  78.2 16.3 %collective-permute-start.19 = (bf16[2,256,256]{2,1,0:T(8,128)(2,1)S(1)}, bf16[2,256,256]{2,1,0:T(8,128)(2,1)S(1)}, u32[]{:S(2)}, u32[]{:S(2)}) collective-permute-start(bf16[2,256,256]{2,1,0:T(8,128)(2,1)S(1)} %get-tuple-element.41), channel_id=1, source_target_pairs={{0,12},{4,8},{8,4},{12,0},{16,28},{20,24},{24,20},{28,16},{1,13},{... | collective-permute-start | bytes 786440 | tf_op jit(solution)/shard_map/ppermute | solution.py:18
  82.9 14.1 %collective-permute-start.21 = (bf16[1,256,256]{2,1,0:T(8,128)(2,1)S(1)}, bf16[1,256,256]{2,1,0:T(8,128)(2,1)S(1)}, u32[]{:S(2)}, u32[]{:S(2)}) collective-permute-start(bf16[1,256,256]{2,1,0:T(8,128)(2,1)S(1)} %get-tuple-element.42), channel_id=1, source_target_pairs={{0,4},{4,0},{8,12},{12,8},{16,20},{20,16},{24,28},{28,24},{1,5},{5... | collective-permute-start | bytes 393224 | tf_op jit(solution)/shard_map/ppermute | solution.py:18
  84.4 12.5 %collective-permute-start.22 = (bf16[1,256,256]{2,1,0:T(8,128)(2,1)S(1)}, bf16[1,256,256]{2,1,0:T(8,128)(2,1)S(1)}, u32[]{:S(2)}, u32[]{:S(2)}) collective-permute-start(bf16[1,256,256]{2,1,0:T(8,128)(2,1)S(1)} %get-tuple-element.43), channel_id=1, source_target_pairs={{0,8},{4,12},{8,0},{12,4},{16,24},{20,28},{24,16},{28,20},{1,9},{5... | collective-permute-start | bytes 393224 | tf_op jit(solution)/shard_map/ppermute | solution.py:18
  84.5 14.2 %collective-permute-start.23 = (bf16[1,256,256]{2,1,0:T(8,128)(2,1)S(1)}, bf16[1,256,256]{2,1,0:T(8,128)(2,1)S(1)}, u32[]{:S(2)}, u32[]{:S(2)}) collective-permute-start(bf16[1,256,256]{2,1,0:T(8,128)(2,1)S(1)} %get-tuple-element.44), channel_id=1, source_target_pairs={{0,12},{4,8},{8,4},{12,0},{16,28},{20,24},{24,20},{28,16},{1,13},{... | collective-permute-start | bytes 393224 | tf_op jit(solution)/shard_map/ppermute | solution.py:18

commit v14 on v13

--- a/solution.py
+++ b/solution.py
@@ -89,23 +89,22 @@
         send[0] = solved[picks[0, myself ^ step, myself]]
 
 
-def relay_kernel(half, source, follow, waits, through, picks, far, *refs):
-    own, refs = take(refs, follow)
+def relay_kernel(half, source, waits, through, picks, far, *refs):
     sends = refs[waits + through:][:half - 1]
     myself = lax.axis_index("leaf")
     for step, send in enumerate(sends, 1):
         send[0] = far[picks[source, myself ^ step, myself ^ half]]
-        if follow:
-            send[1] = own[0][picks[source, myself ^ step, myself]]
 
 
 def level_kernel(
-    level, owners, held, width, chunk, places, stored, sides, picks, lists, counts, noise, *refs
+    level, owners, held, width, chunk, places, stored, sides, mates,
+    picks, lists, counts, noise, *refs,
 ):
     half = owners // 2
     packs, refs = take(refs, len(held))
     known, refs = take(refs, level * owners)
     done, refs = take(refs, len(stored))
+    chunks, refs = take(refs, mates)
     target, *refs = refs
     sends, (table, inv, *refs) = take(refs, sides)
     myself, draw = lax.axis_index("leaf"), lax.axis_index("draw")
@@ -146,7 +145,9 @@
         right_side = (noise[level, node, :, columns].astype(F32) - total).astype(BF16)
         solved[node] = transposed_dot(inv[node], right_side).astype(BF16)
     for step, send in enumerate(sends, 1):
-        send[0] = solved[picks[level, myself ^ step, myself]]
+        node = picks[level, myself ^ step, myself]
+        for at, ref in enumerate([*chunks, solved]):
+            send[at] = ref[node]
     if done:
         here = target.at[level, :, :, pl.ds(chunk * wide, wide)]
         copies.append(pltpu.make_async_copy(solved, here, sems.at[len(done)]))
@@ -183,7 +184,7 @@
     far, got = leaf(solved, half), near(sends)
     values, steps = far_rows(raw, "draw", draws)
     sends = call(
-        functools.partial(relay_kernel, half, 0, 0, len(got), len(values)),
+        functools.partial(relay_kernel, half, 0, len(got), len(values)),
         [shape(1, rows, columns)] * (half - 1) + [shape(*value.shape) for value in values],
         [],
         (picks,),
@@ -199,7 +200,8 @@
         last_level = level == levels - 1
         solved, sends = [], []
         for at in chunks:
-            sides = half - 1 if at == 0 and not last_level else 0
+            ends = at == CHUNKS - 1 and not last_level
+            sides, mates = (half - 1, list(solved)) if ends else (0, [])
             final = last_level and at == CHUNKS - 1
             known = [entry for below in range(level) for entry in pieces[below][at]]
             stored = done if final else []
@@ -212,12 +214,12 @@
             here, *sent = call(
                 functools.partial(
                     level_kernel, level, owners, steps, width, at,
-                    [place for _, place in known], [place for _, place in stored], sides,
+                    [place for _, place in known], [place for _, place in stored], sides, len(mates),
                 ),
-                [shape(*noise.shape) if final else part] + [shape(1, rows, wide)] * sides,
+                [shape(*noise.shape) if final else part] + [shape(CHUNKS, rows, wide)] * sides,
                 scratch,
                 (picks, lists, counts),
-                (noise, *packs, *(ref for ref, _ in known), *(ref for ref, _ in stored)),
+                (noise, *packs, *(ref for ref, _ in known), *(ref for ref, _ in stored), *mates),
                 out_spec=ANY if final else VMEM,
                 flops=nodes * (draws * width + 1) * dot_flops,
             )
@@ -228,22 +230,20 @@
             return here
         far = [leaf(value, half) for value in solved]
         got = near(sends)
-        close, distant, waits = [[(ref, 0) for ref in got]], [], got
+        pieces.append([])
         for at in chunks:
-            follow = solved[at + 1:at + 2]
+            waits = got if at == CHUNKS - 1 else []
             sends = call(
-                functools.partial(relay_kernel, half, level, len(follow), len(waits), 0),
-                [shape(1 + len(follow), rows, wide)] * (half - 1),
+                functools.partial(relay_kernel, half, level, len(waits), 0),
+                [shape(1, rows, wide)] * (half - 1),
                 [],
                 (picks,),
-                (far[at], *follow, *waits),
+                (far[at], *waits),
             )
-            got, waits = near(sends), []
-            distant.append([(ref, 0) for ref in got])
-            close.append([(ref, 1) for ref in got])
-        pieces.append([
-            [(solved[at], 0), *close[at], (far[at], 0), *distant[at]] for at in chunks
-        ])
+            pieces[level].append([
+                (solved[at], 0), *((ref, at) for ref in got),
+                (far[at], 0), *((ref, 0) for ref in near(sends)),
+            ])
 
 
 def solution(mesh):

time: 102 us -> 101 us (level)
  starting transfers between devices: 28.6 us -> 26.2 us
    ppermute x24, starting transfers between devices: 28.6 us -> 26.2 us  [hop(): return lax.ppermute(value, axis, [(at, at ^ step) for at in range(size)])]
  transfers between devices with their start and end apart: 24 -> 24, of which waited for: 16 -> 13; matrix products, arithmetic and copies ran while one was open for 1% -> 1% of each run, Pallas kernels for 6% -> 6%
where the time goes in v14:
time: 101 us; the launch traced here: 100 us
  waiting for transfers between devices  58 us (57%)
  starting transfers between devices  26.2 us (26%)
  Pallas kernels  13.7 us (14%)
  local copies, waits for them, and re-layouts  2.24 us (2%)
    ppermute x24, waiting for transfers between devices, hop(): return lax.ppermute(value, axis, [(at, at ^ step) for at in range(size)])  58 us
    ppermute x24, starting transfers between devices, hop(): return lax.ppermute(value, axis, [(at, at ^ step) for at in range(size)])  26.2 us
    pallas_call x8, Pallas kernels, call(): pl.pallas_call(kernel, out_shape=outs, in_specs=[SMEM] * len(small) + [VM...  13.7 us
  transfers between devices with their start and end apart: 24, of which 13 were waited for; matrix products, arithmetic and copies ran while one was open for 1% of the time, Pallas kernels for 6%

profile of v14, /device:TPU:0, one launch (start us, length us, event | category | flops | bytes accessed | tf_op | source)
XLA Modules:
  0.0 100.4 jit_solution(5509795780452882447)
XLA Ops:
  1.4 2.6 %collective-permute-start = (bf16[128,256]{1,0:T(8,128)(2,1)S(1)}, bf16[128,256]{1,0:T(8,128)(2,1)S(1)}, u32[]{:S(2)}, u32[]{:S(2)}) collective-permute-start(bf16[128,256]{1,0:T(8,128)(2,1)S(1)} %bitcast.8), channel_id=1, source_target_pairs={{0,2},{1,3},{2,0},{3,1},{4,6},{5,7},{6,4},{7,5},{8,10},{9,11},{10,... | collective-permute-start | bytes 196616 | tf_op jit(solution)/shard_map/ppermute | solution.py:18
  4.0 1.3 %fusion = (bf16[1,2,2,256,256]{4,3,2,1,0:T(8,128)(2,1)S(1)}, bf16[1,2,2,256,256]{4,3,2,1,0:T(8,128)(2,1)S(1)}) fusion(bf16[2,2,2,256,256]{4,3,2,1,0:T(8,128)(2,1)} %param.8), kind=kLoop, calls=%fused_computation.2 | loop fusion | bytes 2097152 | tf_op jit(solution)/shard_map/slice | solution.py:171
  5.4 1.3 %collective-permute-done.refs_1_ = bf16[128,256]{1,0:T(8,128)(2,1)S(1)} collective-permute-done((bf16[128,256]{1,0:T(8,128)(2,1)S(1)}, bf16[128,256]{1,0:T(8,128)(2,1)S(1)}, u32[]{:S(2)}, u32[]{:S(2)}) %collective-permute-start) | collective-permute-done | bytes 65568 | tf_op jit(solution)/shard_map/ppermute | solution.py:18
  6.7 1.2 %collective-permute-done.2.refs_3_ = bf16[128,256]{1,0:T(8,128)(2,1)S(1)} collective-permute-done((bf16[128,256]{1,0:T(8,128)(2,1)S(1)}, bf16[128,256]{1,0:T(8,128)(2,1)S(1)}, u32[]{:S(2)}, u32[]{:S(2)}) %collective-permute-start.2) | collective-permute-done | bytes 65568 | tf_op jit(solution)/shard_map/ppermute | solution.py:18
  9.0 1.8 %collective-permute-start.7 = (bf16[2304,256]{1,0:T(8,128)(2,1)S(1)}, bf16[2304,256]{1,0:T(8,128)(2,1)S(1)}, u32[]{:S(2)}, u32[]{:S(2)}) collective-permute-start(bf16[2304,256]{1,0:T(8,128)(2,1)S(1)} %get-tuple-element.29.refs_3_), channel_id=1, source_target_pairs={{0,2},{1,3},{2,0},{3,1},{4,6},{5,7},{6,4},{7,5},{8,10},{9,11},{10,... | collective-permute-start | bytes 3538952 | tf_op jit(solution)/shard_map/ppermute | solution.py:18
  10.8 2.6 %collective-permute-start.3 = (bf16[2,256,512]{2,1,0:T(8,128)(2,1)S(1)}, bf16[2,256,512]{2,1,0:T(8,128)(2,1)S(1)}, u32[]{:S(2)}, u32[]{:S(2)}) collective-permute-start(bf16[2,256,512]{2,1,0:T(8,128)(2,1)S(1)} %get-tuple-element.25.refs_4_.refs_20_), channel_id=1, source_target_pairs={{0,16},{4,20},{8,24},{12,28},{16,0},{20,4},{24,8},{28,12},{1,17},{... | collective-permute-start | bytes 1572872 | tf_op jit(solution)/shard_map/ppermute | solution.py:18
  13.4 1.5 %collective-permute-start.4 = (bf16[1,256,512]{2,1,0:T(8,128)(2,1)S(1)}, bf16[1,256,512]{2,1,0:T(8,128)(2,1)S(1)}, u32[]{:S(2)}, u32[]{:S(2)}) collective-permute-start(bf16[1,256,512]{2,1,0:T(8,128)(2,1)S(1)} %get-tuple-element.26), channel_id=1, source_target_pairs={{0,4},{4,0},{8,12},{12,8},{16,20},{20,16},{24,28},{28,24},{1,5},{5... | collective-permute-start | bytes 786440 | tf_op jit(solution)/shard_map/ppermute | solution.py:18
  15.0 1.6 %collective-permute-start.5 = (bf16[1,256,512]{2,1,0:T(8,128)(2,1)S(1)}, bf16[1,256,512]{2,1,0:T(8,128)(2,1)S(1)}, u32[]{:S(2)}, u32[]{:S(2)}) collective-permute-start(bf16[1,256,512]{2,1,0:T(8,128)(2,1)S(1)} %get-tuple-element.27), channel_id=1, source_target_pairs={{0,8},{4,12},{8,0},{12,4},{16,24},{20,28},{24,16},{28,20},{1,9},{5... | collective-permute-start | bytes 786440 | tf_op jit(solution)/shard_map/ppermute | solution.py:18
  16.9 4.8 %collective-permute-done.4.refs_0_.refs_5_ = bf16[1,256,512]{2,1,0:T(8,128)(2,1)S(1)} collective-permute-done((bf16[1,256,512]{2,1,0:T(8,128)(2,1)S(1)}, bf16[1,256,512]{2,1,0:T(8,128)(2,1)S(1)}, u32[]{:S(2)}, u32[]{:S(2)}) %collective-permute-start.4) | collective-permute-done | bytes 262176 | tf_op jit(solution)/shard_map/ppermute | solution.py:18
  21.8 9.6 %collective-permute-done.5.refs_1_.refs_6_ = bf16[1,256,512]{2,1,0:T(8,128)(2,1)S(1)} collective-permute-done((bf16[1,256,512]{2,1,0:T(8,128)(2,1)S(1)}, bf16[1,256,512]{2,1,0:T(8,128)(2,1)S(1)}, u32[]{:S(2)}, u32[]{:S(2)}) %collective-permute-start.5) | collective-permute-done | bytes 262176 | tf_op jit(solution)/shard_map/ppermute | solution.py:18
  31.4 6.7 %collective-permute-done.6.refs_2_.refs_7_ = bf16[1,256,512]{2,1,0:T(8,128)(2,1)S(1)} collective-permute-done((bf16[1,256,512]{2,1,0:T(8,128)(2,1)S(1)}, bf16[1,256,512]{2,1,0:T(8,128)(2,1)S(1)}, u32[]{:S(2)}, u32[]{:S(2)}) %collective-permute-start.6) | collective-permute-done | bytes 262176 | tf_op jit(solution)/shard_map/ppermute | solution.py:18
  39.5 1.5 %collective-permute-start.10 = (bf16[1,256,512]{2,1,0:T(8,128)(2,1)S(1)}, bf16[1,256,512]{2,1,0:T(8,128)(2,1)S(1)}, u32[]{:S(2)}, u32[]{:S(2)}) collective-permute-start(bf16[1,256,512]{2,1,0:T(8,128)(2,1)S(1)} %get-tuple-element.32), channel_id=1, source_target_pairs={{0,4},{4,0},{8,12},{12,8},{16,20},{20,16},{24,28},{28,24},{1,5},{5... | collective-permute-start | bytes 786440 | tf_op jit(solution)/shard_map/ppermute | solution.py:18
  41.8 1.2 %collective-permute-start.12 = (bf16[1,256,512]{2,1,0:T(8,128)(2,1)S(1)}, bf16[1,256,512]{2,1,0:T(8,128)(2,1)S(1)}, u32[]{:S(2)}, u32[]{:S(2)}) collective-permute-start(bf16[1,256,512]{2,1,0:T(8,128)(2,1)S(1)} %get-tuple-element.34), channel_id=1, source_target_pairs={{0,12},{4,8},{8,4},{12,0},{16,28},{20,24},{24,20},{28,16},{1,13},{... | collective-permute-start | bytes 786440 | tf_op jit(solution)/shard_map/ppermute | solution.py:18
  43.0 4.8 %collective-permute-done.10.refs_9_ = bf16[1,256,512]{2,1,0:T(8,128)(2,1)S(1)} collective-permute-done((bf16[1,256,512]{2,1,0:T(8,128)(2,1)S(1)}, bf16[1,256,512]{2,1,0:T(8,128)(2,1)S(1)}, u32[]{:S(2)}, u32[]{:S(2)}) %collective-permute-start.10) | collective-permute-done | bytes 262176 | tf_op jit(solution)/shard_map/ppermute | solution.py:18
  47.8 2.4 %collective-permute-done.11.refs_10_ = bf16[1,256,512]{2,1,0:T(8,128)(2,1)S(1)} collective-permute-done((bf16[1,256,512]{2,1,0:T(8,128)(2,1)S(1)}, bf16[1,256,512]{2,1,0:T(8,128)(2,1)S(1)}, u32[]{:S(2)}, u32[]{:S(2)}) %collective-permute-start.11) | collective-permute-done | bytes 262176 | tf_op jit(solution)/shard_map/ppermute | solution.py:18
  50.2 4.4 %collective-permute-done.12.refs_11_ = bf16[1,256,512]{2,1,0:T(8,128)(2,1)S(1)} collective-permute-done((bf16[1,256,512]{2,1,0:T(8,128)(2,1)S(1)}, bf16[1,256,512]{2,1,0:T(8,128)(2,1)S(1)}, u32[]{:S(2)}, u32[]{:S(2)}) %collective-permute-start.12) | collective-permute-done | bytes 262176 | tf_op jit(solution)/shard_map/ppermute | solution.py:18
  54.6 2.4 %shard_map.66.refs_12_.refs_21_ = bf16[2,256,256]{2,1,0:T(8,128)(2,1)S(1)} custom-call(s32[2,8,8]{2,1,0:T(8,128)S(1)} %copy-done.1, s32[2,2,8]{2,1,0:T(2,128)S(1)} %copy-done.2, s32[2,2]{1,0:T(2,128)S(1)} %copy-done.3, bf16[3,2,256,512]{3,2,1,0:T(8,128)(2,1)S(1)} %copy-done, bf16[2304,256]{1,0:T(8,128)(2,1)S(1)} %get-tuple-element.30.refs_0_, ...), custom_call_target="tpu_custom_call" | custom-call | flops 603979776 | bytes 9175040 | tf_op jit(solution)/shard_map/pallas_call | solution.py:51
  57.0 1.9 %collective-permute-start.20 = (bf16[2,256,256]{2,1,0:T(8,128)(2,1)S(1)}, bf16[2,256,256]{2,1,0:T(8,128)(2,1)S(1)}, u32[]{:S(2)}, u32[]{:S(2)}) collective-permute-start(bf16[2,256,256]{2,1,0:T(8,128)(2,1)S(1)} %shard_map.66.refs_12_.refs_21_), channel_id=1, source_target_pairs={{0,16},{4,20},{8,24},{12,28},{16,0},{20,4},{24,8},{28,12},{1,17},{... | collective-permute-start | bytes 786440 | tf_op jit(solution)/shard_map/ppermute | solution.py:18
  58.9 2.4 %shard_map.67 = (bf16[2,256,256]{2,1,0:T(8,128)(2,1)S(1)}, bf16[2,256,256]{2,1,0:T(8,128)(2,1)S(1)}, bf16[2,256,256]{2,1,0:T(8,128)(2,1)S(1)}, bf16[2,256,256]{2,1,0:T(8,128)(2,1)S(1)}) custom-call(s32[2,8,8]{2,1,0:T(8,128)S(1)} %copy-done.1, s32[2,2,8]{2,1,0:T(2,128)S(1)} %copy-done.2, s32[2,2]{1,0:T(2,128)S(1)} %copy-done.3, ...), custom_call_target="tpu_custom_call" | custom-call | flops 603979776 | bytes 10223616 | tf_op jit(solution)/shard_map/pallas_call | solution.py:51
  61.3 1.6 %collective-permute-start.13 = (bf16[2,256,256]{2,1,0:T(8,128)(2,1)S(1)}, bf16[2,256,256]{2,1,0:T(8,128)(2,1)S(1)}, u32[]{:S(2)}, u32[]{:S(2)}) collective-permute-start(bf16[2,256,256]{2,1,0:T(8,128)(2,1)S(1)} %get-tuple-element.36), channel_id=1, source_target_pairs={{0,4},{4,0},{8,12},{12,8},{16,20},{20,16},{24,28},{28,24},{1,5},{5... | collective-permute-start | bytes 786440 | tf_op jit(solution)/shard_map/ppermute | solution.py:18
  62.9 1.6 %collective-permute-start.14 = (bf16[2,256,256]{2,1,0:T(8,128)(2,1)S(1)}, bf16[2,256,256]{2,1,0:T(8,128)(2,1)S(1)}, u32[]{:S(2)}, u32[]{:S(2)}) collective-permute-start(bf16[2,256,256]{2,1,0:T(8,128)(2,1)S(1)} %get-tuple-element.37), channel_id=1, source_target_pairs={{0,8},{4,12},{8,0},{12,4},{16,24},{20,28},{24,16},{28,20},{1,9},{5... | collective-permute-start | bytes 786440 | tf_op jit(solution)/shard_map/ppermute | solution.py:18
  64.9 1.1 %collective-permute-start.16 = (bf16[2,256,256]{2,1,0:T(8,128)(2,1)S(1)}, bf16[2,256,256]{2,1,0:T(8,128)(2,1)S(1)}, u32[]{:S(2)}, u32[]{:S(2)}) collective-permute-start(bf16[2,256,256]{2,1,0:T(8,128)(2,1)S(1)} %get-tuple-element.35.refs_12_.refs_22_), channel_id=1, source_target_pairs={{0,16},{4,20},{8,24},{12,28},{16,0},{20,4},{24,8},{28,12},{1,17},{... | collective-permute-start | bytes 786440 | tf_op jit(solution)/shard_map/ppermute | solution.py:18
  66.0 5.6 %collective-permute-done.20.far.refs_16_ = bf16[2,256,256]{2,1,0:T(8,128)(2,1)S(1)} collective-permute-done((bf16[2,256,256]{2,1,0:T(8,128)(2,1)S(1)}, bf16[2,256,256]{2,1,0:T(8,128)(2,1)S(1)}, u32[]{:S(2)}, u32[]{:S(2)}) %collective-permute-start.20) | collective-permute-done | bytes 262176 | tf_op jit(solution)/shard_map/ppermute | solution.py:18
  72.3 1.1 %collective-permute-start.21 = (bf16[1,256,256]{2,1,0:T(8,128)(2,1)S(1)}, bf16[1,256,256]{2,1,0:T(8,128)(2,1)S(1)}, u32[]{:S(2)}, u32[]{:S(2)}) collective-permute-start(bf16[1,256,256]{2,1,0:T(8,128)(2,1)S(1)} %get-tuple-element.42), channel_id=1, source_target_pairs={{0,4},{4,0},{8,12},{12,8},{16,20},{20,16},{24,28},{28,24},{1,5},{5... | collective-permute-start | bytes 393224 | tf_op jit(solution)/shard_map/ppermute | solution.py:18
  73.4 8.2 %collective-permute-done.14.refs_1_.refs_14_ = bf16[2,256,256]{2,1,0:T(8,128)(2,1)S(1)} collective-permute-done((bf16[2,256,256]{2,1,0:T(8,128)(2,1)S(1)}, bf16[2,256,256]{2,1,0:T(8,128)(2,1)S(1)}, u32[]{:S(2)}, u32[]{:S(2)}) %collective-permute-start.14) | collective-permute-done | bytes 262176 | tf_op jit(solution)/shard_map/ppermute | solution.py:18
  81.7 6.0 %collective-permute-done.15.refs_2_.refs_15_ = bf16[2,256,256]{2,1,0:T(8,128)(2,1)S(1)} collective-permute-done((bf16[2,256,256]{2,1,0:T(8,128)(2,1)S(1)}, bf16[2,256,256]{2,1,0:T(8,128)(2,1)S(1)}, u32[]{:S(2)}, u32[]{:S(2)}) %collective-permute-start.15) | collective-permute-done | bytes 262176 | tf_op jit(solution)/shard_map/ppermute | solution.py:18
  88.4 1.2 %collective-permute-start.17 = (bf16[1,256,256]{2,1,0:T(8,128)(2,1)S(1)}, bf16[1,256,256]{2,1,0:T(8,128)(2,1)S(1)}, u32[]{:S(2)}, u32[]{:S(2)}) collective-permute-start(bf16[1,256,256]{2,1,0:T(8,128)(2,1)S(1)} %get-tuple-element.39), channel_id=1, source_target_pairs={{0,4},{4,0},{8,12},{12,8},{16,20},{20,16},{24,28},{28,24},{1,5},{5... | collective-permute-start | bytes 393224 | tf_op jit(solution)/shard_map/ppermute | solution.py:18
  89.6 2.4 %collective-permute-start.19 = (bf16[1,256,256]{2,1,0:T(8,128)(2,1)S(1)}, bf16[1,256,256]{2,1,0:T(8,128)(2,1)S(1)}, u32[]{:S(2)}, u32[]{:S(2)}) collective-permute-start(bf16[1,256,256]{2,1,0:T(8,128)(2,1)S(1)} %get-tuple-element.41), channel_id=1, source_target_pairs={{0,12},{4,8},{8,4},{12,0},{16,28},{20,24},{24,20},{28,16},{1,13},{... | collective-permute-start | bytes 393224 | tf_op jit(solution)/shard_map/ppermute | solution.py:18
  92.0 1.4 %collective-permute-done.23.refs_19_ = bf16[1,256,256]{2,1,0:T(8,128)(2,1)S(1)} collective-permute-done((bf16[1,256,256]{2,1,0:T(8,128)(2,1)S(1)}, bf16[1,256,256]{2,1,0:T(8,128)(2,1)S(1)}, u32[]{:S(2)}, u32[]{:S(2)}) %collective-permute-start.23) | collective-permute-done | bytes 131104 | tf_op jit(solution)/shard_map/ppermute | solution.py:18
  93.4 2.5 %shard_map.70.refs_23_ = bf16[2,256,256]{2,1,0:T(8,128)(2,1)S(1)} custom-call(s32[2,8,8]{2,1,0:T(8,128)S(1)} %copy-done.1, s32[2,2,8]{2,1,0:T(2,128)S(1)} %copy-done.2, s32[2,2]{1,0:T(2,128)S(1)} %copy-done.3, bf16[3,2,256,512]{3,2,1,0:T(8,128)(2,1)S(1)} %copy-done, bf16[2304,256]{1,0:T(8,128)(2,1)S(1)} %get-tuple-element.30.refs_0_, ...), custom_call_target="tpu_custom_call" | custom-call | flops 603979776 | bytes 10878976 | tf_op jit(solution)/shard_map/pallas_call | solution.py:51
  95.9 1.3 %collective-permute-done.19.refs_19_ = bf16[1,256,256]{2,1,0:T(8,128)(2,1)S(1)} collective-permute-done((bf16[1,256,256]{2,1,0:T(8,128)(2,1)S(1)}, bf16[1,256,256]{2,1,0:T(8,128)(2,1)S(1)}, u32[]{:S(2)}, u32[]{:S(2)}) %collective-permute-start.19) | collective-permute-done | bytes 131104 | tf_op jit(solution)/shard_map/ppermute | solution.py:18
  97.2 3.2 %shard_map.71 = bf16[3,2,256,512]{3,2,1,0:T(8,128)(2,1)} custom-call(s32[2,8,8]{2,1,0:T(8,128)S(1)} %copy-done.1, s32[2,2,8]{2,1,0:T(2,128)S(1)} %copy-done.2, s32[2,2]{1,0:T(2,128)S(1)} %copy-done.3, bf16[3,2,256,512]{3,2,1,0:T(8,128)(2,1)S(1)} %copy-done, bf16[2304,256]{1,0:T(8,128)(2,1)S(1)} %get-tuple-element.30.refs_0_, ...), custom_call_target="tpu_custom_call" | custom-call | flops 603979776 | bytes 13500416 | tf_op jit(solution)/shard_map/pallas_call | solution.py:51
  (36 shorter events, 7.0 us)
Async XLA Ops:
  0.9 5.8 %collective-permute-start.1 = (bf16[128,256]{1,0:T(8,128)(2,1)S(1)}, bf16[128,256]{1,0:T(8,128)(2,1)S(1)}, u32[]{:S(2)}, u32[]{:S(2)}) collective-permute-start(bf16[128,256]{1,0:T(8,128)(2,1)S(1)} %bitcast.7), channel_id=1, source_target_pairs={{0,1},{1,0},{2,3},{3,2},{4,5},{5,4},{6,7},{7,6},{8,9},{9,8},{10,11... | collective-permute-start | bytes 196616 | tf_op jit(solution)/shard_map/ppermute | solution.py:18
  1.4 5.3 %collective-permute-start = (bf16[128,256]{1,0:T(8,128)(2,1)S(1)}, bf16[128,256]{1,0:T(8,128)(2,1)S(1)}, u32[]{:S(2)}, u32[]{:S(2)}) collective-permute-start(bf16[128,256]{1,0:T(8,128)(2,1)S(1)} %bitcast.8), channel_id=1, source_target_pairs={{0,2},{1,3},{2,0},{3,1},{4,6},{5,7},{6,4},{7,5},{8,10},{9,11},{10,... | collective-permute-start | bytes 196616 | tf_op jit(solution)/shard_map/ppermute | solution.py:18
  5.3 1.4 %copy-start = (bf16[3,2,256,512]{3,2,1,0:T(8,128)(2,1)S(1)}, bf16[3,2,256,512]{3,2,1,0:T(8,128)(2,1)}, u32[]{:S(2)}) copy-start(bf16[3,2,256,512]{3,2,1,0:T(8,128)(2,1)} %noise.7) | copy-start | bytes 4718596
  5.3 2.7 %copy-start.1 = (s32[2,8,8]{2,1,0:T(8,128)S(1)}, s32[2,8,8]{2,1,0:T(8,128)}, u32[]{:S(2)}) copy-start(s32[2,8,8]{2,1,0:T(8,128)} %picks.15) | copy-start | bytes 1540
  6.7 1.3 %collective-permute-start.2 = (bf16[128,256]{1,0:T(8,128)(2,1)S(1)}, bf16[128,256]{1,0:T(8,128)(2,1)S(1)}, u32[]{:S(2)}, u32[]{:S(2)}) collective-permute-start(bf16[128,256]{1,0:T(8,128)(2,1)S(1)} %collective-permute-done.refs_1_), channel_id=1, source_target_pairs={{0,1},{1,0},{2,3},{3,2},{4,5},{5,4},{6,7},{7,6},{8,9},{9,8},{10,11... | collective-permute-start | bytes 196616 | tf_op jit(solution)/shard_map/ppermute | solution.py:18
  9.0 29.1 %collective-permute-start.7 = (bf16[2304,256]{1,0:T(8,128)(2,1)S(1)}, bf16[2304,256]{1,0:T(8,128)(2,1)S(1)}, u32[]{:S(2)}, u32[]{:S(2)}) collective-permute-start(bf16[2304,256]{1,0:T(8,128)(2,1)S(1)} %get-tuple-element.29.refs_3_), channel_id=1, source_target_pairs={{0,2},{1,3},{2,0},{3,1},{4,6},{5,7},{6,4},{7,5},{8,10},{9,11},{10,... | collective-permute-start | bytes 3538952 | tf_op jit(solution)/shard_map/ppermute | solution.py:18
  10.8 27.3 %collective-permute-start.3 = (bf16[2,256,512]{2,1,0:T(8,128)(2,1)S(1)}, bf16[2,256,512]{2,1,0:T(8,128)(2,1)S(1)}, u32[]{:S(2)}, u32[]{:S(2)}) collective-permute-start(bf16[2,256,512]{2,1,0:T(8,128)(2,1)S(1)} %get-tuple-element.25.refs_4_.refs_20_), channel_id=1, source_target_pairs={{0,16},{4,20},{8,24},{12,28},{16,0},{20,4},{24,8},{28,12},{1,17},{... | collective-permute-start | bytes 1572872 | tf_op jit(solution)/shard_map/ppermute | solution.py:18
  13.4 8.3 %collective-permute-start.4 = (bf16[1,256,512]{2,1,0:T(8,128)(2,1)S(1)}, bf16[1,256,512]{2,1,0:T(8,128)(2,1)S(1)}, u32[]{:S(2)}, u32[]{:S(2)}) collective-permute-start(bf16[1,256,512]{2,1,0:T(8,128)(2,1)S(1)} %get-tuple-element.26), channel_id=1, source_target_pairs={{0,4},{4,0},{8,12},{12,8},{16,20},{20,16},{24,28},{28,24},{1,5},{5... | collective-permute-start | bytes 786440 | tf_op jit(solution)/shard_map/ppermute | solution.py:18
  15.0 16.5 %collective-permute-start.5 = (bf16[1,256,512]{2,1,0:T(8,128)(2,1)S(1)}, bf16[1,256,512]{2,1,0:T(8,128)(2,1)S(1)}, u32[]{:S(2)}, u32[]{:S(2)}) collective-permute-start(bf16[1,256,512]{2,1,0:T(8,128)(2,1)S(1)} %get-tuple-element.27), channel_id=1, source_target_pairs={{0,8},{4,12},{8,0},{12,4},{16,24},{20,28},{24,16},{28,20},{1,9},{5... | collective-permute-start | bytes 786440 | tf_op jit(solution)/shard_map/ppermute | solution.py:18
  16.5 38.1 %copy-start.2 = (s32[2,2,8]{2,1,0:T(2,128)S(1)}, s32[2,2,8]{2,1,0:T(2,128)}, u32[]{:S(2)}) copy-start(s32[2,2,8]{2,1,0:T(2,128)} %lists.7) | copy-start | bytes 388
  16.5 38.1 %copy-start.3 = (s32[2,2]{1,0:T(2,128)S(1)}, s32[2,2]{1,0:T(2,128)}, u32[]{:S(2)}) copy-start(s32[2,2]{1,0:T(2,128)} %counts.7) | copy-start | bytes 52
  16.5 21.6 %collective-permute-start.6 = (bf16[1,256,512]{2,1,0:T(8,128)(2,1)S(1)}, bf16[1,256,512]{2,1,0:T(8,128)(2,1)S(1)}, u32[]{:S(2)}, u32[]{:S(2)}) collective-permute-start(bf16[1,256,512]{2,1,0:T(8,128)(2,1)S(1)} %get-tuple-element.28), channel_id=1, source_target_pairs={{0,12},{4,8},{8,4},{12,0},{16,28},{20,24},{24,20},{28,16},{1,13},{... | collective-permute-start | bytes 786440 | tf_op jit(solution)/shard_map/ppermute | solution.py:18
  38.9 15.7 %collective-permute-start.8 = (bf16[2304,256]{1,0:T(8,128)(2,1)S(1)}, bf16[2304,256]{1,0:T(8,128)(2,1)S(1)}, u32[]{:S(2)}, u32[]{:S(2)}) collective-permute-start(bf16[2304,256]{1,0:T(8,128)(2,1)S(1)} %get-tuple-element.30.refs_0_), channel_id=1, source_target_pairs={{0,1},{1,0},{2,3},{3,2},{4,5},{5,4},{6,7},{7,6},{8,9},{9,8},{10,11... | collective-permute-start | bytes 3538952 | tf_op jit(solution)/shard_map/ppermute | solution.py:18
  39.0 15.6 %collective-permute-start.9 = (bf16[2304,256]{1,0:T(8,128)(2,1)S(1)}, bf16[2304,256]{1,0:T(8,128)(2,1)S(1)}, u32[]{:S(2)}, u32[]{:S(2)}) collective-permute-start(bf16[2304,256]{1,0:T(8,128)(2,1)S(1)} %get-tuple-element.31.refs_1_), channel_id=1, source_target_pairs={{0,1},{1,0},{2,3},{3,2},{4,5},{5,4},{6,7},{7,6},{8,9},{9,8},{10,11... | collective-permute-start | bytes 3538952 | tf_op jit(solution)/shard_map/ppermute | solution.py:18
  39.5 8.3 %collective-permute-start.10 = (bf16[1,256,512]{2,1,0:T(8,128)(2,1)S(1)}, bf16[1,256,512]{2,1,0:T(8,128)(2,1)S(1)}, u32[]{:S(2)}, u32[]{:S(2)}) collective-permute-start(bf16[1,256,512]{2,1,0:T(8,128)(2,1)S(1)} %get-tuple-element.32), channel_id=1, source_target_pairs={{0,4},{4,0},{8,12},{12,8},{16,20},{20,16},{24,28},{28,24},{1,5},{5... | collective-permute-start | bytes 786440 | tf_op jit(solution)/shard_map/ppermute | solution.py:18
  41.0 9.2 %collective-permute-start.11 = (bf16[1,256,512]{2,1,0:T(8,128)(2,1)S(1)}, bf16[1,256,512]{2,1,0:T(8,128)(2,1)S(1)}, u32[]{:S(2)}, u32[]{:S(2)}) collective-permute-start(bf16[1,256,512]{2,1,0:T(8,128)(2,1)S(1)} %get-tuple-element.33), channel_id=1, source_target_pairs={{0,8},{4,12},{8,0},{12,4},{16,24},{20,28},{24,16},{28,20},{1,9},{5... | collective-permute-start | bytes 786440 | tf_op jit(solution)/shard_map/ppermute | solution.py:18
  41.8 12.8 %collective-permute-start.12 = (bf16[1,256,512]{2,1,0:T(8,128)(2,1)S(1)}, bf16[1,256,512]{2,1,0:T(8,128)(2,1)S(1)}, u32[]{:S(2)}, u32[]{:S(2)}) collective-permute-start(bf16[1,256,512]{2,1,0:T(8,128)(2,1)S(1)} %get-tuple-element.34), channel_id=1, source_target_pairs={{0,12},{4,8},{8,4},{12,0},{16,28},{20,24},{24,20},{28,16},{1,13},{... | collective-permute-start | bytes 786440 | tf_op jit(solution)/shard_map/ppermute | solution.py:18
  57.0 14.6 %collective-permute-start.20 = (bf16[2,256,256]{2,1,0:T(8,128)(2,1)S(1)}, bf16[2,256,256]{2,1,0:T(8,128)(2,1)S(1)}, u32[]{:S(2)}, u32[]{:S(2)}) collective-permute-start(bf16[2,256,256]{2,1,0:T(8,128)(2,1)S(1)} %shard_map.66.refs_12_.refs_21_), channel_id=1, source_target_pairs={{0,16},{4,20},{8,24},{12,28},{16,0},{20,4},{24,8},{28,12},{1,17},{... | collective-permute-start | bytes 786440 | tf_op jit(solution)/shard_map/ppermute | solution.py:18
  61.3 12.1 %collective-permute-start.13 = (bf16[2,256,256]{2,1,0:T(8,128)(2,1)S(1)}, bf16[2,256,256]{2,1,0:T(8,128)(2,1)S(1)}, u32[]{:S(2)}, u32[]{:S(2)}) collective-permute-start(bf16[2,256,256]{2,1,0:T(8,128)(2,1)S(1)} %get-tuple-element.36), channel_id=1, source_target_pairs={{0,4},{4,0},{8,12},{12,8},{16,20},{20,16},{24,28},{28,24},{1,5},{5... | collective-permute-start | bytes 786440 | tf_op jit(solution)/shard_map/ppermute | solution.py:18
  62.9 18.8 %collective-permute-start.14 = (bf16[2,256,256]{2,1,0:T(8,128)(2,1)S(1)}, bf16[2,256,256]{2,1,0:T(8,128)(2,1)S(1)}, u32[]{:S(2)}, u32[]{:S(2)}) collective-permute-start(bf16[2,256,256]{2,1,0:T(8,128)(2,1)S(1)} %get-tuple-element.37), channel_id=1, source_target_pairs={{0,8},{4,12},{8,0},{12,4},{16,24},{20,28},{24,16},{28,20},{1,9},{5... | collective-permute-start | bytes 786440 | tf_op jit(solution)/shard_map/ppermute | solution.py:18
  64.5 23.2 %collective-permute-start.15 = (bf16[2,256,256]{2,1,0:T(8,128)(2,1)S(1)}, bf16[2,256,256]{2,1,0:T(8,128)(2,1)S(1)}, u32[]{:S(2)}, u32[]{:S(2)}) collective-permute-start(bf16[2,256,256]{2,1,0:T(8,128)(2,1)S(1)} %get-tuple-element.38), channel_id=1, source_target_pairs={{0,12},{4,8},{8,4},{12,0},{16,28},{20,24},{24,20},{28,16},{1,13},{... | collective-permute-start | bytes 786440 | tf_op jit(solution)/shard_map/ppermute | solution.py:18
  64.9 22.8 %collective-permute-start.16 = (bf16[2,256,256]{2,1,0:T(8,128)(2,1)S(1)}, bf16[2,256,256]{2,1,0:T(8,128)(2,1)S(1)}, u32[]{:S(2)}, u32[]{:S(2)}) collective-permute-start(bf16[2,256,256]{2,1,0:T(8,128)(2,1)S(1)} %get-tuple-element.35.refs_12_.refs_22_), channel_id=1, source_target_pairs={{0,16},{4,20},{8,24},{12,28},{16,0},{20,4},{24,8},{28,12},{1,17},{... | collective-permute-start | bytes 786440 | tf_op jit(solution)/shard_map/ppermute | solution.py:18
  72.3 17.2 %collective-permute-start.21 = (bf16[1,256,256]{2,1,0:T(8,128)(2,1)S(1)}, bf16[1,256,256]{2,1,0:T(8,128)(2,1)S(1)}, u32[]{:S(2)}, u32[]{:S(2)}) collective-permute-start(bf16[1,256,256]{2,1,0:T(8,128)(2,1)S(1)} %get-tuple-element.42), channel_id=1, source_target_pairs={{0,4},{4,0},{8,12},{12,8},{16,20},{20,16},{24,28},{28,24},{1,5},{5... | collective-permute-start | bytes 393224 | tf_op jit(solution)/shard_map/ppermute | solution.py:18
  73.4 18.5 %collective-permute-start.22 = (bf16[1,256,256]{2,1,0:T(8,128)(2,1)S(1)}, bf16[1,256,256]{2,1,0:T(8,128)(2,1)S(1)}, u32[]{:S(2)}, u32[]{:S(2)}) collective-permute-start(bf16[1,256,256]{2,1,0:T(8,128)(2,1)S(1)} %get-tuple-element.43), channel_id=1, source_target_pairs={{0,8},{4,12},{8,0},{12,4},{16,24},{20,28},{24,16},{28,20},{1,9},{5... | collective-permute-start | bytes 393224 | tf_op jit(solution)/shard_map/ppermute | solution.py:18
  81.7 11.7 %collective-permute-start.23 = (bf16[1,256,256]{2,1,0:T(8,128)(2,1)S(1)}, bf16[1,256,256]{2,1,0:T(8,128)(2,1)S(1)}, u32[]{:S(2)}, u32[]{:S(2)}) collective-permute-start(bf16[1,256,256]{2,1,0:T(8,128)(2,1)S(1)} %get-tuple-element.44), channel_id=1, source_target_pairs={{0,12},{4,8},{8,4},{12,0},{16,28},{20,24},{24,20},{28,16},{1,13},{... | collective-permute-start | bytes 393224 | tf_op jit(solution)/shard_map/ppermute | solution.py:18
  88.4 7.5 %collective-permute-start.17 = (bf16[1,256,256]{2,1,0:T(8,128)(2,1)S(1)}, bf16[1,256,256]{2,1,0:T(8,128)(2,1)S(1)}, u32[]{:S(2)}, u32[]{:S(2)}) collective-permute-start(bf16[1,256,256]{2,1,0:T(8,128)(2,1)S(1)} %get-tuple-element.39), channel_id=1, source_target_pairs={{0,4},{4,0},{8,12},{12,8},{16,20},{20,16},{24,28},{28,24},{1,5},{5... | collective-permute-start | bytes 393224 | tf_op jit(solution)/shard_map/ppermute | solution.py:18
  89.6 6.3 %collective-permute-start.18 = (bf16[1,256,256]{2,1,0:T(8,128)(2,1)S(1)}, bf16[1,256,256]{2,1,0:T(8,128)(2,1)S(1)}, u32[]{:S(2)}, u32[]{:S(2)}) collective-permute-start(bf16[1,256,256]{2,1,0:T(8,128)(2,1)S(1)} %get-tuple-element.40), channel_id=1, source_target_pairs={{0,8},{4,12},{8,0},{12,4},{16,24},{20,28},{24,16},{28,20},{1,9},{5... | collective-permute-start | bytes 393224 | tf_op jit(solution)/shard_map/ppermute | solution.py:18
  89.6 7.6 %collective-permute-start.19 = (bf16[1,256,256]{2,1,0:T(8,128)(2,1)S(1)}, bf16[1,256,256]{2,1,0:T(8,128)(2,1)S(1)}, u32[]{:S(2)}, u32[]{:S(2)}) collective-permute-start(bf16[1,256,256]{2,1,0:T(8,128)(2,1)S(1)} %get-tuple-element.41), channel_id=1, source_target_pairs={{0,12},{4,8},{8,4},{12,0},{16,28},{20,24},{24,20},{28,16},{1,13},{... | collective-permute-start | bytes 393224 | tf_op jit(solution)/shard_map/ppermute | solution.py:18

commit v15 on v14

--- a/solution.py
+++ b/solution.py
@@ -90,10 +90,13 @@
 
 
 def relay_kernel(half, source, waits, through, picks, far, *refs):
-    sends = refs[waits + through:][:half - 1]
+    sends = refs[waits + through:len(refs) - through]
     myself = lax.axis_index("leaf")
-    for step, send in enumerate(sends, 1):
-        send[0] = far[picks[source, myself ^ step, myself ^ half]]
+    for at, send in enumerate(sends):
+        chunk, step = divmod(at, half - 1)
+        wide = send.shape[-1]
+        node = picks[source, myself ^ (step + 1), myself ^ half]
+        send[0] = far[node, :, chunk * wide:(chunk + 1) * wide]
 
 
 def level_kernel(
@@ -185,16 +188,21 @@
     values, steps = far_rows(raw, "draw", draws)
     sends = call(
         functools.partial(relay_kernel, half, 0, len(got), len(values)),
-        [shape(1, rows, columns)] * (half - 1) + [shape(*value.shape) for value in values],
+        [shape(1, rows, wide)] * (CHUNKS * (half - 1)) + [shape(*value.shape) for value in values],
         [],
         (picks,),
         (far, *got, *values),
-        aliases={2 + len(got) + at: half - 1 + at for at in range(len(values))},
-    )
-    sends, values = take(sends, half - 1)
+        aliases={2 + len(got) + at: CHUNKS * (half - 1) + at for at in range(len(values))},
+    )
+    sends, values = take(sends, CHUNKS * (half - 1))
     packs, steps = near_rows(values, steps, "draw", draws)
-    entries = [(solved, 0), *((ref, 0) for ref in got), (far, 0), *((ref, 0) for ref in near(sends))]
-    pieces, done = [[entries] * CHUNKS], [(solved, (0, 0))]
+    pieces, done = [[]], [(solved, (0, 0))]
+    for at in chunks:
+        distant, sends = take(sends, half - 1)
+        pieces[0].append([
+            (solved, 0), *((ref, 0) for ref in got),
+            (far, 0), *((ref, 0) for ref in near(distant)),
+        ])
 
     for level in range(1, levels):
         last_level = level == levels - 1

time: 101 us -> 96.2 us (0.952)
  waiting for transfers between devices: 58 us -> 48.2 us
  starting transfers between devices: 26.2 us -> 31.5 us
    ppermute x24 -> x27, waiting for transfers between devices: 58 us -> 48.2 us  [hop(): return lax.ppermute(value, axis, [(at, at ^ step) for at in range(size)])]
    ppermute x24 -> x27, starting transfers between devices: 26.2 us -> 31.5 us  [hop(): return lax.ppermute(value, axis, [(at, at ^ step) for at in range(size)])]
  transfers between devices with their start and end apart: 24 -> 27, of which waited for: 13 -> 13; matrix products, arithmetic and copies ran while one was open for 1% -> 1% of each run, Pallas kernels for 6% -> 9%
where the time goes in v15:
time: 96.2 us; the launch traced here: 96 us
  waiting for transfers between devices  48.2 us (50%)
  starting transfers between devices  31.5 us (33%)
  Pallas kernels  13.7 us (14%)
  local copies, waits for them, and re-layouts  2.24 us (2%)
    ppermute x27, waiting for transfers between devices, hop(): return lax.ppermute(value, axis, [(at, at ^ step) for at in range(size)])  48.2 us
    ppermute x27, starting transfers between devices, hop(): return lax.ppermute(value, axis, [(at, at ^ step) for at in range(size)])  31.5 us
    pallas_call x8, Pallas kernels, call(): pl.pallas_call(kernel, out_shape=outs, in_specs=[SMEM] * len(small) + [VM...  13.7 us
  transfers between devices with their start and end apart: 27, of which 13 were waited for; matrix products, arithmetic and copies ran while one was open for 1% of the time, Pallas kernels for 9%

profile of v15, /device:TPU:0, one launch (start us, length us, event | category | flops | bytes accessed | tf_op | source)
XLA Modules:
  0.0 96.0 jit_solution(12736015830522295577)
XLA Ops:
  1.4 2.6 %collective-permute-start = (bf16[128,256]{1,0:T(8,128)(2,1)S(1)}, bf16[128,256]{1,0:T(8,128)(2,1)S(1)}, u32[]{:S(2)}, u32[]{:S(2)}) collective-permute-start(bf16[128,256]{1,0:T(8,128)(2,1)S(1)} %bitcast.8), channel_id=1, source_target_pairs={{0,2},{1,3},{2,0},{3,1},{4,6},{5,7},{6,4},{7,5},{8,10},{9,11},{10,... | collective-permute-start | bytes 196616 | tf_op jit(solution)/shard_map/ppermute | solution.py:18
  4.0 1.3 %fusion = (bf16[1,2,2,256,256]{4,3,2,1,0:T(8,128)(2,1)S(1)}, bf16[1,2,2,256,256]{4,3,2,1,0:T(8,128)(2,1)S(1)}) fusion(bf16[2,2,2,256,256]{4,3,2,1,0:T(8,128)(2,1)} %param.8), kind=kLoop, calls=%fused_computation.2 | loop fusion | bytes 2097152 | tf_op jit(solution)/shard_map/slice | solution.py:174
  5.4 1.3 %collective-permute-done.refs_1_ = bf16[128,256]{1,0:T(8,128)(2,1)S(1)} collective-permute-done((bf16[128,256]{1,0:T(8,128)(2,1)S(1)}, bf16[128,256]{1,0:T(8,128)(2,1)S(1)}, u32[]{:S(2)}, u32[]{:S(2)}) %collective-permute-start) | collective-permute-done | bytes 65568 | tf_op jit(solution)/shard_map/ppermute | solution.py:18
  6.7 1.2 %collective-permute-done.2.refs_3_ = bf16[128,256]{1,0:T(8,128)(2,1)S(1)} collective-permute-done((bf16[128,256]{1,0:T(8,128)(2,1)S(1)}, bf16[128,256]{1,0:T(8,128)(2,1)S(1)}, u32[]{:S(2)}, u32[]{:S(2)}) %collective-permute-start.2) | collective-permute-done | bytes 65568 | tf_op jit(solution)/shard_map/ppermute | solution.py:18
  7.9 1.1 %shard_map.64 = (bf16[2,256,512]{2,1,0:T(8,128)(2,1)S(1)}, bf16[1,256,512]{2,1,0:T(8,128)(2,1)S(1)}, bf16[1,256,512]{2,1,0:T(8,128)(2,1)S(1)}, bf16[1,256,512]{2,1,0:T(8,128)(2,1)S(1)}, bf16[2304,256]{1,0:T(8,128)(2,1)S(1)}) custom-call(s32[2,8,8]{2,1,0:T(8,128)S(1)} %copy-done.1, ...), custom_call_target="tpu_custom_call", output_to_operand_aliasing={{4}: (6, {})} | custom-call | flops 134217728 | bytes 4456448 | tf_op jit(solution)/shard_map/pallas_call | solution.py:51
  9.0 1.8 %collective-permute-start.7 = (bf16[2304,256]{1,0:T(8,128)(2,1)S(1)}, bf16[2304,256]{1,0:T(8,128)(2,1)S(1)}, u32[]{:S(2)}, u32[]{:S(2)}) collective-permute-start(bf16[2304,256]{1,0:T(8,128)(2,1)S(1)} %get-tuple-element.32.refs_3_), channel_id=1, source_target_pairs={{0,2},{1,3},{2,0},{3,1},{4,6},{5,7},{6,4},{7,5},{8,10},{9,11},{10,... | collective-permute-start | bytes 3538952 | tf_op jit(solution)/shard_map/ppermute | solution.py:18
  10.8 2.6 %collective-permute-start.3 = (bf16[2,256,512]{2,1,0:T(8,128)(2,1)S(1)}, bf16[2,256,512]{2,1,0:T(8,128)(2,1)S(1)}, u32[]{:S(2)}, u32[]{:S(2)}) collective-permute-start(bf16[2,256,512]{2,1,0:T(8,128)(2,1)S(1)} %get-tuple-element.28.refs_4_.refs_20_), channel_id=1, source_target_pairs={{0,16},{4,20},{8,24},{12,28},{16,0},{20,4},{24,8},{28,12},{1,17},{... | collective-permute-start | bytes 1572872 | tf_op jit(solution)/shard_map/ppermute | solution.py:18
  13.4 1.5 %collective-permute-start.4 = (bf16[1,256,512]{2,1,0:T(8,128)(2,1)S(1)}, bf16[1,256,512]{2,1,0:T(8,128)(2,1)S(1)}, u32[]{:S(2)}, u32[]{:S(2)}) collective-permute-start(bf16[1,256,512]{2,1,0:T(8,128)(2,1)S(1)} %get-tuple-element.29), channel_id=1, source_target_pairs={{0,4},{4,0},{8,12},{12,8},{16,20},{20,16},{24,28},{28,24},{1,5},{5... | collective-permute-start | bytes 786440 | tf_op jit(solution)/shard_map/ppermute | solution.py:18
  15.0 1.6 %collective-permute-start.5 = (bf16[1,256,512]{2,1,0:T(8,128)(2,1)S(1)}, bf16[1,256,512]{2,1,0:T(8,128)(2,1)S(1)}, u32[]{:S(2)}, u32[]{:S(2)}) collective-permute-start(bf16[1,256,512]{2,1,0:T(8,128)(2,1)S(1)} %get-tuple-element.30), channel_id=1, source_target_pairs={{0,8},{4,12},{8,0},{12,4},{16,24},{20,28},{24,16},{28,20},{1,9},{5... | collective-permute-start | bytes 786440 | tf_op jit(solution)/shard_map/ppermute | solution.py:18
  16.9 4.8 %collective-permute-done.4.refs_0_.refs_5_ = bf16[1,256,512]{2,1,0:T(8,128)(2,1)S(1)} collective-permute-done((bf16[1,256,512]{2,1,0:T(8,128)(2,1)S(1)}, bf16[1,256,512]{2,1,0:T(8,128)(2,1)S(1)}, u32[]{:S(2)}, u32[]{:S(2)}) %collective-permute-start.4) | collective-permute-done | bytes 262176 | tf_op jit(solution)/shard_map/ppermute | solution.py:18
  21.8 9.6 %collective-permute-done.5.refs_1_.refs_6_ = bf16[1,256,512]{2,1,0:T(8,128)(2,1)S(1)} collective-permute-done((bf16[1,256,512]{2,1,0:T(8,128)(2,1)S(1)}, bf16[1,256,512]{2,1,0:T(8,128)(2,1)S(1)}, u32[]{:S(2)}, u32[]{:S(2)}) %collective-permute-start.5) | collective-permute-done | bytes 262176 | tf_op jit(solution)/shard_map/ppermute | solution.py:18
  31.4 6.7 %collective-permute-done.6.refs_2_.refs_7_ = bf16[1,256,512]{2,1,0:T(8,128)(2,1)S(1)} collective-permute-done((bf16[1,256,512]{2,1,0:T(8,128)(2,1)S(1)}, bf16[1,256,512]{2,1,0:T(8,128)(2,1)S(1)}, u32[]{:S(2)}, u32[]{:S(2)}) %collective-permute-start.6) | collective-permute-done | bytes 262176 | tf_op jit(solution)/shard_map/ppermute | solution.py:18
  39.5 1.5 %collective-permute-start.13 = (bf16[1,256,256]{2,1,0:T(8,128)(2,1)S(1)}, bf16[1,256,256]{2,1,0:T(8,128)(2,1)S(1)}, u32[]{:S(2)}, u32[]{:S(2)}) collective-permute-start(bf16[1,256,256]{2,1,0:T(8,128)(2,1)S(1)} %get-tuple-element.38), channel_id=1, source_target_pairs={{0,4},{4,0},{8,12},{12,8},{16,20},{20,16},{24,28},{28,24},{1,5},{5... | collective-permute-start | bytes 393224 | tf_op jit(solution)/shard_map/ppermute | solution.py:18
  41.8 1.2 %collective-permute-start.15 = (bf16[1,256,256]{2,1,0:T(8,128)(2,1)S(1)}, bf16[1,256,256]{2,1,0:T(8,128)(2,1)S(1)}, u32[]{:S(2)}, u32[]{:S(2)}) collective-permute-start(bf16[1,256,256]{2,1,0:T(8,128)(2,1)S(1)} %get-tuple-element.40), channel_id=1, source_target_pairs={{0,12},{4,8},{8,4},{12,0},{16,28},{20,24},{24,20},{28,16},{1,13},{... | collective-permute-start | bytes 393224 | tf_op jit(solution)/shard_map/ppermute | solution.py:18
  43.0 2.0 %collective-permute-done.13.refs_9_ = bf16[1,256,256]{2,1,0:T(8,128)(2,1)S(1)} collective-permute-done((bf16[1,256,256]{2,1,0:T(8,128)(2,1)S(1)}, bf16[1,256,256]{2,1,0:T(8,128)(2,1)S(1)}, u32[]{:S(2)}, u32[]{:S(2)}) %collective-permute-start.13) | collective-permute-done | bytes 131104 | tf_op jit(solution)/shard_map/ppermute | solution.py:18
  45.0 1.5 %collective-permute-start.10 = (bf16[1,256,256]{2,1,0:T(8,128)(2,1)S(1)}, bf16[1,256,256]{2,1,0:T(8,128)(2,1)S(1)}, u32[]{:S(2)}, u32[]{:S(2)}) collective-permute-start(bf16[1,256,256]{2,1,0:T(8,128)(2,1)S(1)} %get-tuple-element.35), channel_id=1, source_target_pairs={{0,4},{4,0},{8,12},{12,8},{16,20},{20,16},{24,28},{28,24},{1,5},{5... | collective-permute-start | bytes 393224 | tf_op jit(solution)/shard_map/ppermute | solution.py:18
  48.2 1.7 %collective-permute-done.15.refs_11_ = bf16[1,256,256]{2,1,0:T(8,128)(2,1)S(1)} collective-permute-done((bf16[1,256,256]{2,1,0:T(8,128)(2,1)S(1)}, bf16[1,256,256]{2,1,0:T(8,128)(2,1)S(1)}, u32[]{:S(2)}, u32[]{:S(2)}) %collective-permute-start.15) | collective-permute-done | bytes 131104 | tf_op jit(solution)/shard_map/ppermute | solution.py:18
  49.9 1.7 %collective-permute-start.12 = (bf16[1,256,256]{2,1,0:T(8,128)(2,1)S(1)}, bf16[1,256,256]{2,1,0:T(8,128)(2,1)S(1)}, u32[]{:S(2)}, u32[]{:S(2)}) collective-permute-start(bf16[1,256,256]{2,1,0:T(8,128)(2,1)S(1)} %get-tuple-element.37), channel_id=1, source_target_pairs={{0,12},{4,8},{8,4},{12,0},{16,28},{20,24},{24,20},{28,16},{1,13},{... | collective-permute-start | bytes 393224 | tf_op jit(solution)/shard_map/ppermute | solution.py:18
  51.6 2.4 %shard_map.66.refs_12_.refs_21_ = bf16[2,256,256]{2,1,0:T(8,128)(2,1)S(1)} custom-call(s32[2,8,8]{2,1,0:T(8,128)S(1)} %copy-done.1, s32[2,2,8]{2,1,0:T(2,128)S(1)} %copy-done.2, s32[2,2]{1,0:T(2,128)S(1)} %copy-done.3, bf16[3,2,256,512]{3,2,1,0:T(8,128)(2,1)S(1)} %copy-done, bf16[2304,256]{1,0:T(8,128)(2,1)S(1)} %get-tuple-element.33.refs_0_, ...), custom_call_target="tpu_custom_call" | custom-call | flops 603979776 | bytes 8781824 | tf_op jit(solution)/shard_map/pallas_call | solution.py:51
  54.0 2.7 %collective-permute-start.23 = (bf16[2,256,256]{2,1,0:T(8,128)(2,1)S(1)}, bf16[2,256,256]{2,1,0:T(8,128)(2,1)S(1)}, u32[]{:S(2)}, u32[]{:S(2)}) collective-permute-start(bf16[2,256,256]{2,1,0:T(8,128)(2,1)S(1)} %shard_map.66.refs_12_.refs_21_), channel_id=1, source_target_pairs={{0,16},{4,20},{8,24},{12,28},{16,0},{20,4},{24,8},{28,12},{1,17},{... | collective-permute-start | bytes 786440 | tf_op jit(solution)/shard_map/ppermute | solution.py:18
  56.7 2.5 %shard_map.67 = (bf16[2,256,256]{2,1,0:T(8,128)(2,1)S(1)}, bf16[2,256,256]{2,1,0:T(8,128)(2,1)S(1)}, bf16[2,256,256]{2,1,0:T(8,128)(2,1)S(1)}, bf16[2,256,256]{2,1,0:T(8,128)(2,1)S(1)}) custom-call(s32[2,8,8]{2,1,0:T(8,128)S(1)} %copy-done.1, s32[2,2,8]{2,1,0:T(2,128)S(1)} %copy-done.2, s32[2,2]{1,0:T(2,128)S(1)} %copy-done.3, ...), custom_call_target="tpu_custom_call" | custom-call | flops 603979776 | bytes 9830400 | tf_op jit(solution)/shard_map/pallas_call | solution.py:51
  59.2 1.7 %collective-permute-start.16 = (bf16[2,256,256]{2,1,0:T(8,128)(2,1)S(1)}, bf16[2,256,256]{2,1,0:T(8,128)(2,1)S(1)}, u32[]{:S(2)}, u32[]{:S(2)}) collective-permute-start(bf16[2,256,256]{2,1,0:T(8,128)(2,1)S(1)} %get-tuple-element.42), channel_id=1, source_target_pairs={{0,4},{4,0},{8,12},{12,8},{16,20},{20,16},{24,28},{28,24},{1,5},{5... | collective-permute-start | bytes 786440 | tf_op jit(solution)/shard_map/ppermute | solution.py:18
  60.8 1.9 %collective-permute-start.18 = (bf16[2,256,256]{2,1,0:T(8,128)(2,1)S(1)}, bf16[2,256,256]{2,1,0:T(8,128)(2,1)S(1)}, u32[]{:S(2)}, u32[]{:S(2)}) collective-permute-start(bf16[2,256,256]{2,1,0:T(8,128)(2,1)S(1)} %get-tuple-element.44), channel_id=1, source_target_pairs={{0,12},{4,8},{8,4},{12,0},{16,28},{20,24},{24,20},{28,16},{1,13},{... | collective-permute-start | bytes 786440 | tf_op jit(solution)/shard_map/ppermute | solution.py:18
  62.7 1.9 %collective-permute-start.19 = (bf16[2,256,256]{2,1,0:T(8,128)(2,1)S(1)}, bf16[2,256,256]{2,1,0:T(8,128)(2,1)S(1)}, u32[]{:S(2)}, u32[]{:S(2)}) collective-permute-start(bf16[2,256,256]{2,1,0:T(8,128)(2,1)S(1)} %get-tuple-element.41.refs_12_.refs_22_), channel_id=1, source_target_pairs={{0,16},{4,20},{8,24},{12,28},{16,0},{20,4},{24,8},{28,12},{1,17},{... | collective-permute-start | bytes 786440 | tf_op jit(solution)/shard_map/ppermute | solution.py:18
  64.7 3.8 %collective-permute-done.23.far.refs_16_ = bf16[2,256,256]{2,1,0:T(8,128)(2,1)S(1)} collective-permute-done((bf16[2,256,256]{2,1,0:T(8,128)(2,1)S(1)}, bf16[2,256,256]{2,1,0:T(8,128)(2,1)S(1)}, u32[]{:S(2)}, u32[]{:S(2)}) %collective-permute-start.23) | collective-permute-done | bytes 262176 | tf_op jit(solution)/shard_map/ppermute | solution.py:18
  69.9 8.1 %collective-permute-done.17.refs_1_.refs_14_ = bf16[2,256,256]{2,1,0:T(8,128)(2,1)S(1)} collective-permute-done((bf16[2,256,256]{2,1,0:T(8,128)(2,1)S(1)}, bf16[2,256,256]{2,1,0:T(8,128)(2,1)S(1)}, u32[]{:S(2)}, u32[]{:S(2)}) %collective-permute-start.17) | collective-permute-done | bytes 262176 | tf_op jit(solution)/shard_map/ppermute | solution.py:18
  78.0 5.9 %collective-permute-done.18.refs_2_.refs_15_ = bf16[2,256,256]{2,1,0:T(8,128)(2,1)S(1)} collective-permute-done((bf16[2,256,256]{2,1,0:T(8,128)(2,1)S(1)}, bf16[2,256,256]{2,1,0:T(8,128)(2,1)S(1)}, u32[]{:S(2)}, u32[]{:S(2)}) %collective-permute-start.18) | collective-permute-done | bytes 262176 | tf_op jit(solution)/shard_map/ppermute | solution.py:18
  84.6 1.3 %collective-permute-start.20 = (bf16[1,256,256]{2,1,0:T(8,128)(2,1)S(1)}, bf16[1,256,256]{2,1,0:T(8,128)(2,1)S(1)}, u32[]{:S(2)}, u32[]{:S(2)}) collective-permute-start(bf16[1,256,256]{2,1,0:T(8,128)(2,1)S(1)} %get-tuple-element.45), channel_id=1, source_target_pairs={{0,4},{4,0},{8,12},{12,8},{16,20},{20,16},{24,28},{28,24},{1,5},{5... | collective-permute-start | bytes 393224 | tf_op jit(solution)/shard_map/ppermute | solution.py:18
  85.9 2.3 %collective-permute-start.22 = (bf16[1,256,256]{2,1,0:T(8,128)(2,1)S(1)}, bf16[1,256,256]{2,1,0:T(8,128)(2,1)S(1)}, u32[]{:S(2)}, u32[]{:S(2)}) collective-permute-start(bf16[1,256,256]{2,1,0:T(8,128)(2,1)S(1)} %get-tuple-element.47), channel_id=1, source_target_pairs={{0,12},{4,8},{8,4},{12,0},{16,28},{20,24},{24,20},{28,16},{1,13},{... | collective-permute-start | bytes 393224 | tf_op jit(solution)/shard_map/ppermute | solution.py:18
  88.2 1.3 %collective-permute-done.26.refs_19_ = bf16[1,256,256]{2,1,0:T(8,128)(2,1)S(1)} collective-permute-done((bf16[1,256,256]{2,1,0:T(8,128)(2,1)S(1)}, bf16[1,256,256]{2,1,0:T(8,128)(2,1)S(1)}, u32[]{:S(2)}, u32[]{:S(2)}) %collective-permute-start.26) | collective-permute-done | bytes 131104 | tf_op jit(solution)/shard_map/ppermute | solution.py:18
  89.5 2.5 %shard_map.70.refs_23_ = bf16[2,256,256]{2,1,0:T(8,128)(2,1)S(1)} custom-call(s32[2,8,8]{2,1,0:T(8,128)S(1)} %copy-done.1, s32[2,2,8]{2,1,0:T(2,128)S(1)} %copy-done.2, s32[2,2]{1,0:T(2,128)S(1)} %copy-done.3, bf16[3,2,256,512]{3,2,1,0:T(8,128)(2,1)S(1)} %copy-done, bf16[2304,256]{1,0:T(8,128)(2,1)S(1)} %get-tuple-element.33.refs_0_, ...), custom_call_target="tpu_custom_call" | custom-call | flops 603979776 | bytes 10485760 | tf_op jit(solution)/shard_map/pallas_call | solution.py:51
  92.7 3.2 %shard_map.71 = bf16[3,2,256,512]{3,2,1,0:T(8,128)(2,1)} custom-call(s32[2,8,8]{2,1,0:T(8,128)S(1)} %copy-done.1, s32[2,2,8]{2,1,0:T(2,128)S(1)} %copy-done.2, s32[2,2]{1,0:T(2,128)S(1)} %copy-done.3, bf16[3,2,256,512]{3,2,1,0:T(8,128)(2,1)S(1)} %copy-done, bf16[2304,256]{1,0:T(8,128)(2,1)S(1)} %get-tuple-element.33.refs_0_, ...), custom_call_target="tpu_custom_call" | custom-call | flops 603979776 | bytes 13107200 | tf_op jit(solution)/shard_map/pallas_call | solution.py:51
  (42 shorter events, 8.7 us)
Async XLA Ops:
  0.9 5.8 %collective-permute-start.1 = (bf16[128,256]{1,0:T(8,128)(2,1)S(1)}, bf16[128,256]{1,0:T(8,128)(2,1)S(1)}, u32[]{:S(2)}, u32[]{:S(2)}) collective-permute-start(bf16[128,256]{1,0:T(8,128)(2,1)S(1)} %bitcast.7), channel_id=1, source_target_pairs={{0,1},{1,0},{2,3},{3,2},{4,5},{5,4},{6,7},{7,6},{8,9},{9,8},{10,11... | collective-permute-start | bytes 196616 | tf_op jit(solution)/shard_map/ppermute | solution.py:18
  1.4 5.3 %collective-permute-start = (bf16[128,256]{1,0:T(8,128)(2,1)S(1)}, bf16[128,256]{1,0:T(8,128)(2,1)S(1)}, u32[]{:S(2)}, u32[]{:S(2)}) collective-permute-start(bf16[128,256]{1,0:T(8,128)(2,1)S(1)} %bitcast.8), channel_id=1, source_target_pairs={{0,2},{1,3},{2,0},{3,1},{4,6},{5,7},{6,4},{7,5},{8,10},{9,11},{10,... | collective-permute-start | bytes 196616 | tf_op jit(solution)/shard_map/ppermute | solution.py:18
  5.3 1.4 %copy-start = (bf16[3,2,256,512]{3,2,1,0:T(8,128)(2,1)S(1)}, bf16[3,2,256,512]{3,2,1,0:T(8,128)(2,1)}, u32[]{:S(2)}) copy-start(bf16[3,2,256,512]{3,2,1,0:T(8,128)(2,1)} %noise.7) | copy-start | bytes 4718596
  5.3 2.7 %copy-start.1 = (s32[2,8,8]{2,1,0:T(8,128)S(1)}, s32[2,8,8]{2,1,0:T(8,128)}, u32[]{:S(2)}) copy-start(s32[2,8,8]{2,1,0:T(8,128)} %picks.15) | copy-start | bytes 1540
  6.7 1.3 %collective-permute-start.2 = (bf16[128,256]{1,0:T(8,128)(2,1)S(1)}, bf16[128,256]{1,0:T(8,128)(2,1)S(1)}, u32[]{:S(2)}, u32[]{:S(2)}) collective-permute-start(bf16[128,256]{1,0:T(8,128)(2,1)S(1)} %collective-permute-done.refs_1_), channel_id=1, source_target_pairs={{0,1},{1,0},{2,3},{3,2},{4,5},{5,4},{6,7},{7,6},{8,9},{9,8},{10,11... | collective-permute-start | bytes 196616 | tf_op jit(solution)/shard_map/ppermute | solution.py:18
  9.0 29.1 %collective-permute-start.7 = (bf16[2304,256]{1,0:T(8,128)(2,1)S(1)}, bf16[2304,256]{1,0:T(8,128)(2,1)S(1)}, u32[]{:S(2)}, u32[]{:S(2)}) collective-permute-start(bf16[2304,256]{1,0:T(8,128)(2,1)S(1)} %get-tuple-element.32.refs_3_), channel_id=1, source_target_pairs={{0,2},{1,3},{2,0},{3,1},{4,6},{5,7},{6,4},{7,5},{8,10},{9,11},{10,... | collective-permute-start | bytes 3538952 | tf_op jit(solution)/shard_map/ppermute | solution.py:18
  10.8 27.3 %collective-permute-start.3 = (bf16[2,256,512]{2,1,0:T(8,128)(2,1)S(1)}, bf16[2,256,512]{2,1,0:T(8,128)(2,1)S(1)}, u32[]{:S(2)}, u32[]{:S(2)}) collective-permute-start(bf16[2,256,512]{2,1,0:T(8,128)(2,1)S(1)} %get-tuple-element.28.refs_4_.refs_20_), channel_id=1, source_target_pairs={{0,16},{4,20},{8,24},{12,28},{16,0},{20,4},{24,8},{28,12},{1,17},{... | collective-permute-start | bytes 1572872 | tf_op jit(solution)/shard_map/ppermute | solution.py:18
  13.4 8.3 %collective-permute-start.4 = (bf16[1,256,512]{2,1,0:T(8,128)(2,1)S(1)}, bf16[1,256,512]{2,1,0:T(8,128)(2,1)S(1)}, u32[]{:S(2)}, u32[]{:S(2)}) collective-permute-start(bf16[1,256,512]{2,1,0:T(8,128)(2,1)S(1)} %get-tuple-element.29), channel_id=1, source_target_pairs={{0,4},{4,0},{8,12},{12,8},{16,20},{20,16},{24,28},{28,24},{1,5},{5... | collective-permute-start | bytes 786440 | tf_op jit(solution)/shard_map/ppermute | solution.py:18
  15.0 16.5 %collective-permute-start.5 = (bf16[1,256,512]{2,1,0:T(8,128)(2,1)S(1)}, bf16[1,256,512]{2,1,0:T(8,128)(2,1)S(1)}, u32[]{:S(2)}, u32[]{:S(2)}) collective-permute-start(bf16[1,256,512]{2,1,0:T(8,128)(2,1)S(1)} %get-tuple-element.30), channel_id=1, source_target_pairs={{0,8},{4,12},{8,0},{12,4},{16,24},{20,28},{24,16},{28,20},{1,9},{5... | collective-permute-start | bytes 786440 | tf_op jit(solution)/shard_map/ppermute | solution.py:18
  16.5 35.1 %copy-start.2 = (s32[2,2,8]{2,1,0:T(2,128)S(1)}, s32[2,2,8]{2,1,0:T(2,128)}, u32[]{:S(2)}) copy-start(s32[2,2,8]{2,1,0:T(2,128)} %lists.7) | copy-start | bytes 388
  16.5 35.1 %copy-start.3 = (s32[2,2]{1,0:T(2,128)S(1)}, s32[2,2]{1,0:T(2,128)}, u32[]{:S(2)}) copy-start(s32[2,2]{1,0:T(2,128)} %counts.7) | copy-start | bytes 52
  16.5 21.6 %collective-permute-start.6 = (bf16[1,256,512]{2,1,0:T(8,128)(2,1)S(1)}, bf16[1,256,512]{2,1,0:T(8,128)(2,1)S(1)}, u32[]{:S(2)}, u32[]{:S(2)}) collective-permute-start(bf16[1,256,512]{2,1,0:T(8,128)(2,1)S(1)} %get-tuple-element.31), channel_id=1, source_target_pairs={{0,12},{4,8},{8,4},{12,0},{16,28},{20,24},{24,20},{28,16},{1,13},{... | collective-permute-start | bytes 786440 | tf_op jit(solution)/shard_map/ppermute | solution.py:18
  38.9 12.7 %collective-permute-start.8 = (bf16[2304,256]{1,0:T(8,128)(2,1)S(1)}, bf16[2304,256]{1,0:T(8,128)(2,1)S(1)}, u32[]{:S(2)}, u32[]{:S(2)}) collective-permute-start(bf16[2304,256]{1,0:T(8,128)(2,1)S(1)} %get-tuple-element.33.refs_0_), channel_id=1, source_target_pairs={{0,1},{1,0},{2,3},{3,2},{4,5},{5,4},{6,7},{7,6},{8,9},{9,8},{10,11... | collective-permute-start | bytes 3538952 | tf_op jit(solution)/shard_map/ppermute | solution.py:18
  39.0 12.6 %collective-permute-start.9 = (bf16[2304,256]{1,0:T(8,128)(2,1)S(1)}, bf16[2304,256]{1,0:T(8,128)(2,1)S(1)}, u32[]{:S(2)}, u32[]{:S(2)}) collective-permute-start(bf16[2304,256]{1,0:T(8,128)(2,1)S(1)} %get-tuple-element.34.refs_1_), channel_id=1, source_target_pairs={{0,1},{1,0},{2,3},{3,2},{4,5},{5,4},{6,7},{7,6},{8,9},{9,8},{10,11... | collective-permute-start | bytes 3538952 | tf_op jit(solution)/shard_map/ppermute | solution.py:18
  39.5 5.5 %collective-permute-start.13 = (bf16[1,256,256]{2,1,0:T(8,128)(2,1)S(1)}, bf16[1,256,256]{2,1,0:T(8,128)(2,1)S(1)}, u32[]{:S(2)}, u32[]{:S(2)}) collective-permute-start(bf16[1,256,256]{2,1,0:T(8,128)(2,1)S(1)} %get-tuple-element.38), channel_id=1, source_target_pairs={{0,4},{4,0},{8,12},{12,8},{16,20},{20,16},{24,28},{28,24},{1,5},{5... | collective-permute-start | bytes 393224 | tf_op jit(solution)/shard_map/ppermute | solution.py:18
  41.0 6.4 %collective-permute-start.14 = (bf16[1,256,256]{2,1,0:T(8,128)(2,1)S(1)}, bf16[1,256,256]{2,1,0:T(8,128)(2,1)S(1)}, u32[]{:S(2)}, u32[]{:S(2)}) collective-permute-start(bf16[1,256,256]{2,1,0:T(8,128)(2,1)S(1)} %get-tuple-element.39), channel_id=1, source_target_pairs={{0,8},{4,12},{8,0},{12,4},{16,24},{20,28},{24,16},{28,20},{1,9},{5... | collective-permute-start | bytes 393224 | tf_op jit(solution)/shard_map/ppermute | solution.py:18
  41.8 8.1 %collective-permute-start.15 = (bf16[1,256,256]{2,1,0:T(8,128)(2,1)S(1)}, bf16[1,256,256]{2,1,0:T(8,128)(2,1)S(1)}, u32[]{:S(2)}, u32[]{:S(2)}) collective-permute-start(bf16[1,256,256]{2,1,0:T(8,128)(2,1)S(1)} %get-tuple-element.40), channel_id=1, source_target_pairs={{0,12},{4,8},{8,4},{12,0},{16,28},{20,24},{24,20},{28,16},{1,13},{... | collective-permute-start | bytes 393224 | tf_op jit(solution)/shard_map/ppermute | solution.py:18
  45.0 11.7 %collective-permute-start.10 = (bf16[1,256,256]{2,1,0:T(8,128)(2,1)S(1)}, bf16[1,256,256]{2,1,0:T(8,128)(2,1)S(1)}, u32[]{:S(2)}, u32[]{:S(2)}) collective-permute-start(bf16[1,256,256]{2,1,0:T(8,128)(2,1)S(1)} %get-tuple-element.35), channel_id=1, source_target_pairs={{0,4},{4,0},{8,12},{12,8},{16,20},{20,16},{24,28},{28,24},{1,5},{5... | collective-permute-start | bytes 393224 | tf_op jit(solution)/shard_map/ppermute | solution.py:18
  47.4 9.3 %collective-permute-start.11 = (bf16[1,256,256]{2,1,0:T(8,128)(2,1)S(1)}, bf16[1,256,256]{2,1,0:T(8,128)(2,1)S(1)}, u32[]{:S(2)}, u32[]{:S(2)}) collective-permute-start(bf16[1,256,256]{2,1,0:T(8,128)(2,1)S(1)} %get-tuple-element.36), channel_id=1, source_target_pairs={{0,8},{4,12},{8,0},{12,4},{16,24},{20,28},{24,16},{28,20},{1,9},{5... | collective-permute-start | bytes 393224 | tf_op jit(solution)/shard_map/ppermute | solution.py:18
  49.9 6.8 %collective-permute-start.12 = (bf16[1,256,256]{2,1,0:T(8,128)(2,1)S(1)}, bf16[1,256,256]{2,1,0:T(8,128)(2,1)S(1)}, u32[]{:S(2)}, u32[]{:S(2)}) collective-permute-start(bf16[1,256,256]{2,1,0:T(8,128)(2,1)S(1)} %get-tuple-element.37), channel_id=1, source_target_pairs={{0,12},{4,8},{8,4},{12,0},{16,28},{20,24},{24,20},{28,16},{1,13},{... | collective-permute-start | bytes 393224 | tf_op jit(solution)/shard_map/ppermute | solution.py:18
  54.0 14.4 %collective-permute-start.23 = (bf16[2,256,256]{2,1,0:T(8,128)(2,1)S(1)}, bf16[2,256,256]{2,1,0:T(8,128)(2,1)S(1)}, u32[]{:S(2)}, u32[]{:S(2)}) collective-permute-start(bf16[2,256,256]{2,1,0:T(8,128)(2,1)S(1)} %shard_map.66.refs_12_.refs_21_), channel_id=1, source_target_pairs={{0,16},{4,20},{8,24},{12,28},{16,0},{20,4},{24,8},{28,12},{1,17},{... | collective-permute-start | bytes 786440 | tf_op jit(solution)/shard_map/ppermute | solution.py:18
  59.2 10.7 %collective-permute-start.16 = (bf16[2,256,256]{2,1,0:T(8,128)(2,1)S(1)}, bf16[2,256,256]{2,1,0:T(8,128)(2,1)S(1)}, u32[]{:S(2)}, u32[]{:S(2)}) collective-permute-start(bf16[2,256,256]{2,1,0:T(8,128)(2,1)S(1)} %get-tuple-element.42), channel_id=1, source_target_pairs={{0,4},{4,0},{8,12},{12,8},{16,20},{20,16},{24,28},{28,24},{1,5},{5... | collective-permute-start | bytes 786440 | tf_op jit(solution)/shard_map/ppermute | solution.py:18
  60.8 17.1 %collective-permute-start.17 = (bf16[2,256,256]{2,1,0:T(8,128)(2,1)S(1)}, bf16[2,256,256]{2,1,0:T(8,128)(2,1)S(1)}, u32[]{:S(2)}, u32[]{:S(2)}) collective-permute-start(bf16[2,256,256]{2,1,0:T(8,128)(2,1)S(1)} %get-tuple-element.43), channel_id=1, source_target_pairs={{0,8},{4,12},{8,0},{12,4},{16,24},{20,28},{24,16},{28,20},{1,9},{5... | collective-permute-start | bytes 786440 | tf_op jit(solution)/shard_map/ppermute | solution.py:18
  60.8 23.1 %collective-permute-start.18 = (bf16[2,256,256]{2,1,0:T(8,128)(2,1)S(1)}, bf16[2,256,256]{2,1,0:T(8,128)(2,1)S(1)}, u32[]{:S(2)}, u32[]{:S(2)}) collective-permute-start(bf16[2,256,256]{2,1,0:T(8,128)(2,1)S(1)} %get-tuple-element.44), channel_id=1, source_target_pairs={{0,12},{4,8},{8,4},{12,0},{16,28},{20,24},{24,20},{28,16},{1,13},{... | collective-permute-start | bytes 786440 | tf_op jit(solution)/shard_map/ppermute | solution.py:18
  62.7 21.2 %collective-permute-start.19 = (bf16[2,256,256]{2,1,0:T(8,128)(2,1)S(1)}, bf16[2,256,256]{2,1,0:T(8,128)(2,1)S(1)}, u32[]{:S(2)}, u32[]{:S(2)}) collective-permute-start(bf16[2,256,256]{2,1,0:T(8,128)(2,1)S(1)} %get-tuple-element.41.refs_12_.refs_22_), channel_id=1, source_target_pairs={{0,16},{4,20},{8,24},{12,28},{16,0},{20,4},{24,8},{28,12},{1,17},{... | collective-permute-start | bytes 786440 | tf_op jit(solution)/shard_map/ppermute | solution.py:18
  69.2 16.7 %collective-permute-start.24 = (bf16[1,256,256]{2,1,0:T(8,128)(2,1)S(1)}, bf16[1,256,256]{2,1,0:T(8,128)(2,1)S(1)}, u32[]{:S(2)}, u32[]{:S(2)}) collective-permute-start(bf16[1,256,256]{2,1,0:T(8,128)(2,1)S(1)} %get-tuple-element.48), channel_id=1, source_target_pairs={{0,4},{4,0},{8,12},{12,8},{16,20},{20,16},{24,28},{28,24},{1,5},{5... | collective-permute-start | bytes 393224 | tf_op jit(solution)/shard_map/ppermute | solution.py:18
  69.9 18.3 %collective-permute-start.25 = (bf16[1,256,256]{2,1,0:T(8,128)(2,1)S(1)}, bf16[1,256,256]{2,1,0:T(8,128)(2,1)S(1)}, u32[]{:S(2)}, u32[]{:S(2)}) collective-permute-start(bf16[1,256,256]{2,1,0:T(8,128)(2,1)S(1)} %get-tuple-element.49), channel_id=1, source_target_pairs={{0,8},{4,12},{8,0},{12,4},{16,24},{20,28},{24,16},{28,20},{1,9},{5... | collective-permute-start | bytes 393224 | tf_op jit(solution)/shard_map/ppermute | solution.py:18
  78.0 11.5 %collective-permute-start.26 = (bf16[1,256,256]{2,1,0:T(8,128)(2,1)S(1)}, bf16[1,256,256]{2,1,0:T(8,128)(2,1)S(1)}, u32[]{:S(2)}, u32[]{:S(2)}) collective-permute-start(bf16[1,256,256]{2,1,0:T(8,128)(2,1)S(1)} %get-tuple-element.50), channel_id=1, source_target_pairs={{0,12},{4,8},{8,4},{12,0},{16,28},{20,24},{24,20},{28,16},{1,13},{... | collective-permute-start | bytes 393224 | tf_op jit(solution)/shard_map/ppermute | solution.py:18
  84.6 7.4 %collective-permute-start.20 = (bf16[1,256,256]{2,1,0:T(8,128)(2,1)S(1)}, bf16[1,256,256]{2,1,0:T(8,128)(2,1)S(1)}, u32[]{:S(2)}, u32[]{:S(2)}) collective-permute-start(bf16[1,256,256]{2,1,0:T(8,128)(2,1)S(1)} %get-tuple-element.45), channel_id=1, source_target_pairs={{0,4},{4,0},{8,12},{12,8},{16,20},{20,16},{24,28},{28,24},{1,5},{5... | collective-permute-start | bytes 393224 | tf_op jit(solution)/shard_map/ppermute | solution.py:18
  85.9 6.1 %collective-permute-start.21 = (bf16[1,256,256]{2,1,0:T(8,128)(2,1)S(1)}, bf16[1,256,256]{2,1,0:T(8,128)(2,1)S(1)}, u32[]{:S(2)}, u32[]{:S(2)}) collective-permute-start(bf16[1,256,256]{2,1,0:T(8,128)(2,1)S(1)} %get-tuple-element.46), channel_id=1, source_target_pairs={{0,8},{4,12},{8,0},{12,4},{16,24},{20,28},{24,16},{28,20},{1,9},{5... | collective-permute-start | bytes 393224 | tf_op jit(solution)/shard_map/ppermute | solution.py:18
  85.9 6.9 %collective-permute-start.22 = (bf16[1,256,256]{2,1,0:T(8,128)(2,1)S(1)}, bf16[1,256,256]{2,1,0:T(8,128)(2,1)S(1)}, u32[]{:S(2)}, u32[]{:S(2)}) collective-permute-start(bf16[1,256,256]{2,1,0:T(8,128)(2,1)S(1)} %get-tuple-element.47), channel_id=1, source_target_pairs={{0,12},{4,8},{8,4},{12,0},{16,28},{20,24},{24,20},{28,16},{1,13},{... | collective-permute-start | bytes 393224 | tf_op jit(solution)/shard_map/ppermute | solution.py:18

commit v16 on v15

--- a/solution.py
+++ b/solution.py
@@ -147,14 +147,14 @@
                 total = term if total is None else total + term
         right_side = (noise[level, node, :, columns].astype(F32) - total).astype(BF16)
         solved[node] = transposed_dot(inv[node], right_side).astype(BF16)
+        if done:
+            here = target.at[level, node, :, pl.ds(chunk * wide, wide)]
+            copies.append(pltpu.make_async_copy(solved.at[node], here, sems.at[len(copies)]))
+            copies[-1].start()
     for step, send in enumerate(sends, 1):
         node = picks[level, myself ^ step, myself]
         for at, ref in enumerate([*chunks, solved]):
             send[at] = ref[node]
-    if done:
-        here = target.at[level, :, :, pl.ds(chunk * wide, wide)]
-        copies.append(pltpu.make_async_copy(solved, here, sems.at[len(done)]))
-        copies[-1].start()
     for copy in copies:
         copy.wait()
 
@@ -217,7 +217,7 @@
             if final:
                 scratch += [
                     pltpu.VMEM((nodes, rows, wide), BF16),
-                    pltpu.SemaphoreType.DMA((len(stored) + 1,)),
+                    pltpu.SemaphoreType.DMA((len(stored) + nodes,)),
                 ]
             here, *sent = call(
                 functools.partial(
@@ -240,13 +240,12 @@
         got = near(sends)
         pieces.append([])
         for at in chunks:
-            waits = got if at == CHUNKS - 1 else []
             sends = call(
-                functools.partial(relay_kernel, half, level, len(waits), 0),
+                functools.partial(relay_kernel, half, level, 0, 0),
                 [shape(1, rows, wide)] * (half - 1),
                 [],
                 (picks,),
-                (far[at], *waits),
+                (far[at],),
             )
             pieces[level].append([
                 (solved[at], 0), *((ref, at) for ref in got),

time: 96.2 us -> 97.2 us (1.010)
  transfers between devices with their start and end apart: 27 -> 27, of which waited for: 13 -> 14; matrix products, arithmetic and copies ran while one was open for 1% -> 1% of each run, Pallas kernels for 9% -> 9%
where the time goes in v16:
time: 97.2 us; the launch traced here: 97 us
  waiting for transfers between devices  48.9 us (50%)
  starting transfers between devices  31.9 us (33%)
  Pallas kernels  13.7 us (14%)
  local copies, waits for them, and re-layouts  2.24 us (2%)
    ppermute x27, waiting for transfers between devices, hop(): return lax.ppermute(value, axis, [(at, at ^ step) for at in range(size)])  48.9 us
    ppermute x27, starting transfers between devices, hop(): return lax.ppermute(value, axis, [(at, at ^ step) for at in range(size)])  31.9 us
    pallas_call x8, Pallas kernels, call(): pl.pallas_call(kernel, out_shape=outs, in_specs=[SMEM] * len(small) + [VM...  13.7 us
  transfers between devices with their start and end apart: 27, of which 14 were waited for; matrix products, arithmetic and copies ran while one was open for 1% of the time, Pallas kernels for 9%

profile of v16, /device:TPU:0, one launch (start us, length us, event | category | flops | bytes accessed | tf_op | source)
XLA Modules:
  0.0 97.0 jit_solution(15235467800148218370)
XLA Ops:
  1.4 2.6 %collective-permute-start = (bf16[128,256]{1,0:T(8,128)(2,1)S(1)}, bf16[128,256]{1,0:T(8,128)(2,1)S(1)}, u32[]{:S(2)}, u32[]{:S(2)}) collective-permute-start(bf16[128,256]{1,0:T(8,128)(2,1)S(1)} %bitcast.8), channel_id=1, source_target_pairs={{0,2},{1,3},{2,0},{3,1},{4,6},{5,7},{6,4},{7,5},{8,10},{9,11},{10,... | collective-permute-start | bytes 196616 | tf_op jit(solution)/shard_map/ppermute | solution.py:18
  4.0 1.3 %fusion = (bf16[1,2,2,256,256]{4,3,2,1,0:T(8,128)(2,1)S(1)}, bf16[1,2,2,256,256]{4,3,2,1,0:T(8,128)(2,1)S(1)}) fusion(bf16[2,2,2,256,256]{4,3,2,1,0:T(8,128)(2,1)} %param.8), kind=kLoop, calls=%fused_computation.2 | loop fusion | bytes 2097152 | tf_op jit(solution)/shard_map/slice | solution.py:174
  5.4 1.3 %collective-permute-done.refs_1_ = bf16[128,256]{1,0:T(8,128)(2,1)S(1)} collective-permute-done((bf16[128,256]{1,0:T(8,128)(2,1)S(1)}, bf16[128,256]{1,0:T(8,128)(2,1)S(1)}, u32[]{:S(2)}, u32[]{:S(2)}) %collective-permute-start) | collective-permute-done | bytes 65568 | tf_op jit(solution)/shard_map/ppermute | solution.py:18
  6.7 1.2 %collective-permute-done.2.refs_3_ = bf16[128,256]{1,0:T(8,128)(2,1)S(1)} collective-permute-done((bf16[128,256]{1,0:T(8,128)(2,1)S(1)}, bf16[128,256]{1,0:T(8,128)(2,1)S(1)}, u32[]{:S(2)}, u32[]{:S(2)}) %collective-permute-start.2) | collective-permute-done | bytes 65568 | tf_op jit(solution)/shard_map/ppermute | solution.py:18
  7.9 1.1 %shard_map.64 = (bf16[2,256,512]{2,1,0:T(8,128)(2,1)S(1)}, bf16[1,256,512]{2,1,0:T(8,128)(2,1)S(1)}, bf16[1,256,512]{2,1,0:T(8,128)(2,1)S(1)}, bf16[1,256,512]{2,1,0:T(8,128)(2,1)S(1)}, bf16[2304,256]{1,0:T(8,128)(2,1)S(1)}) custom-call(s32[2,8,8]{2,1,0:T(8,128)S(1)} %copy-done.1, ...), custom_call_target="tpu_custom_call", output_to_operand_aliasing={{4}: (6, {})} | custom-call | flops 134217728 | bytes 4456448 | tf_op jit(solution)/shard_map/pallas_call | solution.py:51
  9.0 1.8 %collective-permute-start.7 = (bf16[2304,256]{1,0:T(8,128)(2,1)S(1)}, bf16[2304,256]{1,0:T(8,128)(2,1)S(1)}, u32[]{:S(2)}, u32[]{:S(2)}) collective-permute-start(bf16[2304,256]{1,0:T(8,128)(2,1)S(1)} %get-tuple-element.32.refs_3_), channel_id=1, source_target_pairs={{0,2},{1,3},{2,0},{3,1},{4,6},{5,7},{6,4},{7,5},{8,10},{9,11},{10,... | collective-permute-start | bytes 3538952 | tf_op jit(solution)/shard_map/ppermute | solution.py:18
  10.8 2.6 %collective-permute-start.3 = (bf16[2,256,512]{2,1,0:T(8,128)(2,1)S(1)}, bf16[2,256,512]{2,1,0:T(8,128)(2,1)S(1)}, u32[]{:S(2)}, u32[]{:S(2)}) collective-permute-start(bf16[2,256,512]{2,1,0:T(8,128)(2,1)S(1)} %get-tuple-element.28.refs_4_.refs_20_), channel_id=1, source_target_pairs={{0,16},{4,20},{8,24},{12,28},{16,0},{20,4},{24,8},{28,12},{1,17},{... | collective-permute-start | bytes 1572872 | tf_op jit(solution)/shard_map/ppermute | solution.py:18
  13.4 1.5 %collective-permute-start.4 = (bf16[1,256,512]{2,1,0:T(8,128)(2,1)S(1)}, bf16[1,256,512]{2,1,0:T(8,128)(2,1)S(1)}, u32[]{:S(2)}, u32[]{:S(2)}) collective-permute-start(bf16[1,256,512]{2,1,0:T(8,128)(2,1)S(1)} %get-tuple-element.29), channel_id=1, source_target_pairs={{0,4},{4,0},{8,12},{12,8},{16,20},{20,16},{24,28},{28,24},{1,5},{5... | collective-permute-start | bytes 786440 | tf_op jit(solution)/shard_map/ppermute | solution.py:18
  15.0 1.6 %collective-permute-start.5 = (bf16[1,256,512]{2,1,0:T(8,128)(2,1)S(1)}, bf16[1,256,512]{2,1,0:T(8,128)(2,1)S(1)}, u32[]{:S(2)}, u32[]{:S(2)}) collective-permute-start(bf16[1,256,512]{2,1,0:T(8,128)(2,1)S(1)} %get-tuple-element.30), channel_id=1, source_target_pairs={{0,8},{4,12},{8,0},{12,4},{16,24},{20,28},{24,16},{28,20},{1,9},{5... | collective-permute-start | bytes 786440 | tf_op jit(solution)/shard_map/ppermute | solution.py:18
  16.9 4.8 %collective-permute-done.4.refs_0_.refs_5_ = bf16[1,256,512]{2,1,0:T(8,128)(2,1)S(1)} collective-permute-done((bf16[1,256,512]{2,1,0:T(8,128)(2,1)S(1)}, bf16[1,256,512]{2,1,0:T(8,128)(2,1)S(1)}, u32[]{:S(2)}, u32[]{:S(2)}) %collective-permute-start.4) | collective-permute-done | bytes 262176 | tf_op jit(solution)/shard_map/ppermute | solution.py:18
  21.8 9.6 %collective-permute-done.5.refs_1_.refs_6_ = bf16[1,256,512]{2,1,0:T(8,128)(2,1)S(1)} collective-permute-done((bf16[1,256,512]{2,1,0:T(8,128)(2,1)S(1)}, bf16[1,256,512]{2,1,0:T(8,128)(2,1)S(1)}, u32[]{:S(2)}, u32[]{:S(2)}) %collective-permute-start.5) | collective-permute-done | bytes 262176 | tf_op jit(solution)/shard_map/ppermute | solution.py:18
  31.4 6.7 %collective-permute-done.6.refs_2_.refs_7_ = bf16[1,256,512]{2,1,0:T(8,128)(2,1)S(1)} collective-permute-done((bf16[1,256,512]{2,1,0:T(8,128)(2,1)S(1)}, bf16[1,256,512]{2,1,0:T(8,128)(2,1)S(1)}, u32[]{:S(2)}, u32[]{:S(2)}) %collective-permute-start.6) | collective-permute-done | bytes 262176 | tf_op jit(solution)/shard_map/ppermute | solution.py:18
  39.5 1.5 %collective-permute-start.13 = (bf16[1,256,256]{2,1,0:T(8,128)(2,1)S(1)}, bf16[1,256,256]{2,1,0:T(8,128)(2,1)S(1)}, u32[]{:S(2)}, u32[]{:S(2)}) collective-permute-start(bf16[1,256,256]{2,1,0:T(8,128)(2,1)S(1)} %get-tuple-element.38), channel_id=1, source_target_pairs={{0,4},{4,0},{8,12},{12,8},{16,20},{20,16},{24,28},{28,24},{1,5},{5... | collective-permute-start | bytes 393224 | tf_op jit(solution)/shard_map/ppermute | solution.py:18
  41.8 1.2 %collective-permute-start.15 = (bf16[1,256,256]{2,1,0:T(8,128)(2,1)S(1)}, bf16[1,256,256]{2,1,0:T(8,128)(2,1)S(1)}, u32[]{:S(2)}, u32[]{:S(2)}) collective-permute-start(bf16[1,256,256]{2,1,0:T(8,128)(2,1)S(1)} %get-tuple-element.40), channel_id=1, source_target_pairs={{0,12},{4,8},{8,4},{12,0},{16,28},{20,24},{24,20},{28,16},{1,13},{... | collective-permute-start | bytes 393224 | tf_op jit(solution)/shard_map/ppermute | solution.py:18
  43.0 2.0 %collective-permute-done.13.refs_9_ = bf16[1,256,256]{2,1,0:T(8,128)(2,1)S(1)} collective-permute-done((bf16[1,256,256]{2,1,0:T(8,128)(2,1)S(1)}, bf16[1,256,256]{2,1,0:T(8,128)(2,1)S(1)}, u32[]{:S(2)}, u32[]{:S(2)}) %collective-permute-start.13) | collective-permute-done | bytes 131104 | tf_op jit(solution)/shard_map/ppermute | solution.py:18
  45.0 1.5 %collective-permute-start.10 = (bf16[1,256,256]{2,1,0:T(8,128)(2,1)S(1)}, bf16[1,256,256]{2,1,0:T(8,128)(2,1)S(1)}, u32[]{:S(2)}, u32[]{:S(2)}) collective-permute-start(bf16[1,256,256]{2,1,0:T(8,128)(2,1)S(1)} %get-tuple-element.35), channel_id=1, source_target_pairs={{0,4},{4,0},{8,12},{12,8},{16,20},{20,16},{24,28},{28,24},{1,5},{5... | collective-permute-start | bytes 393224 | tf_op jit(solution)/shard_map/ppermute | solution.py:18
  48.2 1.7 %collective-permute-done.15.refs_11_ = bf16[1,256,256]{2,1,0:T(8,128)(2,1)S(1)} collective-permute-done((bf16[1,256,256]{2,1,0:T(8,128)(2,1)S(1)}, bf16[1,256,256]{2,1,0:T(8,128)(2,1)S(1)}, u32[]{:S(2)}, u32[]{:S(2)}) %collective-permute-start.15) | collective-permute-done | bytes 131104 | tf_op jit(solution)/shard_map/ppermute | solution.py:18
  49.9 1.7 %collective-permute-start.12 = (bf16[1,256,256]{2,1,0:T(8,128)(2,1)S(1)}, bf16[1,256,256]{2,1,0:T(8,128)(2,1)S(1)}, u32[]{:S(2)}, u32[]{:S(2)}) collective-permute-start(bf16[1,256,256]{2,1,0:T(8,128)(2,1)S(1)} %get-tuple-element.37), channel_id=1, source_target_pairs={{0,12},{4,8},{8,4},{12,0},{16,28},{20,24},{24,20},{28,16},{1,13},{... | collective-permute-start | bytes 393224 | tf_op jit(solution)/shard_map/ppermute | solution.py:18
  51.6 2.4 %shard_map.66.refs_12_.refs_21_ = bf16[2,256,256]{2,1,0:T(8,128)(2,1)S(1)} custom-call(s32[2,8,8]{2,1,0:T(8,128)S(1)} %copy-done.1, s32[2,2,8]{2,1,0:T(2,128)S(1)} %copy-done.2, s32[2,2]{1,0:T(2,128)S(1)} %copy-done.3, bf16[3,2,256,512]{3,2,1,0:T(8,128)(2,1)S(1)} %copy-done, bf16[2304,256]{1,0:T(8,128)(2,1)S(1)} %get-tuple-element.33.refs_0_, ...), custom_call_target="tpu_custom_call" | custom-call | flops 603979776 | bytes 8781824 | tf_op jit(solution)/shard_map/pallas_call | solution.py:51
  54.0 2.7 %collective-permute-start.23 = (bf16[2,256,256]{2,1,0:T(8,128)(2,1)S(1)}, bf16[2,256,256]{2,1,0:T(8,128)(2,1)S(1)}, u32[]{:S(2)}, u32[]{:S(2)}) collective-permute-start(bf16[2,256,256]{2,1,0:T(8,128)(2,1)S(1)} %shard_map.66.refs_12_.refs_21_), channel_id=1, source_target_pairs={{0,16},{4,20},{8,24},{12,28},{16,0},{20,4},{24,8},{28,12},{1,17},{... | collective-permute-start | bytes 786440 | tf_op jit(solution)/shard_map/ppermute | solution.py:18
  56.7 2.5 %shard_map.67 = (bf16[2,256,256]{2,1,0:T(8,128)(2,1)S(1)}, bf16[2,256,256]{2,1,0:T(8,128)(2,1)S(1)}, bf16[2,256,256]{2,1,0:T(8,128)(2,1)S(1)}, bf16[2,256,256]{2,1,0:T(8,128)(2,1)S(1)}) custom-call(s32[2,8,8]{2,1,0:T(8,128)S(1)} %copy-done.1, s32[2,2,8]{2,1,0:T(2,128)S(1)} %copy-done.2, s32[2,2]{1,0:T(2,128)S(1)} %copy-done.3, ...), custom_call_target="tpu_custom_call" | custom-call | flops 603979776 | bytes 9830400 | tf_op jit(solution)/shard_map/pallas_call | solution.py:51
  59.2 1.7 %collective-permute-start.16 = (bf16[2,256,256]{2,1,0:T(8,128)(2,1)S(1)}, bf16[2,256,256]{2,1,0:T(8,128)(2,1)S(1)}, u32[]{:S(2)}, u32[]{:S(2)}) collective-permute-start(bf16[2,256,256]{2,1,0:T(8,128)(2,1)S(1)} %get-tuple-element.42), channel_id=1, source_target_pairs={{0,4},{4,0},{8,12},{12,8},{16,20},{20,16},{24,28},{28,24},{1,5},{5... | collective-permute-start | bytes 786440 | tf_op jit(solution)/shard_map/ppermute | solution.py:18
  60.8 1.9 %collective-permute-start.19 = (bf16[2,256,256]{2,1,0:T(8,128)(2,1)S(1)}, bf16[2,256,256]{2,1,0:T(8,128)(2,1)S(1)}, u32[]{:S(2)}, u32[]{:S(2)}) collective-permute-start(bf16[2,256,256]{2,1,0:T(8,128)(2,1)S(1)} %get-tuple-element.41.refs_12_.refs_22_), channel_id=1, source_target_pairs={{0,16},{4,20},{8,24},{12,28},{16,0},{20,4},{24,8},{28,12},{1,17},{... | collective-permute-start | bytes 786440 | tf_op jit(solution)/shard_map/ppermute | solution.py:18
  62.7 1.5 %collective-permute-start.17 = (bf16[2,256,256]{2,1,0:T(8,128)(2,1)S(1)}, bf16[2,256,256]{2,1,0:T(8,128)(2,1)S(1)}, u32[]{:S(2)}, u32[]{:S(2)}) collective-permute-start(bf16[2,256,256]{2,1,0:T(8,128)(2,1)S(1)} %get-tuple-element.43), channel_id=1, source_target_pairs={{0,8},{4,12},{8,0},{12,4},{16,24},{20,28},{24,16},{28,20},{1,9},{5... | collective-permute-start | bytes 786440 | tf_op jit(solution)/shard_map/ppermute | solution.py:18
  64.7 9.4 %collective-permute-done.23.far.refs_16_ = bf16[2,256,256]{2,1,0:T(8,128)(2,1)S(1)} collective-permute-done((bf16[2,256,256]{2,1,0:T(8,128)(2,1)S(1)}, bf16[2,256,256]{2,1,0:T(8,128)(2,1)S(1)}, u32[]{:S(2)}, u32[]{:S(2)}) %collective-permute-start.23) | collective-permute-done | bytes 262176 | tf_op jit(solution)/shard_map/ppermute | solution.py:18
  75.5 2.4 %collective-permute-done.19.far.refs_16_ = bf16[2,256,256]{2,1,0:T(8,128)(2,1)S(1)} collective-permute-done((bf16[2,256,256]{2,1,0:T(8,128)(2,1)S(1)}, bf16[2,256,256]{2,1,0:T(8,128)(2,1)S(1)}, u32[]{:S(2)}, u32[]{:S(2)}) %collective-permute-start.19) | collective-permute-done | bytes 262176 | tf_op jit(solution)/shard_map/ppermute | solution.py:18
  79.0 1.8 %collective-permute-done.17.refs_14_ = bf16[2,256,256]{2,1,0:T(8,128)(2,1)S(1)} collective-permute-done((bf16[2,256,256]{2,1,0:T(8,128)(2,1)S(1)}, bf16[2,256,256]{2,1,0:T(8,128)(2,1)S(1)}, u32[]{:S(2)}, u32[]{:S(2)}) %collective-permute-start.17) | collective-permute-done | bytes 262176 | tf_op jit(solution)/shard_map/ppermute | solution.py:18
  81.2 5.1 %collective-permute-done.18.refs_15_ = bf16[2,256,256]{2,1,0:T(8,128)(2,1)S(1)} collective-permute-done((bf16[2,256,256]{2,1,0:T(8,128)(2,1)S(1)}, bf16[2,256,256]{2,1,0:T(8,128)(2,1)S(1)}, u32[]{:S(2)}, u32[]{:S(2)}) %collective-permute-start.18) | collective-permute-done | bytes 262176 | tf_op jit(solution)/shard_map/ppermute | solution.py:18
  86.3 3.1 %collective-permute-start.22 = (bf16[1,256,256]{2,1,0:T(8,128)(2,1)S(1)}, bf16[1,256,256]{2,1,0:T(8,128)(2,1)S(1)}, u32[]{:S(2)}, u32[]{:S(2)}) collective-permute-start(bf16[1,256,256]{2,1,0:T(8,128)(2,1)S(1)} %get-tuple-element.47), channel_id=1, source_target_pairs={{0,12},{4,8},{8,4},{12,0},{16,28},{20,24},{24,20},{28,16},{1,13},{... | collective-permute-start | bytes 393224 | tf_op jit(solution)/shard_map/ppermute | solution.py:18
  89.4 1.3 %collective-permute-done.26.refs_19_ = bf16[1,256,256]{2,1,0:T(8,128)(2,1)S(1)} collective-permute-done((bf16[1,256,256]{2,1,0:T(8,128)(2,1)S(1)}, bf16[1,256,256]{2,1,0:T(8,128)(2,1)S(1)}, u32[]{:S(2)}, u32[]{:S(2)}) %collective-permute-start.26) | collective-permute-done | bytes 131104 | tf_op jit(solution)/shard_map/ppermute | solution.py:18
  90.8 2.5 %shard_map.70.refs_23_ = bf16[2,256,256]{2,1,0:T(8,128)(2,1)S(1)} custom-call(s32[2,8,8]{2,1,0:T(8,128)S(1)} %copy-done.1, s32[2,2,8]{2,1,0:T(2,128)S(1)} %copy-done.2, s32[2,2]{1,0:T(2,128)S(1)} %copy-done.3, bf16[3,2,256,512]{3,2,1,0:T(8,128)(2,1)S(1)} %copy-done, bf16[2304,256]{1,0:T(8,128)(2,1)S(1)} %get-tuple-element.33.refs_0_, ...), custom_call_target="tpu_custom_call" | custom-call | flops 603979776 | bytes 10485760 | tf_op jit(solution)/shard_map/pallas_call | solution.py:51
  93.8 3.2 %shard_map.71 = bf16[3,2,256,512]{3,2,1,0:T(8,128)(2,1)} custom-call(s32[2,8,8]{2,1,0:T(8,128)S(1)} %copy-done.1, s32[2,2,8]{2,1,0:T(2,128)S(1)} %copy-done.2, s32[2,2]{1,0:T(2,128)S(1)} %copy-done.3, bf16[3,2,256,512]{3,2,1,0:T(8,128)(2,1)S(1)} %copy-done, bf16[2304,256]{1,0:T(8,128)(2,1)S(1)} %get-tuple-element.33.refs_0_, ...), custom_call_target="tpu_custom_call" | custom-call | flops 603979776 | bytes 13107200 | tf_op jit(solution)/shard_map/pallas_call | solution.py:51
  (42 shorter events, 9.7 us)
Async XLA Ops:
  0.9 5.8 %collective-permute-start.1 = (bf16[128,256]{1,0:T(8,128)(2,1)S(1)}, bf16[128,256]{1,0:T(8,128)(2,1)S(1)}, u32[]{:S(2)}, u32[]{:S(2)}) collective-permute-start(bf16[128,256]{1,0:T(8,128)(2,1)S(1)} %bitcast.7), channel_id=1, source_target_pairs={{0,1},{1,0},{2,3},{3,2},{4,5},{5,4},{6,7},{7,6},{8,9},{9,8},{10,11... | collective-permute-start | bytes 196616 | tf_op jit(solution)/shard_map/ppermute | solution.py:18
  1.4 5.3 %collective-permute-start = (bf16[128,256]{1,0:T(8,128)(2,1)S(1)}, bf16[128,256]{1,0:T(8,128)(2,1)S(1)}, u32[]{:S(2)}, u32[]{:S(2)}) collective-permute-start(bf16[128,256]{1,0:T(8,128)(2,1)S(1)} %bitcast.8), channel_id=1, source_target_pairs={{0,2},{1,3},{2,0},{3,1},{4,6},{5,7},{6,4},{7,5},{8,10},{9,11},{10,... | collective-permute-start | bytes 196616 | tf_op jit(solution)/shard_map/ppermute | solution.py:18
  5.3 1.4 %copy-start = (bf16[3,2,256,512]{3,2,1,0:T(8,128)(2,1)S(1)}, bf16[3,2,256,512]{3,2,1,0:T(8,128)(2,1)}, u32[]{:S(2)}) copy-start(bf16[3,2,256,512]{3,2,1,0:T(8,128)(2,1)} %noise.7) | copy-start | bytes 4718596
  5.3 2.7 %copy-start.1 = (s32[2,8,8]{2,1,0:T(8,128)S(1)}, s32[2,8,8]{2,1,0:T(8,128)}, u32[]{:S(2)}) copy-start(s32[2,8,8]{2,1,0:T(8,128)} %picks.15) | copy-start | bytes 1540
  6.7 1.3 %collective-permute-start.2 = (bf16[128,256]{1,0:T(8,128)(2,1)S(1)}, bf16[128,256]{1,0:T(8,128)(2,1)S(1)}, u32[]{:S(2)}, u32[]{:S(2)}) collective-permute-start(bf16[128,256]{1,0:T(8,128)(2,1)S(1)} %collective-permute-done.refs_1_), channel_id=1, source_target_pairs={{0,1},{1,0},{2,3},{3,2},{4,5},{5,4},{6,7},{7,6},{8,9},{9,8},{10,11... | collective-permute-start | bytes 196616 | tf_op jit(solution)/shard_map/ppermute | solution.py:18
  9.0 29.1 %collective-permute-start.7 = (bf16[2304,256]{1,0:T(8,128)(2,1)S(1)}, bf16[2304,256]{1,0:T(8,128)(2,1)S(1)}, u32[]{:S(2)}, u32[]{:S(2)}) collective-permute-start(bf16[2304,256]{1,0:T(8,128)(2,1)S(1)} %get-tuple-element.32.refs_3_), channel_id=1, source_target_pairs={{0,2},{1,3},{2,0},{3,1},{4,6},{5,7},{6,4},{7,5},{8,10},{9,11},{10,... | collective-permute-start | bytes 3538952 | tf_op jit(solution)/shard_map/ppermute | solution.py:18
  10.8 27.3 %collective-permute-start.3 = (bf16[2,256,512]{2,1,0:T(8,128)(2,1)S(1)}, bf16[2,256,512]{2,1,0:T(8,128)(2,1)S(1)}, u32[]{:S(2)}, u32[]{:S(2)}) collective-permute-start(bf16[2,256,512]{2,1,0:T(8,128)(2,1)S(1)} %get-tuple-element.28.refs_4_.refs_20_), channel_id=1, source_target_pairs={{0,16},{4,20},{8,24},{12,28},{16,0},{20,4},{24,8},{28,12},{1,17},{... | collective-permute-start | bytes 1572872 | tf_op jit(solution)/shard_map/ppermute | solution.py:18
  13.4 8.3 %collective-permute-start.4 = (bf16[1,256,512]{2,1,0:T(8,128)(2,1)S(1)}, bf16[1,256,512]{2,1,0:T(8,128)(2,1)S(1)}, u32[]{:S(2)}, u32[]{:S(2)}) collective-permute-start(bf16[1,256,512]{2,1,0:T(8,128)(2,1)S(1)} %get-tuple-element.29), channel_id=1, source_target_pairs={{0,4},{4,0},{8,12},{12,8},{16,20},{20,16},{24,28},{28,24},{1,5},{5... | collective-permute-start | bytes 786440 | tf_op jit(solution)/shard_map/ppermute | solution.py:18
  15.0 16.5 %collective-permute-start.5 = (bf16[1,256,512]{2,1,0:T(8,128)(2,1)S(1)}, bf16[1,256,512]{2,1,0:T(8,128)(2,1)S(1)}, u32[]{:S(2)}, u32[]{:S(2)}) collective-permute-start(bf16[1,256,512]{2,1,0:T(8,128)(2,1)S(1)} %get-tuple-element.30), channel_id=1, source_target_pairs={{0,8},{4,12},{8,0},{12,4},{16,24},{20,28},{24,16},{28,20},{1,9},{5... | collective-permute-start | bytes 786440 | tf_op jit(solution)/shard_map/ppermute | solution.py:18
  16.5 35.1 %copy-start.2 = (s32[2,2,8]{2,1,0:T(2,128)S(1)}, s32[2,2,8]{2,1,0:T(2,128)}, u32[]{:S(2)}) copy-start(s32[2,2,8]{2,1,0:T(2,128)} %lists.7) | copy-start | bytes 388
  16.5 35.1 %copy-start.3 = (s32[2,2]{1,0:T(2,128)S(1)}, s32[2,2]{1,0:T(2,128)}, u32[]{:S(2)}) copy-start(s32[2,2]{1,0:T(2,128)} %counts.7) | copy-start | bytes 52
  16.5 21.6 %collective-permute-start.6 = (bf16[1,256,512]{2,1,0:T(8,128)(2,1)S(1)}, bf16[1,256,512]{2,1,0:T(8,128)(2,1)S(1)}, u32[]{:S(2)}, u32[]{:S(2)}) collective-permute-start(bf16[1,256,512]{2,1,0:T(8,128)(2,1)S(1)} %get-tuple-element.31), channel_id=1, source_target_pairs={{0,12},{4,8},{8,4},{12,0},{16,28},{20,24},{24,20},{28,16},{1,13},{... | collective-permute-start | bytes 786440 | tf_op jit(solution)/shard_map/ppermute | solution.py:18
  38.9 12.7 %collective-permute-start.8 = (bf16[2304,256]{1,0:T(8,128)(2,1)S(1)}, bf16[2304,256]{1,0:T(8,128)(2,1)S(1)}, u32[]{:S(2)}, u32[]{:S(2)}) collective-permute-start(bf16[2304,256]{1,0:T(8,128)(2,1)S(1)} %get-tuple-element.33.refs_0_), channel_id=1, source_target_pairs={{0,1},{1,0},{2,3},{3,2},{4,5},{5,4},{6,7},{7,6},{8,9},{9,8},{10,11... | collective-permute-start | bytes 3538952 | tf_op jit(solution)/shard_map/ppermute | solution.py:18
  39.0 12.6 %collective-permute-start.9 = (bf16[2304,256]{1,0:T(8,128)(2,1)S(1)}, bf16[2304,256]{1,0:T(8,128)(2,1)S(1)}, u32[]{:S(2)}, u32[]{:S(2)}) collective-permute-start(bf16[2304,256]{1,0:T(8,128)(2,1)S(1)} %get-tuple-element.34.refs_1_), channel_id=1, source_target_pairs={{0,1},{1,0},{2,3},{3,2},{4,5},{5,4},{6,7},{7,6},{8,9},{9,8},{10,11... | collective-permute-start | bytes 3538952 | tf_op jit(solution)/shard_map/ppermute | solution.py:18
  39.5 5.5 %collective-permute-start.13 = (bf16[1,256,256]{2,1,0:T(8,128)(2,1)S(1)}, bf16[1,256,256]{2,1,0:T(8,128)(2,1)S(1)}, u32[]{:S(2)}, u32[]{:S(2)}) collective-permute-start(bf16[1,256,256]{2,1,0:T(8,128)(2,1)S(1)} %get-tuple-element.38), channel_id=1, source_target_pairs={{0,4},{4,0},{8,12},{12,8},{16,20},{20,16},{24,28},{28,24},{1,5},{5... | collective-permute-start | bytes 393224 | tf_op jit(solution)/shard_map/ppermute | solution.py:18
  41.0 6.4 %collective-permute-start.14 = (bf16[1,256,256]{2,1,0:T(8,128)(2,1)S(1)}, bf16[1,256,256]{2,1,0:T(8,128)(2,1)S(1)}, u32[]{:S(2)}, u32[]{:S(2)}) collective-permute-start(bf16[1,256,256]{2,1,0:T(8,128)(2,1)S(1)} %get-tuple-element.39), channel_id=1, source_target_pairs={{0,8},{4,12},{8,0},{12,4},{16,24},{20,28},{24,16},{28,20},{1,9},{5... | collective-permute-start | bytes 393224 | tf_op jit(solution)/shard_map/ppermute | solution.py:18
  41.8 8.1 %collective-permute-start.15 = (bf16[1,256,256]{2,1,0:T(8,128)(2,1)S(1)}, bf16[1,256,256]{2,1,0:T(8,128)(2,1)S(1)}, u32[]{:S(2)}, u32[]{:S(2)}) collective-permute-start(bf16[1,256,256]{2,1,0:T(8,128)(2,1)S(1)} %get-tuple-element.40), channel_id=1, source_target_pairs={{0,12},{4,8},{8,4},{12,0},{16,28},{20,24},{24,20},{28,16},{1,13},{... | collective-permute-start | bytes 393224 | tf_op jit(solution)/shard_map/ppermute | solution.py:18
  45.0 11.7 %collective-permute-start.10 = (bf16[1,256,256]{2,1,0:T(8,128)(2,1)S(1)}, bf16[1,256,256]{2,1,0:T(8,128)(2,1)S(1)}, u32[]{:S(2)}, u32[]{:S(2)}) collective-permute-start(bf16[1,256,256]{2,1,0:T(8,128)(2,1)S(1)} %get-tuple-element.35), channel_id=1, source_target_pairs={{0,4},{4,0},{8,12},{12,8},{16,20},{20,16},{24,28},{28,24},{1,5},{5... | collective-permute-start | bytes 393224 | tf_op jit(solution)/shard_map/ppermute | solution.py:18
  47.4 9.3 %collective-permute-start.11 = (bf16[1,256,256]{2,1,0:T(8,128)(2,1)S(1)}, bf16[1,256,256]{2,1,0:T(8,128)(2,1)S(1)}, u32[]{:S(2)}, u32[]{:S(2)}) collective-permute-start(bf16[1,256,256]{2,1,0:T(8,128)(2,1)S(1)} %get-tuple-element.36), channel_id=1, source_target_pairs={{0,8},{4,12},{8,0},{12,4},{16,24},{20,28},{24,16},{28,20},{1,9},{5... | collective-permute-start | bytes 393224 | tf_op jit(solution)/shard_map/ppermute | solution.py:18
  49.9 6.8 %collective-permute-start.12 = (bf16[1,256,256]{2,1,0:T(8,128)(2,1)S(1)}, bf16[1,256,256]{2,1,0:T(8,128)(2,1)S(1)}, u32[]{:S(2)}, u32[]{:S(2)}) collective-permute-start(bf16[1,256,256]{2,1,0:T(8,128)(2,1)S(1)} %get-tuple-element.37), channel_id=1, source_target_pairs={{0,12},{4,8},{8,4},{12,0},{16,28},{20,24},{24,20},{28,16},{1,13},{... | collective-permute-start | bytes 393224 | tf_op jit(solution)/shard_map/ppermute | solution.py:18
  54.0 20.0 %collective-permute-start.23 = (bf16[2,256,256]{2,1,0:T(8,128)(2,1)S(1)}, bf16[2,256,256]{2,1,0:T(8,128)(2,1)S(1)}, u32[]{:S(2)}, u32[]{:S(2)}) collective-permute-start(bf16[2,256,256]{2,1,0:T(8,128)(2,1)S(1)} %shard_map.66.refs_12_.refs_21_), channel_id=1, source_target_pairs={{0,16},{4,20},{8,24},{12,28},{16,0},{20,4},{24,8},{28,12},{1,17},{... | collective-permute-start | bytes 786440 | tf_op jit(solution)/shard_map/ppermute | solution.py:18
  59.2 16.3 %collective-permute-start.16 = (bf16[2,256,256]{2,1,0:T(8,128)(2,1)S(1)}, bf16[2,256,256]{2,1,0:T(8,128)(2,1)S(1)}, u32[]{:S(2)}, u32[]{:S(2)}) collective-permute-start(bf16[2,256,256]{2,1,0:T(8,128)(2,1)S(1)} %get-tuple-element.42), channel_id=1, source_target_pairs={{0,4},{4,0},{8,12},{12,8},{16,20},{20,16},{24,28},{28,24},{1,5},{5... | collective-permute-start | bytes 786440 | tf_op jit(solution)/shard_map/ppermute | solution.py:18
  60.8 17.1 %collective-permute-start.19 = (bf16[2,256,256]{2,1,0:T(8,128)(2,1)S(1)}, bf16[2,256,256]{2,1,0:T(8,128)(2,1)S(1)}, u32[]{:S(2)}, u32[]{:S(2)}) collective-permute-start(bf16[2,256,256]{2,1,0:T(8,128)(2,1)S(1)} %get-tuple-element.41.refs_12_.refs_22_), channel_id=1, source_target_pairs={{0,16},{4,20},{8,24},{12,28},{16,0},{20,4},{24,8},{28,12},{1,17},{... | collective-permute-start | bytes 786440 | tf_op jit(solution)/shard_map/ppermute | solution.py:18
  62.7 18.2 %collective-permute-start.17 = (bf16[2,256,256]{2,1,0:T(8,128)(2,1)S(1)}, bf16[2,256,256]{2,1,0:T(8,128)(2,1)S(1)}, u32[]{:S(2)}, u32[]{:S(2)}) collective-permute-start(bf16[2,256,256]{2,1,0:T(8,128)(2,1)S(1)} %get-tuple-element.43), channel_id=1, source_target_pairs={{0,8},{4,12},{8,0},{12,4},{16,24},{20,28},{24,16},{28,20},{1,9},{5... | collective-permute-start | bytes 786440 | tf_op jit(solution)/shard_map/ppermute | solution.py:18
  64.2 22.1 %collective-permute-start.18 = (bf16[2,256,256]{2,1,0:T(8,128)(2,1)S(1)}, bf16[2,256,256]{2,1,0:T(8,128)(2,1)S(1)}, u32[]{:S(2)}, u32[]{:S(2)}) collective-permute-start(bf16[2,256,256]{2,1,0:T(8,128)(2,1)S(1)} %get-tuple-element.44), channel_id=1, source_target_pairs={{0,12},{4,8},{8,4},{12,0},{16,28},{20,24},{24,20},{28,16},{1,13},{... | collective-permute-start | bytes 786440 | tf_op jit(solution)/shard_map/ppermute | solution.py:18
  74.8 11.5 %collective-permute-start.24 = (bf16[1,256,256]{2,1,0:T(8,128)(2,1)S(1)}, bf16[1,256,256]{2,1,0:T(8,128)(2,1)S(1)}, u32[]{:S(2)}, u32[]{:S(2)}) collective-permute-start(bf16[1,256,256]{2,1,0:T(8,128)(2,1)S(1)} %get-tuple-element.48), channel_id=1, source_target_pairs={{0,4},{4,0},{8,12},{12,8},{16,20},{20,16},{24,28},{28,24},{1,5},{5... | collective-permute-start | bytes 393224 | tf_op jit(solution)/shard_map/ppermute | solution.py:18
  75.5 13.9 %collective-permute-start.25 = (bf16[1,256,256]{2,1,0:T(8,128)(2,1)S(1)}, bf16[1,256,256]{2,1,0:T(8,128)(2,1)S(1)}, u32[]{:S(2)}, u32[]{:S(2)}) collective-permute-start(bf16[1,256,256]{2,1,0:T(8,128)(2,1)S(1)} %get-tuple-element.49), channel_id=1, source_target_pairs={{0,8},{4,12},{8,0},{12,4},{16,24},{20,28},{24,16},{28,20},{1,9},{5... | collective-permute-start | bytes 393224 | tf_op jit(solution)/shard_map/ppermute | solution.py:18
  77.9 12.8 %collective-permute-start.26 = (bf16[1,256,256]{2,1,0:T(8,128)(2,1)S(1)}, bf16[1,256,256]{2,1,0:T(8,128)(2,1)S(1)}, u32[]{:S(2)}, u32[]{:S(2)}) collective-permute-start(bf16[1,256,256]{2,1,0:T(8,128)(2,1)S(1)} %get-tuple-element.50), channel_id=1, source_target_pairs={{0,12},{4,8},{8,4},{12,0},{16,28},{20,24},{24,20},{28,16},{1,13},{... | collective-permute-start | bytes 393224 | tf_op jit(solution)/shard_map/ppermute | solution.py:18
  80.8 12.4 %collective-permute-start.20 = (bf16[1,256,256]{2,1,0:T(8,128)(2,1)S(1)}, bf16[1,256,256]{2,1,0:T(8,128)(2,1)S(1)}, u32[]{:S(2)}, u32[]{:S(2)}) collective-permute-start(bf16[1,256,256]{2,1,0:T(8,128)(2,1)S(1)} %get-tuple-element.45), channel_id=1, source_target_pairs={{0,4},{4,0},{8,12},{12,8},{16,20},{20,16},{24,28},{28,24},{1,5},{5... | collective-permute-start | bytes 393224 | tf_op jit(solution)/shard_map/ppermute | solution.py:18
  86.3 7.0 %collective-permute-start.21 = (bf16[1,256,256]{2,1,0:T(8,128)(2,1)S(1)}, bf16[1,256,256]{2,1,0:T(8,128)(2,1)S(1)}, u32[]{:S(2)}, u32[]{:S(2)}) collective-permute-start(bf16[1,256,256]{2,1,0:T(8,128)(2,1)S(1)} %get-tuple-element.46), channel_id=1, source_target_pairs={{0,8},{4,12},{8,0},{12,4},{16,24},{20,28},{24,16},{28,20},{1,9},{5... | collective-permute-start | bytes 393224 | tf_op jit(solution)/shard_map/ppermute | solution.py:18
  86.3 7.5 %collective-permute-start.22 = (bf16[1,256,256]{2,1,0:T(8,128)(2,1)S(1)}, bf16[1,256,256]{2,1,0:T(8,128)(2,1)S(1)}, u32[]{:S(2)}, u32[]{:S(2)}) collective-permute-start(bf16[1,256,256]{2,1,0:T(8,128)(2,1)S(1)} %get-tuple-element.47), channel_id=1, source_target_pairs={{0,12},{4,8},{8,4},{12,0},{16,28},{20,24},{24,20},{28,16},{1,13},{... | collective-permute-start | bytes 393224 | tf_op jit(solution)/shard_map/ppermute | solution.py:18

commit v17 on v14

--- a/solution.py
+++ b/solution.py
@@ -77,23 +77,31 @@
 
 
 def first_kernel(held, picks, noise, *refs):
-    parts, (_, solved, *sends, _, inv) = take(refs, len(held))
+    parts, (_, *solved, inv) = take(refs, len(held))
+    solved, (*sends, _) = take(solved, CHUNKS)
     myself, draw = lax.axis_index("leaf"), lax.axis_index("draw")
-    nodes = noise.shape[0]
+    nodes, wide = noise.shape[0], solved[0].shape[-1]
     draws = sum(map(len, held))
     rows = inv.shape[1] // draws
     fill_inverse(inv, row_blocks(parts, held, nodes * rows), 0, draw)
-    for node in range(nodes):
-        solved[node] = transposed_dot(inv[node], noise[node]).astype(BF16)
+    for at, target in enumerate(solved):
+        for node in range(nodes):
+            right = noise[node, :, at * wide:(at + 1) * wide]
+            target[node] = transposed_dot(inv[node], right).astype(BF16)
     for step, send in enumerate(sends, 1):
-        send[0] = solved[picks[0, myself ^ step, myself]]
-
-
-def relay_kernel(half, source, waits, through, picks, far, *refs):
-    sends = refs[waits + through:][:half - 1]
+        node = picks[0, myself ^ step, myself]
+        for at, target in enumerate(solved):
+            send[at] = target[node]
+
+
+def relay_kernel(half, source, late, waits, through, picks, far, *refs):
+    own, refs = take(refs, bool(late))
+    sends = refs[waits + through:len(refs) - through]
     myself = lax.axis_index("leaf")
     for step, send in enumerate(sends, 1):
         send[0] = far[picks[source, myself ^ step, myself ^ half]]
+        if step >= half - late:
+            send[1] = own[0][picks[source, myself ^ step, myself]]
 
 
 def level_kernel(
@@ -172,29 +180,38 @@
     ])
     values, steps = far_rows(flat(inverse[0]), "draw", draws)
     values, steps = near_rows(values, steps, "draw", draws)
-    solved, *sends, raw = call(
+    late = 1
+    *solved, raw = call(
         functools.partial(first_kernel, steps),
-        [shape(nodes, rows, columns)] + [shape(1, rows, columns)] * (half - 1) + [shape(*raw.shape)],
+        [part] * CHUNKS + [shape(CHUNKS, rows, wide)] * (half - 1 - late) + [shape(*raw.shape)],
         [inv_here],
         (picks,),
         (noise[0], *values, raw),
         flops=nodes * CHUNKS * dot_flops,
-        aliases={2 + len(values): half},
+        aliases={2 + len(values): CHUNKS + half - 1 - late},
     )
-    far, got = leaf(solved, half), near(sends)
+    solved, sends = take(solved, CHUNKS)
+    far, got = [leaf(value, half) for value in solved], near(sends)
     values, steps = far_rows(raw, "draw", draws)
-    sends = call(
-        functools.partial(relay_kernel, half, 0, len(got), len(values)),
-        [shape(1, rows, columns)] * (half - 1) + [shape(*value.shape) for value in values],
-        [],
-        (picks,),
-        (far, *got, *values),
-        aliases={2 + len(got) + at: half - 1 + at for at in range(len(values))},
-    )
-    sends, values = take(sends, half - 1)
-    packs, steps = near_rows(values, steps, "draw", draws)
-    entries = [(solved, 0), *((ref, 0) for ref in got), (far, 0), *((ref, 0) for ref in near(sends))]
-    pieces, done = [[entries] * CHUNKS], [(solved, (0, 0))]
+    pieces, done = [[]], [(value, (0, at * wide)) for at, value in enumerate(solved)]
+    for at in chunks:
+        waits, through = (got, []) if at == 0 else ([], values)
+        sends = call(
+            functools.partial(relay_kernel, half, 0, late, len(waits), len(through)),
+            [shape(1, rows, wide)] * (half - 1 - late) + [shape(2, rows, wide)] * late
+            + [shape(*value.shape) for value in through],
+            [],
+            (picks,),
+            (far[at], solved[at], *waits, *through),
+            aliases={3 + len(waits) + to: half - 1 + to for to in range(len(through))},
+        )
+        sends, through = take(sends, half - 1)
+        distant = near(sends)
+        pieces[0].append([
+            (solved[at], 0), *((ref, at) for ref in got), *((ref, 1) for ref in distant[-late:]),
+            (far[at], 0), *((ref, 0) for ref in distant),
+        ])
+    packs, steps = near_rows(through, steps, "draw", draws)
 
     for level in range(1, levels):
         last_level = level == levels - 1
@@ -234,7 +251,7 @@
         for at in chunks:
             waits = got if at == CHUNKS - 1 else []
             sends = call(
-                functools.partial(relay_kernel, half, level, len(waits), 0),
+                functools.partial(relay_kernel, half, level, 0, len(waits), 0),
                 [shape(1, rows, wide)] * (half - 1),
                 [],
                 (picks,),

time: 101 us -> 117 us (1.16)
  waiting for transfers between devices: 58 us -> 66.8 us
  starting transfers between devices: 26.2 us -> 33 us
    ppermute x24 -> x27, waiting for transfers between devices: 58 us -> 66.8 us  [hop(): return lax.ppermute(value, axis, [(at, at ^ step) for at in range(size)])]
    ppermute x24 -> x27, starting transfers between devices: 26.2 us -> 33 us  [hop(): return lax.ppermute(value, axis, [(at, at ^ step) for at in range(size)])]
    pallas_call x8 -> x9, Pallas kernels: 13.7 us -> 14.4 us  [call(): pl.pallas_call(kernel, out_shape=outs, in_specs=[SMEM] * len(small) + [VM...]
  transfers between devices with their start and end apart: 24 -> 27, of which waited for: 13 -> 15; matrix products, arithmetic and copies ran while one was open for 1% -> 1% of each run, Pallas kernels for 6% -> 8%
where the time goes in v17:
time: 117 us
  waiting for transfers between devices  66.8 us (57%)
  starting transfers between devices  33 us (28%)
  Pallas kernels  14.4 us (12%)
  local copies, waits for them, and re-layouts  2.24 us (2%)
    ppermute x27, waiting for transfers between devices, hop(): return lax.ppermute(value, axis, [(at, at ^ step) for at in range(size)])  66.8 us
    ppermute x27, starting transfers between devices, hop(): return lax.ppermute(value, axis, [(at, at ^ step) for at in range(size)])  33 us
    pallas_call x9, Pallas kernels, call(): pl.pallas_call(kernel, out_shape=outs, in_specs=[SMEM] * len(small) + [VM...  14.4 us
  transfers between devices with their start and end apart: 27, of which 15 were waited for; matrix products, arithmetic and copies ran while one was open for 1% of the time, Pallas kernels for 8%

profile of v17, /device:TPU:0, one launch (start us, length us, event | category | flops | bytes accessed | tf_op | source)
XLA Modules:
  0.0 116.7 jit_solution(11248493897009130998)
XLA Ops:
  1.4 2.6 %collective-permute-start = (bf16[128,256]{1,0:T(8,128)(2,1)S(1)}, bf16[128,256]{1,0:T(8,128)(2,1)S(1)}, u32[]{:S(2)}, u32[]{:S(2)}) collective-permute-start(bf16[128,256]{1,0:T(8,128)(2,1)S(1)} %bitcast.8), channel_id=1, source_target_pairs={{0,2},{1,3},{2,0},{3,1},{4,6},{5,7},{6,4},{7,5},{8,10},{9,11},{10,... | collective-permute-start | bytes 196616 | tf_op jit(solution)/shard_map/ppermute | solution.py:18
  4.0 1.3 %fusion = (bf16[1,2,2,256,256]{4,3,2,1,0:T(8,128)(2,1)S(1)}, bf16[1,2,2,256,256]{4,3,2,1,0:T(8,128)(2,1)S(1)}) fusion(bf16[2,2,2,256,256]{4,3,2,1,0:T(8,128)(2,1)} %param.8), kind=kLoop, calls=%fused_computation.2 | loop fusion | bytes 2097152 | tf_op jit(solution)/shard_map/slice | solution.py:179
  5.4 1.3 %collective-permute-done.refs_1_ = bf16[128,256]{1,0:T(8,128)(2,1)S(1)} collective-permute-done((bf16[128,256]{1,0:T(8,128)(2,1)S(1)}, bf16[128,256]{1,0:T(8,128)(2,1)S(1)}, u32[]{:S(2)}, u32[]{:S(2)}) %collective-permute-start) | collective-permute-done | bytes 65568 | tf_op jit(solution)/shard_map/ppermute | solution.py:18
  9.0 1.8 %collective-permute-start.4 = (bf16[2304,256]{1,0:T(8,128)(2,1)S(1)}, bf16[2304,256]{1,0:T(8,128)(2,1)S(1)}, u32[]{:S(2)}, u32[]{:S(2)}) collective-permute-start(bf16[2304,256]{1,0:T(8,128)(2,1)S(1)} %get-tuple-element.29.refs_1_), channel_id=1, source_target_pairs={{0,2},{1,3},{2,0},{3,1},{4,6},{5,7},{6,4},{7,5},{8,10},{9,11},{10,... | collective-permute-start | bytes 3538952 | tf_op jit(solution)/shard_map/ppermute | solution.py:18
  10.8 2.6 %collective-permute-start.3 = (bf16[2,256,256]{2,1,0:T(8,128)(2,1)S(1)}, bf16[2,256,256]{2,1,0:T(8,128)(2,1)S(1)}, u32[]{:S(2)}, u32[]{:S(2)}) collective-permute-start(bf16[2,256,256]{2,1,0:T(8,128)(2,1)S(1)} %get-tuple-element.28.refs_0_.refs_4_.refs_21_), channel_id=1, source_target_pairs={{0,16},{4,20},{8,24},{12,28},{16,0},{20,4},{24,8},{28,12},{1,17},{... | collective-permute-start | bytes 786440 | tf_op jit(solution)/shard_map/ppermute | solution.py:18
  13.4 12.0 %collective-permute-done.3.far.refs_8_ = bf16[2,256,256]{2,1,0:T(8,128)(2,1)S(1)} collective-permute-done((bf16[2,256,256]{2,1,0:T(8,128)(2,1)S(1)}, bf16[2,256,256]{2,1,0:T(8,128)(2,1)S(1)}, u32[]{:S(2)}, u32[]{:S(2)}) %collective-permute-start.3) | collective-permute-done | bytes 262176 | tf_op jit(solution)/shard_map/ppermute | solution.py:18
  25.4 11.7 %collective-permute-done.4.refs_2_ = bf16[2304,256]{1,0:T(8,128)(2,1)S(1)} collective-permute-done((bf16[2304,256]{1,0:T(8,128)(2,1)S(1)}, bf16[2304,256]{1,0:T(8,128)(2,1)S(1)}, u32[]{:S(2)}, u32[]{:S(2)}) %collective-permute-start.4) | collective-permute-done | bytes 1179680 | tf_op jit(solution)/shard_map/ppermute | solution.py:18
  38.4 1.8 %collective-permute-start.7 = (bf16[2,256,256]{2,1,0:T(8,128)(2,1)S(1)}, bf16[2,256,256]{2,1,0:T(8,128)(2,1)S(1)}, u32[]{:S(2)}, u32[]{:S(2)}) collective-permute-start(bf16[2,256,256]{2,1,0:T(8,128)(2,1)S(1)} %get-tuple-element.32), channel_id=1, source_target_pairs={{0,4},{4,0},{8,12},{12,8},{16,20},{20,16},{24,28},{28,24},{1,5},{5... | collective-permute-start | bytes 786440 | tf_op jit(solution)/shard_map/ppermute | solution.py:18
  40.2 1.6 %collective-permute-start.8 = (bf16[2,256,256]{2,1,0:T(8,128)(2,1)S(1)}, bf16[2,256,256]{2,1,0:T(8,128)(2,1)S(1)}, u32[]{:S(2)}, u32[]{:S(2)}) collective-permute-start(bf16[2,256,256]{2,1,0:T(8,128)(2,1)S(1)} %get-tuple-element.33), channel_id=1, source_target_pairs={{0,8},{4,12},{8,0},{12,4},{16,24},{20,28},{24,16},{28,20},{1,9},{5... | collective-permute-start | bytes 786440 | tf_op jit(solution)/shard_map/ppermute | solution.py:18
  41.8 2.6 %collective-permute-start.12 = (bf16[2,256,256]{2,1,0:T(8,128)(2,1)S(1)}, bf16[2,256,256]{2,1,0:T(8,128)(2,1)S(1)}, u32[]{:S(2)}, u32[]{:S(2)}) collective-permute-start(bf16[2,256,256]{2,1,0:T(8,128)(2,1)S(1)} %get-tuple-element.37.refs_0_.refs_4_.refs_20_), channel_id=1, source_target_pairs={{0,16},{4,20},{8,24},{12,28},{16,0},{20,4},{24,8},{28,12},{1,17},{... | collective-permute-start | bytes 786440 | tf_op jit(solution)/shard_map/ppermute | solution.py:18
  44.4 2.4 %collective-permute-done.7.refs_1_.refs_5_ = bf16[2,256,256]{2,1,0:T(8,128)(2,1)S(1)} collective-permute-done((bf16[2,256,256]{2,1,0:T(8,128)(2,1)S(1)}, bf16[2,256,256]{2,1,0:T(8,128)(2,1)S(1)}, u32[]{:S(2)}, u32[]{:S(2)}) %collective-permute-start.7) | collective-permute-done | bytes 262176 | tf_op jit(solution)/shard_map/ppermute | solution.py:18
  46.7 7.0 %collective-permute-done.8.refs_2_.refs_6_ = bf16[2,256,256]{2,1,0:T(8,128)(2,1)S(1)} collective-permute-done((bf16[2,256,256]{2,1,0:T(8,128)(2,1)S(1)}, bf16[2,256,256]{2,1,0:T(8,128)(2,1)S(1)}, u32[]{:S(2)}, u32[]{:S(2)}) %collective-permute-start.8) | collective-permute-done | bytes 262176 | tf_op jit(solution)/shard_map/ppermute | solution.py:18
  53.7 2.4 %collective-permute-done.12.far.refs_8_ = bf16[2,256,256]{2,1,0:T(8,128)(2,1)S(1)} collective-permute-done((bf16[2,256,256]{2,1,0:T(8,128)(2,1)S(1)}, bf16[2,256,256]{2,1,0:T(8,128)(2,1)S(1)}, u32[]{:S(2)}, u32[]{:S(2)}) %collective-permute-start.12) | collective-permute-done | bytes 262176 | tf_op jit(solution)/shard_map/ppermute | solution.py:18
  57.2 1.5 %collective-permute-start.14 = (bf16[1,256,256]{2,1,0:T(8,128)(2,1)S(1)}, bf16[1,256,256]{2,1,0:T(8,128)(2,1)S(1)}, u32[]{:S(2)}, u32[]{:S(2)}) collective-permute-start(bf16[1,256,256]{2,1,0:T(8,128)(2,1)S(1)} %get-tuple-element.39), channel_id=1, source_target_pairs={{0,4},{4,0},{8,12},{12,8},{16,20},{20,16},{24,28},{28,24},{1,5},{5... | collective-permute-start | bytes 393224 | tf_op jit(solution)/shard_map/ppermute | solution.py:18
  58.8 1.6 %collective-permute-start.15 = (bf16[1,256,256]{2,1,0:T(8,128)(2,1)S(1)}, bf16[1,256,256]{2,1,0:T(8,128)(2,1)S(1)}, u32[]{:S(2)}, u32[]{:S(2)}) collective-permute-start(bf16[1,256,256]{2,1,0:T(8,128)(2,1)S(1)} %get-tuple-element.40), channel_id=1, source_target_pairs={{0,8},{4,12},{8,0},{12,4},{16,24},{20,28},{24,16},{28,20},{1,9},{5... | collective-permute-start | bytes 393224 | tf_op jit(solution)/shard_map/ppermute | solution.py:18
  60.3 5.0 %collective-permute-done.14.refs_9_ = bf16[1,256,256]{2,1,0:T(8,128)(2,1)S(1)} collective-permute-done((bf16[1,256,256]{2,1,0:T(8,128)(2,1)S(1)}, bf16[1,256,256]{2,1,0:T(8,128)(2,1)S(1)}, u32[]{:S(2)}, u32[]{:S(2)}) %collective-permute-start.14) | collective-permute-done | bytes 131104 | tf_op jit(solution)/shard_map/ppermute | solution.py:18
  65.4 1.8 %collective-permute-start.9 = (bf16[2,256,256]{2,1,0:T(8,128)(2,1)S(1)}, bf16[2,256,256]{2,1,0:T(8,128)(2,1)S(1)}, u32[]{:S(2)}, u32[]{:S(2)}) collective-permute-start(bf16[2,256,256]{2,1,0:T(8,128)(2,1)S(1)} %get-tuple-element.34), channel_id=1, source_target_pairs={{0,12},{4,8},{8,4},{12,0},{16,28},{20,24},{24,20},{28,16},{1,13},{... | collective-permute-start | bytes 786440 | tf_op jit(solution)/shard_map/ppermute | solution.py:18
  67.2 1.5 %collective-permute-start.10 = (bf16[1,256,256]{2,1,0:T(8,128)(2,1)S(1)}, bf16[1,256,256]{2,1,0:T(8,128)(2,1)S(1)}, u32[]{:S(2)}, u32[]{:S(2)}) collective-permute-start(bf16[1,256,256]{2,1,0:T(8,128)(2,1)S(1)} %get-tuple-element.35), channel_id=1, source_target_pairs={{0,4},{4,0},{8,12},{12,8},{16,20},{20,16},{24,28},{28,24},{1,5},{5... | collective-permute-start | bytes 393224 | tf_op jit(solution)/shard_map/ppermute | solution.py:18
  68.9 2.4 %shard_map.67.refs_12_.refs_22_ = bf16[2,256,256]{2,1,0:T(8,128)(2,1)S(1)} custom-call(s32[2,8,8]{2,1,0:T(8,128)S(1)} %copy-done.1, s32[2,2,8]{2,1,0:T(2,128)S(1)} %copy-done.2, s32[2,2]{1,0:T(2,128)S(1)} %copy-done.3, bf16[3,2,256,512]{3,2,1,0:T(8,128)(2,1)S(1)} %copy-done, bf16[2304,256]{1,0:T(8,128)(2,1)S(1)} %get-tuple-element.30.refs_0_, ...), custom_call_target="tpu_custom_call" | custom-call | flops 603979776 | bytes 8388608 | tf_op jit(solution)/shard_map/pallas_call | solution.py:51
  71.3 1.8 %collective-permute-start.23 = (bf16[2,256,256]{2,1,0:T(8,128)(2,1)S(1)}, bf16[2,256,256]{2,1,0:T(8,128)(2,1)S(1)}, u32[]{:S(2)}, u32[]{:S(2)}) collective-permute-start(bf16[2,256,256]{2,1,0:T(8,128)(2,1)S(1)} %shard_map.67.refs_12_.refs_22_), channel_id=1, source_target_pairs={{0,16},{4,20},{8,24},{12,28},{16,0},{20,4},{24,8},{28,12},{1,17},{... | collective-permute-start | bytes 786440 | tf_op jit(solution)/shard_map/ppermute | solution.py:18
  73.1 2.7 %collective-permute-done.10.refs_9_ = bf16[1,256,256]{2,1,0:T(8,128)(2,1)S(1)} collective-permute-done((bf16[1,256,256]{2,1,0:T(8,128)(2,1)S(1)}, bf16[1,256,256]{2,1,0:T(8,128)(2,1)S(1)}, u32[]{:S(2)}, u32[]{:S(2)}) %collective-permute-start.10) | collective-permute-done | bytes 131104 | tf_op jit(solution)/shard_map/ppermute | solution.py:18
  75.8 5.2 %collective-permute-done.11.refs_10_ = bf16[1,256,256]{2,1,0:T(8,128)(2,1)S(1)} collective-permute-done((bf16[1,256,256]{2,1,0:T(8,128)(2,1)S(1)}, bf16[1,256,256]{2,1,0:T(8,128)(2,1)S(1)}, u32[]{:S(2)}, u32[]{:S(2)}) %collective-permute-start.11) | collective-permute-done | bytes 131104 | tf_op jit(solution)/shard_map/ppermute | solution.py:18
  81.0 2.4 %shard_map.68 = (bf16[2,256,256]{2,1,0:T(8,128)(2,1)S(1)}, bf16[2,256,256]{2,1,0:T(8,128)(2,1)S(1)}, bf16[2,256,256]{2,1,0:T(8,128)(2,1)S(1)}, bf16[2,256,256]{2,1,0:T(8,128)(2,1)S(1)}) custom-call(s32[2,8,8]{2,1,0:T(8,128)S(1)} %copy-done.1, s32[2,2,8]{2,1,0:T(2,128)S(1)} %copy-done.2, s32[2,2]{1,0:T(2,128)S(1)} %copy-done.3, ...), custom_call_target="tpu_custom_call" | custom-call | flops 603979776 | bytes 9437184 | tf_op jit(solution)/shard_map/pallas_call | solution.py:51
  83.6 3.4 %collective-permute-start.18 = (bf16[2,256,256]{2,1,0:T(8,128)(2,1)S(1)}, bf16[2,256,256]{2,1,0:T(8,128)(2,1)S(1)}, u32[]{:S(2)}, u32[]{:S(2)}) collective-permute-start(bf16[2,256,256]{2,1,0:T(8,128)(2,1)S(1)} %get-tuple-element.44), channel_id=1, source_target_pairs={{0,12},{4,8},{8,4},{12,0},{16,28},{20,24},{24,20},{28,16},{1,13},{... | collective-permute-start | bytes 786440 | tf_op jit(solution)/shard_map/ppermute | solution.py:18
  88.3 2.9 %collective-permute-done.16.refs_0_.refs_13_ = bf16[2,256,256]{2,1,0:T(8,128)(2,1)S(1)} collective-permute-done((bf16[2,256,256]{2,1,0:T(8,128)(2,1)S(1)}, bf16[2,256,256]{2,1,0:T(8,128)(2,1)S(1)}, u32[]{:S(2)}, u32[]{:S(2)}) %collective-permute-start.16) | collective-permute-done | bytes 262176 | tf_op jit(solution)/shard_map/ppermute | solution.py:18
  91.3 2.4 %collective-permute-start.25 = (bf16[1,256,256]{2,1,0:T(8,128)(2,1)S(1)}, bf16[1,256,256]{2,1,0:T(8,128)(2,1)S(1)}, u32[]{:S(2)}, u32[]{:S(2)}) collective-permute-start(bf16[1,256,256]{2,1,0:T(8,128)(2,1)S(1)} %get-tuple-element.49), channel_id=1, source_target_pairs={{0,8},{4,12},{8,0},{12,4},{16,24},{20,28},{24,16},{28,20},{1,9},{5... | collective-permute-start | bytes 393224 | tf_op jit(solution)/shard_map/ppermute | solution.py:18
  93.6 4.8 %collective-permute-done.17.refs_1_.refs_14_ = bf16[2,256,256]{2,1,0:T(8,128)(2,1)S(1)} collective-permute-done((bf16[2,256,256]{2,1,0:T(8,128)(2,1)S(1)}, bf16[2,256,256]{2,1,0:T(8,128)(2,1)S(1)}, u32[]{:S(2)}, u32[]{:S(2)}) %collective-permute-start.17) | collective-permute-done | bytes 262176 | tf_op jit(solution)/shard_map/ppermute | solution.py:18
  98.4 6.0 %collective-permute-done.18.refs_2_.refs_15_ = bf16[2,256,256]{2,1,0:T(8,128)(2,1)S(1)} collective-permute-done((bf16[2,256,256]{2,1,0:T(8,128)(2,1)S(1)}, bf16[2,256,256]{2,1,0:T(8,128)(2,1)S(1)}, u32[]{:S(2)}, u32[]{:S(2)}) %collective-permute-start.18) | collective-permute-done | bytes 262176 | tf_op jit(solution)/shard_map/ppermute | solution.py:18
  106.4 2.3 %collective-permute-start.22 = (bf16[1,256,256]{2,1,0:T(8,128)(2,1)S(1)}, bf16[1,256,256]{2,1,0:T(8,128)(2,1)S(1)}, u32[]{:S(2)}, u32[]{:S(2)}) collective-permute-start(bf16[1,256,256]{2,1,0:T(8,128)(2,1)S(1)} %get-tuple-element.47), channel_id=1, source_target_pairs={{0,12},{4,8},{8,4},{12,0},{16,28},{20,24},{24,20},{28,16},{1,13},{... | collective-permute-start | bytes 393224 | tf_op jit(solution)/shard_map/ppermute | solution.py:18
  108.7 1.4 %collective-permute-done.26.refs_19_ = bf16[1,256,256]{2,1,0:T(8,128)(2,1)S(1)} collective-permute-done((bf16[1,256,256]{2,1,0:T(8,128)(2,1)S(1)}, bf16[1,256,256]{2,1,0:T(8,128)(2,1)S(1)}, u32[]{:S(2)}, u32[]{:S(2)}) %collective-permute-start.26) | collective-permute-done | bytes 131104 | tf_op jit(solution)/shard_map/ppermute | solution.py:18
  110.1 2.5 %shard_map.71.refs_24_ = bf16[2,256,256]{2,1,0:T(8,128)(2,1)S(1)} custom-call(s32[2,8,8]{2,1,0:T(8,128)S(1)} %copy-done.1, s32[2,2,8]{2,1,0:T(2,128)S(1)} %copy-done.2, s32[2,2]{1,0:T(2,128)S(1)} %copy-done.3, bf16[3,2,256,512]{3,2,1,0:T(8,128)(2,1)S(1)} %copy-done, bf16[2304,256]{1,0:T(8,128)(2,1)S(1)} %get-tuple-element.30.refs_0_, ...), custom_call_target="tpu_custom_call" | custom-call | flops 603979776 | bytes 10092544 | tf_op jit(solution)/shard_map/pallas_call | solution.py:51
  113.4 3.2 %shard_map.72 = bf16[3,2,256,512]{3,2,1,0:T(8,128)(2,1)} custom-call(s32[2,8,8]{2,1,0:T(8,128)S(1)} %copy-done.1, s32[2,2,8]{2,1,0:T(2,128)S(1)} %copy-done.2, s32[2,2]{1,0:T(2,128)S(1)} %copy-done.3, bf16[3,2,256,512]{3,2,1,0:T(8,128)(2,1)S(1)} %copy-done, bf16[2304,256]{1,0:T(8,128)(2,1)S(1)} %get-tuple-element.30.refs_0_, ...), custom_call_target="tpu_custom_call" | custom-call | flops 603979776 | bytes 12713984 | tf_op jit(solution)/shard_map/pallas_call | solution.py:51
  (43 shorter events, 10.8 us)
Async XLA Ops:
  0.9 5.8 %collective-permute-start.1 = (bf16[128,256]{1,0:T(8,128)(2,1)S(1)}, bf16[128,256]{1,0:T(8,128)(2,1)S(1)}, u32[]{:S(2)}, u32[]{:S(2)}) collective-permute-start(bf16[128,256]{1,0:T(8,128)(2,1)S(1)} %bitcast.7), channel_id=1, source_target_pairs={{0,1},{1,0},{2,3},{3,2},{4,5},{5,4},{6,7},{7,6},{8,9},{9,8},{10,11... | collective-permute-start | bytes 196616 | tf_op jit(solution)/shard_map/ppermute | solution.py:18
  1.4 5.3 %collective-permute-start = (bf16[128,256]{1,0:T(8,128)(2,1)S(1)}, bf16[128,256]{1,0:T(8,128)(2,1)S(1)}, u32[]{:S(2)}, u32[]{:S(2)}) collective-permute-start(bf16[128,256]{1,0:T(8,128)(2,1)S(1)} %bitcast.8), channel_id=1, source_target_pairs={{0,2},{1,3},{2,0},{3,1},{4,6},{5,7},{6,4},{7,5},{8,10},{9,11},{10,... | collective-permute-start | bytes 196616 | tf_op jit(solution)/shard_map/ppermute | solution.py:18
  5.3 1.4 %copy-start = (bf16[3,2,256,512]{3,2,1,0:T(8,128)(2,1)S(1)}, bf16[3,2,256,512]{3,2,1,0:T(8,128)(2,1)}, u32[]{:S(2)}) copy-start(bf16[3,2,256,512]{3,2,1,0:T(8,128)(2,1)} %noise.7) | copy-start | bytes 4718596
  5.3 2.7 %copy-start.1 = (s32[2,8,8]{2,1,0:T(8,128)S(1)}, s32[2,8,8]{2,1,0:T(8,128)}, u32[]{:S(2)}) copy-start(s32[2,8,8]{2,1,0:T(8,128)} %picks.17) | copy-start | bytes 1540
  6.7 1.3 %collective-permute-start.2 = (bf16[128,256]{1,0:T(8,128)(2,1)S(1)}, bf16[128,256]{1,0:T(8,128)(2,1)S(1)}, u32[]{:S(2)}, u32[]{:S(2)}) collective-permute-start(bf16[128,256]{1,0:T(8,128)(2,1)S(1)} %collective-permute-done.refs_1_), channel_id=1, source_target_pairs={{0,1},{1,0},{2,3},{3,2},{4,5},{5,4},{6,7},{7,6},{8,9},{9,8},{10,11... | collective-permute-start | bytes 196616 | tf_op jit(solution)/shard_map/ppermute | solution.py:18
  9.0 28.1 %collective-permute-start.4 = (bf16[2304,256]{1,0:T(8,128)(2,1)S(1)}, bf16[2304,256]{1,0:T(8,128)(2,1)S(1)}, u32[]{:S(2)}, u32[]{:S(2)}) collective-permute-start(bf16[2304,256]{1,0:T(8,128)(2,1)S(1)} %get-tuple-element.29.refs_1_), channel_id=1, source_target_pairs={{0,2},{1,3},{2,0},{3,1},{4,6},{5,7},{6,4},{7,5},{8,10},{9,11},{10,... | collective-permute-start | bytes 3538952 | tf_op jit(solution)/shard_map/ppermute | solution.py:18
  10.8 58.1 %copy-start.2 = (s32[2,2,8]{2,1,0:T(2,128)S(1)}, s32[2,2,8]{2,1,0:T(2,128)}, u32[]{:S(2)}) copy-start(s32[2,2,8]{2,1,0:T(2,128)} %lists.7) | copy-start | bytes 388
  10.8 58.1 %copy-start.3 = (s32[2,2]{1,0:T(2,128)S(1)}, s32[2,2]{1,0:T(2,128)}, u32[]{:S(2)}) copy-start(s32[2,2]{1,0:T(2,128)} %counts.7) | copy-start | bytes 52
  10.8 14.6 %collective-permute-start.3 = (bf16[2,256,256]{2,1,0:T(8,128)(2,1)S(1)}, bf16[2,256,256]{2,1,0:T(8,128)(2,1)S(1)}, u32[]{:S(2)}, u32[]{:S(2)}) collective-permute-start(bf16[2,256,256]{2,1,0:T(8,128)(2,1)S(1)} %get-tuple-element.28.refs_0_.refs_4_.refs_21_), channel_id=1, source_target_pairs={{0,16},{4,20},{8,24},{12,28},{16,0},{20,4},{24,8},{28,12},{1,17},{... | collective-permute-start | bytes 786440 | tf_op jit(solution)/shard_map/ppermute | solution.py:18
  37.8 31.0 %collective-permute-start.5 = (bf16[2304,256]{1,0:T(8,128)(2,1)S(1)}, bf16[2304,256]{1,0:T(8,128)(2,1)S(1)}, u32[]{:S(2)}, u32[]{:S(2)}) collective-permute-start(bf16[2304,256]{1,0:T(8,128)(2,1)S(1)} %get-tuple-element.30.refs_0_), channel_id=1, source_target_pairs={{0,1},{1,0},{2,3},{3,2},{4,5},{5,4},{6,7},{7,6},{8,9},{9,8},{10,11... | collective-permute-start | bytes 3538952 | tf_op jit(solution)/shard_map/ppermute | solution.py:18
  37.9 31.0 %collective-permute-start.6 = (bf16[2304,256]{1,0:T(8,128)(2,1)S(1)}, bf16[2304,256]{1,0:T(8,128)(2,1)S(1)}, u32[]{:S(2)}, u32[]{:S(2)}) collective-permute-start(bf16[2304,256]{1,0:T(8,128)(2,1)S(1)} %get-tuple-element.31.refs_1_), channel_id=1, source_target_pairs={{0,1},{1,0},{2,3},{3,2},{4,5},{5,4},{6,7},{7,6},{8,9},{9,8},{10,11... | collective-permute-start | bytes 3538952 | tf_op jit(solution)/shard_map/ppermute | solution.py:18
  38.4 8.3 %collective-permute-start.7 = (bf16[2,256,256]{2,1,0:T(8,128)(2,1)S(1)}, bf16[2,256,256]{2,1,0:T(8,128)(2,1)S(1)}, u32[]{:S(2)}, u32[]{:S(2)}) collective-permute-start(bf16[2,256,256]{2,1,0:T(8,128)(2,1)S(1)} %get-tuple-element.32), channel_id=1, source_target_pairs={{0,4},{4,0},{8,12},{12,8},{16,20},{20,16},{24,28},{28,24},{1,5},{5... | collective-permute-start | bytes 786440 | tf_op jit(solution)/shard_map/ppermute | solution.py:18
  40.2 13.5 %collective-permute-start.8 = (bf16[2,256,256]{2,1,0:T(8,128)(2,1)S(1)}, bf16[2,256,256]{2,1,0:T(8,128)(2,1)S(1)}, u32[]{:S(2)}, u32[]{:S(2)}) collective-permute-start(bf16[2,256,256]{2,1,0:T(8,128)(2,1)S(1)} %get-tuple-element.33), channel_id=1, source_target_pairs={{0,8},{4,12},{8,0},{12,4},{16,24},{20,28},{24,16},{28,20},{1,9},{5... | collective-permute-start | bytes 786440 | tf_op jit(solution)/shard_map/ppermute | solution.py:18
  41.8 14.3 %collective-permute-start.12 = (bf16[2,256,256]{2,1,0:T(8,128)(2,1)S(1)}, bf16[2,256,256]{2,1,0:T(8,128)(2,1)S(1)}, u32[]{:S(2)}, u32[]{:S(2)}) collective-permute-start(bf16[2,256,256]{2,1,0:T(8,128)(2,1)S(1)} %get-tuple-element.37.refs_0_.refs_4_.refs_20_), channel_id=1, source_target_pairs={{0,16},{4,20},{8,24},{12,28},{16,0},{20,4},{24,8},{28,12},{1,17},{... | collective-permute-start | bytes 786440 | tf_op jit(solution)/shard_map/ppermute | solution.py:18
  56.8 11.9 %collective-permute-start.13 = (bf16[2,256,256]{2,1,0:T(8,128)(2,1)S(1)}, bf16[2,256,256]{2,1,0:T(8,128)(2,1)S(1)}, u32[]{:S(2)}, u32[]{:S(2)}) collective-permute-start(bf16[2,256,256]{2,1,0:T(8,128)(2,1)S(1)} %get-tuple-element.38), channel_id=1, source_target_pairs={{0,12},{4,8},{8,4},{12,0},{16,28},{20,24},{24,20},{28,16},{1,13},{... | collective-permute-start | bytes 786440 | tf_op jit(solution)/shard_map/ppermute | solution.py:18
  57.2 8.1 %collective-permute-start.14 = (bf16[1,256,256]{2,1,0:T(8,128)(2,1)S(1)}, bf16[1,256,256]{2,1,0:T(8,128)(2,1)S(1)}, u32[]{:S(2)}, u32[]{:S(2)}) collective-permute-start(bf16[1,256,256]{2,1,0:T(8,128)(2,1)S(1)} %get-tuple-element.39), channel_id=1, source_target_pairs={{0,4},{4,0},{8,12},{12,8},{16,20},{20,16},{24,28},{28,24},{1,5},{5... | collective-permute-start | bytes 393224 | tf_op jit(solution)/shard_map/ppermute | solution.py:18
  58.8 8.4 %collective-permute-start.15 = (bf16[1,256,256]{2,1,0:T(8,128)(2,1)S(1)}, bf16[1,256,256]{2,1,0:T(8,128)(2,1)S(1)}, u32[]{:S(2)}, u32[]{:S(2)}) collective-permute-start(bf16[1,256,256]{2,1,0:T(8,128)(2,1)S(1)} %get-tuple-element.40), channel_id=1, source_target_pairs={{0,8},{4,12},{8,0},{12,4},{16,24},{20,28},{24,16},{28,20},{1,9},{5... | collective-permute-start | bytes 393224 | tf_op jit(solution)/shard_map/ppermute | solution.py:18
  65.4 15.6 %collective-permute-start.9 = (bf16[2,256,256]{2,1,0:T(8,128)(2,1)S(1)}, bf16[2,256,256]{2,1,0:T(8,128)(2,1)S(1)}, u32[]{:S(2)}, u32[]{:S(2)}) collective-permute-start(bf16[2,256,256]{2,1,0:T(8,128)(2,1)S(1)} %get-tuple-element.34), channel_id=1, source_target_pairs={{0,12},{4,8},{8,4},{12,0},{16,28},{20,24},{24,20},{28,16},{1,13},{... | collective-permute-start | bytes 786440 | tf_op jit(solution)/shard_map/ppermute | solution.py:18
  67.2 8.6 %collective-permute-start.10 = (bf16[1,256,256]{2,1,0:T(8,128)(2,1)S(1)}, bf16[1,256,256]{2,1,0:T(8,128)(2,1)S(1)}, u32[]{:S(2)}, u32[]{:S(2)}) collective-permute-start(bf16[1,256,256]{2,1,0:T(8,128)(2,1)S(1)} %get-tuple-element.35), channel_id=1, source_target_pairs={{0,4},{4,0},{8,12},{12,8},{16,20},{20,16},{24,28},{28,24},{1,5},{5... | collective-permute-start | bytes 393224 | tf_op jit(solution)/shard_map/ppermute | solution.py:18
  68.7 12.2 %collective-permute-start.11 = (bf16[1,256,256]{2,1,0:T(8,128)(2,1)S(1)}, bf16[1,256,256]{2,1,0:T(8,128)(2,1)S(1)}, u32[]{:S(2)}, u32[]{:S(2)}) collective-permute-start(bf16[1,256,256]{2,1,0:T(8,128)(2,1)S(1)} %get-tuple-element.36), channel_id=1, source_target_pairs={{0,8},{4,12},{8,0},{12,4},{16,24},{20,28},{24,16},{28,20},{1,9},{5... | collective-permute-start | bytes 393224 | tf_op jit(solution)/shard_map/ppermute | solution.py:18
  71.3 15.7 %collective-permute-start.23 = (bf16[2,256,256]{2,1,0:T(8,128)(2,1)S(1)}, bf16[2,256,256]{2,1,0:T(8,128)(2,1)S(1)}, u32[]{:S(2)}, u32[]{:S(2)}) collective-permute-start(bf16[2,256,256]{2,1,0:T(8,128)(2,1)S(1)} %shard_map.67.refs_12_.refs_22_), channel_id=1, source_target_pairs={{0,16},{4,20},{8,24},{12,28},{16,0},{20,4},{24,8},{28,12},{1,17},{... | collective-permute-start | bytes 786440 | tf_op jit(solution)/shard_map/ppermute | solution.py:18
  83.4 7.8 %collective-permute-start.16 = (bf16[2,256,256]{2,1,0:T(8,128)(2,1)S(1)}, bf16[2,256,256]{2,1,0:T(8,128)(2,1)S(1)}, u32[]{:S(2)}, u32[]{:S(2)}) collective-permute-start(bf16[2,256,256]{2,1,0:T(8,128)(2,1)S(1)} %get-tuple-element.42), channel_id=1, source_target_pairs={{0,4},{4,0},{8,12},{12,8},{16,20},{20,16},{24,28},{28,24},{1,5},{5... | collective-permute-start | bytes 786440 | tf_op jit(solution)/shard_map/ppermute | solution.py:18
  83.5 14.9 %collective-permute-start.17 = (bf16[2,256,256]{2,1,0:T(8,128)(2,1)S(1)}, bf16[2,256,256]{2,1,0:T(8,128)(2,1)S(1)}, u32[]{:S(2)}, u32[]{:S(2)}) collective-permute-start(bf16[2,256,256]{2,1,0:T(8,128)(2,1)S(1)} %get-tuple-element.43), channel_id=1, source_target_pairs={{0,8},{4,12},{8,0},{12,4},{16,24},{20,28},{24,16},{28,20},{1,9},{5... | collective-permute-start | bytes 786440 | tf_op jit(solution)/shard_map/ppermute | solution.py:18
  83.6 20.9 %collective-permute-start.18 = (bf16[2,256,256]{2,1,0:T(8,128)(2,1)S(1)}, bf16[2,256,256]{2,1,0:T(8,128)(2,1)S(1)}, u32[]{:S(2)}, u32[]{:S(2)}) collective-permute-start(bf16[2,256,256]{2,1,0:T(8,128)(2,1)S(1)} %get-tuple-element.44), channel_id=1, source_target_pairs={{0,12},{4,8},{8,4},{12,0},{16,28},{20,24},{24,20},{28,16},{1,13},{... | collective-permute-start | bytes 786440 | tf_op jit(solution)/shard_map/ppermute | solution.py:18
  87.0 17.5 %collective-permute-start.19 = (bf16[2,256,256]{2,1,0:T(8,128)(2,1)S(1)}, bf16[2,256,256]{2,1,0:T(8,128)(2,1)S(1)}, u32[]{:S(2)}, u32[]{:S(2)}) collective-permute-start(bf16[2,256,256]{2,1,0:T(8,128)(2,1)S(1)} %get-tuple-element.41.refs_12_.refs_23_), channel_id=1, source_target_pairs={{0,16},{4,20},{8,24},{12,28},{16,0},{20,4},{24,8},{28,12},{1,17},{... | collective-permute-start | bytes 786440 | tf_op jit(solution)/shard_map/ppermute | solution.py:18
  87.7 18.7 %collective-permute-start.24 = (bf16[1,256,256]{2,1,0:T(8,128)(2,1)S(1)}, bf16[1,256,256]{2,1,0:T(8,128)(2,1)S(1)}, u32[]{:S(2)}, u32[]{:S(2)}) collective-permute-start(bf16[1,256,256]{2,1,0:T(8,128)(2,1)S(1)} %get-tuple-element.48), channel_id=1, source_target_pairs={{0,4},{4,0},{8,12},{12,8},{16,20},{20,16},{24,28},{28,24},{1,5},{5... | collective-permute-start | bytes 393224 | tf_op jit(solution)/shard_map/ppermute | solution.py:18
  91.3 17.5 %collective-permute-start.25 = (bf16[1,256,256]{2,1,0:T(8,128)(2,1)S(1)}, bf16[1,256,256]{2,1,0:T(8,128)(2,1)S(1)}, u32[]{:S(2)}, u32[]{:S(2)}) collective-permute-start(bf16[1,256,256]{2,1,0:T(8,128)(2,1)S(1)} %get-tuple-element.49), channel_id=1, source_target_pairs={{0,8},{4,12},{8,0},{12,4},{16,24},{20,28},{24,16},{28,20},{1,9},{5... | collective-permute-start | bytes 393224 | tf_op jit(solution)/shard_map/ppermute | solution.py:18
  98.4 11.6 %collective-permute-start.26 = (bf16[1,256,256]{2,1,0:T(8,128)(2,1)S(1)}, bf16[1,256,256]{2,1,0:T(8,128)(2,1)S(1)}, u32[]{:S(2)}, u32[]{:S(2)}) collective-permute-start(bf16[1,256,256]{2,1,0:T(8,128)(2,1)S(1)} %get-tuple-element.50), channel_id=1, source_target_pairs={{0,12},{4,8},{8,4},{12,0},{16,28},{20,24},{24,20},{28,16},{1,13},{... | collective-permute-start | bytes 393224 | tf_op jit(solution)/shard_map/ppermute | solution.py:18
  105.2 7.4 %collective-permute-start.20 = (bf16[1,256,256]{2,1,0:T(8,128)(2,1)S(1)}, bf16[1,256,256]{2,1,0:T(8,128)(2,1)S(1)}, u32[]{:S(2)}, u32[]{:S(2)}) collective-permute-start(bf16[1,256,256]{2,1,0:T(8,128)(2,1)S(1)} %get-tuple-element.45), channel_id=1, source_target_pairs={{0,4},{4,0},{8,12},{12,8},{16,20},{20,16},{24,28},{28,24},{1,5},{5... | collective-permute-start | bytes 393224 | tf_op jit(solution)/shard_map/ppermute | solution.py:18
  106.4 6.2 %collective-permute-start.21 = (bf16[1,256,256]{2,1,0:T(8,128)(2,1)S(1)}, bf16[1,256,256]{2,1,0:T(8,128)(2,1)S(1)}, u32[]{:S(2)}, u32[]{:S(2)}) collective-permute-start(bf16[1,256,256]{2,1,0:T(8,128)(2,1)S(1)} %get-tuple-element.46), channel_id=1, source_target_pairs={{0,8},{4,12},{8,0},{12,4},{16,24},{20,28},{24,16},{28,20},{1,9},{5... | collective-permute-start | bytes 393224 | tf_op jit(solution)/shard_map/ppermute | solution.py:18
  106.4 7.0 %collective-permute-start.22 = (bf16[1,256,256]{2,1,0:T(8,128)(2,1)S(1)}, bf16[1,256,256]{2,1,0:T(8,128)(2,1)S(1)}, u32[]{:S(2)}, u32[]{:S(2)}) collective-permute-start(bf16[1,256,256]{2,1,0:T(8,128)(2,1)S(1)} %get-tuple-element.47), channel_id=1, source_target_pairs={{0,12},{4,8},{8,4},{12,0},{16,28},{20,24},{24,20},{28,16},{1,13},{... | collective-permute-start | bytes 393224 | tf_op jit(solution)/shard_map/ppermute | solution.py:18

commit v18 on v17

--- a/solution.py
+++ b/solution.py
@@ -191,26 +191,30 @@
         aliases={2 + len(values): CHUNKS + half - 1 - late},
     )
     solved, sends = take(solved, CHUNKS)
-    far, got = [leaf(value, half) for value in solved], near(sends)
+    got = near(sends)
     values, steps = far_rows(raw, "draw", draws)
-    pieces, done = [[]], [(value, (0, at * wide)) for at, value in enumerate(solved)]
+    pieces = [[]]
     for at in chunks:
-        waits, through = (got, []) if at == 0 else ([], values)
+        far, later = leaf(solved[at], half), solved[at + 1:]
+        waits, through = got if at == 0 else [], later or values
         sends = call(
             functools.partial(relay_kernel, half, 0, late, len(waits), len(through)),
             [shape(1, rows, wide)] * (half - 1 - late) + [shape(2, rows, wide)] * late
             + [shape(*value.shape) for value in through],
             [],
             (picks,),
-            (far[at], solved[at], *waits, *through),
+            (far, solved[at], *waits, *through),
             aliases={3 + len(waits) + to: half - 1 + to for to in range(len(through))},
         )
         sends, through = take(sends, half - 1)
         distant = near(sends)
+        if later:
+            solved[at + 1:] = through
         pieces[0].append([
             (solved[at], 0), *((ref, at) for ref in got), *((ref, 1) for ref in distant[-late:]),
-            (far[at], 0), *((ref, 0) for ref in distant),
+            (far, 0), *((ref, 0) for ref in distant),
         ])
+    done = [(value, (0, at * wide)) for at, value in enumerate(solved)]
     packs, steps = near_rows(through, steps, "draw", draws)
 
     for level in range(1, levels):

time: 117 us -> 105 us (0.90)
  waiting for transfers between devices: 66.8 us -> 58.4 us
  starting transfers between devices: 33 us -> 29.6 us
    ppermute x27, waiting for transfers between devices: 66.8 us -> 58.4 us  [hop(): return lax.ppermute(value, axis, [(at, at ^ step) for at in range(size)])]
    ppermute x27, starting transfers between devices: 33 us -> 29.6 us  [hop(): return lax.ppermute(value, axis, [(at, at ^ step) for at in range(size)])]
  transfers between devices with their start and end apart: 27 -> 27, of which waited for: 15 -> 14; matrix products, arithmetic and copies ran while one was open for 1% -> 1% of each run, Pallas kernels for 8% -> 9%
where the time goes in v18:
time: 105 us
  waiting for transfers between devices  58.4 us (56%)
  starting transfers between devices  29.6 us (28%)
  Pallas kernels  14.4 us (14%)
  local copies, waits for them, and re-layouts  2.25 us (2%)
    ppermute x27, waiting for transfers between devices, hop(): return lax.ppermute(value, axis, [(at, at ^ step) for at in range(size)])  58.4 us
    ppermute x27, starting transfers between devices, hop(): return lax.ppermute(value, axis, [(at, at ^ step) for at in range(size)])  29.6 us
    pallas_call x9, Pallas kernels, call(): pl.pallas_call(kernel, out_shape=outs, in_specs=[SMEM] * len(small) + [VM...  14.4 us
  transfers between devices with their start and end apart: 27, of which 14 were waited for; matrix products, arithmetic and copies ran while one was open for 1% of the time, Pallas kernels for 9%

profile of v18, /device:TPU:0, one launch (start us, length us, event | category | flops | bytes accessed | tf_op | source)
XLA Modules:
  0.0 104.9 jit_solution(12640090535120061850)
XLA Ops:
  1.4 2.6 %collective-permute-start = (bf16[128,256]{1,0:T(8,128)(2,1)S(1)}, bf16[128,256]{1,0:T(8,128)(2,1)S(1)}, u32[]{:S(2)}, u32[]{:S(2)}) collective-permute-start(bf16[128,256]{1,0:T(8,128)(2,1)S(1)} %bitcast.8), channel_id=1, source_target_pairs={{0,2},{1,3},{2,0},{3,1},{4,6},{5,7},{6,4},{7,5},{8,10},{9,11},{10,... | collective-permute-start | bytes 196616 | tf_op jit(solution)/shard_map/ppermute | solution.py:18
  4.0 1.3 %fusion = (bf16[1,2,2,256,256]{4,3,2,1,0:T(8,128)(2,1)S(1)}, bf16[1,2,2,256,256]{4,3,2,1,0:T(8,128)(2,1)S(1)}) fusion(bf16[2,2,2,256,256]{4,3,2,1,0:T(8,128)(2,1)} %param.8), kind=kLoop, calls=%fused_computation.2 | loop fusion | bytes 2097152 | tf_op jit(solution)/shard_map/slice | solution.py:179
  5.4 1.3 %collective-permute-done.refs_1_ = bf16[128,256]{1,0:T(8,128)(2,1)S(1)} collective-permute-done((bf16[128,256]{1,0:T(8,128)(2,1)S(1)}, bf16[128,256]{1,0:T(8,128)(2,1)S(1)}, u32[]{:S(2)}, u32[]{:S(2)}) %collective-permute-start) | collective-permute-done | bytes 65568 | tf_op jit(solution)/shard_map/ppermute | solution.py:18
  6.7 1.2 %collective-permute-done.2.refs_3_ = bf16[128,256]{1,0:T(8,128)(2,1)S(1)} collective-permute-done((bf16[128,256]{1,0:T(8,128)(2,1)S(1)}, bf16[128,256]{1,0:T(8,128)(2,1)S(1)}, u32[]{:S(2)}, u32[]{:S(2)}) %collective-permute-start.2) | collective-permute-done | bytes 65568 | tf_op jit(solution)/shard_map/ppermute | solution.py:18
  7.9 1.1 %shard_map.64 = (bf16[2,256,256]{2,1,0:T(8,128)(2,1)S(1)}, bf16[2,256,256]{2,1,0:T(8,128)(2,1)S(1)}, bf16[2,256,256]{2,1,0:T(8,128)(2,1)S(1)}, bf16[2,256,256]{2,1,0:T(8,128)(2,1)S(1)}, bf16[2304,256]{1,0:T(8,128)(2,1)S(1)}) custom-call(s32[2,8,8]{2,1,0:T(8,128)S(1)} %copy-done.1, ...), custom_call_target="tpu_custom_call", output_to_operand_aliasing={{4}: (6, {})} | custom-call | flops 134217728 | bytes 4194304 | tf_op jit(solution)/shard_map/pallas_call | solution.py:51
  9.0 1.8 %collective-permute-start.7 = (bf16[2304,256]{1,0:T(8,128)(2,1)S(1)}, bf16[2304,256]{1,0:T(8,128)(2,1)S(1)}, u32[]{:S(2)}, u32[]{:S(2)}) collective-permute-start(bf16[2304,256]{1,0:T(8,128)(2,1)S(1)} %get-tuple-element.34.refs_1_), channel_id=1, source_target_pairs={{0,2},{1,3},{2,0},{3,1},{4,6},{5,7},{6,4},{7,5},{8,10},{9,11},{10,... | collective-permute-start | bytes 3538952 | tf_op jit(solution)/shard_map/ppermute | solution.py:18
  10.8 1.5 %collective-permute-start.4 = (bf16[2,256,256]{2,1,0:T(8,128)(2,1)S(1)}, bf16[2,256,256]{2,1,0:T(8,128)(2,1)S(1)}, u32[]{:S(2)}, u32[]{:S(2)}) collective-permute-start(bf16[2,256,256]{2,1,0:T(8,128)(2,1)S(1)} %get-tuple-element.30), channel_id=1, source_target_pairs={{0,4},{4,0},{8,12},{12,8},{16,20},{20,16},{24,28},{28,24},{1,5},{5... | collective-permute-start | bytes 786440 | tf_op jit(solution)/shard_map/ppermute | solution.py:18
  12.4 1.6 %collective-permute-start.5 = (bf16[2,256,256]{2,1,0:T(8,128)(2,1)S(1)}, bf16[2,256,256]{2,1,0:T(8,128)(2,1)S(1)}, u32[]{:S(2)}, u32[]{:S(2)}) collective-permute-start(bf16[2,256,256]{2,1,0:T(8,128)(2,1)S(1)} %get-tuple-element.31), channel_id=1, source_target_pairs={{0,8},{4,12},{8,0},{12,4},{16,24},{20,28},{24,16},{28,20},{1,9},{5... | collective-permute-start | bytes 786440 | tf_op jit(solution)/shard_map/ppermute | solution.py:18
  13.9 2.6 %collective-permute-start.3 = (bf16[2,256,256]{2,1,0:T(8,128)(2,1)S(1)}, bf16[2,256,256]{2,1,0:T(8,128)(2,1)S(1)}, u32[]{:S(2)}, u32[]{:S(2)}) collective-permute-start(bf16[2,256,256]{2,1,0:T(8,128)(2,1)S(1)} %get-tuple-element.29.refs_0_.refs_4_.refs_20_), channel_id=1, source_target_pairs={{0,16},{4,20},{8,24},{12,28},{16,0},{20,4},{24,8},{28,12},{1,17},{... | collective-permute-start | bytes 786440 | tf_op jit(solution)/shard_map/ppermute | solution.py:18
  16.5 2.4 %collective-permute-done.4.refs_1_.refs_5_ = bf16[2,256,256]{2,1,0:T(8,128)(2,1)S(1)} collective-permute-done((bf16[2,256,256]{2,1,0:T(8,128)(2,1)S(1)}, bf16[2,256,256]{2,1,0:T(8,128)(2,1)S(1)}, u32[]{:S(2)}, u32[]{:S(2)}) %collective-permute-start.4) | collective-permute-done | bytes 262176 | tf_op jit(solution)/shard_map/ppermute | solution.py:18
  18.9 6.7 %collective-permute-done.5.refs_2_.refs_6_ = bf16[2,256,256]{2,1,0:T(8,128)(2,1)S(1)} collective-permute-done((bf16[2,256,256]{2,1,0:T(8,128)(2,1)S(1)}, bf16[2,256,256]{2,1,0:T(8,128)(2,1)S(1)}, u32[]{:S(2)}, u32[]{:S(2)}) %collective-permute-start.5) | collective-permute-done | bytes 262176 | tf_op jit(solution)/shard_map/ppermute | solution.py:18
  25.7 2.4 %collective-permute-done.3.far.refs_8_ = bf16[2,256,256]{2,1,0:T(8,128)(2,1)S(1)} collective-permute-done((bf16[2,256,256]{2,1,0:T(8,128)(2,1)S(1)}, bf16[2,256,256]{2,1,0:T(8,128)(2,1)S(1)}, u32[]{:S(2)}, u32[]{:S(2)}) %collective-permute-start.3) | collective-permute-done | bytes 262176 | tf_op jit(solution)/shard_map/ppermute | solution.py:18
  29.2 10.7 %collective-permute-done.6.far.refs_8_ = bf16[2,256,256]{2,1,0:T(8,128)(2,1)S(1)} collective-permute-done((bf16[2,256,256]{2,1,0:T(8,128)(2,1)S(1)}, bf16[2,256,256]{2,1,0:T(8,128)(2,1)S(1)}, u32[]{:S(2)}, u32[]{:S(2)}) %collective-permute-start.6) | collective-permute-done | bytes 262176 | tf_op jit(solution)/shard_map/ppermute | solution.py:18
  41.2 1.3 %collective-permute-start.14 = (bf16[1,256,256]{2,1,0:T(8,128)(2,1)S(1)}, bf16[1,256,256]{2,1,0:T(8,128)(2,1)S(1)}, u32[]{:S(2)}, u32[]{:S(2)}) collective-permute-start(bf16[1,256,256]{2,1,0:T(8,128)(2,1)S(1)} %get-tuple-element.41), channel_id=1, source_target_pairs={{0,4},{4,0},{8,12},{12,8},{16,20},{20,16},{24,28},{28,24},{1,5},{5... | collective-permute-start | bytes 393224 | tf_op jit(solution)/shard_map/ppermute | solution.py:18
  42.5 2.2 %collective-permute-start.15 = (bf16[1,256,256]{2,1,0:T(8,128)(2,1)S(1)}, bf16[1,256,256]{2,1,0:T(8,128)(2,1)S(1)}, u32[]{:S(2)}, u32[]{:S(2)}) collective-permute-start(bf16[1,256,256]{2,1,0:T(8,128)(2,1)S(1)} %get-tuple-element.42), channel_id=1, source_target_pairs={{0,8},{4,12},{8,0},{12,4},{16,24},{20,28},{24,16},{28,20},{1,9},{5... | collective-permute-start | bytes 393224 | tf_op jit(solution)/shard_map/ppermute | solution.py:18
  44.7 7.6 %collective-permute-done.14.refs_9_ = bf16[1,256,256]{2,1,0:T(8,128)(2,1)S(1)} collective-permute-done((bf16[1,256,256]{2,1,0:T(8,128)(2,1)S(1)}, bf16[1,256,256]{2,1,0:T(8,128)(2,1)S(1)}, u32[]{:S(2)}, u32[]{:S(2)}) %collective-permute-start.14) | collective-permute-done | bytes 131104 | tf_op jit(solution)/shard_map/ppermute | solution.py:18
  52.3 1.2 %collective-permute-start.10 = (bf16[2,256,256]{2,1,0:T(8,128)(2,1)S(1)}, bf16[2,256,256]{2,1,0:T(8,128)(2,1)S(1)}, u32[]{:S(2)}, u32[]{:S(2)}) collective-permute-start(bf16[2,256,256]{2,1,0:T(8,128)(2,1)S(1)} %get-tuple-element.37), channel_id=1, source_target_pairs={{0,12},{4,8},{8,4},{12,0},{16,28},{20,24},{24,20},{28,16},{1,13},{... | collective-permute-start | bytes 786440 | tf_op jit(solution)/shard_map/ppermute | solution.py:18
  54.5 1.3 %collective-permute-start.12 = (bf16[1,256,256]{2,1,0:T(8,128)(2,1)S(1)}, bf16[1,256,256]{2,1,0:T(8,128)(2,1)S(1)}, u32[]{:S(2)}, u32[]{:S(2)}) collective-permute-start(bf16[1,256,256]{2,1,0:T(8,128)(2,1)S(1)} %get-tuple-element.39), channel_id=1, source_target_pairs={{0,8},{4,12},{8,0},{12,4},{16,24},{20,28},{24,16},{28,20},{1,9},{5... | collective-permute-start | bytes 393224 | tf_op jit(solution)/shard_map/ppermute | solution.py:18
  55.8 2.4 %shard_map.67.refs_12_.refs_22_ = bf16[2,256,256]{2,1,0:T(8,128)(2,1)S(1)} custom-call(s32[2,8,8]{2,1,0:T(8,128)S(1)} %copy-done.1, s32[2,2,8]{2,1,0:T(2,128)S(1)} %copy-done.2, s32[2,2]{1,0:T(2,128)S(1)} %copy-done.3, bf16[3,2,256,512]{3,2,1,0:T(8,128)(2,1)S(1)} %copy-done, bf16[2304,256]{1,0:T(8,128)(2,1)S(1)} %get-tuple-element.35.refs_0_, ...), custom_call_target="tpu_custom_call" | custom-call | flops 603979776 | bytes 8388608 | tf_op jit(solution)/shard_map/pallas_call | solution.py:51
  58.2 1.5 %collective-permute-start.23 = (bf16[2,256,256]{2,1,0:T(8,128)(2,1)S(1)}, bf16[2,256,256]{2,1,0:T(8,128)(2,1)S(1)}, u32[]{:S(2)}, u32[]{:S(2)}) collective-permute-start(bf16[2,256,256]{2,1,0:T(8,128)(2,1)S(1)} %shard_map.67.refs_12_.refs_22_), channel_id=1, source_target_pairs={{0,16},{4,20},{8,24},{12,28},{16,0},{20,4},{24,8},{28,12},{1,17},{... | collective-permute-start | bytes 786440 | tf_op jit(solution)/shard_map/ppermute | solution.py:18
  59.7 3.1 %collective-permute-done.11.refs_9_ = bf16[1,256,256]{2,1,0:T(8,128)(2,1)S(1)} collective-permute-done((bf16[1,256,256]{2,1,0:T(8,128)(2,1)S(1)}, bf16[1,256,256]{2,1,0:T(8,128)(2,1)S(1)}, u32[]{:S(2)}, u32[]{:S(2)}) %collective-permute-start.11) | collective-permute-done | bytes 131104 | tf_op jit(solution)/shard_map/ppermute | solution.py:18
  62.8 5.8 %collective-permute-done.12.refs_10_ = bf16[1,256,256]{2,1,0:T(8,128)(2,1)S(1)} collective-permute-done((bf16[1,256,256]{2,1,0:T(8,128)(2,1)S(1)}, bf16[1,256,256]{2,1,0:T(8,128)(2,1)S(1)}, u32[]{:S(2)}, u32[]{:S(2)}) %collective-permute-start.12) | collective-permute-done | bytes 131104 | tf_op jit(solution)/shard_map/ppermute | solution.py:18
  68.6 2.4 %shard_map.68 = (bf16[2,256,256]{2,1,0:T(8,128)(2,1)S(1)}, bf16[2,256,256]{2,1,0:T(8,128)(2,1)S(1)}, bf16[2,256,256]{2,1,0:T(8,128)(2,1)S(1)}, bf16[2,256,256]{2,1,0:T(8,128)(2,1)S(1)}) custom-call(s32[2,8,8]{2,1,0:T(8,128)S(1)} %copy-done.1, s32[2,2,8]{2,1,0:T(2,128)S(1)} %copy-done.2, s32[2,2]{1,0:T(2,128)S(1)} %copy-done.3, ...), custom_call_target="tpu_custom_call" | custom-call | flops 603979776 | bytes 9437184 | tf_op jit(solution)/shard_map/pallas_call | solution.py:51
  71.2 3.4 %collective-permute-start.18 = (bf16[2,256,256]{2,1,0:T(8,128)(2,1)S(1)}, bf16[2,256,256]{2,1,0:T(8,128)(2,1)S(1)}, u32[]{:S(2)}, u32[]{:S(2)}) collective-permute-start(bf16[2,256,256]{2,1,0:T(8,128)(2,1)S(1)} %get-tuple-element.46), channel_id=1, source_target_pairs={{0,12},{4,8},{8,4},{12,0},{16,28},{20,24},{24,20},{28,16},{1,13},{... | collective-permute-start | bytes 786440 | tf_op jit(solution)/shard_map/ppermute | solution.py:18
  75.9 3.6 %collective-permute-done.16.refs_0_.refs_13_ = bf16[2,256,256]{2,1,0:T(8,128)(2,1)S(1)} collective-permute-done((bf16[2,256,256]{2,1,0:T(8,128)(2,1)S(1)}, bf16[2,256,256]{2,1,0:T(8,128)(2,1)S(1)}, u32[]{:S(2)}, u32[]{:S(2)}) %collective-permute-start.16) | collective-permute-done | bytes 262176 | tf_op jit(solution)/shard_map/ppermute | solution.py:18
  79.5 1.3 %collective-permute-start.25 = (bf16[1,256,256]{2,1,0:T(8,128)(2,1)S(1)}, bf16[1,256,256]{2,1,0:T(8,128)(2,1)S(1)}, u32[]{:S(2)}, u32[]{:S(2)}) collective-permute-start(bf16[1,256,256]{2,1,0:T(8,128)(2,1)S(1)} %get-tuple-element.51), channel_id=1, source_target_pairs={{0,8},{4,12},{8,0},{12,4},{16,24},{20,28},{24,16},{28,20},{1,9},{5... | collective-permute-start | bytes 393224 | tf_op jit(solution)/shard_map/ppermute | solution.py:18
  80.7 5.3 %collective-permute-done.17.refs_1_.refs_14_ = bf16[2,256,256]{2,1,0:T(8,128)(2,1)S(1)} collective-permute-done((bf16[2,256,256]{2,1,0:T(8,128)(2,1)S(1)}, bf16[2,256,256]{2,1,0:T(8,128)(2,1)S(1)}, u32[]{:S(2)}, u32[]{:S(2)}) %collective-permute-start.17) | collective-permute-done | bytes 262176 | tf_op jit(solution)/shard_map/ppermute | solution.py:18
  86.7 6.2 %collective-permute-done.18.refs_2_.refs_15_ = bf16[2,256,256]{2,1,0:T(8,128)(2,1)S(1)} collective-permute-done((bf16[2,256,256]{2,1,0:T(8,128)(2,1)S(1)}, bf16[2,256,256]{2,1,0:T(8,128)(2,1)S(1)}, u32[]{:S(2)}, u32[]{:S(2)}) %collective-permute-start.18) | collective-permute-done | bytes 262176 | tf_op jit(solution)/shard_map/ppermute | solution.py:18
  94.0 3.2 %collective-permute-start.22 = (bf16[1,256,256]{2,1,0:T(8,128)(2,1)S(1)}, bf16[1,256,256]{2,1,0:T(8,128)(2,1)S(1)}, u32[]{:S(2)}, u32[]{:S(2)}) collective-permute-start(bf16[1,256,256]{2,1,0:T(8,128)(2,1)S(1)} %get-tuple-element.49), channel_id=1, source_target_pairs={{0,12},{4,8},{8,4},{12,0},{16,28},{20,24},{24,20},{28,16},{1,13},{... | collective-permute-start | bytes 393224 | tf_op jit(solution)/shard_map/ppermute | solution.py:18
  97.2 1.3 %collective-permute-done.26.refs_19_ = bf16[1,256,256]{2,1,0:T(8,128)(2,1)S(1)} collective-permute-done((bf16[1,256,256]{2,1,0:T(8,128)(2,1)S(1)}, bf16[1,256,256]{2,1,0:T(8,128)(2,1)S(1)}, u32[]{:S(2)}, u32[]{:S(2)}) %collective-permute-start.26) | collective-permute-done | bytes 131104 | tf_op jit(solution)/shard_map/ppermute | solution.py:18
  98.5 2.5 %shard_map.71.refs_24_ = bf16[2,256,256]{2,1,0:T(8,128)(2,1)S(1)} custom-call(s32[2,8,8]{2,1,0:T(8,128)S(1)} %copy-done.1, s32[2,2,8]{2,1,0:T(2,128)S(1)} %copy-done.2, s32[2,2]{1,0:T(2,128)S(1)} %copy-done.3, bf16[3,2,256,512]{3,2,1,0:T(8,128)(2,1)S(1)} %copy-done, bf16[2304,256]{1,0:T(8,128)(2,1)S(1)} %get-tuple-element.35.refs_0_, ...), custom_call_target="tpu_custom_call" | custom-call | flops 603979776 | bytes 10092544 | tf_op jit(solution)/shard_map/pallas_call | solution.py:51
  101.7 3.2 %shard_map.72 = bf16[3,2,256,512]{3,2,1,0:T(8,128)(2,1)} custom-call(s32[2,8,8]{2,1,0:T(8,128)S(1)} %copy-done.1, s32[2,2,8]{2,1,0:T(2,128)S(1)} %copy-done.2, s32[2,2]{1,0:T(2,128)S(1)} %copy-done.3, bf16[3,2,256,512]{3,2,1,0:T(8,128)(2,1)S(1)} %copy-done, bf16[2304,256]{1,0:T(8,128)(2,1)S(1)} %get-tuple-element.35.refs_0_, ...), custom_call_target="tpu_custom_call" | custom-call | flops 603979776 | bytes 12713984 | tf_op jit(solution)/shard_map/pallas_call | solution.py:51
  (43 shorter events, 9.0 us)
Async XLA Ops:
  0.9 5.8 %collective-permute-start.1 = (bf16[128,256]{1,0:T(8,128)(2,1)S(1)}, bf16[128,256]{1,0:T(8,128)(2,1)S(1)}, u32[]{:S(2)}, u32[]{:S(2)}) collective-permute-start(bf16[128,256]{1,0:T(8,128)(2,1)S(1)} %bitcast.7), channel_id=1, source_target_pairs={{0,1},{1,0},{2,3},{3,2},{4,5},{5,4},{6,7},{7,6},{8,9},{9,8},{10,11... | collective-permute-start | bytes 196616 | tf_op jit(solution)/shard_map/ppermute | solution.py:18
  1.4 5.3 %collective-permute-start = (bf16[128,256]{1,0:T(8,128)(2,1)S(1)}, bf16[128,256]{1,0:T(8,128)(2,1)S(1)}, u32[]{:S(2)}, u32[]{:S(2)}) collective-permute-start(bf16[128,256]{1,0:T(8,128)(2,1)S(1)} %bitcast.8), channel_id=1, source_target_pairs={{0,2},{1,3},{2,0},{3,1},{4,6},{5,7},{6,4},{7,5},{8,10},{9,11},{10,... | collective-permute-start | bytes 196616 | tf_op jit(solution)/shard_map/ppermute | solution.py:18
  5.3 1.4 %copy-start = (bf16[3,2,256,512]{3,2,1,0:T(8,128)(2,1)S(1)}, bf16[3,2,256,512]{3,2,1,0:T(8,128)(2,1)}, u32[]{:S(2)}) copy-start(bf16[3,2,256,512]{3,2,1,0:T(8,128)(2,1)} %noise.7) | copy-start | bytes 4718596
  5.3 2.7 %copy-start.1 = (s32[2,8,8]{2,1,0:T(8,128)S(1)}, s32[2,8,8]{2,1,0:T(8,128)}, u32[]{:S(2)}) copy-start(s32[2,8,8]{2,1,0:T(8,128)} %picks.17) | copy-start | bytes 1540
  6.7 1.3 %collective-permute-start.2 = (bf16[128,256]{1,0:T(8,128)(2,1)S(1)}, bf16[128,256]{1,0:T(8,128)(2,1)S(1)}, u32[]{:S(2)}, u32[]{:S(2)}) collective-permute-start(bf16[128,256]{1,0:T(8,128)(2,1)S(1)} %collective-permute-done.refs_1_), channel_id=1, source_target_pairs={{0,1},{1,0},{2,3},{3,2},{4,5},{5,4},{6,7},{7,6},{8,9},{9,8},{10,11... | collective-permute-start | bytes 196616 | tf_op jit(solution)/shard_map/ppermute | solution.py:18
  9.0 30.9 %collective-permute-start.7 = (bf16[2304,256]{1,0:T(8,128)(2,1)S(1)}, bf16[2304,256]{1,0:T(8,128)(2,1)S(1)}, u32[]{:S(2)}, u32[]{:S(2)}) collective-permute-start(bf16[2304,256]{1,0:T(8,128)(2,1)S(1)} %get-tuple-element.34.refs_1_), channel_id=1, source_target_pairs={{0,2},{1,3},{2,0},{3,1},{4,6},{5,7},{6,4},{7,5},{8,10},{9,11},{10,... | collective-permute-start | bytes 3538952 | tf_op jit(solution)/shard_map/ppermute | solution.py:18
  10.8 8.1 %collective-permute-start.4 = (bf16[2,256,256]{2,1,0:T(8,128)(2,1)S(1)}, bf16[2,256,256]{2,1,0:T(8,128)(2,1)S(1)}, u32[]{:S(2)}, u32[]{:S(2)}) collective-permute-start(bf16[2,256,256]{2,1,0:T(8,128)(2,1)S(1)} %get-tuple-element.30), channel_id=1, source_target_pairs={{0,4},{4,0},{8,12},{12,8},{16,20},{20,16},{24,28},{28,24},{1,5},{5... | collective-permute-start | bytes 786440 | tf_op jit(solution)/shard_map/ppermute | solution.py:18
  12.4 13.3 %collective-permute-start.5 = (bf16[2,256,256]{2,1,0:T(8,128)(2,1)S(1)}, bf16[2,256,256]{2,1,0:T(8,128)(2,1)S(1)}, u32[]{:S(2)}, u32[]{:S(2)}) collective-permute-start(bf16[2,256,256]{2,1,0:T(8,128)(2,1)S(1)} %get-tuple-element.31), channel_id=1, source_target_pairs={{0,8},{4,12},{8,0},{12,4},{16,24},{20,28},{24,16},{28,20},{1,9},{5... | collective-permute-start | bytes 786440 | tf_op jit(solution)/shard_map/ppermute | solution.py:18
  13.9 14.1 %collective-permute-start.3 = (bf16[2,256,256]{2,1,0:T(8,128)(2,1)S(1)}, bf16[2,256,256]{2,1,0:T(8,128)(2,1)S(1)}, u32[]{:S(2)}, u32[]{:S(2)}) collective-permute-start(bf16[2,256,256]{2,1,0:T(8,128)(2,1)S(1)} %get-tuple-element.29.refs_0_.refs_4_.refs_20_), channel_id=1, source_target_pairs={{0,16},{4,20},{8,24},{12,28},{16,0},{20,4},{24,8},{28,12},{1,17},{... | collective-permute-start | bytes 786440 | tf_op jit(solution)/shard_map/ppermute | solution.py:18
  28.7 27.1 %copy-start.2 = (s32[2,2,8]{2,1,0:T(2,128)S(1)}, s32[2,2,8]{2,1,0:T(2,128)}, u32[]{:S(2)}) copy-start(s32[2,2,8]{2,1,0:T(2,128)} %lists.7) | copy-start | bytes 388
  28.8 27.1 %copy-start.3 = (s32[2,2]{1,0:T(2,128)S(1)}, s32[2,2]{1,0:T(2,128)}, u32[]{:S(2)}) copy-start(s32[2,2]{1,0:T(2,128)} %counts.7) | copy-start | bytes 52
  28.8 11.1 %collective-permute-start.6 = (bf16[2,256,256]{2,1,0:T(8,128)(2,1)S(1)}, bf16[2,256,256]{2,1,0:T(8,128)(2,1)S(1)}, u32[]{:S(2)}, u32[]{:S(2)}) collective-permute-start(bf16[2,256,256]{2,1,0:T(8,128)(2,1)S(1)} %get-tuple-element.33.refs_0_.refs_4_.refs_21_), channel_id=1, source_target_pairs={{0,16},{4,20},{8,24},{12,28},{16,0},{20,4},{24,8},{28,12},{1,17},{... | collective-permute-start | bytes 786440 | tf_op jit(solution)/shard_map/ppermute | solution.py:18
  40.6 15.2 %collective-permute-start.8 = (bf16[2304,256]{1,0:T(8,128)(2,1)S(1)}, bf16[2304,256]{1,0:T(8,128)(2,1)S(1)}, u32[]{:S(2)}, u32[]{:S(2)}) collective-permute-start(bf16[2304,256]{1,0:T(8,128)(2,1)S(1)} %get-tuple-element.35.refs_0_), channel_id=1, source_target_pairs={{0,1},{1,0},{2,3},{3,2},{4,5},{5,4},{6,7},{7,6},{8,9},{9,8},{10,11... | collective-permute-start | bytes 3538952 | tf_op jit(solution)/shard_map/ppermute | solution.py:18
  40.7 15.1 %collective-permute-start.9 = (bf16[2304,256]{1,0:T(8,128)(2,1)S(1)}, bf16[2304,256]{1,0:T(8,128)(2,1)S(1)}, u32[]{:S(2)}, u32[]{:S(2)}) collective-permute-start(bf16[2304,256]{1,0:T(8,128)(2,1)S(1)} %get-tuple-element.36.refs_1_), channel_id=1, source_target_pairs={{0,1},{1,0},{2,3},{3,2},{4,5},{5,4},{6,7},{7,6},{8,9},{9,8},{10,11... | collective-permute-start | bytes 3538952 | tf_op jit(solution)/shard_map/ppermute | solution.py:18
  41.2 13.3 %collective-permute-start.13 = (bf16[2,256,256]{2,1,0:T(8,128)(2,1)S(1)}, bf16[2,256,256]{2,1,0:T(8,128)(2,1)S(1)}, u32[]{:S(2)}, u32[]{:S(2)}) collective-permute-start(bf16[2,256,256]{2,1,0:T(8,128)(2,1)S(1)} %get-tuple-element.40), channel_id=1, source_target_pairs={{0,12},{4,8},{8,4},{12,0},{16,28},{20,24},{24,20},{28,16},{1,13},{... | collective-permute-start | bytes 786440 | tf_op jit(solution)/shard_map/ppermute | solution.py:18
  41.2 11.1 %collective-permute-start.14 = (bf16[1,256,256]{2,1,0:T(8,128)(2,1)S(1)}, bf16[1,256,256]{2,1,0:T(8,128)(2,1)S(1)}, u32[]{:S(2)}, u32[]{:S(2)}) collective-permute-start(bf16[1,256,256]{2,1,0:T(8,128)(2,1)S(1)} %get-tuple-element.41), channel_id=1, source_target_pairs={{0,4},{4,0},{8,12},{12,8},{16,20},{20,16},{24,28},{28,24},{1,5},{5... | collective-permute-start | bytes 393224 | tf_op jit(solution)/shard_map/ppermute | solution.py:18
  42.5 10.9 %collective-permute-start.15 = (bf16[1,256,256]{2,1,0:T(8,128)(2,1)S(1)}, bf16[1,256,256]{2,1,0:T(8,128)(2,1)S(1)}, u32[]{:S(2)}, u32[]{:S(2)}) collective-permute-start(bf16[1,256,256]{2,1,0:T(8,128)(2,1)S(1)} %get-tuple-element.42), channel_id=1, source_target_pairs={{0,8},{4,12},{8,0},{12,4},{16,24},{20,28},{24,16},{28,20},{1,9},{5... | collective-permute-start | bytes 393224 | tf_op jit(solution)/shard_map/ppermute | solution.py:18
  52.3 16.3 %collective-permute-start.10 = (bf16[2,256,256]{2,1,0:T(8,128)(2,1)S(1)}, bf16[2,256,256]{2,1,0:T(8,128)(2,1)S(1)}, u32[]{:S(2)}, u32[]{:S(2)}) collective-permute-start(bf16[2,256,256]{2,1,0:T(8,128)(2,1)S(1)} %get-tuple-element.37), channel_id=1, source_target_pairs={{0,12},{4,8},{8,4},{12,0},{16,28},{20,24},{24,20},{28,16},{1,13},{... | collective-permute-start | bytes 786440 | tf_op jit(solution)/shard_map/ppermute | solution.py:18
  53.5 9.3 %collective-permute-start.11 = (bf16[1,256,256]{2,1,0:T(8,128)(2,1)S(1)}, bf16[1,256,256]{2,1,0:T(8,128)(2,1)S(1)}, u32[]{:S(2)}, u32[]{:S(2)}) collective-permute-start(bf16[1,256,256]{2,1,0:T(8,128)(2,1)S(1)} %get-tuple-element.38), channel_id=1, source_target_pairs={{0,4},{4,0},{8,12},{12,8},{16,20},{20,16},{24,28},{28,24},{1,5},{5... | collective-permute-start | bytes 393224 | tf_op jit(solution)/shard_map/ppermute | solution.py:18
  54.5 14.1 %collective-permute-start.12 = (bf16[1,256,256]{2,1,0:T(8,128)(2,1)S(1)}, bf16[1,256,256]{2,1,0:T(8,128)(2,1)S(1)}, u32[]{:S(2)}, u32[]{:S(2)}) collective-permute-start(bf16[1,256,256]{2,1,0:T(8,128)(2,1)S(1)} %get-tuple-element.39), channel_id=1, source_target_pairs={{0,8},{4,12},{8,0},{12,4},{16,24},{20,28},{24,16},{28,20},{1,9},{5... | collective-permute-start | bytes 393224 | tf_op jit(solution)/shard_map/ppermute | solution.py:18
  58.2 16.4 %collective-permute-start.23 = (bf16[2,256,256]{2,1,0:T(8,128)(2,1)S(1)}, bf16[2,256,256]{2,1,0:T(8,128)(2,1)S(1)}, u32[]{:S(2)}, u32[]{:S(2)}) collective-permute-start(bf16[2,256,256]{2,1,0:T(8,128)(2,1)S(1)} %shard_map.67.refs_12_.refs_22_), channel_id=1, source_target_pairs={{0,16},{4,20},{8,24},{12,28},{16,0},{20,4},{24,8},{28,12},{1,17},{... | collective-permute-start | bytes 786440 | tf_op jit(solution)/shard_map/ppermute | solution.py:18
  71.0 8.4 %collective-permute-start.16 = (bf16[2,256,256]{2,1,0:T(8,128)(2,1)S(1)}, bf16[2,256,256]{2,1,0:T(8,128)(2,1)S(1)}, u32[]{:S(2)}, u32[]{:S(2)}) collective-permute-start(bf16[2,256,256]{2,1,0:T(8,128)(2,1)S(1)} %get-tuple-element.44), channel_id=1, source_target_pairs={{0,4},{4,0},{8,12},{12,8},{16,20},{20,16},{24,28},{28,24},{1,5},{5... | collective-permute-start | bytes 786440 | tf_op jit(solution)/shard_map/ppermute | solution.py:18
  71.1 14.9 %collective-permute-start.17 = (bf16[2,256,256]{2,1,0:T(8,128)(2,1)S(1)}, bf16[2,256,256]{2,1,0:T(8,128)(2,1)S(1)}, u32[]{:S(2)}, u32[]{:S(2)}) collective-permute-start(bf16[2,256,256]{2,1,0:T(8,128)(2,1)S(1)} %get-tuple-element.45), channel_id=1, source_target_pairs={{0,8},{4,12},{8,0},{12,4},{16,24},{20,28},{24,16},{28,20},{1,9},{5... | collective-permute-start | bytes 786440 | tf_op jit(solution)/shard_map/ppermute | solution.py:18
  71.2 21.7 %collective-permute-start.18 = (bf16[2,256,256]{2,1,0:T(8,128)(2,1)S(1)}, bf16[2,256,256]{2,1,0:T(8,128)(2,1)S(1)}, u32[]{:S(2)}, u32[]{:S(2)}) collective-permute-start(bf16[2,256,256]{2,1,0:T(8,128)(2,1)S(1)} %get-tuple-element.46), channel_id=1, source_target_pairs={{0,12},{4,8},{8,4},{12,0},{16,28},{20,24},{24,20},{28,16},{1,13},{... | collective-permute-start | bytes 786440 | tf_op jit(solution)/shard_map/ppermute | solution.py:18
  74.6 18.3 %collective-permute-start.19 = (bf16[2,256,256]{2,1,0:T(8,128)(2,1)S(1)}, bf16[2,256,256]{2,1,0:T(8,128)(2,1)S(1)}, u32[]{:S(2)}, u32[]{:S(2)}) collective-permute-start(bf16[2,256,256]{2,1,0:T(8,128)(2,1)S(1)} %get-tuple-element.43.refs_12_.refs_23_), channel_id=1, source_target_pairs={{0,16},{4,20},{8,24},{12,28},{16,0},{20,4},{24,8},{28,12},{1,17},{... | collective-permute-start | bytes 786440 | tf_op jit(solution)/shard_map/ppermute | solution.py:18
  75.3 18.7 %collective-permute-start.24 = (bf16[1,256,256]{2,1,0:T(8,128)(2,1)S(1)}, bf16[1,256,256]{2,1,0:T(8,128)(2,1)S(1)}, u32[]{:S(2)}, u32[]{:S(2)}) collective-permute-start(bf16[1,256,256]{2,1,0:T(8,128)(2,1)S(1)} %get-tuple-element.50), channel_id=1, source_target_pairs={{0,4},{4,0},{8,12},{12,8},{16,20},{20,16},{24,28},{28,24},{1,5},{5... | collective-permute-start | bytes 393224 | tf_op jit(solution)/shard_map/ppermute | solution.py:18
  79.5 17.7 %collective-permute-start.25 = (bf16[1,256,256]{2,1,0:T(8,128)(2,1)S(1)}, bf16[1,256,256]{2,1,0:T(8,128)(2,1)S(1)}, u32[]{:S(2)}, u32[]{:S(2)}) collective-permute-start(bf16[1,256,256]{2,1,0:T(8,128)(2,1)S(1)} %get-tuple-element.51), channel_id=1, source_target_pairs={{0,8},{4,12},{8,0},{12,4},{16,24},{20,28},{24,16},{28,20},{1,9},{5... | collective-permute-start | bytes 393224 | tf_op jit(solution)/shard_map/ppermute | solution.py:18
  86.0 12.5 %collective-permute-start.26 = (bf16[1,256,256]{2,1,0:T(8,128)(2,1)S(1)}, bf16[1,256,256]{2,1,0:T(8,128)(2,1)S(1)}, u32[]{:S(2)}, u32[]{:S(2)}) collective-permute-start(bf16[1,256,256]{2,1,0:T(8,128)(2,1)S(1)} %get-tuple-element.52), channel_id=1, source_target_pairs={{0,12},{4,8},{8,4},{12,0},{16,28},{20,24},{24,20},{28,16},{1,13},{... | collective-permute-start | bytes 393224 | tf_op jit(solution)/shard_map/ppermute | solution.py:18
  93.6 7.4 %collective-permute-start.20 = (bf16[1,256,256]{2,1,0:T(8,128)(2,1)S(1)}, bf16[1,256,256]{2,1,0:T(8,128)(2,1)S(1)}, u32[]{:S(2)}, u32[]{:S(2)}) collective-permute-start(bf16[1,256,256]{2,1,0:T(8,128)(2,1)S(1)} %get-tuple-element.47), channel_id=1, source_target_pairs={{0,4},{4,0},{8,12},{12,8},{16,20},{20,16},{24,28},{28,24},{1,5},{5... | collective-permute-start | bytes 393224 | tf_op jit(solution)/shard_map/ppermute | solution.py:18
  94.0 7.0 %collective-permute-start.21 = (bf16[1,256,256]{2,1,0:T(8,128)(2,1)S(1)}, bf16[1,256,256]{2,1,0:T(8,128)(2,1)S(1)}, u32[]{:S(2)}, u32[]{:S(2)}) collective-permute-start(bf16[1,256,256]{2,1,0:T(8,128)(2,1)S(1)} %get-tuple-element.48), channel_id=1, source_target_pairs={{0,8},{4,12},{8,0},{12,4},{16,24},{20,28},{24,16},{28,20},{1,9},{5... | collective-permute-start | bytes 393224 | tf_op jit(solution)/shard_map/ppermute | solution.py:18
  94.0 7.7 %collective-permute-start.22 = (bf16[1,256,256]{2,1,0:T(8,128)(2,1)S(1)}, bf16[1,256,256]{2,1,0:T(8,128)(2,1)S(1)}, u32[]{:S(2)}, u32[]{:S(2)}) collective-permute-start(bf16[1,256,256]{2,1,0:T(8,128)(2,1)S(1)} %get-tuple-element.49), channel_id=1, source_target_pairs={{0,12},{4,8},{8,4},{12,0},{16,28},{20,24},{24,20},{28,16},{1,13},{... | collective-permute-start | bytes 393224 | tf_op jit(solution)/shard_map/ppermute | solution.py:18

commit v19 on v18

--- a/solution.py
+++ b/solution.py
@@ -196,7 +196,7 @@
     pieces = [[]]
     for at in chunks:
         far, later = leaf(solved[at], half), solved[at + 1:]
-        waits, through = got if at == 0 else [], later or values
+        waits, through = distant if at else got, later or values
         sends = call(
             functools.partial(relay_kernel, half, 0, late, len(waits), len(through)),
             [shape(1, rows, wide)] * (half - 1 - late) + [shape(2, rows, wide)] * late

time: 105 us -> 97.3 us (0.927)
  waiting for transfers between devices: 58.4 us -> 48.6 us
  starting transfers between devices: 29.6 us -> 31.6 us
    ppermute x27, waiting for transfers between devices: 58.4 us -> 48.6 us  [hop(): return lax.ppermute(value, axis, [(at, at ^ step) for at in range(size)])]
    ppermute x27, starting transfers between devices: 29.6 us -> 31.6 us  [hop(): return lax.ppermute(value, axis, [(at, at ^ step) for at in range(size)])]
  transfers between devices with their start and end apart: 27 -> 27, of which waited for: 14 -> 16; matrix products, arithmetic and copies ran while one was open for 1% -> 1% of each run, Pallas kernels for 9% -> 10%
where the time goes in v19:
time: 97.3 us; the launch traced here: 97.1 us
  waiting for transfers between devices  48.6 us (50%)
  starting transfers between devices  31.6 us (32%)
  Pallas kernels  14.4 us (15%)
  local copies, waits for them, and re-layouts  2.24 us (2%)
    ppermute x27, waiting for transfers between devices, hop(): return lax.ppermute(value, axis, [(at, at ^ step) for at in range(size)])  48.6 us
    ppermute x27, starting transfers between devices, hop(): return lax.ppermute(value, axis, [(at, at ^ step) for at in range(size)])  31.6 us
    pallas_call x9, Pallas kernels, call(): pl.pallas_call(kernel, out_shape=outs, in_specs=[SMEM] * len(small) + [VM...  14.4 us
  transfers between devices with their start and end apart: 27, of which 16 were waited for; matrix products, arithmetic and copies ran while one was open for 1% of the time, Pallas kernels for 10%

profile of v19, /device:TPU:0, one launch (start us, length us, event | category | flops | bytes accessed | tf_op | source)
XLA Modules:
  0.0 97.1 jit_solution(3412239735269326083)
XLA Ops:
  1.4 2.6 %collective-permute-start = (bf16[128,256]{1,0:T(8,128)(2,1)S(1)}, bf16[128,256]{1,0:T(8,128)(2,1)S(1)}, u32[]{:S(2)}, u32[]{:S(2)}) collective-permute-start(bf16[128,256]{1,0:T(8,128)(2,1)S(1)} %bitcast.8), channel_id=1, source_target_pairs={{0,2},{1,3},{2,0},{3,1},{4,6},{5,7},{6,4},{7,5},{8,10},{9,11},{10,... | collective-permute-start | bytes 196616 | tf_op jit(solution)/shard_map/ppermute | solution.py:18
  4.0 1.3 %fusion = (bf16[1,2,2,256,256]{4,3,2,1,0:T(8,128)(2,1)S(1)}, bf16[1,2,2,256,256]{4,3,2,1,0:T(8,128)(2,1)S(1)}) fusion(bf16[2,2,2,256,256]{4,3,2,1,0:T(8,128)(2,1)} %param.8), kind=kLoop, calls=%fused_computation.2 | loop fusion | bytes 2097152 | tf_op jit(solution)/shard_map/slice | solution.py:179
  5.4 1.3 %collective-permute-done.refs_1_ = bf16[128,256]{1,0:T(8,128)(2,1)S(1)} collective-permute-done((bf16[128,256]{1,0:T(8,128)(2,1)S(1)}, bf16[128,256]{1,0:T(8,128)(2,1)S(1)}, u32[]{:S(2)}, u32[]{:S(2)}) %collective-permute-start) | collective-permute-done | bytes 65568 | tf_op jit(solution)/shard_map/ppermute | solution.py:18
  6.7 1.2 %collective-permute-done.2.refs_3_ = bf16[128,256]{1,0:T(8,128)(2,1)S(1)} collective-permute-done((bf16[128,256]{1,0:T(8,128)(2,1)S(1)}, bf16[128,256]{1,0:T(8,128)(2,1)S(1)}, u32[]{:S(2)}, u32[]{:S(2)}) %collective-permute-start.2) | collective-permute-done | bytes 65568 | tf_op jit(solution)/shard_map/ppermute | solution.py:18
  9.0 1.8 %collective-permute-start.10 = (bf16[2304,256]{1,0:T(8,128)(2,1)S(1)}, bf16[2304,256]{1,0:T(8,128)(2,1)S(1)}, u32[]{:S(2)}, u32[]{:S(2)}) collective-permute-start(bf16[2304,256]{1,0:T(8,128)(2,1)S(1)} %get-tuple-element.37.refs_4_), channel_id=1, source_target_pairs={{0,2},{1,3},{2,0},{3,1},{4,6},{5,7},{6,4},{7,5},{8,10},{9,11},{10,... | collective-permute-start | bytes 3538952 | tf_op jit(solution)/shard_map/ppermute | solution.py:18
  10.8 1.5 %collective-permute-start.4 = (bf16[2,256,256]{2,1,0:T(8,128)(2,1)S(1)}, bf16[2,256,256]{2,1,0:T(8,128)(2,1)S(1)}, u32[]{:S(2)}, u32[]{:S(2)}) collective-permute-start(bf16[2,256,256]{2,1,0:T(8,128)(2,1)S(1)} %get-tuple-element.30), channel_id=1, source_target_pairs={{0,4},{4,0},{8,12},{12,8},{16,20},{20,16},{24,28},{28,24},{1,5},{5... | collective-permute-start | bytes 786440 | tf_op jit(solution)/shard_map/ppermute | solution.py:18
  12.4 1.6 %collective-permute-start.5 = (bf16[2,256,256]{2,1,0:T(8,128)(2,1)S(1)}, bf16[2,256,256]{2,1,0:T(8,128)(2,1)S(1)}, u32[]{:S(2)}, u32[]{:S(2)}) collective-permute-start(bf16[2,256,256]{2,1,0:T(8,128)(2,1)S(1)} %get-tuple-element.31), channel_id=1, source_target_pairs={{0,8},{4,12},{8,0},{12,4},{16,24},{20,28},{24,16},{28,20},{1,9},{5... | collective-permute-start | bytes 786440 | tf_op jit(solution)/shard_map/ppermute | solution.py:18
  13.9 2.6 %collective-permute-start.3 = (bf16[2,256,256]{2,1,0:T(8,128)(2,1)S(1)}, bf16[2,256,256]{2,1,0:T(8,128)(2,1)S(1)}, u32[]{:S(2)}, u32[]{:S(2)}) collective-permute-start(bf16[2,256,256]{2,1,0:T(8,128)(2,1)S(1)} %get-tuple-element.29.refs_0_.refs_4_.refs_20_), channel_id=1, source_target_pairs={{0,16},{4,20},{8,24},{12,28},{16,0},{20,4},{24,8},{28,12},{1,17},{... | collective-permute-start | bytes 786440 | tf_op jit(solution)/shard_map/ppermute | solution.py:18
  16.5 2.4 %collective-permute-done.4.refs_1_.refs_5_ = bf16[2,256,256]{2,1,0:T(8,128)(2,1)S(1)} collective-permute-done((bf16[2,256,256]{2,1,0:T(8,128)(2,1)S(1)}, bf16[2,256,256]{2,1,0:T(8,128)(2,1)S(1)}, u32[]{:S(2)}, u32[]{:S(2)}) %collective-permute-start.4) | collective-permute-done | bytes 262176 | tf_op jit(solution)/shard_map/ppermute | solution.py:18
  18.9 6.7 %collective-permute-done.5.refs_2_.refs_6_ = bf16[2,256,256]{2,1,0:T(8,128)(2,1)S(1)} collective-permute-done((bf16[2,256,256]{2,1,0:T(8,128)(2,1)S(1)}, bf16[2,256,256]{2,1,0:T(8,128)(2,1)S(1)}, u32[]{:S(2)}, u32[]{:S(2)}) %collective-permute-start.5) | collective-permute-done | bytes 262176 | tf_op jit(solution)/shard_map/ppermute | solution.py:18
  25.7 2.4 %collective-permute-done.3.far.refs_8_ = bf16[2,256,256]{2,1,0:T(8,128)(2,1)S(1)} collective-permute-done((bf16[2,256,256]{2,1,0:T(8,128)(2,1)S(1)}, bf16[2,256,256]{2,1,0:T(8,128)(2,1)S(1)}, u32[]{:S(2)}, u32[]{:S(2)}) %collective-permute-start.3) | collective-permute-done | bytes 262176 | tf_op jit(solution)/shard_map/ppermute | solution.py:18
  29.2 2.6 %collective-permute-start.6 = (bf16[2,256,256]{2,1,0:T(8,128)(2,1)S(1)}, bf16[2,256,256]{2,1,0:T(8,128)(2,1)S(1)}, u32[]{:S(2)}, u32[]{:S(2)}) collective-permute-start(bf16[2,256,256]{2,1,0:T(8,128)(2,1)S(1)} %get-tuple-element.33.refs_0_.refs_4_.refs_21_), channel_id=1, source_target_pairs={{0,16},{4,20},{8,24},{12,28},{16,0},{20,4},{24,8},{28,12},{1,17},{... | collective-permute-start | bytes 786440 | tf_op jit(solution)/shard_map/ppermute | solution.py:18
  31.8 1.5 %collective-permute-start.7 = (bf16[1,256,256]{2,1,0:T(8,128)(2,1)S(1)}, bf16[1,256,256]{2,1,0:T(8,128)(2,1)S(1)}, u32[]{:S(2)}, u32[]{:S(2)}) collective-permute-start(bf16[1,256,256]{2,1,0:T(8,128)(2,1)S(1)} %get-tuple-element.34), channel_id=1, source_target_pairs={{0,4},{4,0},{8,12},{12,8},{16,20},{20,16},{24,28},{28,24},{1,5},{5... | collective-permute-start | bytes 393224 | tf_op jit(solution)/shard_map/ppermute | solution.py:18
  33.3 3.9 %collective-permute-done.7.refs_1_.refs_9_ = bf16[1,256,256]{2,1,0:T(8,128)(2,1)S(1)} collective-permute-done((bf16[1,256,256]{2,1,0:T(8,128)(2,1)S(1)}, bf16[1,256,256]{2,1,0:T(8,128)(2,1)S(1)}, u32[]{:S(2)}, u32[]{:S(2)}) %collective-permute-start.7) | collective-permute-done | bytes 131104 | tf_op jit(solution)/shard_map/ppermute | solution.py:18
  37.2 5.6 %collective-permute-done.8.refs_2_.refs_10_ = bf16[1,256,256]{2,1,0:T(8,128)(2,1)S(1)} collective-permute-done((bf16[1,256,256]{2,1,0:T(8,128)(2,1)S(1)}, bf16[1,256,256]{2,1,0:T(8,128)(2,1)S(1)}, u32[]{:S(2)}, u32[]{:S(2)}) %collective-permute-start.8) | collective-permute-done | bytes 131104 | tf_op jit(solution)/shard_map/ppermute | solution.py:18
  44.1 2.7 %collective-permute-start.13 = (bf16[2,256,256]{2,1,0:T(8,128)(2,1)S(1)}, bf16[2,256,256]{2,1,0:T(8,128)(2,1)S(1)}, u32[]{:S(2)}, u32[]{:S(2)}) collective-permute-start(bf16[2,256,256]{2,1,0:T(8,128)(2,1)S(1)} %get-tuple-element.40), channel_id=1, source_target_pairs={{0,12},{4,8},{8,4},{12,0},{16,28},{20,24},{24,20},{28,16},{1,13},{... | collective-permute-start | bytes 786440 | tf_op jit(solution)/shard_map/ppermute | solution.py:18
  48.1 2.4 %shard_map.67.refs_12_.refs_22_ = bf16[2,256,256]{2,1,0:T(8,128)(2,1)S(1)} custom-call(s32[2,8,8]{2,1,0:T(8,128)S(1)} %copy-done.1, s32[2,2,8]{2,1,0:T(2,128)S(1)} %copy-done.2, s32[2,2]{1,0:T(2,128)S(1)} %copy-done.3, bf16[3,2,256,512]{3,2,1,0:T(8,128)(2,1)S(1)} %copy-done, bf16[2304,256]{1,0:T(8,128)(2,1)S(1)} %get-tuple-element.38.refs_0_, ...), custom_call_target="tpu_custom_call" | custom-call | flops 603979776 | bytes 8388608 | tf_op jit(solution)/shard_map/pallas_call | solution.py:51
  50.5 1.6 %collective-permute-start.23 = (bf16[2,256,256]{2,1,0:T(8,128)(2,1)S(1)}, bf16[2,256,256]{2,1,0:T(8,128)(2,1)S(1)}, u32[]{:S(2)}, u32[]{:S(2)}) collective-permute-start(bf16[2,256,256]{2,1,0:T(8,128)(2,1)S(1)} %shard_map.67.refs_12_.refs_22_), channel_id=1, source_target_pairs={{0,16},{4,20},{8,24},{12,28},{16,0},{20,4},{24,8},{28,12},{1,17},{... | collective-permute-start | bytes 786440 | tf_op jit(solution)/shard_map/ppermute | solution.py:18
  52.2 4.0 %collective-permute-done.14.refs_9_ = bf16[1,256,256]{2,1,0:T(8,128)(2,1)S(1)} collective-permute-done((bf16[1,256,256]{2,1,0:T(8,128)(2,1)S(1)}, bf16[1,256,256]{2,1,0:T(8,128)(2,1)S(1)}, u32[]{:S(2)}, u32[]{:S(2)}) %collective-permute-start.14) | collective-permute-done | bytes 131104 | tf_op jit(solution)/shard_map/ppermute | solution.py:18
  56.1 2.4 %collective-permute-done.15.refs_10_ = bf16[1,256,256]{2,1,0:T(8,128)(2,1)S(1)} collective-permute-done((bf16[1,256,256]{2,1,0:T(8,128)(2,1)S(1)}, bf16[1,256,256]{2,1,0:T(8,128)(2,1)S(1)}, u32[]{:S(2)}, u32[]{:S(2)}) %collective-permute-start.15) | collective-permute-done | bytes 131104 | tf_op jit(solution)/shard_map/ppermute | solution.py:18
  58.5 2.4 %shard_map.68 = (bf16[2,256,256]{2,1,0:T(8,128)(2,1)S(1)}, bf16[2,256,256]{2,1,0:T(8,128)(2,1)S(1)}, bf16[2,256,256]{2,1,0:T(8,128)(2,1)S(1)}, bf16[2,256,256]{2,1,0:T(8,128)(2,1)S(1)}) custom-call(s32[2,8,8]{2,1,0:T(8,128)S(1)} %copy-done.1, s32[2,2,8]{2,1,0:T(2,128)S(1)} %copy-done.2, s32[2,2]{1,0:T(2,128)S(1)} %copy-done.3, ...), custom_call_target="tpu_custom_call" | custom-call | flops 603979776 | bytes 9437184 | tf_op jit(solution)/shard_map/pallas_call | solution.py:51
  62.1 2.5 %collective-permute-start.18 = (bf16[2,256,256]{2,1,0:T(8,128)(2,1)S(1)}, bf16[2,256,256]{2,1,0:T(8,128)(2,1)S(1)}, u32[]{:S(2)}, u32[]{:S(2)}) collective-permute-start(bf16[2,256,256]{2,1,0:T(8,128)(2,1)S(1)} %get-tuple-element.46), channel_id=1, source_target_pairs={{0,12},{4,8},{8,4},{12,0},{16,28},{20,24},{24,20},{28,16},{1,13},{... | collective-permute-start | bytes 786440 | tf_op jit(solution)/shard_map/ppermute | solution.py:18
  64.5 1.7 %collective-permute-start.19 = (bf16[2,256,256]{2,1,0:T(8,128)(2,1)S(1)}, bf16[2,256,256]{2,1,0:T(8,128)(2,1)S(1)}, u32[]{:S(2)}, u32[]{:S(2)}) collective-permute-start(bf16[2,256,256]{2,1,0:T(8,128)(2,1)S(1)} %get-tuple-element.43.refs_12_.refs_23_), channel_id=1, source_target_pairs={{0,16},{4,20},{8,24},{12,28},{16,0},{20,4},{24,8},{28,12},{1,17},{... | collective-permute-start | bytes 786440 | tf_op jit(solution)/shard_map/ppermute | solution.py:18
  67.8 1.3 %collective-permute-start.25 = (bf16[1,256,256]{2,1,0:T(8,128)(2,1)S(1)}, bf16[1,256,256]{2,1,0:T(8,128)(2,1)S(1)}, u32[]{:S(2)}, u32[]{:S(2)}) collective-permute-start(bf16[1,256,256]{2,1,0:T(8,128)(2,1)S(1)} %get-tuple-element.51), channel_id=1, source_target_pairs={{0,8},{4,12},{8,0},{12,4},{16,24},{20,28},{24,16},{28,20},{1,9},{5... | collective-permute-start | bytes 393224 | tf_op jit(solution)/shard_map/ppermute | solution.py:18
  69.1 7.7 %collective-permute-done.17.refs_1_.refs_14_ = bf16[2,256,256]{2,1,0:T(8,128)(2,1)S(1)} collective-permute-done((bf16[2,256,256]{2,1,0:T(8,128)(2,1)S(1)}, bf16[2,256,256]{2,1,0:T(8,128)(2,1)S(1)}, u32[]{:S(2)}, u32[]{:S(2)}) %collective-permute-start.17) | collective-permute-done | bytes 262176 | tf_op jit(solution)/shard_map/ppermute | solution.py:18
  76.9 6.1 %collective-permute-done.18.refs_2_.refs_15_ = bf16[2,256,256]{2,1,0:T(8,128)(2,1)S(1)} collective-permute-done((bf16[2,256,256]{2,1,0:T(8,128)(2,1)S(1)}, bf16[2,256,256]{2,1,0:T(8,128)(2,1)S(1)}, u32[]{:S(2)}, u32[]{:S(2)}) %collective-permute-start.18) | collective-permute-done | bytes 262176 | tf_op jit(solution)/shard_map/ppermute | solution.py:18
  84.7 1.3 %collective-permute-start.21 = (bf16[1,256,256]{2,1,0:T(8,128)(2,1)S(1)}, bf16[1,256,256]{2,1,0:T(8,128)(2,1)S(1)}, u32[]{:S(2)}, u32[]{:S(2)}) collective-permute-start(bf16[1,256,256]{2,1,0:T(8,128)(2,1)S(1)} %get-tuple-element.48), channel_id=1, source_target_pairs={{0,8},{4,12},{8,0},{12,4},{16,24},{20,28},{24,16},{28,20},{1,9},{5... | collective-permute-start | bytes 393224 | tf_op jit(solution)/shard_map/ppermute | solution.py:18
  86.0 1.1 %collective-permute-start.22 = (bf16[1,256,256]{2,1,0:T(8,128)(2,1)S(1)}, bf16[1,256,256]{2,1,0:T(8,128)(2,1)S(1)}, u32[]{:S(2)}, u32[]{:S(2)}) collective-permute-start(bf16[1,256,256]{2,1,0:T(8,128)(2,1)S(1)} %get-tuple-element.49), channel_id=1, source_target_pairs={{0,12},{4,8},{8,4},{12,0},{16,28},{20,24},{24,20},{28,16},{1,13},{... | collective-permute-start | bytes 393224 | tf_op jit(solution)/shard_map/ppermute | solution.py:18
  87.2 1.4 %collective-permute-done.26.refs_19_ = bf16[1,256,256]{2,1,0:T(8,128)(2,1)S(1)} collective-permute-done((bf16[1,256,256]{2,1,0:T(8,128)(2,1)S(1)}, bf16[1,256,256]{2,1,0:T(8,128)(2,1)S(1)}, u32[]{:S(2)}, u32[]{:S(2)}) %collective-permute-start.26) | collective-permute-done | bytes 131104 | tf_op jit(solution)/shard_map/ppermute | solution.py:18
  88.6 2.5 %shard_map.71.refs_24_ = bf16[2,256,256]{2,1,0:T(8,128)(2,1)S(1)} custom-call(s32[2,8,8]{2,1,0:T(8,128)S(1)} %copy-done.1, s32[2,2,8]{2,1,0:T(2,128)S(1)} %copy-done.2, s32[2,2]{1,0:T(2,128)S(1)} %copy-done.3, bf16[3,2,256,512]{3,2,1,0:T(8,128)(2,1)S(1)} %copy-done, bf16[2304,256]{1,0:T(8,128)(2,1)S(1)} %get-tuple-element.38.refs_0_, ...), custom_call_target="tpu_custom_call" | custom-call | flops 603979776 | bytes 10092544 | tf_op jit(solution)/shard_map/pallas_call | solution.py:51
  91.5 2.3 %collective-permute-done.22.refs_19_ = bf16[1,256,256]{2,1,0:T(8,128)(2,1)S(1)} collective-permute-done((bf16[1,256,256]{2,1,0:T(8,128)(2,1)S(1)}, bf16[1,256,256]{2,1,0:T(8,128)(2,1)S(1)}, u32[]{:S(2)}, u32[]{:S(2)}) %collective-permute-start.22) | collective-permute-done | bytes 131104 | tf_op jit(solution)/shard_map/ppermute | solution.py:18
  93.8 3.2 %shard_map.72 = bf16[3,2,256,512]{3,2,1,0:T(8,128)(2,1)} custom-call(s32[2,8,8]{2,1,0:T(8,128)S(1)} %copy-done.1, s32[2,2,8]{2,1,0:T(2,128)S(1)} %copy-done.2, s32[2,2]{1,0:T(2,128)S(1)} %copy-done.3, bf16[3,2,256,512]{3,2,1,0:T(8,128)(2,1)S(1)} %copy-done, bf16[2304,256]{1,0:T(8,128)(2,1)S(1)} %get-tuple-element.38.refs_0_, ...), custom_call_target="tpu_custom_call" | custom-call | flops 603979776 | bytes 12713984 | tf_op jit(solution)/shard_map/pallas_call | solution.py:51
  (43 shorter events, 11.4 us)
Async XLA Ops:
  0.9 5.8 %collective-permute-start.1 = (bf16[128,256]{1,0:T(8,128)(2,1)S(1)}, bf16[128,256]{1,0:T(8,128)(2,1)S(1)}, u32[]{:S(2)}, u32[]{:S(2)}) collective-permute-start(bf16[128,256]{1,0:T(8,128)(2,1)S(1)} %bitcast.7), channel_id=1, source_target_pairs={{0,1},{1,0},{2,3},{3,2},{4,5},{5,4},{6,7},{7,6},{8,9},{9,8},{10,11... | collective-permute-start | bytes 196616 | tf_op jit(solution)/shard_map/ppermute | solution.py:18
  1.4 5.3 %collective-permute-start = (bf16[128,256]{1,0:T(8,128)(2,1)S(1)}, bf16[128,256]{1,0:T(8,128)(2,1)S(1)}, u32[]{:S(2)}, u32[]{:S(2)}) collective-permute-start(bf16[128,256]{1,0:T(8,128)(2,1)S(1)} %bitcast.8), channel_id=1, source_target_pairs={{0,2},{1,3},{2,0},{3,1},{4,6},{5,7},{6,4},{7,5},{8,10},{9,11},{10,... | collective-permute-start | bytes 196616 | tf_op jit(solution)/shard_map/ppermute | solution.py:18
  5.3 1.4 %copy-start = (bf16[3,2,256,512]{3,2,1,0:T(8,128)(2,1)S(1)}, bf16[3,2,256,512]{3,2,1,0:T(8,128)(2,1)}, u32[]{:S(2)}) copy-start(bf16[3,2,256,512]{3,2,1,0:T(8,128)(2,1)} %noise.7) | copy-start | bytes 4718596
  5.3 2.7 %copy-start.1 = (s32[2,8,8]{2,1,0:T(8,128)S(1)}, s32[2,8,8]{2,1,0:T(8,128)}, u32[]{:S(2)}) copy-start(s32[2,8,8]{2,1,0:T(8,128)} %picks.17) | copy-start | bytes 1540
  6.7 1.3 %collective-permute-start.2 = (bf16[128,256]{1,0:T(8,128)(2,1)S(1)}, bf16[128,256]{1,0:T(8,128)(2,1)S(1)}, u32[]{:S(2)}, u32[]{:S(2)}) collective-permute-start(bf16[128,256]{1,0:T(8,128)(2,1)S(1)} %collective-permute-done.refs_1_), channel_id=1, source_target_pairs={{0,1},{1,0},{2,3},{3,2},{4,5},{5,4},{6,7},{7,6},{8,9},{9,8},{10,11... | collective-permute-start | bytes 196616 | tf_op jit(solution)/shard_map/ppermute | solution.py:18
  9.0 33.8 %collective-permute-start.10 = (bf16[2304,256]{1,0:T(8,128)(2,1)S(1)}, bf16[2304,256]{1,0:T(8,128)(2,1)S(1)}, u32[]{:S(2)}, u32[]{:S(2)}) collective-permute-start(bf16[2304,256]{1,0:T(8,128)(2,1)S(1)} %get-tuple-element.37.refs_4_), channel_id=1, source_target_pairs={{0,2},{1,3},{2,0},{3,1},{4,6},{5,7},{6,4},{7,5},{8,10},{9,11},{10,... | collective-permute-start | bytes 3538952 | tf_op jit(solution)/shard_map/ppermute | solution.py:18
  10.8 8.1 %collective-permute-start.4 = (bf16[2,256,256]{2,1,0:T(8,128)(2,1)S(1)}, bf16[2,256,256]{2,1,0:T(8,128)(2,1)S(1)}, u32[]{:S(2)}, u32[]{:S(2)}) collective-permute-start(bf16[2,256,256]{2,1,0:T(8,128)(2,1)S(1)} %get-tuple-element.30), channel_id=1, source_target_pairs={{0,4},{4,0},{8,12},{12,8},{16,20},{20,16},{24,28},{28,24},{1,5},{5... | collective-permute-start | bytes 786440 | tf_op jit(solution)/shard_map/ppermute | solution.py:18
  12.4 13.3 %collective-permute-start.5 = (bf16[2,256,256]{2,1,0:T(8,128)(2,1)S(1)}, bf16[2,256,256]{2,1,0:T(8,128)(2,1)S(1)}, u32[]{:S(2)}, u32[]{:S(2)}) collective-permute-start(bf16[2,256,256]{2,1,0:T(8,128)(2,1)S(1)} %get-tuple-element.31), channel_id=1, source_target_pairs={{0,8},{4,12},{8,0},{12,4},{16,24},{20,28},{24,16},{28,20},{1,9},{5... | collective-permute-start | bytes 786440 | tf_op jit(solution)/shard_map/ppermute | solution.py:18
  13.9 14.1 %collective-permute-start.3 = (bf16[2,256,256]{2,1,0:T(8,128)(2,1)S(1)}, bf16[2,256,256]{2,1,0:T(8,128)(2,1)S(1)}, u32[]{:S(2)}, u32[]{:S(2)}) collective-permute-start(bf16[2,256,256]{2,1,0:T(8,128)(2,1)S(1)} %get-tuple-element.29.refs_0_.refs_4_.refs_20_), channel_id=1, source_target_pairs={{0,16},{4,20},{8,24},{12,28},{16,0},{20,4},{24,8},{28,12},{1,17},{... | collective-permute-start | bytes 786440 | tf_op jit(solution)/shard_map/ppermute | solution.py:18
  28.7 14.0 %collective-permute-start.9 = (bf16[2,256,256]{2,1,0:T(8,128)(2,1)S(1)}, bf16[2,256,256]{2,1,0:T(8,128)(2,1)S(1)}, u32[]{:S(2)}, u32[]{:S(2)}) collective-permute-start(bf16[2,256,256]{2,1,0:T(8,128)(2,1)S(1)} %get-tuple-element.36), channel_id=1, source_target_pairs={{0,12},{4,8},{8,4},{12,0},{16,28},{20,24},{24,20},{28,16},{1,13},{... | collective-permute-start | bytes 786440 | tf_op jit(solution)/shard_map/ppermute | solution.py:18
  29.2 13.6 %collective-permute-start.6 = (bf16[2,256,256]{2,1,0:T(8,128)(2,1)S(1)}, bf16[2,256,256]{2,1,0:T(8,128)(2,1)S(1)}, u32[]{:S(2)}, u32[]{:S(2)}) collective-permute-start(bf16[2,256,256]{2,1,0:T(8,128)(2,1)S(1)} %get-tuple-element.33.refs_0_.refs_4_.refs_21_), channel_id=1, source_target_pairs={{0,16},{4,20},{8,24},{12,28},{16,0},{20,4},{24,8},{28,12},{1,17},{... | collective-permute-start | bytes 786440 | tf_op jit(solution)/shard_map/ppermute | solution.py:18
  31.8 5.4 %collective-permute-start.7 = (bf16[1,256,256]{2,1,0:T(8,128)(2,1)S(1)}, bf16[1,256,256]{2,1,0:T(8,128)(2,1)S(1)}, u32[]{:S(2)}, u32[]{:S(2)}) collective-permute-start(bf16[1,256,256]{2,1,0:T(8,128)(2,1)S(1)} %get-tuple-element.34), channel_id=1, source_target_pairs={{0,4},{4,0},{8,12},{12,8},{16,20},{20,16},{24,28},{28,24},{1,5},{5... | collective-permute-start | bytes 393224 | tf_op jit(solution)/shard_map/ppermute | solution.py:18
  33.3 14.8 %copy-start.2 = (s32[2,2,8]{2,1,0:T(2,128)S(1)}, s32[2,2,8]{2,1,0:T(2,128)}, u32[]{:S(2)}) copy-start(s32[2,2,8]{2,1,0:T(2,128)} %lists.7) | copy-start | bytes 388
  33.3 14.8 %copy-start.3 = (s32[2,2]{1,0:T(2,128)S(1)}, s32[2,2]{1,0:T(2,128)}, u32[]{:S(2)}) copy-start(s32[2,2]{1,0:T(2,128)} %counts.7) | copy-start | bytes 52
  33.3 9.5 %collective-permute-start.8 = (bf16[1,256,256]{2,1,0:T(8,128)(2,1)S(1)}, bf16[1,256,256]{2,1,0:T(8,128)(2,1)S(1)}, u32[]{:S(2)}, u32[]{:S(2)}) collective-permute-start(bf16[1,256,256]{2,1,0:T(8,128)(2,1)S(1)} %get-tuple-element.35), channel_id=1, source_target_pairs={{0,8},{4,12},{8,0},{12,4},{16,24},{20,28},{24,16},{28,20},{1,9},{5... | collective-permute-start | bytes 393224 | tf_op jit(solution)/shard_map/ppermute | solution.py:18
  43.5 4.1 %collective-permute-start.11 = (bf16[2304,256]{1,0:T(8,128)(2,1)S(1)}, bf16[2304,256]{1,0:T(8,128)(2,1)S(1)}, u32[]{:S(2)}, u32[]{:S(2)}) collective-permute-start(bf16[2304,256]{1,0:T(8,128)(2,1)S(1)} %get-tuple-element.38.refs_0_), channel_id=1, source_target_pairs={{0,1},{1,0},{2,3},{3,2},{4,5},{5,4},{6,7},{7,6},{8,9},{9,8},{10,11... | collective-permute-start | bytes 3538952 | tf_op jit(solution)/shard_map/ppermute | solution.py:18
  43.6 4.5 %collective-permute-start.12 = (bf16[2304,256]{1,0:T(8,128)(2,1)S(1)}, bf16[2304,256]{1,0:T(8,128)(2,1)S(1)}, u32[]{:S(2)}, u32[]{:S(2)}) collective-permute-start(bf16[2304,256]{1,0:T(8,128)(2,1)S(1)} %get-tuple-element.39.refs_1_), channel_id=1, source_target_pairs={{0,1},{1,0},{2,3},{3,2},{4,5},{5,4},{6,7},{7,6},{8,9},{9,8},{10,11... | collective-permute-start | bytes 3538952 | tf_op jit(solution)/shard_map/ppermute | solution.py:18
  44.1 14.4 %collective-permute-start.13 = (bf16[2,256,256]{2,1,0:T(8,128)(2,1)S(1)}, bf16[2,256,256]{2,1,0:T(8,128)(2,1)S(1)}, u32[]{:S(2)}, u32[]{:S(2)}) collective-permute-start(bf16[2,256,256]{2,1,0:T(8,128)(2,1)S(1)} %get-tuple-element.40), channel_id=1, source_target_pairs={{0,12},{4,8},{8,4},{12,0},{16,28},{20,24},{24,20},{28,16},{1,13},{... | collective-permute-start | bytes 786440 | tf_op jit(solution)/shard_map/ppermute | solution.py:18
  46.8 9.4 %collective-permute-start.14 = (bf16[1,256,256]{2,1,0:T(8,128)(2,1)S(1)}, bf16[1,256,256]{2,1,0:T(8,128)(2,1)S(1)}, u32[]{:S(2)}, u32[]{:S(2)}) collective-permute-start(bf16[1,256,256]{2,1,0:T(8,128)(2,1)S(1)} %get-tuple-element.41), channel_id=1, source_target_pairs={{0,4},{4,0},{8,12},{12,8},{16,20},{20,16},{24,28},{28,24},{1,5},{5... | collective-permute-start | bytes 393224 | tf_op jit(solution)/shard_map/ppermute | solution.py:18
  47.3 11.2 %collective-permute-start.15 = (bf16[1,256,256]{2,1,0:T(8,128)(2,1)S(1)}, bf16[1,256,256]{2,1,0:T(8,128)(2,1)S(1)}, u32[]{:S(2)}, u32[]{:S(2)}) collective-permute-start(bf16[1,256,256]{2,1,0:T(8,128)(2,1)S(1)} %get-tuple-element.42), channel_id=1, source_target_pairs={{0,8},{4,12},{8,0},{12,4},{16,24},{20,28},{24,16},{28,20},{1,9},{5... | collective-permute-start | bytes 393224 | tf_op jit(solution)/shard_map/ppermute | solution.py:18
  50.5 15.7 %collective-permute-start.23 = (bf16[2,256,256]{2,1,0:T(8,128)(2,1)S(1)}, bf16[2,256,256]{2,1,0:T(8,128)(2,1)S(1)}, u32[]{:S(2)}, u32[]{:S(2)}) collective-permute-start(bf16[2,256,256]{2,1,0:T(8,128)(2,1)S(1)} %shard_map.67.refs_12_.refs_22_), channel_id=1, source_target_pairs={{0,16},{4,20},{8,24},{12,28},{16,0},{20,4},{24,8},{28,12},{1,17},{... | collective-permute-start | bytes 786440 | tf_op jit(solution)/shard_map/ppermute | solution.py:18
  61.0 6.8 %collective-permute-start.16 = (bf16[2,256,256]{2,1,0:T(8,128)(2,1)S(1)}, bf16[2,256,256]{2,1,0:T(8,128)(2,1)S(1)}, u32[]{:S(2)}, u32[]{:S(2)}) collective-permute-start(bf16[2,256,256]{2,1,0:T(8,128)(2,1)S(1)} %get-tuple-element.44), channel_id=1, source_target_pairs={{0,4},{4,0},{8,12},{12,8},{16,20},{20,16},{24,28},{28,24},{1,5},{5... | collective-permute-start | bytes 786440 | tf_op jit(solution)/shard_map/ppermute | solution.py:18
  62.1 14.8 %collective-permute-start.17 = (bf16[2,256,256]{2,1,0:T(8,128)(2,1)S(1)}, bf16[2,256,256]{2,1,0:T(8,128)(2,1)S(1)}, u32[]{:S(2)}, u32[]{:S(2)}) collective-permute-start(bf16[2,256,256]{2,1,0:T(8,128)(2,1)S(1)} %get-tuple-element.45), channel_id=1, source_target_pairs={{0,8},{4,12},{8,0},{12,4},{16,24},{20,28},{24,16},{28,20},{1,9},{5... | collective-permute-start | bytes 786440 | tf_op jit(solution)/shard_map/ppermute | solution.py:18
  62.1 20.8 %collective-permute-start.18 = (bf16[2,256,256]{2,1,0:T(8,128)(2,1)S(1)}, bf16[2,256,256]{2,1,0:T(8,128)(2,1)S(1)}, u32[]{:S(2)}, u32[]{:S(2)}) collective-permute-start(bf16[2,256,256]{2,1,0:T(8,128)(2,1)S(1)} %get-tuple-element.46), channel_id=1, source_target_pairs={{0,12},{4,8},{8,4},{12,0},{16,28},{20,24},{24,20},{28,16},{1,13},{... | collective-permute-start | bytes 786440 | tf_op jit(solution)/shard_map/ppermute | solution.py:18
  64.5 18.4 %collective-permute-start.19 = (bf16[2,256,256]{2,1,0:T(8,128)(2,1)S(1)}, bf16[2,256,256]{2,1,0:T(8,128)(2,1)S(1)}, u32[]{:S(2)}, u32[]{:S(2)}) collective-permute-start(bf16[2,256,256]{2,1,0:T(8,128)(2,1)S(1)} %get-tuple-element.43.refs_12_.refs_23_), channel_id=1, source_target_pairs={{0,16},{4,20},{8,24},{12,28},{16,0},{20,4},{24,8},{28,12},{1,17},{... | collective-permute-start | bytes 786440 | tf_op jit(solution)/shard_map/ppermute | solution.py:18
  66.9 19.1 %collective-permute-start.24 = (bf16[1,256,256]{2,1,0:T(8,128)(2,1)S(1)}, bf16[1,256,256]{2,1,0:T(8,128)(2,1)S(1)}, u32[]{:S(2)}, u32[]{:S(2)}) collective-permute-start(bf16[1,256,256]{2,1,0:T(8,128)(2,1)S(1)} %get-tuple-element.50), channel_id=1, source_target_pairs={{0,4},{4,0},{8,12},{12,8},{16,20},{20,16},{24,28},{28,24},{1,5},{5... | collective-permute-start | bytes 393224 | tf_op jit(solution)/shard_map/ppermute | solution.py:18
  67.8 19.4 %collective-permute-start.25 = (bf16[1,256,256]{2,1,0:T(8,128)(2,1)S(1)}, bf16[1,256,256]{2,1,0:T(8,128)(2,1)S(1)}, u32[]{:S(2)}, u32[]{:S(2)}) collective-permute-start(bf16[1,256,256]{2,1,0:T(8,128)(2,1)S(1)} %get-tuple-element.51), channel_id=1, source_target_pairs={{0,8},{4,12},{8,0},{12,4},{16,24},{20,28},{24,16},{28,20},{1,9},{5... | collective-permute-start | bytes 393224 | tf_op jit(solution)/shard_map/ppermute | solution.py:18
  76.8 11.7 %collective-permute-start.26 = (bf16[1,256,256]{2,1,0:T(8,128)(2,1)S(1)}, bf16[1,256,256]{2,1,0:T(8,128)(2,1)S(1)}, u32[]{:S(2)}, u32[]{:S(2)}) collective-permute-start(bf16[1,256,256]{2,1,0:T(8,128)(2,1)S(1)} %get-tuple-element.52), channel_id=1, source_target_pairs={{0,12},{4,8},{8,4},{12,0},{16,28},{20,24},{24,20},{28,16},{1,13},{... | collective-permute-start | bytes 393224 | tf_op jit(solution)/shard_map/ppermute | solution.py:18
  83.6 7.9 %collective-permute-start.20 = (bf16[1,256,256]{2,1,0:T(8,128)(2,1)S(1)}, bf16[1,256,256]{2,1,0:T(8,128)(2,1)S(1)}, u32[]{:S(2)}, u32[]{:S(2)}) collective-permute-start(bf16[1,256,256]{2,1,0:T(8,128)(2,1)S(1)} %get-tuple-element.47), channel_id=1, source_target_pairs={{0,4},{4,0},{8,12},{12,8},{16,20},{20,16},{24,28},{28,24},{1,5},{5... | collective-permute-start | bytes 393224 | tf_op jit(solution)/shard_map/ppermute | solution.py:18
  84.7 6.8 %collective-permute-start.21 = (bf16[1,256,256]{2,1,0:T(8,128)(2,1)S(1)}, bf16[1,256,256]{2,1,0:T(8,128)(2,1)S(1)}, u32[]{:S(2)}, u32[]{:S(2)}) collective-permute-start(bf16[1,256,256]{2,1,0:T(8,128)(2,1)S(1)} %get-tuple-element.48), channel_id=1, source_target_pairs={{0,8},{4,12},{8,0},{12,4},{16,24},{20,28},{24,16},{28,20},{1,9},{5... | collective-permute-start | bytes 393224 | tf_op jit(solution)/shard_map/ppermute | solution.py:18
  86.0 7.8 %collective-permute-start.22 = (bf16[1,256,256]{2,1,0:T(8,128)(2,1)S(1)}, bf16[1,256,256]{2,1,0:T(8,128)(2,1)S(1)}, u32[]{:S(2)}, u32[]{:S(2)}) collective-permute-start(bf16[1,256,256]{2,1,0:T(8,128)(2,1)S(1)} %get-tuple-element.49), channel_id=1, source_target_pairs={{0,12},{4,8},{8,4},{12,0},{16,28},{20,24},{24,20},{28,16},{1,13},{... | collective-permute-start | bytes 393224 | tf_op jit(solution)/shard_map/ppermute | solution.py:18

commit v20 on v15

--- a/solution.py
+++ b/solution.py
@@ -187,12 +187,12 @@
     far, got = leaf(solved, half), near(sends)
     values, steps = far_rows(raw, "draw", draws)
     sends = call(
-        functools.partial(relay_kernel, half, 0, len(got), len(values)),
+        functools.partial(relay_kernel, half, 0, 0, len(values)),
         [shape(1, rows, wide)] * (CHUNKS * (half - 1)) + [shape(*value.shape) for value in values],
         [],
         (picks,),
-        (far, *got, *values),
-        aliases={2 + len(got) + at: CHUNKS * (half - 1) + at for at in range(len(values))},
+        (far, *values),
+        aliases={2 + at: CHUNKS * (half - 1) + at for at in range(len(values))},
     )
     sends, values = take(sends, CHUNKS * (half - 1))
     packs, steps = near_rows(values, steps, "draw", draws)

time: 96.2 us -> 106 us (1.10)
  starting transfers between devices: 31.5 us -> 37.7 us
  waiting for transfers between devices: 48.2 us -> 52.2 us
    ppermute x27, starting transfers between devices: 31.5 us -> 37.7 us  [hop(): return lax.ppermute(value, axis, [(at, at ^ step) for at in range(size)])]
    ppermute x27, waiting for transfers between devices: 48.2 us -> 52.2 us  [hop(): return lax.ppermute(value, axis, [(at, at ^ step) for at in range(size)])]
  transfers between devices with their start and end apart: 27 -> 27, of which waited for: 13 -> 13; matrix products, arithmetic and copies ran while one was open for 1% -> 1% of each run, Pallas kernels for 9% -> 8%
where the time goes in v20:
time: 106 us
  waiting for transfers between devices  52.2 us (49%)
  starting transfers between devices  37.7 us (36%)
  Pallas kernels  13.7 us (13%)
  local copies, waits for them, and re-layouts  2.24 us (2%)
    ppermute x27, waiting for transfers between devices, hop(): return lax.ppermute(value, axis, [(at, at ^ step) for at in range(size)])  52.2 us
    ppermute x27, starting transfers between devices, hop(): return lax.ppermute(value, axis, [(at, at ^ step) for at in range(size)])  37.7 us
    pallas_call x8, Pallas kernels, call(): pl.pallas_call(kernel, out_shape=outs, in_specs=[SMEM] * len(small) + [VM...  13.7 us
  transfers between devices with their start and end apart: 27, of which 13 were waited for; matrix products, arithmetic and copies ran while one was open for 1% of the time, Pallas kernels for 8%

profile of v20, /device:TPU:0, one launch (start us, length us, event | category | flops | bytes accessed | tf_op | source)
XLA Modules:
  0.0 106.2 jit_solution(8883002638819045611)
XLA Ops:
  1.4 2.6 %collective-permute-start = (bf16[128,256]{1,0:T(8,128)(2,1)S(1)}, bf16[128,256]{1,0:T(8,128)(2,1)S(1)}, u32[]{:S(2)}, u32[]{:S(2)}) collective-permute-start(bf16[128,256]{1,0:T(8,128)(2,1)S(1)} %bitcast.8), channel_id=1, source_target_pairs={{0,2},{1,3},{2,0},{3,1},{4,6},{5,7},{6,4},{7,5},{8,10},{9,11},{10,... | collective-permute-start | bytes 196616 | tf_op jit(solution)/shard_map/ppermute | solution.py:18
  4.0 1.3 %fusion = (bf16[1,2,2,256,256]{4,3,2,1,0:T(8,128)(2,1)S(1)}, bf16[1,2,2,256,256]{4,3,2,1,0:T(8,128)(2,1)S(1)}) fusion(bf16[2,2,2,256,256]{4,3,2,1,0:T(8,128)(2,1)} %param.8), kind=kLoop, calls=%fused_computation.2 | loop fusion | bytes 2097152 | tf_op jit(solution)/shard_map/slice | solution.py:174
  5.4 1.3 %collective-permute-done.refs_1_ = bf16[128,256]{1,0:T(8,128)(2,1)S(1)} collective-permute-done((bf16[128,256]{1,0:T(8,128)(2,1)S(1)}, bf16[128,256]{1,0:T(8,128)(2,1)S(1)}, u32[]{:S(2)}, u32[]{:S(2)}) %collective-permute-start) | collective-permute-done | bytes 65568 | tf_op jit(solution)/shard_map/ppermute | solution.py:18
  6.7 1.2 %collective-permute-done.2.refs_3_ = bf16[128,256]{1,0:T(8,128)(2,1)S(1)} collective-permute-done((bf16[128,256]{1,0:T(8,128)(2,1)S(1)}, bf16[128,256]{1,0:T(8,128)(2,1)S(1)}, u32[]{:S(2)}, u32[]{:S(2)}) %collective-permute-start.2) | collective-permute-done | bytes 65568 | tf_op jit(solution)/shard_map/ppermute | solution.py:18
  7.9 1.1 %shard_map.64 = (bf16[2,256,512]{2,1,0:T(8,128)(2,1)S(1)}, bf16[1,256,512]{2,1,0:T(8,128)(2,1)S(1)}, bf16[1,256,512]{2,1,0:T(8,128)(2,1)S(1)}, bf16[1,256,512]{2,1,0:T(8,128)(2,1)S(1)}, bf16[2304,256]{1,0:T(8,128)(2,1)S(1)}) custom-call(s32[2,8,8]{2,1,0:T(8,128)S(1)} %copy-done.1, ...), custom_call_target="tpu_custom_call", output_to_operand_aliasing={{4}: (6, {})} | custom-call | flops 134217728 | bytes 4456448 | tf_op jit(solution)/shard_map/pallas_call | solution.py:51
  9.0 1.8 %collective-permute-start.4 = (bf16[2304,256]{1,0:T(8,128)(2,1)S(1)}, bf16[2304,256]{1,0:T(8,128)(2,1)S(1)}, u32[]{:S(2)}, u32[]{:S(2)}) collective-permute-start(bf16[2304,256]{1,0:T(8,128)(2,1)S(1)} %get-tuple-element.29.refs_0_), channel_id=1, source_target_pairs={{0,2},{1,3},{2,0},{3,1},{4,6},{5,7},{6,4},{7,5},{8,10},{9,11},{10,... | collective-permute-start | bytes 3538952 | tf_op jit(solution)/shard_map/ppermute | solution.py:18
  10.8 2.6 %collective-permute-start.3 = (bf16[2,256,512]{2,1,0:T(8,128)(2,1)S(1)}, bf16[2,256,512]{2,1,0:T(8,128)(2,1)S(1)}, u32[]{:S(2)}, u32[]{:S(2)}) collective-permute-start(bf16[2,256,512]{2,1,0:T(8,128)(2,1)S(1)} %get-tuple-element.28.refs_4_.refs_20_), channel_id=1, source_target_pairs={{0,16},{4,20},{8,24},{12,28},{16,0},{20,4},{24,8},{28,12},{1,17},{... | collective-permute-start | bytes 1572872 | tf_op jit(solution)/shard_map/ppermute | solution.py:18
  13.4 23.3 %collective-permute-done.3.far.refs_8_ = bf16[2,256,512]{2,1,0:T(8,128)(2,1)S(1)} collective-permute-done((bf16[2,256,512]{2,1,0:T(8,128)(2,1)S(1)}, bf16[2,256,512]{2,1,0:T(8,128)(2,1)S(1)}, u32[]{:S(2)}, u32[]{:S(2)}) %collective-permute-start.3) | collective-permute-done | bytes 524320 | tf_op jit(solution)/shard_map/ppermute | solution.py:18
  38.5 1.8 %collective-permute-start.7 = (bf16[1,256,512]{2,1,0:T(8,128)(2,1)S(1)}, bf16[1,256,512]{2,1,0:T(8,128)(2,1)S(1)}, u32[]{:S(2)}, u32[]{:S(2)}) collective-permute-start(bf16[1,256,512]{2,1,0:T(8,128)(2,1)S(1)} %get-tuple-element.32), channel_id=1, source_target_pairs={{0,4},{4,0},{8,12},{12,8},{16,20},{20,16},{24,28},{28,24},{1,5},{5... | collective-permute-start | bytes 786440 | tf_op jit(solution)/shard_map/ppermute | solution.py:18
  40.2 1.6 %collective-permute-start.8 = (bf16[1,256,512]{2,1,0:T(8,128)(2,1)S(1)}, bf16[1,256,512]{2,1,0:T(8,128)(2,1)S(1)}, u32[]{:S(2)}, u32[]{:S(2)}) collective-permute-start(bf16[1,256,512]{2,1,0:T(8,128)(2,1)S(1)} %get-tuple-element.33), channel_id=1, source_target_pairs={{0,8},{4,12},{8,0},{12,4},{16,24},{20,28},{24,16},{28,20},{1,9},{5... | collective-permute-start | bytes 786440 | tf_op jit(solution)/shard_map/ppermute | solution.py:18
  41.9 4.8 %collective-permute-done.7.refs_5_ = bf16[1,256,512]{2,1,0:T(8,128)(2,1)S(1)} collective-permute-done((bf16[1,256,512]{2,1,0:T(8,128)(2,1)S(1)}, bf16[1,256,512]{2,1,0:T(8,128)(2,1)S(1)}, u32[]{:S(2)}, u32[]{:S(2)}) %collective-permute-start.7) | collective-permute-done | bytes 262176 | tf_op jit(solution)/shard_map/ppermute | solution.py:18
  46.8 1.7 %collective-permute-start.13 = (bf16[1,256,256]{2,1,0:T(8,128)(2,1)S(1)}, bf16[1,256,256]{2,1,0:T(8,128)(2,1)S(1)}, u32[]{:S(2)}, u32[]{:S(2)}) collective-permute-start(bf16[1,256,256]{2,1,0:T(8,128)(2,1)S(1)} %get-tuple-element.38), channel_id=1, source_target_pairs={{0,4},{4,0},{8,12},{12,8},{16,20},{20,16},{24,28},{28,24},{1,5},{5... | collective-permute-start | bytes 393224 | tf_op jit(solution)/shard_map/ppermute | solution.py:18
  49.4 1.6 %collective-permute-start.14 = (bf16[1,256,256]{2,1,0:T(8,128)(2,1)S(1)}, bf16[1,256,256]{2,1,0:T(8,128)(2,1)S(1)}, u32[]{:S(2)}, u32[]{:S(2)}) collective-permute-start(bf16[1,256,256]{2,1,0:T(8,128)(2,1)S(1)} %get-tuple-element.39), channel_id=1, source_target_pairs={{0,8},{4,12},{8,0},{12,4},{16,24},{20,28},{24,16},{28,20},{1,9},{5... | collective-permute-start | bytes 393224 | tf_op jit(solution)/shard_map/ppermute | solution.py:18
  51.0 3.8 %collective-permute-done.9.refs_7_ = bf16[1,256,512]{2,1,0:T(8,128)(2,1)S(1)} collective-permute-done((bf16[1,256,512]{2,1,0:T(8,128)(2,1)S(1)}, bf16[1,256,512]{2,1,0:T(8,128)(2,1)S(1)}, u32[]{:S(2)}, u32[]{:S(2)}) %collective-permute-start.9) | collective-permute-done | bytes 262176 | tf_op jit(solution)/shard_map/ppermute | solution.py:18
  54.8 2.8 %collective-permute-start.15 = (bf16[1,256,256]{2,1,0:T(8,128)(2,1)S(1)}, bf16[1,256,256]{2,1,0:T(8,128)(2,1)S(1)}, u32[]{:S(2)}, u32[]{:S(2)}) collective-permute-start(bf16[1,256,256]{2,1,0:T(8,128)(2,1)S(1)} %get-tuple-element.40), channel_id=1, source_target_pairs={{0,12},{4,8},{8,4},{12,0},{16,28},{20,24},{24,20},{28,16},{1,13},{... | collective-permute-start | bytes 393224 | tf_op jit(solution)/shard_map/ppermute | solution.py:18
  58.1 1.4 %collective-permute-start.11 = (bf16[1,256,256]{2,1,0:T(8,128)(2,1)S(1)}, bf16[1,256,256]{2,1,0:T(8,128)(2,1)S(1)}, u32[]{:S(2)}, u32[]{:S(2)}) collective-permute-start(bf16[1,256,256]{2,1,0:T(8,128)(2,1)S(1)} %get-tuple-element.36), channel_id=1, source_target_pairs={{0,8},{4,12},{8,0},{12,4},{16,24},{20,28},{24,16},{28,20},{1,9},{5... | collective-permute-start | bytes 393224 | tf_op jit(solution)/shard_map/ppermute | solution.py:18
  59.4 2.2 %collective-permute-done.15.refs_11_ = bf16[1,256,256]{2,1,0:T(8,128)(2,1)S(1)} collective-permute-done((bf16[1,256,256]{2,1,0:T(8,128)(2,1)S(1)}, bf16[1,256,256]{2,1,0:T(8,128)(2,1)S(1)}, u32[]{:S(2)}, u32[]{:S(2)}) %collective-permute-start.15) | collective-permute-done | bytes 131104 | tf_op jit(solution)/shard_map/ppermute | solution.py:18
  61.6 2.9 %collective-permute-start.12 = (bf16[1,256,256]{2,1,0:T(8,128)(2,1)S(1)}, bf16[1,256,256]{2,1,0:T(8,128)(2,1)S(1)}, u32[]{:S(2)}, u32[]{:S(2)}) collective-permute-start(bf16[1,256,256]{2,1,0:T(8,128)(2,1)S(1)} %get-tuple-element.37), channel_id=1, source_target_pairs={{0,12},{4,8},{8,4},{12,0},{16,28},{20,24},{24,20},{28,16},{1,13},{... | collective-permute-start | bytes 393224 | tf_op jit(solution)/shard_map/ppermute | solution.py:18
  64.6 2.4 %shard_map.66.refs_12_.refs_21_ = bf16[2,256,256]{2,1,0:T(8,128)(2,1)S(1)} custom-call(s32[2,8,8]{2,1,0:T(8,128)S(1)} %copy-done.1, s32[2,2,8]{2,1,0:T(2,128)S(1)} %copy-done.2, s32[2,2]{1,0:T(2,128)S(1)} %copy-done.3, bf16[3,2,256,512]{3,2,1,0:T(8,128)(2,1)S(1)} %copy-done, bf16[2304,256]{1,0:T(8,128)(2,1)S(1)} %get-tuple-element.30.refs_0_, ...), custom_call_target="tpu_custom_call" | custom-call | flops 603979776 | bytes 8781824 | tf_op jit(solution)/shard_map/pallas_call | solution.py:51
  67.0 2.7 %collective-permute-start.23 = (bf16[2,256,256]{2,1,0:T(8,128)(2,1)S(1)}, bf16[2,256,256]{2,1,0:T(8,128)(2,1)S(1)}, u32[]{:S(2)}, u32[]{:S(2)}) collective-permute-start(bf16[2,256,256]{2,1,0:T(8,128)(2,1)S(1)} %shard_map.66.refs_12_.refs_21_), channel_id=1, source_target_pairs={{0,16},{4,20},{8,24},{12,28},{16,0},{20,4},{24,8},{28,12},{1,17},{... | collective-permute-start | bytes 786440 | tf_op jit(solution)/shard_map/ppermute | solution.py:18
  69.6 2.4 %shard_map.67 = (bf16[2,256,256]{2,1,0:T(8,128)(2,1)S(1)}, bf16[2,256,256]{2,1,0:T(8,128)(2,1)S(1)}, bf16[2,256,256]{2,1,0:T(8,128)(2,1)S(1)}, bf16[2,256,256]{2,1,0:T(8,128)(2,1)S(1)}) custom-call(s32[2,8,8]{2,1,0:T(8,128)S(1)} %copy-done.1, s32[2,2,8]{2,1,0:T(2,128)S(1)} %copy-done.2, s32[2,2]{1,0:T(2,128)S(1)} %copy-done.3, ...), custom_call_target="tpu_custom_call" | custom-call | flops 603979776 | bytes 9830400 | tf_op jit(solution)/shard_map/pallas_call | solution.py:51
  72.7 2.2 %collective-permute-start.17 = (bf16[2,256,256]{2,1,0:T(8,128)(2,1)S(1)}, bf16[2,256,256]{2,1,0:T(8,128)(2,1)S(1)}, u32[]{:S(2)}, u32[]{:S(2)}) collective-permute-start(bf16[2,256,256]{2,1,0:T(8,128)(2,1)S(1)} %get-tuple-element.43), channel_id=1, source_target_pairs={{0,8},{4,12},{8,0},{12,4},{16,24},{20,28},{24,16},{28,20},{1,9},{5... | collective-permute-start | bytes 786440 | tf_op jit(solution)/shard_map/ppermute | solution.py:18
  75.6 2.3 %collective-permute-start.19 = (bf16[2,256,256]{2,1,0:T(8,128)(2,1)S(1)}, bf16[2,256,256]{2,1,0:T(8,128)(2,1)S(1)}, u32[]{:S(2)}, u32[]{:S(2)}) collective-permute-start(bf16[2,256,256]{2,1,0:T(8,128)(2,1)S(1)} %get-tuple-element.41.refs_12_.refs_22_), channel_id=1, source_target_pairs={{0,16},{4,20},{8,24},{12,28},{16,0},{20,4},{24,8},{28,12},{1,17},{... | collective-permute-start | bytes 786440 | tf_op jit(solution)/shard_map/ppermute | solution.py:18
  77.9 2.1 %collective-permute-done.23.far.refs_16_ = bf16[2,256,256]{2,1,0:T(8,128)(2,1)S(1)} collective-permute-done((bf16[2,256,256]{2,1,0:T(8,128)(2,1)S(1)}, bf16[2,256,256]{2,1,0:T(8,128)(2,1)S(1)}, u32[]{:S(2)}, u32[]{:S(2)}) %collective-permute-start.23) | collective-permute-done | bytes 262176 | tf_op jit(solution)/shard_map/ppermute | solution.py:18
  80.8 3.1 %collective-permute-start.25 = (bf16[1,256,256]{2,1,0:T(8,128)(2,1)S(1)}, bf16[1,256,256]{2,1,0:T(8,128)(2,1)S(1)}, u32[]{:S(2)}, u32[]{:S(2)}) collective-permute-start(bf16[1,256,256]{2,1,0:T(8,128)(2,1)S(1)} %get-tuple-element.49), channel_id=1, source_target_pairs={{0,8},{4,12},{8,0},{12,4},{16,24},{20,28},{24,16},{28,20},{1,9},{5... | collective-permute-start | bytes 393224 | tf_op jit(solution)/shard_map/ppermute | solution.py:18
  83.9 4.8 %collective-permute-done.17.refs_1_.refs_14_ = bf16[2,256,256]{2,1,0:T(8,128)(2,1)S(1)} collective-permute-done((bf16[2,256,256]{2,1,0:T(8,128)(2,1)S(1)}, bf16[2,256,256]{2,1,0:T(8,128)(2,1)S(1)}, u32[]{:S(2)}, u32[]{:S(2)}) %collective-permute-start.17) | collective-permute-done | bytes 262176 | tf_op jit(solution)/shard_map/ppermute | solution.py:18
  88.7 5.6 %collective-permute-done.18.refs_2_.refs_15_ = bf16[2,256,256]{2,1,0:T(8,128)(2,1)S(1)} collective-permute-done((bf16[2,256,256]{2,1,0:T(8,128)(2,1)S(1)}, bf16[2,256,256]{2,1,0:T(8,128)(2,1)S(1)}, u32[]{:S(2)}, u32[]{:S(2)}) %collective-permute-start.18) | collective-permute-done | bytes 262176 | tf_op jit(solution)/shard_map/ppermute | solution.py:18
  95.1 1.6 %collective-permute-start.20 = (bf16[1,256,256]{2,1,0:T(8,128)(2,1)S(1)}, bf16[1,256,256]{2,1,0:T(8,128)(2,1)S(1)}, u32[]{:S(2)}, u32[]{:S(2)}) collective-permute-start(bf16[1,256,256]{2,1,0:T(8,128)(2,1)S(1)} %get-tuple-element.45), channel_id=1, source_target_pairs={{0,4},{4,0},{8,12},{12,8},{16,20},{20,16},{24,28},{28,24},{1,5},{5... | collective-permute-start | bytes 393224 | tf_op jit(solution)/shard_map/ppermute | solution.py:18
  96.7 2.0 %collective-permute-start.22 = (bf16[1,256,256]{2,1,0:T(8,128)(2,1)S(1)}, bf16[1,256,256]{2,1,0:T(8,128)(2,1)S(1)}, u32[]{:S(2)}, u32[]{:S(2)}) collective-permute-start(bf16[1,256,256]{2,1,0:T(8,128)(2,1)S(1)} %get-tuple-element.47), channel_id=1, source_target_pairs={{0,12},{4,8},{8,4},{12,0},{16,28},{20,24},{24,20},{28,16},{1,13},{... | collective-permute-start | bytes 393224 | tf_op jit(solution)/shard_map/ppermute | solution.py:18
  98.6 1.2 %collective-permute-done.26.refs_19_ = bf16[1,256,256]{2,1,0:T(8,128)(2,1)S(1)} collective-permute-done((bf16[1,256,256]{2,1,0:T(8,128)(2,1)S(1)}, bf16[1,256,256]{2,1,0:T(8,128)(2,1)S(1)}, u32[]{:S(2)}, u32[]{:S(2)}) %collective-permute-start.26) | collective-permute-done | bytes 131104 | tf_op jit(solution)/shard_map/ppermute | solution.py:18
  99.8 2.5 %shard_map.70.refs_23_ = bf16[2,256,256]{2,1,0:T(8,128)(2,1)S(1)} custom-call(s32[2,8,8]{2,1,0:T(8,128)S(1)} %copy-done.1, s32[2,2,8]{2,1,0:T(2,128)S(1)} %copy-done.2, s32[2,2]{1,0:T(2,128)S(1)} %copy-done.3, bf16[3,2,256,512]{3,2,1,0:T(8,128)(2,1)S(1)} %copy-done, bf16[2304,256]{1,0:T(8,128)(2,1)S(1)} %get-tuple-element.30.refs_0_, ...), custom_call_target="tpu_custom_call" | custom-call | flops 603979776 | bytes 10485760 | tf_op jit(solution)/shard_map/pallas_call | solution.py:51
  103.0 3.2 %shard_map.71 = bf16[3,2,256,512]{3,2,1,0:T(8,128)(2,1)} custom-call(s32[2,8,8]{2,1,0:T(8,128)S(1)} %copy-done.1, s32[2,2,8]{2,1,0:T(2,128)S(1)} %copy-done.2, s32[2,2]{1,0:T(2,128)S(1)} %copy-done.3, bf16[3,2,256,512]{3,2,1,0:T(8,128)(2,1)S(1)} %copy-done, bf16[2304,256]{1,0:T(8,128)(2,1)S(1)} %get-tuple-element.30.refs_0_, ...), custom_call_target="tpu_custom_call" | custom-call | flops 603979776 | bytes 13107200 | tf_op jit(solution)/shard_map/pallas_call | solution.py:51
  (42 shorter events, 8.4 us)
Async XLA Ops:
  0.9 5.8 %collective-permute-start.1 = (bf16[128,256]{1,0:T(8,128)(2,1)S(1)}, bf16[128,256]{1,0:T(8,128)(2,1)S(1)}, u32[]{:S(2)}, u32[]{:S(2)}) collective-permute-start(bf16[128,256]{1,0:T(8,128)(2,1)S(1)} %bitcast.7), channel_id=1, source_target_pairs={{0,1},{1,0},{2,3},{3,2},{4,5},{5,4},{6,7},{7,6},{8,9},{9,8},{10,11... | collective-permute-start | bytes 196616 | tf_op jit(solution)/shard_map/ppermute | solution.py:18
  1.4 5.3 %collective-permute-start = (bf16[128,256]{1,0:T(8,128)(2,1)S(1)}, bf16[128,256]{1,0:T(8,128)(2,1)S(1)}, u32[]{:S(2)}, u32[]{:S(2)}) collective-permute-start(bf16[128,256]{1,0:T(8,128)(2,1)S(1)} %bitcast.8), channel_id=1, source_target_pairs={{0,2},{1,3},{2,0},{3,1},{4,6},{5,7},{6,4},{7,5},{8,10},{9,11},{10,... | collective-permute-start | bytes 196616 | tf_op jit(solution)/shard_map/ppermute | solution.py:18
  5.3 1.4 %copy-start = (bf16[3,2,256,512]{3,2,1,0:T(8,128)(2,1)S(1)}, bf16[3,2,256,512]{3,2,1,0:T(8,128)(2,1)}, u32[]{:S(2)}) copy-start(bf16[3,2,256,512]{3,2,1,0:T(8,128)(2,1)} %noise.7) | copy-start | bytes 4718596
  5.3 2.7 %copy-start.1 = (s32[2,8,8]{2,1,0:T(8,128)S(1)}, s32[2,8,8]{2,1,0:T(8,128)}, u32[]{:S(2)}) copy-start(s32[2,8,8]{2,1,0:T(8,128)} %picks.15) | copy-start | bytes 1540
  6.7 1.3 %collective-permute-start.2 = (bf16[128,256]{1,0:T(8,128)(2,1)S(1)}, bf16[128,256]{1,0:T(8,128)(2,1)S(1)}, u32[]{:S(2)}, u32[]{:S(2)}) collective-permute-start(bf16[128,256]{1,0:T(8,128)(2,1)S(1)} %collective-permute-done.refs_1_), channel_id=1, source_target_pairs={{0,1},{1,0},{2,3},{3,2},{4,5},{5,4},{6,7},{7,6},{8,9},{9,8},{10,11... | collective-permute-start | bytes 196616 | tf_op jit(solution)/shard_map/ppermute | solution.py:18
  9.0 28.1 %collective-permute-start.4 = (bf16[2304,256]{1,0:T(8,128)(2,1)S(1)}, bf16[2304,256]{1,0:T(8,128)(2,1)S(1)}, u32[]{:S(2)}, u32[]{:S(2)}) collective-permute-start(bf16[2304,256]{1,0:T(8,128)(2,1)S(1)} %get-tuple-element.29.refs_0_), channel_id=1, source_target_pairs={{0,2},{1,3},{2,0},{3,1},{4,6},{5,7},{6,4},{7,5},{8,10},{9,11},{10,... | collective-permute-start | bytes 3538952 | tf_op jit(solution)/shard_map/ppermute | solution.py:18
  10.8 53.7 %copy-start.2 = (s32[2,2,8]{2,1,0:T(2,128)S(1)}, s32[2,2,8]{2,1,0:T(2,128)}, u32[]{:S(2)}) copy-start(s32[2,2,8]{2,1,0:T(2,128)} %lists.7) | copy-start | bytes 388
  10.8 53.7 %copy-start.3 = (s32[2,2]{1,0:T(2,128)S(1)}, s32[2,2]{1,0:T(2,128)}, u32[]{:S(2)}) copy-start(s32[2,2]{1,0:T(2,128)} %counts.7) | copy-start | bytes 52
  10.8 25.8 %collective-permute-start.3 = (bf16[2,256,512]{2,1,0:T(8,128)(2,1)S(1)}, bf16[2,256,512]{2,1,0:T(8,128)(2,1)S(1)}, u32[]{:S(2)}, u32[]{:S(2)}) collective-permute-start(bf16[2,256,512]{2,1,0:T(8,128)(2,1)S(1)} %get-tuple-element.28.refs_4_.refs_20_), channel_id=1, source_target_pairs={{0,16},{4,20},{8,24},{12,28},{16,0},{20,4},{24,8},{28,12},{1,17},{... | collective-permute-start | bytes 1572872 | tf_op jit(solution)/shard_map/ppermute | solution.py:18
  37.9 26.7 %collective-permute-start.5 = (bf16[2304,256]{1,0:T(8,128)(2,1)S(1)}, bf16[2304,256]{1,0:T(8,128)(2,1)S(1)}, u32[]{:S(2)}, u32[]{:S(2)}) collective-permute-start(bf16[2304,256]{1,0:T(8,128)(2,1)S(1)} %get-tuple-element.30.refs_0_), channel_id=1, source_target_pairs={{0,1},{1,0},{2,3},{3,2},{4,5},{5,4},{6,7},{7,6},{8,9},{9,8},{10,11... | collective-permute-start | bytes 3538952 | tf_op jit(solution)/shard_map/ppermute | solution.py:18
  38.0 26.6 %collective-permute-start.6 = (bf16[2304,256]{1,0:T(8,128)(2,1)S(1)}, bf16[2304,256]{1,0:T(8,128)(2,1)S(1)}, u32[]{:S(2)}, u32[]{:S(2)}) collective-permute-start(bf16[2304,256]{1,0:T(8,128)(2,1)S(1)} %get-tuple-element.31.refs_1_), channel_id=1, source_target_pairs={{0,1},{1,0},{2,3},{3,2},{4,5},{5,4},{6,7},{7,6},{8,9},{9,8},{10,11... | collective-permute-start | bytes 3538952 | tf_op jit(solution)/shard_map/ppermute | solution.py:18
  38.5 8.3 %collective-permute-start.7 = (bf16[1,256,512]{2,1,0:T(8,128)(2,1)S(1)}, bf16[1,256,512]{2,1,0:T(8,128)(2,1)S(1)}, u32[]{:S(2)}, u32[]{:S(2)}) collective-permute-start(bf16[1,256,512]{2,1,0:T(8,128)(2,1)S(1)} %get-tuple-element.32), channel_id=1, source_target_pairs={{0,4},{4,0},{8,12},{12,8},{16,20},{20,16},{24,28},{28,24},{1,5},{5... | collective-permute-start | bytes 786440 | tf_op jit(solution)/shard_map/ppermute | solution.py:18
  40.2 9.2 %collective-permute-start.8 = (bf16[1,256,512]{2,1,0:T(8,128)(2,1)S(1)}, bf16[1,256,512]{2,1,0:T(8,128)(2,1)S(1)}, u32[]{:S(2)}, u32[]{:S(2)}) collective-permute-start(bf16[1,256,512]{2,1,0:T(8,128)(2,1)S(1)} %get-tuple-element.33), channel_id=1, source_target_pairs={{0,8},{4,12},{8,0},{12,4},{16,24},{20,28},{24,16},{28,20},{1,9},{5... | collective-permute-start | bytes 786440 | tf_op jit(solution)/shard_map/ppermute | solution.py:18
  41.8 13.0 %collective-permute-start.9 = (bf16[1,256,512]{2,1,0:T(8,128)(2,1)S(1)}, bf16[1,256,512]{2,1,0:T(8,128)(2,1)S(1)}, u32[]{:S(2)}, u32[]{:S(2)}) collective-permute-start(bf16[1,256,512]{2,1,0:T(8,128)(2,1)S(1)} %get-tuple-element.34), channel_id=1, source_target_pairs={{0,12},{4,8},{8,4},{12,0},{16,28},{20,24},{24,20},{28,16},{1,13},{... | collective-permute-start | bytes 786440 | tf_op jit(solution)/shard_map/ppermute | solution.py:18
  46.8 10.8 %collective-permute-start.13 = (bf16[1,256,256]{2,1,0:T(8,128)(2,1)S(1)}, bf16[1,256,256]{2,1,0:T(8,128)(2,1)S(1)}, u32[]{:S(2)}, u32[]{:S(2)}) collective-permute-start(bf16[1,256,256]{2,1,0:T(8,128)(2,1)S(1)} %get-tuple-element.38), channel_id=1, source_target_pairs={{0,4},{4,0},{8,12},{12,8},{16,20},{20,16},{24,28},{28,24},{1,5},{5... | collective-permute-start | bytes 393224 | tf_op jit(solution)/shard_map/ppermute | solution.py:18
  49.4 8.7 %collective-permute-start.14 = (bf16[1,256,256]{2,1,0:T(8,128)(2,1)S(1)}, bf16[1,256,256]{2,1,0:T(8,128)(2,1)S(1)}, u32[]{:S(2)}, u32[]{:S(2)}) collective-permute-start(bf16[1,256,256]{2,1,0:T(8,128)(2,1)S(1)} %get-tuple-element.39), channel_id=1, source_target_pairs={{0,8},{4,12},{8,0},{12,4},{16,24},{20,28},{24,16},{28,20},{1,9},{5... | collective-permute-start | bytes 393224 | tf_op jit(solution)/shard_map/ppermute | solution.py:18
  54.8 6.8 %collective-permute-start.15 = (bf16[1,256,256]{2,1,0:T(8,128)(2,1)S(1)}, bf16[1,256,256]{2,1,0:T(8,128)(2,1)S(1)}, u32[]{:S(2)}, u32[]{:S(2)}) collective-permute-start(bf16[1,256,256]{2,1,0:T(8,128)(2,1)S(1)} %get-tuple-element.40), channel_id=1, source_target_pairs={{0,12},{4,8},{8,4},{12,0},{16,28},{20,24},{24,20},{28,16},{1,13},{... | collective-permute-start | bytes 393224 | tf_op jit(solution)/shard_map/ppermute | solution.py:18
  57.6 12.1 %collective-permute-start.10 = (bf16[1,256,256]{2,1,0:T(8,128)(2,1)S(1)}, bf16[1,256,256]{2,1,0:T(8,128)(2,1)S(1)}, u32[]{:S(2)}, u32[]{:S(2)}) collective-permute-start(bf16[1,256,256]{2,1,0:T(8,128)(2,1)S(1)} %get-tuple-element.35), channel_id=1, source_target_pairs={{0,4},{4,0},{8,12},{12,8},{16,20},{20,16},{24,28},{28,24},{1,5},{5... | collective-permute-start | bytes 393224 | tf_op jit(solution)/shard_map/ppermute | solution.py:18
  58.1 11.6 %collective-permute-start.11 = (bf16[1,256,256]{2,1,0:T(8,128)(2,1)S(1)}, bf16[1,256,256]{2,1,0:T(8,128)(2,1)S(1)}, u32[]{:S(2)}, u32[]{:S(2)}) collective-permute-start(bf16[1,256,256]{2,1,0:T(8,128)(2,1)S(1)} %get-tuple-element.36), channel_id=1, source_target_pairs={{0,8},{4,12},{8,0},{12,4},{16,24},{20,28},{24,16},{28,20},{1,9},{5... | collective-permute-start | bytes 393224 | tf_op jit(solution)/shard_map/ppermute | solution.py:18
  61.6 8.0 %collective-permute-start.12 = (bf16[1,256,256]{2,1,0:T(8,128)(2,1)S(1)}, bf16[1,256,256]{2,1,0:T(8,128)(2,1)S(1)}, u32[]{:S(2)}, u32[]{:S(2)}) collective-permute-start(bf16[1,256,256]{2,1,0:T(8,128)(2,1)S(1)} %get-tuple-element.37), channel_id=1, source_target_pairs={{0,12},{4,8},{8,4},{12,0},{16,28},{20,24},{24,20},{28,16},{1,13},{... | collective-permute-start | bytes 393224 | tf_op jit(solution)/shard_map/ppermute | solution.py:18
  67.0 13.1 %collective-permute-start.23 = (bf16[2,256,256]{2,1,0:T(8,128)(2,1)S(1)}, bf16[2,256,256]{2,1,0:T(8,128)(2,1)S(1)}, u32[]{:S(2)}, u32[]{:S(2)}) collective-permute-start(bf16[2,256,256]{2,1,0:T(8,128)(2,1)S(1)} %shard_map.66.refs_12_.refs_21_), channel_id=1, source_target_pairs={{0,16},{4,20},{8,24},{12,28},{16,0},{20,4},{24,8},{28,12},{1,17},{... | collective-permute-start | bytes 786440 | tf_op jit(solution)/shard_map/ppermute | solution.py:18
  72.1 8.7 %collective-permute-start.16 = (bf16[2,256,256]{2,1,0:T(8,128)(2,1)S(1)}, bf16[2,256,256]{2,1,0:T(8,128)(2,1)S(1)}, u32[]{:S(2)}, u32[]{:S(2)}) collective-permute-start(bf16[2,256,256]{2,1,0:T(8,128)(2,1)S(1)} %get-tuple-element.42), channel_id=1, source_target_pairs={{0,4},{4,0},{8,12},{12,8},{16,20},{20,16},{24,28},{28,24},{1,5},{5... | collective-permute-start | bytes 786440 | tf_op jit(solution)/shard_map/ppermute | solution.py:18
  72.7 16.1 %collective-permute-start.17 = (bf16[2,256,256]{2,1,0:T(8,128)(2,1)S(1)}, bf16[2,256,256]{2,1,0:T(8,128)(2,1)S(1)}, u32[]{:S(2)}, u32[]{:S(2)}) collective-permute-start(bf16[2,256,256]{2,1,0:T(8,128)(2,1)S(1)} %get-tuple-element.43), channel_id=1, source_target_pairs={{0,8},{4,12},{8,0},{12,4},{16,24},{20,28},{24,16},{28,20},{1,9},{5... | collective-permute-start | bytes 786440 | tf_op jit(solution)/shard_map/ppermute | solution.py:18
  74.9 19.5 %collective-permute-start.18 = (bf16[2,256,256]{2,1,0:T(8,128)(2,1)S(1)}, bf16[2,256,256]{2,1,0:T(8,128)(2,1)S(1)}, u32[]{:S(2)}, u32[]{:S(2)}) collective-permute-start(bf16[2,256,256]{2,1,0:T(8,128)(2,1)S(1)} %get-tuple-element.44), channel_id=1, source_target_pairs={{0,12},{4,8},{8,4},{12,0},{16,28},{20,24},{24,20},{28,16},{1,13},{... | collective-permute-start | bytes 786440 | tf_op jit(solution)/shard_map/ppermute | solution.py:18
  75.6 18.7 %collective-permute-start.19 = (bf16[2,256,256]{2,1,0:T(8,128)(2,1)S(1)}, bf16[2,256,256]{2,1,0:T(8,128)(2,1)S(1)}, u32[]{:S(2)}, u32[]{:S(2)}) collective-permute-start(bf16[2,256,256]{2,1,0:T(8,128)(2,1)S(1)} %get-tuple-element.41.refs_12_.refs_22_), channel_id=1, source_target_pairs={{0,16},{4,20},{8,24},{12,28},{16,0},{20,4},{24,8},{28,12},{1,17},{... | collective-permute-start | bytes 786440 | tf_op jit(solution)/shard_map/ppermute | solution.py:18
  80.8 15.9 %collective-permute-start.24 = (bf16[1,256,256]{2,1,0:T(8,128)(2,1)S(1)}, bf16[1,256,256]{2,1,0:T(8,128)(2,1)S(1)}, u32[]{:S(2)}, u32[]{:S(2)}) collective-permute-start(bf16[1,256,256]{2,1,0:T(8,128)(2,1)S(1)} %get-tuple-element.48), channel_id=1, source_target_pairs={{0,4},{4,0},{8,12},{12,8},{16,20},{20,16},{24,28},{28,24},{1,5},{5... | collective-permute-start | bytes 393224 | tf_op jit(solution)/shard_map/ppermute | solution.py:18
  80.8 17.8 %collective-permute-start.25 = (bf16[1,256,256]{2,1,0:T(8,128)(2,1)S(1)}, bf16[1,256,256]{2,1,0:T(8,128)(2,1)S(1)}, u32[]{:S(2)}, u32[]{:S(2)}) collective-permute-start(bf16[1,256,256]{2,1,0:T(8,128)(2,1)S(1)} %get-tuple-element.49), channel_id=1, source_target_pairs={{0,8},{4,12},{8,0},{12,4},{16,24},{20,28},{24,16},{28,20},{1,9},{5... | collective-permute-start | bytes 393224 | tf_op jit(solution)/shard_map/ppermute | solution.py:18
  88.7 11.1 %collective-permute-start.26 = (bf16[1,256,256]{2,1,0:T(8,128)(2,1)S(1)}, bf16[1,256,256]{2,1,0:T(8,128)(2,1)S(1)}, u32[]{:S(2)}, u32[]{:S(2)}) collective-permute-start(bf16[1,256,256]{2,1,0:T(8,128)(2,1)S(1)} %get-tuple-element.50), channel_id=1, source_target_pairs={{0,12},{4,8},{8,4},{12,0},{16,28},{20,24},{24,20},{28,16},{1,13},{... | collective-permute-start | bytes 393224 | tf_op jit(solution)/shard_map/ppermute | solution.py:18
  95.1 7.2 %collective-permute-start.20 = (bf16[1,256,256]{2,1,0:T(8,128)(2,1)S(1)}, bf16[1,256,256]{2,1,0:T(8,128)(2,1)S(1)}, u32[]{:S(2)}, u32[]{:S(2)}) collective-permute-start(bf16[1,256,256]{2,1,0:T(8,128)(2,1)S(1)} %get-tuple-element.45), channel_id=1, source_target_pairs={{0,4},{4,0},{8,12},{12,8},{16,20},{20,16},{24,28},{28,24},{1,5},{5... | collective-permute-start | bytes 393224 | tf_op jit(solution)/shard_map/ppermute | solution.py:18
  96.6 5.6 %collective-permute-start.21 = (bf16[1,256,256]{2,1,0:T(8,128)(2,1)S(1)}, bf16[1,256,256]{2,1,0:T(8,128)(2,1)S(1)}, u32[]{:S(2)}, u32[]{:S(2)}) collective-permute-start(bf16[1,256,256]{2,1,0:T(8,128)(2,1)S(1)} %get-tuple-element.46), channel_id=1, source_target_pairs={{0,8},{4,12},{8,0},{12,4},{16,24},{20,28},{24,16},{28,20},{1,9},{5... | collective-permute-start | bytes 393224 | tf_op jit(solution)/shard_map/ppermute | solution.py:18
  96.7 6.3 %collective-permute-start.22 = (bf16[1,256,256]{2,1,0:T(8,128)(2,1)S(1)}, bf16[1,256,256]{2,1,0:T(8,128)(2,1)S(1)}, u32[]{:S(2)}, u32[]{:S(2)}) collective-permute-start(bf16[1,256,256]{2,1,0:T(8,128)(2,1)S(1)} %get-tuple-element.47), channel_id=1, source_target_pairs={{0,12},{4,8},{8,4},{12,0},{16,28},{20,24},{24,20},{28,16},{1,13},{... | collective-permute-start | bytes 393224 | tf_op jit(solution)/shard_map/ppermute | solution.py:18

commit v21 on v15

--- a/solution.py
+++ b/solution.py
@@ -99,9 +99,20 @@
         send[0] = far[node, :, chunk * wide:(chunk + 1) * wide]
 
 
+def inverse_kernel(held, span, *refs):
+    packs, refs = take(refs, len(held))
+    draw = lax.axis_index("draw")
+    levels = sum(ref.shape[0] > 1 for ref in refs)
+    draws = sum(map(len, held))
+    found = row_blocks(packs, held, levels * span)
+    for level, target in enumerate(refs[-levels:]):
+        nodes, rows = target.shape[0], target.shape[1] // draws
+        fill_inverse(target, found, (level + 1) * span - nodes * rows, draw)
+
+
 def level_kernel(
     level, owners, held, width, chunk, places, stored, sides, mates,
-    picks, lists, counts, noise, *refs,
+    picks, lists, counts, noise, inv, *refs,
 ):
     half = owners // 2
     packs, refs = take(refs, len(held))
@@ -109,7 +120,7 @@
     done, refs = take(refs, len(stored))
     chunks, refs = take(refs, mates)
     target, *refs = refs
-    sends, (table, inv, *refs) = take(refs, sides)
+    sends, (table, *refs) = take(refs, sides)
     myself, draw = lax.axis_index("leaf"), lax.axis_index("draw")
     levels, nodes = noise.shape[:2]
     wide = table.shape[-1]
@@ -134,7 +145,6 @@
         table[at] = ref[place] if ref.shape[-1] == wide else ref[place, :, columns]
     empty = level * owners
     table[empty] = jnp.zeros_like(table[empty])
-    fill_inverse(inv, found, offset + nodes * width * depth, draw)
     for node in range(nodes):
         total = None
         for pack, start, step in found:
@@ -196,6 +206,18 @@
     )
     sends, values = take(sends, CHUNKS * (half - 1))
     packs, steps = near_rows(values, steps, "draw", draws)
+    first, later = take(sends, half - 1)
+    span = nodes * (width * rows + inverse.shape[2])
+    outs = call(
+        functools.partial(inverse_kernel, steps, span),
+        [shape(*value.shape) for value in later] + [shape(nodes, rows, rows)] * (levels - 1),
+        [],
+        (),
+        (*packs, *later),
+        aliases={len(packs) + at: at for at in range(len(later))},
+    )
+    later, inverses = take(outs, len(later))
+    sends = first + later
     pieces, done = [[]], [(solved, (0, 0))]
     for at in chunks:
         distant, sends = take(sends, half - 1)
@@ -213,7 +235,7 @@
             final = last_level and at == CHUNKS - 1
             known = [entry for below in range(level) for entry in pieces[below][at]]
             stored = done if final else []
-            scratch = [pltpu.VMEM((level * owners + 1, rows, wide), BF16), inv_here]
+            scratch = [pltpu.VMEM((level * owners + 1, rows, wide), BF16)]
             if final:
                 scratch += [
                     pltpu.VMEM((nodes, rows, wide), BF16),
@@ -227,7 +249,7 @@
                 [shape(*noise.shape) if final else part] + [shape(CHUNKS, rows, wide)] * sides,
                 scratch,
                 (picks, lists, counts),
-                (noise, *packs, *(ref for ref, _ in known), *(ref for ref, _ in stored), *mates),
+                (noise, inverses[level - 1], *packs, *(ref for ref, _ in known), *(ref for ref, _ in stored), *mates),
                 out_spec=ANY if final else VMEM,
                 flops=nodes * (draws * width + 1) * dot_flops,
             )

time: 96.2 us -> 95.8 us (level)
    pallas_call x8 -> x9, Pallas kernels: 13.7 us -> 13.7 us  [call(): pl.pallas_call(kernel, out_shape=outs, in_specs=[SMEM] * len(small) + [VM...]
  transfers between devices with their start and end apart: 27 -> 27, of which waited for: 13 -> 14; matrix products, arithmetic and copies ran while one was open for 1% -> 1% of each run, Pallas kernels for 9% -> 9%
where the time goes in v21:
time: 95.8 us; the launch traced here: 95.6 us
  waiting for transfers between devices  48.2 us (50%)
  starting transfers between devices  31.2 us (33%)
  Pallas kernels  13.7 us (14%)
  local copies, waits for them, and re-layouts  2.24 us (2%)
    ppermute x27, waiting for transfers between devices, hop(): return lax.ppermute(value, axis, [(at, at ^ step) for at in range(size)])  48.2 us
    ppermute x27, starting transfers between devices, hop(): return lax.ppermute(value, axis, [(at, at ^ step) for at in range(size)])  31.2 us
    pallas_call x9, Pallas kernels, call(): pl.pallas_call(kernel, out_shape=outs, in_specs=[SMEM] * len(small) + [VM...  13.7 us
  transfers between devices with their start and end apart: 27, of which 14 were waited for; matrix products, arithmetic and copies ran while one was open for 1% of the time, Pallas kernels for 9%

profile of v21, /device:TPU:0, one launch (start us, length us, event | category | flops | bytes accessed | tf_op | source)
XLA Modules:
  0.0 95.6 jit_solution(5832393691124395876)
XLA Ops:
  0.0 0.9 fusion.1
  1.4 2.6 %collective-permute-start = (bf16[128,256]{1,0:T(8,128)(2,1)S(1)}, bf16[128,256]{1,0:T(8,128)(2,1)S(1)}, u32[]{:S(2)}, u32[]{:S(2)}) collective-permute-start(bf16[128,256]{1,0:T(8,128)(2,1)S(1)} %bitcast.8), channel_id=1, source_target_pairs={{0,2},{1,3},{2,0},{3,1},{4,6},{5,7},{6,4},{7,5},{8,10},{9,11},{10,... | collective-permute-start | bytes 196616 | tf_op jit(solution)/shard_map/ppermute | solution.py:18
  4.0 1.3 %fusion = (bf16[1,2,2,256,256]{4,3,2,1,0:T(8,128)(2,1)S(1)}, bf16[1,2,2,256,256]{4,3,2,1,0:T(8,128)(2,1)S(1)}) fusion(bf16[2,2,2,256,256]{4,3,2,1,0:T(8,128)(2,1)} %param.8), kind=kLoop, calls=%fused_computation.2 | loop fusion | bytes 2097152 | tf_op jit(solution)/shard_map/slice | solution.py:184
  5.4 1.3 %collective-permute-done.refs_1_ = bf16[128,256]{1,0:T(8,128)(2,1)S(1)} collective-permute-done((bf16[128,256]{1,0:T(8,128)(2,1)S(1)}, bf16[128,256]{1,0:T(8,128)(2,1)S(1)}, u32[]{:S(2)}, u32[]{:S(2)}) %collective-permute-start) | collective-permute-done | bytes 65568 | tf_op jit(solution)/shard_map/ppermute | solution.py:18
  6.7 1.2 %collective-permute-done.2.refs_3_ = bf16[128,256]{1,0:T(8,128)(2,1)S(1)} collective-permute-done((bf16[128,256]{1,0:T(8,128)(2,1)S(1)}, bf16[128,256]{1,0:T(8,128)(2,1)S(1)}, u32[]{:S(2)}, u32[]{:S(2)}) %collective-permute-start.2) | collective-permute-done | bytes 65568 | tf_op jit(solution)/shard_map/ppermute | solution.py:18
  7.9 1.1 %shard_map.64 = (bf16[2,256,512]{2,1,0:T(8,128)(2,1)S(1)}, bf16[1,256,512]{2,1,0:T(8,128)(2,1)S(1)}, bf16[1,256,512]{2,1,0:T(8,128)(2,1)S(1)}, bf16[1,256,512]{2,1,0:T(8,128)(2,1)S(1)}, bf16[2304,256]{1,0:T(8,128)(2,1)S(1)}) custom-call(s32[2,8,8]{2,1,0:T(8,128)S(1)} %copy-done.1, ...), custom_call_target="tpu_custom_call", output_to_operand_aliasing={{4}: (6, {})} | custom-call | flops 134217728 | bytes 4456448 | tf_op jit(solution)/shard_map/pallas_call | solution.py:51
  9.0 1.8 %collective-permute-start.7 = (bf16[2304,256]{1,0:T(8,128)(2,1)S(1)}, bf16[2304,256]{1,0:T(8,128)(2,1)S(1)}, u32[]{:S(2)}, u32[]{:S(2)}) collective-permute-start(bf16[2304,256]{1,0:T(8,128)(2,1)S(1)} %get-tuple-element.37.refs_3_), channel_id=1, source_target_pairs={{0,2},{1,3},{2,0},{3,1},{4,6},{5,7},{6,4},{7,5},{8,10},{9,11},{10,... | collective-permute-start | bytes 3538952 | tf_op jit(solution)/shard_map/ppermute | solution.py:18
  10.8 2.6 %collective-permute-start.3 = (bf16[2,256,512]{2,1,0:T(8,128)(2,1)S(1)}, bf16[2,256,512]{2,1,0:T(8,128)(2,1)S(1)}, u32[]{:S(2)}, u32[]{:S(2)}) collective-permute-start(bf16[2,256,512]{2,1,0:T(8,128)(2,1)S(1)} %get-tuple-element.33.refs_4_.refs_20_), channel_id=1, source_target_pairs={{0,16},{4,20},{8,24},{12,28},{16,0},{20,4},{24,8},{28,12},{1,17},{... | collective-permute-start | bytes 1572872 | tf_op jit(solution)/shard_map/ppermute | solution.py:18
  13.4 1.5 %collective-permute-start.4 = (bf16[1,256,512]{2,1,0:T(8,128)(2,1)S(1)}, bf16[1,256,512]{2,1,0:T(8,128)(2,1)S(1)}, u32[]{:S(2)}, u32[]{:S(2)}) collective-permute-start(bf16[1,256,512]{2,1,0:T(8,128)(2,1)S(1)} %get-tuple-element.34), channel_id=1, source_target_pairs={{0,4},{4,0},{8,12},{12,8},{16,20},{20,16},{24,28},{28,24},{1,5},{5... | collective-permute-start | bytes 786440 | tf_op jit(solution)/shard_map/ppermute | solution.py:18
  15.0 1.6 %collective-permute-start.5 = (bf16[1,256,512]{2,1,0:T(8,128)(2,1)S(1)}, bf16[1,256,512]{2,1,0:T(8,128)(2,1)S(1)}, u32[]{:S(2)}, u32[]{:S(2)}) collective-permute-start(bf16[1,256,512]{2,1,0:T(8,128)(2,1)S(1)} %get-tuple-element.35), channel_id=1, source_target_pairs={{0,8},{4,12},{8,0},{12,4},{16,24},{20,28},{24,16},{28,20},{1,9},{5... | collective-permute-start | bytes 786440 | tf_op jit(solution)/shard_map/ppermute | solution.py:18
  16.9 4.9 %collective-permute-done.4.refs_0_.refs_5_ = bf16[1,256,512]{2,1,0:T(8,128)(2,1)S(1)} collective-permute-done((bf16[1,256,512]{2,1,0:T(8,128)(2,1)S(1)}, bf16[1,256,512]{2,1,0:T(8,128)(2,1)S(1)}, u32[]{:S(2)}, u32[]{:S(2)}) %collective-permute-start.4) | collective-permute-done | bytes 262176 | tf_op jit(solution)/shard_map/ppermute | solution.py:18
  21.8 9.6 %collective-permute-done.5.refs_1_.refs_6_ = bf16[1,256,512]{2,1,0:T(8,128)(2,1)S(1)} collective-permute-done((bf16[1,256,512]{2,1,0:T(8,128)(2,1)S(1)}, bf16[1,256,512]{2,1,0:T(8,128)(2,1)S(1)}, u32[]{:S(2)}, u32[]{:S(2)}) %collective-permute-start.5) | collective-permute-done | bytes 262176 | tf_op jit(solution)/shard_map/ppermute | solution.py:18
  31.4 6.7 %collective-permute-done.6.refs_2_.refs_7_ = bf16[1,256,512]{2,1,0:T(8,128)(2,1)S(1)} collective-permute-done((bf16[1,256,512]{2,1,0:T(8,128)(2,1)S(1)}, bf16[1,256,512]{2,1,0:T(8,128)(2,1)S(1)}, u32[]{:S(2)}, u32[]{:S(2)}) %collective-permute-start.6) | collective-permute-done | bytes 262176 | tf_op jit(solution)/shard_map/ppermute | solution.py:18
  39.5 1.5 %collective-permute-start.13 = (bf16[1,256,256]{2,1,0:T(8,128)(2,1)S(1)}, bf16[1,256,256]{2,1,0:T(8,128)(2,1)S(1)}, u32[]{:S(2)}, u32[]{:S(2)}) collective-permute-start(bf16[1,256,256]{2,1,0:T(8,128)(2,1)S(1)} %get-tuple-element.48), channel_id=1, source_target_pairs={{0,4},{4,0},{8,12},{12,8},{16,20},{20,16},{24,28},{28,24},{1,5},{5... | collective-permute-start | bytes 393224 | tf_op jit(solution)/shard_map/ppermute | solution.py:18
  41.8 1.2 %collective-permute-start.15 = (bf16[1,256,256]{2,1,0:T(8,128)(2,1)S(1)}, bf16[1,256,256]{2,1,0:T(8,128)(2,1)S(1)}, u32[]{:S(2)}, u32[]{:S(2)}) collective-permute-start(bf16[1,256,256]{2,1,0:T(8,128)(2,1)S(1)} %get-tuple-element.50), channel_id=1, source_target_pairs={{0,12},{4,8},{8,4},{12,0},{16,28},{20,24},{24,20},{28,16},{1,13},{... | collective-permute-start | bytes 393224 | tf_op jit(solution)/shard_map/ppermute | solution.py:18
  43.6 1.6 %collective-permute-start.10 = (bf16[1,256,256]{2,1,0:T(8,128)(2,1)S(1)}, bf16[1,256,256]{2,1,0:T(8,128)(2,1)S(1)}, u32[]{:S(2)}, u32[]{:S(2)}) collective-permute-start(bf16[1,256,256]{2,1,0:T(8,128)(2,1)S(1)} %get-tuple-element.44), channel_id=1, source_target_pairs={{0,4},{4,0},{8,12},{12,8},{16,20},{20,16},{24,28},{28,24},{1,5},{5... | collective-permute-start | bytes 393224 | tf_op jit(solution)/shard_map/ppermute | solution.py:18
  45.9 1.2 %collective-permute-start.12 = (bf16[1,256,256]{2,1,0:T(8,128)(2,1)S(1)}, bf16[1,256,256]{2,1,0:T(8,128)(2,1)S(1)}, u32[]{:S(2)}, u32[]{:S(2)}) collective-permute-start(bf16[1,256,256]{2,1,0:T(8,128)(2,1)S(1)} %get-tuple-element.46), channel_id=1, source_target_pairs={{0,12},{4,8},{8,4},{12,0},{16,28},{20,24},{24,20},{28,16},{1,13},{... | collective-permute-start | bytes 393224 | tf_op jit(solution)/shard_map/ppermute | solution.py:18
  47.4 2.8 %collective-permute-done.15.refs_11_ = bf16[1,256,256]{2,1,0:T(8,128)(2,1)S(1)} collective-permute-done((bf16[1,256,256]{2,1,0:T(8,128)(2,1)S(1)}, bf16[1,256,256]{2,1,0:T(8,128)(2,1)S(1)}, u32[]{:S(2)}, u32[]{:S(2)}) %collective-permute-start.15) | collective-permute-done | bytes 131104 | tf_op jit(solution)/shard_map/ppermute | solution.py:18
  50.2 2.4 %shard_map.67.refs_12_.refs_21_ = bf16[2,256,256]{2,1,0:T(8,128)(2,1)S(1)} custom-call(s32[2,8,8]{2,1,0:T(8,128)S(1)} %copy-done.1, s32[2,2,8]{2,1,0:T(2,128)S(1)} %copy-done.2, s32[2,2]{1,0:T(2,128)S(1)} %copy-done.3, bf16[3,2,256,512]{3,2,1,0:T(8,128)(2,1)S(1)} %copy-done, bf16[2,256,256]{2,1,0:T(8,128)(2,1)S(1)} %get-tuple-element.47.inv, ...), custom_call_target="tpu_custom_call" | custom-call | flops 603979776 | bytes 9043968 | tf_op jit(solution)/shard_map/pallas_call | solution.py:51
  52.6 1.7 %collective-permute-start.23 = (bf16[2,256,256]{2,1,0:T(8,128)(2,1)S(1)}, bf16[2,256,256]{2,1,0:T(8,128)(2,1)S(1)}, u32[]{:S(2)}, u32[]{:S(2)}) collective-permute-start(bf16[2,256,256]{2,1,0:T(8,128)(2,1)S(1)} %shard_map.67.refs_12_.refs_21_), channel_id=1, source_target_pairs={{0,16},{4,20},{8,24},{12,28},{16,0},{20,4},{24,8},{28,12},{1,17},{... | collective-permute-start | bytes 786440 | tf_op jit(solution)/shard_map/ppermute | solution.py:18
  54.6 2.4 %shard_map.68 = (bf16[2,256,256]{2,1,0:T(8,128)(2,1)S(1)}, bf16[2,256,256]{2,1,0:T(8,128)(2,1)S(1)}, bf16[2,256,256]{2,1,0:T(8,128)(2,1)S(1)}, bf16[2,256,256]{2,1,0:T(8,128)(2,1)S(1)}) custom-call(s32[2,8,8]{2,1,0:T(8,128)S(1)} %copy-done.1, s32[2,2,8]{2,1,0:T(2,128)S(1)} %copy-done.2, s32[2,2]{1,0:T(2,128)S(1)} %copy-done.3, ...), custom_call_target="tpu_custom_call" | custom-call | flops 603979776 | bytes 10092544 | tf_op jit(solution)/shard_map/pallas_call | solution.py:51
  57.0 3.2 %collective-permute-start.16 = (bf16[2,256,256]{2,1,0:T(8,128)(2,1)S(1)}, bf16[2,256,256]{2,1,0:T(8,128)(2,1)S(1)}, u32[]{:S(2)}, u32[]{:S(2)}) collective-permute-start(bf16[2,256,256]{2,1,0:T(8,128)(2,1)S(1)} %get-tuple-element.52), channel_id=1, source_target_pairs={{0,4},{4,0},{8,12},{12,8},{16,20},{20,16},{24,28},{28,24},{1,5},{5... | collective-permute-start | bytes 786440 | tf_op jit(solution)/shard_map/ppermute | solution.py:18
  60.2 1.5 %collective-permute-start.18 = (bf16[2,256,256]{2,1,0:T(8,128)(2,1)S(1)}, bf16[2,256,256]{2,1,0:T(8,128)(2,1)S(1)}, u32[]{:S(2)}, u32[]{:S(2)}) collective-permute-start(bf16[2,256,256]{2,1,0:T(8,128)(2,1)S(1)} %get-tuple-element.54), channel_id=1, source_target_pairs={{0,12},{4,8},{8,4},{12,0},{16,28},{20,24},{24,20},{28,16},{1,13},{... | collective-permute-start | bytes 786440 | tf_op jit(solution)/shard_map/ppermute | solution.py:18
  61.8 1.4 %collective-permute-start.19 = (bf16[2,256,256]{2,1,0:T(8,128)(2,1)S(1)}, bf16[2,256,256]{2,1,0:T(8,128)(2,1)S(1)}, u32[]{:S(2)}, u32[]{:S(2)}) collective-permute-start(bf16[2,256,256]{2,1,0:T(8,128)(2,1)S(1)} %get-tuple-element.51.refs_12_.refs_22_), channel_id=1, source_target_pairs={{0,16},{4,20},{8,24},{12,28},{16,0},{20,4},{24,8},{28,12},{1,17},{... | collective-permute-start | bytes 786440 | tf_op jit(solution)/shard_map/ppermute | solution.py:18
  63.2 4.1 %collective-permute-done.23.far.refs_16_ = bf16[2,256,256]{2,1,0:T(8,128)(2,1)S(1)} collective-permute-done((bf16[2,256,256]{2,1,0:T(8,128)(2,1)S(1)}, bf16[2,256,256]{2,1,0:T(8,128)(2,1)S(1)}, u32[]{:S(2)}, u32[]{:S(2)}) %collective-permute-start.23) | collective-permute-done | bytes 262176 | tf_op jit(solution)/shard_map/ppermute | solution.py:18
  68.7 7.8 %collective-permute-done.17.refs_1_.refs_14_ = bf16[2,256,256]{2,1,0:T(8,128)(2,1)S(1)} collective-permute-done((bf16[2,256,256]{2,1,0:T(8,128)(2,1)S(1)}, bf16[2,256,256]{2,1,0:T(8,128)(2,1)S(1)}, u32[]{:S(2)}, u32[]{:S(2)}) %collective-permute-start.17) | collective-permute-done | bytes 262176 | tf_op jit(solution)/shard_map/ppermute | solution.py:18
  77.0 6.1 %collective-permute-done.18.refs_2_.refs_15_ = bf16[2,256,256]{2,1,0:T(8,128)(2,1)S(1)} collective-permute-done((bf16[2,256,256]{2,1,0:T(8,128)(2,1)S(1)}, bf16[2,256,256]{2,1,0:T(8,128)(2,1)S(1)}, u32[]{:S(2)}, u32[]{:S(2)}) %collective-permute-start.18) | collective-permute-done | bytes 262176 | tf_op jit(solution)/shard_map/ppermute | solution.py:18
  84.4 3.0 %collective-permute-start.22 = (bf16[1,256,256]{2,1,0:T(8,128)(2,1)S(1)}, bf16[1,256,256]{2,1,0:T(8,128)(2,1)S(1)}, u32[]{:S(2)}, u32[]{:S(2)}) collective-permute-start(bf16[1,256,256]{2,1,0:T(8,128)(2,1)S(1)} %get-tuple-element.57), channel_id=1, source_target_pairs={{0,12},{4,8},{8,4},{12,0},{16,28},{20,24},{24,20},{28,16},{1,13},{... | collective-permute-start | bytes 393224 | tf_op jit(solution)/shard_map/ppermute | solution.py:18
  87.4 1.4 %collective-permute-done.26.refs_19_ = bf16[1,256,256]{2,1,0:T(8,128)(2,1)S(1)} collective-permute-done((bf16[1,256,256]{2,1,0:T(8,128)(2,1)S(1)}, bf16[1,256,256]{2,1,0:T(8,128)(2,1)S(1)}, u32[]{:S(2)}, u32[]{:S(2)}) %collective-permute-start.26) | collective-permute-done | bytes 131104 | tf_op jit(solution)/shard_map/ppermute | solution.py:18
  88.8 2.5 %shard_map.71.refs_23_ = bf16[2,256,256]{2,1,0:T(8,128)(2,1)S(1)} custom-call(s32[2,8,8]{2,1,0:T(8,128)S(1)} %copy-done.1, s32[2,2,8]{2,1,0:T(2,128)S(1)} %copy-done.2, s32[2,2]{1,0:T(2,128)S(1)} %copy-done.3, bf16[3,2,256,512]{3,2,1,0:T(8,128)(2,1)S(1)} %copy-done, bf16[2,256,256]{2,1,0:T(8,128)(2,1)S(1)} %get-tuple-element.43.inv, ...), custom_call_target="tpu_custom_call" | custom-call | flops 603979776 | bytes 10747904 | tf_op jit(solution)/shard_map/pallas_call | solution.py:51
  91.3 1.1 %collective-permute-done.22.refs_19_ = bf16[1,256,256]{2,1,0:T(8,128)(2,1)S(1)} collective-permute-done((bf16[1,256,256]{2,1,0:T(8,128)(2,1)S(1)}, bf16[1,256,256]{2,1,0:T(8,128)(2,1)S(1)}, u32[]{:S(2)}, u32[]{:S(2)}) %collective-permute-start.22) | collective-permute-done | bytes 131104 | tf_op jit(solution)/shard_map/ppermute | solution.py:18
  92.4 3.2 %shard_map.72 = bf16[3,2,256,512]{3,2,1,0:T(8,128)(2,1)} custom-call(s32[2,8,8]{2,1,0:T(8,128)S(1)} %copy-done.1, s32[2,2,8]{2,1,0:T(2,128)S(1)} %copy-done.2, s32[2,2]{1,0:T(2,128)S(1)} %copy-done.3, bf16[3,2,256,512]{3,2,1,0:T(8,128)(2,1)S(1)} %copy-done, bf16[2,256,256]{2,1,0:T(8,128)(2,1)S(1)} %get-tuple-element.43.inv, ...), custom_call_target="tpu_custom_call" | custom-call | flops 603979776 | bytes 13369344 | tf_op jit(solution)/shard_map/pallas_call | solution.py:51
  (43 shorter events, 8.4 us)
Async XLA Ops:
  0.9 5.8 %collective-permute-start.1 = (bf16[128,256]{1,0:T(8,128)(2,1)S(1)}, bf16[128,256]{1,0:T(8,128)(2,1)S(1)}, u32[]{:S(2)}, u32[]{:S(2)}) collective-permute-start(bf16[128,256]{1,0:T(8,128)(2,1)S(1)} %bitcast.7), channel_id=1, source_target_pairs={{0,1},{1,0},{2,3},{3,2},{4,5},{5,4},{6,7},{7,6},{8,9},{9,8},{10,11... | collective-permute-start | bytes 196616 | tf_op jit(solution)/shard_map/ppermute | solution.py:18
  1.4 5.3 %collective-permute-start = (bf16[128,256]{1,0:T(8,128)(2,1)S(1)}, bf16[128,256]{1,0:T(8,128)(2,1)S(1)}, u32[]{:S(2)}, u32[]{:S(2)}) collective-permute-start(bf16[128,256]{1,0:T(8,128)(2,1)S(1)} %bitcast.8), channel_id=1, source_target_pairs={{0,2},{1,3},{2,0},{3,1},{4,6},{5,7},{6,4},{7,5},{8,10},{9,11},{10,... | collective-permute-start | bytes 196616 | tf_op jit(solution)/shard_map/ppermute | solution.py:18
  5.3 1.4 %copy-start = (bf16[3,2,256,512]{3,2,1,0:T(8,128)(2,1)S(1)}, bf16[3,2,256,512]{3,2,1,0:T(8,128)(2,1)}, u32[]{:S(2)}) copy-start(bf16[3,2,256,512]{3,2,1,0:T(8,128)(2,1)} %noise.7) | copy-start | bytes 4718596
  5.3 2.7 %copy-start.1 = (s32[2,8,8]{2,1,0:T(8,128)S(1)}, s32[2,8,8]{2,1,0:T(8,128)}, u32[]{:S(2)}) copy-start(s32[2,8,8]{2,1,0:T(8,128)} %picks.15) | copy-start | bytes 1540
  6.7 1.3 %collective-permute-start.2 = (bf16[128,256]{1,0:T(8,128)(2,1)S(1)}, bf16[128,256]{1,0:T(8,128)(2,1)S(1)}, u32[]{:S(2)}, u32[]{:S(2)}) collective-permute-start(bf16[128,256]{1,0:T(8,128)(2,1)S(1)} %collective-permute-done.refs_1_), channel_id=1, source_target_pairs={{0,1},{1,0},{2,3},{3,2},{4,5},{5,4},{6,7},{7,6},{8,9},{9,8},{10,11... | collective-permute-start | bytes 196616 | tf_op jit(solution)/shard_map/ppermute | solution.py:18
  9.0 29.1 %collective-permute-start.7 = (bf16[2304,256]{1,0:T(8,128)(2,1)S(1)}, bf16[2304,256]{1,0:T(8,128)(2,1)S(1)}, u32[]{:S(2)}, u32[]{:S(2)}) collective-permute-start(bf16[2304,256]{1,0:T(8,128)(2,1)S(1)} %get-tuple-element.37.refs_3_), channel_id=1, source_target_pairs={{0,2},{1,3},{2,0},{3,1},{4,6},{5,7},{6,4},{7,5},{8,10},{9,11},{10,... | collective-permute-start | bytes 3538952 | tf_op jit(solution)/shard_map/ppermute | solution.py:18
  10.8 27.3 %collective-permute-start.3 = (bf16[2,256,512]{2,1,0:T(8,128)(2,1)S(1)}, bf16[2,256,512]{2,1,0:T(8,128)(2,1)S(1)}, u32[]{:S(2)}, u32[]{:S(2)}) collective-permute-start(bf16[2,256,512]{2,1,0:T(8,128)(2,1)S(1)} %get-tuple-element.33.refs_4_.refs_20_), channel_id=1, source_target_pairs={{0,16},{4,20},{8,24},{12,28},{16,0},{20,4},{24,8},{28,12},{1,17},{... | collective-permute-start | bytes 1572872 | tf_op jit(solution)/shard_map/ppermute | solution.py:18
  13.4 8.3 %collective-permute-start.4 = (bf16[1,256,512]{2,1,0:T(8,128)(2,1)S(1)}, bf16[1,256,512]{2,1,0:T(8,128)(2,1)S(1)}, u32[]{:S(2)}, u32[]{:S(2)}) collective-permute-start(bf16[1,256,512]{2,1,0:T(8,128)(2,1)S(1)} %get-tuple-element.34), channel_id=1, source_target_pairs={{0,4},{4,0},{8,12},{12,8},{16,20},{20,16},{24,28},{28,24},{1,5},{5... | collective-permute-start | bytes 786440 | tf_op jit(solution)/shard_map/ppermute | solution.py:18
  15.0 16.5 %collective-permute-start.5 = (bf16[1,256,512]{2,1,0:T(8,128)(2,1)S(1)}, bf16[1,256,512]{2,1,0:T(8,128)(2,1)S(1)}, u32[]{:S(2)}, u32[]{:S(2)}) collective-permute-start(bf16[1,256,512]{2,1,0:T(8,128)(2,1)S(1)} %get-tuple-element.35), channel_id=1, source_target_pairs={{0,8},{4,12},{8,0},{12,4},{16,24},{20,28},{24,16},{28,20},{1,9},{5... | collective-permute-start | bytes 786440 | tf_op jit(solution)/shard_map/ppermute | solution.py:18
  16.5 21.6 %collective-permute-start.6 = (bf16[1,256,512]{2,1,0:T(8,128)(2,1)S(1)}, bf16[1,256,512]{2,1,0:T(8,128)(2,1)S(1)}, u32[]{:S(2)}, u32[]{:S(2)}) collective-permute-start(bf16[1,256,512]{2,1,0:T(8,128)(2,1)S(1)} %get-tuple-element.36), channel_id=1, source_target_pairs={{0,12},{4,8},{8,4},{12,0},{16,28},{20,24},{24,20},{28,16},{1,13},{... | collective-permute-start | bytes 786440 | tf_op jit(solution)/shard_map/ppermute | solution.py:18
  38.9 4.1 %collective-permute-start.8 = (bf16[2304,256]{1,0:T(8,128)(2,1)S(1)}, bf16[2304,256]{1,0:T(8,128)(2,1)S(1)}, u32[]{:S(2)}, u32[]{:S(2)}) collective-permute-start(bf16[2304,256]{1,0:T(8,128)(2,1)S(1)} %get-tuple-element.38.refs_0_), channel_id=1, source_target_pairs={{0,1},{1,0},{2,3},{3,2},{4,5},{5,4},{6,7},{7,6},{8,9},{9,8},{10,11... | collective-permute-start | bytes 3538952 | tf_op jit(solution)/shard_map/ppermute | solution.py:18
  39.0 4.5 %collective-permute-start.9 = (bf16[2304,256]{1,0:T(8,128)(2,1)S(1)}, bf16[2304,256]{1,0:T(8,128)(2,1)S(1)}, u32[]{:S(2)}, u32[]{:S(2)}) collective-permute-start(bf16[2304,256]{1,0:T(8,128)(2,1)S(1)} %get-tuple-element.39.refs_1_), channel_id=1, source_target_pairs={{0,1},{1,0},{2,3},{3,2},{4,5},{5,4},{6,7},{7,6},{8,9},{9,8},{10,11... | collective-permute-start | bytes 3538952 | tf_op jit(solution)/shard_map/ppermute | solution.py:18
  39.5 6.4 %collective-permute-start.13 = (bf16[1,256,256]{2,1,0:T(8,128)(2,1)S(1)}, bf16[1,256,256]{2,1,0:T(8,128)(2,1)S(1)}, u32[]{:S(2)}, u32[]{:S(2)}) collective-permute-start(bf16[1,256,256]{2,1,0:T(8,128)(2,1)S(1)} %get-tuple-element.48), channel_id=1, source_target_pairs={{0,4},{4,0},{8,12},{12,8},{16,20},{20,16},{24,28},{28,24},{1,5},{5... | collective-permute-start | bytes 393224 | tf_op jit(solution)/shard_map/ppermute | solution.py:18
  41.0 6.4 %collective-permute-start.14 = (bf16[1,256,256]{2,1,0:T(8,128)(2,1)S(1)}, bf16[1,256,256]{2,1,0:T(8,128)(2,1)S(1)}, u32[]{:S(2)}, u32[]{:S(2)}) collective-permute-start(bf16[1,256,256]{2,1,0:T(8,128)(2,1)S(1)} %get-tuple-element.49), channel_id=1, source_target_pairs={{0,8},{4,12},{8,0},{12,4},{16,24},{20,28},{24,16},{28,20},{1,9},{5... | collective-permute-start | bytes 393224 | tf_op jit(solution)/shard_map/ppermute | solution.py:18
  41.8 8.4 %collective-permute-start.15 = (bf16[1,256,256]{2,1,0:T(8,128)(2,1)S(1)}, bf16[1,256,256]{2,1,0:T(8,128)(2,1)S(1)}, u32[]{:S(2)}, u32[]{:S(2)}) collective-permute-start(bf16[1,256,256]{2,1,0:T(8,128)(2,1)S(1)} %get-tuple-element.50), channel_id=1, source_target_pairs={{0,12},{4,8},{8,4},{12,0},{16,28},{20,24},{24,20},{28,16},{1,13},{... | collective-permute-start | bytes 393224 | tf_op jit(solution)/shard_map/ppermute | solution.py:18
  43.5 6.6 %copy-start.2 = (s32[2,2,8]{2,1,0:T(2,128)S(1)}, s32[2,2,8]{2,1,0:T(2,128)}, u32[]{:S(2)}) copy-start(s32[2,2,8]{2,1,0:T(2,128)} %lists.7) | copy-start | bytes 388
  43.5 6.6 %copy-start.3 = (s32[2,2]{1,0:T(2,128)S(1)}, s32[2,2]{1,0:T(2,128)}, u32[]{:S(2)}) copy-start(s32[2,2]{1,0:T(2,128)} %counts.7) | copy-start | bytes 52
  43.6 10.7 %collective-permute-start.10 = (bf16[1,256,256]{2,1,0:T(8,128)(2,1)S(1)}, bf16[1,256,256]{2,1,0:T(8,128)(2,1)S(1)}, u32[]{:S(2)}, u32[]{:S(2)}) collective-permute-start(bf16[1,256,256]{2,1,0:T(8,128)(2,1)S(1)} %get-tuple-element.44), channel_id=1, source_target_pairs={{0,4},{4,0},{8,12},{12,8},{16,20},{20,16},{24,28},{28,24},{1,5},{5... | collective-permute-start | bytes 393224 | tf_op jit(solution)/shard_map/ppermute | solution.py:18
  45.1 9.1 %collective-permute-start.11 = (bf16[1,256,256]{2,1,0:T(8,128)(2,1)S(1)}, bf16[1,256,256]{2,1,0:T(8,128)(2,1)S(1)}, u32[]{:S(2)}, u32[]{:S(2)}) collective-permute-start(bf16[1,256,256]{2,1,0:T(8,128)(2,1)S(1)} %get-tuple-element.45), channel_id=1, source_target_pairs={{0,8},{4,12},{8,0},{12,4},{16,24},{20,28},{24,16},{28,20},{1,9},{5... | collective-permute-start | bytes 393224 | tf_op jit(solution)/shard_map/ppermute | solution.py:18
  45.9 8.6 %collective-permute-start.12 = (bf16[1,256,256]{2,1,0:T(8,128)(2,1)S(1)}, bf16[1,256,256]{2,1,0:T(8,128)(2,1)S(1)}, u32[]{:S(2)}, u32[]{:S(2)}) collective-permute-start(bf16[1,256,256]{2,1,0:T(8,128)(2,1)S(1)} %get-tuple-element.46), channel_id=1, source_target_pairs={{0,12},{4,8},{8,4},{12,0},{16,28},{20,24},{24,20},{28,16},{1,13},{... | collective-permute-start | bytes 393224 | tf_op jit(solution)/shard_map/ppermute | solution.py:18
  52.6 14.7 %collective-permute-start.23 = (bf16[2,256,256]{2,1,0:T(8,128)(2,1)S(1)}, bf16[2,256,256]{2,1,0:T(8,128)(2,1)S(1)}, u32[]{:S(2)}, u32[]{:S(2)}) collective-permute-start(bf16[2,256,256]{2,1,0:T(8,128)(2,1)S(1)} %shard_map.67.refs_12_.refs_21_), channel_id=1, source_target_pairs={{0,16},{4,20},{8,24},{12,28},{16,0},{20,4},{24,8},{28,12},{1,17},{... | collective-permute-start | bytes 786440 | tf_op jit(solution)/shard_map/ppermute | solution.py:18
  57.0 11.7 %collective-permute-start.16 = (bf16[2,256,256]{2,1,0:T(8,128)(2,1)S(1)}, bf16[2,256,256]{2,1,0:T(8,128)(2,1)S(1)}, u32[]{:S(2)}, u32[]{:S(2)}) collective-permute-start(bf16[2,256,256]{2,1,0:T(8,128)(2,1)S(1)} %get-tuple-element.52), channel_id=1, source_target_pairs={{0,4},{4,0},{8,12},{12,8},{16,20},{20,16},{24,28},{28,24},{1,5},{5... | collective-permute-start | bytes 786440 | tf_op jit(solution)/shard_map/ppermute | solution.py:18
  60.2 16.2 %collective-permute-start.17 = (bf16[2,256,256]{2,1,0:T(8,128)(2,1)S(1)}, bf16[2,256,256]{2,1,0:T(8,128)(2,1)S(1)}, u32[]{:S(2)}, u32[]{:S(2)}) collective-permute-start(bf16[2,256,256]{2,1,0:T(8,128)(2,1)S(1)} %get-tuple-element.53), channel_id=1, source_target_pairs={{0,8},{4,12},{8,0},{12,4},{16,24},{20,28},{24,16},{28,20},{1,9},{5... | collective-permute-start | bytes 786440 | tf_op jit(solution)/shard_map/ppermute | solution.py:18
  60.2 22.9 %collective-permute-start.18 = (bf16[2,256,256]{2,1,0:T(8,128)(2,1)S(1)}, bf16[2,256,256]{2,1,0:T(8,128)(2,1)S(1)}, u32[]{:S(2)}, u32[]{:S(2)}) collective-permute-start(bf16[2,256,256]{2,1,0:T(8,128)(2,1)S(1)} %get-tuple-element.54), channel_id=1, source_target_pairs={{0,12},{4,8},{8,4},{12,0},{16,28},{20,24},{24,20},{28,16},{1,13},{... | collective-permute-start | bytes 786440 | tf_op jit(solution)/shard_map/ppermute | solution.py:18
  61.8 21.3 %collective-permute-start.19 = (bf16[2,256,256]{2,1,0:T(8,128)(2,1)S(1)}, bf16[2,256,256]{2,1,0:T(8,128)(2,1)S(1)}, u32[]{:S(2)}, u32[]{:S(2)}) collective-permute-start(bf16[2,256,256]{2,1,0:T(8,128)(2,1)S(1)} %get-tuple-element.51.refs_12_.refs_22_), channel_id=1, source_target_pairs={{0,16},{4,20},{8,24},{12,28},{16,0},{20,4},{24,8},{28,12},{1,17},{... | collective-permute-start | bytes 786440 | tf_op jit(solution)/shard_map/ppermute | solution.py:18
  68.0 16.4 %collective-permute-start.24 = (bf16[1,256,256]{2,1,0:T(8,128)(2,1)S(1)}, bf16[1,256,256]{2,1,0:T(8,128)(2,1)S(1)}, u32[]{:S(2)}, u32[]{:S(2)}) collective-permute-start(bf16[1,256,256]{2,1,0:T(8,128)(2,1)S(1)} %get-tuple-element.58), channel_id=1, source_target_pairs={{0,4},{4,0},{8,12},{12,8},{16,20},{20,16},{24,28},{28,24},{1,5},{5... | collective-permute-start | bytes 393224 | tf_op jit(solution)/shard_map/ppermute | solution.py:18
  68.7 18.7 %collective-permute-start.25 = (bf16[1,256,256]{2,1,0:T(8,128)(2,1)S(1)}, bf16[1,256,256]{2,1,0:T(8,128)(2,1)S(1)}, u32[]{:S(2)}, u32[]{:S(2)}) collective-permute-start(bf16[1,256,256]{2,1,0:T(8,128)(2,1)S(1)} %get-tuple-element.59), channel_id=1, source_target_pairs={{0,8},{4,12},{8,0},{12,4},{16,24},{20,28},{24,16},{28,20},{1,9},{5... | collective-permute-start | bytes 393224 | tf_op jit(solution)/shard_map/ppermute | solution.py:18
  76.5 12.3 %collective-permute-start.26 = (bf16[1,256,256]{2,1,0:T(8,128)(2,1)S(1)}, bf16[1,256,256]{2,1,0:T(8,128)(2,1)S(1)}, u32[]{:S(2)}, u32[]{:S(2)}) collective-permute-start(bf16[1,256,256]{2,1,0:T(8,128)(2,1)S(1)} %get-tuple-element.60), channel_id=1, source_target_pairs={{0,12},{4,8},{8,4},{12,0},{16,28},{20,24},{24,20},{28,16},{1,13},{... | collective-permute-start | bytes 393224 | tf_op jit(solution)/shard_map/ppermute | solution.py:18
  83.8 7.4 %collective-permute-start.20 = (bf16[1,256,256]{2,1,0:T(8,128)(2,1)S(1)}, bf16[1,256,256]{2,1,0:T(8,128)(2,1)S(1)}, u32[]{:S(2)}, u32[]{:S(2)}) collective-permute-start(bf16[1,256,256]{2,1,0:T(8,128)(2,1)S(1)} %get-tuple-element.55), channel_id=1, source_target_pairs={{0,4},{4,0},{8,12},{12,8},{16,20},{20,16},{24,28},{28,24},{1,5},{5... | collective-permute-start | bytes 393224 | tf_op jit(solution)/shard_map/ppermute | solution.py:18
  84.4 6.9 %collective-permute-start.21 = (bf16[1,256,256]{2,1,0:T(8,128)(2,1)S(1)}, bf16[1,256,256]{2,1,0:T(8,128)(2,1)S(1)}, u32[]{:S(2)}, u32[]{:S(2)}) collective-permute-start(bf16[1,256,256]{2,1,0:T(8,128)(2,1)S(1)} %get-tuple-element.56), channel_id=1, source_target_pairs={{0,8},{4,12},{8,0},{12,4},{16,24},{20,28},{24,16},{28,20},{1,9},{5... | collective-permute-start | bytes 393224 | tf_op jit(solution)/shard_map/ppermute | solution.py:18
  84.4 8.0 %collective-permute-start.22 = (bf16[1,256,256]{2,1,0:T(8,128)(2,1)S(1)}, bf16[1,256,256]{2,1,0:T(8,128)(2,1)S(1)}, u32[]{:S(2)}, u32[]{:S(2)}) collective-permute-start(bf16[1,256,256]{2,1,0:T(8,128)(2,1)S(1)} %get-tuple-element.57), channel_id=1, source_target_pairs={{0,12},{4,8},{8,4},{12,0},{16,28},{20,24},{24,20},{28,16},{1,13},{... | collective-permute-start | bytes 393224 | tf_op jit(solution)/shard_map/ppermute | solution.py:18

commit v22 on v21

--- a/solution.py
+++ b/solution.py
@@ -9,7 +9,6 @@
 
 CHUNKS = 2
 VMEM = pl.BlockSpec(memory_space=pltpu.VMEM)
-SMEM = pl.BlockSpec(memory_space=pltpu.SMEM)
 ANY = pl.BlockSpec(memory_space=pl.ANY)
 BF16, F32 = jnp.bfloat16, jnp.float32
 
@@ -46,18 +45,24 @@
     return jax.ShapeDtypeStruct(dims, BF16)
 
 
-def call(kernel, outs, scratch, small, arrays, out_spec=VMEM, flops=0, aliases={}):
+def entry_of(tile, row, column):
+    rows = lax.broadcasted_iota(jnp.int32, tile.shape, 0)
+    columns = lax.broadcasted_iota(jnp.int32, tile.shape, 1)
+    return jnp.sum(jnp.where((rows == row) & (columns == column), tile, 0))
+
+
+def call(kernel, outs, scratch, arrays, out_spec=VMEM, flops=0, aliases={}):
     size = sum(value.size * value.dtype.itemsize for value in (*arrays, *outs))
     return list(pl.pallas_call(
         kernel,
         out_shape=outs,
-        in_specs=[SMEM] * len(small) + [VMEM] * len(arrays),
+        in_specs=[VMEM] * len(arrays),
         out_specs=[out_spec] * len(outs),
         scratch_shapes=scratch,
         input_output_aliases=aliases,
         cost_estimate=pl.CostEstimate(flops=flops, bytes_accessed=size, transcendentals=0),
         compiler_params=pltpu.CompilerParams(vmem_limit_bytes=16 * 1024 * 1024),
-    )(*small, *arrays))
+    )(*arrays))
 
 
 def row_blocks(refs, held, block):
@@ -86,7 +91,7 @@
     for node in range(nodes):
         solved[node] = transposed_dot(inv[node], noise[node]).astype(BF16)
     for step, send in enumerate(sends, 1):
-        send[0] = solved[picks[0, myself ^ step, myself]]
+        send[0] = solved[entry_of(picks[0], myself ^ step, myself)]
 
 
 def relay_kernel(half, source, waits, through, picks, far, *refs):
@@ -95,14 +100,13 @@
     for at, send in enumerate(sends):
         chunk, step = divmod(at, half - 1)
         wide = send.shape[-1]
-        node = picks[source, myself ^ (step + 1), myself ^ half]
+        node = entry_of(picks[source], myself ^ (step + 1), myself ^ half)
         send[0] = far[node, :, chunk * wide:(chunk + 1) * wide]
 
 
-def inverse_kernel(held, span, *refs):
+def inverse_kernel(held, levels, span, *refs):
     packs, refs = take(refs, len(held))
     draw = lax.axis_index("draw")
-    levels = sum(ref.shape[0] > 1 for ref in refs)
     draws = sum(map(len, held))
     found = row_blocks(packs, held, levels * span)
     for level, target in enumerate(refs[-levels:]):
@@ -141,24 +145,29 @@
     for at, (ref, place) in enumerate(zip(known, places, strict=True)):
         step = at % owners
         if step % half == 0:
-            place = picks[at // owners, myself, myself ^ step]
+            place = entry_of(picks[at // owners], myself, myself ^ step)
         table[at] = ref[place] if ref.shape[-1] == wide else ref[place, :, columns]
     empty = level * owners
     table[empty] = jnp.zeros_like(table[empty])
+    entries = lists[level - 1]
+    slots = lax.broadcasted_iota(jnp.int32, entries.shape, 1)
+    live = jnp.zeros(entries.shape, jnp.int32)
+    for node in range(nodes):
+        here = lax.broadcasted_iota(jnp.int32, entries.shape, 0) == node
+        live = jnp.where(here, entry_of(counts[...], level - 1, node), live)
+    entries = jnp.where(slots < live, entries ^ myself, empty)
     for node in range(nodes):
         total = None
         for pack, start, step in found:
             for slot in range(width):
-                entry = (draw ^ step) * width + slot
-                live = entry < counts[level - 1, node]
-                entry = jnp.where(live, lists[level - 1, node, entry] ^ myself, empty)
+                entry = entry_of(entries, node, (draw ^ step) * width + slot)
                 at = start + offset + (node * width + slot) * depth
                 term = transposed_dot(pack[at:at + depth, :], table[entry])
                 total = term if total is None else total + term
         right_side = (noise[level, node, :, columns].astype(F32) - total).astype(BF16)
         solved[node] = transposed_dot(inv[node], right_side).astype(BF16)
     for step, send in enumerate(sends, 1):
-        node = picks[level, myself ^ step, myself]
+        node = entry_of(picks[level], myself ^ step, myself)
         for at, ref in enumerate([*chunks, solved]):
             send[at] = ref[node]
     if done:
@@ -189,8 +198,7 @@
         functools.partial(first_kernel, steps),
         [shape(nodes, rows, columns)] + [shape(1, rows, columns)] * (half - 1) + [shape(*raw.shape)],
         [inv_here],
-        (picks,),
-        (noise[0], *values, raw),
+        (picks, noise[0], *values, raw),
         flops=nodes * CHUNKS * dot_flops,
         aliases={2 + len(values): half},
     )
@@ -200,8 +208,7 @@
         functools.partial(relay_kernel, half, 0, len(got), len(values)),
         [shape(1, rows, wide)] * (CHUNKS * (half - 1)) + [shape(*value.shape) for value in values],
         [],
-        (picks,),
-        (far, *got, *values),
+        (picks, far, *got, *values),
         aliases={2 + len(got) + at: CHUNKS * (half - 1) + at for at in range(len(values))},
     )
     sends, values = take(sends, CHUNKS * (half - 1))
@@ -209,10 +216,9 @@
     first, later = take(sends, half - 1)
     span = nodes * (width * rows + inverse.shape[2])
     outs = call(
-        functools.partial(inverse_kernel, steps, span),
+        functools.partial(inverse_kernel, steps, levels - 1, span),
         [shape(*value.shape) for value in later] + [shape(nodes, rows, rows)] * (levels - 1),
         [],
-        (),
         (*packs, *later),
         aliases={len(packs) + at: at for at in range(len(later))},
     )
@@ -248,8 +254,7 @@
                 ),
                 [shape(*noise.shape) if final else part] + [shape(CHUNKS, rows, wide)] * sides,
                 scratch,
-                (picks, lists, counts),
-                (noise, inverses[level - 1], *packs, *(ref for ref, _ in known), *(ref for ref, _ in stored), *mates),
+                (picks, lists, counts, noise, inverses[level - 1], *packs, *(ref for ref, _ in known), *(ref for ref, _ in stored), *mates),
                 out_spec=ANY if final else VMEM,
                 flops=nodes * (draws * width + 1) * dot_flops,
             )
@@ -267,8 +272,7 @@
                 functools.partial(relay_kernel, half, level, len(waits), 0),
                 [shape(1, rows, wide)] * (half - 1),
                 [],
-                (picks,),
-                (far[at], *waits),
+                (picks, far[at], *waits),
             )
             pieces[level].append([
                 (solved[at], 0), *((ref, at) for ref in got),

time: 95.8 us -> 93.2 us (0.973)
  Pallas kernels: 13.7 us -> 9.54 us
  waiting for transfers between devices: 48.2 us -> 50.2 us
    pallas_call x9, Pallas kernels: 13.7 us -> 9.54 us  [call(): pl.pallas_call(kernel, out_shape=outs, in_specs=[VMEM] * len(arrays), out...]
    ppermute x27, waiting for transfers between devices: 48.2 us -> 50.2 us  [hop(): return lax.ppermute(value, axis, [(at, at ^ step) for at in range(size)])]
  transfers between devices with their start and end apart: 27 -> 27, of which waited for: 14 -> 14; matrix products, arithmetic and copies ran while one was open for 1% -> 1% of each run, Pallas kernels for 9% -> 7%
where the time goes in v22:
time: 93.2 us; the launch traced here: 93 us
  waiting for transfers between devices  50.2 us (54%)
  starting transfers between devices  30.8 us (33%)
  Pallas kernels  9.54 us (10%)
  local copies, waits for them, and re-layouts  2.24 us (2%)
    ppermute x27, waiting for transfers between devices, hop(): return lax.ppermute(value, axis, [(at, at ^ step) for at in range(size)])  50.2 us
    ppermute x27, starting transfers between devices, hop(): return lax.ppermute(value, axis, [(at, at ^ step) for at in range(size)])  30.8 us
    pallas_call x9, Pallas kernels, call(): pl.pallas_call(kernel, out_shape=outs, in_specs=[VMEM] * len(arrays), out...  9.54 us
  transfers between devices with their start and end apart: 27, of which 14 were waited for; matrix products, arithmetic and copies ran while one was open for 1% of the time, Pallas kernels for 7%

profile of v22, /device:TPU:0, one launch (start us, length us, event | category | flops | bytes accessed | tf_op | source)
XLA Modules:
  0.0 93.0 jit_solution(8084303698973482353)
XLA Ops:
  0.0 0.9 fusion.1
  1.4 2.6 %collective-permute-start = (bf16[128,256]{1,0:T(8,128)(2,1)S(1)}, bf16[128,256]{1,0:T(8,128)(2,1)S(1)}, u32[]{:S(2)}, u32[]{:S(2)}) collective-permute-start(bf16[128,256]{1,0:T(8,128)(2,1)S(1)} %bitcast.8), channel_id=1, source_target_pairs={{0,2},{1,3},{2,0},{3,1},{4,6},{5,7},{6,4},{7,5},{8,10},{9,11},{10,... | collective-permute-start | bytes 196616 | tf_op jit(solution)/shard_map/ppermute | solution.py:17
  4.0 1.3 %fusion = (bf16[1,2,2,256,256]{4,3,2,1,0:T(8,128)(2,1)S(1)}, bf16[1,2,2,256,256]{4,3,2,1,0:T(8,128)(2,1)S(1)}) fusion(bf16[2,2,2,256,256]{4,3,2,1,0:T(8,128)(2,1)} %param.8), kind=kLoop, calls=%fused_computation.2 | loop fusion | bytes 2097152 | tf_op jit(solution)/shard_map/slice | solution.py:193
  5.4 1.3 %collective-permute-done.refs_1_ = bf16[128,256]{1,0:T(8,128)(2,1)S(1)} collective-permute-done((bf16[128,256]{1,0:T(8,128)(2,1)S(1)}, bf16[128,256]{1,0:T(8,128)(2,1)S(1)}, u32[]{:S(2)}, u32[]{:S(2)}) %collective-permute-start) | collective-permute-done | bytes 65568 | tf_op jit(solution)/shard_map/ppermute | solution.py:17
  6.7 1.2 %collective-permute-done.2.refs_3_ = bf16[128,256]{1,0:T(8,128)(2,1)S(1)} collective-permute-done((bf16[128,256]{1,0:T(8,128)(2,1)S(1)}, bf16[128,256]{1,0:T(8,128)(2,1)S(1)}, u32[]{:S(2)}, u32[]{:S(2)}) %collective-permute-start.2) | collective-permute-done | bytes 65568 | tf_op jit(solution)/shard_map/ppermute | solution.py:17
  8.4 1.8 %collective-permute-start.7 = (bf16[2304,256]{1,0:T(8,128)(2,1)S(1)}, bf16[2304,256]{1,0:T(8,128)(2,1)S(1)}, u32[]{:S(2)}, u32[]{:S(2)}) collective-permute-start(bf16[2304,256]{1,0:T(8,128)(2,1)S(1)} %get-tuple-element.37.refs_3_), channel_id=1, source_target_pairs={{0,2},{1,3},{2,0},{3,1},{4,6},{5,7},{6,4},{7,5},{8,10},{9,11},{10,... | collective-permute-start | bytes 3538952 | tf_op jit(solution)/shard_map/ppermute | solution.py:17
  10.2 2.6 %collective-permute-start.3 = (bf16[2,256,512]{2,1,0:T(8,128)(2,1)S(1)}, bf16[2,256,512]{2,1,0:T(8,128)(2,1)S(1)}, u32[]{:S(2)}, u32[]{:S(2)}) collective-permute-start(bf16[2,256,512]{2,1,0:T(8,128)(2,1)S(1)} %get-tuple-element.33.refs_4_.refs_20_), channel_id=1, source_target_pairs={{0,16},{4,20},{8,24},{12,28},{16,0},{20,4},{24,8},{28,12},{1,17},{... | collective-permute-start | bytes 1572872 | tf_op jit(solution)/shard_map/ppermute | solution.py:17
  12.8 1.5 %collective-permute-start.4 = (bf16[1,256,512]{2,1,0:T(8,128)(2,1)S(1)}, bf16[1,256,512]{2,1,0:T(8,128)(2,1)S(1)}, u32[]{:S(2)}, u32[]{:S(2)}) collective-permute-start(bf16[1,256,512]{2,1,0:T(8,128)(2,1)S(1)} %get-tuple-element.34), channel_id=1, source_target_pairs={{0,4},{4,0},{8,12},{12,8},{16,20},{20,16},{24,28},{28,24},{1,5},{5... | collective-permute-start | bytes 786440 | tf_op jit(solution)/shard_map/ppermute | solution.py:17
  14.3 1.6 %collective-permute-start.5 = (bf16[1,256,512]{2,1,0:T(8,128)(2,1)S(1)}, bf16[1,256,512]{2,1,0:T(8,128)(2,1)S(1)}, u32[]{:S(2)}, u32[]{:S(2)}) collective-permute-start(bf16[1,256,512]{2,1,0:T(8,128)(2,1)S(1)} %get-tuple-element.35), channel_id=1, source_target_pairs={{0,8},{4,12},{8,0},{12,4},{16,24},{20,28},{24,16},{28,20},{1,9},{5... | collective-permute-start | bytes 786440 | tf_op jit(solution)/shard_map/ppermute | solution.py:17
  16.3 4.9 %collective-permute-done.4.refs_0_.refs_5_ = bf16[1,256,512]{2,1,0:T(8,128)(2,1)S(1)} collective-permute-done((bf16[1,256,512]{2,1,0:T(8,128)(2,1)S(1)}, bf16[1,256,512]{2,1,0:T(8,128)(2,1)S(1)}, u32[]{:S(2)}, u32[]{:S(2)}) %collective-permute-start.4) | collective-permute-done | bytes 262176 | tf_op jit(solution)/shard_map/ppermute | solution.py:17
  21.1 9.6 %collective-permute-done.5.refs_1_.refs_6_ = bf16[1,256,512]{2,1,0:T(8,128)(2,1)S(1)} collective-permute-done((bf16[1,256,512]{2,1,0:T(8,128)(2,1)S(1)}, bf16[1,256,512]{2,1,0:T(8,128)(2,1)S(1)}, u32[]{:S(2)}, u32[]{:S(2)}) %collective-permute-start.5) | collective-permute-done | bytes 262176 | tf_op jit(solution)/shard_map/ppermute | solution.py:17
  30.8 6.7 %collective-permute-done.6.refs_2_.refs_7_ = bf16[1,256,512]{2,1,0:T(8,128)(2,1)S(1)} collective-permute-done((bf16[1,256,512]{2,1,0:T(8,128)(2,1)S(1)}, bf16[1,256,512]{2,1,0:T(8,128)(2,1)S(1)}, u32[]{:S(2)}, u32[]{:S(2)}) %collective-permute-start.6) | collective-permute-done | bytes 262176 | tf_op jit(solution)/shard_map/ppermute | solution.py:17
  38.3 1.5 %collective-permute-start.13 = (bf16[1,256,256]{2,1,0:T(8,128)(2,1)S(1)}, bf16[1,256,256]{2,1,0:T(8,128)(2,1)S(1)}, u32[]{:S(2)}, u32[]{:S(2)}) collective-permute-start(bf16[1,256,256]{2,1,0:T(8,128)(2,1)S(1)} %get-tuple-element.48), channel_id=1, source_target_pairs={{0,4},{4,0},{8,12},{12,8},{16,20},{20,16},{24,28},{28,24},{1,5},{5... | collective-permute-start | bytes 393224 | tf_op jit(solution)/shard_map/ppermute | solution.py:17
  40.6 1.2 %collective-permute-start.15 = (bf16[1,256,256]{2,1,0:T(8,128)(2,1)S(1)}, bf16[1,256,256]{2,1,0:T(8,128)(2,1)S(1)}, u32[]{:S(2)}, u32[]{:S(2)}) collective-permute-start(bf16[1,256,256]{2,1,0:T(8,128)(2,1)S(1)} %get-tuple-element.50), channel_id=1, source_target_pairs={{0,12},{4,8},{8,4},{12,0},{16,28},{20,24},{24,20},{28,16},{1,13},{... | collective-permute-start | bytes 393224 | tf_op jit(solution)/shard_map/ppermute | solution.py:17
  42.3 1.6 %collective-permute-start.10 = (bf16[1,256,256]{2,1,0:T(8,128)(2,1)S(1)}, bf16[1,256,256]{2,1,0:T(8,128)(2,1)S(1)}, u32[]{:S(2)}, u32[]{:S(2)}) collective-permute-start(bf16[1,256,256]{2,1,0:T(8,128)(2,1)S(1)} %get-tuple-element.44), channel_id=1, source_target_pairs={{0,4},{4,0},{8,12},{12,8},{16,20},{20,16},{24,28},{28,24},{1,5},{5... | collective-permute-start | bytes 393224 | tf_op jit(solution)/shard_map/ppermute | solution.py:17
  44.7 1.2 %collective-permute-start.12 = (bf16[1,256,256]{2,1,0:T(8,128)(2,1)S(1)}, bf16[1,256,256]{2,1,0:T(8,128)(2,1)S(1)}, u32[]{:S(2)}, u32[]{:S(2)}) collective-permute-start(bf16[1,256,256]{2,1,0:T(8,128)(2,1)S(1)} %get-tuple-element.46), channel_id=1, source_target_pairs={{0,12},{4,8},{8,4},{12,0},{16,28},{20,24},{24,20},{28,16},{1,13},{... | collective-permute-start | bytes 393224 | tf_op jit(solution)/shard_map/ppermute | solution.py:17
  46.2 2.8 %collective-permute-done.15.refs_11_ = bf16[1,256,256]{2,1,0:T(8,128)(2,1)S(1)} collective-permute-done((bf16[1,256,256]{2,1,0:T(8,128)(2,1)S(1)}, bf16[1,256,256]{2,1,0:T(8,128)(2,1)S(1)}, u32[]{:S(2)}, u32[]{:S(2)}) %collective-permute-start.15) | collective-permute-done | bytes 131104 | tf_op jit(solution)/shard_map/ppermute | solution.py:17
  48.9 1.9 %shard_map.67.refs_12_.refs_21_ = bf16[2,256,256]{2,1,0:T(8,128)(2,1)S(1)} custom-call(s32[2,8,8]{2,1,0:T(8,128)S(1)} %copy-done.1, s32[2,2,8]{2,1,0:T(2,128)S(1)} %copy-done.2, s32[2,2]{1,0:T(2,128)S(1)} %copy-done.3, bf16[3,2,256,512]{3,2,1,0:T(8,128)(2,1)S(1)} %copy-done, bf16[2,256,256]{2,1,0:T(8,128)(2,1)S(1)} %get-tuple-element.47.inv, ...), custom_call_target="tpu_custom_call" | custom-call | flops 603979776 | bytes 9044624 | tf_op jit(solution)/shard_map/pallas_call | solution.py:56
  50.9 1.7 %collective-permute-start.23 = (bf16[2,256,256]{2,1,0:T(8,128)(2,1)S(1)}, bf16[2,256,256]{2,1,0:T(8,128)(2,1)S(1)}, u32[]{:S(2)}, u32[]{:S(2)}) collective-permute-start(bf16[2,256,256]{2,1,0:T(8,128)(2,1)S(1)} %shard_map.67.refs_12_.refs_21_), channel_id=1, source_target_pairs={{0,16},{4,20},{8,24},{12,28},{16,0},{20,4},{24,8},{28,12},{1,17},{... | collective-permute-start | bytes 786440 | tf_op jit(solution)/shard_map/ppermute | solution.py:17
  52.6 1.6 %collective-permute-done.12.refs_11_ = bf16[1,256,256]{2,1,0:T(8,128)(2,1)S(1)} collective-permute-done((bf16[1,256,256]{2,1,0:T(8,128)(2,1)S(1)}, bf16[1,256,256]{2,1,0:T(8,128)(2,1)S(1)}, u32[]{:S(2)}, u32[]{:S(2)}) %collective-permute-start.12) | collective-permute-done | bytes 131104 | tf_op jit(solution)/shard_map/ppermute | solution.py:17
  54.2 2.0 %shard_map.68 = (bf16[2,256,256]{2,1,0:T(8,128)(2,1)S(1)}, bf16[2,256,256]{2,1,0:T(8,128)(2,1)S(1)}, bf16[2,256,256]{2,1,0:T(8,128)(2,1)S(1)}, bf16[2,256,256]{2,1,0:T(8,128)(2,1)S(1)}) custom-call(s32[2,8,8]{2,1,0:T(8,128)S(1)} %copy-done.1, s32[2,2,8]{2,1,0:T(2,128)S(1)} %copy-done.2, s32[2,2]{1,0:T(2,128)S(1)} %copy-done.3, ...), custom_call_target="tpu_custom_call" | custom-call | flops 603979776 | bytes 10093200 | tf_op jit(solution)/shard_map/pallas_call | solution.py:56
  56.1 3.3 %collective-permute-start.16 = (bf16[2,256,256]{2,1,0:T(8,128)(2,1)S(1)}, bf16[2,256,256]{2,1,0:T(8,128)(2,1)S(1)}, u32[]{:S(2)}, u32[]{:S(2)}) collective-permute-start(bf16[2,256,256]{2,1,0:T(8,128)(2,1)S(1)} %get-tuple-element.52), channel_id=1, source_target_pairs={{0,4},{4,0},{8,12},{12,8},{16,20},{20,16},{24,28},{28,24},{1,5},{5... | collective-permute-start | bytes 786440 | tf_op jit(solution)/shard_map/ppermute | solution.py:17
  59.5 1.5 %collective-permute-start.18 = (bf16[2,256,256]{2,1,0:T(8,128)(2,1)S(1)}, bf16[2,256,256]{2,1,0:T(8,128)(2,1)S(1)}, u32[]{:S(2)}, u32[]{:S(2)}) collective-permute-start(bf16[2,256,256]{2,1,0:T(8,128)(2,1)S(1)} %get-tuple-element.54), channel_id=1, source_target_pairs={{0,12},{4,8},{8,4},{12,0},{16,28},{20,24},{24,20},{28,16},{1,13},{... | collective-permute-start | bytes 786440 | tf_op jit(solution)/shard_map/ppermute | solution.py:17
  61.7 4.1 %collective-permute-done.23.far.refs_16_ = bf16[2,256,256]{2,1,0:T(8,128)(2,1)S(1)} collective-permute-done((bf16[2,256,256]{2,1,0:T(8,128)(2,1)S(1)}, bf16[2,256,256]{2,1,0:T(8,128)(2,1)S(1)}, u32[]{:S(2)}, u32[]{:S(2)}) %collective-permute-start.23) | collective-permute-done | bytes 262176 | tf_op jit(solution)/shard_map/ppermute | solution.py:17
  66.0 0.9 %collective-permute-start.24 = (bf16[1,256,256]{2,1,0:T(8,128)(2,1)S(1)}, bf16[1,256,256]{2,1,0:T(8,128)(2,1)S(1)}, u32[]{:S(2)}, u32[]{:S(2)}) collective-permute-start(bf16[1,256,256]{2,1,0:T(8,128)(2,1)S(1)} %get-tuple-element.58), channel_id=1, source_target_pairs={{0,4},{4,0},{8,12},{12,8},{16,20},{20,16},{24,28},{28,24},{1,5},{5... | collective-permute-start | bytes 393224 | tf_op jit(solution)/shard_map/ppermute | solution.py:17
  66.9 7.9 %collective-permute-done.17.refs_1_.refs_14_ = bf16[2,256,256]{2,1,0:T(8,128)(2,1)S(1)} collective-permute-done((bf16[2,256,256]{2,1,0:T(8,128)(2,1)S(1)}, bf16[2,256,256]{2,1,0:T(8,128)(2,1)S(1)}, u32[]{:S(2)}, u32[]{:S(2)}) %collective-permute-start.17) | collective-permute-done | bytes 262176 | tf_op jit(solution)/shard_map/ppermute | solution.py:17
  75.3 6.2 %collective-permute-done.18.refs_2_.refs_15_ = bf16[2,256,256]{2,1,0:T(8,128)(2,1)S(1)} collective-permute-done((bf16[2,256,256]{2,1,0:T(8,128)(2,1)S(1)}, bf16[2,256,256]{2,1,0:T(8,128)(2,1)S(1)}, u32[]{:S(2)}, u32[]{:S(2)}) %collective-permute-start.18) | collective-permute-done | bytes 262176 | tf_op jit(solution)/shard_map/ppermute | solution.py:17
  82.3 2.9 %collective-permute-start.22 = (bf16[1,256,256]{2,1,0:T(8,128)(2,1)S(1)}, bf16[1,256,256]{2,1,0:T(8,128)(2,1)S(1)}, u32[]{:S(2)}, u32[]{:S(2)}) collective-permute-start(bf16[1,256,256]{2,1,0:T(8,128)(2,1)S(1)} %get-tuple-element.57), channel_id=1, source_target_pairs={{0,12},{4,8},{8,4},{12,0},{16,28},{20,24},{24,20},{28,16},{1,13},{... | collective-permute-start | bytes 393224 | tf_op jit(solution)/shard_map/ppermute | solution.py:17
  85.2 1.9 %collective-permute-done.26.refs_19_ = bf16[1,256,256]{2,1,0:T(8,128)(2,1)S(1)} collective-permute-done((bf16[1,256,256]{2,1,0:T(8,128)(2,1)S(1)}, bf16[1,256,256]{2,1,0:T(8,128)(2,1)S(1)}, u32[]{:S(2)}, u32[]{:S(2)}) %collective-permute-start.26) | collective-permute-done | bytes 131104 | tf_op jit(solution)/shard_map/ppermute | solution.py:17
  87.1 2.0 %shard_map.71.refs_23_ = bf16[2,256,256]{2,1,0:T(8,128)(2,1)S(1)} custom-call(s32[2,8,8]{2,1,0:T(8,128)S(1)} %copy-done.1, s32[2,2,8]{2,1,0:T(2,128)S(1)} %copy-done.2, s32[2,2]{1,0:T(2,128)S(1)} %copy-done.3, bf16[3,2,256,512]{3,2,1,0:T(8,128)(2,1)S(1)} %copy-done, bf16[2,256,256]{2,1,0:T(8,128)(2,1)S(1)} %get-tuple-element.43.inv, ...), custom_call_target="tpu_custom_call" | custom-call | flops 603979776 | bytes 10748560 | tf_op jit(solution)/shard_map/pallas_call | solution.py:56
  89.1 1.1 %collective-permute-done.22.refs_19_ = bf16[1,256,256]{2,1,0:T(8,128)(2,1)S(1)} collective-permute-done((bf16[1,256,256]{2,1,0:T(8,128)(2,1)S(1)}, bf16[1,256,256]{2,1,0:T(8,128)(2,1)S(1)}, u32[]{:S(2)}, u32[]{:S(2)}) %collective-permute-start.22) | collective-permute-done | bytes 131104 | tf_op jit(solution)/shard_map/ppermute | solution.py:17
  90.3 2.7 %shard_map.72 = bf16[3,2,256,512]{3,2,1,0:T(8,128)(2,1)} custom-call(s32[2,8,8]{2,1,0:T(8,128)S(1)} %copy-done.1, s32[2,2,8]{2,1,0:T(2,128)S(1)} %copy-done.2, s32[2,2]{1,0:T(2,128)S(1)} %copy-done.3, bf16[3,2,256,512]{3,2,1,0:T(8,128)(2,1)S(1)} %copy-done, bf16[2,256,256]{2,1,0:T(8,128)(2,1)S(1)} %get-tuple-element.43.inv, ...), custom_call_target="tpu_custom_call" | custom-call | flops 603979776 | bytes 13370000 | tf_op jit(solution)/shard_map/pallas_call | solution.py:56
  (43 shorter events, 6.7 us)
Async XLA Ops:
  0.9 5.8 %collective-permute-start.1 = (bf16[128,256]{1,0:T(8,128)(2,1)S(1)}, bf16[128,256]{1,0:T(8,128)(2,1)S(1)}, u32[]{:S(2)}, u32[]{:S(2)}) collective-permute-start(bf16[128,256]{1,0:T(8,128)(2,1)S(1)} %bitcast.7), channel_id=1, source_target_pairs={{0,1},{1,0},{2,3},{3,2},{4,5},{5,4},{6,7},{7,6},{8,9},{9,8},{10,11... | collective-permute-start | bytes 196616 | tf_op jit(solution)/shard_map/ppermute | solution.py:17
  1.4 5.3 %collective-permute-start = (bf16[128,256]{1,0:T(8,128)(2,1)S(1)}, bf16[128,256]{1,0:T(8,128)(2,1)S(1)}, u32[]{:S(2)}, u32[]{:S(2)}) collective-permute-start(bf16[128,256]{1,0:T(8,128)(2,1)S(1)} %bitcast.8), channel_id=1, source_target_pairs={{0,2},{1,3},{2,0},{3,1},{4,6},{5,7},{6,4},{7,5},{8,10},{9,11},{10,... | collective-permute-start | bytes 196616 | tf_op jit(solution)/shard_map/ppermute | solution.py:17
  5.3 1.4 %copy-start = (bf16[3,2,256,512]{3,2,1,0:T(8,128)(2,1)S(1)}, bf16[3,2,256,512]{3,2,1,0:T(8,128)(2,1)}, u32[]{:S(2)}) copy-start(bf16[3,2,256,512]{3,2,1,0:T(8,128)(2,1)} %noise.7) | copy-start | bytes 4718596
  5.3 2.7 %copy-start.1 = (s32[2,8,8]{2,1,0:T(8,128)S(1)}, s32[2,8,8]{2,1,0:T(8,128)}, u32[]{:S(2)}) copy-start(s32[2,8,8]{2,1,0:T(8,128)} %picks.15) | copy-start | bytes 1540
  6.7 1.3 %collective-permute-start.2 = (bf16[128,256]{1,0:T(8,128)(2,1)S(1)}, bf16[128,256]{1,0:T(8,128)(2,1)S(1)}, u32[]{:S(2)}, u32[]{:S(2)}) collective-permute-start(bf16[128,256]{1,0:T(8,128)(2,1)S(1)} %collective-permute-done.refs_1_), channel_id=1, source_target_pairs={{0,1},{1,0},{2,3},{3,2},{4,5},{5,4},{6,7},{7,6},{8,9},{9,8},{10,11... | collective-permute-start | bytes 196616 | tf_op jit(solution)/shard_map/ppermute | solution.py:17
  8.4 29.1 %collective-permute-start.7 = (bf16[2304,256]{1,0:T(8,128)(2,1)S(1)}, bf16[2304,256]{1,0:T(8,128)(2,1)S(1)}, u32[]{:S(2)}, u32[]{:S(2)}) collective-permute-start(bf16[2304,256]{1,0:T(8,128)(2,1)S(1)} %get-tuple-element.37.refs_3_), channel_id=1, source_target_pairs={{0,2},{1,3},{2,0},{3,1},{4,6},{5,7},{6,4},{7,5},{8,10},{9,11},{10,... | collective-permute-start | bytes 3538952 | tf_op jit(solution)/shard_map/ppermute | solution.py:17
  10.2 27.3 %collective-permute-start.3 = (bf16[2,256,512]{2,1,0:T(8,128)(2,1)S(1)}, bf16[2,256,512]{2,1,0:T(8,128)(2,1)S(1)}, u32[]{:S(2)}, u32[]{:S(2)}) collective-permute-start(bf16[2,256,512]{2,1,0:T(8,128)(2,1)S(1)} %get-tuple-element.33.refs_4_.refs_20_), channel_id=1, source_target_pairs={{0,16},{4,20},{8,24},{12,28},{16,0},{20,4},{24,8},{28,12},{1,17},{... | collective-permute-start | bytes 1572872 | tf_op jit(solution)/shard_map/ppermute | solution.py:17
  12.8 8.3 %collective-permute-start.4 = (bf16[1,256,512]{2,1,0:T(8,128)(2,1)S(1)}, bf16[1,256,512]{2,1,0:T(8,128)(2,1)S(1)}, u32[]{:S(2)}, u32[]{:S(2)}) collective-permute-start(bf16[1,256,512]{2,1,0:T(8,128)(2,1)S(1)} %get-tuple-element.34), channel_id=1, source_target_pairs={{0,4},{4,0},{8,12},{12,8},{16,20},{20,16},{24,28},{28,24},{1,5},{5... | collective-permute-start | bytes 786440 | tf_op jit(solution)/shard_map/ppermute | solution.py:17
  14.3 16.5 %collective-permute-start.5 = (bf16[1,256,512]{2,1,0:T(8,128)(2,1)S(1)}, bf16[1,256,512]{2,1,0:T(8,128)(2,1)S(1)}, u32[]{:S(2)}, u32[]{:S(2)}) collective-permute-start(bf16[1,256,512]{2,1,0:T(8,128)(2,1)S(1)} %get-tuple-element.35), channel_id=1, source_target_pairs={{0,8},{4,12},{8,0},{12,4},{16,24},{20,28},{24,16},{28,20},{1,9},{5... | collective-permute-start | bytes 786440 | tf_op jit(solution)/shard_map/ppermute | solution.py:17
  15.9 21.6 %collective-permute-start.6 = (bf16[1,256,512]{2,1,0:T(8,128)(2,1)S(1)}, bf16[1,256,512]{2,1,0:T(8,128)(2,1)S(1)}, u32[]{:S(2)}, u32[]{:S(2)}) collective-permute-start(bf16[1,256,512]{2,1,0:T(8,128)(2,1)S(1)} %get-tuple-element.36), channel_id=1, source_target_pairs={{0,12},{4,8},{8,4},{12,0},{16,28},{20,24},{24,20},{28,16},{1,13},{... | collective-permute-start | bytes 786440 | tf_op jit(solution)/shard_map/ppermute | solution.py:17
  37.7 4.1 %collective-permute-start.8 = (bf16[2304,256]{1,0:T(8,128)(2,1)S(1)}, bf16[2304,256]{1,0:T(8,128)(2,1)S(1)}, u32[]{:S(2)}, u32[]{:S(2)}) collective-permute-start(bf16[2304,256]{1,0:T(8,128)(2,1)S(1)} %get-tuple-element.38.refs_0_), channel_id=1, source_target_pairs={{0,1},{1,0},{2,3},{3,2},{4,5},{5,4},{6,7},{7,6},{8,9},{9,8},{10,11... | collective-permute-start | bytes 3538952 | tf_op jit(solution)/shard_map/ppermute | solution.py:17
  37.8 4.5 %collective-permute-start.9 = (bf16[2304,256]{1,0:T(8,128)(2,1)S(1)}, bf16[2304,256]{1,0:T(8,128)(2,1)S(1)}, u32[]{:S(2)}, u32[]{:S(2)}) collective-permute-start(bf16[2304,256]{1,0:T(8,128)(2,1)S(1)} %get-tuple-element.39.refs_1_), channel_id=1, source_target_pairs={{0,1},{1,0},{2,3},{3,2},{4,5},{5,4},{6,7},{7,6},{8,9},{9,8},{10,11... | collective-permute-start | bytes 3538952 | tf_op jit(solution)/shard_map/ppermute | solution.py:17
  38.3 6.4 %collective-permute-start.13 = (bf16[1,256,256]{2,1,0:T(8,128)(2,1)S(1)}, bf16[1,256,256]{2,1,0:T(8,128)(2,1)S(1)}, u32[]{:S(2)}, u32[]{:S(2)}) collective-permute-start(bf16[1,256,256]{2,1,0:T(8,128)(2,1)S(1)} %get-tuple-element.48), channel_id=1, source_target_pairs={{0,4},{4,0},{8,12},{12,8},{16,20},{20,16},{24,28},{28,24},{1,5},{5... | collective-permute-start | bytes 393224 | tf_op jit(solution)/shard_map/ppermute | solution.py:17
  39.8 6.4 %collective-permute-start.14 = (bf16[1,256,256]{2,1,0:T(8,128)(2,1)S(1)}, bf16[1,256,256]{2,1,0:T(8,128)(2,1)S(1)}, u32[]{:S(2)}, u32[]{:S(2)}) collective-permute-start(bf16[1,256,256]{2,1,0:T(8,128)(2,1)S(1)} %get-tuple-element.49), channel_id=1, source_target_pairs={{0,8},{4,12},{8,0},{12,4},{16,24},{20,28},{24,16},{28,20},{1,9},{5... | collective-permute-start | bytes 393224 | tf_op jit(solution)/shard_map/ppermute | solution.py:17
  40.6 8.4 %collective-permute-start.15 = (bf16[1,256,256]{2,1,0:T(8,128)(2,1)S(1)}, bf16[1,256,256]{2,1,0:T(8,128)(2,1)S(1)}, u32[]{:S(2)}, u32[]{:S(2)}) collective-permute-start(bf16[1,256,256]{2,1,0:T(8,128)(2,1)S(1)} %get-tuple-element.50), channel_id=1, source_target_pairs={{0,12},{4,8},{8,4},{12,0},{16,28},{20,24},{24,20},{28,16},{1,13},{... | collective-permute-start | bytes 393224 | tf_op jit(solution)/shard_map/ppermute | solution.py:17
  42.3 6.6 %copy-start.2 = (s32[2,2,8]{2,1,0:T(2,128)S(1)}, s32[2,2,8]{2,1,0:T(2,128)}, u32[]{:S(2)}) copy-start(s32[2,2,8]{2,1,0:T(2,128)} %lists.7) | copy-start | bytes 388
  42.3 6.6 %copy-start.3 = (s32[2,2]{1,0:T(2,128)S(1)}, s32[2,2]{1,0:T(2,128)}, u32[]{:S(2)}) copy-start(s32[2,2]{1,0:T(2,128)} %counts.7) | copy-start | bytes 52
  42.3 10.2 %collective-permute-start.10 = (bf16[1,256,256]{2,1,0:T(8,128)(2,1)S(1)}, bf16[1,256,256]{2,1,0:T(8,128)(2,1)S(1)}, u32[]{:S(2)}, u32[]{:S(2)}) collective-permute-start(bf16[1,256,256]{2,1,0:T(8,128)(2,1)S(1)} %get-tuple-element.44), channel_id=1, source_target_pairs={{0,4},{4,0},{8,12},{12,8},{16,20},{20,16},{24,28},{28,24},{1,5},{5... | collective-permute-start | bytes 393224 | tf_op jit(solution)/shard_map/ppermute | solution.py:17
  43.9 8.6 %collective-permute-start.11 = (bf16[1,256,256]{2,1,0:T(8,128)(2,1)S(1)}, bf16[1,256,256]{2,1,0:T(8,128)(2,1)S(1)}, u32[]{:S(2)}, u32[]{:S(2)}) collective-permute-start(bf16[1,256,256]{2,1,0:T(8,128)(2,1)S(1)} %get-tuple-element.45), channel_id=1, source_target_pairs={{0,8},{4,12},{8,0},{12,4},{16,24},{20,28},{24,16},{28,20},{1,9},{5... | collective-permute-start | bytes 393224 | tf_op jit(solution)/shard_map/ppermute | solution.py:17
  44.7 9.4 %collective-permute-start.12 = (bf16[1,256,256]{2,1,0:T(8,128)(2,1)S(1)}, bf16[1,256,256]{2,1,0:T(8,128)(2,1)S(1)}, u32[]{:S(2)}, u32[]{:S(2)}) collective-permute-start(bf16[1,256,256]{2,1,0:T(8,128)(2,1)S(1)} %get-tuple-element.46), channel_id=1, source_target_pairs={{0,12},{4,8},{8,4},{12,0},{16,28},{20,24},{24,20},{28,16},{1,13},{... | collective-permute-start | bytes 393224 | tf_op jit(solution)/shard_map/ppermute | solution.py:17
  50.9 15.0 %collective-permute-start.23 = (bf16[2,256,256]{2,1,0:T(8,128)(2,1)S(1)}, bf16[2,256,256]{2,1,0:T(8,128)(2,1)S(1)}, u32[]{:S(2)}, u32[]{:S(2)}) collective-permute-start(bf16[2,256,256]{2,1,0:T(8,128)(2,1)S(1)} %shard_map.67.refs_12_.refs_21_), channel_id=1, source_target_pairs={{0,16},{4,20},{8,24},{12,28},{16,0},{20,4},{24,8},{28,12},{1,17},{... | collective-permute-start | bytes 786440 | tf_op jit(solution)/shard_map/ppermute | solution.py:17
  56.1 10.8 %collective-permute-start.16 = (bf16[2,256,256]{2,1,0:T(8,128)(2,1)S(1)}, bf16[2,256,256]{2,1,0:T(8,128)(2,1)S(1)}, u32[]{:S(2)}, u32[]{:S(2)}) collective-permute-start(bf16[2,256,256]{2,1,0:T(8,128)(2,1)S(1)} %get-tuple-element.52), channel_id=1, source_target_pairs={{0,4},{4,0},{8,12},{12,8},{16,20},{20,16},{24,28},{28,24},{1,5},{5... | collective-permute-start | bytes 786440 | tf_op jit(solution)/shard_map/ppermute | solution.py:17
  59.5 15.4 %collective-permute-start.17 = (bf16[2,256,256]{2,1,0:T(8,128)(2,1)S(1)}, bf16[2,256,256]{2,1,0:T(8,128)(2,1)S(1)}, u32[]{:S(2)}, u32[]{:S(2)}) collective-permute-start(bf16[2,256,256]{2,1,0:T(8,128)(2,1)S(1)} %get-tuple-element.53), channel_id=1, source_target_pairs={{0,8},{4,12},{8,0},{12,4},{16,24},{20,28},{24,16},{28,20},{1,9},{5... | collective-permute-start | bytes 786440 | tf_op jit(solution)/shard_map/ppermute | solution.py:17
  59.5 22.0 %collective-permute-start.18 = (bf16[2,256,256]{2,1,0:T(8,128)(2,1)S(1)}, bf16[2,256,256]{2,1,0:T(8,128)(2,1)S(1)}, u32[]{:S(2)}, u32[]{:S(2)}) collective-permute-start(bf16[2,256,256]{2,1,0:T(8,128)(2,1)S(1)} %get-tuple-element.54), channel_id=1, source_target_pairs={{0,12},{4,8},{8,4},{12,0},{16,28},{20,24},{24,20},{28,16},{1,13},{... | collective-permute-start | bytes 786440 | tf_op jit(solution)/shard_map/ppermute | solution.py:17
  61.0 20.5 %collective-permute-start.19 = (bf16[2,256,256]{2,1,0:T(8,128)(2,1)S(1)}, bf16[2,256,256]{2,1,0:T(8,128)(2,1)S(1)}, u32[]{:S(2)}, u32[]{:S(2)}) collective-permute-start(bf16[2,256,256]{2,1,0:T(8,128)(2,1)S(1)} %get-tuple-element.51.refs_12_.refs_22_), channel_id=1, source_target_pairs={{0,16},{4,20},{8,24},{12,28},{16,0},{20,4},{24,8},{28,12},{1,17},{... | collective-permute-start | bytes 786440 | tf_op jit(solution)/shard_map/ppermute | solution.py:17
  66.0 16.3 %collective-permute-start.24 = (bf16[1,256,256]{2,1,0:T(8,128)(2,1)S(1)}, bf16[1,256,256]{2,1,0:T(8,128)(2,1)S(1)}, u32[]{:S(2)}, u32[]{:S(2)}) collective-permute-start(bf16[1,256,256]{2,1,0:T(8,128)(2,1)S(1)} %get-tuple-element.58), channel_id=1, source_target_pairs={{0,4},{4,0},{8,12},{12,8},{16,20},{20,16},{24,28},{28,24},{1,5},{5... | collective-permute-start | bytes 393224 | tf_op jit(solution)/shard_map/ppermute | solution.py:17
  66.9 18.3 %collective-permute-start.25 = (bf16[1,256,256]{2,1,0:T(8,128)(2,1)S(1)}, bf16[1,256,256]{2,1,0:T(8,128)(2,1)S(1)}, u32[]{:S(2)}, u32[]{:S(2)}) collective-permute-start(bf16[1,256,256]{2,1,0:T(8,128)(2,1)S(1)} %get-tuple-element.59), channel_id=1, source_target_pairs={{0,8},{4,12},{8,0},{12,4},{16,24},{20,28},{24,16},{28,20},{1,9},{5... | collective-permute-start | bytes 393224 | tf_op jit(solution)/shard_map/ppermute | solution.py:17
  74.8 12.3 %collective-permute-start.26 = (bf16[1,256,256]{2,1,0:T(8,128)(2,1)S(1)}, bf16[1,256,256]{2,1,0:T(8,128)(2,1)S(1)}, u32[]{:S(2)}, u32[]{:S(2)}) collective-permute-start(bf16[1,256,256]{2,1,0:T(8,128)(2,1)S(1)} %get-tuple-element.60), channel_id=1, source_target_pairs={{0,12},{4,8},{8,4},{12,0},{16,28},{20,24},{24,20},{28,16},{1,13},{... | collective-permute-start | bytes 393224 | tf_op jit(solution)/shard_map/ppermute | solution.py:17
  81.6 7.5 %collective-permute-start.20 = (bf16[1,256,256]{2,1,0:T(8,128)(2,1)S(1)}, bf16[1,256,256]{2,1,0:T(8,128)(2,1)S(1)}, u32[]{:S(2)}, u32[]{:S(2)}) collective-permute-start(bf16[1,256,256]{2,1,0:T(8,128)(2,1)S(1)} %get-tuple-element.55), channel_id=1, source_target_pairs={{0,4},{4,0},{8,12},{12,8},{16,20},{20,16},{24,28},{28,24},{1,5},{5... | collective-permute-start | bytes 393224 | tf_op jit(solution)/shard_map/ppermute | solution.py:17
  82.3 6.9 %collective-permute-start.21 = (bf16[1,256,256]{2,1,0:T(8,128)(2,1)S(1)}, bf16[1,256,256]{2,1,0:T(8,128)(2,1)S(1)}, u32[]{:S(2)}, u32[]{:S(2)}) collective-permute-start(bf16[1,256,256]{2,1,0:T(8,128)(2,1)S(1)} %get-tuple-element.56), channel_id=1, source_target_pairs={{0,8},{4,12},{8,0},{12,4},{16,24},{20,28},{24,16},{28,20},{1,9},{5... | collective-permute-start | bytes 393224 | tf_op jit(solution)/shard_map/ppermute | solution.py:17
  82.3 8.0 %collective-permute-start.22 = (bf16[1,256,256]{2,1,0:T(8,128)(2,1)S(1)}, bf16[1,256,256]{2,1,0:T(8,128)(2,1)S(1)}, u32[]{:S(2)}, u32[]{:S(2)}) collective-permute-start(bf16[1,256,256]{2,1,0:T(8,128)(2,1)S(1)} %get-tuple-element.57), channel_id=1, source_target_pairs={{0,12},{4,8},{8,4},{12,0},{16,28},{20,24},{24,20},{28,16},{1,13},{... | collective-permute-start | bytes 393224 | tf_op jit(solution)/shard_map/ppermute | solution.py:17

commit v23 on v22

--- a/solution.py
+++ b/solution.py
@@ -94,7 +94,8 @@
         send[0] = solved[entry_of(picks[0], myself ^ step, myself)]
 
 
-def relay_kernel(half, source, waits, through, picks, far, *refs):
+def relay_kernel(half, source, owned, waits, through, picks, far, *refs):
+    own, refs = take(refs, owned)
     sends = refs[waits + through:len(refs) - through]
     myself = lax.axis_index("leaf")
     for at, send in enumerate(sends):
@@ -102,6 +103,10 @@
         wide = send.shape[-1]
         node = entry_of(picks[source], myself ^ (step + 1), myself ^ half)
         send[0] = far[node, :, chunk * wide:(chunk + 1) * wide]
+        if send.shape[0] > 1:
+            node = entry_of(picks[source], myself ^ (step + 1), myself)
+            for to, ref in enumerate(own, 1):
+                send[to] = ref[node]
 
 
 def inverse_kernel(held, levels, span, *refs):
@@ -205,7 +210,7 @@
     far, got = leaf(solved, half), near(sends)
     values, steps = far_rows(raw, "draw", draws)
     sends = call(
-        functools.partial(relay_kernel, half, 0, len(got), len(values)),
+        functools.partial(relay_kernel, half, 0, 0, len(got), len(values)),
         [shape(1, rows, wide)] * (CHUNKS * (half - 1)) + [shape(*value.shape) for value in values],
         [],
         (picks, far, *got, *values),
@@ -237,7 +242,7 @@
         solved, sends = [], []
         for at in chunks:
             ends = at == CHUNKS - 1 and not last_level
-            sides, mates = (half - 1, list(solved)) if ends else (0, [])
+            sides, mates = (half - 2, list(solved)) if ends else (0, [])
             final = last_level and at == CHUNKS - 1
             known = [entry for below in range(level) for entry in pieces[below][at]]
             stored = done if final else []
@@ -267,16 +272,18 @@
         got = near(sends)
         pieces.append([])
         for at in chunks:
-            waits = got if at == CHUNKS - 1 else []
+            own, waits = (solved, []) if at == 0 else ([], got)
             sends = call(
-                functools.partial(relay_kernel, half, level, len(waits), 0),
-                [shape(1, rows, wide)] * (half - 1),
+                functools.partial(relay_kernel, half, level, len(own), len(waits), 0),
+                [shape(1, rows, wide)] * (half - 2) + [shape(1 + len(own), rows, wide)],
                 [],
-                (picks, far[at], *waits),
+                (picks, far[at], *own, *waits),
             )
+            distant = near(sends)
+            late = distant[-1] if at == 0 else late
             pieces[level].append([
-                (solved[at], 0), *((ref, at) for ref in got),
-                (far[at], 0), *((ref, 0) for ref in near(sends)),
+                (solved[at], 0), *((ref, at) for ref in got), (late, 1 + at),
+                (far[at], 0), *((ref, 0) for ref in distant),
             ])
 
 

time: 93.2 us -> 100 us (1.073)
  waiting for transfers between devices: 50.2 us -> 55 us
  starting transfers between devices: 30.8 us -> 33.2 us
    ppermute x27 -> x26, waiting for transfers between devices: 50.2 us -> 55 us  [hop(): return lax.ppermute(value, axis, [(at, at ^ step) for at in range(size)])]
    ppermute x27 -> x26, starting transfers between devices: 30.8 us -> 33.2 us  [hop(): return lax.ppermute(value, axis, [(at, at ^ step) for at in range(size)])]
  transfers between devices with their start and end apart: 27 -> 26, of which waited for: 14 -> 17; matrix products, arithmetic and copies ran while one was open for 1% -> 1% of each run, Pallas kernels for 7% -> 4%
where the time goes in v23:
time: 100 us
  waiting for transfers between devices  55 us (55%)
  starting transfers between devices  33.2 us (33%)
  Pallas kernels  9.55 us (10%)
  local copies, waits for them, and re-layouts  2.24 us (2%)
    ppermute x26, waiting for transfers between devices, hop(): return lax.ppermute(value, axis, [(at, at ^ step) for at in range(size)])  55 us
    ppermute x26, starting transfers between devices, hop(): return lax.ppermute(value, axis, [(at, at ^ step) for at in range(size)])  33.2 us
    pallas_call x9, Pallas kernels, call(): pl.pallas_call(kernel, out_shape=outs, in_specs=[VMEM] * len(arrays), out...  9.55 us
  transfers between devices with their start and end apart: 26, of which 17 were waited for; matrix products, arithmetic and copies ran while one was open for 1% of the time, Pallas kernels for 4%

profile of v23, /device:TPU:0, one launch (start us, length us, event | category | flops | bytes accessed | tf_op | source)
XLA Modules:
  0.0 100.2 jit_solution(16320673084180362083)
XLA Ops:
  1.4 2.6 %collective-permute-start = (bf16[128,256]{1,0:T(8,128)(2,1)S(1)}, bf16[128,256]{1,0:T(8,128)(2,1)S(1)}, u32[]{:S(2)}, u32[]{:S(2)}) collective-permute-start(bf16[128,256]{1,0:T(8,128)(2,1)S(1)} %bitcast.8), channel_id=1, source_target_pairs={{0,2},{1,3},{2,0},{3,1},{4,6},{5,7},{6,4},{7,5},{8,10},{9,11},{10,... | collective-permute-start | bytes 196616 | tf_op jit(solution)/shard_map/ppermute | solution.py:17
  4.0 1.3 %fusion = (bf16[1,2,2,256,256]{4,3,2,1,0:T(8,128)(2,1)S(1)}, bf16[1,2,2,256,256]{4,3,2,1,0:T(8,128)(2,1)S(1)}) fusion(bf16[2,2,2,256,256]{4,3,2,1,0:T(8,128)(2,1)} %param.8), kind=kLoop, calls=%fused_computation.2 | loop fusion | bytes 2097152 | tf_op jit(solution)/shard_map/slice | solution.py:198
  5.4 1.3 %collective-permute-done.refs_1_ = bf16[128,256]{1,0:T(8,128)(2,1)S(1)} collective-permute-done((bf16[128,256]{1,0:T(8,128)(2,1)S(1)}, bf16[128,256]{1,0:T(8,128)(2,1)S(1)}, u32[]{:S(2)}, u32[]{:S(2)}) %collective-permute-start) | collective-permute-done | bytes 65568 | tf_op jit(solution)/shard_map/ppermute | solution.py:17
  6.7 1.2 %collective-permute-done.2.refs_3_ = bf16[128,256]{1,0:T(8,128)(2,1)S(1)} collective-permute-done((bf16[128,256]{1,0:T(8,128)(2,1)S(1)}, bf16[128,256]{1,0:T(8,128)(2,1)S(1)}, u32[]{:S(2)}, u32[]{:S(2)}) %collective-permute-start.2) | collective-permute-done | bytes 65568 | tf_op jit(solution)/shard_map/ppermute | solution.py:17
  8.4 1.8 %collective-permute-start.7 = (bf16[2304,256]{1,0:T(8,128)(2,1)S(1)}, bf16[2304,256]{1,0:T(8,128)(2,1)S(1)}, u32[]{:S(2)}, u32[]{:S(2)}) collective-permute-start(bf16[2304,256]{1,0:T(8,128)(2,1)S(1)} %get-tuple-element.36.refs_3_), channel_id=1, source_target_pairs={{0,2},{1,3},{2,0},{3,1},{4,6},{5,7},{6,4},{7,5},{8,10},{9,11},{10,... | collective-permute-start | bytes 3538952 | tf_op jit(solution)/shard_map/ppermute | solution.py:17
  10.2 2.6 %collective-permute-start.3 = (bf16[2,256,512]{2,1,0:T(8,128)(2,1)S(1)}, bf16[2,256,512]{2,1,0:T(8,128)(2,1)S(1)}, u32[]{:S(2)}, u32[]{:S(2)}) collective-permute-start(bf16[2,256,512]{2,1,0:T(8,128)(2,1)S(1)} %get-tuple-element.32.refs_4_.refs_20_), channel_id=1, source_target_pairs={{0,16},{4,20},{8,24},{12,28},{16,0},{20,4},{24,8},{28,12},{1,17},{... | collective-permute-start | bytes 1572872 | tf_op jit(solution)/shard_map/ppermute | solution.py:17
  12.8 1.5 %collective-permute-start.4 = (bf16[1,256,512]{2,1,0:T(8,128)(2,1)S(1)}, bf16[1,256,512]{2,1,0:T(8,128)(2,1)S(1)}, u32[]{:S(2)}, u32[]{:S(2)}) collective-permute-start(bf16[1,256,512]{2,1,0:T(8,128)(2,1)S(1)} %get-tuple-element.33), channel_id=1, source_target_pairs={{0,4},{4,0},{8,12},{12,8},{16,20},{20,16},{24,28},{28,24},{1,5},{5... | collective-permute-start | bytes 786440 | tf_op jit(solution)/shard_map/ppermute | solution.py:17
  14.3 1.6 %collective-permute-start.5 = (bf16[1,256,512]{2,1,0:T(8,128)(2,1)S(1)}, bf16[1,256,512]{2,1,0:T(8,128)(2,1)S(1)}, u32[]{:S(2)}, u32[]{:S(2)}) collective-permute-start(bf16[1,256,512]{2,1,0:T(8,128)(2,1)S(1)} %get-tuple-element.34), channel_id=1, source_target_pairs={{0,8},{4,12},{8,0},{12,4},{16,24},{20,28},{24,16},{28,20},{1,9},{5... | collective-permute-start | bytes 786440 | tf_op jit(solution)/shard_map/ppermute | solution.py:17
  16.3 4.9 %collective-permute-done.4.refs_0_.refs_5_ = bf16[1,256,512]{2,1,0:T(8,128)(2,1)S(1)} collective-permute-done((bf16[1,256,512]{2,1,0:T(8,128)(2,1)S(1)}, bf16[1,256,512]{2,1,0:T(8,128)(2,1)S(1)}, u32[]{:S(2)}, u32[]{:S(2)}) %collective-permute-start.4) | collective-permute-done | bytes 262176 | tf_op jit(solution)/shard_map/ppermute | solution.py:17
  21.1 9.6 %collective-permute-done.5.refs_1_.refs_6_ = bf16[1,256,512]{2,1,0:T(8,128)(2,1)S(1)} collective-permute-done((bf16[1,256,512]{2,1,0:T(8,128)(2,1)S(1)}, bf16[1,256,512]{2,1,0:T(8,128)(2,1)S(1)}, u32[]{:S(2)}, u32[]{:S(2)}) %collective-permute-start.5) | collective-permute-done | bytes 262176 | tf_op jit(solution)/shard_map/ppermute | solution.py:17
  30.8 6.7 %collective-permute-done.6.refs_2_.refs_7_ = bf16[1,256,512]{2,1,0:T(8,128)(2,1)S(1)} collective-permute-done((bf16[1,256,512]{2,1,0:T(8,128)(2,1)S(1)}, bf16[1,256,512]{2,1,0:T(8,128)(2,1)S(1)}, u32[]{:S(2)}, u32[]{:S(2)}) %collective-permute-start.6) | collective-permute-done | bytes 262176 | tf_op jit(solution)/shard_map/ppermute | solution.py:17
  38.3 1.5 %collective-permute-start.13 = (bf16[1,256,256]{2,1,0:T(8,128)(2,1)S(1)}, bf16[1,256,256]{2,1,0:T(8,128)(2,1)S(1)}, u32[]{:S(2)}, u32[]{:S(2)}) collective-permute-start(bf16[1,256,256]{2,1,0:T(8,128)(2,1)S(1)} %get-tuple-element.47), channel_id=1, source_target_pairs={{0,4},{4,0},{8,12},{12,8},{16,20},{20,16},{24,28},{28,24},{1,5},{5... | collective-permute-start | bytes 393224 | tf_op jit(solution)/shard_map/ppermute | solution.py:17
  40.6 1.2 %collective-permute-start.15 = (bf16[1,256,256]{2,1,0:T(8,128)(2,1)S(1)}, bf16[1,256,256]{2,1,0:T(8,128)(2,1)S(1)}, u32[]{:S(2)}, u32[]{:S(2)}) collective-permute-start(bf16[1,256,256]{2,1,0:T(8,128)(2,1)S(1)} %get-tuple-element.49), channel_id=1, source_target_pairs={{0,12},{4,8},{8,4},{12,0},{16,28},{20,24},{24,20},{28,16},{1,13},{... | collective-permute-start | bytes 393224 | tf_op jit(solution)/shard_map/ppermute | solution.py:17
  42.3 1.4 %collective-permute-done.13.refs_9_ = bf16[1,256,256]{2,1,0:T(8,128)(2,1)S(1)} collective-permute-done((bf16[1,256,256]{2,1,0:T(8,128)(2,1)S(1)}, bf16[1,256,256]{2,1,0:T(8,128)(2,1)S(1)}, u32[]{:S(2)}, u32[]{:S(2)}) %collective-permute-start.13) | collective-permute-done | bytes 131104 | tf_op jit(solution)/shard_map/ppermute | solution.py:17
  43.8 2.4 %collective-permute-done.14.refs_10_ = bf16[1,256,256]{2,1,0:T(8,128)(2,1)S(1)} collective-permute-done((bf16[1,256,256]{2,1,0:T(8,128)(2,1)S(1)}, bf16[1,256,256]{2,1,0:T(8,128)(2,1)S(1)}, u32[]{:S(2)}, u32[]{:S(2)}) %collective-permute-start.14) | collective-permute-done | bytes 131104 | tf_op jit(solution)/shard_map/ppermute | solution.py:17
  46.2 1.6 %collective-permute-done.15.refs_11_ = bf16[1,256,256]{2,1,0:T(8,128)(2,1)S(1)} collective-permute-done((bf16[1,256,256]{2,1,0:T(8,128)(2,1)S(1)}, bf16[1,256,256]{2,1,0:T(8,128)(2,1)S(1)}, u32[]{:S(2)}, u32[]{:S(2)}) %collective-permute-start.15) | collective-permute-done | bytes 131104 | tf_op jit(solution)/shard_map/ppermute | solution.py:17
  47.8 1.9 %shard_map.67.refs_12_.refs_0_.refs_21_ = bf16[2,256,256]{2,1,0:T(8,128)(2,1)S(1)} custom-call(s32[2,8,8]{2,1,0:T(8,128)S(1)} %copy-done.1, s32[2,2,8]{2,1,0:T(2,128)S(1)} %copy-done.2, s32[2,2]{1,0:T(2,128)S(1)} %copy-done.3, bf16[3,2,256,512]{3,2,1,0:T(8,128)(2,1)S(1)} %copy-done, bf16[2,256,256]{2,1,0:T(8,128)(2,1)S(1)} %get-tuple-element.46.inv, ...), custom_call_target="tpu_custom_call" | custom-call | flops 603979776 | bytes 9044624 | tf_op jit(solution)/shard_map/pallas_call | solution.py:56
  49.7 1.9 %collective-permute-start.18 = (bf16[2,256,256]{2,1,0:T(8,128)(2,1)S(1)}, bf16[2,256,256]{2,1,0:T(8,128)(2,1)S(1)}, u32[]{:S(2)}, u32[]{:S(2)}) collective-permute-start(bf16[2,256,256]{2,1,0:T(8,128)(2,1)S(1)} %shard_map.67.refs_12_.refs_0_.refs_21_), channel_id=1, source_target_pairs={{0,16},{4,20},{8,24},{12,28},{16,0},{20,4},{24,8},{28,12},{1,17},{... | collective-permute-start | bytes 786440 | tf_op jit(solution)/shard_map/ppermute | solution.py:17
  51.6 1.5 %collective-permute-start.10 = (bf16[1,256,256]{2,1,0:T(8,128)(2,1)S(1)}, bf16[1,256,256]{2,1,0:T(8,128)(2,1)S(1)}, u32[]{:S(2)}, u32[]{:S(2)}) collective-permute-start(bf16[1,256,256]{2,1,0:T(8,128)(2,1)S(1)} %get-tuple-element.43), channel_id=1, source_target_pairs={{0,4},{4,0},{8,12},{12,8},{16,20},{20,16},{24,28},{28,24},{1,5},{5... | collective-permute-start | bytes 393224 | tf_op jit(solution)/shard_map/ppermute | solution.py:17
  53.1 1.6 %collective-permute-start.11 = (bf16[1,256,256]{2,1,0:T(8,128)(2,1)S(1)}, bf16[1,256,256]{2,1,0:T(8,128)(2,1)S(1)}, u32[]{:S(2)}, u32[]{:S(2)}) collective-permute-start(bf16[1,256,256]{2,1,0:T(8,128)(2,1)S(1)} %get-tuple-element.44), channel_id=1, source_target_pairs={{0,8},{4,12},{8,0},{12,4},{16,24},{20,28},{24,16},{28,20},{1,9},{5... | collective-permute-start | bytes 393224 | tf_op jit(solution)/shard_map/ppermute | solution.py:17
  55.0 2.0 %collective-permute-done.10.refs_9_ = bf16[1,256,256]{2,1,0:T(8,128)(2,1)S(1)} collective-permute-done((bf16[1,256,256]{2,1,0:T(8,128)(2,1)S(1)}, bf16[1,256,256]{2,1,0:T(8,128)(2,1)S(1)}, u32[]{:S(2)}, u32[]{:S(2)}) %collective-permute-start.10) | collective-permute-done | bytes 131104 | tf_op jit(solution)/shard_map/ppermute | solution.py:17
  57.1 3.6 %collective-permute-done.11.refs_10_ = bf16[1,256,256]{2,1,0:T(8,128)(2,1)S(1)} collective-permute-done((bf16[1,256,256]{2,1,0:T(8,128)(2,1)S(1)}, bf16[1,256,256]{2,1,0:T(8,128)(2,1)S(1)}, u32[]{:S(2)}, u32[]{:S(2)}) %collective-permute-start.11) | collective-permute-done | bytes 131104 | tf_op jit(solution)/shard_map/ppermute | solution.py:17
  60.7 5.1 %collective-permute-done.12.refs_11_ = bf16[1,256,256]{2,1,0:T(8,128)(2,1)S(1)} collective-permute-done((bf16[1,256,256]{2,1,0:T(8,128)(2,1)S(1)}, bf16[1,256,256]{2,1,0:T(8,128)(2,1)S(1)}, u32[]{:S(2)}, u32[]{:S(2)}) %collective-permute-start.12) | collective-permute-done | bytes 131104 | tf_op jit(solution)/shard_map/ppermute | solution.py:17
  65.8 2.0 %shard_map.68 = (bf16[2,256,256]{2,1,0:T(8,128)(2,1)S(1)}, bf16[2,256,256]{2,1,0:T(8,128)(2,1)S(1)}, bf16[2,256,256]{2,1,0:T(8,128)(2,1)S(1)}) custom-call(s32[2,8,8]{2,1,0:T(8,128)S(1)} %copy-done.1, s32[2,2,8]{2,1,0:T(2,128)S(1)} %copy-done.2, s32[2,2]{1,0:T(2,128)S(1)} %copy-done.3, bf16[3,2,256,512]{3,2,1,0:T(8,128)(2,1)S(1)} %copy-done, ...), custom_call_target="tpu_custom_call" | custom-call | flops 603979776 | bytes 9831056 | tf_op jit(solution)/shard_map/pallas_call | solution.py:56
  69.0 2.5 %collective-permute-start.17 = (bf16[2,256,256]{2,1,0:T(8,128)(2,1)S(1)}, bf16[2,256,256]{2,1,0:T(8,128)(2,1)S(1)}, u32[]{:S(2)}, u32[]{:S(2)}) collective-permute-start(bf16[2,256,256]{2,1,0:T(8,128)(2,1)S(1)} %get-tuple-element.52), channel_id=1, source_target_pairs={{0,8},{4,12},{8,0},{12,4},{16,24},{20,28},{24,16},{28,20},{1,9},{5... | collective-permute-start | bytes 786440 | tf_op jit(solution)/shard_map/ppermute | solution.py:17
  72.3 5.9 %collective-permute-done.16.refs_0_.refs_13_ = bf16[2,256,256]{2,1,0:T(8,128)(2,1)S(1)} collective-permute-done((bf16[2,256,256]{2,1,0:T(8,128)(2,1)S(1)}, bf16[2,256,256]{2,1,0:T(8,128)(2,1)S(1)}, u32[]{:S(2)}, u32[]{:S(2)}) %collective-permute-start.16) | collective-permute-done | bytes 262176 | tf_op jit(solution)/shard_map/ppermute | solution.py:17
  78.3 4.8 %collective-permute-start.25 = (bf16[1,256,256]{2,1,0:T(8,128)(2,1)S(1)}, bf16[1,256,256]{2,1,0:T(8,128)(2,1)S(1)}, u32[]{:S(2)}, u32[]{:S(2)}) collective-permute-start(bf16[1,256,256]{2,1,0:T(8,128)(2,1)S(1)} %get-tuple-element.58), channel_id=1, source_target_pairs={{0,8},{4,12},{8,0},{12,4},{16,24},{20,28},{24,16},{28,20},{1,9},{5... | collective-permute-start | bytes 393224 | tf_op jit(solution)/shard_map/ppermute | solution.py:17
  83.1 5.8 %collective-permute-done.17.refs_1_.refs_14_ = bf16[2,256,256]{2,1,0:T(8,128)(2,1)S(1)} collective-permute-done((bf16[2,256,256]{2,1,0:T(8,128)(2,1)S(1)}, bf16[2,256,256]{2,1,0:T(8,128)(2,1)S(1)}, u32[]{:S(2)}, u32[]{:S(2)}) %collective-permute-start.17) | collective-permute-done | bytes 262176 | tf_op jit(solution)/shard_map/ppermute | solution.py:17
  91.6 1.5 %collective-permute-start.23 = (bf16[1,256,256]{2,1,0:T(8,128)(2,1)S(1)}, bf16[1,256,256]{2,1,0:T(8,128)(2,1)S(1)}, u32[]{:S(2)}, u32[]{:S(2)}) collective-permute-start(bf16[1,256,256]{2,1,0:T(8,128)(2,1)S(1)} %get-tuple-element.56), channel_id=1, source_target_pairs={{0,12},{4,8},{8,4},{12,0},{16,28},{20,24},{24,20},{28,16},{1,13},{... | collective-permute-start | bytes 393224 | tf_op jit(solution)/shard_map/ppermute | solution.py:17
  93.1 2.0 %shard_map.71.refs_23_ = bf16[2,256,256]{2,1,0:T(8,128)(2,1)S(1)} custom-call(s32[2,8,8]{2,1,0:T(8,128)S(1)} %copy-done.1, s32[2,2,8]{2,1,0:T(2,128)S(1)} %copy-done.2, s32[2,2]{1,0:T(2,128)S(1)} %copy-done.3, bf16[3,2,256,512]{3,2,1,0:T(8,128)(2,1)S(1)} %copy-done, bf16[2,256,256]{2,1,0:T(8,128)(2,1)S(1)} %get-tuple-element.42.inv, ...), custom_call_target="tpu_custom_call" | custom-call | flops 603979776 | bytes 11141776 | tf_op jit(solution)/shard_map/pallas_call | solution.py:56
  95.5 2.0 %collective-permute-done.23.refs_19_ = bf16[1,256,256]{2,1,0:T(8,128)(2,1)S(1)} collective-permute-done((bf16[1,256,256]{2,1,0:T(8,128)(2,1)S(1)}, bf16[1,256,256]{2,1,0:T(8,128)(2,1)S(1)}, u32[]{:S(2)}, u32[]{:S(2)}) %collective-permute-start.23) | collective-permute-done | bytes 131104 | tf_op jit(solution)/shard_map/ppermute | solution.py:17
  97.5 2.7 %shard_map.72 = bf16[3,2,256,512]{3,2,1,0:T(8,128)(2,1)} custom-call(s32[2,8,8]{2,1,0:T(8,128)S(1)} %copy-done.1, s32[2,2,8]{2,1,0:T(2,128)S(1)} %copy-done.2, s32[2,2]{1,0:T(2,128)S(1)} %copy-done.3, bf16[3,2,256,512]{3,2,1,0:T(8,128)(2,1)S(1)} %copy-done, bf16[2,256,256]{2,1,0:T(8,128)(2,1)S(1)} %get-tuple-element.42.inv, ...), custom_call_target="tpu_custom_call" | custom-call | flops 603979776 | bytes 13501072 | tf_op jit(solution)/shard_map/pallas_call | solution.py:56
  (41 shorter events, 10.0 us)
Async XLA Ops:
  0.9 5.8 %collective-permute-start.1 = (bf16[128,256]{1,0:T(8,128)(2,1)S(1)}, bf16[128,256]{1,0:T(8,128)(2,1)S(1)}, u32[]{:S(2)}, u32[]{:S(2)}) collective-permute-start(bf16[128,256]{1,0:T(8,128)(2,1)S(1)} %bitcast.7), channel_id=1, source_target_pairs={{0,1},{1,0},{2,3},{3,2},{4,5},{5,4},{6,7},{7,6},{8,9},{9,8},{10,11... | collective-permute-start | bytes 196616 | tf_op jit(solution)/shard_map/ppermute | solution.py:17
  1.4 5.3 %collective-permute-start = (bf16[128,256]{1,0:T(8,128)(2,1)S(1)}, bf16[128,256]{1,0:T(8,128)(2,1)S(1)}, u32[]{:S(2)}, u32[]{:S(2)}) collective-permute-start(bf16[128,256]{1,0:T(8,128)(2,1)S(1)} %bitcast.8), channel_id=1, source_target_pairs={{0,2},{1,3},{2,0},{3,1},{4,6},{5,7},{6,4},{7,5},{8,10},{9,11},{10,... | collective-permute-start | bytes 196616 | tf_op jit(solution)/shard_map/ppermute | solution.py:17
  5.3 1.4 %copy-start = (bf16[3,2,256,512]{3,2,1,0:T(8,128)(2,1)S(1)}, bf16[3,2,256,512]{3,2,1,0:T(8,128)(2,1)}, u32[]{:S(2)}) copy-start(bf16[3,2,256,512]{3,2,1,0:T(8,128)(2,1)} %noise.7) | copy-start | bytes 4718596
  5.3 2.7 %copy-start.1 = (s32[2,8,8]{2,1,0:T(8,128)S(1)}, s32[2,8,8]{2,1,0:T(8,128)}, u32[]{:S(2)}) copy-start(s32[2,8,8]{2,1,0:T(8,128)} %picks.15) | copy-start | bytes 1540
  6.7 1.3 %collective-permute-start.2 = (bf16[128,256]{1,0:T(8,128)(2,1)S(1)}, bf16[128,256]{1,0:T(8,128)(2,1)S(1)}, u32[]{:S(2)}, u32[]{:S(2)}) collective-permute-start(bf16[128,256]{1,0:T(8,128)(2,1)S(1)} %collective-permute-done.refs_1_), channel_id=1, source_target_pairs={{0,1},{1,0},{2,3},{3,2},{4,5},{5,4},{6,7},{7,6},{8,9},{9,8},{10,11... | collective-permute-start | bytes 196616 | tf_op jit(solution)/shard_map/ppermute | solution.py:17
  8.4 29.1 %collective-permute-start.7 = (bf16[2304,256]{1,0:T(8,128)(2,1)S(1)}, bf16[2304,256]{1,0:T(8,128)(2,1)S(1)}, u32[]{:S(2)}, u32[]{:S(2)}) collective-permute-start(bf16[2304,256]{1,0:T(8,128)(2,1)S(1)} %get-tuple-element.36.refs_3_), channel_id=1, source_target_pairs={{0,2},{1,3},{2,0},{3,1},{4,6},{5,7},{6,4},{7,5},{8,10},{9,11},{10,... | collective-permute-start | bytes 3538952 | tf_op jit(solution)/shard_map/ppermute | solution.py:17
  10.2 27.3 %collective-permute-start.3 = (bf16[2,256,512]{2,1,0:T(8,128)(2,1)S(1)}, bf16[2,256,512]{2,1,0:T(8,128)(2,1)S(1)}, u32[]{:S(2)}, u32[]{:S(2)}) collective-permute-start(bf16[2,256,512]{2,1,0:T(8,128)(2,1)S(1)} %get-tuple-element.32.refs_4_.refs_20_), channel_id=1, source_target_pairs={{0,16},{4,20},{8,24},{12,28},{16,0},{20,4},{24,8},{28,12},{1,17},{... | collective-permute-start | bytes 1572872 | tf_op jit(solution)/shard_map/ppermute | solution.py:17
  12.8 8.3 %collective-permute-start.4 = (bf16[1,256,512]{2,1,0:T(8,128)(2,1)S(1)}, bf16[1,256,512]{2,1,0:T(8,128)(2,1)S(1)}, u32[]{:S(2)}, u32[]{:S(2)}) collective-permute-start(bf16[1,256,512]{2,1,0:T(8,128)(2,1)S(1)} %get-tuple-element.33), channel_id=1, source_target_pairs={{0,4},{4,0},{8,12},{12,8},{16,20},{20,16},{24,28},{28,24},{1,5},{5... | collective-permute-start | bytes 786440 | tf_op jit(solution)/shard_map/ppermute | solution.py:17
  14.3 16.5 %collective-permute-start.5 = (bf16[1,256,512]{2,1,0:T(8,128)(2,1)S(1)}, bf16[1,256,512]{2,1,0:T(8,128)(2,1)S(1)}, u32[]{:S(2)}, u32[]{:S(2)}) collective-permute-start(bf16[1,256,512]{2,1,0:T(8,128)(2,1)S(1)} %get-tuple-element.34), channel_id=1, source_target_pairs={{0,8},{4,12},{8,0},{12,4},{16,24},{20,28},{24,16},{28,20},{1,9},{5... | collective-permute-start | bytes 786440 | tf_op jit(solution)/shard_map/ppermute | solution.py:17
  15.9 21.6 %collective-permute-start.6 = (bf16[1,256,512]{2,1,0:T(8,128)(2,1)S(1)}, bf16[1,256,512]{2,1,0:T(8,128)(2,1)S(1)}, u32[]{:S(2)}, u32[]{:S(2)}) collective-permute-start(bf16[1,256,512]{2,1,0:T(8,128)(2,1)S(1)} %get-tuple-element.35), channel_id=1, source_target_pairs={{0,12},{4,8},{8,4},{12,0},{16,28},{20,24},{24,20},{28,16},{1,13},{... | collective-permute-start | bytes 786440 | tf_op jit(solution)/shard_map/ppermute | solution.py:17
  37.7 4.1 %collective-permute-start.8 = (bf16[2304,256]{1,0:T(8,128)(2,1)S(1)}, bf16[2304,256]{1,0:T(8,128)(2,1)S(1)}, u32[]{:S(2)}, u32[]{:S(2)}) collective-permute-start(bf16[2304,256]{1,0:T(8,128)(2,1)S(1)} %get-tuple-element.37.refs_0_), channel_id=1, source_target_pairs={{0,1},{1,0},{2,3},{3,2},{4,5},{5,4},{6,7},{7,6},{8,9},{9,8},{10,11... | collective-permute-start | bytes 3538952 | tf_op jit(solution)/shard_map/ppermute | solution.py:17
  37.8 4.5 %collective-permute-start.9 = (bf16[2304,256]{1,0:T(8,128)(2,1)S(1)}, bf16[2304,256]{1,0:T(8,128)(2,1)S(1)}, u32[]{:S(2)}, u32[]{:S(2)}) collective-permute-start(bf16[2304,256]{1,0:T(8,128)(2,1)S(1)} %get-tuple-element.38.refs_1_), channel_id=1, source_target_pairs={{0,1},{1,0},{2,3},{3,2},{4,5},{5,4},{6,7},{7,6},{8,9},{9,8},{10,11... | collective-permute-start | bytes 3538952 | tf_op jit(solution)/shard_map/ppermute | solution.py:17
  38.3 5.5 %collective-permute-start.13 = (bf16[1,256,256]{2,1,0:T(8,128)(2,1)S(1)}, bf16[1,256,256]{2,1,0:T(8,128)(2,1)S(1)}, u32[]{:S(2)}, u32[]{:S(2)}) collective-permute-start(bf16[1,256,256]{2,1,0:T(8,128)(2,1)S(1)} %get-tuple-element.47), channel_id=1, source_target_pairs={{0,4},{4,0},{8,12},{12,8},{16,20},{20,16},{24,28},{28,24},{1,5},{5... | collective-permute-start | bytes 393224 | tf_op jit(solution)/shard_map/ppermute | solution.py:17
  39.8 6.4 %collective-permute-start.14 = (bf16[1,256,256]{2,1,0:T(8,128)(2,1)S(1)}, bf16[1,256,256]{2,1,0:T(8,128)(2,1)S(1)}, u32[]{:S(2)}, u32[]{:S(2)}) collective-permute-start(bf16[1,256,256]{2,1,0:T(8,128)(2,1)S(1)} %get-tuple-element.48), channel_id=1, source_target_pairs={{0,8},{4,12},{8,0},{12,4},{16,24},{20,28},{24,16},{28,20},{1,9},{5... | collective-permute-start | bytes 393224 | tf_op jit(solution)/shard_map/ppermute | solution.py:17
  40.6 7.2 %collective-permute-start.15 = (bf16[1,256,256]{2,1,0:T(8,128)(2,1)S(1)}, bf16[1,256,256]{2,1,0:T(8,128)(2,1)S(1)}, u32[]{:S(2)}, u32[]{:S(2)}) collective-permute-start(bf16[1,256,256]{2,1,0:T(8,128)(2,1)S(1)} %get-tuple-element.49), channel_id=1, source_target_pairs={{0,12},{4,8},{8,4},{12,0},{16,28},{20,24},{24,20},{28,16},{1,13},{... | collective-permute-start | bytes 393224 | tf_op jit(solution)/shard_map/ppermute | solution.py:17
  42.3 5.5 %copy-start.2 = (s32[2,2,8]{2,1,0:T(2,128)S(1)}, s32[2,2,8]{2,1,0:T(2,128)}, u32[]{:S(2)}) copy-start(s32[2,2,8]{2,1,0:T(2,128)} %lists.7) | copy-start | bytes 388
  42.3 5.5 %copy-start.3 = (s32[2,2]{1,0:T(2,128)S(1)}, s32[2,2]{1,0:T(2,128)}, u32[]{:S(2)}) copy-start(s32[2,2]{1,0:T(2,128)} %counts.7) | copy-start | bytes 52
  49.7 18.4 %collective-permute-start.18 = (bf16[2,256,256]{2,1,0:T(8,128)(2,1)S(1)}, bf16[2,256,256]{2,1,0:T(8,128)(2,1)S(1)}, u32[]{:S(2)}, u32[]{:S(2)}) collective-permute-start(bf16[2,256,256]{2,1,0:T(8,128)(2,1)S(1)} %shard_map.67.refs_12_.refs_0_.refs_21_), channel_id=1, source_target_pairs={{0,16},{4,20},{8,24},{12,28},{16,0},{20,4},{24,8},{28,12},{1,17},{... | collective-permute-start | bytes 786440 | tf_op jit(solution)/shard_map/ppermute | solution.py:17
  51.6 5.5 %collective-permute-start.10 = (bf16[1,256,256]{2,1,0:T(8,128)(2,1)S(1)}, bf16[1,256,256]{2,1,0:T(8,128)(2,1)S(1)}, u32[]{:S(2)}, u32[]{:S(2)}) collective-permute-start(bf16[1,256,256]{2,1,0:T(8,128)(2,1)S(1)} %get-tuple-element.43), channel_id=1, source_target_pairs={{0,4},{4,0},{8,12},{12,8},{16,20},{20,16},{24,28},{28,24},{1,5},{5... | collective-permute-start | bytes 393224 | tf_op jit(solution)/shard_map/ppermute | solution.py:17
  53.1 7.6 %collective-permute-start.11 = (bf16[1,256,256]{2,1,0:T(8,128)(2,1)S(1)}, bf16[1,256,256]{2,1,0:T(8,128)(2,1)S(1)}, u32[]{:S(2)}, u32[]{:S(2)}) collective-permute-start(bf16[1,256,256]{2,1,0:T(8,128)(2,1)S(1)} %get-tuple-element.44), channel_id=1, source_target_pairs={{0,8},{4,12},{8,0},{12,4},{16,24},{20,28},{24,16},{28,20},{1,9},{5... | collective-permute-start | bytes 393224 | tf_op jit(solution)/shard_map/ppermute | solution.py:17
  54.7 11.1 %collective-permute-start.12 = (bf16[1,256,256]{2,1,0:T(8,128)(2,1)S(1)}, bf16[1,256,256]{2,1,0:T(8,128)(2,1)S(1)}, u32[]{:S(2)}, u32[]{:S(2)}) collective-permute-start(bf16[1,256,256]{2,1,0:T(8,128)(2,1)S(1)} %get-tuple-element.45), channel_id=1, source_target_pairs={{0,12},{4,8},{8,4},{12,0},{16,28},{20,24},{24,20},{28,16},{1,13},{... | collective-permute-start | bytes 393224 | tf_op jit(solution)/shard_map/ppermute | solution.py:17
  67.8 10.5 %collective-permute-start.16 = (bf16[2,256,256]{2,1,0:T(8,128)(2,1)S(1)}, bf16[2,256,256]{2,1,0:T(8,128)(2,1)S(1)}, u32[]{:S(2)}, u32[]{:S(2)}) collective-permute-start(bf16[2,256,256]{2,1,0:T(8,128)(2,1)S(1)} %get-tuple-element.51), channel_id=1, source_target_pairs={{0,4},{4,0},{8,12},{12,8},{16,20},{20,16},{24,28},{28,24},{1,5},{5... | collective-permute-start | bytes 786440 | tf_op jit(solution)/shard_map/ppermute | solution.py:17
  68.2 24.9 %collective-permute-start.19 = (bf16[3,256,256]{2,1,0:T(8,128)(2,1)S(1)}, bf16[3,256,256]{2,1,0:T(8,128)(2,1)S(1)}, u32[]{:S(2)}, u32[]{:S(2)}) collective-permute-start(bf16[3,256,256]{2,1,0:T(8,128)(2,1)S(1)} %get-tuple-element.53), channel_id=1, source_target_pairs={{0,12},{4,8},{8,4},{12,0},{16,28},{20,24},{24,20},{28,16},{1,13},{... | collective-permute-start | bytes 1179656 | tf_op jit(solution)/shard_map/ppermute | solution.py:17
  69.0 19.9 %collective-permute-start.17 = (bf16[2,256,256]{2,1,0:T(8,128)(2,1)S(1)}, bf16[2,256,256]{2,1,0:T(8,128)(2,1)S(1)}, u32[]{:S(2)}, u32[]{:S(2)}) collective-permute-start(bf16[2,256,256]{2,1,0:T(8,128)(2,1)S(1)} %get-tuple-element.52), channel_id=1, source_target_pairs={{0,8},{4,12},{8,0},{12,4},{16,24},{20,28},{24,16},{28,20},{1,9},{5... | collective-permute-start | bytes 786440 | tf_op jit(solution)/shard_map/ppermute | solution.py:17
  71.6 17.9 %collective-permute-start.20 = (bf16[2,256,256]{2,1,0:T(8,128)(2,1)S(1)}, bf16[2,256,256]{2,1,0:T(8,128)(2,1)S(1)}, u32[]{:S(2)}, u32[]{:S(2)}) collective-permute-start(bf16[2,256,256]{2,1,0:T(8,128)(2,1)S(1)} %get-tuple-element.50.refs_1_.refs_12_.refs_22_), channel_id=1, source_target_pairs={{0,16},{4,20},{8,24},{12,28},{16,0},{20,4},{24,8},{28,12},{1,17},{... | collective-permute-start | bytes 786440 | tf_op jit(solution)/shard_map/ppermute | solution.py:17
  71.6 20.1 %collective-permute-start.24 = (bf16[1,256,256]{2,1,0:T(8,128)(2,1)S(1)}, bf16[1,256,256]{2,1,0:T(8,128)(2,1)S(1)}, u32[]{:S(2)}, u32[]{:S(2)}) collective-permute-start(bf16[1,256,256]{2,1,0:T(8,128)(2,1)S(1)} %get-tuple-element.57), channel_id=1, source_target_pairs={{0,4},{4,0},{8,12},{12,8},{16,20},{20,16},{24,28},{28,24},{1,5},{5... | collective-permute-start | bytes 393224 | tf_op jit(solution)/shard_map/ppermute | solution.py:17
  78.3 14.9 %collective-permute-start.25 = (bf16[1,256,256]{2,1,0:T(8,128)(2,1)S(1)}, bf16[1,256,256]{2,1,0:T(8,128)(2,1)S(1)}, u32[]{:S(2)}, u32[]{:S(2)}) collective-permute-start(bf16[1,256,256]{2,1,0:T(8,128)(2,1)S(1)} %get-tuple-element.58), channel_id=1, source_target_pairs={{0,8},{4,12},{8,0},{12,4},{16,24},{20,28},{24,16},{28,20},{1,9},{5... | collective-permute-start | bytes 393224 | tf_op jit(solution)/shard_map/ppermute | solution.py:17
  89.6 5.6 %collective-permute-start.21 = (bf16[1,256,256]{2,1,0:T(8,128)(2,1)S(1)}, bf16[1,256,256]{2,1,0:T(8,128)(2,1)S(1)}, u32[]{:S(2)}, u32[]{:S(2)}) collective-permute-start(bf16[1,256,256]{2,1,0:T(8,128)(2,1)S(1)} %get-tuple-element.54), channel_id=1, source_target_pairs={{0,4},{4,0},{8,12},{12,8},{16,20},{20,16},{24,28},{28,24},{1,5},{5... | collective-permute-start | bytes 393224 | tf_op jit(solution)/shard_map/ppermute | solution.py:17
  90.5 5.0 %collective-permute-start.22 = (bf16[1,256,256]{2,1,0:T(8,128)(2,1)S(1)}, bf16[1,256,256]{2,1,0:T(8,128)(2,1)S(1)}, u32[]{:S(2)}, u32[]{:S(2)}) collective-permute-start(bf16[1,256,256]{2,1,0:T(8,128)(2,1)S(1)} %get-tuple-element.55), channel_id=1, source_target_pairs={{0,8},{4,12},{8,0},{12,4},{16,24},{20,28},{24,16},{28,20},{1,9},{5... | collective-permute-start | bytes 393224 | tf_op jit(solution)/shard_map/ppermute | solution.py:17
  91.6 5.9 %collective-permute-start.23 = (bf16[1,256,256]{2,1,0:T(8,128)(2,1)S(1)}, bf16[1,256,256]{2,1,0:T(8,128)(2,1)S(1)}, u32[]{:S(2)}, u32[]{:S(2)}) collective-permute-start(bf16[1,256,256]{2,1,0:T(8,128)(2,1)S(1)} %get-tuple-element.56), channel_id=1, source_target_pairs={{0,12},{4,8},{8,4},{12,0},{16,28},{20,24},{24,20},{28,16},{1,13},{... | collective-permute-start | bytes 393224 | tf_op jit(solution)/shard_map/ppermute | solution.py:17

commit v24 on v22

--- a/solution.py
+++ b/solution.py
@@ -142,11 +142,12 @@
             here = target.at[into, :, :, pl.ds(first, ref.shape[-1])]
             copies.append(pltpu.make_async_copy(ref, here, sems.at[at]))
             copies[-1].start()
+    steps = [0, half, *range(1, half), *range(half + 1, owners)]
     for at, (ref, place) in enumerate(zip(known, places, strict=True)):
-        step = at % owners
+        source, step = at // owners, steps[at % owners]
         if step % half == 0:
-            place = entry_of(picks[at // owners], myself, myself ^ step)
-        table[at] = ref[place] if ref.shape[-1] == wide else ref[place, :, columns]
+            place = entry_of(picks[source], myself, myself ^ step)
+        table[source * owners + step] = ref[place] if ref.shape[-1] == wide else ref[place, :, columns]
     empty = level * owners
     table[empty] = jnp.zeros_like(table[empty])
     entries = lists[level - 1]
@@ -228,8 +229,8 @@
     for at in chunks:
         distant, sends = take(sends, half - 1)
         pieces[0].append([
-            (solved, 0), *((ref, 0) for ref in got),
-            (far, 0), *((ref, 0) for ref in near(distant)),
+            (solved, 0), (far, 0), *((ref, 0) for ref in got),
+            *((ref, 0) for ref in near(distant)),
         ])
 
     for level in range(1, levels):
@@ -275,8 +276,8 @@
                 (picks, far[at], *waits),
             )
             pieces[level].append([
-                (solved[at], 0), *((ref, at) for ref in got),
-                (far[at], 0), *((ref, 0) for ref in near(sends)),
+                (solved[at], 0), (far[at], 0), *((ref, at) for ref in got),
+                *((ref, 0) for ref in near(sends)),
             ])
 
 

time: 93.2 us -> 93.2 us (level)
  no operation moved by 1% of the time
where the time goes in v24:
time: 93.2 us; the launch traced here: 93 us
  waiting for transfers between devices  50.2 us (54%)
  starting transfers between devices  30.8 us (33%)
  Pallas kernels  9.54 us (10%)
  local copies, waits for them, and re-layouts  2.24 us (2%)
    ppermute x27, waiting for transfers between devices, hop(): return lax.ppermute(value, axis, [(at, at ^ step) for at in range(size)])  50.2 us
    ppermute x27, starting transfers between devices, hop(): return lax.ppermute(value, axis, [(at, at ^ step) for at in range(size)])  30.8 us
    pallas_call x9, Pallas kernels, call(): pl.pallas_call(kernel, out_shape=outs, in_specs=[VMEM] * len(arrays), out...  9.54 us
  transfers between devices with their start and end apart: 27, of which 14 were waited for; matrix products, arithmetic and copies ran while one was open for 1% of the time, Pallas kernels for 7%

profile of v24, /device:TPU:0, one launch (start us, length us, event | category | flops | bytes accessed | tf_op | source)
XLA Modules:
  0.0 93.0 jit_solution(1353108650304500491)
XLA Ops:
  0.0 0.9 fusion.1
  1.4 2.6 %collective-permute-start = (bf16[128,256]{1,0:T(8,128)(2,1)S(1)}, bf16[128,256]{1,0:T(8,128)(2,1)S(1)}, u32[]{:S(2)}, u32[]{:S(2)}) collective-permute-start(bf16[128,256]{1,0:T(8,128)(2,1)S(1)} %bitcast.8), channel_id=1, source_target_pairs={{0,2},{1,3},{2,0},{3,1},{4,6},{5,7},{6,4},{7,5},{8,10},{9,11},{10,... | collective-permute-start | bytes 196616 | tf_op jit(solution)/shard_map/ppermute | solution.py:17
  4.0 1.3 %fusion = (bf16[1,2,2,256,256]{4,3,2,1,0:T(8,128)(2,1)S(1)}, bf16[1,2,2,256,256]{4,3,2,1,0:T(8,128)(2,1)S(1)}) fusion(bf16[2,2,2,256,256]{4,3,2,1,0:T(8,128)(2,1)} %param.8), kind=kLoop, calls=%fused_computation.2 | loop fusion | bytes 2097152 | tf_op jit(solution)/shard_map/slice | solution.py:194
  5.4 1.3 %collective-permute-done.refs_1_ = bf16[128,256]{1,0:T(8,128)(2,1)S(1)} collective-permute-done((bf16[128,256]{1,0:T(8,128)(2,1)S(1)}, bf16[128,256]{1,0:T(8,128)(2,1)S(1)}, u32[]{:S(2)}, u32[]{:S(2)}) %collective-permute-start) | collective-permute-done | bytes 65568 | tf_op jit(solution)/shard_map/ppermute | solution.py:17
  6.7 1.2 %collective-permute-done.2.refs_3_ = bf16[128,256]{1,0:T(8,128)(2,1)S(1)} collective-permute-done((bf16[128,256]{1,0:T(8,128)(2,1)S(1)}, bf16[128,256]{1,0:T(8,128)(2,1)S(1)}, u32[]{:S(2)}, u32[]{:S(2)}) %collective-permute-start.2) | collective-permute-done | bytes 65568 | tf_op jit(solution)/shard_map/ppermute | solution.py:17
  8.4 1.8 %collective-permute-start.7 = (bf16[2304,256]{1,0:T(8,128)(2,1)S(1)}, bf16[2304,256]{1,0:T(8,128)(2,1)S(1)}, u32[]{:S(2)}, u32[]{:S(2)}) collective-permute-start(bf16[2304,256]{1,0:T(8,128)(2,1)S(1)} %get-tuple-element.37.refs_3_), channel_id=1, source_target_pairs={{0,2},{1,3},{2,0},{3,1},{4,6},{5,7},{6,4},{7,5},{8,10},{9,11},{10,... | collective-permute-start | bytes 3538952 | tf_op jit(solution)/shard_map/ppermute | solution.py:17
  10.2 2.6 %collective-permute-start.3 = (bf16[2,256,512]{2,1,0:T(8,128)(2,1)S(1)}, bf16[2,256,512]{2,1,0:T(8,128)(2,1)S(1)}, u32[]{:S(2)}, u32[]{:S(2)}) collective-permute-start(bf16[2,256,512]{2,1,0:T(8,128)(2,1)S(1)} %get-tuple-element.33.refs_4_.refs_20_), channel_id=1, source_target_pairs={{0,16},{4,20},{8,24},{12,28},{16,0},{20,4},{24,8},{28,12},{1,17},{... | collective-permute-start | bytes 1572872 | tf_op jit(solution)/shard_map/ppermute | solution.py:17
  12.8 1.5 %collective-permute-start.4 = (bf16[1,256,512]{2,1,0:T(8,128)(2,1)S(1)}, bf16[1,256,512]{2,1,0:T(8,128)(2,1)S(1)}, u32[]{:S(2)}, u32[]{:S(2)}) collective-permute-start(bf16[1,256,512]{2,1,0:T(8,128)(2,1)S(1)} %get-tuple-element.34), channel_id=1, source_target_pairs={{0,4},{4,0},{8,12},{12,8},{16,20},{20,16},{24,28},{28,24},{1,5},{5... | collective-permute-start | bytes 786440 | tf_op jit(solution)/shard_map/ppermute | solution.py:17
  14.3 1.6 %collective-permute-start.5 = (bf16[1,256,512]{2,1,0:T(8,128)(2,1)S(1)}, bf16[1,256,512]{2,1,0:T(8,128)(2,1)S(1)}, u32[]{:S(2)}, u32[]{:S(2)}) collective-permute-start(bf16[1,256,512]{2,1,0:T(8,128)(2,1)S(1)} %get-tuple-element.35), channel_id=1, source_target_pairs={{0,8},{4,12},{8,0},{12,4},{16,24},{20,28},{24,16},{28,20},{1,9},{5... | collective-permute-start | bytes 786440 | tf_op jit(solution)/shard_map/ppermute | solution.py:17
  16.3 4.9 %collective-permute-done.4.refs_0_.refs_6_ = bf16[1,256,512]{2,1,0:T(8,128)(2,1)S(1)} collective-permute-done((bf16[1,256,512]{2,1,0:T(8,128)(2,1)S(1)}, bf16[1,256,512]{2,1,0:T(8,128)(2,1)S(1)}, u32[]{:S(2)}, u32[]{:S(2)}) %collective-permute-start.4) | collective-permute-done | bytes 262176 | tf_op jit(solution)/shard_map/ppermute | solution.py:17
  21.1 9.6 %collective-permute-done.5.refs_1_.refs_7_ = bf16[1,256,512]{2,1,0:T(8,128)(2,1)S(1)} collective-permute-done((bf16[1,256,512]{2,1,0:T(8,128)(2,1)S(1)}, bf16[1,256,512]{2,1,0:T(8,128)(2,1)S(1)}, u32[]{:S(2)}, u32[]{:S(2)}) %collective-permute-start.5) | collective-permute-done | bytes 262176 | tf_op jit(solution)/shard_map/ppermute | solution.py:17
  30.8 6.7 %collective-permute-done.6.refs_2_.refs_8_ = bf16[1,256,512]{2,1,0:T(8,128)(2,1)S(1)} collective-permute-done((bf16[1,256,512]{2,1,0:T(8,128)(2,1)S(1)}, bf16[1,256,512]{2,1,0:T(8,128)(2,1)S(1)}, u32[]{:S(2)}, u32[]{:S(2)}) %collective-permute-start.6) | collective-permute-done | bytes 262176 | tf_op jit(solution)/shard_map/ppermute | solution.py:17
  38.3 1.5 %collective-permute-start.13 = (bf16[1,256,256]{2,1,0:T(8,128)(2,1)S(1)}, bf16[1,256,256]{2,1,0:T(8,128)(2,1)S(1)}, u32[]{:S(2)}, u32[]{:S(2)}) collective-permute-start(bf16[1,256,256]{2,1,0:T(8,128)(2,1)S(1)} %get-tuple-element.48), channel_id=1, source_target_pairs={{0,4},{4,0},{8,12},{12,8},{16,20},{20,16},{24,28},{28,24},{1,5},{5... | collective-permute-start | bytes 393224 | tf_op jit(solution)/shard_map/ppermute | solution.py:17
  40.6 1.2 %collective-permute-start.15 = (bf16[1,256,256]{2,1,0:T(8,128)(2,1)S(1)}, bf16[1,256,256]{2,1,0:T(8,128)(2,1)S(1)}, u32[]{:S(2)}, u32[]{:S(2)}) collective-permute-start(bf16[1,256,256]{2,1,0:T(8,128)(2,1)S(1)} %get-tuple-element.50), channel_id=1, source_target_pairs={{0,12},{4,8},{8,4},{12,0},{16,28},{20,24},{24,20},{28,16},{1,13},{... | collective-permute-start | bytes 393224 | tf_op jit(solution)/shard_map/ppermute | solution.py:17
  42.3 1.6 %collective-permute-start.10 = (bf16[1,256,256]{2,1,0:T(8,128)(2,1)S(1)}, bf16[1,256,256]{2,1,0:T(8,128)(2,1)S(1)}, u32[]{:S(2)}, u32[]{:S(2)}) collective-permute-start(bf16[1,256,256]{2,1,0:T(8,128)(2,1)S(1)} %get-tuple-element.44), channel_id=1, source_target_pairs={{0,4},{4,0},{8,12},{12,8},{16,20},{20,16},{24,28},{28,24},{1,5},{5... | collective-permute-start | bytes 393224 | tf_op jit(solution)/shard_map/ppermute | solution.py:17
  44.7 1.2 %collective-permute-start.12 = (bf16[1,256,256]{2,1,0:T(8,128)(2,1)S(1)}, bf16[1,256,256]{2,1,0:T(8,128)(2,1)S(1)}, u32[]{:S(2)}, u32[]{:S(2)}) collective-permute-start(bf16[1,256,256]{2,1,0:T(8,128)(2,1)S(1)} %get-tuple-element.46), channel_id=1, source_target_pairs={{0,12},{4,8},{8,4},{12,0},{16,28},{20,24},{24,20},{28,16},{1,13},{... | collective-permute-start | bytes 393224 | tf_op jit(solution)/shard_map/ppermute | solution.py:17
  46.2 2.8 %collective-permute-done.15.refs_11_ = bf16[1,256,256]{2,1,0:T(8,128)(2,1)S(1)} collective-permute-done((bf16[1,256,256]{2,1,0:T(8,128)(2,1)S(1)}, bf16[1,256,256]{2,1,0:T(8,128)(2,1)S(1)}, u32[]{:S(2)}, u32[]{:S(2)}) %collective-permute-start.15) | collective-permute-done | bytes 131104 | tf_op jit(solution)/shard_map/ppermute | solution.py:17
  48.9 1.9 %shard_map.67.refs_12_.refs_21_ = bf16[2,256,256]{2,1,0:T(8,128)(2,1)S(1)} custom-call(s32[2,8,8]{2,1,0:T(8,128)S(1)} %copy-done.1, s32[2,2,8]{2,1,0:T(2,128)S(1)} %copy-done.2, s32[2,2]{1,0:T(2,128)S(1)} %copy-done.3, bf16[3,2,256,512]{3,2,1,0:T(8,128)(2,1)S(1)} %copy-done, bf16[2,256,256]{2,1,0:T(8,128)(2,1)S(1)} %get-tuple-element.47.inv, ...), custom_call_target="tpu_custom_call" | custom-call | flops 603979776 | bytes 9044624 | tf_op jit(solution)/shard_map/pallas_call | solution.py:56
  50.9 1.7 %collective-permute-start.23 = (bf16[2,256,256]{2,1,0:T(8,128)(2,1)S(1)}, bf16[2,256,256]{2,1,0:T(8,128)(2,1)S(1)}, u32[]{:S(2)}, u32[]{:S(2)}) collective-permute-start(bf16[2,256,256]{2,1,0:T(8,128)(2,1)S(1)} %shard_map.67.refs_12_.refs_21_), channel_id=1, source_target_pairs={{0,16},{4,20},{8,24},{12,28},{16,0},{20,4},{24,8},{28,12},{1,17},{... | collective-permute-start | bytes 786440 | tf_op jit(solution)/shard_map/ppermute | solution.py:17
  52.6 1.6 %collective-permute-done.12.refs_11_ = bf16[1,256,256]{2,1,0:T(8,128)(2,1)S(1)} collective-permute-done((bf16[1,256,256]{2,1,0:T(8,128)(2,1)S(1)}, bf16[1,256,256]{2,1,0:T(8,128)(2,1)S(1)}, u32[]{:S(2)}, u32[]{:S(2)}) %collective-permute-start.12) | collective-permute-done | bytes 131104 | tf_op jit(solution)/shard_map/ppermute | solution.py:17
  54.2 2.0 %shard_map.68 = (bf16[2,256,256]{2,1,0:T(8,128)(2,1)S(1)}, bf16[2,256,256]{2,1,0:T(8,128)(2,1)S(1)}, bf16[2,256,256]{2,1,0:T(8,128)(2,1)S(1)}, bf16[2,256,256]{2,1,0:T(8,128)(2,1)S(1)}) custom-call(s32[2,8,8]{2,1,0:T(8,128)S(1)} %copy-done.1, s32[2,2,8]{2,1,0:T(2,128)S(1)} %copy-done.2, s32[2,2]{1,0:T(2,128)S(1)} %copy-done.3, ...), custom_call_target="tpu_custom_call" | custom-call | flops 603979776 | bytes 10093200 | tf_op jit(solution)/shard_map/pallas_call | solution.py:56
  56.1 3.3 %collective-permute-start.17 = (bf16[2,256,256]{2,1,0:T(8,128)(2,1)S(1)}, bf16[2,256,256]{2,1,0:T(8,128)(2,1)S(1)}, u32[]{:S(2)}, u32[]{:S(2)}) collective-permute-start(bf16[2,256,256]{2,1,0:T(8,128)(2,1)S(1)} %get-tuple-element.52), channel_id=1, source_target_pairs={{0,4},{4,0},{8,12},{12,8},{16,20},{20,16},{24,28},{28,24},{1,5},{5... | collective-permute-start | bytes 786440 | tf_op jit(solution)/shard_map/ppermute | solution.py:17
  59.5 1.5 %collective-permute-start.19 = (bf16[2,256,256]{2,1,0:T(8,128)(2,1)S(1)}, bf16[2,256,256]{2,1,0:T(8,128)(2,1)S(1)}, u32[]{:S(2)}, u32[]{:S(2)}) collective-permute-start(bf16[2,256,256]{2,1,0:T(8,128)(2,1)S(1)} %get-tuple-element.54), channel_id=1, source_target_pairs={{0,12},{4,8},{8,4},{12,0},{16,28},{20,24},{24,20},{28,16},{1,13},{... | collective-permute-start | bytes 786440 | tf_op jit(solution)/shard_map/ppermute | solution.py:17
  61.7 4.1 %collective-permute-done.23.far.refs_13_ = bf16[2,256,256]{2,1,0:T(8,128)(2,1)S(1)} collective-permute-done((bf16[2,256,256]{2,1,0:T(8,128)(2,1)S(1)}, bf16[2,256,256]{2,1,0:T(8,128)(2,1)S(1)}, u32[]{:S(2)}, u32[]{:S(2)}) %collective-permute-start.23) | collective-permute-done | bytes 262176 | tf_op jit(solution)/shard_map/ppermute | solution.py:17
  66.0 0.9 %collective-permute-start.24 = (bf16[1,256,256]{2,1,0:T(8,128)(2,1)S(1)}, bf16[1,256,256]{2,1,0:T(8,128)(2,1)S(1)}, u32[]{:S(2)}, u32[]{:S(2)}) collective-permute-start(bf16[1,256,256]{2,1,0:T(8,128)(2,1)S(1)} %get-tuple-element.58), channel_id=1, source_target_pairs={{0,4},{4,0},{8,12},{12,8},{16,20},{20,16},{24,28},{28,24},{1,5},{5... | collective-permute-start | bytes 393224 | tf_op jit(solution)/shard_map/ppermute | solution.py:17
  66.9 7.9 %collective-permute-done.18.refs_1_.refs_15_ = bf16[2,256,256]{2,1,0:T(8,128)(2,1)S(1)} collective-permute-done((bf16[2,256,256]{2,1,0:T(8,128)(2,1)S(1)}, bf16[2,256,256]{2,1,0:T(8,128)(2,1)S(1)}, u32[]{:S(2)}, u32[]{:S(2)}) %collective-permute-start.18) | collective-permute-done | bytes 262176 | tf_op jit(solution)/shard_map/ppermute | solution.py:17
  75.3 6.2 %collective-permute-done.19.refs_2_.refs_16_ = bf16[2,256,256]{2,1,0:T(8,128)(2,1)S(1)} collective-permute-done((bf16[2,256,256]{2,1,0:T(8,128)(2,1)S(1)}, bf16[2,256,256]{2,1,0:T(8,128)(2,1)S(1)}, u32[]{:S(2)}, u32[]{:S(2)}) %collective-permute-start.19) | collective-permute-done | bytes 262176 | tf_op jit(solution)/shard_map/ppermute | solution.py:17
  82.3 2.9 %collective-permute-start.22 = (bf16[1,256,256]{2,1,0:T(8,128)(2,1)S(1)}, bf16[1,256,256]{2,1,0:T(8,128)(2,1)S(1)}, u32[]{:S(2)}, u32[]{:S(2)}) collective-permute-start(bf16[1,256,256]{2,1,0:T(8,128)(2,1)S(1)} %get-tuple-element.57), channel_id=1, source_target_pairs={{0,12},{4,8},{8,4},{12,0},{16,28},{20,24},{24,20},{28,16},{1,13},{... | collective-permute-start | bytes 393224 | tf_op jit(solution)/shard_map/ppermute | solution.py:17
  85.2 1.9 %collective-permute-done.26.refs_19_ = bf16[1,256,256]{2,1,0:T(8,128)(2,1)S(1)} collective-permute-done((bf16[1,256,256]{2,1,0:T(8,128)(2,1)S(1)}, bf16[1,256,256]{2,1,0:T(8,128)(2,1)S(1)}, u32[]{:S(2)}, u32[]{:S(2)}) %collective-permute-start.26) | collective-permute-done | bytes 131104 | tf_op jit(solution)/shard_map/ppermute | solution.py:17
  87.1 2.0 %shard_map.71.refs_23_ = bf16[2,256,256]{2,1,0:T(8,128)(2,1)S(1)} custom-call(s32[2,8,8]{2,1,0:T(8,128)S(1)} %copy-done.1, s32[2,2,8]{2,1,0:T(2,128)S(1)} %copy-done.2, s32[2,2]{1,0:T(2,128)S(1)} %copy-done.3, bf16[3,2,256,512]{3,2,1,0:T(8,128)(2,1)S(1)} %copy-done, bf16[2,256,256]{2,1,0:T(8,128)(2,1)S(1)} %get-tuple-element.43.inv, ...), custom_call_target="tpu_custom_call" | custom-call | flops 603979776 | bytes 10748560 | tf_op jit(solution)/shard_map/pallas_call | solution.py:56
  89.1 1.1 %collective-permute-done.22.refs_19_ = bf16[1,256,256]{2,1,0:T(8,128)(2,1)S(1)} collective-permute-done((bf16[1,256,256]{2,1,0:T(8,128)(2,1)S(1)}, bf16[1,256,256]{2,1,0:T(8,128)(2,1)S(1)}, u32[]{:S(2)}, u32[]{:S(2)}) %collective-permute-start.22) | collective-permute-done | bytes 131104 | tf_op jit(solution)/shard_map/ppermute | solution.py:17
  90.3 2.7 %shard_map.72 = bf16[3,2,256,512]{3,2,1,0:T(8,128)(2,1)} custom-call(s32[2,8,8]{2,1,0:T(8,128)S(1)} %copy-done.1, s32[2,2,8]{2,1,0:T(2,128)S(1)} %copy-done.2, s32[2,2]{1,0:T(2,128)S(1)} %copy-done.3, bf16[3,2,256,512]{3,2,1,0:T(8,128)(2,1)S(1)} %copy-done, bf16[2,256,256]{2,1,0:T(8,128)(2,1)S(1)} %get-tuple-element.43.inv, ...), custom_call_target="tpu_custom_call" | custom-call | flops 603979776 | bytes 13370000 | tf_op jit(solution)/shard_map/pallas_call | solution.py:56
  (43 shorter events, 6.7 us)
Async XLA Ops:
  0.9 5.8 %collective-permute-start.1 = (bf16[128,256]{1,0:T(8,128)(2,1)S(1)}, bf16[128,256]{1,0:T(8,128)(2,1)S(1)}, u32[]{:S(2)}, u32[]{:S(2)}) collective-permute-start(bf16[128,256]{1,0:T(8,128)(2,1)S(1)} %bitcast.7), channel_id=1, source_target_pairs={{0,1},{1,0},{2,3},{3,2},{4,5},{5,4},{6,7},{7,6},{8,9},{9,8},{10,11... | collective-permute-start | bytes 196616 | tf_op jit(solution)/shard_map/ppermute | solution.py:17
  1.4 5.3 %collective-permute-start = (bf16[128,256]{1,0:T(8,128)(2,1)S(1)}, bf16[128,256]{1,0:T(8,128)(2,1)S(1)}, u32[]{:S(2)}, u32[]{:S(2)}) collective-permute-start(bf16[128,256]{1,0:T(8,128)(2,1)S(1)} %bitcast.8), channel_id=1, source_target_pairs={{0,2},{1,3},{2,0},{3,1},{4,6},{5,7},{6,4},{7,5},{8,10},{9,11},{10,... | collective-permute-start | bytes 196616 | tf_op jit(solution)/shard_map/ppermute | solution.py:17
  5.3 1.4 %copy-start = (bf16[3,2,256,512]{3,2,1,0:T(8,128)(2,1)S(1)}, bf16[3,2,256,512]{3,2,1,0:T(8,128)(2,1)}, u32[]{:S(2)}) copy-start(bf16[3,2,256,512]{3,2,1,0:T(8,128)(2,1)} %noise.7) | copy-start | bytes 4718596
  5.3 2.7 %copy-start.1 = (s32[2,8,8]{2,1,0:T(8,128)S(1)}, s32[2,8,8]{2,1,0:T(8,128)}, u32[]{:S(2)}) copy-start(s32[2,8,8]{2,1,0:T(8,128)} %picks.15) | copy-start | bytes 1540
  6.7 1.3 %collective-permute-start.2 = (bf16[128,256]{1,0:T(8,128)(2,1)S(1)}, bf16[128,256]{1,0:T(8,128)(2,1)S(1)}, u32[]{:S(2)}, u32[]{:S(2)}) collective-permute-start(bf16[128,256]{1,0:T(8,128)(2,1)S(1)} %collective-permute-done.refs_1_), channel_id=1, source_target_pairs={{0,1},{1,0},{2,3},{3,2},{4,5},{5,4},{6,7},{7,6},{8,9},{9,8},{10,11... | collective-permute-start | bytes 196616 | tf_op jit(solution)/shard_map/ppermute | solution.py:17
  8.4 29.1 %collective-permute-start.7 = (bf16[2304,256]{1,0:T(8,128)(2,1)S(1)}, bf16[2304,256]{1,0:T(8,128)(2,1)S(1)}, u32[]{:S(2)}, u32[]{:S(2)}) collective-permute-start(bf16[2304,256]{1,0:T(8,128)(2,1)S(1)} %get-tuple-element.37.refs_3_), channel_id=1, source_target_pairs={{0,2},{1,3},{2,0},{3,1},{4,6},{5,7},{6,4},{7,5},{8,10},{9,11},{10,... | collective-permute-start | bytes 3538952 | tf_op jit(solution)/shard_map/ppermute | solution.py:17
  10.2 27.3 %collective-permute-start.3 = (bf16[2,256,512]{2,1,0:T(8,128)(2,1)S(1)}, bf16[2,256,512]{2,1,0:T(8,128)(2,1)S(1)}, u32[]{:S(2)}, u32[]{:S(2)}) collective-permute-start(bf16[2,256,512]{2,1,0:T(8,128)(2,1)S(1)} %get-tuple-element.33.refs_4_.refs_20_), channel_id=1, source_target_pairs={{0,16},{4,20},{8,24},{12,28},{16,0},{20,4},{24,8},{28,12},{1,17},{... | collective-permute-start | bytes 1572872 | tf_op jit(solution)/shard_map/ppermute | solution.py:17
  12.8 8.3 %collective-permute-start.4 = (bf16[1,256,512]{2,1,0:T(8,128)(2,1)S(1)}, bf16[1,256,512]{2,1,0:T(8,128)(2,1)S(1)}, u32[]{:S(2)}, u32[]{:S(2)}) collective-permute-start(bf16[1,256,512]{2,1,0:T(8,128)(2,1)S(1)} %get-tuple-element.34), channel_id=1, source_target_pairs={{0,4},{4,0},{8,12},{12,8},{16,20},{20,16},{24,28},{28,24},{1,5},{5... | collective-permute-start | bytes 786440 | tf_op jit(solution)/shard_map/ppermute | solution.py:17
  14.3 16.5 %collective-permute-start.5 = (bf16[1,256,512]{2,1,0:T(8,128)(2,1)S(1)}, bf16[1,256,512]{2,1,0:T(8,128)(2,1)S(1)}, u32[]{:S(2)}, u32[]{:S(2)}) collective-permute-start(bf16[1,256,512]{2,1,0:T(8,128)(2,1)S(1)} %get-tuple-element.35), channel_id=1, source_target_pairs={{0,8},{4,12},{8,0},{12,4},{16,24},{20,28},{24,16},{28,20},{1,9},{5... | collective-permute-start | bytes 786440 | tf_op jit(solution)/shard_map/ppermute | solution.py:17
  15.9 21.6 %collective-permute-start.6 = (bf16[1,256,512]{2,1,0:T(8,128)(2,1)S(1)}, bf16[1,256,512]{2,1,0:T(8,128)(2,1)S(1)}, u32[]{:S(2)}, u32[]{:S(2)}) collective-permute-start(bf16[1,256,512]{2,1,0:T(8,128)(2,1)S(1)} %get-tuple-element.36), channel_id=1, source_target_pairs={{0,12},{4,8},{8,4},{12,0},{16,28},{20,24},{24,20},{28,16},{1,13},{... | collective-permute-start | bytes 786440 | tf_op jit(solution)/shard_map/ppermute | solution.py:17
  37.7 4.1 %collective-permute-start.8 = (bf16[2304,256]{1,0:T(8,128)(2,1)S(1)}, bf16[2304,256]{1,0:T(8,128)(2,1)S(1)}, u32[]{:S(2)}, u32[]{:S(2)}) collective-permute-start(bf16[2304,256]{1,0:T(8,128)(2,1)S(1)} %get-tuple-element.38.refs_0_), channel_id=1, source_target_pairs={{0,1},{1,0},{2,3},{3,2},{4,5},{5,4},{6,7},{7,6},{8,9},{9,8},{10,11... | collective-permute-start | bytes 3538952 | tf_op jit(solution)/shard_map/ppermute | solution.py:17
  37.8 4.5 %collective-permute-start.9 = (bf16[2304,256]{1,0:T(8,128)(2,1)S(1)}, bf16[2304,256]{1,0:T(8,128)(2,1)S(1)}, u32[]{:S(2)}, u32[]{:S(2)}) collective-permute-start(bf16[2304,256]{1,0:T(8,128)(2,1)S(1)} %get-tuple-element.39.refs_1_), channel_id=1, source_target_pairs={{0,1},{1,0},{2,3},{3,2},{4,5},{5,4},{6,7},{7,6},{8,9},{9,8},{10,11... | collective-permute-start | bytes 3538952 | tf_op jit(solution)/shard_map/ppermute | solution.py:17
  38.3 6.4 %collective-permute-start.13 = (bf16[1,256,256]{2,1,0:T(8,128)(2,1)S(1)}, bf16[1,256,256]{2,1,0:T(8,128)(2,1)S(1)}, u32[]{:S(2)}, u32[]{:S(2)}) collective-permute-start(bf16[1,256,256]{2,1,0:T(8,128)(2,1)S(1)} %get-tuple-element.48), channel_id=1, source_target_pairs={{0,4},{4,0},{8,12},{12,8},{16,20},{20,16},{24,28},{28,24},{1,5},{5... | collective-permute-start | bytes 393224 | tf_op jit(solution)/shard_map/ppermute | solution.py:17
  39.8 6.4 %collective-permute-start.14 = (bf16[1,256,256]{2,1,0:T(8,128)(2,1)S(1)}, bf16[1,256,256]{2,1,0:T(8,128)(2,1)S(1)}, u32[]{:S(2)}, u32[]{:S(2)}) collective-permute-start(bf16[1,256,256]{2,1,0:T(8,128)(2,1)S(1)} %get-tuple-element.49), channel_id=1, source_target_pairs={{0,8},{4,12},{8,0},{12,4},{16,24},{20,28},{24,16},{28,20},{1,9},{5... | collective-permute-start | bytes 393224 | tf_op jit(solution)/shard_map/ppermute | solution.py:17
  40.6 8.4 %collective-permute-start.15 = (bf16[1,256,256]{2,1,0:T(8,128)(2,1)S(1)}, bf16[1,256,256]{2,1,0:T(8,128)(2,1)S(1)}, u32[]{:S(2)}, u32[]{:S(2)}) collective-permute-start(bf16[1,256,256]{2,1,0:T(8,128)(2,1)S(1)} %get-tuple-element.50), channel_id=1, source_target_pairs={{0,12},{4,8},{8,4},{12,0},{16,28},{20,24},{24,20},{28,16},{1,13},{... | collective-permute-start | bytes 393224 | tf_op jit(solution)/shard_map/ppermute | solution.py:17
  42.3 6.6 %copy-start.2 = (s32[2,2,8]{2,1,0:T(2,128)S(1)}, s32[2,2,8]{2,1,0:T(2,128)}, u32[]{:S(2)}) copy-start(s32[2,2,8]{2,1,0:T(2,128)} %lists.7) | copy-start | bytes 388
  42.3 6.6 %copy-start.3 = (s32[2,2]{1,0:T(2,128)S(1)}, s32[2,2]{1,0:T(2,128)}, u32[]{:S(2)}) copy-start(s32[2,2]{1,0:T(2,128)} %counts.7) | copy-start | bytes 52
  42.3 10.2 %collective-permute-start.10 = (bf16[1,256,256]{2,1,0:T(8,128)(2,1)S(1)}, bf16[1,256,256]{2,1,0:T(8,128)(2,1)S(1)}, u32[]{:S(2)}, u32[]{:S(2)}) collective-permute-start(bf16[1,256,256]{2,1,0:T(8,128)(2,1)S(1)} %get-tuple-element.44), channel_id=1, source_target_pairs={{0,4},{4,0},{8,12},{12,8},{16,20},{20,16},{24,28},{28,24},{1,5},{5... | collective-permute-start | bytes 393224 | tf_op jit(solution)/shard_map/ppermute | solution.py:17
  43.9 8.6 %collective-permute-start.11 = (bf16[1,256,256]{2,1,0:T(8,128)(2,1)S(1)}, bf16[1,256,256]{2,1,0:T(8,128)(2,1)S(1)}, u32[]{:S(2)}, u32[]{:S(2)}) collective-permute-start(bf16[1,256,256]{2,1,0:T(8,128)(2,1)S(1)} %get-tuple-element.45), channel_id=1, source_target_pairs={{0,8},{4,12},{8,0},{12,4},{16,24},{20,28},{24,16},{28,20},{1,9},{5... | collective-permute-start | bytes 393224 | tf_op jit(solution)/shard_map/ppermute | solution.py:17
  44.7 9.4 %collective-permute-start.12 = (bf16[1,256,256]{2,1,0:T(8,128)(2,1)S(1)}, bf16[1,256,256]{2,1,0:T(8,128)(2,1)S(1)}, u32[]{:S(2)}, u32[]{:S(2)}) collective-permute-start(bf16[1,256,256]{2,1,0:T(8,128)(2,1)S(1)} %get-tuple-element.46), channel_id=1, source_target_pairs={{0,12},{4,8},{8,4},{12,0},{16,28},{20,24},{24,20},{28,16},{1,13},{... | collective-permute-start | bytes 393224 | tf_op jit(solution)/shard_map/ppermute | solution.py:17
  50.9 15.0 %collective-permute-start.23 = (bf16[2,256,256]{2,1,0:T(8,128)(2,1)S(1)}, bf16[2,256,256]{2,1,0:T(8,128)(2,1)S(1)}, u32[]{:S(2)}, u32[]{:S(2)}) collective-permute-start(bf16[2,256,256]{2,1,0:T(8,128)(2,1)S(1)} %shard_map.67.refs_12_.refs_21_), channel_id=1, source_target_pairs={{0,16},{4,20},{8,24},{12,28},{16,0},{20,4},{24,8},{28,12},{1,17},{... | collective-permute-start | bytes 786440 | tf_op jit(solution)/shard_map/ppermute | solution.py:17
  56.1 10.8 %collective-permute-start.17 = (bf16[2,256,256]{2,1,0:T(8,128)(2,1)S(1)}, bf16[2,256,256]{2,1,0:T(8,128)(2,1)S(1)}, u32[]{:S(2)}, u32[]{:S(2)}) collective-permute-start(bf16[2,256,256]{2,1,0:T(8,128)(2,1)S(1)} %get-tuple-element.52), channel_id=1, source_target_pairs={{0,4},{4,0},{8,12},{12,8},{16,20},{20,16},{24,28},{28,24},{1,5},{5... | collective-permute-start | bytes 786440 | tf_op jit(solution)/shard_map/ppermute | solution.py:17
  59.5 15.4 %collective-permute-start.18 = (bf16[2,256,256]{2,1,0:T(8,128)(2,1)S(1)}, bf16[2,256,256]{2,1,0:T(8,128)(2,1)S(1)}, u32[]{:S(2)}, u32[]{:S(2)}) collective-permute-start(bf16[2,256,256]{2,1,0:T(8,128)(2,1)S(1)} %get-tuple-element.53), channel_id=1, source_target_pairs={{0,8},{4,12},{8,0},{12,4},{16,24},{20,28},{24,16},{28,20},{1,9},{5... | collective-permute-start | bytes 786440 | tf_op jit(solution)/shard_map/ppermute | solution.py:17
  59.5 22.0 %collective-permute-start.19 = (bf16[2,256,256]{2,1,0:T(8,128)(2,1)S(1)}, bf16[2,256,256]{2,1,0:T(8,128)(2,1)S(1)}, u32[]{:S(2)}, u32[]{:S(2)}) collective-permute-start(bf16[2,256,256]{2,1,0:T(8,128)(2,1)S(1)} %get-tuple-element.54), channel_id=1, source_target_pairs={{0,12},{4,8},{8,4},{12,0},{16,28},{20,24},{24,20},{28,16},{1,13},{... | collective-permute-start | bytes 786440 | tf_op jit(solution)/shard_map/ppermute | solution.py:17
  61.0 20.5 %collective-permute-start.16 = (bf16[2,256,256]{2,1,0:T(8,128)(2,1)S(1)}, bf16[2,256,256]{2,1,0:T(8,128)(2,1)S(1)}, u32[]{:S(2)}, u32[]{:S(2)}) collective-permute-start(bf16[2,256,256]{2,1,0:T(8,128)(2,1)S(1)} %get-tuple-element.51.refs_12_.refs_22_), channel_id=1, source_target_pairs={{0,16},{4,20},{8,24},{12,28},{16,0},{20,4},{24,8},{28,12},{1,17},{... | collective-permute-start | bytes 786440 | tf_op jit(solution)/shard_map/ppermute | solution.py:17
  66.0 16.3 %collective-permute-start.24 = (bf16[1,256,256]{2,1,0:T(8,128)(2,1)S(1)}, bf16[1,256,256]{2,1,0:T(8,128)(2,1)S(1)}, u32[]{:S(2)}, u32[]{:S(2)}) collective-permute-start(bf16[1,256,256]{2,1,0:T(8,128)(2,1)S(1)} %get-tuple-element.58), channel_id=1, source_target_pairs={{0,4},{4,0},{8,12},{12,8},{16,20},{20,16},{24,28},{28,24},{1,5},{5... | collective-permute-start | bytes 393224 | tf_op jit(solution)/shard_map/ppermute | solution.py:17
  66.9 18.3 %collective-permute-start.25 = (bf16[1,256,256]{2,1,0:T(8,128)(2,1)S(1)}, bf16[1,256,256]{2,1,0:T(8,128)(2,1)S(1)}, u32[]{:S(2)}, u32[]{:S(2)}) collective-permute-start(bf16[1,256,256]{2,1,0:T(8,128)(2,1)S(1)} %get-tuple-element.59), channel_id=1, source_target_pairs={{0,8},{4,12},{8,0},{12,4},{16,24},{20,28},{24,16},{28,20},{1,9},{5... | collective-permute-start | bytes 393224 | tf_op jit(solution)/shard_map/ppermute | solution.py:17
  74.8 12.3 %collective-permute-start.26 = (bf16[1,256,256]{2,1,0:T(8,128)(2,1)S(1)}, bf16[1,256,256]{2,1,0:T(8,128)(2,1)S(1)}, u32[]{:S(2)}, u32[]{:S(2)}) collective-permute-start(bf16[1,256,256]{2,1,0:T(8,128)(2,1)S(1)} %get-tuple-element.60), channel_id=1, source_target_pairs={{0,12},{4,8},{8,4},{12,0},{16,28},{20,24},{24,20},{28,16},{1,13},{... | collective-permute-start | bytes 393224 | tf_op jit(solution)/shard_map/ppermute | solution.py:17
  81.6 7.5 %collective-permute-start.20 = (bf16[1,256,256]{2,1,0:T(8,128)(2,1)S(1)}, bf16[1,256,256]{2,1,0:T(8,128)(2,1)S(1)}, u32[]{:S(2)}, u32[]{:S(2)}) collective-permute-start(bf16[1,256,256]{2,1,0:T(8,128)(2,1)S(1)} %get-tuple-element.55), channel_id=1, source_target_pairs={{0,4},{4,0},{8,12},{12,8},{16,20},{20,16},{24,28},{28,24},{1,5},{5... | collective-permute-start | bytes 393224 | tf_op jit(solution)/shard_map/ppermute | solution.py:17
  82.3 6.9 %collective-permute-start.21 = (bf16[1,256,256]{2,1,0:T(8,128)(2,1)S(1)}, bf16[1,256,256]{2,1,0:T(8,128)(2,1)S(1)}, u32[]{:S(2)}, u32[]{:S(2)}) collective-permute-start(bf16[1,256,256]{2,1,0:T(8,128)(2,1)S(1)} %get-tuple-element.56), channel_id=1, source_target_pairs={{0,8},{4,12},{8,0},{12,4},{16,24},{20,28},{24,16},{28,20},{1,9},{5... | collective-permute-start | bytes 393224 | tf_op jit(solution)/shard_map/ppermute | solution.py:17
  82.3 8.0 %collective-permute-start.22 = (bf16[1,256,256]{2,1,0:T(8,128)(2,1)S(1)}, bf16[1,256,256]{2,1,0:T(8,128)(2,1)S(1)}, u32[]{:S(2)}, u32[]{:S(2)}) collective-permute-start(bf16[1,256,256]{2,1,0:T(8,128)(2,1)S(1)} %get-tuple-element.57), channel_id=1, source_target_pairs={{0,12},{4,8},{8,4},{12,0},{16,28},{20,24},{24,20},{28,16},{1,13},{... | collective-permute-start | bytes 393224 | tf_op jit(solution)/shard_map/ppermute | solution.py:17

commit v25 on v22

--- a/solution.py
+++ b/solution.py
@@ -7,7 +7,8 @@
 from jax.experimental.pallas import tpu as pltpu
 from jax.sharding import PartitionSpec as P
 
-CHUNKS = 2
+SHARES = (3, 1)
+LANES = 128
 VMEM = pl.BlockSpec(memory_space=pltpu.VMEM)
 ANY = pl.BlockSpec(memory_space=pl.ANY)
 BF16, F32 = jnp.bfloat16, jnp.float32
@@ -31,6 +32,15 @@
 def near_rows(values, held, axis, size):
     others = [hop(value, axis, size, 1) for value in values]
     return values + others, held + [[have ^ 1 for have in steps] for steps in held]
+
+
+def column_chunks(columns):
+    chunks, first, left = [], 0, sum(SHARES)
+    for share in SHARES:
+        wide = max((columns - first) * share // left // LANES, 1) * LANES
+        chunks.append((first, wide))
+        first, left = first + wide, left - share
+    return chunks
 
 
 def transposed_dot(left, right):
@@ -94,14 +104,14 @@
         send[0] = solved[entry_of(picks[0], myself ^ step, myself)]
 
 
-def relay_kernel(half, source, waits, through, picks, far, *refs):
+def relay_kernel(half, source, starts, waits, through, picks, far, *refs):
     sends = refs[waits + through:len(refs) - through]
     myself = lax.axis_index("leaf")
     for at, send in enumerate(sends):
         chunk, step = divmod(at, half - 1)
         wide = send.shape[-1]
         node = entry_of(picks[source], myself ^ (step + 1), myself ^ half)
-        send[0] = far[node, :, chunk * wide:(chunk + 1) * wide]
+        send[0] = far[node, :, starts[chunk]:starts[chunk] + wide]
 
 
 def inverse_kernel(held, levels, span, *refs):
@@ -115,7 +125,7 @@
 
 
 def level_kernel(
-    level, owners, held, width, chunk, places, stored, sides, mates,
+    level, owners, held, width, start, places, stored, sides, mates,
     picks, lists, counts, noise, inv, *refs,
 ):
     half = owners // 2
@@ -128,7 +138,7 @@
     myself, draw = lax.axis_index("leaf"), lax.axis_index("draw")
     levels, nodes = noise.shape[:2]
     wide = table.shape[-1]
-    columns = slice(chunk * wide, (chunk + 1) * wide)
+    columns = slice(start, start + wide)
     depth = inv.shape[1]
     rows = depth // sum(map(len, held))
     span = nodes * (width * depth + rows)
@@ -158,36 +168,37 @@
     entries = jnp.where(slots < live, entries ^ myself, empty)
     for node in range(nodes):
         total = None
-        for pack, start, step in found:
+        for pack, base, step in found:
             for slot in range(width):
                 entry = entry_of(entries, node, (draw ^ step) * width + slot)
-                at = start + offset + (node * width + slot) * depth
+                at = base + offset + (node * width + slot) * depth
                 term = transposed_dot(pack[at:at + depth, :], table[entry])
                 total = term if total is None else total + term
         right_side = (noise[level, node, :, columns].astype(F32) - total).astype(BF16)
         solved[node] = transposed_dot(inv[node], right_side).astype(BF16)
+        if done:
+            here = target.at[level, node, :, pl.ds(start, wide)]
+            copies.append(pltpu.make_async_copy(solved.at[node], here, sems.at[len(copies)]))
+            copies[-1].start()
     for step, send in enumerate(sends, 1):
         node = entry_of(picks[level], myself ^ step, myself)
-        for at, ref in enumerate([*chunks, solved]):
-            send[at] = ref[node]
-    if done:
-        here = target.at[level, :, :, pl.ds(chunk * wide, wide)]
-        copies.append(pltpu.make_async_copy(solved, here, sems.at[len(done)]))
-        copies[-1].start()
+        at = 0
+        for ref in (*chunks, solved):
+            send[0, :, at:at + ref.shape[-1]] = ref[node]
+            at += ref.shape[-1]
     for copy in copies:
         copy.wait()
 
 
 def on_device(owners, draws, noise, inverse, coupling, picks, lists, counts):
     levels, nodes, rows, columns = noise.shape
-    wide, half, chunks = columns // CHUNKS, owners // 2, range(CHUNKS)
+    half, chunks = owners // 2, column_chunks(columns)
     width = coupling.shape[2]
-    part = shape(nodes, rows, wide)
     flat = lambda value: value.reshape(-1, rows)
     leaf = lambda value, step: hop(value, "leaf", owners, step)
     near = lambda values: [leaf(value, step) for step, value in enumerate(values, 1)]
     inv_here = pltpu.VMEM((nodes, rows, rows), BF16)
-    dot_flops = 2 * rows * rows * wide
+    dot_flops = 2 * rows * rows * columns
 
     raw = jnp.concatenate([
         flat(value) for level in range(1, levels) for value in (coupling[level - 1], inverse[level])
@@ -199,19 +210,20 @@
         [shape(nodes, rows, columns)] + [shape(1, rows, columns)] * (half - 1) + [shape(*raw.shape)],
         [inv_here],
         (picks, noise[0], *values, raw),
-        flops=nodes * CHUNKS * dot_flops,
+        flops=nodes * dot_flops,
         aliases={2 + len(values): half},
     )
     far, got = leaf(solved, half), near(sends)
     values, steps = far_rows(raw, "draw", draws)
     sends = call(
-        functools.partial(relay_kernel, half, 0, len(got), len(values)),
-        [shape(1, rows, wide)] * (CHUNKS * (half - 1)) + [shape(*value.shape) for value in values],
+        functools.partial(relay_kernel, half, 0, [at for at, _ in chunks], len(got), len(values)),
+        [shape(1, rows, wide) for _, wide in chunks for _ in range(half - 1)]
+        + [shape(*value.shape) for value in values],
         [],
         (picks, far, *got, *values),
-        aliases={2 + len(got) + at: CHUNKS * (half - 1) + at for at in range(len(values))},
-    )
-    sends, values = take(sends, CHUNKS * (half - 1))
+        aliases={2 + len(got) + at: len(chunks) * (half - 1) + at for at in range(len(values))},
+    )
+    sends, values = take(sends, len(chunks) * (half - 1))
     packs, steps = near_rows(values, steps, "draw", draws)
     first, later = take(sends, half - 1)
     span = nodes * (width * rows + inverse.shape[2])
@@ -225,7 +237,7 @@
     later, inverses = take(outs, len(later))
     sends = first + later
     pieces, done = [[]], [(solved, (0, 0))]
-    for at in chunks:
+    for _ in chunks:
         distant, sends = take(sends, half - 1)
         pieces[0].append([
             (solved, 0), *((ref, 0) for ref in got),
@@ -235,47 +247,48 @@
     for level in range(1, levels):
         last_level = level == levels - 1
         solved, sends = [], []
-        for at in chunks:
-            ends = at == CHUNKS - 1 and not last_level
+        for at, (start, wide) in enumerate(chunks):
+            ends = at == len(chunks) - 1 and not last_level
             sides, mates = (half - 1, list(solved)) if ends else (0, [])
-            final = last_level and at == CHUNKS - 1
+            final = last_level and at == len(chunks) - 1
             known = [entry for below in range(level) for entry in pieces[below][at]]
             stored = done if final else []
             scratch = [pltpu.VMEM((level * owners + 1, rows, wide), BF16)]
             if final:
                 scratch += [
                     pltpu.VMEM((nodes, rows, wide), BF16),
-                    pltpu.SemaphoreType.DMA((len(stored) + 1,)),
+                    pltpu.SemaphoreType.DMA((len(stored) + nodes,)),
                 ]
             here, *sent = call(
                 functools.partial(
-                    level_kernel, level, owners, steps, width, at,
+                    level_kernel, level, owners, steps, width, start,
                     [place for _, place in known], [place for _, place in stored], sides, len(mates),
                 ),
-                [shape(*noise.shape) if final else part] + [shape(CHUNKS, rows, wide)] * sides,
+                [shape(*noise.shape) if final else shape(nodes, rows, wide)]
+                + [shape(1, rows, columns)] * sides,
                 scratch,
                 (picks, lists, counts, noise, inverses[level - 1], *packs, *(ref for ref, _ in known), *(ref for ref, _ in stored), *mates),
                 out_spec=ANY if final else VMEM,
-                flops=nodes * (draws * width + 1) * dot_flops,
+                flops=nodes * (draws * width + 1) * dot_flops * wide // columns,
             )
             solved.append(here)
-            done.append((here, (level, at * wide)))
+            done.append((here, (level, start)))
             sends += sent
         if last_level:
             return here
         far = [leaf(value, half) for value in solved]
         got = near(sends)
         pieces.append([])
-        for at in chunks:
-            waits = got if at == CHUNKS - 1 else []
+        for at, (_, wide) in enumerate(chunks):
+            waits = got if at == len(chunks) - 1 else []
             sends = call(
-                functools.partial(relay_kernel, half, level, len(waits), 0),
+                functools.partial(relay_kernel, half, level, [0], len(waits), 0),
                 [shape(1, rows, wide)] * (half - 1),
                 [],
                 (picks, far[at], *waits),
             )
             pieces[level].append([
-                (solved[at], 0), *((ref, at) for ref in got),
+                (solved[at], 0), *((ref, 0) for ref in got),
                 (far[at], 0), *((ref, 0) for ref in near(sends)),
             ])
 

time: 93.2 us -> 102 us (1.094)
  waiting for transfers between devices: 50.2 us -> 55.1 us
  starting transfers between devices: 30.8 us -> 34.9 us
    ppermute x27, waiting for transfers between devices: 50.2 us -> 55.1 us  [hop(): return lax.ppermute(value, axis, [(at, at ^ step) for at in range(size)])]
    ppermute x27, starting transfers between devices: 30.8 us -> 34.9 us  [hop(): return lax.ppermute(value, axis, [(at, at ^ step) for at in range(size)])]
  transfers between devices with their start and end apart: 27 -> 27, of which waited for: 14 -> 17; matrix products, arithmetic and copies ran while one was open for 1% -> 1% of each run, Pallas kernels for 7% -> 4%
where the time goes in v25:
time: 102 us; the launch traced here: 101 us
  waiting for transfers between devices  55.1 us (54%)
  starting transfers between devices  34.9 us (34%)
  Pallas kernels  9.05 us (9%)
  local copies, waits for them, and re-layouts  2.24 us (2%)
    ppermute x27, waiting for transfers between devices, hop(): return lax.ppermute(value, axis, [(at, at ^ step) for at in range(size)])  55.1 us
    ppermute x27, starting transfers between devices, hop(): return lax.ppermute(value, axis, [(at, at ^ step) for at in range(size)])  34.9 us
    pallas_call x9, Pallas kernels, call(): pl.pallas_call(kernel, out_shape=outs, in_specs=[VMEM] * len(arrays), out...  9.05 us
  transfers between devices with their start and end apart: 27, of which 17 were waited for; matrix products, arithmetic and copies ran while one was open for 1% of the time, Pallas kernels for 4%

profile of v25, /device:TPU:0, one launch (start us, length us, event | category | flops | bytes accessed | tf_op | source)
XLA Modules:
  0.0 101.5 jit_solution(3538650948464366060)
XLA Ops:
  1.4 2.6 %collective-permute-start = (bf16[128,256]{1,0:T(8,128)(2,1)S(1)}, bf16[128,256]{1,0:T(8,128)(2,1)S(1)}, u32[]{:S(2)}, u32[]{:S(2)}) collective-permute-start(bf16[128,256]{1,0:T(8,128)(2,1)S(1)} %bitcast.8), channel_id=1, source_target_pairs={{0,2},{1,3},{2,0},{3,1},{4,6},{5,7},{6,4},{7,5},{8,10},{9,11},{10,... | collective-permute-start | bytes 196616 | tf_op jit(solution)/shard_map/ppermute | solution.py:18
  4.0 1.3 %fusion = (bf16[1,2,2,256,256]{4,3,2,1,0:T(8,128)(2,1)S(1)}, bf16[1,2,2,256,256]{4,3,2,1,0:T(8,128)(2,1)S(1)}) fusion(bf16[2,2,2,256,256]{4,3,2,1,0:T(8,128)(2,1)} %param.8), kind=kLoop, calls=%fused_computation.2 | loop fusion | bytes 2097152 | tf_op jit(solution)/shard_map/slice | solution.py:204
  5.4 1.3 %collective-permute-done.refs_1_ = bf16[128,256]{1,0:T(8,128)(2,1)S(1)} collective-permute-done((bf16[128,256]{1,0:T(8,128)(2,1)S(1)}, bf16[128,256]{1,0:T(8,128)(2,1)S(1)}, u32[]{:S(2)}, u32[]{:S(2)}) %collective-permute-start) | collective-permute-done | bytes 65568 | tf_op jit(solution)/shard_map/ppermute | solution.py:18
  6.7 1.2 %collective-permute-done.2.refs_3_ = bf16[128,256]{1,0:T(8,128)(2,1)S(1)} collective-permute-done((bf16[128,256]{1,0:T(8,128)(2,1)S(1)}, bf16[128,256]{1,0:T(8,128)(2,1)S(1)}, u32[]{:S(2)}, u32[]{:S(2)}) %collective-permute-start.2) | collective-permute-done | bytes 65568 | tf_op jit(solution)/shard_map/ppermute | solution.py:18
  8.4 1.8 %collective-permute-start.7 = (bf16[2304,256]{1,0:T(8,128)(2,1)S(1)}, bf16[2304,256]{1,0:T(8,128)(2,1)S(1)}, u32[]{:S(2)}, u32[]{:S(2)}) collective-permute-start(bf16[2304,256]{1,0:T(8,128)(2,1)S(1)} %get-tuple-element.37.refs_3_), channel_id=1, source_target_pairs={{0,2},{1,3},{2,0},{3,1},{4,6},{5,7},{6,4},{7,5},{8,10},{9,11},{10,... | collective-permute-start | bytes 3538952 | tf_op jit(solution)/shard_map/ppermute | solution.py:18
  10.2 2.6 %collective-permute-start.3 = (bf16[2,256,512]{2,1,0:T(8,128)(2,1)S(1)}, bf16[2,256,512]{2,1,0:T(8,128)(2,1)S(1)}, u32[]{:S(2)}, u32[]{:S(2)}) collective-permute-start(bf16[2,256,512]{2,1,0:T(8,128)(2,1)S(1)} %get-tuple-element.33.refs_4_.refs_20_), channel_id=1, source_target_pairs={{0,16},{4,20},{8,24},{12,28},{16,0},{20,4},{24,8},{28,12},{1,17},{... | collective-permute-start | bytes 1572872 | tf_op jit(solution)/shard_map/ppermute | solution.py:18
  12.8 1.5 %collective-permute-start.4 = (bf16[1,256,512]{2,1,0:T(8,128)(2,1)S(1)}, bf16[1,256,512]{2,1,0:T(8,128)(2,1)S(1)}, u32[]{:S(2)}, u32[]{:S(2)}) collective-permute-start(bf16[1,256,512]{2,1,0:T(8,128)(2,1)S(1)} %get-tuple-element.34), channel_id=1, source_target_pairs={{0,4},{4,0},{8,12},{12,8},{16,20},{20,16},{24,28},{28,24},{1,5},{5... | collective-permute-start | bytes 786440 | tf_op jit(solution)/shard_map/ppermute | solution.py:18
  14.3 1.6 %collective-permute-start.5 = (bf16[1,256,512]{2,1,0:T(8,128)(2,1)S(1)}, bf16[1,256,512]{2,1,0:T(8,128)(2,1)S(1)}, u32[]{:S(2)}, u32[]{:S(2)}) collective-permute-start(bf16[1,256,512]{2,1,0:T(8,128)(2,1)S(1)} %get-tuple-element.35), channel_id=1, source_target_pairs={{0,8},{4,12},{8,0},{12,4},{16,24},{20,28},{24,16},{28,20},{1,9},{5... | collective-permute-start | bytes 786440 | tf_op jit(solution)/shard_map/ppermute | solution.py:18
  16.3 4.9 %collective-permute-done.4.refs_0_.refs_5_ = bf16[1,256,512]{2,1,0:T(8,128)(2,1)S(1)} collective-permute-done((bf16[1,256,512]{2,1,0:T(8,128)(2,1)S(1)}, bf16[1,256,512]{2,1,0:T(8,128)(2,1)S(1)}, u32[]{:S(2)}, u32[]{:S(2)}) %collective-permute-start.4) | collective-permute-done | bytes 262176 | tf_op jit(solution)/shard_map/ppermute | solution.py:18
  21.1 9.6 %collective-permute-done.5.refs_1_.refs_6_ = bf16[1,256,512]{2,1,0:T(8,128)(2,1)S(1)} collective-permute-done((bf16[1,256,512]{2,1,0:T(8,128)(2,1)S(1)}, bf16[1,256,512]{2,1,0:T(8,128)(2,1)S(1)}, u32[]{:S(2)}, u32[]{:S(2)}) %collective-permute-start.5) | collective-permute-done | bytes 262176 | tf_op jit(solution)/shard_map/ppermute | solution.py:18
  30.8 6.7 %collective-permute-done.6.refs_2_.refs_7_ = bf16[1,256,512]{2,1,0:T(8,128)(2,1)S(1)} collective-permute-done((bf16[1,256,512]{2,1,0:T(8,128)(2,1)S(1)}, bf16[1,256,512]{2,1,0:T(8,128)(2,1)S(1)}, u32[]{:S(2)}, u32[]{:S(2)}) %collective-permute-start.6) | collective-permute-done | bytes 262176 | tf_op jit(solution)/shard_map/ppermute | solution.py:18
  38.3 1.5 %collective-permute-start.13 = (bf16[1,256,384]{2,1,0:T(8,128)(2,1)S(1)}, bf16[1,256,384]{2,1,0:T(8,128)(2,1)S(1)}, u32[]{:S(2)}, u32[]{:S(2)}) collective-permute-start(bf16[1,256,384]{2,1,0:T(8,128)(2,1)S(1)} %get-tuple-element.48), channel_id=1, source_target_pairs={{0,4},{4,0},{8,12},{12,8},{16,20},{20,16},{24,28},{28,24},{1,5},{5... | collective-permute-start | bytes 589832 | tf_op jit(solution)/shard_map/ppermute | solution.py:18
  42.4 2.8 %collective-permute-done.13.refs_9_ = bf16[1,256,384]{2,1,0:T(8,128)(2,1)S(1)} collective-permute-done((bf16[1,256,384]{2,1,0:T(8,128)(2,1)S(1)}, bf16[1,256,384]{2,1,0:T(8,128)(2,1)S(1)}, u32[]{:S(2)}, u32[]{:S(2)}) %collective-permute-start.13) | collective-permute-done | bytes 196640 | tf_op jit(solution)/shard_map/ppermute | solution.py:18
  45.2 2.4 %collective-permute-done.14.refs_10_ = bf16[1,256,384]{2,1,0:T(8,128)(2,1)S(1)} collective-permute-done((bf16[1,256,384]{2,1,0:T(8,128)(2,1)S(1)}, bf16[1,256,384]{2,1,0:T(8,128)(2,1)S(1)}, u32[]{:S(2)}, u32[]{:S(2)}) %collective-permute-start.14) | collective-permute-done | bytes 196640 | tf_op jit(solution)/shard_map/ppermute | solution.py:18
  47.6 3.0 %collective-permute-done.15.refs_11_ = bf16[1,256,384]{2,1,0:T(8,128)(2,1)S(1)} collective-permute-done((bf16[1,256,384]{2,1,0:T(8,128)(2,1)S(1)}, bf16[1,256,384]{2,1,0:T(8,128)(2,1)S(1)}, u32[]{:S(2)}, u32[]{:S(2)}) %collective-permute-start.15) | collective-permute-done | bytes 196640 | tf_op jit(solution)/shard_map/ppermute | solution.py:18
  50.6 2.1 %shard_map.67.refs_12_.refs_21_ = bf16[2,256,384]{2,1,0:T(8,128)(2,1)S(1)} custom-call(s32[2,8,8]{2,1,0:T(8,128)S(1)} %copy-done.1, s32[2,2,8]{2,1,0:T(2,128)S(1)} %copy-done.2, s32[2,2]{1,0:T(2,128)S(1)} %copy-done.3, bf16[3,2,256,512]{3,2,1,0:T(8,128)(2,1)S(1)} %copy-done, bf16[2,256,256]{2,1,0:T(8,128)(2,1)S(1)} %get-tuple-element.47.inv, ...), custom_call_target="tpu_custom_call" | custom-call | flops 905969664 | bytes 9372304 | tf_op jit(solution)/shard_map/pallas_call | solution.py:66
  52.7 1.9 %collective-permute-start.23 = (bf16[2,256,384]{2,1,0:T(8,128)(2,1)S(1)}, bf16[2,256,384]{2,1,0:T(8,128)(2,1)S(1)}, u32[]{:S(2)}, u32[]{:S(2)}) collective-permute-start(bf16[2,256,384]{2,1,0:T(8,128)(2,1)S(1)} %shard_map.67.refs_12_.refs_21_), channel_id=1, source_target_pairs={{0,16},{4,20},{8,24},{12,28},{16,0},{20,4},{24,8},{28,12},{1,17},{... | collective-permute-start | bytes 1179656 | tf_op jit(solution)/shard_map/ppermute | solution.py:18
  54.5 1.5 %collective-permute-start.10 = (bf16[1,256,128]{2,1,0:T(8,128)(2,1)S(1)}, bf16[1,256,128]{2,1,0:T(8,128)(2,1)S(1)}, u32[]{:S(2)}, u32[]{:S(2)}) collective-permute-start(bf16[1,256,128]{2,1,0:T(8,128)(2,1)S(1)} %get-tuple-element.44), channel_id=1, source_target_pairs={{0,4},{4,0},{8,12},{12,8},{16,20},{20,16},{24,28},{28,24},{1,5},{5... | collective-permute-start | bytes 196616 | tf_op jit(solution)/shard_map/ppermute | solution.py:18
  56.1 1.6 %collective-permute-start.11 = (bf16[1,256,128]{2,1,0:T(8,128)(2,1)S(1)}, bf16[1,256,128]{2,1,0:T(8,128)(2,1)S(1)}, u32[]{:S(2)}, u32[]{:S(2)}) collective-permute-start(bf16[1,256,128]{2,1,0:T(8,128)(2,1)S(1)} %get-tuple-element.45), channel_id=1, source_target_pairs={{0,8},{4,12},{8,0},{12,4},{16,24},{20,28},{24,16},{28,20},{1,9},{5... | collective-permute-start | bytes 196616 | tf_op jit(solution)/shard_map/ppermute | solution.py:18
  58.8 5.3 %collective-permute-done.11.refs_10_ = bf16[1,256,128]{2,1,0:T(8,128)(2,1)S(1)} collective-permute-done((bf16[1,256,128]{2,1,0:T(8,128)(2,1)S(1)}, bf16[1,256,128]{2,1,0:T(8,128)(2,1)S(1)}, u32[]{:S(2)}, u32[]{:S(2)}) %collective-permute-start.11) | collective-permute-done | bytes 65568 | tf_op jit(solution)/shard_map/ppermute | solution.py:18
  64.8 1.4 %shard_map.68 = (bf16[2,256,128]{2,1,0:T(8,128)(2,1)S(1)}, bf16[1,256,512]{2,1,0:T(8,128)(2,1)S(1)}, bf16[1,256,512]{2,1,0:T(8,128)(2,1)S(1)}, bf16[1,256,512]{2,1,0:T(8,128)(2,1)S(1)}) custom-call(s32[2,8,8]{2,1,0:T(8,128)S(1)} %copy-done.1, s32[2,2,8]{2,1,0:T(2,128)S(1)} %copy-done.2, s32[2,2]{1,0:T(2,128)S(1)} %copy-done.3, ...), custom_call_target="tpu_custom_call" | custom-call | flops 301989888 | bytes 9896592 | tf_op jit(solution)/shard_map/pallas_call | solution.py:66
  66.3 1.6 %collective-permute-start.16 = (bf16[1,256,512]{2,1,0:T(8,128)(2,1)S(1)}, bf16[1,256,512]{2,1,0:T(8,128)(2,1)S(1)}, u32[]{:S(2)}, u32[]{:S(2)}) collective-permute-start(bf16[1,256,512]{2,1,0:T(8,128)(2,1)S(1)} %get-tuple-element.52), channel_id=1, source_target_pairs={{0,4},{4,0},{8,12},{12,8},{16,20},{20,16},{24,28},{28,24},{1,5},{5... | collective-permute-start | bytes 786440 | tf_op jit(solution)/shard_map/ppermute | solution.py:18
  67.8 2.7 %collective-permute-start.19 = (bf16[2,256,128]{2,1,0:T(8,128)(2,1)S(1)}, bf16[2,256,128]{2,1,0:T(8,128)(2,1)S(1)}, u32[]{:S(2)}, u32[]{:S(2)}) collective-permute-start(bf16[2,256,128]{2,1,0:T(8,128)(2,1)S(1)} %get-tuple-element.51.refs_12_.refs_22_), channel_id=1, source_target_pairs={{0,16},{4,20},{8,24},{12,28},{16,0},{20,4},{24,8},{28,12},{1,17},{... | collective-permute-start | bytes 393224 | tf_op jit(solution)/shard_map/ppermute | solution.py:18
  70.6 2.6 %collective-permute-start.18 = (bf16[1,256,512]{2,1,0:T(8,128)(2,1)S(1)}, bf16[1,256,512]{2,1,0:T(8,128)(2,1)S(1)}, u32[]{:S(2)}, u32[]{:S(2)}) collective-permute-start(bf16[1,256,512]{2,1,0:T(8,128)(2,1)S(1)} %get-tuple-element.54), channel_id=1, source_target_pairs={{0,12},{4,8},{8,4},{12,0},{16,28},{20,24},{24,20},{28,16},{1,13},{... | collective-permute-start | bytes 786440 | tf_op jit(solution)/shard_map/ppermute | solution.py:18
  75.6 2.1 %collective-permute-done.19.far.refs_16_ = bf16[2,256,128]{2,1,0:T(8,128)(2,1)S(1)} collective-permute-done((bf16[2,256,128]{2,1,0:T(8,128)(2,1)S(1)}, bf16[2,256,128]{2,1,0:T(8,128)(2,1)S(1)}, u32[]{:S(2)}, u32[]{:S(2)}) %collective-permute-start.19) | collective-permute-done | bytes 131104 | tf_op jit(solution)/shard_map/ppermute | solution.py:18
  77.7 3.0 %collective-permute-start.26 = (bf16[1,256,384]{2,1,0:T(8,128)(2,1)S(1)}, bf16[1,256,384]{2,1,0:T(8,128)(2,1)S(1)}, u32[]{:S(2)}, u32[]{:S(2)}) collective-permute-start(bf16[1,256,384]{2,1,0:T(8,128)(2,1)S(1)} %get-tuple-element.60), channel_id=1, source_target_pairs={{0,12},{4,8},{8,4},{12,0},{16,28},{20,24},{24,20},{28,16},{1,13},{... | collective-permute-start | bytes 589832 | tf_op jit(solution)/shard_map/ppermute | solution.py:18
  80.7 1.3 %collective-permute-done.17.refs_1_.refs_14_ = bf16[1,256,512]{2,1,0:T(8,128)(2,1)S(1)} collective-permute-done((bf16[1,256,512]{2,1,0:T(8,128)(2,1)S(1)}, bf16[1,256,512]{2,1,0:T(8,128)(2,1)S(1)}, u32[]{:S(2)}, u32[]{:S(2)}) %collective-permute-start.17) | collective-permute-done | bytes 262176 | tf_op jit(solution)/shard_map/ppermute | solution.py:18
  82.0 6.6 %collective-permute-done.18.refs_2_.refs_15_ = bf16[1,256,512]{2,1,0:T(8,128)(2,1)S(1)} collective-permute-done((bf16[1,256,512]{2,1,0:T(8,128)(2,1)S(1)}, bf16[1,256,512]{2,1,0:T(8,128)(2,1)S(1)}, u32[]{:S(2)}, u32[]{:S(2)}) %collective-permute-start.18) | collective-permute-done | bytes 262176 | tf_op jit(solution)/shard_map/ppermute | solution.py:18
  90.0 2.2 %collective-permute-start.22 = (bf16[1,256,128]{2,1,0:T(8,128)(2,1)S(1)}, bf16[1,256,128]{2,1,0:T(8,128)(2,1)S(1)}, u32[]{:S(2)}, u32[]{:S(2)}) collective-permute-start(bf16[1,256,128]{2,1,0:T(8,128)(2,1)S(1)} %get-tuple-element.57), channel_id=1, source_target_pairs={{0,12},{4,8},{8,4},{12,0},{16,28},{20,24},{24,20},{28,16},{1,13},{... | collective-permute-start | bytes 196616 | tf_op jit(solution)/shard_map/ppermute | solution.py:18
  92.3 4.6 %collective-permute-done.26.refs_19_ = bf16[1,256,384]{2,1,0:T(8,128)(2,1)S(1)} collective-permute-done((bf16[1,256,384]{2,1,0:T(8,128)(2,1)S(1)}, bf16[1,256,384]{2,1,0:T(8,128)(2,1)S(1)}, u32[]{:S(2)}, u32[]{:S(2)}) %collective-permute-start.26) | collective-permute-done | bytes 196640 | tf_op jit(solution)/shard_map/ppermute | solution.py:18
  96.9 2.2 %shard_map.71.refs_23_ = bf16[2,256,384]{2,1,0:T(8,128)(2,1)S(1)} custom-call(s32[2,8,8]{2,1,0:T(8,128)S(1)} %copy-done.1, s32[2,2,8]{2,1,0:T(2,128)S(1)} %copy-done.2, s32[2,2]{1,0:T(2,128)S(1)} %copy-done.3, bf16[3,2,256,512]{3,2,1,0:T(8,128)(2,1)S(1)} %copy-done, bf16[2,256,256]{2,1,0:T(8,128)(2,1)S(1)} %get-tuple-element.43.inv, ...), custom_call_target="tpu_custom_call" | custom-call | flops 905969664 | bytes 11534992 | tf_op jit(solution)/shard_map/pallas_call | solution.py:66
  99.1 2.4 %shard_map.72 = bf16[3,2,256,512]{3,2,1,0:T(8,128)(2,1)} custom-call(s32[2,8,8]{2,1,0:T(8,128)S(1)} %copy-done.1, s32[2,2,8]{2,1,0:T(2,128)S(1)} %copy-done.2, s32[2,2]{1,0:T(2,128)S(1)} %copy-done.3, bf16[3,2,256,512]{3,2,1,0:T(8,128)(2,1)S(1)} %copy-done, bf16[2,256,256]{2,1,0:T(8,128)(2,1)S(1)} %get-tuple-element.43.inv, ...), custom_call_target="tpu_custom_call" | custom-call | flops 301989888 | bytes 12845712 | tf_op jit(solution)/shard_map/pallas_call | solution.py:66
  (43 shorter events, 11.5 us)
Async XLA Ops:
  0.9 5.8 %collective-permute-start.1 = (bf16[128,256]{1,0:T(8,128)(2,1)S(1)}, bf16[128,256]{1,0:T(8,128)(2,1)S(1)}, u32[]{:S(2)}, u32[]{:S(2)}) collective-permute-start(bf16[128,256]{1,0:T(8,128)(2,1)S(1)} %bitcast.7), channel_id=1, source_target_pairs={{0,1},{1,0},{2,3},{3,2},{4,5},{5,4},{6,7},{7,6},{8,9},{9,8},{10,11... | collective-permute-start | bytes 196616 | tf_op jit(solution)/shard_map/ppermute | solution.py:18
  1.4 5.3 %collective-permute-start = (bf16[128,256]{1,0:T(8,128)(2,1)S(1)}, bf16[128,256]{1,0:T(8,128)(2,1)S(1)}, u32[]{:S(2)}, u32[]{:S(2)}) collective-permute-start(bf16[128,256]{1,0:T(8,128)(2,1)S(1)} %bitcast.8), channel_id=1, source_target_pairs={{0,2},{1,3},{2,0},{3,1},{4,6},{5,7},{6,4},{7,5},{8,10},{9,11},{10,... | collective-permute-start | bytes 196616 | tf_op jit(solution)/shard_map/ppermute | solution.py:18
  5.3 1.4 %copy-start = (bf16[3,2,256,512]{3,2,1,0:T(8,128)(2,1)S(1)}, bf16[3,2,256,512]{3,2,1,0:T(8,128)(2,1)}, u32[]{:S(2)}) copy-start(bf16[3,2,256,512]{3,2,1,0:T(8,128)(2,1)} %noise.7) | copy-start | bytes 4718596
  5.3 2.7 %copy-start.1 = (s32[2,8,8]{2,1,0:T(8,128)S(1)}, s32[2,8,8]{2,1,0:T(8,128)}, u32[]{:S(2)}) copy-start(s32[2,8,8]{2,1,0:T(8,128)} %picks.15) | copy-start | bytes 1540
  6.7 1.3 %collective-permute-start.2 = (bf16[128,256]{1,0:T(8,128)(2,1)S(1)}, bf16[128,256]{1,0:T(8,128)(2,1)S(1)}, u32[]{:S(2)}, u32[]{:S(2)}) collective-permute-start(bf16[128,256]{1,0:T(8,128)(2,1)S(1)} %collective-permute-done.refs_1_), channel_id=1, source_target_pairs={{0,1},{1,0},{2,3},{3,2},{4,5},{5,4},{6,7},{7,6},{8,9},{9,8},{10,11... | collective-permute-start | bytes 196616 | tf_op jit(solution)/shard_map/ppermute | solution.py:18
  8.4 29.1 %collective-permute-start.7 = (bf16[2304,256]{1,0:T(8,128)(2,1)S(1)}, bf16[2304,256]{1,0:T(8,128)(2,1)S(1)}, u32[]{:S(2)}, u32[]{:S(2)}) collective-permute-start(bf16[2304,256]{1,0:T(8,128)(2,1)S(1)} %get-tuple-element.37.refs_3_), channel_id=1, source_target_pairs={{0,2},{1,3},{2,0},{3,1},{4,6},{5,7},{6,4},{7,5},{8,10},{9,11},{10,... | collective-permute-start | bytes 3538952 | tf_op jit(solution)/shard_map/ppermute | solution.py:18
  10.2 27.3 %collective-permute-start.3 = (bf16[2,256,512]{2,1,0:T(8,128)(2,1)S(1)}, bf16[2,256,512]{2,1,0:T(8,128)(2,1)S(1)}, u32[]{:S(2)}, u32[]{:S(2)}) collective-permute-start(bf16[2,256,512]{2,1,0:T(8,128)(2,1)S(1)} %get-tuple-element.33.refs_4_.refs_20_), channel_id=1, source_target_pairs={{0,16},{4,20},{8,24},{12,28},{16,0},{20,4},{24,8},{28,12},{1,17},{... | collective-permute-start | bytes 1572872 | tf_op jit(solution)/shard_map/ppermute | solution.py:18
  12.8 8.3 %collective-permute-start.4 = (bf16[1,256,512]{2,1,0:T(8,128)(2,1)S(1)}, bf16[1,256,512]{2,1,0:T(8,128)(2,1)S(1)}, u32[]{:S(2)}, u32[]{:S(2)}) collective-permute-start(bf16[1,256,512]{2,1,0:T(8,128)(2,1)S(1)} %get-tuple-element.34), channel_id=1, source_target_pairs={{0,4},{4,0},{8,12},{12,8},{16,20},{20,16},{24,28},{28,24},{1,5},{5... | collective-permute-start | bytes 786440 | tf_op jit(solution)/shard_map/ppermute | solution.py:18
  14.3 16.5 %collective-permute-start.5 = (bf16[1,256,512]{2,1,0:T(8,128)(2,1)S(1)}, bf16[1,256,512]{2,1,0:T(8,128)(2,1)S(1)}, u32[]{:S(2)}, u32[]{:S(2)}) collective-permute-start(bf16[1,256,512]{2,1,0:T(8,128)(2,1)S(1)} %get-tuple-element.35), channel_id=1, source_target_pairs={{0,8},{4,12},{8,0},{12,4},{16,24},{20,28},{24,16},{28,20},{1,9},{5... | collective-permute-start | bytes 786440 | tf_op jit(solution)/shard_map/ppermute | solution.py:18
  15.9 21.6 %collective-permute-start.6 = (bf16[1,256,512]{2,1,0:T(8,128)(2,1)S(1)}, bf16[1,256,512]{2,1,0:T(8,128)(2,1)S(1)}, u32[]{:S(2)}, u32[]{:S(2)}) collective-permute-start(bf16[1,256,512]{2,1,0:T(8,128)(2,1)S(1)} %get-tuple-element.36), channel_id=1, source_target_pairs={{0,12},{4,8},{8,4},{12,0},{16,28},{20,24},{24,20},{28,16},{1,13},{... | collective-permute-start | bytes 786440 | tf_op jit(solution)/shard_map/ppermute | solution.py:18
  37.7 4.1 %collective-permute-start.8 = (bf16[2304,256]{1,0:T(8,128)(2,1)S(1)}, bf16[2304,256]{1,0:T(8,128)(2,1)S(1)}, u32[]{:S(2)}, u32[]{:S(2)}) collective-permute-start(bf16[2304,256]{1,0:T(8,128)(2,1)S(1)} %get-tuple-element.38.refs_0_), channel_id=1, source_target_pairs={{0,1},{1,0},{2,3},{3,2},{4,5},{5,4},{6,7},{7,6},{8,9},{9,8},{10,11... | collective-permute-start | bytes 3538952 | tf_op jit(solution)/shard_map/ppermute | solution.py:18
  37.8 4.5 %collective-permute-start.9 = (bf16[2304,256]{1,0:T(8,128)(2,1)S(1)}, bf16[2304,256]{1,0:T(8,128)(2,1)S(1)}, u32[]{:S(2)}, u32[]{:S(2)}) collective-permute-start(bf16[2304,256]{1,0:T(8,128)(2,1)S(1)} %get-tuple-element.39.refs_1_), channel_id=1, source_target_pairs={{0,1},{1,0},{2,3},{3,2},{4,5},{5,4},{6,7},{7,6},{8,9},{9,8},{10,11... | collective-permute-start | bytes 3538952 | tf_op jit(solution)/shard_map/ppermute | solution.py:18
  38.3 6.9 %collective-permute-start.13 = (bf16[1,256,384]{2,1,0:T(8,128)(2,1)S(1)}, bf16[1,256,384]{2,1,0:T(8,128)(2,1)S(1)}, u32[]{:S(2)}, u32[]{:S(2)}) collective-permute-start(bf16[1,256,384]{2,1,0:T(8,128)(2,1)S(1)} %get-tuple-element.48), channel_id=1, source_target_pairs={{0,4},{4,0},{8,12},{12,8},{16,20},{20,16},{24,28},{28,24},{1,5},{5... | collective-permute-start | bytes 589832 | tf_op jit(solution)/shard_map/ppermute | solution.py:18
  39.8 7.8 %collective-permute-start.14 = (bf16[1,256,384]{2,1,0:T(8,128)(2,1)S(1)}, bf16[1,256,384]{2,1,0:T(8,128)(2,1)S(1)}, u32[]{:S(2)}, u32[]{:S(2)}) collective-permute-start(bf16[1,256,384]{2,1,0:T(8,128)(2,1)S(1)} %get-tuple-element.49), channel_id=1, source_target_pairs={{0,8},{4,12},{8,0},{12,4},{16,24},{20,28},{24,16},{28,20},{1,9},{5... | collective-permute-start | bytes 589832 | tf_op jit(solution)/shard_map/ppermute | solution.py:18
  40.6 10.0 %collective-permute-start.15 = (bf16[1,256,384]{2,1,0:T(8,128)(2,1)S(1)}, bf16[1,256,384]{2,1,0:T(8,128)(2,1)S(1)}, u32[]{:S(2)}, u32[]{:S(2)}) collective-permute-start(bf16[1,256,384]{2,1,0:T(8,128)(2,1)S(1)} %get-tuple-element.50), channel_id=1, source_target_pairs={{0,12},{4,8},{8,4},{12,0},{16,28},{20,24},{24,20},{28,16},{1,13},{... | collective-permute-start | bytes 589832 | tf_op jit(solution)/shard_map/ppermute | solution.py:18
  42.3 8.3 %copy-start.2 = (s32[2,2,8]{2,1,0:T(2,128)S(1)}, s32[2,2,8]{2,1,0:T(2,128)}, u32[]{:S(2)}) copy-start(s32[2,2,8]{2,1,0:T(2,128)} %lists.7) | copy-start | bytes 388
  42.3 8.3 %copy-start.3 = (s32[2,2]{1,0:T(2,128)S(1)}, s32[2,2]{1,0:T(2,128)}, u32[]{:S(2)}) copy-start(s32[2,2]{1,0:T(2,128)} %counts.7) | copy-start | bytes 52
  52.7 21.6 %collective-permute-start.23 = (bf16[2,256,384]{2,1,0:T(8,128)(2,1)S(1)}, bf16[2,256,384]{2,1,0:T(8,128)(2,1)S(1)}, u32[]{:S(2)}, u32[]{:S(2)}) collective-permute-start(bf16[2,256,384]{2,1,0:T(8,128)(2,1)S(1)} %shard_map.67.refs_12_.refs_21_), channel_id=1, source_target_pairs={{0,16},{4,20},{8,24},{12,28},{16,0},{20,4},{24,8},{28,12},{1,17},{... | collective-permute-start | bytes 1179656 | tf_op jit(solution)/shard_map/ppermute | solution.py:18
  54.5 4.3 %collective-permute-start.10 = (bf16[1,256,128]{2,1,0:T(8,128)(2,1)S(1)}, bf16[1,256,128]{2,1,0:T(8,128)(2,1)S(1)}, u32[]{:S(2)}, u32[]{:S(2)}) collective-permute-start(bf16[1,256,128]{2,1,0:T(8,128)(2,1)S(1)} %get-tuple-element.44), channel_id=1, source_target_pairs={{0,4},{4,0},{8,12},{12,8},{16,20},{20,16},{24,28},{28,24},{1,5},{5... | collective-permute-start | bytes 196616 | tf_op jit(solution)/shard_map/ppermute | solution.py:18
  56.1 8.1 %collective-permute-start.11 = (bf16[1,256,128]{2,1,0:T(8,128)(2,1)S(1)}, bf16[1,256,128]{2,1,0:T(8,128)(2,1)S(1)}, u32[]{:S(2)}, u32[]{:S(2)}) collective-permute-start(bf16[1,256,128]{2,1,0:T(8,128)(2,1)S(1)} %get-tuple-element.45), channel_id=1, source_target_pairs={{0,8},{4,12},{8,0},{12,4},{16,24},{20,28},{24,16},{28,20},{1,9},{5... | collective-permute-start | bytes 196616 | tf_op jit(solution)/shard_map/ppermute | solution.py:18
  57.6 7.2 %collective-permute-start.12 = (bf16[1,256,128]{2,1,0:T(8,128)(2,1)S(1)}, bf16[1,256,128]{2,1,0:T(8,128)(2,1)S(1)}, u32[]{:S(2)}, u32[]{:S(2)}) collective-permute-start(bf16[1,256,128]{2,1,0:T(8,128)(2,1)S(1)} %get-tuple-element.46), channel_id=1, source_target_pairs={{0,12},{4,8},{8,4},{12,0},{16,28},{20,24},{24,20},{28,16},{1,13},{... | collective-permute-start | bytes 196616 | tf_op jit(solution)/shard_map/ppermute | solution.py:18
  66.3 11.5 %collective-permute-start.16 = (bf16[1,256,512]{2,1,0:T(8,128)(2,1)S(1)}, bf16[1,256,512]{2,1,0:T(8,128)(2,1)S(1)}, u32[]{:S(2)}, u32[]{:S(2)}) collective-permute-start(bf16[1,256,512]{2,1,0:T(8,128)(2,1)S(1)} %get-tuple-element.52), channel_id=1, source_target_pairs={{0,4},{4,0},{8,12},{12,8},{16,20},{20,16},{24,28},{28,24},{1,5},{5... | collective-permute-start | bytes 786440 | tf_op jit(solution)/shard_map/ppermute | solution.py:18
  67.8 9.9 %collective-permute-start.19 = (bf16[2,256,128]{2,1,0:T(8,128)(2,1)S(1)}, bf16[2,256,128]{2,1,0:T(8,128)(2,1)S(1)}, u32[]{:S(2)}, u32[]{:S(2)}) collective-permute-start(bf16[2,256,128]{2,1,0:T(8,128)(2,1)S(1)} %get-tuple-element.51.refs_12_.refs_22_), channel_id=1, source_target_pairs={{0,16},{4,20},{8,24},{12,28},{16,0},{20,4},{24,8},{28,12},{1,17},{... | collective-permute-start | bytes 393224 | tf_op jit(solution)/shard_map/ppermute | solution.py:18
  70.6 11.4 %collective-permute-start.17 = (bf16[1,256,512]{2,1,0:T(8,128)(2,1)S(1)}, bf16[1,256,512]{2,1,0:T(8,128)(2,1)S(1)}, u32[]{:S(2)}, u32[]{:S(2)}) collective-permute-start(bf16[1,256,512]{2,1,0:T(8,128)(2,1)S(1)} %get-tuple-element.53), channel_id=1, source_target_pairs={{0,8},{4,12},{8,0},{12,4},{16,24},{20,28},{24,16},{28,20},{1,9},{5... | collective-permute-start | bytes 786440 | tf_op jit(solution)/shard_map/ppermute | solution.py:18
  70.6 18.0 %collective-permute-start.18 = (bf16[1,256,512]{2,1,0:T(8,128)(2,1)S(1)}, bf16[1,256,512]{2,1,0:T(8,128)(2,1)S(1)}, u32[]{:S(2)}, u32[]{:S(2)}) collective-permute-start(bf16[1,256,512]{2,1,0:T(8,128)(2,1)S(1)} %get-tuple-element.54), channel_id=1, source_target_pairs={{0,12},{4,8},{8,4},{12,0},{16,28},{20,24},{24,20},{28,16},{1,13},{... | collective-permute-start | bytes 786440 | tf_op jit(solution)/shard_map/ppermute | solution.py:18
  74.5 15.5 %collective-permute-start.24 = (bf16[1,256,384]{2,1,0:T(8,128)(2,1)S(1)}, bf16[1,256,384]{2,1,0:T(8,128)(2,1)S(1)}, u32[]{:S(2)}, u32[]{:S(2)}) collective-permute-start(bf16[1,256,384]{2,1,0:T(8,128)(2,1)S(1)} %get-tuple-element.58), channel_id=1, source_target_pairs={{0,4},{4,0},{8,12},{12,8},{16,20},{20,16},{24,28},{28,24},{1,5},{5... | collective-permute-start | bytes 589832 | tf_op jit(solution)/shard_map/ppermute | solution.py:18
  77.7 14.5 %collective-permute-start.25 = (bf16[1,256,384]{2,1,0:T(8,128)(2,1)S(1)}, bf16[1,256,384]{2,1,0:T(8,128)(2,1)S(1)}, u32[]{:S(2)}, u32[]{:S(2)}) collective-permute-start(bf16[1,256,384]{2,1,0:T(8,128)(2,1)S(1)} %get-tuple-element.59), channel_id=1, source_target_pairs={{0,8},{4,12},{8,0},{12,4},{16,24},{20,28},{24,16},{28,20},{1,9},{5... | collective-permute-start | bytes 589832 | tf_op jit(solution)/shard_map/ppermute | solution.py:18
  77.7 19.1 %collective-permute-start.26 = (bf16[1,256,384]{2,1,0:T(8,128)(2,1)S(1)}, bf16[1,256,384]{2,1,0:T(8,128)(2,1)S(1)}, u32[]{:S(2)}, u32[]{:S(2)}) collective-permute-start(bf16[1,256,384]{2,1,0:T(8,128)(2,1)S(1)} %get-tuple-element.60), channel_id=1, source_target_pairs={{0,12},{4,8},{8,4},{12,0},{16,28},{20,24},{24,20},{28,16},{1,13},{... | collective-permute-start | bytes 589832 | tf_op jit(solution)/shard_map/ppermute | solution.py:18
  88.7 10.4 %collective-permute-start.20 = (bf16[1,256,128]{2,1,0:T(8,128)(2,1)S(1)}, bf16[1,256,128]{2,1,0:T(8,128)(2,1)S(1)}, u32[]{:S(2)}, u32[]{:S(2)}) collective-permute-start(bf16[1,256,128]{2,1,0:T(8,128)(2,1)S(1)} %get-tuple-element.55), channel_id=1, source_target_pairs={{0,4},{4,0},{8,12},{12,8},{16,20},{20,16},{24,28},{28,24},{1,5},{5... | collective-permute-start | bytes 196616 | tf_op jit(solution)/shard_map/ppermute | solution.py:18
  89.3 9.8 %collective-permute-start.21 = (bf16[1,256,128]{2,1,0:T(8,128)(2,1)S(1)}, bf16[1,256,128]{2,1,0:T(8,128)(2,1)S(1)}, u32[]{:S(2)}, u32[]{:S(2)}) collective-permute-start(bf16[1,256,128]{2,1,0:T(8,128)(2,1)S(1)} %get-tuple-element.56), channel_id=1, source_target_pairs={{0,8},{4,12},{8,0},{12,4},{16,24},{20,28},{24,16},{28,20},{1,9},{5... | collective-permute-start | bytes 196616 | tf_op jit(solution)/shard_map/ppermute | solution.py:18
  90.0 9.1 %collective-permute-start.22 = (bf16[1,256,128]{2,1,0:T(8,128)(2,1)S(1)}, bf16[1,256,128]{2,1,0:T(8,128)(2,1)S(1)}, u32[]{:S(2)}, u32[]{:S(2)}) collective-permute-start(bf16[1,256,128]{2,1,0:T(8,128)(2,1)S(1)} %get-tuple-element.57), channel_id=1, source_target_pairs={{0,12},{4,8},{8,4},{12,0},{16,28},{20,24},{24,20},{28,16},{1,13},{... | collective-permute-start | bytes 196616 | tf_op jit(solution)/shard_map/ppermute | solution.py:18

commit v26 on v25

--- a/solution.py
+++ b/solution.py
@@ -250,6 +250,8 @@
         for at, (start, wide) in enumerate(chunks):
             ends = at == len(chunks) - 1 and not last_level
             sides, mates = (half - 1, list(solved)) if ends else (0, [])
+            if level == 1 and at == 0:
+                mates = [ref for ref, _ in pieces[0][-1][half + 1:]]
             final = last_level and at == len(chunks) - 1
             known = [entry for below in range(level) for entry in pieces[below][at]]
             stored = done if final else []

time: 102 us -> 98.1 us (0.962)
  starting transfers between devices: 34.9 us -> 32.3 us
    ppermute x27, starting transfers between devices: 34.9 us -> 32.3 us  [hop(): return lax.ppermute(value, axis, [(at, at ^ step) for at in range(size)])]
where the time goes in v26:
time: 98.1 us; the launch traced here: 97.9 us
  waiting for transfers between devices  54.1 us (55%)
  starting transfers between devices  32.3 us (33%)
  Pallas kernels  9.04 us (9%)
  local copies, waits for them, and re-layouts  2.24 us (2%)
    ppermute x27, waiting for transfers between devices, hop(): return lax.ppermute(value, axis, [(at, at ^ step) for at in range(size)])  54.1 us
    ppermute x27, starting transfers between devices, hop(): return lax.ppermute(value, axis, [(at, at ^ step) for at in range(size)])  32.3 us
    pallas_call x9, Pallas kernels, call(): pl.pallas_call(kernel, out_shape=outs, in_specs=[VMEM] * len(arrays), out...  9.04 us
  transfers between devices with their start and end apart: 27, of which 17 were waited for; matrix products, arithmetic and copies ran while one was open for 1% of the time, Pallas kernels for 4%

profile of v26, /device:TPU:0, one launch (start us, length us, event | category | flops | bytes accessed | tf_op | source)
XLA Modules:
  0.0 97.9 jit_solution(3612368198318970965)
XLA Ops:
  1.4 2.6 %collective-permute-start = (bf16[128,256]{1,0:T(8,128)(2,1)S(1)}, bf16[128,256]{1,0:T(8,128)(2,1)S(1)}, u32[]{:S(2)}, u32[]{:S(2)}) collective-permute-start(bf16[128,256]{1,0:T(8,128)(2,1)S(1)} %bitcast.8), channel_id=1, source_target_pairs={{0,2},{1,3},{2,0},{3,1},{4,6},{5,7},{6,4},{7,5},{8,10},{9,11},{10,... | collective-permute-start | bytes 196616 | tf_op jit(solution)/shard_map/ppermute | solution.py:18
  4.0 1.3 %fusion = (bf16[1,2,2,256,256]{4,3,2,1,0:T(8,128)(2,1)S(1)}, bf16[1,2,2,256,256]{4,3,2,1,0:T(8,128)(2,1)S(1)}) fusion(bf16[2,2,2,256,256]{4,3,2,1,0:T(8,128)(2,1)} %param.8), kind=kLoop, calls=%fused_computation.2 | loop fusion | bytes 2097152 | tf_op jit(solution)/shard_map/slice | solution.py:204
  5.4 1.3 %collective-permute-done.refs_1_ = bf16[128,256]{1,0:T(8,128)(2,1)S(1)} collective-permute-done((bf16[128,256]{1,0:T(8,128)(2,1)S(1)}, bf16[128,256]{1,0:T(8,128)(2,1)S(1)}, u32[]{:S(2)}, u32[]{:S(2)}) %collective-permute-start) | collective-permute-done | bytes 65568 | tf_op jit(solution)/shard_map/ppermute | solution.py:18
  6.7 1.2 %collective-permute-done.2.refs_3_ = bf16[128,256]{1,0:T(8,128)(2,1)S(1)} collective-permute-done((bf16[128,256]{1,0:T(8,128)(2,1)S(1)}, bf16[128,256]{1,0:T(8,128)(2,1)S(1)}, u32[]{:S(2)}, u32[]{:S(2)}) %collective-permute-start.2) | collective-permute-done | bytes 65568 | tf_op jit(solution)/shard_map/ppermute | solution.py:18
  8.4 1.8 %collective-permute-start.7 = (bf16[2304,256]{1,0:T(8,128)(2,1)S(1)}, bf16[2304,256]{1,0:T(8,128)(2,1)S(1)}, u32[]{:S(2)}, u32[]{:S(2)}) collective-permute-start(bf16[2304,256]{1,0:T(8,128)(2,1)S(1)} %get-tuple-element.37.refs_3_), channel_id=1, source_target_pairs={{0,2},{1,3},{2,0},{3,1},{4,6},{5,7},{6,4},{7,5},{8,10},{9,11},{10,... | collective-permute-start | bytes 3538952 | tf_op jit(solution)/shard_map/ppermute | solution.py:18
  10.2 2.6 %collective-permute-start.3 = (bf16[2,256,512]{2,1,0:T(8,128)(2,1)S(1)}, bf16[2,256,512]{2,1,0:T(8,128)(2,1)S(1)}, u32[]{:S(2)}, u32[]{:S(2)}) collective-permute-start(bf16[2,256,512]{2,1,0:T(8,128)(2,1)S(1)} %get-tuple-element.33.refs_4_.refs_20_), channel_id=1, source_target_pairs={{0,16},{4,20},{8,24},{12,28},{16,0},{20,4},{24,8},{28,12},{1,17},{... | collective-permute-start | bytes 1572872 | tf_op jit(solution)/shard_map/ppermute | solution.py:18
  12.8 1.5 %collective-permute-start.4 = (bf16[1,256,512]{2,1,0:T(8,128)(2,1)S(1)}, bf16[1,256,512]{2,1,0:T(8,128)(2,1)S(1)}, u32[]{:S(2)}, u32[]{:S(2)}) collective-permute-start(bf16[1,256,512]{2,1,0:T(8,128)(2,1)S(1)} %get-tuple-element.34), channel_id=1, source_target_pairs={{0,4},{4,0},{8,12},{12,8},{16,20},{20,16},{24,28},{28,24},{1,5},{5... | collective-permute-start | bytes 786440 | tf_op jit(solution)/shard_map/ppermute | solution.py:18
  14.3 1.6 %collective-permute-start.5 = (bf16[1,256,512]{2,1,0:T(8,128)(2,1)S(1)}, bf16[1,256,512]{2,1,0:T(8,128)(2,1)S(1)}, u32[]{:S(2)}, u32[]{:S(2)}) collective-permute-start(bf16[1,256,512]{2,1,0:T(8,128)(2,1)S(1)} %get-tuple-element.35), channel_id=1, source_target_pairs={{0,8},{4,12},{8,0},{12,4},{16,24},{20,28},{24,16},{28,20},{1,9},{5... | collective-permute-start | bytes 786440 | tf_op jit(solution)/shard_map/ppermute | solution.py:18
  16.3 4.9 %collective-permute-done.4.refs_0_.refs_5_ = bf16[1,256,512]{2,1,0:T(8,128)(2,1)S(1)} collective-permute-done((bf16[1,256,512]{2,1,0:T(8,128)(2,1)S(1)}, bf16[1,256,512]{2,1,0:T(8,128)(2,1)S(1)}, u32[]{:S(2)}, u32[]{:S(2)}) %collective-permute-start.4) | collective-permute-done | bytes 262176 | tf_op jit(solution)/shard_map/ppermute | solution.py:18
  21.1 9.6 %collective-permute-done.5.refs_1_.refs_6_ = bf16[1,256,512]{2,1,0:T(8,128)(2,1)S(1)} collective-permute-done((bf16[1,256,512]{2,1,0:T(8,128)(2,1)S(1)}, bf16[1,256,512]{2,1,0:T(8,128)(2,1)S(1)}, u32[]{:S(2)}, u32[]{:S(2)}) %collective-permute-start.5) | collective-permute-done | bytes 262176 | tf_op jit(solution)/shard_map/ppermute | solution.py:18
  30.8 6.7 %collective-permute-done.6.refs_2_.refs_7_ = bf16[1,256,512]{2,1,0:T(8,128)(2,1)S(1)} collective-permute-done((bf16[1,256,512]{2,1,0:T(8,128)(2,1)S(1)}, bf16[1,256,512]{2,1,0:T(8,128)(2,1)S(1)}, u32[]{:S(2)}, u32[]{:S(2)}) %collective-permute-start.6) | collective-permute-done | bytes 262176 | tf_op jit(solution)/shard_map/ppermute | solution.py:18
  38.3 1.5 %collective-permute-start.13 = (bf16[1,256,384]{2,1,0:T(8,128)(2,1)S(1)}, bf16[1,256,384]{2,1,0:T(8,128)(2,1)S(1)}, u32[]{:S(2)}, u32[]{:S(2)}) collective-permute-start(bf16[1,256,384]{2,1,0:T(8,128)(2,1)S(1)} %get-tuple-element.48), channel_id=1, source_target_pairs={{0,4},{4,0},{8,12},{12,8},{16,20},{20,16},{24,28},{28,24},{1,5},{5... | collective-permute-start | bytes 589832 | tf_op jit(solution)/shard_map/ppermute | solution.py:18
  40.6 1.2 %collective-permute-start.15 = (bf16[1,256,384]{2,1,0:T(8,128)(2,1)S(1)}, bf16[1,256,384]{2,1,0:T(8,128)(2,1)S(1)}, u32[]{:S(2)}, u32[]{:S(2)}) collective-permute-start(bf16[1,256,384]{2,1,0:T(8,128)(2,1)S(1)} %get-tuple-element.50), channel_id=1, source_target_pairs={{0,12},{4,8},{8,4},{12,0},{16,28},{20,24},{24,20},{28,16},{1,13},{... | collective-permute-start | bytes 589832 | tf_op jit(solution)/shard_map/ppermute | solution.py:18
  42.4 1.6 %collective-permute-start.10 = (bf16[1,256,128]{2,1,0:T(8,128)(2,1)S(1)}, bf16[1,256,128]{2,1,0:T(8,128)(2,1)S(1)}, u32[]{:S(2)}, u32[]{:S(2)}) collective-permute-start(bf16[1,256,128]{2,1,0:T(8,128)(2,1)S(1)} %get-tuple-element.44), channel_id=1, source_target_pairs={{0,4},{4,0},{8,12},{12,8},{16,20},{20,16},{24,28},{28,24},{1,5},{5... | collective-permute-start | bytes 196616 | tf_op jit(solution)/shard_map/ppermute | solution.py:18
  45.2 1.7 %collective-permute-start.12 = (bf16[1,256,128]{2,1,0:T(8,128)(2,1)S(1)}, bf16[1,256,128]{2,1,0:T(8,128)(2,1)S(1)}, u32[]{:S(2)}, u32[]{:S(2)}) collective-permute-start(bf16[1,256,128]{2,1,0:T(8,128)(2,1)S(1)} %get-tuple-element.46), channel_id=1, source_target_pairs={{0,12},{4,8},{8,4},{12,0},{16,28},{20,24},{24,20},{28,16},{1,13},{... | collective-permute-start | bytes 196616 | tf_op jit(solution)/shard_map/ppermute | solution.py:18
  47.6 4.2 %collective-permute-done.15.refs_11_ = bf16[1,256,384]{2,1,0:T(8,128)(2,1)S(1)} collective-permute-done((bf16[1,256,384]{2,1,0:T(8,128)(2,1)S(1)}, bf16[1,256,384]{2,1,0:T(8,128)(2,1)S(1)}, u32[]{:S(2)}, u32[]{:S(2)}) %collective-permute-start.15) | collective-permute-done | bytes 196640 | tf_op jit(solution)/shard_map/ppermute | solution.py:18
  53.4 2.1 %shard_map.67.refs_12_.refs_21_ = bf16[2,256,384]{2,1,0:T(8,128)(2,1)S(1)} custom-call(s32[2,8,8]{2,1,0:T(8,128)S(1)} %copy-done.1, s32[2,2,8]{2,1,0:T(2,128)S(1)} %copy-done.2, s32[2,2]{1,0:T(2,128)S(1)} %copy-done.3, bf16[3,2,256,512]{3,2,1,0:T(8,128)(2,1)S(1)} %copy-done, bf16[2,256,256]{2,1,0:T(8,128)(2,1)S(1)} %get-tuple-element.47.inv, ...), custom_call_target="tpu_custom_call" | custom-call | flops 905969664 | bytes 9568912 | tf_op jit(solution)/shard_map/pallas_call | solution.py:66
  55.5 1.9 %collective-permute-start.23 = (bf16[2,256,384]{2,1,0:T(8,128)(2,1)S(1)}, bf16[2,256,384]{2,1,0:T(8,128)(2,1)S(1)}, u32[]{:S(2)}, u32[]{:S(2)}) collective-permute-start(bf16[2,256,384]{2,1,0:T(8,128)(2,1)S(1)} %shard_map.67.refs_12_.refs_21_), channel_id=1, source_target_pairs={{0,16},{4,20},{8,24},{12,28},{16,0},{20,4},{24,8},{28,12},{1,17},{... | collective-permute-start | bytes 1179656 | tf_op jit(solution)/shard_map/ppermute | solution.py:18
  57.4 1.4 %shard_map.68 = (bf16[2,256,128]{2,1,0:T(8,128)(2,1)S(1)}, bf16[1,256,512]{2,1,0:T(8,128)(2,1)S(1)}, bf16[1,256,512]{2,1,0:T(8,128)(2,1)S(1)}, bf16[1,256,512]{2,1,0:T(8,128)(2,1)S(1)}) custom-call(s32[2,8,8]{2,1,0:T(8,128)S(1)} %copy-done.1, s32[2,2,8]{2,1,0:T(2,128)S(1)} %copy-done.2, s32[2,2]{1,0:T(2,128)S(1)} %copy-done.3, ...), custom_call_target="tpu_custom_call" | custom-call | flops 301989888 | bytes 9896592 | tf_op jit(solution)/shard_map/pallas_call | solution.py:66
  58.8 1.6 %collective-permute-start.16 = (bf16[1,256,512]{2,1,0:T(8,128)(2,1)S(1)}, bf16[1,256,512]{2,1,0:T(8,128)(2,1)S(1)}, u32[]{:S(2)}, u32[]{:S(2)}) collective-permute-start(bf16[1,256,512]{2,1,0:T(8,128)(2,1)S(1)} %get-tuple-element.52), channel_id=1, source_target_pairs={{0,4},{4,0},{8,12},{12,8},{16,20},{20,16},{24,28},{28,24},{1,5},{5... | collective-permute-start | bytes 786440 | tf_op jit(solution)/shard_map/ppermute | solution.py:18
  60.4 1.1 %collective-permute-start.19 = (bf16[2,256,128]{2,1,0:T(8,128)(2,1)S(1)}, bf16[2,256,128]{2,1,0:T(8,128)(2,1)S(1)}, u32[]{:S(2)}, u32[]{:S(2)}) collective-permute-start(bf16[2,256,128]{2,1,0:T(8,128)(2,1)S(1)} %get-tuple-element.51.refs_12_.refs_22_), channel_id=1, source_target_pairs={{0,16},{4,20},{8,24},{12,28},{16,0},{20,4},{24,8},{28,12},{1,17},{... | collective-permute-start | bytes 393224 | tf_op jit(solution)/shard_map/ppermute | solution.py:18
  62.3 1.2 %collective-permute-start.18 = (bf16[1,256,512]{2,1,0:T(8,128)(2,1)S(1)}, bf16[1,256,512]{2,1,0:T(8,128)(2,1)S(1)}, u32[]{:S(2)}, u32[]{:S(2)}) collective-permute-start(bf16[1,256,512]{2,1,0:T(8,128)(2,1)S(1)} %get-tuple-element.54), channel_id=1, source_target_pairs={{0,12},{4,8},{8,4},{12,0},{16,28},{20,24},{24,20},{28,16},{1,13},{... | collective-permute-start | bytes 786440 | tf_op jit(solution)/shard_map/ppermute | solution.py:18
  63.5 14.8 %collective-permute-done.23.far.refs_16_ = bf16[2,256,384]{2,1,0:T(8,128)(2,1)S(1)} collective-permute-done((bf16[2,256,384]{2,1,0:T(8,128)(2,1)S(1)}, bf16[2,256,384]{2,1,0:T(8,128)(2,1)S(1)}, u32[]{:S(2)}, u32[]{:S(2)}) %collective-permute-start.23) | collective-permute-done | bytes 393248 | tf_op jit(solution)/shard_map/ppermute | solution.py:18
  78.5 1.1 %collective-permute-start.24 = (bf16[1,256,384]{2,1,0:T(8,128)(2,1)S(1)}, bf16[1,256,384]{2,1,0:T(8,128)(2,1)S(1)}, u32[]{:S(2)}, u32[]{:S(2)}) collective-permute-start(bf16[1,256,384]{2,1,0:T(8,128)(2,1)S(1)} %get-tuple-element.58), channel_id=1, source_target_pairs={{0,4},{4,0},{8,12},{12,8},{16,20},{20,16},{24,28},{28,24},{1,5},{5... | collective-permute-start | bytes 589832 | tf_op jit(solution)/shard_map/ppermute | solution.py:18
  80.3 3.0 %collective-permute-start.26 = (bf16[1,256,384]{2,1,0:T(8,128)(2,1)S(1)}, bf16[1,256,384]{2,1,0:T(8,128)(2,1)S(1)}, u32[]{:S(2)}, u32[]{:S(2)}) collective-permute-start(bf16[1,256,384]{2,1,0:T(8,128)(2,1)S(1)} %get-tuple-element.60), channel_id=1, source_target_pairs={{0,12},{4,8},{8,4},{12,0},{16,28},{20,24},{24,20},{28,16},{1,13},{... | collective-permute-start | bytes 589832 | tf_op jit(solution)/shard_map/ppermute | solution.py:18
  83.3 1.1 %collective-permute-done.18.refs_2_.refs_15_ = bf16[1,256,512]{2,1,0:T(8,128)(2,1)S(1)} collective-permute-done((bf16[1,256,512]{2,1,0:T(8,128)(2,1)S(1)}, bf16[1,256,512]{2,1,0:T(8,128)(2,1)S(1)}, u32[]{:S(2)}, u32[]{:S(2)}) %collective-permute-start.18) | collective-permute-done | bytes 262176 | tf_op jit(solution)/shard_map/ppermute | solution.py:18
  84.6 2.3 %collective-permute-start.20 = (bf16[1,256,128]{2,1,0:T(8,128)(2,1)S(1)}, bf16[1,256,128]{2,1,0:T(8,128)(2,1)S(1)}, u32[]{:S(2)}, u32[]{:S(2)}) collective-permute-start(bf16[1,256,128]{2,1,0:T(8,128)(2,1)S(1)} %get-tuple-element.55), channel_id=1, source_target_pairs={{0,4},{4,0},{8,12},{12,8},{16,20},{20,16},{24,28},{28,24},{1,5},{5... | collective-permute-start | bytes 196616 | tf_op jit(solution)/shard_map/ppermute | solution.py:18
  86.8 1.3 %collective-permute-done.24.refs_17_ = bf16[1,256,384]{2,1,0:T(8,128)(2,1)S(1)} collective-permute-done((bf16[1,256,384]{2,1,0:T(8,128)(2,1)S(1)}, bf16[1,256,384]{2,1,0:T(8,128)(2,1)S(1)}, u32[]{:S(2)}, u32[]{:S(2)}) %collective-permute-start.24) | collective-permute-done | bytes 196640 | tf_op jit(solution)/shard_map/ppermute | solution.py:18
  88.4 1.0 %collective-permute-done.25.refs_18_ = bf16[1,256,384]{2,1,0:T(8,128)(2,1)S(1)} collective-permute-done((bf16[1,256,384]{2,1,0:T(8,128)(2,1)S(1)}, bf16[1,256,384]{2,1,0:T(8,128)(2,1)S(1)}, u32[]{:S(2)}, u32[]{:S(2)}) %collective-permute-start.25) | collective-permute-done | bytes 196640 | tf_op jit(solution)/shard_map/ppermute | solution.py:18
  89.4 3.9 %collective-permute-done.26.refs_19_ = bf16[1,256,384]{2,1,0:T(8,128)(2,1)S(1)} collective-permute-done((bf16[1,256,384]{2,1,0:T(8,128)(2,1)S(1)}, bf16[1,256,384]{2,1,0:T(8,128)(2,1)S(1)}, u32[]{:S(2)}, u32[]{:S(2)}) %collective-permute-start.26) | collective-permute-done | bytes 196640 | tf_op jit(solution)/shard_map/ppermute | solution.py:18
  93.3 2.2 %shard_map.71.refs_23_ = bf16[2,256,384]{2,1,0:T(8,128)(2,1)S(1)} custom-call(s32[2,8,8]{2,1,0:T(8,128)S(1)} %copy-done.1, s32[2,2,8]{2,1,0:T(2,128)S(1)} %copy-done.2, s32[2,2]{1,0:T(2,128)S(1)} %copy-done.3, bf16[3,2,256,512]{3,2,1,0:T(8,128)(2,1)S(1)} %copy-done, bf16[2,256,256]{2,1,0:T(8,128)(2,1)S(1)} %get-tuple-element.43.inv, ...), custom_call_target="tpu_custom_call" | custom-call | flops 905969664 | bytes 11534992 | tf_op jit(solution)/shard_map/pallas_call | solution.py:66
  95.5 2.4 %shard_map.72 = bf16[3,2,256,512]{3,2,1,0:T(8,128)(2,1)} custom-call(s32[2,8,8]{2,1,0:T(8,128)S(1)} %copy-done.1, s32[2,2,8]{2,1,0:T(2,128)S(1)} %copy-done.2, s32[2,2]{1,0:T(2,128)S(1)} %copy-done.3, bf16[3,2,256,512]{3,2,1,0:T(8,128)(2,1)S(1)} %copy-done, bf16[2,256,256]{2,1,0:T(8,128)(2,1)S(1)} %get-tuple-element.43.inv, ...), custom_call_target="tpu_custom_call" | custom-call | flops 301989888 | bytes 12845712 | tf_op jit(solution)/shard_map/pallas_call | solution.py:66
  (43 shorter events, 10.2 us)
Async XLA Ops:
  0.9 5.8 %collective-permute-start.1 = (bf16[128,256]{1,0:T(8,128)(2,1)S(1)}, bf16[128,256]{1,0:T(8,128)(2,1)S(1)}, u32[]{:S(2)}, u32[]{:S(2)}) collective-permute-start(bf16[128,256]{1,0:T(8,128)(2,1)S(1)} %bitcast.7), channel_id=1, source_target_pairs={{0,1},{1,0},{2,3},{3,2},{4,5},{5,4},{6,7},{7,6},{8,9},{9,8},{10,11... | collective-permute-start | bytes 196616 | tf_op jit(solution)/shard_map/ppermute | solution.py:18
  1.4 5.3 %collective-permute-start = (bf16[128,256]{1,0:T(8,128)(2,1)S(1)}, bf16[128,256]{1,0:T(8,128)(2,1)S(1)}, u32[]{:S(2)}, u32[]{:S(2)}) collective-permute-start(bf16[128,256]{1,0:T(8,128)(2,1)S(1)} %bitcast.8), channel_id=1, source_target_pairs={{0,2},{1,3},{2,0},{3,1},{4,6},{5,7},{6,4},{7,5},{8,10},{9,11},{10,... | collective-permute-start | bytes 196616 | tf_op jit(solution)/shard_map/ppermute | solution.py:18
  5.3 1.4 %copy-start = (bf16[3,2,256,512]{3,2,1,0:T(8,128)(2,1)S(1)}, bf16[3,2,256,512]{3,2,1,0:T(8,128)(2,1)}, u32[]{:S(2)}) copy-start(bf16[3,2,256,512]{3,2,1,0:T(8,128)(2,1)} %noise.7) | copy-start | bytes 4718596
  5.3 2.7 %copy-start.1 = (s32[2,8,8]{2,1,0:T(8,128)S(1)}, s32[2,8,8]{2,1,0:T(8,128)}, u32[]{:S(2)}) copy-start(s32[2,8,8]{2,1,0:T(8,128)} %picks.15) | copy-start | bytes 1540
  6.7 1.3 %collective-permute-start.2 = (bf16[128,256]{1,0:T(8,128)(2,1)S(1)}, bf16[128,256]{1,0:T(8,128)(2,1)S(1)}, u32[]{:S(2)}, u32[]{:S(2)}) collective-permute-start(bf16[128,256]{1,0:T(8,128)(2,1)S(1)} %collective-permute-done.refs_1_), channel_id=1, source_target_pairs={{0,1},{1,0},{2,3},{3,2},{4,5},{5,4},{6,7},{7,6},{8,9},{9,8},{10,11... | collective-permute-start | bytes 196616 | tf_op jit(solution)/shard_map/ppermute | solution.py:18
  8.4 29.1 %collective-permute-start.7 = (bf16[2304,256]{1,0:T(8,128)(2,1)S(1)}, bf16[2304,256]{1,0:T(8,128)(2,1)S(1)}, u32[]{:S(2)}, u32[]{:S(2)}) collective-permute-start(bf16[2304,256]{1,0:T(8,128)(2,1)S(1)} %get-tuple-element.37.refs_3_), channel_id=1, source_target_pairs={{0,2},{1,3},{2,0},{3,1},{4,6},{5,7},{6,4},{7,5},{8,10},{9,11},{10,... | collective-permute-start | bytes 3538952 | tf_op jit(solution)/shard_map/ppermute | solution.py:18
  10.2 27.3 %collective-permute-start.3 = (bf16[2,256,512]{2,1,0:T(8,128)(2,1)S(1)}, bf16[2,256,512]{2,1,0:T(8,128)(2,1)S(1)}, u32[]{:S(2)}, u32[]{:S(2)}) collective-permute-start(bf16[2,256,512]{2,1,0:T(8,128)(2,1)S(1)} %get-tuple-element.33.refs_4_.refs_20_), channel_id=1, source_target_pairs={{0,16},{4,20},{8,24},{12,28},{16,0},{20,4},{24,8},{28,12},{1,17},{... | collective-permute-start | bytes 1572872 | tf_op jit(solution)/shard_map/ppermute | solution.py:18
  12.8 8.3 %collective-permute-start.4 = (bf16[1,256,512]{2,1,0:T(8,128)(2,1)S(1)}, bf16[1,256,512]{2,1,0:T(8,128)(2,1)S(1)}, u32[]{:S(2)}, u32[]{:S(2)}) collective-permute-start(bf16[1,256,512]{2,1,0:T(8,128)(2,1)S(1)} %get-tuple-element.34), channel_id=1, source_target_pairs={{0,4},{4,0},{8,12},{12,8},{16,20},{20,16},{24,28},{28,24},{1,5},{5... | collective-permute-start | bytes 786440 | tf_op jit(solution)/shard_map/ppermute | solution.py:18
  14.3 16.5 %collective-permute-start.5 = (bf16[1,256,512]{2,1,0:T(8,128)(2,1)S(1)}, bf16[1,256,512]{2,1,0:T(8,128)(2,1)S(1)}, u32[]{:S(2)}, u32[]{:S(2)}) collective-permute-start(bf16[1,256,512]{2,1,0:T(8,128)(2,1)S(1)} %get-tuple-element.35), channel_id=1, source_target_pairs={{0,8},{4,12},{8,0},{12,4},{16,24},{20,28},{24,16},{28,20},{1,9},{5... | collective-permute-start | bytes 786440 | tf_op jit(solution)/shard_map/ppermute | solution.py:18
  15.9 21.6 %collective-permute-start.6 = (bf16[1,256,512]{2,1,0:T(8,128)(2,1)S(1)}, bf16[1,256,512]{2,1,0:T(8,128)(2,1)S(1)}, u32[]{:S(2)}, u32[]{:S(2)}) collective-permute-start(bf16[1,256,512]{2,1,0:T(8,128)(2,1)S(1)} %get-tuple-element.36), channel_id=1, source_target_pairs={{0,12},{4,8},{8,4},{12,0},{16,28},{20,24},{24,20},{28,16},{1,13},{... | collective-permute-start | bytes 786440 | tf_op jit(solution)/shard_map/ppermute | solution.py:18
  37.7 4.1 %collective-permute-start.8 = (bf16[2304,256]{1,0:T(8,128)(2,1)S(1)}, bf16[2304,256]{1,0:T(8,128)(2,1)S(1)}, u32[]{:S(2)}, u32[]{:S(2)}) collective-permute-start(bf16[2304,256]{1,0:T(8,128)(2,1)S(1)} %get-tuple-element.38.refs_0_), channel_id=1, source_target_pairs={{0,1},{1,0},{2,3},{3,2},{4,5},{5,4},{6,7},{7,6},{8,9},{9,8},{10,11... | collective-permute-start | bytes 3538952 | tf_op jit(solution)/shard_map/ppermute | solution.py:18
  37.8 4.5 %collective-permute-start.9 = (bf16[2304,256]{1,0:T(8,128)(2,1)S(1)}, bf16[2304,256]{1,0:T(8,128)(2,1)S(1)}, u32[]{:S(2)}, u32[]{:S(2)}) collective-permute-start(bf16[2304,256]{1,0:T(8,128)(2,1)S(1)} %get-tuple-element.39.refs_1_), channel_id=1, source_target_pairs={{0,1},{1,0},{2,3},{3,2},{4,5},{5,4},{6,7},{7,6},{8,9},{9,8},{10,11... | collective-permute-start | bytes 3538952 | tf_op jit(solution)/shard_map/ppermute | solution.py:18
  38.3 6.9 %collective-permute-start.13 = (bf16[1,256,384]{2,1,0:T(8,128)(2,1)S(1)}, bf16[1,256,384]{2,1,0:T(8,128)(2,1)S(1)}, u32[]{:S(2)}, u32[]{:S(2)}) collective-permute-start(bf16[1,256,384]{2,1,0:T(8,128)(2,1)S(1)} %get-tuple-element.48), channel_id=1, source_target_pairs={{0,4},{4,0},{8,12},{12,8},{16,20},{20,16},{24,28},{28,24},{1,5},{5... | collective-permute-start | bytes 589832 | tf_op jit(solution)/shard_map/ppermute | solution.py:18
  39.8 7.8 %collective-permute-start.14 = (bf16[1,256,384]{2,1,0:T(8,128)(2,1)S(1)}, bf16[1,256,384]{2,1,0:T(8,128)(2,1)S(1)}, u32[]{:S(2)}, u32[]{:S(2)}) collective-permute-start(bf16[1,256,384]{2,1,0:T(8,128)(2,1)S(1)} %get-tuple-element.49), channel_id=1, source_target_pairs={{0,8},{4,12},{8,0},{12,4},{16,24},{20,28},{24,16},{28,20},{1,9},{5... | collective-permute-start | bytes 589832 | tf_op jit(solution)/shard_map/ppermute | solution.py:18
  40.6 11.2 %collective-permute-start.15 = (bf16[1,256,384]{2,1,0:T(8,128)(2,1)S(1)}, bf16[1,256,384]{2,1,0:T(8,128)(2,1)S(1)}, u32[]{:S(2)}, u32[]{:S(2)}) collective-permute-start(bf16[1,256,384]{2,1,0:T(8,128)(2,1)S(1)} %get-tuple-element.50), channel_id=1, source_target_pairs={{0,12},{4,8},{8,4},{12,0},{16,28},{20,24},{24,20},{28,16},{1,13},{... | collective-permute-start | bytes 589832 | tf_op jit(solution)/shard_map/ppermute | solution.py:18
  42.3 11.1 %copy-start.2 = (s32[2,2,8]{2,1,0:T(2,128)S(1)}, s32[2,2,8]{2,1,0:T(2,128)}, u32[]{:S(2)}) copy-start(s32[2,2,8]{2,1,0:T(2,128)} %lists.7) | copy-start | bytes 388
  42.3 11.1 %copy-start.3 = (s32[2,2]{1,0:T(2,128)S(1)}, s32[2,2]{1,0:T(2,128)}, u32[]{:S(2)}) copy-start(s32[2,2]{1,0:T(2,128)} %counts.7) | copy-start | bytes 52
  42.4 9.4 %collective-permute-start.10 = (bf16[1,256,128]{2,1,0:T(8,128)(2,1)S(1)}, bf16[1,256,128]{2,1,0:T(8,128)(2,1)S(1)}, u32[]{:S(2)}, u32[]{:S(2)}) collective-permute-start(bf16[1,256,128]{2,1,0:T(8,128)(2,1)S(1)} %get-tuple-element.44), channel_id=1, source_target_pairs={{0,4},{4,0},{8,12},{12,8},{16,20},{20,16},{24,28},{28,24},{1,5},{5... | collective-permute-start | bytes 196616 | tf_op jit(solution)/shard_map/ppermute | solution.py:18
  44.0 8.8 %collective-permute-start.11 = (bf16[1,256,128]{2,1,0:T(8,128)(2,1)S(1)}, bf16[1,256,128]{2,1,0:T(8,128)(2,1)S(1)}, u32[]{:S(2)}, u32[]{:S(2)}) collective-permute-start(bf16[1,256,128]{2,1,0:T(8,128)(2,1)S(1)} %get-tuple-element.45), channel_id=1, source_target_pairs={{0,8},{4,12},{8,0},{12,4},{16,24},{20,28},{24,16},{28,20},{1,9},{5... | collective-permute-start | bytes 196616 | tf_op jit(solution)/shard_map/ppermute | solution.py:18
  45.2 8.2 %collective-permute-start.12 = (bf16[1,256,128]{2,1,0:T(8,128)(2,1)S(1)}, bf16[1,256,128]{2,1,0:T(8,128)(2,1)S(1)}, u32[]{:S(2)}, u32[]{:S(2)}) collective-permute-start(bf16[1,256,128]{2,1,0:T(8,128)(2,1)S(1)} %get-tuple-element.46), channel_id=1, source_target_pairs={{0,12},{4,8},{8,4},{12,0},{16,28},{20,24},{24,20},{28,16},{1,13},{... | collective-permute-start | bytes 196616 | tf_op jit(solution)/shard_map/ppermute | solution.py:18
  55.5 22.8 %collective-permute-start.23 = (bf16[2,256,384]{2,1,0:T(8,128)(2,1)S(1)}, bf16[2,256,384]{2,1,0:T(8,128)(2,1)S(1)}, u32[]{:S(2)}, u32[]{:S(2)}) collective-permute-start(bf16[2,256,384]{2,1,0:T(8,128)(2,1)S(1)} %shard_map.67.refs_12_.refs_21_), channel_id=1, source_target_pairs={{0,16},{4,20},{8,24},{12,28},{16,0},{20,4},{24,8},{28,12},{1,17},{... | collective-permute-start | bytes 1179656 | tf_op jit(solution)/shard_map/ppermute | solution.py:18
  58.8 21.5 %collective-permute-start.16 = (bf16[1,256,512]{2,1,0:T(8,128)(2,1)S(1)}, bf16[1,256,512]{2,1,0:T(8,128)(2,1)S(1)}, u32[]{:S(2)}, u32[]{:S(2)}) collective-permute-start(bf16[1,256,512]{2,1,0:T(8,128)(2,1)S(1)} %get-tuple-element.52), channel_id=1, source_target_pairs={{0,4},{4,0},{8,12},{12,8},{16,20},{20,16},{24,28},{28,24},{1,5},{5... | collective-permute-start | bytes 786440 | tf_op jit(solution)/shard_map/ppermute | solution.py:18
  60.4 19.9 %collective-permute-start.19 = (bf16[2,256,128]{2,1,0:T(8,128)(2,1)S(1)}, bf16[2,256,128]{2,1,0:T(8,128)(2,1)S(1)}, u32[]{:S(2)}, u32[]{:S(2)}) collective-permute-start(bf16[2,256,128]{2,1,0:T(8,128)(2,1)S(1)} %get-tuple-element.51.refs_12_.refs_22_), channel_id=1, source_target_pairs={{0,16},{4,20},{8,24},{12,28},{16,0},{20,4},{24,8},{28,12},{1,17},{... | collective-permute-start | bytes 393224 | tf_op jit(solution)/shard_map/ppermute | solution.py:18
  61.5 21.8 %collective-permute-start.17 = (bf16[1,256,512]{2,1,0:T(8,128)(2,1)S(1)}, bf16[1,256,512]{2,1,0:T(8,128)(2,1)S(1)}, u32[]{:S(2)}, u32[]{:S(2)}) collective-permute-start(bf16[1,256,512]{2,1,0:T(8,128)(2,1)S(1)} %get-tuple-element.53), channel_id=1, source_target_pairs={{0,8},{4,12},{8,0},{12,4},{16,24},{20,28},{24,16},{28,20},{1,9},{5... | collective-permute-start | bytes 786440 | tf_op jit(solution)/shard_map/ppermute | solution.py:18
  62.3 22.1 %collective-permute-start.18 = (bf16[1,256,512]{2,1,0:T(8,128)(2,1)S(1)}, bf16[1,256,512]{2,1,0:T(8,128)(2,1)S(1)}, u32[]{:S(2)}, u32[]{:S(2)}) collective-permute-start(bf16[1,256,512]{2,1,0:T(8,128)(2,1)S(1)} %get-tuple-element.54), channel_id=1, source_target_pairs={{0,12},{4,8},{8,4},{12,0},{16,28},{20,24},{24,20},{28,16},{1,13},{... | collective-permute-start | bytes 786440 | tf_op jit(solution)/shard_map/ppermute | solution.py:18
  78.5 9.6 %collective-permute-start.24 = (bf16[1,256,384]{2,1,0:T(8,128)(2,1)S(1)}, bf16[1,256,384]{2,1,0:T(8,128)(2,1)S(1)}, u32[]{:S(2)}, u32[]{:S(2)}) collective-permute-start(bf16[1,256,384]{2,1,0:T(8,128)(2,1)S(1)} %get-tuple-element.58), channel_id=1, source_target_pairs={{0,4},{4,0},{8,12},{12,8},{16,20},{20,16},{24,28},{28,24},{1,5},{5... | collective-permute-start | bytes 589832 | tf_op jit(solution)/shard_map/ppermute | solution.py:18
  80.3 9.1 %collective-permute-start.25 = (bf16[1,256,384]{2,1,0:T(8,128)(2,1)S(1)}, bf16[1,256,384]{2,1,0:T(8,128)(2,1)S(1)}, u32[]{:S(2)}, u32[]{:S(2)}) collective-permute-start(bf16[1,256,384]{2,1,0:T(8,128)(2,1)S(1)} %get-tuple-element.59), channel_id=1, source_target_pairs={{0,8},{4,12},{8,0},{12,4},{16,24},{20,28},{24,16},{28,20},{1,9},{5... | collective-permute-start | bytes 589832 | tf_op jit(solution)/shard_map/ppermute | solution.py:18
  80.3 13.0 %collective-permute-start.26 = (bf16[1,256,384]{2,1,0:T(8,128)(2,1)S(1)}, bf16[1,256,384]{2,1,0:T(8,128)(2,1)S(1)}, u32[]{:S(2)}, u32[]{:S(2)}) collective-permute-start(bf16[1,256,384]{2,1,0:T(8,128)(2,1)S(1)} %get-tuple-element.60), channel_id=1, source_target_pairs={{0,12},{4,8},{8,4},{12,0},{16,28},{20,24},{24,20},{28,16},{1,13},{... | collective-permute-start | bytes 589832 | tf_op jit(solution)/shard_map/ppermute | solution.py:18
  84.6 11.0 %collective-permute-start.20 = (bf16[1,256,128]{2,1,0:T(8,128)(2,1)S(1)}, bf16[1,256,128]{2,1,0:T(8,128)(2,1)S(1)}, u32[]{:S(2)}, u32[]{:S(2)}) collective-permute-start(bf16[1,256,128]{2,1,0:T(8,128)(2,1)S(1)} %get-tuple-element.55), channel_id=1, source_target_pairs={{0,4},{4,0},{8,12},{12,8},{16,20},{20,16},{24,28},{28,24},{1,5},{5... | collective-permute-start | bytes 196616 | tf_op jit(solution)/shard_map/ppermute | solution.py:18
  86.8 8.7 %collective-permute-start.21 = (bf16[1,256,128]{2,1,0:T(8,128)(2,1)S(1)}, bf16[1,256,128]{2,1,0:T(8,128)(2,1)S(1)}, u32[]{:S(2)}, u32[]{:S(2)}) collective-permute-start(bf16[1,256,128]{2,1,0:T(8,128)(2,1)S(1)} %get-tuple-element.56), channel_id=1, source_target_pairs={{0,8},{4,12},{8,0},{12,4},{16,24},{20,28},{24,16},{28,20},{1,9},{5... | collective-permute-start | bytes 196616 | tf_op jit(solution)/shard_map/ppermute | solution.py:18
  88.1 7.5 %collective-permute-start.22 = (bf16[1,256,128]{2,1,0:T(8,128)(2,1)S(1)}, bf16[1,256,128]{2,1,0:T(8,128)(2,1)S(1)}, u32[]{:S(2)}, u32[]{:S(2)}) collective-permute-start(bf16[1,256,128]{2,1,0:T(8,128)(2,1)S(1)} %get-tuple-element.57), channel_id=1, source_target_pairs={{0,12},{4,8},{8,4},{12,0},{16,28},{20,24},{24,20},{28,16},{1,13},{... | collective-permute-start | bytes 196616 | tf_op jit(solution)/shard_map/ppermute | solution.py:18

commit v27 on v22

--- a/solution.py
+++ b/solution.py
@@ -166,14 +166,14 @@
                 total = term if total is None else total + term
         right_side = (noise[level, node, :, columns].astype(F32) - total).astype(BF16)
         solved[node] = transposed_dot(inv[node], right_side).astype(BF16)
+        if done:
+            here = target.at[level, node, :, pl.ds(chunk * wide, wide)]
+            copies.append(pltpu.make_async_copy(solved.at[node], here, sems.at[len(copies)]))
+            copies[-1].start()
     for step, send in enumerate(sends, 1):
         node = entry_of(picks[level], myself ^ step, myself)
         for at, ref in enumerate([*chunks, solved]):
             send[at] = ref[node]
-    if done:
-        here = target.at[level, :, :, pl.ds(chunk * wide, wide)]
-        copies.append(pltpu.make_async_copy(solved, here, sems.at[len(done)]))
-        copies[-1].start()
     for copy in copies:
         copy.wait()
 
@@ -245,7 +245,7 @@
             if final:
                 scratch += [
                     pltpu.VMEM((nodes, rows, wide), BF16),
-                    pltpu.SemaphoreType.DMA((len(stored) + 1,)),
+                    pltpu.SemaphoreType.DMA((len(stored) + nodes,)),
                 ]
             here, *sent = call(
                 functools.partial(
@@ -267,7 +267,7 @@
         got = near(sends)
         pieces.append([])
         for at in chunks:
-            waits = got if at == CHUNKS - 1 else []
+            waits = got[:half // 2] if at == CHUNKS - 1 else []
             sends = call(
                 functools.partial(relay_kernel, half, level, len(waits), 0),
                 [shape(1, rows, wide)] * (half - 1),

time: 93.2 us -> 93.1 us (level)
  no operation moved by 1% of the time
where the time goes in v27:
time: 93.1 us; the launch traced here: 92.9 us
  waiting for transfers between devices  49.3 us (53%)
  starting transfers between devices  31.6 us (34%)
  Pallas kernels  9.5 us (10%)
  local copies, waits for them, and re-layouts  2.24 us (2%)
    ppermute x27, waiting for transfers between devices, hop(): return lax.ppermute(value, axis, [(at, at ^ step) for at in range(size)])  49.3 us
    ppermute x27, starting transfers between devices, hop(): return lax.ppermute(value, axis, [(at, at ^ step) for at in range(size)])  31.6 us
    pallas_call x9, Pallas kernels, call(): pl.pallas_call(kernel, out_shape=outs, in_specs=[VMEM] * len(arrays), out...  9.5 us
  transfers between devices with their start and end apart: 27, of which 14 were waited for; matrix products, arithmetic and copies ran while one was open for 1% of the time, Pallas kernels for 7%

profile of v27, /device:TPU:0, one launch (start us, length us, event | category | flops | bytes accessed | tf_op | source)
XLA Modules:
  0.0 92.9 jit_solution(407515330254160136)
XLA Ops:
  1.4 2.6 %collective-permute-start = (bf16[128,256]{1,0:T(8,128)(2,1)S(1)}, bf16[128,256]{1,0:T(8,128)(2,1)S(1)}, u32[]{:S(2)}, u32[]{:S(2)}) collective-permute-start(bf16[128,256]{1,0:T(8,128)(2,1)S(1)} %bitcast.8), channel_id=1, source_target_pairs={{0,2},{1,3},{2,0},{3,1},{4,6},{5,7},{6,4},{7,5},{8,10},{9,11},{10,... | collective-permute-start | bytes 196616 | tf_op jit(solution)/shard_map/ppermute | solution.py:17
  4.0 1.3 %fusion = (bf16[1,2,2,256,256]{4,3,2,1,0:T(8,128)(2,1)S(1)}, bf16[1,2,2,256,256]{4,3,2,1,0:T(8,128)(2,1)S(1)}) fusion(bf16[2,2,2,256,256]{4,3,2,1,0:T(8,128)(2,1)} %param.8), kind=kLoop, calls=%fused_computation.2 | loop fusion | bytes 2097152 | tf_op jit(solution)/shard_map/slice | solution.py:193
  5.4 1.3 %collective-permute-done.refs_1_ = bf16[128,256]{1,0:T(8,128)(2,1)S(1)} collective-permute-done((bf16[128,256]{1,0:T(8,128)(2,1)S(1)}, bf16[128,256]{1,0:T(8,128)(2,1)S(1)}, u32[]{:S(2)}, u32[]{:S(2)}) %collective-permute-start) | collective-permute-done | bytes 65568 | tf_op jit(solution)/shard_map/ppermute | solution.py:17
  6.7 1.2 %collective-permute-done.2.refs_3_ = bf16[128,256]{1,0:T(8,128)(2,1)S(1)} collective-permute-done((bf16[128,256]{1,0:T(8,128)(2,1)S(1)}, bf16[128,256]{1,0:T(8,128)(2,1)S(1)}, u32[]{:S(2)}, u32[]{:S(2)}) %collective-permute-start.2) | collective-permute-done | bytes 65568 | tf_op jit(solution)/shard_map/ppermute | solution.py:17
  8.4 1.8 %collective-permute-start.7 = (bf16[2304,256]{1,0:T(8,128)(2,1)S(1)}, bf16[2304,256]{1,0:T(8,128)(2,1)S(1)}, u32[]{:S(2)}, u32[]{:S(2)}) collective-permute-start(bf16[2304,256]{1,0:T(8,128)(2,1)S(1)} %get-tuple-element.37.refs_3_), channel_id=1, source_target_pairs={{0,2},{1,3},{2,0},{3,1},{4,6},{5,7},{6,4},{7,5},{8,10},{9,11},{10,... | collective-permute-start | bytes 3538952 | tf_op jit(solution)/shard_map/ppermute | solution.py:17
  10.2 2.6 %collective-permute-start.3 = (bf16[2,256,512]{2,1,0:T(8,128)(2,1)S(1)}, bf16[2,256,512]{2,1,0:T(8,128)(2,1)S(1)}, u32[]{:S(2)}, u32[]{:S(2)}) collective-permute-start(bf16[2,256,512]{2,1,0:T(8,128)(2,1)S(1)} %get-tuple-element.33.refs_4_.refs_20_), channel_id=1, source_target_pairs={{0,16},{4,20},{8,24},{12,28},{16,0},{20,4},{24,8},{28,12},{1,17},{... | collective-permute-start | bytes 1572872 | tf_op jit(solution)/shard_map/ppermute | solution.py:17
  12.8 1.5 %collective-permute-start.4 = (bf16[1,256,512]{2,1,0:T(8,128)(2,1)S(1)}, bf16[1,256,512]{2,1,0:T(8,128)(2,1)S(1)}, u32[]{:S(2)}, u32[]{:S(2)}) collective-permute-start(bf16[1,256,512]{2,1,0:T(8,128)(2,1)S(1)} %get-tuple-element.34), channel_id=1, source_target_pairs={{0,4},{4,0},{8,12},{12,8},{16,20},{20,16},{24,28},{28,24},{1,5},{5... | collective-permute-start | bytes 786440 | tf_op jit(solution)/shard_map/ppermute | solution.py:17
  14.3 1.6 %collective-permute-start.5 = (bf16[1,256,512]{2,1,0:T(8,128)(2,1)S(1)}, bf16[1,256,512]{2,1,0:T(8,128)(2,1)S(1)}, u32[]{:S(2)}, u32[]{:S(2)}) collective-permute-start(bf16[1,256,512]{2,1,0:T(8,128)(2,1)S(1)} %get-tuple-element.35), channel_id=1, source_target_pairs={{0,8},{4,12},{8,0},{12,4},{16,24},{20,28},{24,16},{28,20},{1,9},{5... | collective-permute-start | bytes 786440 | tf_op jit(solution)/shard_map/ppermute | solution.py:17
  16.3 4.9 %collective-permute-done.4.refs_0_.refs_5_ = bf16[1,256,512]{2,1,0:T(8,128)(2,1)S(1)} collective-permute-done((bf16[1,256,512]{2,1,0:T(8,128)(2,1)S(1)}, bf16[1,256,512]{2,1,0:T(8,128)(2,1)S(1)}, u32[]{:S(2)}, u32[]{:S(2)}) %collective-permute-start.4) | collective-permute-done | bytes 262176 | tf_op jit(solution)/shard_map/ppermute | solution.py:17
  21.1 9.6 %collective-permute-done.5.refs_1_.refs_6_ = bf16[1,256,512]{2,1,0:T(8,128)(2,1)S(1)} collective-permute-done((bf16[1,256,512]{2,1,0:T(8,128)(2,1)S(1)}, bf16[1,256,512]{2,1,0:T(8,128)(2,1)S(1)}, u32[]{:S(2)}, u32[]{:S(2)}) %collective-permute-start.5) | collective-permute-done | bytes 262176 | tf_op jit(solution)/shard_map/ppermute | solution.py:17
  30.8 6.7 %collective-permute-done.6.refs_2_.refs_7_ = bf16[1,256,512]{2,1,0:T(8,128)(2,1)S(1)} collective-permute-done((bf16[1,256,512]{2,1,0:T(8,128)(2,1)S(1)}, bf16[1,256,512]{2,1,0:T(8,128)(2,1)S(1)}, u32[]{:S(2)}, u32[]{:S(2)}) %collective-permute-start.6) | collective-permute-done | bytes 262176 | tf_op jit(solution)/shard_map/ppermute | solution.py:17
  38.3 1.5 %collective-permute-start.13 = (bf16[1,256,256]{2,1,0:T(8,128)(2,1)S(1)}, bf16[1,256,256]{2,1,0:T(8,128)(2,1)S(1)}, u32[]{:S(2)}, u32[]{:S(2)}) collective-permute-start(bf16[1,256,256]{2,1,0:T(8,128)(2,1)S(1)} %get-tuple-element.48), channel_id=1, source_target_pairs={{0,4},{4,0},{8,12},{12,8},{16,20},{20,16},{24,28},{28,24},{1,5},{5... | collective-permute-start | bytes 393224 | tf_op jit(solution)/shard_map/ppermute | solution.py:17
  40.6 1.2 %collective-permute-start.15 = (bf16[1,256,256]{2,1,0:T(8,128)(2,1)S(1)}, bf16[1,256,256]{2,1,0:T(8,128)(2,1)S(1)}, u32[]{:S(2)}, u32[]{:S(2)}) collective-permute-start(bf16[1,256,256]{2,1,0:T(8,128)(2,1)S(1)} %get-tuple-element.50), channel_id=1, source_target_pairs={{0,12},{4,8},{8,4},{12,0},{16,28},{20,24},{24,20},{28,16},{1,13},{... | collective-permute-start | bytes 393224 | tf_op jit(solution)/shard_map/ppermute | solution.py:17
  42.3 1.6 %collective-permute-start.10 = (bf16[1,256,256]{2,1,0:T(8,128)(2,1)S(1)}, bf16[1,256,256]{2,1,0:T(8,128)(2,1)S(1)}, u32[]{:S(2)}, u32[]{:S(2)}) collective-permute-start(bf16[1,256,256]{2,1,0:T(8,128)(2,1)S(1)} %get-tuple-element.44), channel_id=1, source_target_pairs={{0,4},{4,0},{8,12},{12,8},{16,20},{20,16},{24,28},{28,24},{1,5},{5... | collective-permute-start | bytes 393224 | tf_op jit(solution)/shard_map/ppermute | solution.py:17
  44.7 1.2 %collective-permute-start.12 = (bf16[1,256,256]{2,1,0:T(8,128)(2,1)S(1)}, bf16[1,256,256]{2,1,0:T(8,128)(2,1)S(1)}, u32[]{:S(2)}, u32[]{:S(2)}) collective-permute-start(bf16[1,256,256]{2,1,0:T(8,128)(2,1)S(1)} %get-tuple-element.46), channel_id=1, source_target_pairs={{0,12},{4,8},{8,4},{12,0},{16,28},{20,24},{24,20},{28,16},{1,13},{... | collective-permute-start | bytes 393224 | tf_op jit(solution)/shard_map/ppermute | solution.py:17
  46.2 2.8 %collective-permute-done.15.refs_11_ = bf16[1,256,256]{2,1,0:T(8,128)(2,1)S(1)} collective-permute-done((bf16[1,256,256]{2,1,0:T(8,128)(2,1)S(1)}, bf16[1,256,256]{2,1,0:T(8,128)(2,1)S(1)}, u32[]{:S(2)}, u32[]{:S(2)}) %collective-permute-start.15) | collective-permute-done | bytes 131104 | tf_op jit(solution)/shard_map/ppermute | solution.py:17
  48.9 1.9 %shard_map.67.refs_12_.refs_21_ = bf16[2,256,256]{2,1,0:T(8,128)(2,1)S(1)} custom-call(s32[2,8,8]{2,1,0:T(8,128)S(1)} %copy-done.1, s32[2,2,8]{2,1,0:T(2,128)S(1)} %copy-done.2, s32[2,2]{1,0:T(2,128)S(1)} %copy-done.3, bf16[3,2,256,512]{3,2,1,0:T(8,128)(2,1)S(1)} %copy-done, bf16[2,256,256]{2,1,0:T(8,128)(2,1)S(1)} %get-tuple-element.47.inv, ...), custom_call_target="tpu_custom_call" | custom-call | flops 603979776 | bytes 9044624 | tf_op jit(solution)/shard_map/pallas_call | solution.py:56
  50.9 1.7 %collective-permute-start.23 = (bf16[2,256,256]{2,1,0:T(8,128)(2,1)S(1)}, bf16[2,256,256]{2,1,0:T(8,128)(2,1)S(1)}, u32[]{:S(2)}, u32[]{:S(2)}) collective-permute-start(bf16[2,256,256]{2,1,0:T(8,128)(2,1)S(1)} %shard_map.67.refs_12_.refs_21_), channel_id=1, source_target_pairs={{0,16},{4,20},{8,24},{12,28},{16,0},{20,4},{24,8},{28,12},{1,17},{... | collective-permute-start | bytes 786440 | tf_op jit(solution)/shard_map/ppermute | solution.py:17
  52.6 1.6 %collective-permute-done.12.refs_11_ = bf16[1,256,256]{2,1,0:T(8,128)(2,1)S(1)} collective-permute-done((bf16[1,256,256]{2,1,0:T(8,128)(2,1)S(1)}, bf16[1,256,256]{2,1,0:T(8,128)(2,1)S(1)}, u32[]{:S(2)}, u32[]{:S(2)}) %collective-permute-start.12) | collective-permute-done | bytes 131104 | tf_op jit(solution)/shard_map/ppermute | solution.py:17
  54.2 2.0 %shard_map.68 = (bf16[2,256,256]{2,1,0:T(8,128)(2,1)S(1)}, bf16[2,256,256]{2,1,0:T(8,128)(2,1)S(1)}, bf16[2,256,256]{2,1,0:T(8,128)(2,1)S(1)}, bf16[2,256,256]{2,1,0:T(8,128)(2,1)S(1)}) custom-call(s32[2,8,8]{2,1,0:T(8,128)S(1)} %copy-done.1, s32[2,2,8]{2,1,0:T(2,128)S(1)} %copy-done.2, s32[2,2]{1,0:T(2,128)S(1)} %copy-done.3, ...), custom_call_target="tpu_custom_call" | custom-call | flops 603979776 | bytes 10093200 | tf_op jit(solution)/shard_map/pallas_call | solution.py:56
  56.1 3.3 %collective-permute-start.16 = (bf16[2,256,256]{2,1,0:T(8,128)(2,1)S(1)}, bf16[2,256,256]{2,1,0:T(8,128)(2,1)S(1)}, u32[]{:S(2)}, u32[]{:S(2)}) collective-permute-start(bf16[2,256,256]{2,1,0:T(8,128)(2,1)S(1)} %get-tuple-element.52), channel_id=1, source_target_pairs={{0,4},{4,0},{8,12},{12,8},{16,20},{20,16},{24,28},{28,24},{1,5},{5... | collective-permute-start | bytes 786440 | tf_op jit(solution)/shard_map/ppermute | solution.py:17
  59.5 2.0 %collective-permute-start.19 = (bf16[2,256,256]{2,1,0:T(8,128)(2,1)S(1)}, bf16[2,256,256]{2,1,0:T(8,128)(2,1)S(1)}, u32[]{:S(2)}, u32[]{:S(2)}) collective-permute-start(bf16[2,256,256]{2,1,0:T(8,128)(2,1)S(1)} %get-tuple-element.51.refs_12_.refs_22_), channel_id=1, source_target_pairs={{0,16},{4,20},{8,24},{12,28},{16,0},{20,4},{24,8},{28,12},{1,17},{... | collective-permute-start | bytes 786440 | tf_op jit(solution)/shard_map/ppermute | solution.py:17
  61.7 6.6 %collective-permute-done.23.far.refs_16_ = bf16[2,256,256]{2,1,0:T(8,128)(2,1)S(1)} collective-permute-done((bf16[2,256,256]{2,1,0:T(8,128)(2,1)S(1)}, bf16[2,256,256]{2,1,0:T(8,128)(2,1)S(1)}, u32[]{:S(2)}, u32[]{:S(2)}) %collective-permute-start.23) | collective-permute-done | bytes 262176 | tf_op jit(solution)/shard_map/ppermute | solution.py:17
  68.4 1.8 %collective-permute-start.24 = (bf16[1,256,256]{2,1,0:T(8,128)(2,1)S(1)}, bf16[1,256,256]{2,1,0:T(8,128)(2,1)S(1)}, u32[]{:S(2)}, u32[]{:S(2)}) collective-permute-start(bf16[1,256,256]{2,1,0:T(8,128)(2,1)S(1)} %get-tuple-element.58), channel_id=1, source_target_pairs={{0,4},{4,0},{8,12},{12,8},{16,20},{20,16},{24,28},{28,24},{1,5},{5... | collective-permute-start | bytes 393224 | tf_op jit(solution)/shard_map/ppermute | solution.py:17
  70.2 4.6 %collective-permute-done.17.refs_1_.refs_14_ = bf16[2,256,256]{2,1,0:T(8,128)(2,1)S(1)} collective-permute-done((bf16[2,256,256]{2,1,0:T(8,128)(2,1)S(1)}, bf16[2,256,256]{2,1,0:T(8,128)(2,1)S(1)}, u32[]{:S(2)}, u32[]{:S(2)}) %collective-permute-start.17) | collective-permute-done | bytes 262176 | tf_op jit(solution)/shard_map/ppermute | solution.py:17
  75.0 1.5 %collective-permute-start.20 = (bf16[1,256,256]{2,1,0:T(8,128)(2,1)S(1)}, bf16[1,256,256]{2,1,0:T(8,128)(2,1)S(1)}, u32[]{:S(2)}, u32[]{:S(2)}) collective-permute-start(bf16[1,256,256]{2,1,0:T(8,128)(2,1)S(1)} %get-tuple-element.55), channel_id=1, source_target_pairs={{0,4},{4,0},{8,12},{12,8},{16,20},{20,16},{24,28},{28,24},{1,5},{5... | collective-permute-start | bytes 393224 | tf_op jit(solution)/shard_map/ppermute | solution.py:17
  76.6 2.0 %collective-permute-start.21 = (bf16[1,256,256]{2,1,0:T(8,128)(2,1)S(1)}, bf16[1,256,256]{2,1,0:T(8,128)(2,1)S(1)}, u32[]{:S(2)}, u32[]{:S(2)}) collective-permute-start(bf16[1,256,256]{2,1,0:T(8,128)(2,1)S(1)} %get-tuple-element.56), channel_id=1, source_target_pairs={{0,8},{4,12},{8,0},{12,4},{16,24},{20,28},{24,16},{28,20},{1,9},{5... | collective-permute-start | bytes 393224 | tf_op jit(solution)/shard_map/ppermute | solution.py:17
  78.6 4.7 %collective-permute-done.25.refs_18_ = bf16[1,256,256]{2,1,0:T(8,128)(2,1)S(1)} collective-permute-done((bf16[1,256,256]{2,1,0:T(8,128)(2,1)S(1)}, bf16[1,256,256]{2,1,0:T(8,128)(2,1)S(1)}, u32[]{:S(2)}, u32[]{:S(2)}) %collective-permute-start.25) | collective-permute-done | bytes 131104 | tf_op jit(solution)/shard_map/ppermute | solution.py:17
  83.7 3.3 %collective-permute-done.26.refs_19_ = bf16[1,256,256]{2,1,0:T(8,128)(2,1)S(1)} collective-permute-done((bf16[1,256,256]{2,1,0:T(8,128)(2,1)S(1)}, bf16[1,256,256]{2,1,0:T(8,128)(2,1)S(1)}, u32[]{:S(2)}, u32[]{:S(2)}) %collective-permute-start.26) | collective-permute-done | bytes 131104 | tf_op jit(solution)/shard_map/ppermute | solution.py:17
  87.0 2.0 %shard_map.71.refs_23_ = bf16[2,256,256]{2,1,0:T(8,128)(2,1)S(1)} custom-call(s32[2,8,8]{2,1,0:T(8,128)S(1)} %copy-done.1, s32[2,2,8]{2,1,0:T(2,128)S(1)} %copy-done.2, s32[2,2]{1,0:T(2,128)S(1)} %copy-done.3, bf16[3,2,256,512]{3,2,1,0:T(8,128)(2,1)S(1)} %copy-done, bf16[2,256,256]{2,1,0:T(8,128)(2,1)S(1)} %get-tuple-element.43.inv, ...), custom_call_target="tpu_custom_call" | custom-call | flops 603979776 | bytes 10748560 | tf_op jit(solution)/shard_map/pallas_call | solution.py:56
  89.0 1.2 %collective-permute-done.22.refs_19_ = bf16[1,256,256]{2,1,0:T(8,128)(2,1)S(1)} collective-permute-done((bf16[1,256,256]{2,1,0:T(8,128)(2,1)S(1)}, bf16[1,256,256]{2,1,0:T(8,128)(2,1)S(1)}, u32[]{:S(2)}, u32[]{:S(2)}) %collective-permute-start.22) | collective-permute-done | bytes 131104 | tf_op jit(solution)/shard_map/ppermute | solution.py:17
  90.2 2.7 %shard_map.72 = bf16[3,2,256,512]{3,2,1,0:T(8,128)(2,1)} custom-call(s32[2,8,8]{2,1,0:T(8,128)S(1)} %copy-done.1, s32[2,2,8]{2,1,0:T(2,128)S(1)} %copy-done.2, s32[2,2]{1,0:T(2,128)S(1)} %copy-done.3, bf16[3,2,256,512]{3,2,1,0:T(8,128)(2,1)S(1)} %copy-done, bf16[2,256,256]{2,1,0:T(8,128)(2,1)S(1)} %get-tuple-element.43.inv, ...), custom_call_target="tpu_custom_call" | custom-call | flops 603979776 | bytes 13370000 | tf_op jit(solution)/shard_map/pallas_call | solution.py:56
  (43 shorter events, 6.6 us)
Async XLA Ops:
  0.9 5.8 %collective-permute-start.1 = (bf16[128,256]{1,0:T(8,128)(2,1)S(1)}, bf16[128,256]{1,0:T(8,128)(2,1)S(1)}, u32[]{:S(2)}, u32[]{:S(2)}) collective-permute-start(bf16[128,256]{1,0:T(8,128)(2,1)S(1)} %bitcast.7), channel_id=1, source_target_pairs={{0,1},{1,0},{2,3},{3,2},{4,5},{5,4},{6,7},{7,6},{8,9},{9,8},{10,11... | collective-permute-start | bytes 196616 | tf_op jit(solution)/shard_map/ppermute | solution.py:17
  1.4 5.3 %collective-permute-start = (bf16[128,256]{1,0:T(8,128)(2,1)S(1)}, bf16[128,256]{1,0:T(8,128)(2,1)S(1)}, u32[]{:S(2)}, u32[]{:S(2)}) collective-permute-start(bf16[128,256]{1,0:T(8,128)(2,1)S(1)} %bitcast.8), channel_id=1, source_target_pairs={{0,2},{1,3},{2,0},{3,1},{4,6},{5,7},{6,4},{7,5},{8,10},{9,11},{10,... | collective-permute-start | bytes 196616 | tf_op jit(solution)/shard_map/ppermute | solution.py:17
  5.3 1.4 %copy-start = (bf16[3,2,256,512]{3,2,1,0:T(8,128)(2,1)S(1)}, bf16[3,2,256,512]{3,2,1,0:T(8,128)(2,1)}, u32[]{:S(2)}) copy-start(bf16[3,2,256,512]{3,2,1,0:T(8,128)(2,1)} %noise.7) | copy-start | bytes 4718596
  5.3 2.7 %copy-start.1 = (s32[2,8,8]{2,1,0:T(8,128)S(1)}, s32[2,8,8]{2,1,0:T(8,128)}, u32[]{:S(2)}) copy-start(s32[2,8,8]{2,1,0:T(8,128)} %picks.15) | copy-start | bytes 1540
  6.7 1.3 %collective-permute-start.2 = (bf16[128,256]{1,0:T(8,128)(2,1)S(1)}, bf16[128,256]{1,0:T(8,128)(2,1)S(1)}, u32[]{:S(2)}, u32[]{:S(2)}) collective-permute-start(bf16[128,256]{1,0:T(8,128)(2,1)S(1)} %collective-permute-done.refs_1_), channel_id=1, source_target_pairs={{0,1},{1,0},{2,3},{3,2},{4,5},{5,4},{6,7},{7,6},{8,9},{9,8},{10,11... | collective-permute-start | bytes 196616 | tf_op jit(solution)/shard_map/ppermute | solution.py:17
  8.4 29.1 %collective-permute-start.7 = (bf16[2304,256]{1,0:T(8,128)(2,1)S(1)}, bf16[2304,256]{1,0:T(8,128)(2,1)S(1)}, u32[]{:S(2)}, u32[]{:S(2)}) collective-permute-start(bf16[2304,256]{1,0:T(8,128)(2,1)S(1)} %get-tuple-element.37.refs_3_), channel_id=1, source_target_pairs={{0,2},{1,3},{2,0},{3,1},{4,6},{5,7},{6,4},{7,5},{8,10},{9,11},{10,... | collective-permute-start | bytes 3538952 | tf_op jit(solution)/shard_map/ppermute | solution.py:17
  10.2 27.3 %collective-permute-start.3 = (bf16[2,256,512]{2,1,0:T(8,128)(2,1)S(1)}, bf16[2,256,512]{2,1,0:T(8,128)(2,1)S(1)}, u32[]{:S(2)}, u32[]{:S(2)}) collective-permute-start(bf16[2,256,512]{2,1,0:T(8,128)(2,1)S(1)} %get-tuple-element.33.refs_4_.refs_20_), channel_id=1, source_target_pairs={{0,16},{4,20},{8,24},{12,28},{16,0},{20,4},{24,8},{28,12},{1,17},{... | collective-permute-start | bytes 1572872 | tf_op jit(solution)/shard_map/ppermute | solution.py:17
  12.8 8.3 %collective-permute-start.4 = (bf16[1,256,512]{2,1,0:T(8,128)(2,1)S(1)}, bf16[1,256,512]{2,1,0:T(8,128)(2,1)S(1)}, u32[]{:S(2)}, u32[]{:S(2)}) collective-permute-start(bf16[1,256,512]{2,1,0:T(8,128)(2,1)S(1)} %get-tuple-element.34), channel_id=1, source_target_pairs={{0,4},{4,0},{8,12},{12,8},{16,20},{20,16},{24,28},{28,24},{1,5},{5... | collective-permute-start | bytes 786440 | tf_op jit(solution)/shard_map/ppermute | solution.py:17
  14.3 16.5 %collective-permute-start.5 = (bf16[1,256,512]{2,1,0:T(8,128)(2,1)S(1)}, bf16[1,256,512]{2,1,0:T(8,128)(2,1)S(1)}, u32[]{:S(2)}, u32[]{:S(2)}) collective-permute-start(bf16[1,256,512]{2,1,0:T(8,128)(2,1)S(1)} %get-tuple-element.35), channel_id=1, source_target_pairs={{0,8},{4,12},{8,0},{12,4},{16,24},{20,28},{24,16},{28,20},{1,9},{5... | collective-permute-start | bytes 786440 | tf_op jit(solution)/shard_map/ppermute | solution.py:17
  15.9 21.6 %collective-permute-start.6 = (bf16[1,256,512]{2,1,0:T(8,128)(2,1)S(1)}, bf16[1,256,512]{2,1,0:T(8,128)(2,1)S(1)}, u32[]{:S(2)}, u32[]{:S(2)}) collective-permute-start(bf16[1,256,512]{2,1,0:T(8,128)(2,1)S(1)} %get-tuple-element.36), channel_id=1, source_target_pairs={{0,12},{4,8},{8,4},{12,0},{16,28},{20,24},{24,20},{28,16},{1,13},{... | collective-permute-start | bytes 786440 | tf_op jit(solution)/shard_map/ppermute | solution.py:17
  37.7 4.1 %collective-permute-start.8 = (bf16[2304,256]{1,0:T(8,128)(2,1)S(1)}, bf16[2304,256]{1,0:T(8,128)(2,1)S(1)}, u32[]{:S(2)}, u32[]{:S(2)}) collective-permute-start(bf16[2304,256]{1,0:T(8,128)(2,1)S(1)} %get-tuple-element.38.refs_0_), channel_id=1, source_target_pairs={{0,1},{1,0},{2,3},{3,2},{4,5},{5,4},{6,7},{7,6},{8,9},{9,8},{10,11... | collective-permute-start | bytes 3538952 | tf_op jit(solution)/shard_map/ppermute | solution.py:17
  37.8 4.5 %collective-permute-start.9 = (bf16[2304,256]{1,0:T(8,128)(2,1)S(1)}, bf16[2304,256]{1,0:T(8,128)(2,1)S(1)}, u32[]{:S(2)}, u32[]{:S(2)}) collective-permute-start(bf16[2304,256]{1,0:T(8,128)(2,1)S(1)} %get-tuple-element.39.refs_1_), channel_id=1, source_target_pairs={{0,1},{1,0},{2,3},{3,2},{4,5},{5,4},{6,7},{7,6},{8,9},{9,8},{10,11... | collective-permute-start | bytes 3538952 | tf_op jit(solution)/shard_map/ppermute | solution.py:17
  38.3 6.4 %collective-permute-start.13 = (bf16[1,256,256]{2,1,0:T(8,128)(2,1)S(1)}, bf16[1,256,256]{2,1,0:T(8,128)(2,1)S(1)}, u32[]{:S(2)}, u32[]{:S(2)}) collective-permute-start(bf16[1,256,256]{2,1,0:T(8,128)(2,1)S(1)} %get-tuple-element.48), channel_id=1, source_target_pairs={{0,4},{4,0},{8,12},{12,8},{16,20},{20,16},{24,28},{28,24},{1,5},{5... | collective-permute-start | bytes 393224 | tf_op jit(solution)/shard_map/ppermute | solution.py:17
  39.8 6.4 %collective-permute-start.14 = (bf16[1,256,256]{2,1,0:T(8,128)(2,1)S(1)}, bf16[1,256,256]{2,1,0:T(8,128)(2,1)S(1)}, u32[]{:S(2)}, u32[]{:S(2)}) collective-permute-start(bf16[1,256,256]{2,1,0:T(8,128)(2,1)S(1)} %get-tuple-element.49), channel_id=1, source_target_pairs={{0,8},{4,12},{8,0},{12,4},{16,24},{20,28},{24,16},{28,20},{1,9},{5... | collective-permute-start | bytes 393224 | tf_op jit(solution)/shard_map/ppermute | solution.py:17
  40.6 8.4 %collective-permute-start.15 = (bf16[1,256,256]{2,1,0:T(8,128)(2,1)S(1)}, bf16[1,256,256]{2,1,0:T(8,128)(2,1)S(1)}, u32[]{:S(2)}, u32[]{:S(2)}) collective-permute-start(bf16[1,256,256]{2,1,0:T(8,128)(2,1)S(1)} %get-tuple-element.50), channel_id=1, source_target_pairs={{0,12},{4,8},{8,4},{12,0},{16,28},{20,24},{24,20},{28,16},{1,13},{... | collective-permute-start | bytes 393224 | tf_op jit(solution)/shard_map/ppermute | solution.py:17
  42.3 6.6 %copy-start.2 = (s32[2,2,8]{2,1,0:T(2,128)S(1)}, s32[2,2,8]{2,1,0:T(2,128)}, u32[]{:S(2)}) copy-start(s32[2,2,8]{2,1,0:T(2,128)} %lists.7) | copy-start | bytes 388
  42.3 6.6 %copy-start.3 = (s32[2,2]{1,0:T(2,128)S(1)}, s32[2,2]{1,0:T(2,128)}, u32[]{:S(2)}) copy-start(s32[2,2]{1,0:T(2,128)} %counts.7) | copy-start | bytes 52
  42.3 10.2 %collective-permute-start.10 = (bf16[1,256,256]{2,1,0:T(8,128)(2,1)S(1)}, bf16[1,256,256]{2,1,0:T(8,128)(2,1)S(1)}, u32[]{:S(2)}, u32[]{:S(2)}) collective-permute-start(bf16[1,256,256]{2,1,0:T(8,128)(2,1)S(1)} %get-tuple-element.44), channel_id=1, source_target_pairs={{0,4},{4,0},{8,12},{12,8},{16,20},{20,16},{24,28},{28,24},{1,5},{5... | collective-permute-start | bytes 393224 | tf_op jit(solution)/shard_map/ppermute | solution.py:17
  43.9 8.6 %collective-permute-start.11 = (bf16[1,256,256]{2,1,0:T(8,128)(2,1)S(1)}, bf16[1,256,256]{2,1,0:T(8,128)(2,1)S(1)}, u32[]{:S(2)}, u32[]{:S(2)}) collective-permute-start(bf16[1,256,256]{2,1,0:T(8,128)(2,1)S(1)} %get-tuple-element.45), channel_id=1, source_target_pairs={{0,8},{4,12},{8,0},{12,4},{16,24},{20,28},{24,16},{28,20},{1,9},{5... | collective-permute-start | bytes 393224 | tf_op jit(solution)/shard_map/ppermute | solution.py:17
  44.7 9.4 %collective-permute-start.12 = (bf16[1,256,256]{2,1,0:T(8,128)(2,1)S(1)}, bf16[1,256,256]{2,1,0:T(8,128)(2,1)S(1)}, u32[]{:S(2)}, u32[]{:S(2)}) collective-permute-start(bf16[1,256,256]{2,1,0:T(8,128)(2,1)S(1)} %get-tuple-element.46), channel_id=1, source_target_pairs={{0,12},{4,8},{8,4},{12,0},{16,28},{20,24},{24,20},{28,16},{1,13},{... | collective-permute-start | bytes 393224 | tf_op jit(solution)/shard_map/ppermute | solution.py:17
  50.9 17.4 %collective-permute-start.23 = (bf16[2,256,256]{2,1,0:T(8,128)(2,1)S(1)}, bf16[2,256,256]{2,1,0:T(8,128)(2,1)S(1)}, u32[]{:S(2)}, u32[]{:S(2)}) collective-permute-start(bf16[2,256,256]{2,1,0:T(8,128)(2,1)S(1)} %shard_map.67.refs_12_.refs_21_), channel_id=1, source_target_pairs={{0,16},{4,20},{8,24},{12,28},{16,0},{20,4},{24,8},{28,12},{1,17},{... | collective-permute-start | bytes 786440 | tf_op jit(solution)/shard_map/ppermute | solution.py:17
  56.1 14.1 %collective-permute-start.16 = (bf16[2,256,256]{2,1,0:T(8,128)(2,1)S(1)}, bf16[2,256,256]{2,1,0:T(8,128)(2,1)S(1)}, u32[]{:S(2)}, u32[]{:S(2)}) collective-permute-start(bf16[2,256,256]{2,1,0:T(8,128)(2,1)S(1)} %get-tuple-element.52), channel_id=1, source_target_pairs={{0,4},{4,0},{8,12},{12,8},{16,20},{20,16},{24,28},{28,24},{1,5},{5... | collective-permute-start | bytes 786440 | tf_op jit(solution)/shard_map/ppermute | solution.py:17
  59.5 15.4 %collective-permute-start.17 = (bf16[2,256,256]{2,1,0:T(8,128)(2,1)S(1)}, bf16[2,256,256]{2,1,0:T(8,128)(2,1)S(1)}, u32[]{:S(2)}, u32[]{:S(2)}) collective-permute-start(bf16[2,256,256]{2,1,0:T(8,128)(2,1)S(1)} %get-tuple-element.53), channel_id=1, source_target_pairs={{0,8},{4,12},{8,0},{12,4},{16,24},{20,28},{24,16},{28,20},{1,9},{5... | collective-permute-start | bytes 786440 | tf_op jit(solution)/shard_map/ppermute | solution.py:17
  59.5 15.4 %collective-permute-start.19 = (bf16[2,256,256]{2,1,0:T(8,128)(2,1)S(1)}, bf16[2,256,256]{2,1,0:T(8,128)(2,1)S(1)}, u32[]{:S(2)}, u32[]{:S(2)}) collective-permute-start(bf16[2,256,256]{2,1,0:T(8,128)(2,1)S(1)} %get-tuple-element.51.refs_12_.refs_22_), channel_id=1, source_target_pairs={{0,16},{4,20},{8,24},{12,28},{16,0},{20,4},{24,8},{28,12},{1,17},{... | collective-permute-start | bytes 786440 | tf_op jit(solution)/shard_map/ppermute | solution.py:17
  61.4 25.6 %collective-permute-start.18 = (bf16[2,256,256]{2,1,0:T(8,128)(2,1)S(1)}, bf16[2,256,256]{2,1,0:T(8,128)(2,1)S(1)}, u32[]{:S(2)}, u32[]{:S(2)}) collective-permute-start(bf16[2,256,256]{2,1,0:T(8,128)(2,1)S(1)} %get-tuple-element.54), channel_id=1, source_target_pairs={{0,12},{4,8},{8,4},{12,0},{16,28},{20,24},{24,20},{28,16},{1,13},{... | collective-permute-start | bytes 786440 | tf_op jit(solution)/shard_map/ppermute | solution.py:17
  68.4 8.1 %collective-permute-start.24 = (bf16[1,256,256]{2,1,0:T(8,128)(2,1)S(1)}, bf16[1,256,256]{2,1,0:T(8,128)(2,1)S(1)}, u32[]{:S(2)}, u32[]{:S(2)}) collective-permute-start(bf16[1,256,256]{2,1,0:T(8,128)(2,1)S(1)} %get-tuple-element.58), channel_id=1, source_target_pairs={{0,4},{4,0},{8,12},{12,8},{16,20},{20,16},{24,28},{28,24},{1,5},{5... | collective-permute-start | bytes 393224 | tf_op jit(solution)/shard_map/ppermute | solution.py:17
  70.2 13.1 %collective-permute-start.25 = (bf16[1,256,256]{2,1,0:T(8,128)(2,1)S(1)}, bf16[1,256,256]{2,1,0:T(8,128)(2,1)S(1)}, u32[]{:S(2)}, u32[]{:S(2)}) collective-permute-start(bf16[1,256,256]{2,1,0:T(8,128)(2,1)S(1)} %get-tuple-element.59), channel_id=1, source_target_pairs={{0,8},{4,12},{8,0},{12,4},{16,24},{20,28},{24,16},{28,20},{1,9},{5... | collective-permute-start | bytes 393224 | tf_op jit(solution)/shard_map/ppermute | solution.py:17
  74.8 12.1 %collective-permute-start.26 = (bf16[1,256,256]{2,1,0:T(8,128)(2,1)S(1)}, bf16[1,256,256]{2,1,0:T(8,128)(2,1)S(1)}, u32[]{:S(2)}, u32[]{:S(2)}) collective-permute-start(bf16[1,256,256]{2,1,0:T(8,128)(2,1)S(1)} %get-tuple-element.60), channel_id=1, source_target_pairs={{0,12},{4,8},{8,4},{12,0},{16,28},{20,24},{24,20},{28,16},{1,13},{... | collective-permute-start | bytes 393224 | tf_op jit(solution)/shard_map/ppermute | solution.py:17
  75.0 14.0 %collective-permute-start.20 = (bf16[1,256,256]{2,1,0:T(8,128)(2,1)S(1)}, bf16[1,256,256]{2,1,0:T(8,128)(2,1)S(1)}, u32[]{:S(2)}, u32[]{:S(2)}) collective-permute-start(bf16[1,256,256]{2,1,0:T(8,128)(2,1)S(1)} %get-tuple-element.55), channel_id=1, source_target_pairs={{0,4},{4,0},{8,12},{12,8},{16,20},{20,16},{24,28},{28,24},{1,5},{5... | collective-permute-start | bytes 393224 | tf_op jit(solution)/shard_map/ppermute | solution.py:17
  76.6 12.4 %collective-permute-start.21 = (bf16[1,256,256]{2,1,0:T(8,128)(2,1)S(1)}, bf16[1,256,256]{2,1,0:T(8,128)(2,1)S(1)}, u32[]{:S(2)}, u32[]{:S(2)}) collective-permute-start(bf16[1,256,256]{2,1,0:T(8,128)(2,1)S(1)} %get-tuple-element.56), channel_id=1, source_target_pairs={{0,8},{4,12},{8,0},{12,4},{16,24},{20,28},{24,16},{28,20},{1,9},{5... | collective-permute-start | bytes 393224 | tf_op jit(solution)/shard_map/ppermute | solution.py:17
  83.3 6.9 %collective-permute-start.22 = (bf16[1,256,256]{2,1,0:T(8,128)(2,1)S(1)}, bf16[1,256,256]{2,1,0:T(8,128)(2,1)S(1)}, u32[]{:S(2)}, u32[]{:S(2)}) collective-permute-start(bf16[1,256,256]{2,1,0:T(8,128)(2,1)S(1)} %get-tuple-element.57), channel_id=1, source_target_pairs={{0,12},{4,8},{8,4},{12,0},{16,28},{20,24},{24,20},{28,16},{1,13},{... | collective-permute-start | bytes 393224 | tf_op jit(solution)/shard_map/ppermute | solution.py:17

commit v28 on v27

--- a/solution.py
+++ b/solution.py
@@ -236,8 +236,7 @@
         last_level = level == levels - 1
         solved, sends = [], []
         for at in chunks:
-            ends = at == CHUNKS - 1 and not last_level
-            sides, mates = (half - 1, list(solved)) if ends else (0, [])
+            sides, mates = 0 if last_level else half - 1, []
             final = last_level and at == CHUNKS - 1
             known = [entry for below in range(level) for entry in pieces[below][at]]
             stored = done if final else []
@@ -252,7 +251,7 @@
                     level_kernel, level, owners, steps, width, at,
                     [place for _, place in known], [place for _, place in stored], sides, len(mates),
                 ),
-                [shape(*noise.shape) if final else part] + [shape(CHUNKS, rows, wide)] * sides,
+                [shape(*noise.shape) if final else part] + [shape(1, rows, wide)] * sides,
                 scratch,
                 (picks, lists, counts, noise, inverses[level - 1], *packs, *(ref for ref, _ in known), *(ref for ref, _ in stored), *mates),
                 out_spec=ANY if final else VMEM,
@@ -260,14 +259,14 @@
             )
             solved.append(here)
             done.append((here, (level, at * wide)))
-            sends += sent
+            sends.append(sent)
         if last_level:
             return here
         far = [leaf(value, half) for value in solved]
-        got = near(sends)
+        got = [near(sent) for sent in sends]
         pieces.append([])
         for at in chunks:
-            waits = got[:half // 2] if at == CHUNKS - 1 else []
+            waits = got[0] if at == 0 else got[1][:half // 2]
             sends = call(
                 functools.partial(relay_kernel, half, level, len(waits), 0),
                 [shape(1, rows, wide)] * (half - 1),
@@ -275,7 +274,7 @@
                 (picks, far[at], *waits),
             )
             pieces[level].append([
-                (solved[at], 0), *((ref, at) for ref in got),
+                (solved[at], 0), *((ref, 0) for ref in got[at]),
                 (far[at], 0), *((ref, 0) for ref in near(sends)),
             ])
 

time: 93.1 us -> 90.2 us (0.969)
  waiting for transfers between devices: 49.3 us -> 36.9 us
  starting transfers between devices: 31.6 us -> 41.1 us
    ppermute x27 -> x30, waiting for transfers between devices: 49.3 us -> 36.9 us  [hop(): return lax.ppermute(value, axis, [(at, at ^ step) for at in range(size)])]
    ppermute x27 -> x30, starting transfers between devices: 31.6 us -> 41.1 us  [hop(): return lax.ppermute(value, axis, [(at, at ^ step) for at in range(size)])]
  transfers between devices with their start and end apart: 27 -> 30, of which waited for: 14 -> 17; matrix products, arithmetic and copies ran while one was open for 1% -> 2% of each run, Pallas kernels for 7% -> 7%
where the time goes in v28:
time: 90.2 us; the launch traced here: 90 us
  starting transfers between devices  41.1 us (46%)
  waiting for transfers between devices  36.9 us (41%)
  Pallas kernels  9.53 us (11%)
  local copies, waits for them, and re-layouts  2.24 us (2%)
    ppermute x30, starting transfers between devices, hop(): return lax.ppermute(value, axis, [(at, at ^ step) for at in range(size)])  41.1 us
    ppermute x30, waiting for transfers between devices, hop(): return lax.ppermute(value, axis, [(at, at ^ step) for at in range(size)])  36.9 us
    pallas_call x9, Pallas kernels, call(): pl.pallas_call(kernel, out_shape=outs, in_specs=[VMEM] * len(arrays), out...  9.53 us
  transfers between devices with their start and end apart: 30, of which 17 were waited for; matrix products, arithmetic and copies ran while one was open for 2% of the time, Pallas kernels for 7%

profile of v28, /device:TPU:0, one launch (start us, length us, event | category | flops | bytes accessed | tf_op | source)
XLA Modules:
  0.0 90.0 jit_solution(7972655162456760224)
XLA Ops:
  1.4 2.6 %collective-permute-start = (bf16[128,256]{1,0:T(8,128)(2,1)S(1)}, bf16[128,256]{1,0:T(8,128)(2,1)S(1)}, u32[]{:S(2)}, u32[]{:S(2)}) collective-permute-start(bf16[128,256]{1,0:T(8,128)(2,1)S(1)} %bitcast.8), channel_id=1, source_target_pairs={{0,2},{1,3},{2,0},{3,1},{4,6},{5,7},{6,4},{7,5},{8,10},{9,11},{10,... | collective-permute-start | bytes 196616 | tf_op jit(solution)/shard_map/ppermute | solution.py:17
  4.0 1.3 %fusion = (bf16[1,2,2,256,256]{4,3,2,1,0:T(8,128)(2,1)S(1)}, bf16[1,2,2,256,256]{4,3,2,1,0:T(8,128)(2,1)S(1)}) fusion(bf16[2,2,2,256,256]{4,3,2,1,0:T(8,128)(2,1)} %param.8), kind=kLoop, calls=%fused_computation.2 | loop fusion | bytes 2097152 | tf_op jit(solution)/shard_map/slice | solution.py:193
  5.4 1.3 %collective-permute-done.refs_1_ = bf16[128,256]{1,0:T(8,128)(2,1)S(1)} collective-permute-done((bf16[128,256]{1,0:T(8,128)(2,1)S(1)}, bf16[128,256]{1,0:T(8,128)(2,1)S(1)}, u32[]{:S(2)}, u32[]{:S(2)}) %collective-permute-start) | collective-permute-done | bytes 65568 | tf_op jit(solution)/shard_map/ppermute | solution.py:17
  6.7 1.2 %collective-permute-done.2.refs_3_ = bf16[128,256]{1,0:T(8,128)(2,1)S(1)} collective-permute-done((bf16[128,256]{1,0:T(8,128)(2,1)S(1)}, bf16[128,256]{1,0:T(8,128)(2,1)S(1)}, u32[]{:S(2)}, u32[]{:S(2)}) %collective-permute-start.2) | collective-permute-done | bytes 65568 | tf_op jit(solution)/shard_map/ppermute | solution.py:17
  8.4 1.8 %collective-permute-start.7 = (bf16[2304,256]{1,0:T(8,128)(2,1)S(1)}, bf16[2304,256]{1,0:T(8,128)(2,1)S(1)}, u32[]{:S(2)}, u32[]{:S(2)}) collective-permute-start(bf16[2304,256]{1,0:T(8,128)(2,1)S(1)} %get-tuple-element.41.refs_3_), channel_id=1, source_target_pairs={{0,2},{1,3},{2,0},{3,1},{4,6},{5,7},{6,4},{7,5},{8,10},{9,11},{10,... | collective-permute-start | bytes 3538952 | tf_op jit(solution)/shard_map/ppermute | solution.py:17
  10.2 2.6 %collective-permute-start.3 = (bf16[2,256,512]{2,1,0:T(8,128)(2,1)S(1)}, bf16[2,256,512]{2,1,0:T(8,128)(2,1)S(1)}, u32[]{:S(2)}, u32[]{:S(2)}) collective-permute-start(bf16[2,256,512]{2,1,0:T(8,128)(2,1)S(1)} %get-tuple-element.37.refs_4_.refs_20_), channel_id=1, source_target_pairs={{0,16},{4,20},{8,24},{12,28},{16,0},{20,4},{24,8},{28,12},{1,17},{... | collective-permute-start | bytes 1572872 | tf_op jit(solution)/shard_map/ppermute | solution.py:17
  12.8 1.5 %collective-permute-start.4 = (bf16[1,256,512]{2,1,0:T(8,128)(2,1)S(1)}, bf16[1,256,512]{2,1,0:T(8,128)(2,1)S(1)}, u32[]{:S(2)}, u32[]{:S(2)}) collective-permute-start(bf16[1,256,512]{2,1,0:T(8,128)(2,1)S(1)} %get-tuple-element.38), channel_id=1, source_target_pairs={{0,4},{4,0},{8,12},{12,8},{16,20},{20,16},{24,28},{28,24},{1,5},{5... | collective-permute-start | bytes 786440 | tf_op jit(solution)/shard_map/ppermute | solution.py:17
  14.3 1.6 %collective-permute-start.5 = (bf16[1,256,512]{2,1,0:T(8,128)(2,1)S(1)}, bf16[1,256,512]{2,1,0:T(8,128)(2,1)S(1)}, u32[]{:S(2)}, u32[]{:S(2)}) collective-permute-start(bf16[1,256,512]{2,1,0:T(8,128)(2,1)S(1)} %get-tuple-element.39), channel_id=1, source_target_pairs={{0,8},{4,12},{8,0},{12,4},{16,24},{20,28},{24,16},{28,20},{1,9},{5... | collective-permute-start | bytes 786440 | tf_op jit(solution)/shard_map/ppermute | solution.py:17
  16.3 4.9 %collective-permute-done.4.refs_0_.refs_5_ = bf16[1,256,512]{2,1,0:T(8,128)(2,1)S(1)} collective-permute-done((bf16[1,256,512]{2,1,0:T(8,128)(2,1)S(1)}, bf16[1,256,512]{2,1,0:T(8,128)(2,1)S(1)}, u32[]{:S(2)}, u32[]{:S(2)}) %collective-permute-start.4) | collective-permute-done | bytes 262176 | tf_op jit(solution)/shard_map/ppermute | solution.py:17
  21.1 9.6 %collective-permute-done.5.refs_1_.refs_6_ = bf16[1,256,512]{2,1,0:T(8,128)(2,1)S(1)} collective-permute-done((bf16[1,256,512]{2,1,0:T(8,128)(2,1)S(1)}, bf16[1,256,512]{2,1,0:T(8,128)(2,1)S(1)}, u32[]{:S(2)}, u32[]{:S(2)}) %collective-permute-start.5) | collective-permute-done | bytes 262176 | tf_op jit(solution)/shard_map/ppermute | solution.py:17
  30.8 6.7 %collective-permute-done.6.refs_2_.refs_7_ = bf16[1,256,512]{2,1,0:T(8,128)(2,1)S(1)} collective-permute-done((bf16[1,256,512]{2,1,0:T(8,128)(2,1)S(1)}, bf16[1,256,512]{2,1,0:T(8,128)(2,1)S(1)}, u32[]{:S(2)}, u32[]{:S(2)}) %collective-permute-start.6) | collective-permute-done | bytes 262176 | tf_op jit(solution)/shard_map/ppermute | solution.py:17
  38.3 1.5 %collective-permute-start.20 = (bf16[1,256,256]{2,1,0:T(8,128)(2,1)S(1)}, bf16[1,256,256]{2,1,0:T(8,128)(2,1)S(1)}, u32[]{:S(2)}, u32[]{:S(2)}) collective-permute-start(bf16[1,256,256]{2,1,0:T(8,128)(2,1)S(1)} %get-tuple-element.59), channel_id=1, source_target_pairs={{0,4},{4,0},{8,12},{12,8},{16,20},{20,16},{24,28},{28,24},{1,5},{5... | collective-permute-start | bytes 393224 | tf_op jit(solution)/shard_map/ppermute | solution.py:17
  42.3 1.6 %collective-permute-start.10 = (bf16[1,256,256]{2,1,0:T(8,128)(2,1)S(1)}, bf16[1,256,256]{2,1,0:T(8,128)(2,1)S(1)}, u32[]{:S(2)}, u32[]{:S(2)}) collective-permute-start(bf16[1,256,256]{2,1,0:T(8,128)(2,1)S(1)} %get-tuple-element.48), channel_id=1, source_target_pairs={{0,4},{4,0},{8,12},{12,8},{16,20},{20,16},{24,28},{28,24},{1,5},{5... | collective-permute-start | bytes 393224 | tf_op jit(solution)/shard_map/ppermute | solution.py:17
  46.2 2.8 %collective-permute-done.22.refs_11_ = bf16[1,256,256]{2,1,0:T(8,128)(2,1)S(1)} collective-permute-done((bf16[1,256,256]{2,1,0:T(8,128)(2,1)S(1)}, bf16[1,256,256]{2,1,0:T(8,128)(2,1)S(1)}, u32[]{:S(2)}, u32[]{:S(2)}) %collective-permute-start.22) | collective-permute-done | bytes 131104 | tf_op jit(solution)/shard_map/ppermute | solution.py:17
  48.9 2.0 %shard_map.69 = (bf16[2,256,256]{2,1,0:T(8,128)(2,1)S(1)}, bf16[1,256,256]{2,1,0:T(8,128)(2,1)S(1)}, bf16[1,256,256]{2,1,0:T(8,128)(2,1)S(1)}, bf16[1,256,256]{2,1,0:T(8,128)(2,1)S(1)}) custom-call(s32[2,8,8]{2,1,0:T(8,128)S(1)} %copy-done.1, s32[2,2,8]{2,1,0:T(2,128)S(1)} %copy-done.2, s32[2,2]{1,0:T(2,128)S(1)} %copy-done.3, ...), custom_call_target="tpu_custom_call" | custom-call | flops 603979776 | bytes 9437840 | tf_op jit(solution)/shard_map/pallas_call | solution.py:56
  50.9 1.7 %collective-permute-start.26 = (bf16[2,256,256]{2,1,0:T(8,128)(2,1)S(1)}, bf16[2,256,256]{2,1,0:T(8,128)(2,1)S(1)}, u32[]{:S(2)}, u32[]{:S(2)}) collective-permute-start(bf16[2,256,256]{2,1,0:T(8,128)(2,1)S(1)} %get-tuple-element.62.refs_12_.refs_21_), channel_id=1, source_target_pairs={{0,16},{4,20},{8,24},{12,28},{16,0},{20,4},{24,8},{28,12},{1,17},{... | collective-permute-start | bytes 786440 | tf_op jit(solution)/shard_map/ppermute | solution.py:17
  52.6 1.7 %collective-permute-start.23 = (bf16[1,256,256]{2,1,0:T(8,128)(2,1)S(1)}, bf16[1,256,256]{2,1,0:T(8,128)(2,1)S(1)}, u32[]{:S(2)}, u32[]{:S(2)}) collective-permute-start(bf16[1,256,256]{2,1,0:T(8,128)(2,1)S(1)} %get-tuple-element.63), channel_id=1, source_target_pairs={{0,4},{4,0},{8,12},{12,8},{16,20},{20,16},{24,28},{28,24},{1,5},{5... | collective-permute-start | bytes 393224 | tf_op jit(solution)/shard_map/ppermute | solution.py:17
  54.3 1.6 %collective-permute-start.24 = (bf16[1,256,256]{2,1,0:T(8,128)(2,1)S(1)}, bf16[1,256,256]{2,1,0:T(8,128)(2,1)S(1)}, u32[]{:S(2)}, u32[]{:S(2)}) collective-permute-start(bf16[1,256,256]{2,1,0:T(8,128)(2,1)S(1)} %get-tuple-element.64), channel_id=1, source_target_pairs={{0,8},{4,12},{8,0},{12,4},{16,24},{20,28},{24,16},{28,20},{1,9},{5... | collective-permute-start | bytes 393224 | tf_op jit(solution)/shard_map/ppermute | solution.py:17
  56.1 2.0 %shard_map.67 = (bf16[2,256,256]{2,1,0:T(8,128)(2,1)S(1)}, bf16[1,256,256]{2,1,0:T(8,128)(2,1)S(1)}, bf16[1,256,256]{2,1,0:T(8,128)(2,1)S(1)}, bf16[1,256,256]{2,1,0:T(8,128)(2,1)S(1)}) custom-call(s32[2,8,8]{2,1,0:T(8,128)S(1)} %copy-done.1, s32[2,2,8]{2,1,0:T(2,128)S(1)} %copy-done.2, s32[2,2]{1,0:T(2,128)S(1)} %copy-done.3, ...), custom_call_target="tpu_custom_call" | custom-call | flops 603979776 | bytes 9437840 | tf_op jit(solution)/shard_map/pallas_call | solution.py:56
  58.1 1.4 %collective-permute-start.16 = (bf16[2,256,256]{2,1,0:T(8,128)(2,1)S(1)}, bf16[2,256,256]{2,1,0:T(8,128)(2,1)S(1)}, u32[]{:S(2)}, u32[]{:S(2)}) collective-permute-start(bf16[2,256,256]{2,1,0:T(8,128)(2,1)S(1)} %get-tuple-element.52.refs_12_.refs_22_), channel_id=1, source_target_pairs={{0,16},{4,20},{8,24},{12,28},{16,0},{20,4},{24,8},{28,12},{1,17},{... | collective-permute-start | bytes 786440 | tf_op jit(solution)/shard_map/ppermute | solution.py:17
  59.4 1.5 %collective-permute-start.13 = (bf16[1,256,256]{2,1,0:T(8,128)(2,1)S(1)}, bf16[1,256,256]{2,1,0:T(8,128)(2,1)S(1)}, u32[]{:S(2)}, u32[]{:S(2)}) collective-permute-start(bf16[1,256,256]{2,1,0:T(8,128)(2,1)S(1)} %get-tuple-element.53), channel_id=1, source_target_pairs={{0,4},{4,0},{8,12},{12,8},{16,20},{20,16},{24,28},{28,24},{1,5},{5... | collective-permute-start | bytes 393224 | tf_op jit(solution)/shard_map/ppermute | solution.py:17
  61.0 1.2 %collective-permute-done.24.refs_1_.refs_14_ = bf16[1,256,256]{2,1,0:T(8,128)(2,1)S(1)} collective-permute-done((bf16[1,256,256]{2,1,0:T(8,128)(2,1)S(1)}, bf16[1,256,256]{2,1,0:T(8,128)(2,1)S(1)}, u32[]{:S(2)}, u32[]{:S(2)}) %collective-permute-start.24) | collective-permute-done | bytes 131104 | tf_op jit(solution)/shard_map/ppermute | solution.py:17
  62.2 2.5 %collective-permute-start.14 = (bf16[1,256,256]{2,1,0:T(8,128)(2,1)S(1)}, bf16[1,256,256]{2,1,0:T(8,128)(2,1)S(1)}, u32[]{:S(2)}, u32[]{:S(2)}) collective-permute-start(bf16[1,256,256]{2,1,0:T(8,128)(2,1)S(1)} %get-tuple-element.54), channel_id=1, source_target_pairs={{0,8},{4,12},{8,0},{12,4},{16,24},{20,28},{24,16},{28,20},{1,9},{5... | collective-permute-start | bytes 393224 | tf_op jit(solution)/shard_map/ppermute | solution.py:17
  64.6 2.0 %collective-permute-done.25.refs_2_.refs_15_ = bf16[1,256,256]{2,1,0:T(8,128)(2,1)S(1)} collective-permute-done((bf16[1,256,256]{2,1,0:T(8,128)(2,1)S(1)}, bf16[1,256,256]{2,1,0:T(8,128)(2,1)S(1)}, u32[]{:S(2)}, u32[]{:S(2)}) %collective-permute-start.25) | collective-permute-done | bytes 131104 | tf_op jit(solution)/shard_map/ppermute | solution.py:17
  67.3 3.3 %collective-permute-start.27 = (bf16[1,256,256]{2,1,0:T(8,128)(2,1)S(1)}, bf16[1,256,256]{2,1,0:T(8,128)(2,1)S(1)}, u32[]{:S(2)}, u32[]{:S(2)}) collective-permute-start(bf16[1,256,256]{2,1,0:T(8,128)(2,1)S(1)} %get-tuple-element.66), channel_id=1, source_target_pairs={{0,4},{4,0},{8,12},{12,8},{16,20},{20,16},{24,28},{28,24},{1,5},{5... | collective-permute-start | bytes 393224 | tf_op jit(solution)/shard_map/ppermute | solution.py:17
  70.6 1.5 %collective-permute-start.29 = (bf16[1,256,256]{2,1,0:T(8,128)(2,1)S(1)}, bf16[1,256,256]{2,1,0:T(8,128)(2,1)S(1)}, u32[]{:S(2)}, u32[]{:S(2)}) collective-permute-start(bf16[1,256,256]{2,1,0:T(8,128)(2,1)S(1)} %get-tuple-element.68), channel_id=1, source_target_pairs={{0,12},{4,8},{8,4},{12,0},{16,28},{20,24},{24,20},{28,16},{1,13},{... | collective-permute-start | bytes 393224 | tf_op jit(solution)/shard_map/ppermute | solution.py:17
  72.2 1.3 %collective-permute-done.14.refs_1_.refs_14_ = bf16[1,256,256]{2,1,0:T(8,128)(2,1)S(1)} collective-permute-done((bf16[1,256,256]{2,1,0:T(8,128)(2,1)S(1)}, bf16[1,256,256]{2,1,0:T(8,128)(2,1)S(1)}, u32[]{:S(2)}, u32[]{:S(2)}) %collective-permute-start.14) | collective-permute-done | bytes 131104 | tf_op jit(solution)/shard_map/ppermute | solution.py:17
  73.4 3.6 %collective-permute-start.15 = (bf16[1,256,256]{2,1,0:T(8,128)(2,1)S(1)}, bf16[1,256,256]{2,1,0:T(8,128)(2,1)S(1)}, u32[]{:S(2)}, u32[]{:S(2)}) collective-permute-start(bf16[1,256,256]{2,1,0:T(8,128)(2,1)S(1)} %get-tuple-element.55), channel_id=1, source_target_pairs={{0,12},{4,8},{8,4},{12,0},{16,28},{20,24},{24,20},{28,16},{1,13},{... | collective-permute-start | bytes 393224 | tf_op jit(solution)/shard_map/ppermute | solution.py:17
  77.8 2.9 %collective-permute-start.19 = (bf16[1,256,256]{2,1,0:T(8,128)(2,1)S(1)}, bf16[1,256,256]{2,1,0:T(8,128)(2,1)S(1)}, u32[]{:S(2)}, u32[]{:S(2)}) collective-permute-start(bf16[1,256,256]{2,1,0:T(8,128)(2,1)S(1)} %get-tuple-element.58), channel_id=1, source_target_pairs={{0,12},{4,8},{8,4},{12,0},{16,28},{20,24},{24,20},{28,16},{1,13},{... | collective-permute-start | bytes 393224 | tf_op jit(solution)/shard_map/ppermute | solution.py:17
  81.4 2.0 %shard_map.71.refs_23_ = bf16[2,256,256]{2,1,0:T(8,128)(2,1)S(1)} custom-call(s32[2,8,8]{2,1,0:T(8,128)S(1)} %copy-done.1, s32[2,2,8]{2,1,0:T(2,128)S(1)} %copy-done.2, s32[2,2]{1,0:T(2,128)S(1)} %copy-done.3, bf16[3,2,256,512]{3,2,1,0:T(8,128)(2,1)S(1)} %copy-done, bf16[2,256,256]{2,1,0:T(8,128)(2,1)S(1)} %get-tuple-element.47.inv, ...), custom_call_target="tpu_custom_call" | custom-call | flops 603979776 | bytes 10355344 | tf_op jit(solution)/shard_map/pallas_call | solution.py:56
  85.8 1.5 %collective-permute-done.19.refs_19_ = bf16[1,256,256]{2,1,0:T(8,128)(2,1)S(1)} collective-permute-done((bf16[1,256,256]{2,1,0:T(8,128)(2,1)S(1)}, bf16[1,256,256]{2,1,0:T(8,128)(2,1)S(1)}, u32[]{:S(2)}, u32[]{:S(2)}) %collective-permute-start.19) | collective-permute-done | bytes 131104 | tf_op jit(solution)/shard_map/ppermute | solution.py:17
  87.3 2.7 %shard_map.72 = bf16[3,2,256,512]{3,2,1,0:T(8,128)(2,1)} custom-call(s32[2,8,8]{2,1,0:T(8,128)S(1)} %copy-done.1, s32[2,2,8]{2,1,0:T(2,128)S(1)} %copy-done.2, s32[2,2]{1,0:T(2,128)S(1)} %copy-done.3, bf16[3,2,256,512]{3,2,1,0:T(8,128)(2,1)S(1)} %copy-done, bf16[2,256,256]{2,1,0:T(8,128)(2,1)S(1)} %get-tuple-element.47.inv, ...), custom_call_target="tpu_custom_call" | custom-call | flops 603979776 | bytes 12976784 | tf_op jit(solution)/shard_map/pallas_call | solution.py:56
  (49 shorter events, 12.7 us)
Async XLA Ops:
  0.9 5.8 %collective-permute-start.1 = (bf16[128,256]{1,0:T(8,128)(2,1)S(1)}, bf16[128,256]{1,0:T(8,128)(2,1)S(1)}, u32[]{:S(2)}, u32[]{:S(2)}) collective-permute-start(bf16[128,256]{1,0:T(8,128)(2,1)S(1)} %bitcast.7), channel_id=1, source_target_pairs={{0,1},{1,0},{2,3},{3,2},{4,5},{5,4},{6,7},{7,6},{8,9},{9,8},{10,11... | collective-permute-start | bytes 196616 | tf_op jit(solution)/shard_map/ppermute | solution.py:17
  1.4 5.3 %collective-permute-start = (bf16[128,256]{1,0:T(8,128)(2,1)S(1)}, bf16[128,256]{1,0:T(8,128)(2,1)S(1)}, u32[]{:S(2)}, u32[]{:S(2)}) collective-permute-start(bf16[128,256]{1,0:T(8,128)(2,1)S(1)} %bitcast.8), channel_id=1, source_target_pairs={{0,2},{1,3},{2,0},{3,1},{4,6},{5,7},{6,4},{7,5},{8,10},{9,11},{10,... | collective-permute-start | bytes 196616 | tf_op jit(solution)/shard_map/ppermute | solution.py:17
  6.7 1.3 %collective-permute-start.2 = (bf16[128,256]{1,0:T(8,128)(2,1)S(1)}, bf16[128,256]{1,0:T(8,128)(2,1)S(1)}, u32[]{:S(2)}, u32[]{:S(2)}) collective-permute-start(bf16[128,256]{1,0:T(8,128)(2,1)S(1)} %collective-permute-done.refs_1_), channel_id=1, source_target_pairs={{0,1},{1,0},{2,3},{3,2},{4,5},{5,4},{6,7},{7,6},{8,9},{9,8},{10,11... | collective-permute-start | bytes 196616 | tf_op jit(solution)/shard_map/ppermute | solution.py:17
  8.4 29.1 %collective-permute-start.7 = (bf16[2304,256]{1,0:T(8,128)(2,1)S(1)}, bf16[2304,256]{1,0:T(8,128)(2,1)S(1)}, u32[]{:S(2)}, u32[]{:S(2)}) collective-permute-start(bf16[2304,256]{1,0:T(8,128)(2,1)S(1)} %get-tuple-element.41.refs_3_), channel_id=1, source_target_pairs={{0,2},{1,3},{2,0},{3,1},{4,6},{5,7},{6,4},{7,5},{8,10},{9,11},{10,... | collective-permute-start | bytes 3538952 | tf_op jit(solution)/shard_map/ppermute | solution.py:17
  10.2 27.3 %collective-permute-start.3 = (bf16[2,256,512]{2,1,0:T(8,128)(2,1)S(1)}, bf16[2,256,512]{2,1,0:T(8,128)(2,1)S(1)}, u32[]{:S(2)}, u32[]{:S(2)}) collective-permute-start(bf16[2,256,512]{2,1,0:T(8,128)(2,1)S(1)} %get-tuple-element.37.refs_4_.refs_20_), channel_id=1, source_target_pairs={{0,16},{4,20},{8,24},{12,28},{16,0},{20,4},{24,8},{28,12},{1,17},{... | collective-permute-start | bytes 1572872 | tf_op jit(solution)/shard_map/ppermute | solution.py:17
  12.8 8.3 %collective-permute-start.4 = (bf16[1,256,512]{2,1,0:T(8,128)(2,1)S(1)}, bf16[1,256,512]{2,1,0:T(8,128)(2,1)S(1)}, u32[]{:S(2)}, u32[]{:S(2)}) collective-permute-start(bf16[1,256,512]{2,1,0:T(8,128)(2,1)S(1)} %get-tuple-element.38), channel_id=1, source_target_pairs={{0,4},{4,0},{8,12},{12,8},{16,20},{20,16},{24,28},{28,24},{1,5},{5... | collective-permute-start | bytes 786440 | tf_op jit(solution)/shard_map/ppermute | solution.py:17
  14.3 16.5 %collective-permute-start.5 = (bf16[1,256,512]{2,1,0:T(8,128)(2,1)S(1)}, bf16[1,256,512]{2,1,0:T(8,128)(2,1)S(1)}, u32[]{:S(2)}, u32[]{:S(2)}) collective-permute-start(bf16[1,256,512]{2,1,0:T(8,128)(2,1)S(1)} %get-tuple-element.39), channel_id=1, source_target_pairs={{0,8},{4,12},{8,0},{12,4},{16,24},{20,28},{24,16},{28,20},{1,9},{5... | collective-permute-start | bytes 786440 | tf_op jit(solution)/shard_map/ppermute | solution.py:17
  15.9 21.6 %collective-permute-start.6 = (bf16[1,256,512]{2,1,0:T(8,128)(2,1)S(1)}, bf16[1,256,512]{2,1,0:T(8,128)(2,1)S(1)}, u32[]{:S(2)}, u32[]{:S(2)}) collective-permute-start(bf16[1,256,512]{2,1,0:T(8,128)(2,1)S(1)} %get-tuple-element.40), channel_id=1, source_target_pairs={{0,12},{4,8},{8,4},{12,0},{16,28},{20,24},{24,20},{28,16},{1,13},{... | collective-permute-start | bytes 786440 | tf_op jit(solution)/shard_map/ppermute | solution.py:17
  37.7 4.1 %collective-permute-start.8 = (bf16[2304,256]{1,0:T(8,128)(2,1)S(1)}, bf16[2304,256]{1,0:T(8,128)(2,1)S(1)}, u32[]{:S(2)}, u32[]{:S(2)}) collective-permute-start(bf16[2304,256]{1,0:T(8,128)(2,1)S(1)} %get-tuple-element.42.refs_0_), channel_id=1, source_target_pairs={{0,1},{1,0},{2,3},{3,2},{4,5},{5,4},{6,7},{7,6},{8,9},{9,8},{10,11... | collective-permute-start | bytes 3538952 | tf_op jit(solution)/shard_map/ppermute | solution.py:17
  37.8 4.5 %collective-permute-start.9 = (bf16[2304,256]{1,0:T(8,128)(2,1)S(1)}, bf16[2304,256]{1,0:T(8,128)(2,1)S(1)}, u32[]{:S(2)}, u32[]{:S(2)}) collective-permute-start(bf16[2304,256]{1,0:T(8,128)(2,1)S(1)} %get-tuple-element.43.refs_1_), channel_id=1, source_target_pairs={{0,1},{1,0},{2,3},{3,2},{4,5},{5,4},{6,7},{7,6},{8,9},{9,8},{10,11... | collective-permute-start | bytes 3538952 | tf_op jit(solution)/shard_map/ppermute | solution.py:17
  38.3 6.4 %collective-permute-start.20 = (bf16[1,256,256]{2,1,0:T(8,128)(2,1)S(1)}, bf16[1,256,256]{2,1,0:T(8,128)(2,1)S(1)}, u32[]{:S(2)}, u32[]{:S(2)}) collective-permute-start(bf16[1,256,256]{2,1,0:T(8,128)(2,1)S(1)} %get-tuple-element.59), channel_id=1, source_target_pairs={{0,4},{4,0},{8,12},{12,8},{16,20},{20,16},{24,28},{28,24},{1,5},{5... | collective-permute-start | bytes 393224 | tf_op jit(solution)/shard_map/ppermute | solution.py:17
  39.8 6.4 %collective-permute-start.21 = (bf16[1,256,256]{2,1,0:T(8,128)(2,1)S(1)}, bf16[1,256,256]{2,1,0:T(8,128)(2,1)S(1)}, u32[]{:S(2)}, u32[]{:S(2)}) collective-permute-start(bf16[1,256,256]{2,1,0:T(8,128)(2,1)S(1)} %get-tuple-element.60), channel_id=1, source_target_pairs={{0,8},{4,12},{8,0},{12,4},{16,24},{20,28},{24,16},{28,20},{1,9},{5... | collective-permute-start | bytes 393224 | tf_op jit(solution)/shard_map/ppermute | solution.py:17
  40.6 8.4 %collective-permute-start.22 = (bf16[1,256,256]{2,1,0:T(8,128)(2,1)S(1)}, bf16[1,256,256]{2,1,0:T(8,128)(2,1)S(1)}, u32[]{:S(2)}, u32[]{:S(2)}) collective-permute-start(bf16[1,256,256]{2,1,0:T(8,128)(2,1)S(1)} %get-tuple-element.61), channel_id=1, source_target_pairs={{0,12},{4,8},{8,4},{12,0},{16,28},{20,24},{24,20},{28,16},{1,13},{... | collective-permute-start | bytes 393224 | tf_op jit(solution)/shard_map/ppermute | solution.py:17
  42.3 6.6 %copy-start.2 = (s32[2,2,8]{2,1,0:T(2,128)S(1)}, s32[2,2,8]{2,1,0:T(2,128)}, u32[]{:S(2)}) copy-start(s32[2,2,8]{2,1,0:T(2,128)} %lists.7) | copy-start | bytes 388
  42.3 6.6 %copy-start.3 = (s32[2,2]{1,0:T(2,128)S(1)}, s32[2,2]{1,0:T(2,128)}, u32[]{:S(2)}) copy-start(s32[2,2]{1,0:T(2,128)} %counts.7) | copy-start | bytes 52
  42.3 12.0 %collective-permute-start.10 = (bf16[1,256,256]{2,1,0:T(8,128)(2,1)S(1)}, bf16[1,256,256]{2,1,0:T(8,128)(2,1)S(1)}, u32[]{:S(2)}, u32[]{:S(2)}) collective-permute-start(bf16[1,256,256]{2,1,0:T(8,128)(2,1)S(1)} %get-tuple-element.48), channel_id=1, source_target_pairs={{0,4},{4,0},{8,12},{12,8},{16,20},{20,16},{24,28},{28,24},{1,5},{5... | collective-permute-start | bytes 393224 | tf_op jit(solution)/shard_map/ppermute | solution.py:17
  43.9 12.0 %collective-permute-start.11 = (bf16[1,256,256]{2,1,0:T(8,128)(2,1)S(1)}, bf16[1,256,256]{2,1,0:T(8,128)(2,1)S(1)}, u32[]{:S(2)}, u32[]{:S(2)}) collective-permute-start(bf16[1,256,256]{2,1,0:T(8,128)(2,1)S(1)} %get-tuple-element.49), channel_id=1, source_target_pairs={{0,8},{4,12},{8,0},{12,4},{16,24},{20,28},{24,16},{28,20},{1,9},{5... | collective-permute-start | bytes 393224 | tf_op jit(solution)/shard_map/ppermute | solution.py:17
  44.7 11.4 %collective-permute-start.12 = (bf16[1,256,256]{2,1,0:T(8,128)(2,1)S(1)}, bf16[1,256,256]{2,1,0:T(8,128)(2,1)S(1)}, u32[]{:S(2)}, u32[]{:S(2)}) collective-permute-start(bf16[1,256,256]{2,1,0:T(8,128)(2,1)S(1)} %get-tuple-element.50), channel_id=1, source_target_pairs={{0,12},{4,8},{8,4},{12,0},{16,28},{20,24},{24,20},{28,16},{1,13},{... | collective-permute-start | bytes 393224 | tf_op jit(solution)/shard_map/ppermute | solution.py:17
  50.9 16.2 %collective-permute-start.26 = (bf16[2,256,256]{2,1,0:T(8,128)(2,1)S(1)}, bf16[2,256,256]{2,1,0:T(8,128)(2,1)S(1)}, u32[]{:S(2)}, u32[]{:S(2)}) collective-permute-start(bf16[2,256,256]{2,1,0:T(8,128)(2,1)S(1)} %get-tuple-element.62.refs_12_.refs_21_), channel_id=1, source_target_pairs={{0,16},{4,20},{8,24},{12,28},{16,0},{20,4},{24,8},{28,12},{1,17},{... | collective-permute-start | bytes 786440 | tf_op jit(solution)/shard_map/ppermute | solution.py:17
  52.6 6.9 %collective-permute-start.23 = (bf16[1,256,256]{2,1,0:T(8,128)(2,1)S(1)}, bf16[1,256,256]{2,1,0:T(8,128)(2,1)S(1)}, u32[]{:S(2)}, u32[]{:S(2)}) collective-permute-start(bf16[1,256,256]{2,1,0:T(8,128)(2,1)S(1)} %get-tuple-element.63), channel_id=1, source_target_pairs={{0,4},{4,0},{8,12},{12,8},{16,20},{20,16},{24,28},{28,24},{1,5},{5... | collective-permute-start | bytes 393224 | tf_op jit(solution)/shard_map/ppermute | solution.py:17
  54.3 7.9 %collective-permute-start.24 = (bf16[1,256,256]{2,1,0:T(8,128)(2,1)S(1)}, bf16[1,256,256]{2,1,0:T(8,128)(2,1)S(1)}, u32[]{:S(2)}, u32[]{:S(2)}) collective-permute-start(bf16[1,256,256]{2,1,0:T(8,128)(2,1)S(1)} %get-tuple-element.64), channel_id=1, source_target_pairs={{0,8},{4,12},{8,0},{12,4},{16,24},{20,28},{24,16},{28,20},{1,9},{5... | collective-permute-start | bytes 393224 | tf_op jit(solution)/shard_map/ppermute | solution.py:17
  55.9 10.7 %collective-permute-start.25 = (bf16[1,256,256]{2,1,0:T(8,128)(2,1)S(1)}, bf16[1,256,256]{2,1,0:T(8,128)(2,1)S(1)}, u32[]{:S(2)}, u32[]{:S(2)}) collective-permute-start(bf16[1,256,256]{2,1,0:T(8,128)(2,1)S(1)} %get-tuple-element.65), channel_id=1, source_target_pairs={{0,12},{4,8},{8,4},{12,0},{16,28},{20,24},{24,20},{28,16},{1,13},{... | collective-permute-start | bytes 393224 | tf_op jit(solution)/shard_map/ppermute | solution.py:17
  58.1 19.0 %collective-permute-start.16 = (bf16[2,256,256]{2,1,0:T(8,128)(2,1)S(1)}, bf16[2,256,256]{2,1,0:T(8,128)(2,1)S(1)}, u32[]{:S(2)}, u32[]{:S(2)}) collective-permute-start(bf16[2,256,256]{2,1,0:T(8,128)(2,1)S(1)} %get-tuple-element.52.refs_12_.refs_22_), channel_id=1, source_target_pairs={{0,16},{4,20},{8,24},{12,28},{16,0},{20,4},{24,8},{28,12},{1,17},{... | collective-permute-start | bytes 786440 | tf_op jit(solution)/shard_map/ppermute | solution.py:17
  59.4 11.2 %collective-permute-start.13 = (bf16[1,256,256]{2,1,0:T(8,128)(2,1)S(1)}, bf16[1,256,256]{2,1,0:T(8,128)(2,1)S(1)}, u32[]{:S(2)}, u32[]{:S(2)}) collective-permute-start(bf16[1,256,256]{2,1,0:T(8,128)(2,1)S(1)} %get-tuple-element.53), channel_id=1, source_target_pairs={{0,4},{4,0},{8,12},{12,8},{16,20},{20,16},{24,28},{28,24},{1,5},{5... | collective-permute-start | bytes 393224 | tf_op jit(solution)/shard_map/ppermute | solution.py:17
  62.2 11.3 %collective-permute-start.14 = (bf16[1,256,256]{2,1,0:T(8,128)(2,1)S(1)}, bf16[1,256,256]{2,1,0:T(8,128)(2,1)S(1)}, u32[]{:S(2)}, u32[]{:S(2)}) collective-permute-start(bf16[1,256,256]{2,1,0:T(8,128)(2,1)S(1)} %get-tuple-element.54), channel_id=1, source_target_pairs={{0,8},{4,12},{8,0},{12,4},{16,24},{20,28},{24,16},{28,20},{1,9},{5... | collective-permute-start | bytes 393224 | tf_op jit(solution)/shard_map/ppermute | solution.py:17
  67.3 10.3 %collective-permute-start.27 = (bf16[1,256,256]{2,1,0:T(8,128)(2,1)S(1)}, bf16[1,256,256]{2,1,0:T(8,128)(2,1)S(1)}, u32[]{:S(2)}, u32[]{:S(2)}) collective-permute-start(bf16[1,256,256]{2,1,0:T(8,128)(2,1)S(1)} %get-tuple-element.66), channel_id=1, source_target_pairs={{0,4},{4,0},{8,12},{12,8},{16,20},{20,16},{24,28},{28,24},{1,5},{5... | collective-permute-start | bytes 393224 | tf_op jit(solution)/shard_map/ppermute | solution.py:17
  70.6 7.2 %collective-permute-start.28 = (bf16[1,256,256]{2,1,0:T(8,128)(2,1)S(1)}, bf16[1,256,256]{2,1,0:T(8,128)(2,1)S(1)}, u32[]{:S(2)}, u32[]{:S(2)}) collective-permute-start(bf16[1,256,256]{2,1,0:T(8,128)(2,1)S(1)} %get-tuple-element.67), channel_id=1, source_target_pairs={{0,8},{4,12},{8,0},{12,4},{16,24},{20,28},{24,16},{28,20},{1,9},{5... | collective-permute-start | bytes 393224 | tf_op jit(solution)/shard_map/ppermute | solution.py:17
  70.6 10.8 %collective-permute-start.29 = (bf16[1,256,256]{2,1,0:T(8,128)(2,1)S(1)}, bf16[1,256,256]{2,1,0:T(8,128)(2,1)S(1)}, u32[]{:S(2)}, u32[]{:S(2)}) collective-permute-start(bf16[1,256,256]{2,1,0:T(8,128)(2,1)S(1)} %get-tuple-element.68), channel_id=1, source_target_pairs={{0,12},{4,8},{8,4},{12,0},{16,28},{20,24},{24,20},{28,16},{1,13},{... | collective-permute-start | bytes 393224 | tf_op jit(solution)/shard_map/ppermute | solution.py:17
  73.4 10.9 %collective-permute-start.15 = (bf16[1,256,256]{2,1,0:T(8,128)(2,1)S(1)}, bf16[1,256,256]{2,1,0:T(8,128)(2,1)S(1)}, u32[]{:S(2)}, u32[]{:S(2)}) collective-permute-start(bf16[1,256,256]{2,1,0:T(8,128)(2,1)S(1)} %get-tuple-element.55), channel_id=1, source_target_pairs={{0,12},{4,8},{8,4},{12,0},{16,28},{20,24},{24,20},{28,16},{1,13},{... | collective-permute-start | bytes 393224 | tf_op jit(solution)/shard_map/ppermute | solution.py:17
  77.2 8.2 %collective-permute-start.17 = (bf16[1,256,256]{2,1,0:T(8,128)(2,1)S(1)}, bf16[1,256,256]{2,1,0:T(8,128)(2,1)S(1)}, u32[]{:S(2)}, u32[]{:S(2)}) collective-permute-start(bf16[1,256,256]{2,1,0:T(8,128)(2,1)S(1)} %get-tuple-element.56), channel_id=1, source_target_pairs={{0,4},{4,0},{8,12},{12,8},{16,20},{20,16},{24,28},{28,24},{1,5},{5... | collective-permute-start | bytes 393224 | tf_op jit(solution)/shard_map/ppermute | solution.py:17
  77.6 8.1 %collective-permute-start.18 = (bf16[1,256,256]{2,1,0:T(8,128)(2,1)S(1)}, bf16[1,256,256]{2,1,0:T(8,128)(2,1)S(1)}, u32[]{:S(2)}, u32[]{:S(2)}) collective-permute-start(bf16[1,256,256]{2,1,0:T(8,128)(2,1)S(1)} %get-tuple-element.57), channel_id=1, source_target_pairs={{0,8},{4,12},{8,0},{12,4},{16,24},{20,28},{24,16},{28,20},{1,9},{5... | collective-permute-start | bytes 393224 | tf_op jit(solution)/shard_map/ppermute | solution.py:17
  77.8 9.5 %collective-permute-start.19 = (bf16[1,256,256]{2,1,0:T(8,128)(2,1)S(1)}, bf16[1,256,256]{2,1,0:T(8,128)(2,1)S(1)}, u32[]{:S(2)}, u32[]{:S(2)}) collective-permute-start(bf16[1,256,256]{2,1,0:T(8,128)(2,1)S(1)} %get-tuple-element.58), channel_id=1, source_target_pairs={{0,12},{4,8},{8,4},{12,0},{16,28},{20,24},{24,20},{28,16},{1,13},{... | collective-permute-start | bytes 393224 | tf_op jit(solution)/shard_map/ppermute | solution.py:17
  (2 other events, 4.1 us)

commit v29 on v28

--- a/solution.py
+++ b/solution.py
@@ -90,8 +90,12 @@
     fill_inverse(inv, row_blocks(parts, held, nodes * rows), 0, draw)
     for node in range(nodes):
         solved[node] = transposed_dot(inv[node], noise[node]).astype(BF16)
-    for step, send in enumerate(sends, 1):
-        send[0] = solved[entry_of(picks[0], myself ^ step, myself)]
+    side = len(sends) // CHUNKS
+    for at, send in enumerate(sends):
+        chunk, step = divmod(at, side)
+        wide = send.shape[-1]
+        node = entry_of(picks[0], myself ^ (step + 1), myself)
+        send[0] = solved[node, :, chunk * wide:(chunk + 1) * wide]
 
 
 def relay_kernel(half, source, waits, through, picks, far, *refs):
@@ -196,20 +200,25 @@
     values, steps = near_rows(values, steps, "draw", draws)
     solved, *sends, raw = call(
         functools.partial(first_kernel, steps),
-        [shape(nodes, rows, columns)] + [shape(1, rows, columns)] * (half - 1) + [shape(*raw.shape)],
+        [shape(nodes, rows, columns)] + [shape(1, rows, wide)] * (CHUNKS * (half - 1))
+        + [shape(*raw.shape)],
         [inv_here],
         (picks, noise[0], *values, raw),
         flops=nodes * CHUNKS * dot_flops,
-        aliases={2 + len(values): half},
-    )
-    far, got = leaf(solved, half), near(sends)
+        aliases={2 + len(values): 1 + CHUNKS * (half - 1)},
+    )
+    far, got = leaf(solved, half), []
+    for _ in chunks:
+        sent, sends = take(sends, half - 1)
+        got.append(near(sent))
+    waits = got[0] + got[1][:2]
     values, steps = far_rows(raw, "draw", draws)
     sends = call(
-        functools.partial(relay_kernel, half, 0, len(got), len(values)),
+        functools.partial(relay_kernel, half, 0, len(waits), len(values)),
         [shape(1, rows, wide)] * (CHUNKS * (half - 1)) + [shape(*value.shape) for value in values],
         [],
-        (picks, far, *got, *values),
-        aliases={2 + len(got) + at: CHUNKS * (half - 1) + at for at in range(len(values))},
+        (picks, far, *waits, *values),
+        aliases={2 + len(waits) + at: CHUNKS * (half - 1) + at for at in range(len(values))},
     )
     sends, values = take(sends, CHUNKS * (half - 1))
     packs, steps = near_rows(values, steps, "draw", draws)
@@ -228,7 +237,7 @@
     for at in chunks:
         distant, sends = take(sends, half - 1)
         pieces[0].append([
-            (solved, 0), *((ref, 0) for ref in got),
+            (solved, 0), *((ref, 0) for ref in got[at]),
             (far, 0), *((ref, 0) for ref in near(distant)),
         ])
 

time: 90.2 us -> 95.7 us (1.061)
  waiting for transfers between devices: 36.9 us -> 40.8 us
  starting transfers between devices: 41.1 us -> 42.7 us
    ppermute x30 -> x33, waiting for transfers between devices: 36.9 us -> 40.8 us  [hop(): return lax.ppermute(value, axis, [(at, at ^ step) for at in range(size)])]
    ppermute x30 -> x33, starting transfers between devices: 41.1 us -> 42.7 us  [hop(): return lax.ppermute(value, axis, [(at, at ^ step) for at in range(size)])]
  transfers between devices with their start and end apart: 30 -> 33, of which waited for: 17 -> 18; matrix products, arithmetic and copies ran while one was open for 2% -> 1% of each run, Pallas kernels for 7% -> 7%
where the time goes in v29:
time: 95.7 us; the launch traced here: 95.5 us
  starting transfers between devices  42.7 us (45%)
  waiting for transfers between devices  40.8 us (43%)
  Pallas kernels  9.52 us (10%)
  local copies, waits for them, and re-layouts  2.24 us (2%)
    ppermute x33, starting transfers between devices, hop(): return lax.ppermute(value, axis, [(at, at ^ step) for at in range(size)])  42.7 us
    ppermute x33, waiting for transfers between devices, hop(): return lax.ppermute(value, axis, [(at, at ^ step) for at in range(size)])  40.8 us
    pallas_call x9, Pallas kernels, call(): pl.pallas_call(kernel, out_shape=outs, in_specs=[VMEM] * len(arrays), out...  9.52 us
  transfers between devices with their start and end apart: 33, of which 18 were waited for; matrix products, arithmetic and copies ran while one was open for 1% of the time, Pallas kernels for 7%

profile of v29, /device:TPU:0, one launch (start us, length us, event | category | flops | bytes accessed | tf_op | source)
XLA Modules:
  0.0 95.5 jit_solution(8399011675220697638)
XLA Ops:
  1.4 2.6 %collective-permute-start = (bf16[128,256]{1,0:T(8,128)(2,1)S(1)}, bf16[128,256]{1,0:T(8,128)(2,1)S(1)}, u32[]{:S(2)}, u32[]{:S(2)}) collective-permute-start(bf16[128,256]{1,0:T(8,128)(2,1)S(1)} %bitcast.8), channel_id=1, source_target_pairs={{0,2},{1,3},{2,0},{3,1},{4,6},{5,7},{6,4},{7,5},{8,10},{9,11},{10,... | collective-permute-start | bytes 196616 | tf_op jit(solution)/shard_map/ppermute | solution.py:17
  8.4 1.8 %collective-permute-start.9 = (bf16[2304,256]{1,0:T(8,128)(2,1)S(1)}, bf16[2304,256]{1,0:T(8,128)(2,1)S(1)}, u32[]{:S(2)}, u32[]{:S(2)}) collective-permute-start(bf16[2304,256]{1,0:T(8,128)(2,1)S(1)} %get-tuple-element.46.refs_5_), channel_id=1, source_target_pairs={{0,2},{1,3},{2,0},{3,1},{4,6},{5,7},{6,4},{7,5},{8,10},{9,11},{10,... | collective-permute-start | bytes 3538952 | tf_op jit(solution)/shard_map/ppermute | solution.py:17
  10.2 2.6 %collective-permute-start.3 = (bf16[2,256,512]{2,1,0:T(8,128)(2,1)S(1)}, bf16[2,256,512]{2,1,0:T(8,128)(2,1)S(1)}, u32[]{:S(2)}, u32[]{:S(2)}) collective-permute-start(bf16[2,256,512]{2,1,0:T(8,128)(2,1)S(1)} %get-tuple-element.40.refs_4_.refs_20_), channel_id=1, source_target_pairs={{0,16},{4,20},{8,24},{12,28},{16,0},{20,4},{24,8},{28,12},{1,17},{... | collective-permute-start | bytes 1572872 | tf_op jit(solution)/shard_map/ppermute | solution.py:17
  12.8 1.5 %collective-permute-start.4 = (bf16[1,256,256]{2,1,0:T(8,128)(2,1)S(1)}, bf16[1,256,256]{2,1,0:T(8,128)(2,1)S(1)}, u32[]{:S(2)}, u32[]{:S(2)}) collective-permute-start(bf16[1,256,256]{2,1,0:T(8,128)(2,1)S(1)} %get-tuple-element.41), channel_id=1, source_target_pairs={{0,4},{4,0},{8,12},{12,8},{16,20},{20,16},{24,28},{28,24},{1,5},{5... | collective-permute-start | bytes 393224 | tf_op jit(solution)/shard_map/ppermute | solution.py:17
  14.3 1.6 %collective-permute-start.5 = (bf16[1,256,256]{2,1,0:T(8,128)(2,1)S(1)}, bf16[1,256,256]{2,1,0:T(8,128)(2,1)S(1)}, u32[]{:S(2)}, u32[]{:S(2)}) collective-permute-start(bf16[1,256,256]{2,1,0:T(8,128)(2,1)S(1)} %get-tuple-element.42), channel_id=1, source_target_pairs={{0,8},{4,12},{8,0},{12,4},{16,24},{20,28},{24,16},{28,20},{1,9},{5... | collective-permute-start | bytes 393224 | tf_op jit(solution)/shard_map/ppermute | solution.py:17
  16.3 1.5 %collective-permute-done.4.refs_0_.refs_5_ = bf16[1,256,256]{2,1,0:T(8,128)(2,1)S(1)} collective-permute-done((bf16[1,256,256]{2,1,0:T(8,128)(2,1)S(1)}, bf16[1,256,256]{2,1,0:T(8,128)(2,1)S(1)}, u32[]{:S(2)}, u32[]{:S(2)}) %collective-permute-start.4) | collective-permute-done | bytes 131104 | tf_op jit(solution)/shard_map/ppermute | solution.py:17
  17.8 2.1 %collective-permute-start.7 = (bf16[1,256,256]{2,1,0:T(8,128)(2,1)S(1)}, bf16[1,256,256]{2,1,0:T(8,128)(2,1)S(1)}, u32[]{:S(2)}, u32[]{:S(2)}) collective-permute-start(bf16[1,256,256]{2,1,0:T(8,128)(2,1)S(1)} %get-tuple-element.44), channel_id=1, source_target_pairs={{0,4},{4,0},{8,12},{12,8},{16,20},{20,16},{24,28},{28,24},{1,5},{5... | collective-permute-start | bytes 393224 | tf_op jit(solution)/shard_map/ppermute | solution.py:17
  19.8 8.1 %collective-permute-done.5.refs_1_.refs_6_ = bf16[1,256,256]{2,1,0:T(8,128)(2,1)S(1)} collective-permute-done((bf16[1,256,256]{2,1,0:T(8,128)(2,1)S(1)}, bf16[1,256,256]{2,1,0:T(8,128)(2,1)S(1)}, u32[]{:S(2)}, u32[]{:S(2)}) %collective-permute-start.5) | collective-permute-done | bytes 131104 | tf_op jit(solution)/shard_map/ppermute | solution.py:17
  27.9 2.5 %collective-permute-start.8 = (bf16[1,256,256]{2,1,0:T(8,128)(2,1)S(1)}, bf16[1,256,256]{2,1,0:T(8,128)(2,1)S(1)}, u32[]{:S(2)}, u32[]{:S(2)}) collective-permute-start(bf16[1,256,256]{2,1,0:T(8,128)(2,1)S(1)} %get-tuple-element.45), channel_id=1, source_target_pairs={{0,8},{4,12},{8,0},{12,4},{16,24},{20,28},{24,16},{28,20},{1,9},{5... | collective-permute-start | bytes 393224 | tf_op jit(solution)/shard_map/ppermute | solution.py:17
  30.8 8.1 %collective-permute-done.8.refs_4_.refs_6_ = bf16[1,256,256]{2,1,0:T(8,128)(2,1)S(1)} collective-permute-done((bf16[1,256,256]{2,1,0:T(8,128)(2,1)S(1)}, bf16[1,256,256]{2,1,0:T(8,128)(2,1)S(1)}, u32[]{:S(2)}, u32[]{:S(2)}) %collective-permute-start.8) | collective-permute-done | bytes 131104 | tf_op jit(solution)/shard_map/ppermute | solution.py:17
  39.6 1.5 %collective-permute-start.23 = (bf16[1,256,256]{2,1,0:T(8,128)(2,1)S(1)}, bf16[1,256,256]{2,1,0:T(8,128)(2,1)S(1)}, u32[]{:S(2)}, u32[]{:S(2)}) collective-permute-start(bf16[1,256,256]{2,1,0:T(8,128)(2,1)S(1)} %get-tuple-element.65), channel_id=1, source_target_pairs={{0,4},{4,0},{8,12},{12,8},{16,20},{20,16},{24,28},{28,24},{1,5},{5... | collective-permute-start | bytes 393224 | tf_op jit(solution)/shard_map/ppermute | solution.py:17
  41.1 2.0 %collective-permute-start.25 = (bf16[1,256,256]{2,1,0:T(8,128)(2,1)S(1)}, bf16[1,256,256]{2,1,0:T(8,128)(2,1)S(1)}, u32[]{:S(2)}, u32[]{:S(2)}) collective-permute-start(bf16[1,256,256]{2,1,0:T(8,128)(2,1)S(1)} %get-tuple-element.67), channel_id=1, source_target_pairs={{0,12},{4,8},{8,4},{12,0},{16,28},{20,24},{24,20},{28,16},{1,13},{... | collective-permute-start | bytes 393224 | tf_op jit(solution)/shard_map/ppermute | solution.py:17
  45.3 1.4 %collective-permute-start.14 = (bf16[1,256,256]{2,1,0:T(8,128)(2,1)S(1)}, bf16[1,256,256]{2,1,0:T(8,128)(2,1)S(1)}, u32[]{:S(2)}, u32[]{:S(2)}) collective-permute-start(bf16[1,256,256]{2,1,0:T(8,128)(2,1)S(1)} %get-tuple-element.55), channel_id=1, source_target_pairs={{0,8},{4,12},{8,0},{12,4},{16,24},{20,28},{24,16},{28,20},{1,9},{5... | collective-permute-start | bytes 393224 | tf_op jit(solution)/shard_map/ppermute | solution.py:17
  48.1 2.3 %collective-permute-done.25.refs_11_ = bf16[1,256,256]{2,1,0:T(8,128)(2,1)S(1)} collective-permute-done((bf16[1,256,256]{2,1,0:T(8,128)(2,1)S(1)}, bf16[1,256,256]{2,1,0:T(8,128)(2,1)S(1)}, u32[]{:S(2)}, u32[]{:S(2)}) %collective-permute-start.25) | collective-permute-done | bytes 131104 | tf_op jit(solution)/shard_map/ppermute | solution.py:17
  50.4 2.0 %shard_map.69 = (bf16[2,256,256]{2,1,0:T(8,128)(2,1)S(1)}, bf16[1,256,256]{2,1,0:T(8,128)(2,1)S(1)}, bf16[1,256,256]{2,1,0:T(8,128)(2,1)S(1)}, bf16[1,256,256]{2,1,0:T(8,128)(2,1)S(1)}) custom-call(s32[2,8,8]{2,1,0:T(8,128)S(1)} %copy-done.1, s32[2,2,8]{2,1,0:T(2,128)S(1)} %copy-done.2, s32[2,2]{1,0:T(2,128)S(1)} %copy-done.3, ...), custom_call_target="tpu_custom_call" | custom-call | flops 603979776 | bytes 9044624 | tf_op jit(solution)/shard_map/pallas_call | solution.py:56
  52.3 2.3 %collective-permute-start.29 = (bf16[2,256,256]{2,1,0:T(8,128)(2,1)S(1)}, bf16[2,256,256]{2,1,0:T(8,128)(2,1)S(1)}, u32[]{:S(2)}, u32[]{:S(2)}) collective-permute-start(bf16[2,256,256]{2,1,0:T(8,128)(2,1)S(1)} %get-tuple-element.68.refs_12_.refs_21_), channel_id=1, source_target_pairs={{0,16},{4,20},{8,24},{12,28},{16,0},{20,4},{24,8},{28,12},{1,17},{... | collective-permute-start | bytes 786440 | tf_op jit(solution)/shard_map/ppermute | solution.py:17
  55.9 2.1 %collective-permute-start.27 = (bf16[1,256,256]{2,1,0:T(8,128)(2,1)S(1)}, bf16[1,256,256]{2,1,0:T(8,128)(2,1)S(1)}, u32[]{:S(2)}, u32[]{:S(2)}) collective-permute-start(bf16[1,256,256]{2,1,0:T(8,128)(2,1)S(1)} %get-tuple-element.70), channel_id=1, source_target_pairs={{0,8},{4,12},{8,0},{12,4},{16,24},{20,28},{24,16},{28,20},{1,9},{5... | collective-permute-start | bytes 393224 | tf_op jit(solution)/shard_map/ppermute | solution.py:17
  58.0 3.4 %collective-permute-done.14.refs_10_ = bf16[1,256,256]{2,1,0:T(8,128)(2,1)S(1)} collective-permute-done((bf16[1,256,256]{2,1,0:T(8,128)(2,1)S(1)}, bf16[1,256,256]{2,1,0:T(8,128)(2,1)S(1)}, u32[]{:S(2)}, u32[]{:S(2)}) %collective-permute-start.14) | collective-permute-done | bytes 131104 | tf_op jit(solution)/shard_map/ppermute | solution.py:17
  61.4 1.7 %collective-permute-done.15.refs_11_ = bf16[1,256,256]{2,1,0:T(8,128)(2,1)S(1)} collective-permute-done((bf16[1,256,256]{2,1,0:T(8,128)(2,1)S(1)}, bf16[1,256,256]{2,1,0:T(8,128)(2,1)S(1)}, u32[]{:S(2)}, u32[]{:S(2)}) %collective-permute-start.15) | collective-permute-done | bytes 131104 | tf_op jit(solution)/shard_map/ppermute | solution.py:17
  63.1 2.0 %shard_map.67 = (bf16[2,256,256]{2,1,0:T(8,128)(2,1)S(1)}, bf16[1,256,256]{2,1,0:T(8,128)(2,1)S(1)}, bf16[1,256,256]{2,1,0:T(8,128)(2,1)S(1)}, bf16[1,256,256]{2,1,0:T(8,128)(2,1)S(1)}) custom-call(s32[2,8,8]{2,1,0:T(8,128)S(1)} %copy-done.1, s32[2,2,8]{2,1,0:T(2,128)S(1)} %copy-done.2, s32[2,2]{1,0:T(2,128)S(1)} %copy-done.3, ...), custom_call_target="tpu_custom_call" | custom-call | flops 603979776 | bytes 9044624 | tf_op jit(solution)/shard_map/pallas_call | solution.py:56
  65.2 2.6 %collective-permute-start.16 = (bf16[1,256,256]{2,1,0:T(8,128)(2,1)S(1)}, bf16[1,256,256]{2,1,0:T(8,128)(2,1)S(1)}, u32[]{:S(2)}, u32[]{:S(2)}) collective-permute-start(bf16[1,256,256]{2,1,0:T(8,128)(2,1)S(1)} %get-tuple-element.59), channel_id=1, source_target_pairs={{0,4},{4,0},{8,12},{12,8},{16,20},{20,16},{24,28},{28,24},{1,5},{5... | collective-permute-start | bytes 393224 | tf_op jit(solution)/shard_map/ppermute | solution.py:17
  67.8 2.8 %collective-permute-done.27.refs_1_.refs_14_ = bf16[1,256,256]{2,1,0:T(8,128)(2,1)S(1)} collective-permute-done((bf16[1,256,256]{2,1,0:T(8,128)(2,1)S(1)}, bf16[1,256,256]{2,1,0:T(8,128)(2,1)S(1)}, u32[]{:S(2)}, u32[]{:S(2)}) %collective-permute-start.27) | collective-permute-done | bytes 131104 | tf_op jit(solution)/shard_map/ppermute | solution.py:17
  70.7 1.4 %collective-permute-done.28.refs_2_.refs_15_ = bf16[1,256,256]{2,1,0:T(8,128)(2,1)S(1)} collective-permute-done((bf16[1,256,256]{2,1,0:T(8,128)(2,1)S(1)}, bf16[1,256,256]{2,1,0:T(8,128)(2,1)S(1)}, u32[]{:S(2)}, u32[]{:S(2)}) %collective-permute-start.28) | collective-permute-done | bytes 131104 | tf_op jit(solution)/shard_map/ppermute | solution.py:17
  72.2 3.5 %collective-permute-start.30 = (bf16[1,256,256]{2,1,0:T(8,128)(2,1)S(1)}, bf16[1,256,256]{2,1,0:T(8,128)(2,1)S(1)}, u32[]{:S(2)}, u32[]{:S(2)}) collective-permute-start(bf16[1,256,256]{2,1,0:T(8,128)(2,1)S(1)} %get-tuple-element.72), channel_id=1, source_target_pairs={{0,4},{4,0},{8,12},{12,8},{16,20},{20,16},{24,28},{28,24},{1,5},{5... | collective-permute-start | bytes 393224 | tf_op jit(solution)/shard_map/ppermute | solution.py:17
  75.7 1.5 %collective-permute-start.32 = (bf16[1,256,256]{2,1,0:T(8,128)(2,1)S(1)}, bf16[1,256,256]{2,1,0:T(8,128)(2,1)S(1)}, u32[]{:S(2)}, u32[]{:S(2)}) collective-permute-start(bf16[1,256,256]{2,1,0:T(8,128)(2,1)S(1)} %get-tuple-element.74), channel_id=1, source_target_pairs={{0,12},{4,8},{8,4},{12,0},{16,28},{20,24},{24,20},{28,16},{1,13},{... | collective-permute-start | bytes 393224 | tf_op jit(solution)/shard_map/ppermute | solution.py:17
  77.3 2.0 %collective-permute-start.18 = (bf16[1,256,256]{2,1,0:T(8,128)(2,1)S(1)}, bf16[1,256,256]{2,1,0:T(8,128)(2,1)S(1)}, u32[]{:S(2)}, u32[]{:S(2)}) collective-permute-start(bf16[1,256,256]{2,1,0:T(8,128)(2,1)S(1)} %get-tuple-element.61), channel_id=1, source_target_pairs={{0,12},{4,8},{8,4},{12,0},{16,28},{20,24},{24,20},{28,16},{1,13},{... | collective-permute-start | bytes 393224 | tf_op jit(solution)/shard_map/ppermute | solution.py:17
  82.2 2.0 %collective-permute-start.22 = (bf16[1,256,256]{2,1,0:T(8,128)(2,1)S(1)}, bf16[1,256,256]{2,1,0:T(8,128)(2,1)S(1)}, u32[]{:S(2)}, u32[]{:S(2)}) collective-permute-start(bf16[1,256,256]{2,1,0:T(8,128)(2,1)S(1)} %get-tuple-element.64), channel_id=1, source_target_pairs={{0,12},{4,8},{8,4},{12,0},{16,28},{20,24},{24,20},{28,16},{1,13},{... | collective-permute-start | bytes 393224 | tf_op jit(solution)/shard_map/ppermute | solution.py:17
  84.2 1.3 %collective-permute-done.32.refs_19_ = bf16[1,256,256]{2,1,0:T(8,128)(2,1)S(1)} collective-permute-done((bf16[1,256,256]{2,1,0:T(8,128)(2,1)S(1)}, bf16[1,256,256]{2,1,0:T(8,128)(2,1)S(1)}, u32[]{:S(2)}, u32[]{:S(2)}) %collective-permute-start.32) | collective-permute-done | bytes 131104 | tf_op jit(solution)/shard_map/ppermute | solution.py:17
  85.6 2.0 %shard_map.71.refs_23_ = bf16[2,256,256]{2,1,0:T(8,128)(2,1)S(1)} custom-call(s32[2,8,8]{2,1,0:T(8,128)S(1)} %copy-done.1, s32[2,2,8]{2,1,0:T(2,128)S(1)} %copy-done.2, s32[2,2]{1,0:T(2,128)S(1)} %copy-done.3, bf16[3,2,256,512]{3,2,1,0:T(8,128)(2,1)S(1)} %copy-done, bf16[2,256,256]{2,1,0:T(8,128)(2,1)S(1)} %get-tuple-element.52.inv, ...), custom_call_target="tpu_custom_call" | custom-call | flops 603979776 | bytes 9962128 | tf_op jit(solution)/shard_map/pallas_call | solution.py:56
  88.5 1.4 %collective-permute-done.21.refs_18_ = bf16[1,256,256]{2,1,0:T(8,128)(2,1)S(1)} collective-permute-done((bf16[1,256,256]{2,1,0:T(8,128)(2,1)S(1)}, bf16[1,256,256]{2,1,0:T(8,128)(2,1)S(1)}, u32[]{:S(2)}, u32[]{:S(2)}) %collective-permute-start.21) | collective-permute-done | bytes 131104 | tf_op jit(solution)/shard_map/ppermute | solution.py:17
  89.9 2.9 %collective-permute-done.22.refs_19_ = bf16[1,256,256]{2,1,0:T(8,128)(2,1)S(1)} collective-permute-done((bf16[1,256,256]{2,1,0:T(8,128)(2,1)S(1)}, bf16[1,256,256]{2,1,0:T(8,128)(2,1)S(1)}, u32[]{:S(2)}, u32[]{:S(2)}) %collective-permute-start.22) | collective-permute-done | bytes 131104 | tf_op jit(solution)/shard_map/ppermute | solution.py:17
  92.8 2.7 %shard_map.72 = bf16[3,2,256,512]{3,2,1,0:T(8,128)(2,1)} custom-call(s32[2,8,8]{2,1,0:T(8,128)S(1)} %copy-done.1, s32[2,2,8]{2,1,0:T(2,128)S(1)} %copy-done.2, s32[2,2]{1,0:T(2,128)S(1)} %copy-done.3, bf16[3,2,256,512]{3,2,1,0:T(8,128)(2,1)S(1)} %copy-done, bf16[2,256,256]{2,1,0:T(8,128)(2,1)S(1)} %get-tuple-element.52.inv, ...), custom_call_target="tpu_custom_call" | custom-call | flops 603979776 | bytes 12583568 | tf_op jit(solution)/shard_map/pallas_call | solution.py:56
  (55 shorter events, 16.2 us)
Async XLA Ops:
  0.9 5.8 %collective-permute-start.1 = (bf16[128,256]{1,0:T(8,128)(2,1)S(1)}, bf16[128,256]{1,0:T(8,128)(2,1)S(1)}, u32[]{:S(2)}, u32[]{:S(2)}) collective-permute-start(bf16[128,256]{1,0:T(8,128)(2,1)S(1)} %bitcast.7), channel_id=1, source_target_pairs={{0,1},{1,0},{2,3},{3,2},{4,5},{5,4},{6,7},{7,6},{8,9},{9,8},{10,11... | collective-permute-start | bytes 196616 | tf_op jit(solution)/shard_map/ppermute | solution.py:17
  1.4 5.3 %collective-permute-start = (bf16[128,256]{1,0:T(8,128)(2,1)S(1)}, bf16[128,256]{1,0:T(8,128)(2,1)S(1)}, u32[]{:S(2)}, u32[]{:S(2)}) collective-permute-start(bf16[128,256]{1,0:T(8,128)(2,1)S(1)} %bitcast.8), channel_id=1, source_target_pairs={{0,2},{1,3},{2,0},{3,1},{4,6},{5,7},{6,4},{7,5},{8,10},{9,11},{10,... | collective-permute-start | bytes 196616 | tf_op jit(solution)/shard_map/ppermute | solution.py:17
  8.4 30.5 %collective-permute-start.9 = (bf16[2304,256]{1,0:T(8,128)(2,1)S(1)}, bf16[2304,256]{1,0:T(8,128)(2,1)S(1)}, u32[]{:S(2)}, u32[]{:S(2)}) collective-permute-start(bf16[2304,256]{1,0:T(8,128)(2,1)S(1)} %get-tuple-element.46.refs_5_), channel_id=1, source_target_pairs={{0,2},{1,3},{2,0},{3,1},{4,6},{5,7},{6,4},{7,5},{8,10},{9,11},{10,... | collective-permute-start | bytes 3538952 | tf_op jit(solution)/shard_map/ppermute | solution.py:17
  10.2 28.7 %collective-permute-start.3 = (bf16[2,256,512]{2,1,0:T(8,128)(2,1)S(1)}, bf16[2,256,512]{2,1,0:T(8,128)(2,1)S(1)}, u32[]{:S(2)}, u32[]{:S(2)}) collective-permute-start(bf16[2,256,512]{2,1,0:T(8,128)(2,1)S(1)} %get-tuple-element.40.refs_4_.refs_20_), channel_id=1, source_target_pairs={{0,16},{4,20},{8,24},{12,28},{16,0},{20,4},{24,8},{28,12},{1,17},{... | collective-permute-start | bytes 1572872 | tf_op jit(solution)/shard_map/ppermute | solution.py:17
  12.8 5.0 %collective-permute-start.4 = (bf16[1,256,256]{2,1,0:T(8,128)(2,1)S(1)}, bf16[1,256,256]{2,1,0:T(8,128)(2,1)S(1)}, u32[]{:S(2)}, u32[]{:S(2)}) collective-permute-start(bf16[1,256,256]{2,1,0:T(8,128)(2,1)S(1)} %get-tuple-element.41), channel_id=1, source_target_pairs={{0,4},{4,0},{8,12},{12,8},{16,20},{20,16},{24,28},{28,24},{1,5},{5... | collective-permute-start | bytes 393224 | tf_op jit(solution)/shard_map/ppermute | solution.py:17
  14.3 13.7 %collective-permute-start.5 = (bf16[1,256,256]{2,1,0:T(8,128)(2,1)S(1)}, bf16[1,256,256]{2,1,0:T(8,128)(2,1)S(1)}, u32[]{:S(2)}, u32[]{:S(2)}) collective-permute-start(bf16[1,256,256]{2,1,0:T(8,128)(2,1)S(1)} %get-tuple-element.42), channel_id=1, source_target_pairs={{0,8},{4,12},{8,0},{12,4},{16,24},{20,28},{24,16},{28,20},{1,9},{5... | collective-permute-start | bytes 393224 | tf_op jit(solution)/shard_map/ppermute | solution.py:17
  15.9 14.9 %collective-permute-start.6 = (bf16[1,256,256]{2,1,0:T(8,128)(2,1)S(1)}, bf16[1,256,256]{2,1,0:T(8,128)(2,1)S(1)}, u32[]{:S(2)}, u32[]{:S(2)}) collective-permute-start(bf16[1,256,256]{2,1,0:T(8,128)(2,1)S(1)} %get-tuple-element.43), channel_id=1, source_target_pairs={{0,12},{4,8},{8,4},{12,0},{16,28},{20,24},{24,20},{28,16},{1,13},{... | collective-permute-start | bytes 393224 | tf_op jit(solution)/shard_map/ppermute | solution.py:17
  17.8 13.0 %collective-permute-start.7 = (bf16[1,256,256]{2,1,0:T(8,128)(2,1)S(1)}, bf16[1,256,256]{2,1,0:T(8,128)(2,1)S(1)}, u32[]{:S(2)}, u32[]{:S(2)}) collective-permute-start(bf16[1,256,256]{2,1,0:T(8,128)(2,1)S(1)} %get-tuple-element.44), channel_id=1, source_target_pairs={{0,4},{4,0},{8,12},{12,8},{16,20},{20,16},{24,28},{28,24},{1,5},{5... | collective-permute-start | bytes 393224 | tf_op jit(solution)/shard_map/ppermute | solution.py:17
  27.9 10.9 %collective-permute-start.8 = (bf16[1,256,256]{2,1,0:T(8,128)(2,1)S(1)}, bf16[1,256,256]{2,1,0:T(8,128)(2,1)S(1)}, u32[]{:S(2)}, u32[]{:S(2)}) collective-permute-start(bf16[1,256,256]{2,1,0:T(8,128)(2,1)S(1)} %get-tuple-element.45), channel_id=1, source_target_pairs={{0,8},{4,12},{8,0},{12,4},{16,24},{20,28},{24,16},{28,20},{1,9},{5... | collective-permute-start | bytes 393224 | tf_op jit(solution)/shard_map/ppermute | solution.py:17
  39.0 4.1 %collective-permute-start.10 = (bf16[2304,256]{1,0:T(8,128)(2,1)S(1)}, bf16[2304,256]{1,0:T(8,128)(2,1)S(1)}, u32[]{:S(2)}, u32[]{:S(2)}) collective-permute-start(bf16[2304,256]{1,0:T(8,128)(2,1)S(1)} %get-tuple-element.47.refs_0_), channel_id=1, source_target_pairs={{0,1},{1,0},{2,3},{3,2},{4,5},{5,4},{6,7},{7,6},{8,9},{9,8},{10,11... | collective-permute-start | bytes 3538952 | tf_op jit(solution)/shard_map/ppermute | solution.py:17
  39.1 4.9 %collective-permute-start.11 = (bf16[2304,256]{1,0:T(8,128)(2,1)S(1)}, bf16[2304,256]{1,0:T(8,128)(2,1)S(1)}, u32[]{:S(2)}, u32[]{:S(2)}) collective-permute-start(bf16[2304,256]{1,0:T(8,128)(2,1)S(1)} %get-tuple-element.48.refs_1_), channel_id=1, source_target_pairs={{0,1},{1,0},{2,3},{3,2},{4,5},{5,4},{6,7},{7,6},{8,9},{9,8},{10,11... | collective-permute-start | bytes 3538952 | tf_op jit(solution)/shard_map/ppermute | solution.py:17
  39.6 5.7 %collective-permute-start.23 = (bf16[1,256,256]{2,1,0:T(8,128)(2,1)S(1)}, bf16[1,256,256]{2,1,0:T(8,128)(2,1)S(1)}, u32[]{:S(2)}, u32[]{:S(2)}) collective-permute-start(bf16[1,256,256]{2,1,0:T(8,128)(2,1)S(1)} %get-tuple-element.65), channel_id=1, source_target_pairs={{0,4},{4,0},{8,12},{12,8},{16,20},{20,16},{24,28},{28,24},{1,5},{5... | collective-permute-start | bytes 393224 | tf_op jit(solution)/shard_map/ppermute | solution.py:17
  41.1 6.4 %collective-permute-start.24 = (bf16[1,256,256]{2,1,0:T(8,128)(2,1)S(1)}, bf16[1,256,256]{2,1,0:T(8,128)(2,1)S(1)}, u32[]{:S(2)}, u32[]{:S(2)}) collective-permute-start(bf16[1,256,256]{2,1,0:T(8,128)(2,1)S(1)} %get-tuple-element.66), channel_id=1, source_target_pairs={{0,8},{4,12},{8,0},{12,4},{16,24},{20,28},{24,16},{28,20},{1,9},{5... | collective-permute-start | bytes 393224 | tf_op jit(solution)/shard_map/ppermute | solution.py:17
  41.1 9.2 %collective-permute-start.25 = (bf16[1,256,256]{2,1,0:T(8,128)(2,1)S(1)}, bf16[1,256,256]{2,1,0:T(8,128)(2,1)S(1)}, u32[]{:S(2)}, u32[]{:S(2)}) collective-permute-start(bf16[1,256,256]{2,1,0:T(8,128)(2,1)S(1)} %get-tuple-element.67), channel_id=1, source_target_pairs={{0,12},{4,8},{8,4},{12,0},{16,28},{20,24},{24,20},{28,16},{1,13},{... | collective-permute-start | bytes 393224 | tf_op jit(solution)/shard_map/ppermute | solution.py:17
  43.1 11.5 %collective-permute-start.12 = (bf16[1,256,256]{2,1,0:T(8,128)(2,1)S(1)}, bf16[1,256,256]{2,1,0:T(8,128)(2,1)S(1)}, u32[]{:S(2)}, u32[]{:S(2)}) collective-permute-start(bf16[1,256,256]{2,1,0:T(8,128)(2,1)S(1)} %get-tuple-element.53), channel_id=1, source_target_pairs={{0,12},{4,8},{8,4},{12,0},{16,28},{20,24},{24,20},{28,16},{1,13},{... | collective-permute-start | bytes 393224 | tf_op jit(solution)/shard_map/ppermute | solution.py:17
  44.1 11.8 %collective-permute-start.13 = (bf16[1,256,256]{2,1,0:T(8,128)(2,1)S(1)}, bf16[1,256,256]{2,1,0:T(8,128)(2,1)S(1)}, u32[]{:S(2)}, u32[]{:S(2)}) collective-permute-start(bf16[1,256,256]{2,1,0:T(8,128)(2,1)S(1)} %get-tuple-element.54), channel_id=1, source_target_pairs={{0,4},{4,0},{8,12},{12,8},{16,20},{20,16},{24,28},{28,24},{1,5},{5... | collective-permute-start | bytes 393224 | tf_op jit(solution)/shard_map/ppermute | solution.py:17
  45.3 16.2 %collective-permute-start.14 = (bf16[1,256,256]{2,1,0:T(8,128)(2,1)S(1)}, bf16[1,256,256]{2,1,0:T(8,128)(2,1)S(1)}, u32[]{:S(2)}, u32[]{:S(2)}) collective-permute-start(bf16[1,256,256]{2,1,0:T(8,128)(2,1)S(1)} %get-tuple-element.55), channel_id=1, source_target_pairs={{0,8},{4,12},{8,0},{12,4},{16,24},{20,28},{24,16},{28,20},{1,9},{5... | collective-permute-start | bytes 393224 | tf_op jit(solution)/shard_map/ppermute | solution.py:17
  47.5 15.6 %collective-permute-start.15 = (bf16[1,256,256]{2,1,0:T(8,128)(2,1)S(1)}, bf16[1,256,256]{2,1,0:T(8,128)(2,1)S(1)}, u32[]{:S(2)}, u32[]{:S(2)}) collective-permute-start(bf16[1,256,256]{2,1,0:T(8,128)(2,1)S(1)} %get-tuple-element.56), channel_id=1, source_target_pairs={{0,12},{4,8},{8,4},{12,0},{16,28},{20,24},{24,20},{28,16},{1,13},{... | collective-permute-start | bytes 393224 | tf_op jit(solution)/shard_map/ppermute | solution.py:17
  52.3 19.7 %collective-permute-start.29 = (bf16[2,256,256]{2,1,0:T(8,128)(2,1)S(1)}, bf16[2,256,256]{2,1,0:T(8,128)(2,1)S(1)}, u32[]{:S(2)}, u32[]{:S(2)}) collective-permute-start(bf16[2,256,256]{2,1,0:T(8,128)(2,1)S(1)} %get-tuple-element.68.refs_12_.refs_21_), channel_id=1, source_target_pairs={{0,16},{4,20},{8,24},{12,28},{16,0},{20,4},{24,8},{28,12},{1,17},{... | collective-permute-start | bytes 786440 | tf_op jit(solution)/shard_map/ppermute | solution.py:17
  54.6 10.5 %collective-permute-start.26 = (bf16[1,256,256]{2,1,0:T(8,128)(2,1)S(1)}, bf16[1,256,256]{2,1,0:T(8,128)(2,1)S(1)}, u32[]{:S(2)}, u32[]{:S(2)}) collective-permute-start(bf16[1,256,256]{2,1,0:T(8,128)(2,1)S(1)} %get-tuple-element.69), channel_id=1, source_target_pairs={{0,4},{4,0},{8,12},{12,8},{16,20},{20,16},{24,28},{28,24},{1,5},{5... | collective-permute-start | bytes 393224 | tf_op jit(solution)/shard_map/ppermute | solution.py:17
  55.9 14.7 %collective-permute-start.27 = (bf16[1,256,256]{2,1,0:T(8,128)(2,1)S(1)}, bf16[1,256,256]{2,1,0:T(8,128)(2,1)S(1)}, u32[]{:S(2)}, u32[]{:S(2)}) collective-permute-start(bf16[1,256,256]{2,1,0:T(8,128)(2,1)S(1)} %get-tuple-element.70), channel_id=1, source_target_pairs={{0,8},{4,12},{8,0},{12,4},{16,24},{20,28},{24,16},{28,20},{1,9},{5... | collective-permute-start | bytes 393224 | tf_op jit(solution)/shard_map/ppermute | solution.py:17
  61.4 10.6 %collective-permute-start.28 = (bf16[1,256,256]{2,1,0:T(8,128)(2,1)S(1)}, bf16[1,256,256]{2,1,0:T(8,128)(2,1)S(1)}, u32[]{:S(2)}, u32[]{:S(2)}) collective-permute-start(bf16[1,256,256]{2,1,0:T(8,128)(2,1)S(1)} %get-tuple-element.71), channel_id=1, source_target_pairs={{0,12},{4,8},{8,4},{12,0},{16,28},{20,24},{24,20},{28,16},{1,13},{... | collective-permute-start | bytes 393224 | tf_op jit(solution)/shard_map/ppermute | solution.py:17
  65.1 14.2 %collective-permute-start.19 = (bf16[2,256,256]{2,1,0:T(8,128)(2,1)S(1)}, bf16[2,256,256]{2,1,0:T(8,128)(2,1)S(1)}, u32[]{:S(2)}, u32[]{:S(2)}) collective-permute-start(bf16[2,256,256]{2,1,0:T(8,128)(2,1)S(1)} %get-tuple-element.58.refs_12_.refs_22_), channel_id=1, source_target_pairs={{0,16},{4,20},{8,24},{12,28},{16,0},{20,4},{24,8},{28,12},{1,17},{... | collective-permute-start | bytes 786440 | tf_op jit(solution)/shard_map/ppermute | solution.py:17
  65.2 10.6 %collective-permute-start.16 = (bf16[1,256,256]{2,1,0:T(8,128)(2,1)S(1)}, bf16[1,256,256]{2,1,0:T(8,128)(2,1)S(1)}, u32[]{:S(2)}, u32[]{:S(2)}) collective-permute-start(bf16[1,256,256]{2,1,0:T(8,128)(2,1)S(1)} %get-tuple-element.59), channel_id=1, source_target_pairs={{0,4},{4,0},{8,12},{12,8},{16,20},{20,16},{24,28},{28,24},{1,5},{5... | collective-permute-start | bytes 393224 | tf_op jit(solution)/shard_map/ppermute | solution.py:17
  70.7 6.6 %collective-permute-start.17 = (bf16[1,256,256]{2,1,0:T(8,128)(2,1)S(1)}, bf16[1,256,256]{2,1,0:T(8,128)(2,1)S(1)}, u32[]{:S(2)}, u32[]{:S(2)}) collective-permute-start(bf16[1,256,256]{2,1,0:T(8,128)(2,1)S(1)} %get-tuple-element.60), channel_id=1, source_target_pairs={{0,8},{4,12},{8,0},{12,4},{16,24},{20,28},{24,16},{28,20},{1,9},{5... | collective-permute-start | bytes 393224 | tf_op jit(solution)/shard_map/ppermute | solution.py:17
  72.2 8.4 %collective-permute-start.30 = (bf16[1,256,256]{2,1,0:T(8,128)(2,1)S(1)}, bf16[1,256,256]{2,1,0:T(8,128)(2,1)S(1)}, u32[]{:S(2)}, u32[]{:S(2)}) collective-permute-start(bf16[1,256,256]{2,1,0:T(8,128)(2,1)S(1)} %get-tuple-element.72), channel_id=1, source_target_pairs={{0,4},{4,0},{8,12},{12,8},{16,20},{20,16},{24,28},{28,24},{1,5},{5... | collective-permute-start | bytes 393224 | tf_op jit(solution)/shard_map/ppermute | solution.py:17
  75.7 6.4 %collective-permute-start.31 = (bf16[1,256,256]{2,1,0:T(8,128)(2,1)S(1)}, bf16[1,256,256]{2,1,0:T(8,128)(2,1)S(1)}, u32[]{:S(2)}, u32[]{:S(2)}) collective-permute-start(bf16[1,256,256]{2,1,0:T(8,128)(2,1)S(1)} %get-tuple-element.73), channel_id=1, source_target_pairs={{0,8},{4,12},{8,0},{12,4},{16,24},{20,28},{24,16},{28,20},{1,9},{5... | collective-permute-start | bytes 393224 | tf_op jit(solution)/shard_map/ppermute | solution.py:17
  75.7 9.8 %collective-permute-start.32 = (bf16[1,256,256]{2,1,0:T(8,128)(2,1)S(1)}, bf16[1,256,256]{2,1,0:T(8,128)(2,1)S(1)}, u32[]{:S(2)}, u32[]{:S(2)}) collective-permute-start(bf16[1,256,256]{2,1,0:T(8,128)(2,1)S(1)} %get-tuple-element.74), channel_id=1, source_target_pairs={{0,12},{4,8},{8,4},{12,0},{16,28},{20,24},{24,20},{28,16},{1,13},{... | collective-permute-start | bytes 393224 | tf_op jit(solution)/shard_map/ppermute | solution.py:17
  77.3 11.0 %collective-permute-start.18 = (bf16[1,256,256]{2,1,0:T(8,128)(2,1)S(1)}, bf16[1,256,256]{2,1,0:T(8,128)(2,1)S(1)}, u32[]{:S(2)}, u32[]{:S(2)}) collective-permute-start(bf16[1,256,256]{2,1,0:T(8,128)(2,1)S(1)} %get-tuple-element.61), channel_id=1, source_target_pairs={{0,12},{4,8},{8,4},{12,0},{16,28},{20,24},{24,20},{28,16},{1,13},{... | collective-permute-start | bytes 393224 | tf_op jit(solution)/shard_map/ppermute | solution.py:17
  79.4 9.1 %collective-permute-start.20 = (bf16[1,256,256]{2,1,0:T(8,128)(2,1)S(1)}, bf16[1,256,256]{2,1,0:T(8,128)(2,1)S(1)}, u32[]{:S(2)}, u32[]{:S(2)}) collective-permute-start(bf16[1,256,256]{2,1,0:T(8,128)(2,1)S(1)} %get-tuple-element.62), channel_id=1, source_target_pairs={{0,4},{4,0},{8,12},{12,8},{16,20},{20,16},{24,28},{28,24},{1,5},{5... | collective-permute-start | bytes 393224 | tf_op jit(solution)/shard_map/ppermute | solution.py:17
  80.6 9.3 %collective-permute-start.21 = (bf16[1,256,256]{2,1,0:T(8,128)(2,1)S(1)}, bf16[1,256,256]{2,1,0:T(8,128)(2,1)S(1)}, u32[]{:S(2)}, u32[]{:S(2)}) collective-permute-start(bf16[1,256,256]{2,1,0:T(8,128)(2,1)S(1)} %get-tuple-element.63), channel_id=1, source_target_pairs={{0,8},{4,12},{8,0},{12,4},{16,24},{20,28},{24,16},{28,20},{1,9},{5... | collective-permute-start | bytes 393224 | tf_op jit(solution)/shard_map/ppermute | solution.py:17
  82.2 10.6 %collective-permute-start.22 = (bf16[1,256,256]{2,1,0:T(8,128)(2,1)S(1)}, bf16[1,256,256]{2,1,0:T(8,128)(2,1)S(1)}, u32[]{:S(2)}, u32[]{:S(2)}) collective-permute-start(bf16[1,256,256]{2,1,0:T(8,128)(2,1)S(1)} %get-tuple-element.64), channel_id=1, source_target_pairs={{0,12},{4,8},{8,4},{12,0},{16,28},{20,24},{24,20},{28,16},{1,13},{... | collective-permute-start | bytes 393224 | tf_op jit(solution)/shard_map/ppermute | solution.py:17
  (5 other events, 17.9 us)

commit v30 on v28

--- a/solution.py
+++ b/solution.py
@@ -90,8 +90,8 @@
     fill_inverse(inv, row_blocks(parts, held, nodes * rows), 0, draw)
     for node in range(nodes):
         solved[node] = transposed_dot(inv[node], noise[node]).astype(BF16)
-    for step, send in enumerate(sends, 1):
-        send[0] = solved[entry_of(picks[0], myself ^ step, myself)]
+    for at, send in enumerate(sends):
+        send[0] = solved[entry_of(picks[0], myself ^ (len(sends) - at), myself)]
 
 
 def relay_kernel(half, source, waits, through, picks, far, *refs):
@@ -100,7 +100,7 @@
     for at, send in enumerate(sends):
         chunk, step = divmod(at, half - 1)
         wide = send.shape[-1]
-        node = entry_of(picks[source], myself ^ (step + 1), myself ^ half)
+        node = entry_of(picks[source], myself ^ (half - 1 - step), myself ^ half)
         send[0] = far[node, :, chunk * wide:(chunk + 1) * wide]
 
 
@@ -142,11 +142,12 @@
             here = target.at[into, :, :, pl.ds(first, ref.shape[-1])]
             copies.append(pltpu.make_async_copy(ref, here, sems.at[at]))
             copies[-1].start()
+    order = [0, *range(half - 1, 0, -1), half, *range(owners - 1, half, -1)]
     for at, (ref, place) in enumerate(zip(known, places, strict=True)):
-        step = at % owners
+        source, step = at // owners, order[at % owners]
         if step % half == 0:
-            place = entry_of(picks[at // owners], myself, myself ^ step)
-        table[at] = ref[place] if ref.shape[-1] == wide else ref[place, :, columns]
+            place = entry_of(picks[source], myself, myself ^ step)
+        table[source * owners + step] = ref[place] if ref.shape[-1] == wide else ref[place, :, columns]
     empty = level * owners
     table[empty] = jnp.zeros_like(table[empty])
     entries = lists[level - 1]
@@ -170,8 +171,8 @@
             here = target.at[level, node, :, pl.ds(chunk * wide, wide)]
             copies.append(pltpu.make_async_copy(solved.at[node], here, sems.at[len(copies)]))
             copies[-1].start()
-    for step, send in enumerate(sends, 1):
-        node = entry_of(picks[level], myself ^ step, myself)
+    for step, send in enumerate(sends):
+        node = entry_of(picks[level], myself ^ (len(sends) - step), myself)
         for at, ref in enumerate([*chunks, solved]):
             send[at] = ref[node]
     for copy in copies:
@@ -185,7 +186,7 @@
     part = shape(nodes, rows, wide)
     flat = lambda value: value.reshape(-1, rows)
     leaf = lambda value, step: hop(value, "leaf", owners, step)
-    near = lambda values: [leaf(value, step) for step, value in enumerate(values, 1)]
+    near = lambda values: [leaf(value, len(values) - at) for at, value in enumerate(values)]
     inv_here = pltpu.VMEM((nodes, rows, rows), BF16)
     dot_flops = 2 * rows * rows * wide
 
@@ -266,7 +267,7 @@
         got = [near(sent) for sent in sends]
         pieces.append([])
         for at in chunks:
-            waits = got[0] if at == 0 else got[1][:half // 2]
+            waits = got[0] if at == 0 else got[1][1:]
             sends = call(
                 functools.partial(relay_kernel, half, level, len(waits), 0),
                 [shape(1, rows, wide)] * (half - 1),

time: 90.2 us -> 91 us (level)
  waiting for transfers between devices: 36.9 us -> 41 us
  starting transfers between devices: 41.1 us -> 37.7 us
    ppermute x30, waiting for transfers between devices: 36.9 us -> 41 us  [hop(): return lax.ppermute(value, axis, [(at, at ^ step) for at in range(size)])]
    ppermute x30, starting transfers between devices: 41.1 us -> 37.7 us  [hop(): return lax.ppermute(value, axis, [(at, at ^ step) for at in range(size)])]
where the time goes in v30:
time: 91 us; the launch traced here: 90.8 us
  waiting for transfers between devices  41 us (45%)
  starting transfers between devices  37.7 us (41%)
  Pallas kernels  9.54 us (10%)
  local copies, waits for them, and re-layouts  2.24 us (2%)
    ppermute x30, waiting for transfers between devices, hop(): return lax.ppermute(value, axis, [(at, at ^ step) for at in range(size)])  41 us
    ppermute x30, starting transfers between devices, hop(): return lax.ppermute(value, axis, [(at, at ^ step) for at in range(size)])  37.7 us
    pallas_call x9, Pallas kernels, call(): pl.pallas_call(kernel, out_shape=outs, in_specs=[VMEM] * len(arrays), out...  9.54 us
  transfers between devices with their start and end apart: 30, of which 17 were waited for; matrix products, arithmetic and copies ran while one was open for 2% of the time, Pallas kernels for 7%

profile of v30, /device:TPU:0, one launch (start us, length us, event | category | flops | bytes accessed | tf_op | source)
XLA Modules:
  0.0 90.8 jit_solution(8001695877414921185)
XLA Ops:
  1.4 2.6 %collective-permute-start = (bf16[128,256]{1,0:T(8,128)(2,1)S(1)}, bf16[128,256]{1,0:T(8,128)(2,1)S(1)}, u32[]{:S(2)}, u32[]{:S(2)}) collective-permute-start(bf16[128,256]{1,0:T(8,128)(2,1)S(1)} %bitcast.8), channel_id=1, source_target_pairs={{0,2},{1,3},{2,0},{3,1},{4,6},{5,7},{6,4},{7,5},{8,10},{9,11},{10,... | collective-permute-start | bytes 196616 | tf_op jit(solution)/shard_map/ppermute | solution.py:17
  4.0 1.3 %fusion = (bf16[1,2,2,256,256]{4,3,2,1,0:T(8,128)(2,1)S(1)}, bf16[1,2,2,256,256]{4,3,2,1,0:T(8,128)(2,1)S(1)}) fusion(bf16[2,2,2,256,256]{4,3,2,1,0:T(8,128)(2,1)} %param.8), kind=kLoop, calls=%fused_computation.2 | loop fusion | bytes 2097152 | tf_op jit(solution)/shard_map/slice | solution.py:194
  5.4 1.3 %collective-permute-done.refs_1_ = bf16[128,256]{1,0:T(8,128)(2,1)S(1)} collective-permute-done((bf16[128,256]{1,0:T(8,128)(2,1)S(1)}, bf16[128,256]{1,0:T(8,128)(2,1)S(1)}, u32[]{:S(2)}, u32[]{:S(2)}) %collective-permute-start) | collective-permute-done | bytes 65568 | tf_op jit(solution)/shard_map/ppermute | solution.py:17
  6.7 1.2 %collective-permute-done.2.refs_3_ = bf16[128,256]{1,0:T(8,128)(2,1)S(1)} collective-permute-done((bf16[128,256]{1,0:T(8,128)(2,1)S(1)}, bf16[128,256]{1,0:T(8,128)(2,1)S(1)}, u32[]{:S(2)}, u32[]{:S(2)}) %collective-permute-start.2) | collective-permute-done | bytes 65568 | tf_op jit(solution)/shard_map/ppermute | solution.py:17
  8.4 1.8 %collective-permute-start.7 = (bf16[2304,256]{1,0:T(8,128)(2,1)S(1)}, bf16[2304,256]{1,0:T(8,128)(2,1)S(1)}, u32[]{:S(2)}, u32[]{:S(2)}) collective-permute-start(bf16[2304,256]{1,0:T(8,128)(2,1)S(1)} %get-tuple-element.41.refs_3_), channel_id=1, source_target_pairs={{0,2},{1,3},{2,0},{3,1},{4,6},{5,7},{6,4},{7,5},{8,10},{9,11},{10,... | collective-permute-start | bytes 3538952 | tf_op jit(solution)/shard_map/ppermute | solution.py:17
  10.2 2.6 %collective-permute-start.3 = (bf16[2,256,512]{2,1,0:T(8,128)(2,1)S(1)}, bf16[2,256,512]{2,1,0:T(8,128)(2,1)S(1)}, u32[]{:S(2)}, u32[]{:S(2)}) collective-permute-start(bf16[2,256,512]{2,1,0:T(8,128)(2,1)S(1)} %get-tuple-element.37.refs_4_.refs_20_), channel_id=1, source_target_pairs={{0,16},{4,20},{8,24},{12,28},{16,0},{20,4},{24,8},{28,12},{1,17},{... | collective-permute-start | bytes 1572872 | tf_op jit(solution)/shard_map/ppermute | solution.py:17
  12.8 2.5 %collective-permute-start.4 = (bf16[1,256,512]{2,1,0:T(8,128)(2,1)S(1)}, bf16[1,256,512]{2,1,0:T(8,128)(2,1)S(1)}, u32[]{:S(2)}, u32[]{:S(2)}) collective-permute-start(bf16[1,256,512]{2,1,0:T(8,128)(2,1)S(1)} %get-tuple-element.38), channel_id=1, source_target_pairs={{0,12},{4,8},{8,4},{12,0},{16,28},{20,24},{24,20},{28,16},{1,13},{... | collective-permute-start | bytes 786440 | tf_op jit(solution)/shard_map/ppermute | solution.py:17
  16.3 14.5 %collective-permute-done.4.refs_0_.refs_5_ = bf16[1,256,512]{2,1,0:T(8,128)(2,1)S(1)} collective-permute-done((bf16[1,256,512]{2,1,0:T(8,128)(2,1)S(1)}, bf16[1,256,512]{2,1,0:T(8,128)(2,1)S(1)}, u32[]{:S(2)}, u32[]{:S(2)}) %collective-permute-start.4) | collective-permute-done | bytes 262176 | tf_op jit(solution)/shard_map/ppermute | solution.py:17
  30.8 6.6 %collective-permute-done.5.refs_1_.refs_6_ = bf16[1,256,512]{2,1,0:T(8,128)(2,1)S(1)} collective-permute-done((bf16[1,256,512]{2,1,0:T(8,128)(2,1)S(1)}, bf16[1,256,512]{2,1,0:T(8,128)(2,1)S(1)}, u32[]{:S(2)}, u32[]{:S(2)}) %collective-permute-start.5) | collective-permute-done | bytes 262176 | tf_op jit(solution)/shard_map/ppermute | solution.py:17
  38.1 1.9 %collective-permute-start.20 = (bf16[1,256,256]{2,1,0:T(8,128)(2,1)S(1)}, bf16[1,256,256]{2,1,0:T(8,128)(2,1)S(1)}, u32[]{:S(2)}, u32[]{:S(2)}) collective-permute-start(bf16[1,256,256]{2,1,0:T(8,128)(2,1)S(1)} %get-tuple-element.59), channel_id=1, source_target_pairs={{0,12},{4,8},{8,4},{12,0},{16,28},{20,24},{24,20},{28,16},{1,13},{... | collective-permute-start | bytes 393224 | tf_op jit(solution)/shard_map/ppermute | solution.py:17
  40.5 1.1 %collective-permute-start.22 = (bf16[1,256,256]{2,1,0:T(8,128)(2,1)S(1)}, bf16[1,256,256]{2,1,0:T(8,128)(2,1)S(1)}, u32[]{:S(2)}, u32[]{:S(2)}) collective-permute-start(bf16[1,256,256]{2,1,0:T(8,128)(2,1)S(1)} %get-tuple-element.61), channel_id=1, source_target_pairs={{0,4},{4,0},{8,12},{12,8},{16,20},{20,16},{24,28},{28,24},{1,5},{5... | collective-permute-start | bytes 393224 | tf_op jit(solution)/shard_map/ppermute | solution.py:17
  42.2 2.0 %collective-permute-start.10 = (bf16[1,256,256]{2,1,0:T(8,128)(2,1)S(1)}, bf16[1,256,256]{2,1,0:T(8,128)(2,1)S(1)}, u32[]{:S(2)}, u32[]{:S(2)}) collective-permute-start(bf16[1,256,256]{2,1,0:T(8,128)(2,1)S(1)} %get-tuple-element.48), channel_id=1, source_target_pairs={{0,12},{4,8},{8,4},{12,0},{16,28},{20,24},{24,20},{28,16},{1,13},{... | collective-permute-start | bytes 393224 | tf_op jit(solution)/shard_map/ppermute | solution.py:17
  46.3 1.3 %collective-permute-done.21.refs_10_ = bf16[1,256,256]{2,1,0:T(8,128)(2,1)S(1)} collective-permute-done((bf16[1,256,256]{2,1,0:T(8,128)(2,1)S(1)}, bf16[1,256,256]{2,1,0:T(8,128)(2,1)S(1)}, u32[]{:S(2)}, u32[]{:S(2)}) %collective-permute-start.21) | collective-permute-done | bytes 131104 | tf_op jit(solution)/shard_map/ppermute | solution.py:17
  47.6 2.0 %collective-permute-done.22.refs_11_ = bf16[1,256,256]{2,1,0:T(8,128)(2,1)S(1)} collective-permute-done((bf16[1,256,256]{2,1,0:T(8,128)(2,1)S(1)}, bf16[1,256,256]{2,1,0:T(8,128)(2,1)S(1)}, u32[]{:S(2)}, u32[]{:S(2)}) %collective-permute-start.22) | collective-permute-done | bytes 131104 | tf_op jit(solution)/shard_map/ppermute | solution.py:17
  49.6 2.0 %shard_map.69 = (bf16[2,256,256]{2,1,0:T(8,128)(2,1)S(1)}, bf16[1,256,256]{2,1,0:T(8,128)(2,1)S(1)}, bf16[1,256,256]{2,1,0:T(8,128)(2,1)S(1)}, bf16[1,256,256]{2,1,0:T(8,128)(2,1)S(1)}) custom-call(s32[2,8,8]{2,1,0:T(8,128)S(1)} %copy-done.1, s32[2,2,8]{2,1,0:T(2,128)S(1)} %copy-done.2, s32[2,2]{1,0:T(2,128)S(1)} %copy-done.3, ...), custom_call_target="tpu_custom_call" | custom-call | flops 603979776 | bytes 9437840 | tf_op jit(solution)/shard_map/pallas_call | solution.py:56
  51.6 2.3 %collective-permute-start.26 = (bf16[2,256,256]{2,1,0:T(8,128)(2,1)S(1)}, bf16[2,256,256]{2,1,0:T(8,128)(2,1)S(1)}, u32[]{:S(2)}, u32[]{:S(2)}) collective-permute-start(bf16[2,256,256]{2,1,0:T(8,128)(2,1)S(1)} %get-tuple-element.62.refs_12_.refs_21_), channel_id=1, source_target_pairs={{0,16},{4,20},{8,24},{12,28},{16,0},{20,4},{24,8},{28,12},{1,17},{... | collective-permute-start | bytes 786440 | tf_op jit(solution)/shard_map/ppermute | solution.py:17
  53.8 1.0 %collective-permute-start.23 = (bf16[1,256,256]{2,1,0:T(8,128)(2,1)S(1)}, bf16[1,256,256]{2,1,0:T(8,128)(2,1)S(1)}, u32[]{:S(2)}, u32[]{:S(2)}) collective-permute-start(bf16[1,256,256]{2,1,0:T(8,128)(2,1)S(1)} %get-tuple-element.63), channel_id=1, source_target_pairs={{0,12},{4,8},{8,4},{12,0},{16,28},{20,24},{24,20},{28,16},{1,13},{... | collective-permute-start | bytes 393224 | tf_op jit(solution)/shard_map/ppermute | solution.py:17
  55.4 1.9 %collective-permute-start.25 = (bf16[1,256,256]{2,1,0:T(8,128)(2,1)S(1)}, bf16[1,256,256]{2,1,0:T(8,128)(2,1)S(1)}, u32[]{:S(2)}, u32[]{:S(2)}) collective-permute-start(bf16[1,256,256]{2,1,0:T(8,128)(2,1)S(1)} %get-tuple-element.65), channel_id=1, source_target_pairs={{0,4},{4,0},{8,12},{12,8},{16,20},{20,16},{24,28},{28,24},{1,5},{5... | collective-permute-start | bytes 393224 | tf_op jit(solution)/shard_map/ppermute | solution.py:17
  57.3 2.0 %shard_map.67 = (bf16[2,256,256]{2,1,0:T(8,128)(2,1)S(1)}, bf16[1,256,256]{2,1,0:T(8,128)(2,1)S(1)}, bf16[1,256,256]{2,1,0:T(8,128)(2,1)S(1)}, bf16[1,256,256]{2,1,0:T(8,128)(2,1)S(1)}) custom-call(s32[2,8,8]{2,1,0:T(8,128)S(1)} %copy-done.1, s32[2,2,8]{2,1,0:T(2,128)S(1)} %copy-done.2, s32[2,2]{1,0:T(2,128)S(1)} %copy-done.3, ...), custom_call_target="tpu_custom_call" | custom-call | flops 603979776 | bytes 9437840 | tf_op jit(solution)/shard_map/pallas_call | solution.py:56
  60.1 3.2 %collective-permute-done.23.refs_0_.refs_13_ = bf16[1,256,256]{2,1,0:T(8,128)(2,1)S(1)} collective-permute-done((bf16[1,256,256]{2,1,0:T(8,128)(2,1)S(1)}, bf16[1,256,256]{2,1,0:T(8,128)(2,1)S(1)}, u32[]{:S(2)}, u32[]{:S(2)}) %collective-permute-start.23) | collective-permute-done | bytes 131104 | tf_op jit(solution)/shard_map/ppermute | solution.py:17
  63.3 2.0 %collective-permute-start.14 = (bf16[1,256,256]{2,1,0:T(8,128)(2,1)S(1)}, bf16[1,256,256]{2,1,0:T(8,128)(2,1)S(1)}, u32[]{:S(2)}, u32[]{:S(2)}) collective-permute-start(bf16[1,256,256]{2,1,0:T(8,128)(2,1)S(1)} %get-tuple-element.54), channel_id=1, source_target_pairs={{0,8},{4,12},{8,0},{12,4},{16,24},{20,28},{24,16},{28,20},{1,9},{5... | collective-permute-start | bytes 393224 | tf_op jit(solution)/shard_map/ppermute | solution.py:17
  66.1 1.1 %collective-permute-start.15 = (bf16[1,256,256]{2,1,0:T(8,128)(2,1)S(1)}, bf16[1,256,256]{2,1,0:T(8,128)(2,1)S(1)}, u32[]{:S(2)}, u32[]{:S(2)}) collective-permute-start(bf16[1,256,256]{2,1,0:T(8,128)(2,1)S(1)} %get-tuple-element.55), channel_id=1, source_target_pairs={{0,4},{4,0},{8,12},{12,8},{16,20},{20,16},{24,28},{28,24},{1,5},{5... | collective-permute-start | bytes 393224 | tf_op jit(solution)/shard_map/ppermute | solution.py:17
  67.2 2.1 %collective-permute-done.26.far.refs_16_ = bf16[2,256,256]{2,1,0:T(8,128)(2,1)S(1)} collective-permute-done((bf16[2,256,256]{2,1,0:T(8,128)(2,1)S(1)}, bf16[2,256,256]{2,1,0:T(8,128)(2,1)S(1)}, u32[]{:S(2)}, u32[]{:S(2)}) %collective-permute-start.26) | collective-permute-done | bytes 262176 | tf_op jit(solution)/shard_map/ppermute | solution.py:17
  70.2 3.0 %collective-permute-start.28 = (bf16[1,256,256]{2,1,0:T(8,128)(2,1)S(1)}, bf16[1,256,256]{2,1,0:T(8,128)(2,1)S(1)}, u32[]{:S(2)}, u32[]{:S(2)}) collective-permute-start(bf16[1,256,256]{2,1,0:T(8,128)(2,1)S(1)} %get-tuple-element.67), channel_id=1, source_target_pairs={{0,8},{4,12},{8,0},{12,4},{16,24},{20,28},{24,16},{28,20},{1,9},{5... | collective-permute-start | bytes 393224 | tf_op jit(solution)/shard_map/ppermute | solution.py:17
  74.7 3.4 %collective-permute-start.13 = (bf16[1,256,256]{2,1,0:T(8,128)(2,1)S(1)}, bf16[1,256,256]{2,1,0:T(8,128)(2,1)S(1)}, u32[]{:S(2)}, u32[]{:S(2)}) collective-permute-start(bf16[1,256,256]{2,1,0:T(8,128)(2,1)S(1)} %get-tuple-element.53), channel_id=1, source_target_pairs={{0,12},{4,8},{8,4},{12,0},{16,28},{20,24},{24,20},{28,16},{1,13},{... | collective-permute-start | bytes 393224 | tf_op jit(solution)/shard_map/ppermute | solution.py:17
  78.3 1.2 %collective-permute-done.27.refs_17_ = bf16[1,256,256]{2,1,0:T(8,128)(2,1)S(1)} collective-permute-done((bf16[1,256,256]{2,1,0:T(8,128)(2,1)S(1)}, bf16[1,256,256]{2,1,0:T(8,128)(2,1)S(1)}, u32[]{:S(2)}, u32[]{:S(2)}) %collective-permute-start.27) | collective-permute-done | bytes 131104 | tf_op jit(solution)/shard_map/ppermute | solution.py:17
  80.3 1.4 %collective-permute-done.28.refs_18_ = bf16[1,256,256]{2,1,0:T(8,128)(2,1)S(1)} collective-permute-done((bf16[1,256,256]{2,1,0:T(8,128)(2,1)S(1)}, bf16[1,256,256]{2,1,0:T(8,128)(2,1)S(1)}, u32[]{:S(2)}, u32[]{:S(2)}) %collective-permute-start.28) | collective-permute-done | bytes 131104 | tf_op jit(solution)/shard_map/ppermute | solution.py:17
  81.7 1.1 %collective-permute-start.19 = (bf16[1,256,256]{2,1,0:T(8,128)(2,1)S(1)}, bf16[1,256,256]{2,1,0:T(8,128)(2,1)S(1)}, u32[]{:S(2)}, u32[]{:S(2)}) collective-permute-start(bf16[1,256,256]{2,1,0:T(8,128)(2,1)S(1)} %get-tuple-element.58), channel_id=1, source_target_pairs={{0,4},{4,0},{8,12},{12,8},{16,20},{20,16},{24,28},{28,24},{1,5},{5... | collective-permute-start | bytes 393224 | tf_op jit(solution)/shard_map/ppermute | solution.py:17
  82.8 1.8 %collective-permute-done.29.refs_19_ = bf16[1,256,256]{2,1,0:T(8,128)(2,1)S(1)} collective-permute-done((bf16[1,256,256]{2,1,0:T(8,128)(2,1)S(1)}, bf16[1,256,256]{2,1,0:T(8,128)(2,1)S(1)}, u32[]{:S(2)}, u32[]{:S(2)}) %collective-permute-start.29) | collective-permute-done | bytes 131104 | tf_op jit(solution)/shard_map/ppermute | solution.py:17
  84.6 2.0 %shard_map.71.refs_23_ = bf16[2,256,256]{2,1,0:T(8,128)(2,1)S(1)} custom-call(s32[2,8,8]{2,1,0:T(8,128)S(1)} %copy-done.1, s32[2,2,8]{2,1,0:T(2,128)S(1)} %copy-done.2, s32[2,2]{1,0:T(2,128)S(1)} %copy-done.3, bf16[3,2,256,512]{3,2,1,0:T(8,128)(2,1)S(1)} %copy-done, bf16[2,256,256]{2,1,0:T(8,128)(2,1)S(1)} %get-tuple-element.47.inv, ...), custom_call_target="tpu_custom_call" | custom-call | flops 603979776 | bytes 10355344 | tf_op jit(solution)/shard_map/pallas_call | solution.py:56
  86.7 1.3 %collective-permute-done.18.refs_18_ = bf16[1,256,256]{2,1,0:T(8,128)(2,1)S(1)} collective-permute-done((bf16[1,256,256]{2,1,0:T(8,128)(2,1)S(1)}, bf16[1,256,256]{2,1,0:T(8,128)(2,1)S(1)}, u32[]{:S(2)}, u32[]{:S(2)}) %collective-permute-start.18) | collective-permute-done | bytes 131104 | tf_op jit(solution)/shard_map/ppermute | solution.py:17
  88.1 2.7 %shard_map.72 = bf16[3,2,256,512]{3,2,1,0:T(8,128)(2,1)} custom-call(s32[2,8,8]{2,1,0:T(8,128)S(1)} %copy-done.1, s32[2,2,8]{2,1,0:T(2,128)S(1)} %copy-done.2, s32[2,2]{1,0:T(2,128)S(1)} %copy-done.3, bf16[3,2,256,512]{3,2,1,0:T(8,128)(2,1)S(1)} %copy-done, bf16[2,256,256]{2,1,0:T(8,128)(2,1)S(1)} %get-tuple-element.47.inv, ...), custom_call_target="tpu_custom_call" | custom-call | flops 603979776 | bytes 12976784 | tf_op jit(solution)/shard_map/pallas_call | solution.py:56
  (49 shorter events, 12.7 us)
Async XLA Ops:
  0.9 5.8 %collective-permute-start.1 = (bf16[128,256]{1,0:T(8,128)(2,1)S(1)}, bf16[128,256]{1,0:T(8,128)(2,1)S(1)}, u32[]{:S(2)}, u32[]{:S(2)}) collective-permute-start(bf16[128,256]{1,0:T(8,128)(2,1)S(1)} %bitcast.7), channel_id=1, source_target_pairs={{0,1},{1,0},{2,3},{3,2},{4,5},{5,4},{6,7},{7,6},{8,9},{9,8},{10,11... | collective-permute-start | bytes 196616 | tf_op jit(solution)/shard_map/ppermute | solution.py:17
  1.4 5.3 %collective-permute-start = (bf16[128,256]{1,0:T(8,128)(2,1)S(1)}, bf16[128,256]{1,0:T(8,128)(2,1)S(1)}, u32[]{:S(2)}, u32[]{:S(2)}) collective-permute-start(bf16[128,256]{1,0:T(8,128)(2,1)S(1)} %bitcast.8), channel_id=1, source_target_pairs={{0,2},{1,3},{2,0},{3,1},{4,6},{5,7},{6,4},{7,5},{8,10},{9,11},{10,... | collective-permute-start | bytes 196616 | tf_op jit(solution)/shard_map/ppermute | solution.py:17
  6.7 1.3 %collective-permute-start.2 = (bf16[128,256]{1,0:T(8,128)(2,1)S(1)}, bf16[128,256]{1,0:T(8,128)(2,1)S(1)}, u32[]{:S(2)}, u32[]{:S(2)}) collective-permute-start(bf16[128,256]{1,0:T(8,128)(2,1)S(1)} %collective-permute-done.refs_1_), channel_id=1, source_target_pairs={{0,1},{1,0},{2,3},{3,2},{4,5},{5,4},{6,7},{7,6},{8,9},{9,8},{10,11... | collective-permute-start | bytes 196616 | tf_op jit(solution)/shard_map/ppermute | solution.py:17
  8.4 29.0 %collective-permute-start.7 = (bf16[2304,256]{1,0:T(8,128)(2,1)S(1)}, bf16[2304,256]{1,0:T(8,128)(2,1)S(1)}, u32[]{:S(2)}, u32[]{:S(2)}) collective-permute-start(bf16[2304,256]{1,0:T(8,128)(2,1)S(1)} %get-tuple-element.41.refs_3_), channel_id=1, source_target_pairs={{0,2},{1,3},{2,0},{3,1},{4,6},{5,7},{6,4},{7,5},{8,10},{9,11},{10,... | collective-permute-start | bytes 3538952 | tf_op jit(solution)/shard_map/ppermute | solution.py:17
  10.2 27.1 %collective-permute-start.3 = (bf16[2,256,512]{2,1,0:T(8,128)(2,1)S(1)}, bf16[2,256,512]{2,1,0:T(8,128)(2,1)S(1)}, u32[]{:S(2)}, u32[]{:S(2)}) collective-permute-start(bf16[2,256,512]{2,1,0:T(8,128)(2,1)S(1)} %get-tuple-element.37.refs_4_.refs_20_), channel_id=1, source_target_pairs={{0,16},{4,20},{8,24},{12,28},{16,0},{20,4},{24,8},{28,12},{1,17},{... | collective-permute-start | bytes 1572872 | tf_op jit(solution)/shard_map/ppermute | solution.py:17
  12.8 18.0 %collective-permute-start.4 = (bf16[1,256,512]{2,1,0:T(8,128)(2,1)S(1)}, bf16[1,256,512]{2,1,0:T(8,128)(2,1)S(1)}, u32[]{:S(2)}, u32[]{:S(2)}) collective-permute-start(bf16[1,256,512]{2,1,0:T(8,128)(2,1)S(1)} %get-tuple-element.38), channel_id=1, source_target_pairs={{0,12},{4,8},{8,4},{12,0},{16,28},{20,24},{24,20},{28,16},{1,13},{... | collective-permute-start | bytes 786440 | tf_op jit(solution)/shard_map/ppermute | solution.py:17
  15.3 22.0 %collective-permute-start.5 = (bf16[1,256,512]{2,1,0:T(8,128)(2,1)S(1)}, bf16[1,256,512]{2,1,0:T(8,128)(2,1)S(1)}, u32[]{:S(2)}, u32[]{:S(2)}) collective-permute-start(bf16[1,256,512]{2,1,0:T(8,128)(2,1)S(1)} %get-tuple-element.39), channel_id=1, source_target_pairs={{0,8},{4,12},{8,0},{12,4},{16,24},{20,28},{24,16},{28,20},{1,9},{5... | collective-permute-start | bytes 786440 | tf_op jit(solution)/shard_map/ppermute | solution.py:17
  15.8 21.6 %collective-permute-start.6 = (bf16[1,256,512]{2,1,0:T(8,128)(2,1)S(1)}, bf16[1,256,512]{2,1,0:T(8,128)(2,1)S(1)}, u32[]{:S(2)}, u32[]{:S(2)}) collective-permute-start(bf16[1,256,512]{2,1,0:T(8,128)(2,1)S(1)} %get-tuple-element.40), channel_id=1, source_target_pairs={{0,4},{4,0},{8,12},{12,8},{16,20},{20,16},{24,28},{28,24},{1,5},{5... | collective-permute-start | bytes 786440 | tf_op jit(solution)/shard_map/ppermute | solution.py:17
  37.5 4.1 %collective-permute-start.8 = (bf16[2304,256]{1,0:T(8,128)(2,1)S(1)}, bf16[2304,256]{1,0:T(8,128)(2,1)S(1)}, u32[]{:S(2)}, u32[]{:S(2)}) collective-permute-start(bf16[2304,256]{1,0:T(8,128)(2,1)S(1)} %get-tuple-element.42.refs_0_), channel_id=1, source_target_pairs={{0,1},{1,0},{2,3},{3,2},{4,5},{5,4},{6,7},{7,6},{8,9},{9,8},{10,11... | collective-permute-start | bytes 3538952 | tf_op jit(solution)/shard_map/ppermute | solution.py:17
  37.6 4.5 %collective-permute-start.9 = (bf16[2304,256]{1,0:T(8,128)(2,1)S(1)}, bf16[2304,256]{1,0:T(8,128)(2,1)S(1)}, u32[]{:S(2)}, u32[]{:S(2)}) collective-permute-start(bf16[2304,256]{1,0:T(8,128)(2,1)S(1)} %get-tuple-element.43.refs_1_), channel_id=1, source_target_pairs={{0,1},{1,0},{2,3},{3,2},{4,5},{5,4},{6,7},{7,6},{8,9},{9,8},{10,11... | collective-permute-start | bytes 3538952 | tf_op jit(solution)/shard_map/ppermute | solution.py:17
  38.1 7.3 %collective-permute-start.20 = (bf16[1,256,256]{2,1,0:T(8,128)(2,1)S(1)}, bf16[1,256,256]{2,1,0:T(8,128)(2,1)S(1)}, u32[]{:S(2)}, u32[]{:S(2)}) collective-permute-start(bf16[1,256,256]{2,1,0:T(8,128)(2,1)S(1)} %get-tuple-element.59), channel_id=1, source_target_pairs={{0,12},{4,8},{8,4},{12,0},{16,28},{20,24},{24,20},{28,16},{1,13},{... | collective-permute-start | bytes 393224 | tf_op jit(solution)/shard_map/ppermute | solution.py:17
  40.0 7.6 %collective-permute-start.21 = (bf16[1,256,256]{2,1,0:T(8,128)(2,1)S(1)}, bf16[1,256,256]{2,1,0:T(8,128)(2,1)S(1)}, u32[]{:S(2)}, u32[]{:S(2)}) collective-permute-start(bf16[1,256,256]{2,1,0:T(8,128)(2,1)S(1)} %get-tuple-element.60), channel_id=1, source_target_pairs={{0,8},{4,12},{8,0},{12,4},{16,24},{20,28},{24,16},{28,20},{1,9},{5... | collective-permute-start | bytes 393224 | tf_op jit(solution)/shard_map/ppermute | solution.py:17
  40.5 9.1 %collective-permute-start.22 = (bf16[1,256,256]{2,1,0:T(8,128)(2,1)S(1)}, bf16[1,256,256]{2,1,0:T(8,128)(2,1)S(1)}, u32[]{:S(2)}, u32[]{:S(2)}) collective-permute-start(bf16[1,256,256]{2,1,0:T(8,128)(2,1)S(1)} %get-tuple-element.61), channel_id=1, source_target_pairs={{0,4},{4,0},{8,12},{12,8},{16,20},{20,16},{24,28},{28,24},{1,5},{5... | collective-permute-start | bytes 393224 | tf_op jit(solution)/shard_map/ppermute | solution.py:17
  42.1 7.5 %copy-start.2 = (s32[2,2,8]{2,1,0:T(2,128)S(1)}, s32[2,2,8]{2,1,0:T(2,128)}, u32[]{:S(2)}) copy-start(s32[2,2,8]{2,1,0:T(2,128)} %lists.7) | copy-start | bytes 388
  42.1 7.5 %copy-start.3 = (s32[2,2]{1,0:T(2,128)S(1)}, s32[2,2]{1,0:T(2,128)}, u32[]{:S(2)}) copy-start(s32[2,2]{1,0:T(2,128)} %counts.7) | copy-start | bytes 52
  42.2 12.6 %collective-permute-start.10 = (bf16[1,256,256]{2,1,0:T(8,128)(2,1)S(1)}, bf16[1,256,256]{2,1,0:T(8,128)(2,1)S(1)}, u32[]{:S(2)}, u32[]{:S(2)}) collective-permute-start(bf16[1,256,256]{2,1,0:T(8,128)(2,1)S(1)} %get-tuple-element.48), channel_id=1, source_target_pairs={{0,12},{4,8},{8,4},{12,0},{16,28},{20,24},{24,20},{28,16},{1,13},{... | collective-permute-start | bytes 393224 | tf_op jit(solution)/shard_map/ppermute | solution.py:17
  44.2 11.3 %collective-permute-start.11 = (bf16[1,256,256]{2,1,0:T(8,128)(2,1)S(1)}, bf16[1,256,256]{2,1,0:T(8,128)(2,1)S(1)}, u32[]{:S(2)}, u32[]{:S(2)}) collective-permute-start(bf16[1,256,256]{2,1,0:T(8,128)(2,1)S(1)} %get-tuple-element.49), channel_id=1, source_target_pairs={{0,8},{4,12},{8,0},{12,4},{16,24},{20,28},{24,16},{28,20},{1,9},{5... | collective-permute-start | bytes 393224 | tf_op jit(solution)/shard_map/ppermute | solution.py:17
  45.4 12.0 %collective-permute-start.12 = (bf16[1,256,256]{2,1,0:T(8,128)(2,1)S(1)}, bf16[1,256,256]{2,1,0:T(8,128)(2,1)S(1)}, u32[]{:S(2)}, u32[]{:S(2)}) collective-permute-start(bf16[1,256,256]{2,1,0:T(8,128)(2,1)S(1)} %get-tuple-element.50), channel_id=1, source_target_pairs={{0,4},{4,0},{8,12},{12,8},{16,20},{20,16},{24,28},{28,24},{1,5},{5... | collective-permute-start | bytes 393224 | tf_op jit(solution)/shard_map/ppermute | solution.py:17
  51.6 17.7 %collective-permute-start.26 = (bf16[2,256,256]{2,1,0:T(8,128)(2,1)S(1)}, bf16[2,256,256]{2,1,0:T(8,128)(2,1)S(1)}, u32[]{:S(2)}, u32[]{:S(2)}) collective-permute-start(bf16[2,256,256]{2,1,0:T(8,128)(2,1)S(1)} %get-tuple-element.62.refs_12_.refs_21_), channel_id=1, source_target_pairs={{0,16},{4,20},{8,24},{12,28},{16,0},{20,4},{24,8},{28,12},{1,17},{... | collective-permute-start | bytes 786440 | tf_op jit(solution)/shard_map/ppermute | solution.py:17
  53.8 9.4 %collective-permute-start.23 = (bf16[1,256,256]{2,1,0:T(8,128)(2,1)S(1)}, bf16[1,256,256]{2,1,0:T(8,128)(2,1)S(1)}, u32[]{:S(2)}, u32[]{:S(2)}) collective-permute-start(bf16[1,256,256]{2,1,0:T(8,128)(2,1)S(1)} %get-tuple-element.63), channel_id=1, source_target_pairs={{0,12},{4,8},{8,4},{12,0},{16,28},{20,24},{24,20},{28,16},{1,13},{... | collective-permute-start | bytes 393224 | tf_op jit(solution)/shard_map/ppermute | solution.py:17
  54.8 11.3 %collective-permute-start.24 = (bf16[1,256,256]{2,1,0:T(8,128)(2,1)S(1)}, bf16[1,256,256]{2,1,0:T(8,128)(2,1)S(1)}, u32[]{:S(2)}, u32[]{:S(2)}) collective-permute-start(bf16[1,256,256]{2,1,0:T(8,128)(2,1)S(1)} %get-tuple-element.64), channel_id=1, source_target_pairs={{0,8},{4,12},{8,0},{12,4},{16,24},{20,28},{24,16},{28,20},{1,9},{5... | collective-permute-start | bytes 393224 | tf_op jit(solution)/shard_map/ppermute | solution.py:17
  55.4 11.8 %collective-permute-start.25 = (bf16[1,256,256]{2,1,0:T(8,128)(2,1)S(1)}, bf16[1,256,256]{2,1,0:T(8,128)(2,1)S(1)}, u32[]{:S(2)}, u32[]{:S(2)}) collective-permute-start(bf16[1,256,256]{2,1,0:T(8,128)(2,1)S(1)} %get-tuple-element.65), channel_id=1, source_target_pairs={{0,4},{4,0},{8,12},{12,8},{16,20},{20,16},{24,28},{28,24},{1,5},{5... | collective-permute-start | bytes 393224 | tf_op jit(solution)/shard_map/ppermute | solution.py:17
  59.3 18.8 %collective-permute-start.16 = (bf16[2,256,256]{2,1,0:T(8,128)(2,1)S(1)}, bf16[2,256,256]{2,1,0:T(8,128)(2,1)S(1)}, u32[]{:S(2)}, u32[]{:S(2)}) collective-permute-start(bf16[2,256,256]{2,1,0:T(8,128)(2,1)S(1)} %get-tuple-element.52.refs_12_.refs_22_), channel_id=1, source_target_pairs={{0,16},{4,20},{8,24},{12,28},{16,0},{20,4},{24,8},{28,12},{1,17},{... | collective-permute-start | bytes 786440 | tf_op jit(solution)/shard_map/ppermute | solution.py:17
  63.3 10.9 %collective-permute-start.14 = (bf16[1,256,256]{2,1,0:T(8,128)(2,1)S(1)}, bf16[1,256,256]{2,1,0:T(8,128)(2,1)S(1)}, u32[]{:S(2)}, u32[]{:S(2)}) collective-permute-start(bf16[1,256,256]{2,1,0:T(8,128)(2,1)S(1)} %get-tuple-element.54), channel_id=1, source_target_pairs={{0,8},{4,12},{8,0},{12,4},{16,24},{20,28},{24,16},{28,20},{1,9},{5... | collective-permute-start | bytes 393224 | tf_op jit(solution)/shard_map/ppermute | solution.py:17
  66.1 8.5 %collective-permute-start.15 = (bf16[1,256,256]{2,1,0:T(8,128)(2,1)S(1)}, bf16[1,256,256]{2,1,0:T(8,128)(2,1)S(1)}, u32[]{:S(2)}, u32[]{:S(2)}) collective-permute-start(bf16[1,256,256]{2,1,0:T(8,128)(2,1)S(1)} %get-tuple-element.55), channel_id=1, source_target_pairs={{0,4},{4,0},{8,12},{12,8},{16,20},{20,16},{24,28},{28,24},{1,5},{5... | collective-permute-start | bytes 393224 | tf_op jit(solution)/shard_map/ppermute | solution.py:17
  69.4 10.1 %collective-permute-start.27 = (bf16[1,256,256]{2,1,0:T(8,128)(2,1)S(1)}, bf16[1,256,256]{2,1,0:T(8,128)(2,1)S(1)}, u32[]{:S(2)}, u32[]{:S(2)}) collective-permute-start(bf16[1,256,256]{2,1,0:T(8,128)(2,1)S(1)} %get-tuple-element.66), channel_id=1, source_target_pairs={{0,12},{4,8},{8,4},{12,0},{16,28},{20,24},{24,20},{28,16},{1,13},{... | collective-permute-start | bytes 393224 | tf_op jit(solution)/shard_map/ppermute | solution.py:17
  70.2 11.5 %collective-permute-start.28 = (bf16[1,256,256]{2,1,0:T(8,128)(2,1)S(1)}, bf16[1,256,256]{2,1,0:T(8,128)(2,1)S(1)}, u32[]{:S(2)}, u32[]{:S(2)}) collective-permute-start(bf16[1,256,256]{2,1,0:T(8,128)(2,1)S(1)} %get-tuple-element.67), channel_id=1, source_target_pairs={{0,8},{4,12},{8,0},{12,4},{16,24},{20,28},{24,16},{28,20},{1,9},{5... | collective-permute-start | bytes 393224 | tf_op jit(solution)/shard_map/ppermute | solution.py:17
  74.1 10.4 %collective-permute-start.29 = (bf16[1,256,256]{2,1,0:T(8,128)(2,1)S(1)}, bf16[1,256,256]{2,1,0:T(8,128)(2,1)S(1)}, u32[]{:S(2)}, u32[]{:S(2)}) collective-permute-start(bf16[1,256,256]{2,1,0:T(8,128)(2,1)S(1)} %get-tuple-element.68), channel_id=1, source_target_pairs={{0,4},{4,0},{8,12},{12,8},{16,20},{20,16},{24,28},{28,24},{1,5},{5... | collective-permute-start | bytes 393224 | tf_op jit(solution)/shard_map/ppermute | solution.py:17
  74.7 11.9 %collective-permute-start.13 = (bf16[1,256,256]{2,1,0:T(8,128)(2,1)S(1)}, bf16[1,256,256]{2,1,0:T(8,128)(2,1)S(1)}, u32[]{:S(2)}, u32[]{:S(2)}) collective-permute-start(bf16[1,256,256]{2,1,0:T(8,128)(2,1)S(1)} %get-tuple-element.53), channel_id=1, source_target_pairs={{0,12},{4,8},{8,4},{12,0},{16,28},{20,24},{24,20},{28,16},{1,13},{... | collective-permute-start | bytes 393224 | tf_op jit(solution)/shard_map/ppermute | solution.py:17
  78.2 8.5 %collective-permute-start.17 = (bf16[1,256,256]{2,1,0:T(8,128)(2,1)S(1)}, bf16[1,256,256]{2,1,0:T(8,128)(2,1)S(1)}, u32[]{:S(2)}, u32[]{:S(2)}) collective-permute-start(bf16[1,256,256]{2,1,0:T(8,128)(2,1)S(1)} %get-tuple-element.56), channel_id=1, source_target_pairs={{0,12},{4,8},{8,4},{12,0},{16,28},{20,24},{24,20},{28,16},{1,13},{... | collective-permute-start | bytes 393224 | tf_op jit(solution)/shard_map/ppermute | solution.py:17
  79.5 8.5 %collective-permute-start.18 = (bf16[1,256,256]{2,1,0:T(8,128)(2,1)S(1)}, bf16[1,256,256]{2,1,0:T(8,128)(2,1)S(1)}, u32[]{:S(2)}, u32[]{:S(2)}) collective-permute-start(bf16[1,256,256]{2,1,0:T(8,128)(2,1)S(1)} %get-tuple-element.57), channel_id=1, source_target_pairs={{0,8},{4,12},{8,0},{12,4},{16,24},{20,28},{24,16},{28,20},{1,9},{5... | collective-permute-start | bytes 393224 | tf_op jit(solution)/shard_map/ppermute | solution.py:17
  81.7 6.3 %collective-permute-start.19 = (bf16[1,256,256]{2,1,0:T(8,128)(2,1)S(1)}, bf16[1,256,256]{2,1,0:T(8,128)(2,1)S(1)}, u32[]{:S(2)}, u32[]{:S(2)}) collective-permute-start(bf16[1,256,256]{2,1,0:T(8,128)(2,1)S(1)} %get-tuple-element.58), channel_id=1, source_target_pairs={{0,4},{4,0},{8,12},{12,8},{16,20},{20,16},{24,28},{28,24},{1,5},{5... | collective-permute-start | bytes 393224 | tf_op jit(solution)/shard_map/ppermute | solution.py:17
  (2 other events, 4.1 us)
